TPU v7x, 32 devices: a whole 2x2x4 slice. The times are simulated.
32 devices in a mesh: wide: 8 (over z, core), node: 4 (over y, x).
Axes of the slice: x: 2, y: 2, z: 4, core: 2. Of those that a mesh axis runs over, the one named last changes fastest.
Arguments:
- act_in: bfloat16 [2, 16, 128, 2560], P(None, 'wide'), may hold values from -6 to 6
- mixing: bfloat16 [2, 16, 32, 128, 128], P(None, 'wide', 'node'), may hold values from 0 to 0.14941406
- cotangent: bfloat16 [2, 16, 128, 2560], P(None, 'wide'), may hold values from -0.125 to 0.125
- w_value: bfloat16 [2560, 2048], P('wide', 'node'), may hold values from -0.125 to 0.125
- w_out: bfloat16 [2560, 2048], P('wide', 'node'), may hold values from -0.125 to 0.125
Outputs:
- layer_out: bfloat16 [2, 16, 128, 2560], P(None, 'wide', None, 'node')
- grad_value: float32 [2560, 2048], P('wide', 'node')
- grad_out: float32 [2560, 2048], P('wide', 'node')
All inputs are finite; a program needn't handle non-finite values.
Results may differ from a plain program's by a relative error of at most 0.0095.
Values may be sent and summed in bfloat16 or wider, within the bound.
No kernel may reach another device: no remote copies, remote signals or barrier semaphores. Data moves between devices by JAX's collectives and lax.ppermute only.
A program may use at most 64 MiB of HBM per device.

v0:
```python
import jax
import jax.numpy as jnp
from jax import lax
from jax.sharding import PartitionSpec as P

HEAD_DIM = 64


def body(act_in, mixing, cotangent, w_value, w_out):
    hd_node = w_value.shape[1]
    heads_here = hd_node // HEAD_DIM
    micro_count = act_in.shape[0]
    images = act_in.shape[1]
    seq_len = act_in.shape[2]
    model_width = act_in.shape[3]
    token_count = images * seq_len
    full_value, full_out = (
        lax.all_gather(w_value, "wide", axis=0, tiled=True),
        lax.all_gather(w_out, "wide", axis=0, tiled=True),
    )
    grad_value = jnp.zeros((w_value.shape[0], hd_node), jnp.float32)
    grad_out = jnp.zeros((w_value.shape[0], hd_node), jnp.float32)
    outputs = []
    for micro_index in range(micro_count):
        token_rows = act_in[micro_index].reshape(token_count, model_width)
        upstream = cotangent[micro_index].reshape(token_count, model_width)
        weights_mix = mixing[micro_index]
        value_rows = jnp.dot(token_rows, full_value, preferred_element_type=jnp.float32).astype(
            jnp.bfloat16
        )
        value_heads = value_rows.reshape(images, seq_len, heads_here, HEAD_DIM)
        mixed_rows = (
            jnp.einsum(
                "ihqk,ikhd->iqhd", weights_mix, value_heads, preferred_element_type=jnp.float32
            )
            .astype(jnp.bfloat16)
            .reshape(token_count, hd_node)
        )
        partial_value = lax.dot_general(
            mixed_rows, full_out, (((1,), (1,)), ((), ())), preferred_element_type=jnp.float32
        )
        summed = lax.psum_scatter(
            partial_value.astype(jnp.bfloat16), "node", scatter_dimension=1, tiled=True
        ).astype(jnp.float32)
        outputs.append(summed.astype(jnp.bfloat16).reshape(images, seq_len, summed.shape[1]))
        d_mixed = jnp.dot(upstream, full_out, preferred_element_type=jnp.float32).astype(
            jnp.bfloat16
        )
        d_heads = d_mixed.reshape(images, seq_len, heads_here, HEAD_DIM)
        d_value = (
            jnp.einsum("ihqk,iqhd->ikhd", weights_mix, d_heads, preferred_element_type=jnp.float32)
            .astype(jnp.bfloat16)
            .reshape(token_count, hd_node)
        )
        term_value = lax.dot_general(
            token_rows, d_value, (((0,), (0,)), ((), ())), preferred_element_type=jnp.float32
        )
        term_out = lax.dot_general(
            upstream, mixed_rows, (((0,), (0,)), ((), ())), preferred_element_type=jnp.float32
        )
        share_value, share_out = (
            lax.psum_scatter(term_value, "wide", scatter_dimension=0, tiled=True),
            lax.psum_scatter(term_out, "wide", scatter_dimension=0, tiled=True),
        )
        grad_value = grad_value + share_value
        grad_out = grad_out + share_out
    return (jnp.stack(outputs, axis=0), grad_value, grad_out)


def solution(mesh):
    return jax.shard_map(
        body,
        mesh=mesh,
        in_specs=(
            P(None, "wide", None, None),
            P(None, "wide", "node", None, None),
            P(None, "wide", None, None),
            P("wide", "node"),
            P("wide", "node"),
        ),
        out_specs=(P(None, "wide", None, "node"), P("wide", "node"), P("wide", "node")),
        check_vma=False,
    )
```

profile of v0, /device:TPU:0, one launch (start us, length us, event | category | flops | bytes accessed | tf_op | source)
XLA Modules:
  0.0 276.0 jit_solution(11237560425408749275)
XLA Ops:
  7.2 0.0 all-gather.3.cloned.1.call-start
  7.2 0.7 all-gather.3.cloned.1.call-update
  7.9 0.0 all-gather.5.cloned.1.call-start
  7.9 0.7 all-gather.5.cloned.1.call-update
  8.6 0.0 reduce-scatter.15.cloned.1.call-start
  8.7 3.0 %fusion.31 = (bf16[1,2,128,2560]{3,2,1,0:T(8,128)(2,1)}, bf16[1,2,128,2560]{3,2,1,0:T(8,128)(2,1)S(1)}) fusion(bf16[2,2,128,2560]{3,2,1,0:T(8,128)(2,1)} %param.5), kind=kLoop, calls=%fused_computation.44 | loop fusion | bytes 5242880 | tf_op jit(solution)/shard_map/slice | solution.py:25
  11.7 0.0 copy-start.1
  11.7 34.5 %all-gather.3.cloned.1.call-done = bf16[2560,512]{1,0:T(8,128)(2,1)} async-done(((bf16[320,512]{1,0:T(8,128)(2,1)}), bf16[2560,512]{1,0:T(8,128)(2,1)}) %all-gather.3.cloned.1.call-update) | async-done | bytes 2621456 | tf_op jit(solution)/shard_map/all_gather | solution.py:18
  46.3 0.0 copy-start.7
  46.3 2.7 convolution_convert_fusion.4
  48.9 0.3 reshape.39
  49.2 0.0 copy-done.1
  49.2 0.0 copy-done.7
  49.2 0.5 fusion.1
  49.7 0.3 copy.33
  50.0 30.8 %all-gather.5.cloned.1.call-done = bf16[2560,512]{1,0:T(8,128)(2,1)} async-done(((bf16[320,512]{1,0:T(8,128)(2,1)}), bf16[2560,512]{1,0:T(8,128)(2,1)}) %all-gather.5.cloned.1.call-update) | async-done | bytes 2621456 | tf_op jit(solution)/shard_map/all_gather | solution.py:19
  80.8 2.6 convolution_convert_fusion
  83.4 1.4 copy.52
  84.9 0.0 reduce-scatter.15.cloned.1.call-update
  84.9 0.0 reduce-scatter.13.cloned.1.call-start
  85.0 0.0 copy-start
  85.0 3.8 %convolution_convert_fusion.5 = bf16[256,512]{1,0:T(8,128)(2,1)} fusion(bf16[256,2560]{1,0:T(8,128)(2,1)} %bitcast.86, bf16[2560,512]{1,0:T(8,128)(2,1)} %all-gather.3.cloned.1.call-done), kind=kOutput, calls=%fused_computation.7 | convolution fusion | flops 671219712 | bytes 4194304 | tf_op jit(solution)/shard_map/dot_general | solution.py:28
  88.8 1.3 reshape.38
  90.1 1.5 fusion
  91.6 0.3 copy.30
  91.9 0.0 copy-done
  91.9 2.0 convolution_convert_fusion.1
  93.9 2.5 copy.50
  96.3 0.0 reduce-scatter.13.cloned.1.call-update
  96.4 0.0 reduce-scatter.17.cloned.1.call-start
  96.4 3.0 %fusion.30 = (bf16[1,2,128,2560]{3,2,1,0:T(8,128)(2,1)S(1)}, bf16[1,2,128,2560]{3,2,1,0:T(8,128)(2,1)}) fusion(bf16[2,2,128,2560]{3,2,1,0:T(8,128)(2,1)} %param.7), kind=kLoop, calls=%fused_computation.43 | loop fusion | bytes 5242880 | tf_op jit(solution)/shard_map/slice | solution.py:26
  99.5 0.0 copy-start.3
  99.5 1.1 copy-done.3
  100.6 0.8 convolution_convert_fusion.2
  101.4 1.1 reshape.41
  102.5 1.5 fusion.3
  104.0 0.3 copy.39
  104.3 2.9 %convolution_convert_fusion.3 = bf16[256,512]{1,0:T(8,128)(2,1)} fusion(bf16[256,2560]{1,0:T(8,128)(2,1)} %bitcast.88, bf16[2560,512]{1,0:T(8,128)(2,1)S(1)} %copy-done), kind=kOutput, calls=%fused_computation.5 | convolution fusion | flops 671219712 | bytes 4194304 | tf_op jit(solution)/shard_map/dot_general | solution.py:46
  107.2 0.0 copy-start.5
  107.2 1.4 reshape.40
  108.5 1.3 fusion.2
  109.9 0.3 copy.36
  110.2 0.0 copy-done.5
  110.2 0.0 copy-start.2
  110.2 0.8 fusion.18
  111.0 0.5 copy-done.2
  111.5 3.2 %add_bitcast_fusion.1 = f32[2560,512]{0,1:T(8,128)} fusion(f32[512,2560]{1,0:T(8,128)S(1)} %fusion.18, bf16[256,2560]{1,0:T(8,128)(2,1)S(1)} %bitcast.81, bf16[64,8,2,128]{3,2,1,0:T(2,128)(2,1)S(1)} %bitcast.96), kind=kOutput, calls=%fused_computation.1 | convolution fusion | flops 672399360 | bytes 12058624 | tf_op jit(solution)/shard_map/dot_general | solution.py:55
  114.7 5.9 %copy.54 = f32[2560,512]{1,0:T(8,128)} copy(f32[2560,512]{0,1:T(8,128)} %add_bitcast_fusion.1) | data formatting | bytes 10485760
  120.6 0.0 reduce-scatter.17.cloned.1.call-update
  120.6 0.0 copy-start.4
  120.7 0.0 reduce-scatter.19.cloned.1.call-start
  120.7 1.2 copy-done.6
  121.9 0.8 fusion.23
  122.8 0.0 copy-done.4
  122.8 3.2 %add_bitcast_fusion = f32[2560,512]{0,1:T(8,128)} fusion(f32[512,2560]{1,0:T(8,128)S(1)} %fusion.23, bf16[256,2560]{1,0:T(8,128)(2,1)S(1)} %bitcast.83, bf16[64,8,2,128]{3,2,1,0:T(2,128)(2,1)S(1)} %bitcast.91), kind=kOutput, calls=%fused_computation | convolution fusion | flops 672399360 | bytes 12058624 | tf_op jit(solution)/shard_map/dot_general | solution.py:58
  126.0 6.0 %copy.56 = f32[2560,512]{1,0:T(8,128)} copy(f32[2560,512]{0,1:T(8,128)} %add_bitcast_fusion) | data formatting | bytes 10485760
  132.0 0.0 reduce-scatter.19.cloned.1.call-update
  132.1 0.0 reduce-scatter.15.cloned.1.call-done
  132.1 1.2 copy.53
  133.3 12.2 %reduce-scatter.13.cloned.1.call-done = bf16[640,256]{1,0:T(8,128)(2,1)} async-done(((bf16[2560,256]{1,0:T(8,128)(2,1)}), bf16[640,256]{1,0:T(8,128)(2,1)}) %reduce-scatter.13.cloned.1.call-update) | async-done | bytes 327696
  145.5 1.2 copy.51
  146.7 0.9 pad_maximum_fusion
  147.6 60.6 %reduce-scatter.17.cloned.1.call-done = f32[320,512]{1,0:T(8,128)} async-done(((f32[2560,512]{1,0:T(8,128)}), f32[320,512]{1,0:T(8,128)}) %reduce-scatter.17.cloned.1.call-update) | async-done | bytes 655376
  208.1 61.0 %reduce-scatter.19.cloned.1.call-done = f32[320,512]{1,0:T(8,128)} async-done(((f32[2560,512]{1,0:T(8,128)}), f32[320,512]{1,0:T(8,128)}) %reduce-scatter.19.cloned.1.call-update) | async-done | bytes 655376
  (1 shorter events, 0.0 us)
Async XLA Ops:
  7.2 39.1 %all-gather.3.cloned.1.call-start = ((), (), s32[]{:S(2)}) async-start(), calls=%async_computation.4 | async-start | bytes 2949120 | tf_op jit(solution)/shard_map/all_gather | solution.py:18
  7.9 72.9 %all-gather.5.cloned.1.call-start = ((), (), s32[]{:S(2)}) async-start(), calls=%async_computation.5 | async-start | bytes 2949120 | tf_op jit(solution)/shard_map/all_gather | solution.py:19
  8.6 123.4 %reduce-scatter.15.cloned.1.call-start = ((), (), s32[]{:S(2)}) async-start(), calls=%async_computation.7 | async-start | bytes 1638400
  11.7 37.5 %copy-start.1 = (bf16[1,2,128,2560]{3,2,1,0:T(8,128)(2,1)}, bf16[1,2,128,2560]{3,2,1,0:T(8,128)(2,1)S(1)}, u32[]{:S(2)}) copy-start(bf16[1,2,128,2560]{3,2,1,0:T(8,128)(2,1)S(1)} %get-tuple-element.15) | copy-start | bytes 3932164
  46.3 3.0 %copy-start.7 = (bf16[2,2,8,128,128]{4,3,2,1,0:T(8,128)(2,1)S(1)}, bf16[2,2,8,128,128]{4,3,2,1,0:T(8,128)(2,1)}, u32[]{:S(2)}) copy-start(bf16[2,2,8,128,128]{4,3,2,1,0:T(8,128)(2,1)} %param.6) | copy-start | bytes 3145732
  84.9 60.6 %reduce-scatter.13.cloned.1.call-start = ((), (), s32[]{:S(2)}) async-start(), calls=%async_computation.6 | async-start | bytes 1638400
  85.0 6.9 %copy-start = (bf16[2560,512]{1,0:T(8,128)(2,1)S(1)}, bf16[2560,512]{1,0:T(8,128)(2,1)}, u32[]{:S(2)}) copy-start(bf16[2560,512]{1,0:T(8,128)(2,1)} %all-gather.5.cloned.1.call-done) | copy-start | bytes 7864324
  96.4 111.8 %reduce-scatter.17.cloned.1.call-start = ((), (), s32[]{:S(2)}) async-start(), calls=%async_computation.8 | async-start | bytes 5898240
  99.5 1.1 copy-start.3
  107.2 3.0 %copy-start.5 = (bf16[1,2,128,2560]{3,2,1,0:T(8,128)(2,1)S(1)}, bf16[1,2,128,2560]{3,2,1,0:T(8,128)(2,1)}, u32[]{:S(2)}) copy-start(bf16[1,2,128,2560]{3,2,1,0:T(8,128)(2,1)} %get-tuple-element.14) | copy-start | bytes 3932164
  110.2 1.3 copy-start.2
  120.6 1.3 copy-start.6
  120.6 2.1 copy-start.4
  120.7 148.5 %reduce-scatter.19.cloned.1.call-start = ((), (), s32[]{:S(2)}) async-start(), calls=%async_computation.9 | async-start | bytes 5898240
Sparse Core Ops, SparseCore 0:
  9.6 36.5 all-gather.2
  47.9 32.8 all-gather.4
  85.0 28.3 reduce-scatter.14
  116.2 29.2 reduce-scatter.12
  148.2 59.8 reduce-scatter.16
  210.9 58.2 reduce-scatter.18
where the time goes:
time: 277 us; the launch traced here: 276 us
  waiting for transfers between devices  201 us (73%)
  local copies, waits for them, and re-layouts  32.2 us (12%)
  matrix products  27.8 us (10%)
  between operations  14.3 us (5%)
    unnamed x10, waiting for transfers between devices  135 us
    all_gather x1, waiting for transfers between devices, body(): lax.all_gather(w_value, 'wide', axis=0, tiled=True)  34.5 us
    all_gather x1, waiting for transfers between devices, body(): lax.all_gather(w_out, 'wide', axis=0, tiled=True)  30.8 us
    unnamed x22, local copies, waits for them, and re-layouts  21 us
    dot_general x2, matrix products, body(): jnp.dot(token_rows, full_value, preferred_element_type=jnp.float32)  6.49 us
  transfers between devices with their start and end apart: 6, of which 5 were waited for; matrix products, arithmetic and copies ran while one was open for 20% of the time, Pallas kernels for 0%

commit v1 on v0

v1 whole, which is shorter than its diff:
```python
import jax
import jax.numpy as jnp
from jax import lax
from jax.sharding import PartitionSpec as P

HEAD_DIM = 64
F32 = jnp.float32
BF16 = jnp.bfloat16


def make_body(n_wide, n_node):
    pairs = n_wide // 2

    def shift(x, j):
        perm = [
            (2 * s + c, 2 * ((s + j) % pairs) + c) for s in range(pairs) for c in range(2)
        ]
        return lax.ppermute(x, "wide", perm)

    def sibling(x):
        return lax.ppermute(x, "wide", [(i, i ^ 1) for i in range(n_wide)])

    def gather(w, z, c):
        depth = w.shape[0]
        full = jnp.zeros((n_wide * depth, w.shape[1]), w.dtype)
        for j in range(pairs):
            own = w if j == 0 else shift(w, j)
            other = sibling(own)
            row = 2 * lax.rem(z - j + pairs, pairs)
            full = lax.dynamic_update_slice(full, own, ((row + c) * depth, 0))
            full = lax.dynamic_update_slice(full, other, ((row + 1 - c) * depth, 0))
        return full

    def scatter(grad, z, c):
        depth = grad.shape[0] // n_wide
        blocks = grad.reshape(pairs, 2, depth, grad.shape[1])
        mine = lax.dynamic_index_in_dim(blocks, c, 1, keepdims=False)
        theirs = lax.dynamic_index_in_dim(blocks, 1 - c, 1, keepdims=False)
        held = mine + sibling(theirs.astype(BF16)).astype(F32)
        total = lax.dynamic_index_in_dim(held, z, 0, keepdims=False)
        for j in range(1, pairs):
            part = lax.dynamic_index_in_dim(held, lax.rem(z + j, pairs), 0, keepdims=False)
            total = total + shift(part.astype(BF16), j).astype(F32)
        return total

    def node_sum(partial, n):
        tokens, width = partial.shape
        blocks = partial.reshape(tokens, n_node, width // n_node)
        total = lax.dynamic_index_in_dim(blocks, n, 1, keepdims=False).astype(F32)
        for j in range(1, n_node):
            dest = lax.bitwise_xor(n, jnp.int32(j))
            part = lax.dynamic_index_in_dim(blocks, dest, 1, keepdims=False)
            got = lax.ppermute(part, "node", [(i, i ^ j) for i in range(n_node)])
            total = total + got.astype(F32)
        return total.astype(BF16)

    def body(act_in, mixing, cotangent, w_value, w_out):
        wide = lax.axis_index("wide")
        n = lax.axis_index("node")
        z, c = wide // 2, lax.rem(wide, 2)
        cols = w_value.shape[1]
        heads = cols // HEAD_DIM
        micro, images, seq, width = act_in.shape
        groups = micro * images
        tokens = groups * seq
        act = act_in.reshape(tokens, width)
        cot = cotangent.reshape(tokens, width)
        mix = mixing.reshape(groups, heads, seq, seq)

        full_value = gather(w_value, z, c)
        full_out = gather(w_out, z, c)

        value = jnp.dot(act, full_value, preferred_element_type=F32).astype(BF16)
        mixed = (
            jnp.einsum(
                "ihqk,ikhd->iqhd",
                mix,
                value.reshape(groups, seq, heads, HEAD_DIM),
                preferred_element_type=F32,
            )
            .astype(BF16)
            .reshape(tokens, cols)
        )
        term_out = lax.dot_general(
            cot, mixed, (((0,), (0,)), ((), ())), preferred_element_type=F32
        )
        grad_out = scatter(term_out, z, c)

        d_mixed = jnp.dot(cot, full_out, preferred_element_type=F32).astype(BF16)
        d_value = (
            jnp.einsum(
                "ihqk,iqhd->ikhd",
                mix,
                d_mixed.reshape(groups, seq, heads, HEAD_DIM),
                preferred_element_type=F32,
            )
            .astype(BF16)
            .reshape(tokens, cols)
        )
        term_value = lax.dot_general(
            act, d_value, (((0,), (0,)), ((), ())), preferred_element_type=F32
        )
        grad_value = scatter(term_value, z, c)

        partial = lax.dot_general(
            mixed, full_out, (((1,), (1,)), ((), ())), preferred_element_type=F32
        ).astype(BF16)
        layer_out = node_sum(partial, n).reshape(micro, images, seq, width // n_node)
        return layer_out, grad_value, grad_out

    return body


def solution(mesh):
    return jax.shard_map(
        make_body(mesh.shape["wide"], mesh.shape["node"]),
        mesh=mesh,
        in_specs=(
            P(None, "wide", None, None),
            P(None, "wide", "node", None, None),
            P(None, "wide", None, None),
            P("wide", "node"),
            P("wide", "node"),
        ),
        out_specs=(P(None, "wide", None, "node"), P("wide", "node"), P("wide", "node")),
        check_vma=False,
    )
```

time: 277 us -> 188 us (0.68)
  waiting for transfers between devices: 201 us -> 87.8 us
  starting transfers between devices: 0.24 us -> 30.3 us
  between operations: 14.3 us -> 0.98 us
  local copies, waits for them, and re-layouts: 32.2 us -> 39.4 us
  other arithmetic: 0.91 us -> 7.55 us
  matrix products: 27.8 us -> 21.4 us
    unnamed x10 -> x0, waiting for transfers between devices: 135 us -> none
    ppermute x0 -> x25, waiting for transfers between devices: none -> 87.8 us  [the longest x12 66.6 us: shift(): return lax.ppermute(x, 'wide', perm)]
    all_gather x2 -> x0, waiting for transfers between devices: 65.3 us -> none  [the longest x1 34.5 us: body(): lax.all_gather(w_value, 'wide', axis=0, tiled=True)]
    ppermute x0 -> x25, starting transfers between devices: none -> 30.3 us  [the longest x12 23.9 us: shift(): return lax.ppermute(x, 'wide', perm)]
    unnamed x22 -> x23, local copies, waits for them, and re-layouts: 21 us -> 2.41 us
    dot_general x0 -> x2, local copies, waits for them, and re-layouts: none -> 11.9 us  [the longest x1 5.96 us: body(): lax.dot_general(cot, mixed, (((0,), (0,)), ((), ())), preferred_element_t...]
    add x0 -> x4, other arithmetic: none -> 6.43 us  [the longest x2 4.42 us: scatter(): held = mine + sibling(theirs.astype(BF16)).astype(F32)]
    dot_general x14 -> x7, matrix products: 27.8 us -> 21.4 us  [the longest x1 4.11 us: body(): d_mixed = jnp.dot(cot, full_out, preferred_element_type=F32).astype(BF16)]
  transfers between devices with their start and end apart: 6 -> 25, of which waited for: 5 -> 10; matrix products, arithmetic and copies ran while one was open for 20% -> 20% of each run, Pallas kernels for 0% -> 0%
where the time goes in v1:
time: 188 us; the launch traced here: 187 us
  waiting for transfers between devices  87.8 us (47%)
  local copies, waits for them, and re-layouts  39.4 us (21%)
  starting transfers between devices  30.3 us (16%)
  matrix products  21.4 us (11%)
  other arithmetic  7.55 us (4%)
    ppermute x12, waiting for transfers between devices, shift(): return lax.ppermute(x, 'wide', perm)  66.6 us
    ppermute x12, starting transfers between devices, shift(): return lax.ppermute(x, 'wide', perm)  23.9 us
    ppermute x3, waiting for transfers between devices, node_sum(): got = lax.ppermute(part, 'node', [(i, i ^ j) for i in range(n_node)])  19.7 us
    convert_element_type x2, local copies, waits for them, and re-layouts, scatter(): held = mine + sibling(theirs.astype(BF16)).astype(F32)  6.28 us
    dot_general x1, local copies, waits for them, and re-layouts, body(): lax.dot_general(cot, mixed, (((0,), (0,)), ((), ())), preferred_element_t...  5.96 us
    dot_general x1, local copies, waits for them, and re-layouts, body(): lax.dot_general(act, d_value, (((0,), (0,)), ((), ())), preferred_element...  5.92 us
    dynamic_slice x1, local copies, waits for them, and re-layouts, node_sum(): total = lax.dynamic_index_in_dim(blocks, n, 1, keepdims=False).astype(F32)  5.49 us
    reshape x1, local copies, waits for them, and re-layouts, node_sum(): blocks = partial.reshape(tokens, n_node, width // n_node)  4.51 us
  transfers between devices with their start and end apart: 25, of which 10 were waited for; matrix products, arithmetic and copies ran while one was open for 20% of the time, Pallas kernels for 0%

profile of v1, /device:TPU:0, one launch (start us, length us, event | category | flops | bytes accessed | tf_op | source)
XLA Modules:
  0.0 187.4 jit_solution(16397012360426082263)
XLA Ops:
  0.7 0.5 collective-permute-start.7
  1.2 2.6 %collective-permute-start.1 = (bf16[320,512]{1,0:T(8,128)(2,1)}, bf16[320,512]{1,0:T(8,128)(2,1)}, u32[]{:S(2)}, u32[]{:S(2)}) collective-permute-start(bf16[320,512]{1,0:T(8,128)(2,1)} %param.8), channel_id=1, source_target_pairs={{0,8},{4,12},{8,16},{12,20},{16,24},{20,28},{24,0},{28,4},{1,9},{5... | collective-permute-start | bytes 983048 | tf_op jit(solution)/shard_map/ppermute | solution.py:18
  3.8 0.2 collective-permute-start
  4.0 2.3 %collective-permute-start.5 = (bf16[320,512]{1,0:T(8,128)(2,1)}, bf16[320,512]{1,0:T(8,128)(2,1)S(1)}, u32[]{:S(2)}, u32[]{:S(2)}) collective-permute-start(bf16[320,512]{1,0:T(8,128)(2,1)} %param.8), channel_id=1, source_target_pairs={{0,24},{4,28},{8,0},{12,4},{16,8},{20,12},{24,16},{28,20},{1,25},{... | collective-permute-start | bytes 983048 | tf_op jit(solution)/shard_map/ppermute | solution.py:18
  6.3 0.2 broadcast.11.clone
  6.5 0.2 broadcast.11.clone.1
  6.7 0.6 copy-done.6
  7.3 2.3 %collective-permute-start.3 = (bf16[320,512]{1,0:T(8,128)(2,1)S(1)}, bf16[320,512]{1,0:T(8,128)(2,1)S(1)}, u32[]{:S(2)}, u32[]{:S(2)}) collective-permute-start(bf16[320,512]{1,0:T(8,128)(2,1)S(1)} %copy-done.6), channel_id=1, source_target_pairs={{0,16},{4,20},{8,24},{12,28},{16,0},{20,4},{24,8},{28,12},{1,17},{... | collective-permute-start | bytes 983048 | tf_op jit(solution)/shard_map/ppermute | solution.py:18
  9.7 1.0 constant_dynamic-update-slice_fusion.6
  10.7 4.1 %collective-permute-done.1 = bf16[320,512]{1,0:T(8,128)(2,1)} collective-permute-done((bf16[320,512]{1,0:T(8,128)(2,1)}, bf16[320,512]{1,0:T(8,128)(2,1)}, u32[]{:S(2)}, u32[]{:S(2)}) %collective-permute-start.1) | collective-permute-done | bytes 327712 | tf_op jit(solution)/shard_map/ppermute | solution.py:18
  14.8 8.9 %collective-permute-start.12 = (bf16[320,512]{1,0:T(8,128)(2,1)S(1)}, bf16[320,512]{1,0:T(8,128)(2,1)S(1)}, u32[]{:S(2)}, u32[]{:S(2)}) collective-permute-start(bf16[320,512]{1,0:T(8,128)(2,1)S(1)} %copy-done.7), channel_id=1, source_target_pairs={{0,24},{4,28},{8,0},{12,4},{16,8},{20,12},{24,16},{28,20},{1,25},{... | collective-permute-start | bytes 983048 | tf_op jit(solution)/shard_map/ppermute | solution.py:18
  23.7 5.2 %collective-permute-done.8 = bf16[320,512]{1,0:T(8,128)(2,1)} collective-permute-done((bf16[320,512]{1,0:T(8,128)(2,1)}, bf16[320,512]{1,0:T(8,128)(2,1)}, u32[]{:S(2)}, u32[]{:S(2)}) %collective-permute-start.8) | collective-permute-done | bytes 327712 | tf_op jit(solution)/shard_map/ppermute | solution.py:18
  28.9 1.0 constant_dynamic-update-slice_fusion.5
  29.9 1.0 constant_dynamic-update-slice_fusion.14
  30.9 0.6 collective-permute-start.2
  31.5 1.0 constant_dynamic-update-slice_fusion.13
  32.5 10.3 %collective-permute-done.3 = bf16[320,512]{1,0:T(8,128)(2,1)S(1)} collective-permute-done((bf16[320,512]{1,0:T(8,128)(2,1)S(1)}, bf16[320,512]{1,0:T(8,128)(2,1)S(1)}, u32[]{:S(2)}, u32[]{:S(2)}) %collective-permute-start.3) | collective-permute-done | bytes 327712 | tf_op jit(solution)/shard_map/ppermute | solution.py:18
  42.8 0.5 collective-permute-start.4
  43.3 20.2 %collective-permute-done.10 = bf16[320,512]{1,0:T(8,128)(2,1)S(1)} collective-permute-done((bf16[320,512]{1,0:T(8,128)(2,1)S(1)}, bf16[320,512]{1,0:T(8,128)(2,1)S(1)}, u32[]{:S(2)}, u32[]{:S(2)}) %collective-permute-start.10) | collective-permute-done | bytes 327712 | tf_op jit(solution)/shard_map/ppermute | solution.py:18
  63.5 0.0 collective-permute-start.13
  63.6 0.5 collective-permute-start.11
  64.2 1.4 collective-permute-done.11
  65.8 0.1 constant_dynamic-update-slice_fusion
  65.9 1.5 copy-done.4
  67.4 2.4 %fusion.5 = bf16[512,512]{0,1:T(8,128)(2,1)} fusion(bf16[2560,512]{1,0:T(8,128)(2,1)S(1)} %get-tuple-element.14, bf16[512,2560]{1,0:T(8,128)(2,1)S(1)} %bitcast.93), kind=kOutput, calls=%fused_computation.17 | convolution fusion | flops 1342439424 | bytes 5767168 | tf_op jit(solution)/shard_map/dot_general | solution.py:73
  69.7 1.2 reshape.50
  70.9 2.2 %fusion.7 = bf16[4,128,8,64]{1,3,2,0:T(8,128)(2,1)S(1)} fusion(bf16[4,8,128,128]{3,2,1,0:T(8,128)(2,1)} %bitcast.101, bf16[4,128,8,64]{1,0,3,2:T(4,128)(2,1)S(1)} %reshape.50), kind=kOutput, calls=%fused_computation.19 | convolution fusion | flops 67371008 | bytes 2097152 | tf_op jit(solution)/shard_map/ihqk,ikhd->iqhd/dot_general | solution.py:75
  73.1 0.4 copy.15
  73.5 4.1 %fusion.6 = bf16[512,512]{0,1:T(8,128)(2,1)} fusion(bf16[2560,512]{1,0:T(8,128)(2,1)} %copy-done.4, bf16[512,2560]{1,0:T(8,128)(2,1)S(1)} %bitcast.103), kind=kOutput, calls=%fused_computation.18 | convolution fusion | flops 1342439424 | bytes 5767168 | tf_op jit(solution)/shard_map/dot_general | solution.py:89
  77.7 2.0 %reshape.56 = bf16[4,128,8,64]{1,0,3,2:T(4,128)(2,1)} reshape(bf16[512,512]{0,1:T(8,128)(2,1)} %fusion.6) | data formatting | bytes 1048576 | tf_op jit(solution)/shard_map/reshape | solution.py:94
  79.6 1.8 fusion.8
  81.4 0.4 copy.21
  81.8 3.9 %convolution_bitcast_fusion.1 = f32[2560,512]{0,1:T(8,128)} fusion(bf16[512,2560]{1,0:T(8,128)(2,1)S(1)} %bitcast.94, bf16[64,8,4,128]{3,2,1,0:T(4,128)(2,1)S(1)} %bitcast.107), kind=kOutput, calls=%fused_computation.1 | convolution fusion | flops 1342177280 | bytes 8388608 | tf_op jit(solution)/shard_map/dot_general | solution.py:100
  85.7 5.9 %copy.22 = f32[2560,512]{1,0:T(8,128)} copy(f32[2560,512]{0,1:T(8,128)} %convolution_bitcast_fusion.1) | data formatting | bytes 10485760 | tf_op jit(solution)/shard_map/dot_general | solution.py:100
  91.7 3.1 %fusion = bf16[4,320,512]{2,1,0:T(8,128)(2,1)} fusion(f32[4,2,320,512]{3,2,1,0:T(8,128)} %bitcast.99, s32[]{:T(128)S(6)} %select_n.90), kind=kLoop, calls=%fused_computation.7 | loop fusion | bytes 2621444 | tf_op jit(solution)/shard_map/convert_element_type | solution.py:39
  94.8 0.1 collective-permute-start.17
  94.9 3.8 %convolution_bitcast_fusion = f32[2560,512]{0,1:T(8,128)} fusion(bf16[512,2560]{1,0:T(8,128)(2,1)S(1)} %bitcast.104, bf16[64,8,4,128]{3,2,1,0:T(4,128)(2,1)S(1)} %bitcast.105), kind=kOutput, calls=%fused_computation | convolution fusion | flops 1342177280 | bytes 8388608 | tf_op jit(solution)/shard_map/dot_general | solution.py:84
  98.8 6.0 %copy.23 = f32[2560,512]{1,0:T(8,128)} copy(f32[2560,512]{0,1:T(8,128)} %convolution_bitcast_fusion) | data formatting | bytes 10485760 | tf_op jit(solution)/shard_map/dot_general | solution.py:84
  104.7 3.1 %fusion.1 = bf16[4,320,512]{2,1,0:T(8,128)(2,1)} fusion(f32[4,2,320,512]{3,2,1,0:T(8,128)} %bitcast.95, s32[]{:T(128)S(6)} %select_n.90), kind=kLoop, calls=%fused_computation.8 | loop fusion | bytes 2621444 | tf_op jit(solution)/shard_map/convert_element_type | solution.py:39
  107.9 0.4 collective-permute-start.21
  108.2 3.2 %convolution_convert_fusion = bf16[512,2560]{1,0:T(8,128)(2,1)} fusion(bf16[2560,512]{1,0:T(8,128)(2,1)S(1)} %copy-done.5, bf16[64,8,4,128]{3,2,1,0:T(4,128)(2,1)S(1)} %bitcast.106), kind=kOutput, calls=%fused_computation.2 | convolution fusion | flops 1343488000 | bytes 5767168 | tf_op jit(solution)/shard_map/dot_general | solution.py:105
  111.4 4.5 %reshape.53 = bf16[512,4,640]{2,1,0:T(4,128)(2,1)S(1)} reshape(bf16[512,2560]{1,0:T(8,128)(2,1)} %convolution_convert_fusion) | data formatting | bytes 5242880 | tf_op jit(solution)/shard_map/reshape | solution.py:48
  115.9 5.5 %constant_dynamic-slice_fusion.3 = (bf16[512,1,640]{2,1,0:T(2,128)(2,1)S(1)}, bf16[512,1,640]{2,1,0:T(2,128)(2,1)S(1)}, bf16[512,1,640]{2,1,0:T(2,128)(2,1)S(1)}, bf16[512,1,640]{2,1,0:T(2,128)(2,1)S(1)}) fusion(bf16[512,4,640]{2,1,0:T(4,128)(2,1)S(1)} %reshape.53, s32[]{:T(128)S(6)} %select_n.85, s32[]{:T(128)S(6)} %select_n.87, s32[]{:T(128)S(6)} %select_n.86, ...), kind=kLoop, calls=%fused_computation.54 | loop fusion | bytes 5242896 | tf_op jit(solution)/shard_map/jit(dynamic_index_in_dim)/dynamic_slice | solution.py:49
  121.4 0.1 copy.53
  121.5 0.1 copy.54
  121.6 0.1 copy.52
  121.7 2.5 %collective-permute-start.16 = (bf16[512,640]{1,0:T(8,128)(2,1)S(1)}, bf16[512,640]{1,0:T(8,128)(2,1)S(1)}, u32[]{:S(2)}, u32[]{:S(2)}) collective-permute-start(bf16[512,640]{1,0:T(8,128)(2,1)S(1)} %bitcast.110), channel_id=1, source_target_pairs={{0,3},{1,2},{2,1},{3,0},{4,7},{5,6},{6,5},{7,4},{8,11},{9,10},{10,... | collective-permute-start | bytes 1966088 | tf_op jit(solution)/shard_map/ppermute | solution.py:53
  124.2 0.5 collective-permute-start.14
  124.8 0.5 collective-permute-start.15
  125.3 2.6 %bitcast_add_fusion.1 = f32[4,320,512]{2,1,0:T(8,128)S(1)} fusion(bf16[4,320,512]{2,1,0:T(8,128)(2,1)} %collective-permute-done.17, f32[4,2,320,512]{3,2,1,0:T(8,128)} %bitcast.100, s32[]{:T(128)S(6)} %select_n.89), kind=kLoop, calls=%fused_computation.4 | loop fusion | flops 1310720 | bytes 6553604 | tf_op jit(solution)/shard_map/add | solution.py:39
  127.9 0.1 fusion.21
  128.0 0.1 collective-permute-start.18
  128.1 3.8 %collective-permute-start.20 = (bf16[320,512]{1,0:T(8,128)(2,1)S(1)}, bf16[320,512]{1,0:T(8,128)(2,1)S(1)}, u32[]{:S(2)}, u32[]{:S(2)}) collective-permute-start(bf16[320,512]{1,0:T(8,128)(2,1)S(1)} %get-tuple-element.7), channel_id=1, source_target_pairs={{0,24},{4,28},{8,0},{12,4},{16,8},{20,12},{24,16},{28,20},{1,25},{... | collective-permute-start | bytes 983048 | tf_op jit(solution)/shard_map/ppermute | solution.py:18
  131.9 1.8 bitcast_add_fusion
  133.8 6.6 %collective-permute-done.16 = bf16[512,640]{1,0:T(8,128)(2,1)S(1)} collective-permute-done((bf16[512,640]{1,0:T(8,128)(2,1)S(1)}, bf16[512,640]{1,0:T(8,128)(2,1)S(1)}, u32[]{:S(2)}, u32[]{:S(2)}) %collective-permute-start.16) | collective-permute-done | bytes 655392 | tf_op jit(solution)/shard_map/ppermute | solution.py:53
  140.3 0.1 fusion.24
  140.5 13.2 %collective-permute-done.14 = bf16[512,640]{1,0:T(8,128)(2,1)S(1)} collective-permute-done((bf16[512,640]{1,0:T(8,128)(2,1)S(1)}, bf16[512,640]{1,0:T(8,128)(2,1)S(1)}, u32[]{:S(2)}, u32[]{:S(2)}) %collective-permute-start.14) | collective-permute-done | bytes 655392 | tf_op jit(solution)/shard_map/ppermute | solution.py:53
  153.6 3.8 %collective-permute-start.24 = (bf16[320,512]{1,0:T(8,128)(2,1)S(1)}, bf16[320,512]{1,0:T(8,128)(2,1)S(1)}, u32[]{:S(2)}, u32[]{:S(2)}) collective-permute-start(bf16[320,512]{1,0:T(8,128)(2,1)S(1)} %get-tuple-element.4), channel_id=1, source_target_pairs={{0,24},{4,28},{8,0},{12,4},{16,8},{20,12},{24,16},{28,20},{1,25},{... | collective-permute-start | bytes 983048 | tf_op jit(solution)/shard_map/ppermute | solution.py:18
  157.5 1.1 fusion.4
  158.6 8.4 %collective-permute-done.19 = bf16[320,512]{1,0:T(8,128)(2,1)S(1)} collective-permute-done((bf16[320,512]{1,0:T(8,128)(2,1)S(1)}, bf16[320,512]{1,0:T(8,128)(2,1)S(1)}, u32[]{:S(2)}, u32[]{:S(2)}) %collective-permute-start.19) | collective-permute-done | bytes 327712 | tf_op jit(solution)/shard_map/ppermute | solution.py:18
  167.0 1.0 fusion.12
  168.0 4.6 %collective-permute-done.24 = bf16[320,512]{1,0:T(8,128)(2,1)S(1)} collective-permute-done((bf16[320,512]{1,0:T(8,128)(2,1)S(1)}, bf16[320,512]{1,0:T(8,128)(2,1)S(1)}, u32[]{:S(2)}, u32[]{:S(2)}) %collective-permute-start.24) | collective-permute-done | bytes 327712 | tf_op jit(solution)/shard_map/ppermute | solution.py:18
  172.6 13.8 %collective-permute-done.23 = bf16[320,512]{1,0:T(8,128)(2,1)S(1)} collective-permute-done((bf16[320,512]{1,0:T(8,128)(2,1)S(1)}, bf16[320,512]{1,0:T(8,128)(2,1)S(1)}, u32[]{:S(2)}, u32[]{:S(2)}) %collective-permute-start.23) | collective-permute-done | bytes 327712 | tf_op jit(solution)/shard_map/ppermute | solution.py:18
  186.4 1.0 fusion.10
  (51 shorter events, 0.4 us)
Async XLA Ops:
  0.6 66.7 %copy-start = (bf16[2,2,128,2560]{3,2,1,0:T(8,128)(2,1)S(1)}, bf16[2,2,128,2560]{3,2,1,0:T(8,128)(2,1)}, u32[]{:S(2)}) copy-start(bf16[2,2,128,2560]{3,2,1,0:T(8,128)(2,1)} %param.5) | copy-start | bytes 7864324
  0.6 5.8 %copy-start.7 = (bf16[320,512]{1,0:T(8,128)(2,1)S(1)}, bf16[320,512]{1,0:T(8,128)(2,1)}, u32[]{:S(2)}) copy-start(bf16[320,512]{1,0:T(8,128)(2,1)} %param.9) | copy-start | bytes 983044
  0.7 6.7 %collective-permute-start.7 = (bf16[320,512]{1,0:T(8,128)(2,1)}, bf16[320,512]{1,0:T(8,128)(2,1)}, u32[]{:S(2)}, u32[]{:S(2)}) collective-permute-start(bf16[320,512]{1,0:T(8,128)(2,1)} %param.9), channel_id=1, source_target_pairs={{0,4},{4,0},{8,12},{12,8},{16,20},{20,16},{24,28},{28,24},{1,5},{5... | collective-permute-start | bytes 983048 | tf_op jit(solution)/shard_map/ppermute | solution.py:21
  1.2 13.6 %collective-permute-start.1 = (bf16[320,512]{1,0:T(8,128)(2,1)}, bf16[320,512]{1,0:T(8,128)(2,1)}, u32[]{:S(2)}, u32[]{:S(2)}) collective-permute-start(bf16[320,512]{1,0:T(8,128)(2,1)} %param.8), channel_id=1, source_target_pairs={{0,8},{4,12},{8,16},{12,20},{16,24},{20,28},{24,0},{28,4},{1,9},{5... | collective-permute-start | bytes 983048 | tf_op jit(solution)/shard_map/ppermute | solution.py:18
  3.8 19.9 %collective-permute-start = (bf16[320,512]{1,0:T(8,128)(2,1)}, bf16[320,512]{1,0:T(8,128)(2,1)}, u32[]{:S(2)}, u32[]{:S(2)}) collective-permute-start(bf16[320,512]{1,0:T(8,128)(2,1)} %param.8), channel_id=1, source_target_pairs={{0,4},{4,0},{8,12},{12,8},{16,20},{20,16},{24,28},{28,24},{1,5},{5... | collective-permute-start | bytes 983048 | tf_op jit(solution)/shard_map/ppermute | solution.py:21
  4.0 26.9 %collective-permute-start.5 = (bf16[320,512]{1,0:T(8,128)(2,1)}, bf16[320,512]{1,0:T(8,128)(2,1)S(1)}, u32[]{:S(2)}, u32[]{:S(2)}) collective-permute-start(bf16[320,512]{1,0:T(8,128)(2,1)} %param.8), channel_id=1, source_target_pairs={{0,24},{4,28},{8,0},{12,4},{16,8},{20,12},{24,16},{28,20},{1,25},{... | collective-permute-start | bytes 983048 | tf_op jit(solution)/shard_map/ppermute | solution.py:18
  6.3 22.6 %collective-permute-start.8 = (bf16[320,512]{1,0:T(8,128)(2,1)}, bf16[320,512]{1,0:T(8,128)(2,1)}, u32[]{:S(2)}, u32[]{:S(2)}) collective-permute-start(bf16[320,512]{1,0:T(8,128)(2,1)} %param.9), channel_id=1, source_target_pairs={{0,8},{4,12},{8,16},{12,20},{16,24},{20,28},{24,0},{28,4},{1,9},{5... | collective-permute-start | bytes 983048 | tf_op jit(solution)/shard_map/ppermute | solution.py:18
  6.3 1.0 copy-start.6
  7.3 35.4 %collective-permute-start.3 = (bf16[320,512]{1,0:T(8,128)(2,1)S(1)}, bf16[320,512]{1,0:T(8,128)(2,1)S(1)}, u32[]{:S(2)}, u32[]{:S(2)}) collective-permute-start(bf16[320,512]{1,0:T(8,128)(2,1)S(1)} %copy-done.6), channel_id=1, source_target_pairs={{0,16},{4,20},{8,24},{12,28},{16,0},{20,4},{24,8},{28,12},{1,17},{... | collective-permute-start | bytes 983048 | tf_op jit(solution)/shard_map/ppermute | solution.py:18
  14.8 28.0 %collective-permute-start.12 = (bf16[320,512]{1,0:T(8,128)(2,1)S(1)}, bf16[320,512]{1,0:T(8,128)(2,1)S(1)}, u32[]{:S(2)}, u32[]{:S(2)}) collective-permute-start(bf16[320,512]{1,0:T(8,128)(2,1)S(1)} %copy-done.7), channel_id=1, source_target_pairs={{0,24},{4,28},{8,0},{12,4},{16,8},{20,12},{24,16},{28,20},{1,25},{... | collective-permute-start | bytes 983048 | tf_op jit(solution)/shard_map/ppermute | solution.py:18
  23.7 39.8 %collective-permute-start.10 = (bf16[320,512]{1,0:T(8,128)(2,1)S(1)}, bf16[320,512]{1,0:T(8,128)(2,1)S(1)}, u32[]{:S(2)}, u32[]{:S(2)}) collective-permute-start(bf16[320,512]{1,0:T(8,128)(2,1)S(1)} %copy-done.7), channel_id=1, source_target_pairs={{0,16},{4,20},{8,24},{12,28},{16,0},{20,4},{24,8},{28,12},{1,17},{... | collective-permute-start | bytes 983048 | tf_op jit(solution)/shard_map/ppermute | solution.py:18
  28.9 34.6 %collective-permute-start.9 = (bf16[320,512]{1,0:T(8,128)(2,1)}, bf16[320,512]{1,0:T(8,128)(2,1)S(1)}, u32[]{:S(2)}, u32[]{:S(2)}) collective-permute-start(bf16[320,512]{1,0:T(8,128)(2,1)} %collective-permute-done.8), channel_id=1, source_target_pairs={{0,4},{4,0},{8,12},{12,8},{16,20},{20,16},{24,28},{28,24},{1,5},{5... | collective-permute-start | bytes 983048 | tf_op jit(solution)/shard_map/ppermute | solution.py:21
  30.9 33.2 %collective-permute-start.2 = (bf16[320,512]{1,0:T(8,128)(2,1)}, bf16[320,512]{1,0:T(8,128)(2,1)S(1)}, u32[]{:S(2)}, u32[]{:S(2)}) collective-permute-start(bf16[320,512]{1,0:T(8,128)(2,1)} %collective-permute-done.1), channel_id=1, source_target_pairs={{0,4},{4,0},{8,12},{12,8},{16,20},{20,16},{24,28},{28,24},{1,5},{5... | collective-permute-start | bytes 983048 | tf_op jit(solution)/shard_map/ppermute | solution.py:21
  42.8 23.0 %collective-permute-start.6 = (bf16[320,512]{1,0:T(8,128)(2,1)S(1)}, bf16[320,512]{1,0:T(8,128)(2,1)S(1)}, u32[]{:S(2)}, u32[]{:S(2)}) collective-permute-start(bf16[320,512]{1,0:T(8,128)(2,1)S(1)} %collective-permute-done.5), channel_id=1, source_target_pairs={{0,4},{4,0},{8,12},{12,8},{16,20},{20,16},{24,28},{28,24},{1,5},{5... | collective-permute-start | bytes 983048 | tf_op jit(solution)/shard_map/ppermute | solution.py:21
  42.8 22.9 %collective-permute-start.4 = (bf16[320,512]{1,0:T(8,128)(2,1)S(1)}, bf16[320,512]{1,0:T(8,128)(2,1)S(1)}, u32[]{:S(2)}, u32[]{:S(2)}) collective-permute-start(bf16[320,512]{1,0:T(8,128)(2,1)S(1)} %collective-permute-done.3), channel_id=1, source_target_pairs={{0,4},{4,0},{8,12},{12,8},{16,20},{20,16},{24,28},{28,24},{1,5},{5... | collective-permute-start | bytes 983048 | tf_op jit(solution)/shard_map/ppermute | solution.py:21
  63.5 2.3 %collective-permute-start.13 = (bf16[320,512]{1,0:T(8,128)(2,1)S(1)}, bf16[320,512]{1,0:T(8,128)(2,1)S(1)}, u32[]{:S(2)}, u32[]{:S(2)}) collective-permute-start(bf16[320,512]{1,0:T(8,128)(2,1)S(1)} %collective-permute-done.12), channel_id=1, source_target_pairs={{0,4},{4,0},{8,12},{12,8},{16,20},{20,16},{24,28},{28,24},{1,5},{5... | collective-permute-start | bytes 983048 | tf_op jit(solution)/shard_map/ppermute | solution.py:21
  63.6 2.1 %collective-permute-start.11 = (bf16[320,512]{1,0:T(8,128)(2,1)S(1)}, bf16[320,512]{1,0:T(8,128)(2,1)S(1)}, u32[]{:S(2)}, u32[]{:S(2)}) collective-permute-start(bf16[320,512]{1,0:T(8,128)(2,1)S(1)} %collective-permute-done.10), channel_id=1, source_target_pairs={{0,4},{4,0},{8,12},{12,8},{16,20},{20,16},{24,28},{28,24},{1,5},{5... | collective-permute-start | bytes 983048 | tf_op jit(solution)/shard_map/ppermute | solution.py:21
  65.8 1.5 copy-start.4
  70.9 2.6 %copy-start.2 = (bf16[2,2,128,2560]{3,2,1,0:T(8,128)(2,1)S(1)}, bf16[2,2,128,2560]{3,2,1,0:T(8,128)(2,1)}, u32[]{:S(2)}) copy-start(bf16[2,2,128,2560]{3,2,1,0:T(8,128)(2,1)} %param.7) | copy-start | bytes 7864324
  91.7 3.3 %copy-start.3 = (bf16[2,2,128,2560]{3,2,1,0:T(8,128)(2,1)S(1)}, bf16[2,2,128,2560]{3,2,1,0:T(8,128)(2,1)}, u32[]{:S(2)}) copy-start(bf16[2,2,128,2560]{3,2,1,0:T(8,128)(2,1)} %param.7) | copy-start | bytes 7864324
  94.8 30.5 %collective-permute-start.17 = (bf16[4,320,512]{2,1,0:T(8,128)(2,1)}, bf16[4,320,512]{2,1,0:T(8,128)(2,1)}, u32[]{:S(2)}, u32[]{:S(2)}) collective-permute-start(bf16[4,320,512]{2,1,0:T(8,128)(2,1)} %fusion), channel_id=1, source_target_pairs={{0,4},{4,0},{8,12},{12,8},{16,20},{20,16},{24,28},{28,24},{1,5},{5... | collective-permute-start | bytes 3932168 | tf_op jit(solution)/shard_map/ppermute | solution.py:21
  104.7 3.5 %copy-start.5 = (bf16[2560,512]{1,0:T(8,128)(2,1)S(1)}, bf16[2560,512]{1,0:T(8,128)(2,1)}, u32[]{:S(2)}) copy-start(bf16[2560,512]{1,0:T(8,128)(2,1)} %copy-done.4) | copy-start | bytes 7864324
  107.9 20.2 %collective-permute-start.21 = (bf16[4,320,512]{2,1,0:T(8,128)(2,1)}, bf16[4,320,512]{2,1,0:T(8,128)(2,1)}, u32[]{:S(2)}, u32[]{:S(2)}) collective-permute-start(bf16[4,320,512]{2,1,0:T(8,128)(2,1)} %fusion.1), channel_id=1, source_target_pairs={{0,4},{4,0},{8,12},{12,8},{16,20},{20,16},{24,28},{28,24},{1,5},{5... | collective-permute-start | bytes 3932168 | tf_op jit(solution)/shard_map/ppermute | solution.py:21
  121.6 10.3 %slice-start = ((s8[5242880]{0:T(1024)(128)(4,1)}), s8[4194304]{0:T(1024)(128)(4,1)S(1)}, s32[]{:S(2)}) async-start(s8[5242880]{0:T(1024)(128)(4,1)} %bitcast.96), calls=%async_computation | async-start | bytes 8388608
  121.7 18.6 %collective-permute-start.16 = (bf16[512,640]{1,0:T(8,128)(2,1)S(1)}, bf16[512,640]{1,0:T(8,128)(2,1)S(1)}, u32[]{:S(2)}, u32[]{:S(2)}) collective-permute-start(bf16[512,640]{1,0:T(8,128)(2,1)S(1)} %bitcast.110), channel_id=1, source_target_pairs={{0,3},{1,2},{2,1},{3,0},{4,7},{5,6},{6,5},{7,4},{8,11},{9,10},{10,... | collective-permute-start | bytes 1966088 | tf_op jit(solution)/shard_map/ppermute | solution.py:53
  124.2 29.4 %collective-permute-start.14 = (bf16[512,640]{1,0:T(8,128)(2,1)S(1)}, bf16[512,640]{1,0:T(8,128)(2,1)S(1)}, u32[]{:S(2)}, u32[]{:S(2)}) collective-permute-start(bf16[512,640]{1,0:T(8,128)(2,1)S(1)} %bitcast.109), channel_id=1, source_target_pairs={{0,1},{1,0},{2,3},{3,2},{4,5},{5,4},{6,7},{7,6},{8,9},{9,8},{10,11... | collective-permute-start | bytes 1966088 | tf_op jit(solution)/shard_map/ppermute | solution.py:53
  124.8 7.1 %slice-start.1 = ((s8[5242880]{0:T(1024)(128)(4,1)}), s8[1048576]{0:T(1024)(128)(4,1)S(1)}, s32[]{:S(2)}) async-start(s8[5242880]{0:T(1024)(128)(4,1)} %bitcast.96), calls=%async_computation.1 | async-start | bytes 2097152
  124.8 28.8 %collective-permute-start.15 = (bf16[512,640]{1,0:T(8,128)(2,1)S(1)}, bf16[512,640]{1,0:T(8,128)(2,1)S(1)}, u32[]{:S(2)}, u32[]{:S(2)}) collective-permute-start(bf16[512,640]{1,0:T(8,128)(2,1)S(1)} %bitcast.108), channel_id=1, source_target_pairs={{0,2},{1,3},{2,0},{3,1},{4,6},{5,7},{6,4},{7,5},{8,10},{9,11},{10,... | collective-permute-start | bytes 1966088 | tf_op jit(solution)/shard_map/ppermute | solution.py:53
  128.0 29.4 %collective-permute-start.18 = (bf16[320,512]{1,0:T(8,128)(2,1)S(1)}, bf16[320,512]{1,0:T(8,128)(2,1)S(1)}, u32[]{:S(2)}, u32[]{:S(2)}) collective-permute-start(bf16[320,512]{1,0:T(8,128)(2,1)S(1)} %get-tuple-element.6), channel_id=1, source_target_pairs={{0,8},{4,12},{8,16},{12,20},{16,24},{20,28},{24,0},{28,4},{1,9},{5... | collective-permute-start | bytes 983048 | tf_op jit(solution)/shard_map/ppermute | solution.py:18
  128.1 30.5 %collective-permute-start.20 = (bf16[320,512]{1,0:T(8,128)(2,1)S(1)}, bf16[320,512]{1,0:T(8,128)(2,1)S(1)}, u32[]{:S(2)}, u32[]{:S(2)}) collective-permute-start(bf16[320,512]{1,0:T(8,128)(2,1)S(1)} %get-tuple-element.7), channel_id=1, source_target_pairs={{0,24},{4,28},{8,0},{12,4},{16,8},{20,12},{24,16},{28,20},{1,25},{... | collective-permute-start | bytes 983048 | tf_op jit(solution)/shard_map/ppermute | solution.py:18
  140.3 26.7 %collective-permute-start.19 = (bf16[320,512]{1,0:T(8,128)(2,1)S(1)}, bf16[320,512]{1,0:T(8,128)(2,1)S(1)}, u32[]{:S(2)}, u32[]{:S(2)}) collective-permute-start(bf16[320,512]{1,0:T(8,128)(2,1)S(1)} %get-tuple-element.8), channel_id=1, source_target_pairs={{0,16},{4,20},{8,24},{12,28},{16,0},{20,4},{24,8},{28,12},{1,17},{... | collective-permute-start | bytes 983048 | tf_op jit(solution)/shard_map/ppermute | solution.py:18
  153.6 14.4 %collective-permute-start.22 = (bf16[320,512]{1,0:T(8,128)(2,1)S(1)}, bf16[320,512]{1,0:T(8,128)(2,1)S(1)}, u32[]{:S(2)}, u32[]{:S(2)}) collective-permute-start(bf16[320,512]{1,0:T(8,128)(2,1)S(1)} %get-tuple-element.3), channel_id=1, source_target_pairs={{0,8},{4,12},{8,16},{12,20},{16,24},{20,28},{24,0},{28,4},{1,9},{5... | collective-permute-start | bytes 983048 | tf_op jit(solution)/shard_map/ppermute | solution.py:18
  153.6 19.0 %collective-permute-start.24 = (bf16[320,512]{1,0:T(8,128)(2,1)S(1)}, bf16[320,512]{1,0:T(8,128)(2,1)S(1)}, u32[]{:S(2)}, u32[]{:S(2)}) collective-permute-start(bf16[320,512]{1,0:T(8,128)(2,1)S(1)} %get-tuple-element.4), channel_id=1, source_target_pairs={{0,24},{4,28},{8,0},{12,4},{16,8},{20,12},{24,16},{28,20},{1,25},{... | collective-permute-start | bytes 983048 | tf_op jit(solution)/shard_map/ppermute | solution.py:18
  157.4 29.0 %collective-permute-start.23 = (bf16[320,512]{1,0:T(8,128)(2,1)S(1)}, bf16[320,512]{1,0:T(8,128)(2,1)S(1)}, u32[]{:S(2)}, u32[]{:S(2)}) collective-permute-start(bf16[320,512]{1,0:T(8,128)(2,1)S(1)} %get-tuple-element.5), channel_id=1, source_target_pairs={{0,16},{4,20},{8,24},{12,28},{16,0},{20,4},{24,8},{28,12},{1,17},{... | collective-permute-start | bytes 983048 | tf_op jit(solution)/shard_map/ppermute | solution.py:18
  157.5 30.0 %copy-start.1 = (bf16[2,2,128,2560]{3,2,1,0:T(8,128)(2,1)S(1)}, bf16[2,2,128,2560]{3,2,1,0:T(8,128)(2,1)}, u32[]{:S(2)}) copy-start(bf16[2,2,128,2560]{3,2,1,0:T(8,128)(2,1)} %param.5) | copy-start | bytes 7864324

commit v2 on v0

v2 whole, which is shorter than its diff:
```python
import functools

import jax
import jax.numpy as jnp
from jax import lax
from jax.experimental import pallas as pl
from jax.experimental.pallas import tpu as pltpu
from jax.sharding import PartitionSpec as P

HEAD_DIM = 64
F32 = jnp.float32
BF16 = jnp.bfloat16
VMEM_LIMIT = 40 * 1024 * 1024


def dot(a, b, ca=1, cb=0):
    return lax.dot_general(a, b, (((ca,), (cb,)), ((), ())), preferred_element_type=F32)


def begin(pairs, sems):
    copies = [pltpu.make_async_copy(s, d, sems.at[i]) for i, (s, d) in enumerate(pairs)]
    for copy in copies:
        copy.start()
    return copies


def rows_at(index, size):
    return pl.ds(pl.multiple_of(index * size, 16), size)


def gradient_rows(left, right_ref, rows_ref, step):
    width = right_ref.shape[1]
    for start in range(0, width, step):
        part = dot(left, right_ref[:, start : start + step])
        rows_ref[start : start + step, :] = part.T.astype(BF16)


def head_pairs(heads):
    return [(h, min(2, heads - h)) for h in range(0, heads, 2)]


def backward_kernel(n_slots, idx, cot_o, cot_s, mix_o, mix_s, act_o, act_s, *rest):
    slots, rest = rest[:n_slots], rest[n_slots:]
    w_out, rest = rest[0], rest[1:]
    outs, (cot_v, act_v, mix_v, left_v, grad_v, sems) = rest[:-6], rest[-6:]
    tokens, cols = cot_o.shape[0], w_out.shape[1]
    groups, _, seq, _ = mix_o.shape
    heads = mix_v.shape[2]
    depth = slots[0].shape[0]
    here = pl.ds(idx[0], heads)
    copies = begin(
        [(cot_o, cot_v.at[0]), (mix_o.at[:, here], mix_v.at[0])]
        + [(cot_s, cot_v.at[1]), (mix_s.at[:, here], mix_v.at[1])]
        + [(act_o, act_v.at[pl.ds(0, tokens)]), (act_s, act_v.at[pl.ds(tokens, tokens)])],
        sems,
    )
    for j in range(n_slots):
        w_out[rows_at(idx[1 + j], depth), :] = slots[j][...]
    for half in range(2):
        copies[2 * half].wait()
        d_mixed = dot(cot_v[half], w_out[...])
        copies[2 * half + 1].wait()
        for g in range(groups):
            turned = d_mixed[g * seq : (g + 1) * seq, :].T.astype(BF16)
            at = (half * groups + g) * seq
            for h, n in head_pairs(heads):
                part = turned[h * HEAD_DIM : (h + n) * HEAD_DIM, :]
                if n == 2:
                    row = lax.broadcasted_iota(jnp.int32, part.shape, 0)
                    zero = jnp.zeros_like(part)
                    part = jnp.concatenate(
                        [
                            jnp.where(row < HEAD_DIM, part, zero),
                            jnp.where(row < HEAD_DIM, zero, part),
                        ],
                        axis=1,
                    )
                weights = mix_v[half, g, h : h + n].reshape(n * seq, seq)
                left_v[h * HEAD_DIM : (h + n) * HEAD_DIM, at : at + seq] = dot(
                    part, weights
                ).astype(BF16)
    copies[4].wait()
    copies[5].wait()
    gradient_rows(left_v[...], act_v, grad_v, 640)
    for i, out in enumerate(outs):
        out[...] = grad_v[rows_at(idx[1 + n_slots + i], depth), :]


def mixed_kernel(n_slots, idx, act_o, act_s, mix_o, mix_s, *rest):
    slots, (mixed_o, mixed_s, w_v, act_v, mix_v, sems) = rest[:n_slots], rest[n_slots:]
    groups, _, seq, _ = mix_o.shape
    heads = mix_v.shape[2]
    depth = slots[0].shape[0]
    here = pl.ds(idx[0], heads)
    copies = begin(
        [(act_o, act_v.at[0]), (mix_o.at[:, here], mix_v.at[0])]
        + [(act_s, act_v.at[1]), (mix_s.at[:, here], mix_v.at[1])],
        sems,
    )
    for j in range(n_slots):
        w_v[rows_at(idx[1 + j], depth), :] = slots[j][...]
    for half, out in enumerate((mixed_o, mixed_s)):
        copies[2 * half].wait()
        value = dot(act_v[half], w_v[...]).astype(BF16)
        copies[2 * half + 1].wait()
        for g in range(groups):
            for h, n in head_pairs(heads):
                part = value[g * seq : (g + 1) * seq, h * HEAD_DIM : (h + n) * HEAD_DIM]
                weights = mix_v[half, g, h]
                if n == 2:
                    lane = lax.broadcasted_iota(jnp.int32, part.shape, 1)
                    zero = jnp.zeros_like(part)
                    part = jnp.concatenate(
                        [
                            jnp.where(lane < HEAD_DIM, part, zero),
                            jnp.where(lane < HEAD_DIM, zero, part),
                        ],
                        axis=0,
                    )
                    weights = jnp.concatenate([weights, mix_v[half, g, h + 1]], axis=1)
                out[g * seq : (g + 1) * seq, h * HEAD_DIM : (h + n) * HEAD_DIM] = dot(
                    weights, part
                ).astype(BF16)


def grad_out_kernel(idx, cot_o, cot_s, mixed_o, mixed_s, *rest):
    outs, (cot_v, left_v, grad_v, sems) = rest[:-4], rest[-4:]
    tokens, _ = cot_o.shape
    depth = outs[0].shape[0]
    copies = begin(
        [(cot_o, cot_v.at[pl.ds(0, tokens)]), (cot_s, cot_v.at[pl.ds(tokens, tokens)])], sems
    )
    left_v[:, :tokens] = mixed_o[...].astype(F32).T.astype(BF16)
    left_v[:, tokens:] = mixed_s[...].astype(F32).T.astype(BF16)
    copies[0].wait()
    copies[1].wait()
    gradient_rows(left_v[...], cot_v, grad_v, 640)
    for i, out in enumerate(outs):
        out[...] = grad_v[rows_at(idx[i], depth), :]


def terms_kernel(n_node, idx, mixed_o, mixed_r, w_o, w_r, *outs):
    depth = w_o.shape[0] // n_node
    half = mixed_o.shape[0] // 2
    for j in range(n_node):
        rows = rows_at(idx[j], depth)
        term = dot(mixed_o[...], w_o[rows, :], 1, 1) + dot(mixed_r[...], w_r[rows, :], 1, 1)
        term = term.astype(BF16)
        if n_node != 4:
            outs[j][...] = term
            continue
        along_x, along_y, kept = outs
        first, second = term[:half], term[half:]
        if j == 0:
            kept[0], kept[2] = first, second
        elif j == 1:
            along_x[0], kept[3] = first, second
        elif j == 2:
            kept[1], along_y[0] = first, second
        else:
            along_x[1], along_y[1] = first, second


ANY = pl.BlockSpec(memory_space=pl.ANY)
SMEM = pl.BlockSpec(memory_space=pltpu.SMEM)
VMEM = pl.BlockSpec(memory_space=pltpu.VMEM)


def call(kernel, name, in_specs, out_shapes, scratch, flops):
    return pl.pallas_call(
        kernel,
        name=name,
        in_specs=in_specs,
        out_specs=[VMEM] * len(out_shapes),
        out_shape=[jax.ShapeDtypeStruct(s, BF16) for s in out_shapes],
        scratch_shapes=scratch,
        compiler_params=pltpu.CompilerParams(vmem_limit_bytes=VMEM_LIMIT),
        cost_estimate=pl.CostEstimate(flops=flops, bytes_accessed=12 << 20, transcendentals=0),
    )


def after(x, *others):
    return lax.optimization_barrier((x, *others))[0]


def make_body(n_wide, n_node):
    planes = n_wide // 2
    line4 = planes == 4

    def move(x, pairs):
        return lax.ppermute(
            x, "wide", [(2 * s + c, 2 * d + c) for s, d in pairs for c in range(2)]
        )

    def sibling(x):
        return lax.ppermute(x, "wide", [(i, i ^ 1) for i in range(n_wide)])

    def flip(x, j):
        return lax.ppermute(x, "node", [(i, i ^ j) for i in range(n_node)])

    def column_half(w, c):
        cols = w.shape[1] // 2
        mine = lax.dynamic_slice_in_dim(w, c * cols, cols, 1)
        got = sibling(lax.dynamic_slice_in_dim(w, (1 - c) * cols, cols, 1))
        low = jnp.where(c == 0, mine, got)
        high = jnp.where(c == 0, got, mine)
        return jnp.concatenate([low, high], axis=0)

    def gather_first(u):
        if not line4:
            return None
        across = move(u, [(0, 2), (1, 3), (2, 0), (3, 1)])
        ends = move(u, [(1, 0), (2, 3)])
        return across, ends

    def gather_rest(u, firsts, z):
        if not line4:
            return [u] + [
                move(u, [(s, (s - j) % planes) for s in range(planes)])
                for j in range(1, planes)
            ]
        across, ends = firsts
        up = move(jnp.where(z == 2, across, u), [(0, 1), (1, 2), (2, 3)])
        down = move(jnp.where(z == 1, across, u), [(3, 2), (2, 1), (1, 0)])
        after_z = jnp.where(z == 0, ends, jnp.where(z == 3, up, down))
        before_z = jnp.where(z == 0, down, jnp.where(z == 3, ends, up))
        return [u, after_z, across, before_z]

    def send_planes(z):
        if not line4:
            return [lax.rem(z + j, planes) for j in range(planes)]
        up = jnp.where(z == 0, 3, jnp.minimum(z + 1, 3))
        down = jnp.where(z == 3, 0, jnp.maximum(z - 1, 0))
        near = jnp.where(z == 0, 1, jnp.where(z == 3, 2, z))
        return [z, up, down, near, lax.rem(z + 2, 4)]

    def scatter(blocks, z):
        if not line4:
            total = blocks[0].astype(F32)
            for j in range(1, planes):
                got = move(blocks[j], [(s, (s + j) % planes) for s in range(planes)])
                total = total + got.astype(F32)
            return total
        own, up, down, near, far = blocks
        up = move(up, [(0, 1), (1, 2), (2, 3)])
        down = move(down, [(3, 2), (2, 1), (1, 0)])
        near = move(near, [(0, 1), (3, 2)])
        add = jnp.where(z == 1, up, jnp.where(z == 2, down, jnp.zeros_like(up)))
        far = move(
            (far.astype(F32) + add.astype(F32)).astype(BF16),
            [(0, 2), (1, 3), (2, 0), (3, 1)],
        )
        total = own.astype(F32) + jnp.where(z <= 1, down, up).astype(F32)
        return total + near.astype(F32) + far.astype(F32)

    def finish(total, c):
        rows = total.shape[0] // 2
        mine = lax.dynamic_slice_in_dim(total, c * rows, rows, 0)
        got = sibling(lax.dynamic_slice_in_dim(total, (1 - c) * rows, rows, 0))
        low = jnp.where(c == 0, mine, got)
        high = jnp.where(c == 0, got, mine)
        return jnp.concatenate([low, high], axis=1)

    def body(act_in, mixing, cotangent, w_value, w_out):
        wide = lax.axis_index("wide")
        n = lax.axis_index("node")
        z, c = wide // 2, lax.rem(wide, 2)
        micro, images, seq, width = act_in.shape
        groups = micro * images
        tokens = groups * seq
        cols = w_value.shape[1] // 2
        heads = cols // HEAD_DIM
        depth = width // planes
        act = act_in.reshape(tokens, width)
        cot = cotangent.reshape(tokens, width)
        mix = mixing.reshape(groups, 2 * heads, seq, seq)
        flops = 4 * tokens * width * cols

        u_out = column_half(w_out, c)
        u_value = column_half(w_value, c)
        out_first = gather_first(u_out)
        cot_s = sibling(after(cot, u_out))
        mix_s = sibling(after(mix, u_out))
        act_s = sibling(after(act, u_out))
        out_slots = gather_rest(u_out, out_first, z)
        if line4:
            u_value = after(u_value, out_first[0])
        value_first = gather_first(u_value)
        value_slots = gather_rest(u_value, value_first, z)

        slot_planes = [lax.rem(z + j, planes) for j in range(planes)]
        sends = send_planes(z)
        first_head = c * heads
        idx_back = jnp.stack([first_head, *slot_planes, *sends]).astype(jnp.int32)
        idx_mixed = jnp.stack([first_head, *slot_planes]).astype(jnp.int32)
        idx_send = jnp.stack(sends).astype(jnp.int32)
        idx_node = jnp.stack([lax.bitwise_xor(n, jnp.int32(j)) for j in range(n_node)])

        mix_scratch = pltpu.VMEM((2, groups, heads, seq, seq), BF16)
        both = pltpu.VMEM((2 * tokens, width), BF16)
        halves = pltpu.VMEM((2, tokens, width), BF16)
        left = pltpu.VMEM((cols, 2 * tokens), BF16)
        rows = pltpu.VMEM((width, cols), BF16)
        send_shapes = [(depth, cols)] * len(sends)

        w_full, *back_sends = call(
            functools.partial(backward_kernel, planes),
            "backward",
            [SMEM] + [ANY] * 6 + [VMEM] * planes,
            [(width, cols)] + send_shapes,
            [halves, both, mix_scratch, left, rows, pltpu.SemaphoreType.DMA((6,))],
            2 * flops,
        )(idx_back, cot, cot_s, mix, mix_s, act, act_s, *out_slots)
        w_full_s = sibling(w_full)
        grad_value = scatter(back_sends, z)

        mixed_o, mixed_s = call(
            functools.partial(mixed_kernel, planes),
            "mixed",
            [SMEM] + [ANY] * 4 + [VMEM] * planes,
            [(tokens, cols)] * 2,
            [rows, halves, mix_scratch, pltpu.SemaphoreType.DMA((4,))],
            flops,
        )(idx_mixed, act, act_s, mix, mix_s, *value_slots)
        mixed_r = sibling(mixed_s)
        out_sends = call(
            grad_out_kernel,
            "grad_out",
            [SMEM] + [ANY] * 2 + [VMEM] * 2,
            send_shapes,
            [both, left, rows, pltpu.SemaphoreType.DMA((2,))],
            flops,
        )(idx_send, cot, cot_s, mixed_o, mixed_s)
        grad_out = scatter(out_sends, z)

        part = width // n_node
        half = tokens // 2
        if n_node == 4:
            term_shapes = [(2, half, part), (2, half, part), (4, half, part)]
        else:
            term_shapes = [(tokens, part)] * n_node
        terms = call(
            functools.partial(terms_kernel, n_node),
            "terms",
            [SMEM] + [VMEM] * 4,
            term_shapes,
            [],
            flops,
        )(idx_node, mixed_o, mixed_r, w_full, w_full_s)
        if n_node == 4:
            along_x, along_y, kept = terms
            kept = kept.astype(F32)
            got_x = flip(along_x, 1).astype(F32)
            got_y = flip(along_y, 2).astype(F32)
            last_y = flip((kept[1] + got_x[1]).astype(BF16), 2)
            last_x = flip((kept[3] + got_y[1]).astype(BF16), 1)
            layer_out = jnp.concatenate(
                [
                    kept[0] + got_x[0] + last_y.astype(F32),
                    kept[2] + got_y[0] + last_x.astype(F32),
                ],
                axis=0,
            )
        else:
            layer_out = terms[0].astype(F32)
            for j in range(1, n_node):
                layer_out = layer_out + flip(terms[j], j).astype(F32)
        layer_out = layer_out.astype(BF16).reshape(micro, images, seq, part)
        return layer_out, finish(grad_value, c), finish(grad_out, c)

    return body


def solution(mesh):
    return jax.shard_map(
        make_body(mesh.shape["wide"], mesh.shape["node"]),
        mesh=mesh,
        in_specs=(
            P(None, "wide", None, None),
            P(None, "wide", "node", None, None),
            P(None, "wide", None, None),
            P("wide", "node"),
            P("wide", "node"),
        ),
        out_specs=(P(None, "wide", None, "node"), P("wide", "node"), P("wide", "node")),
        check_vma=False,
    )
```

time: 277 us -> 147 us (0.53)
  waiting for transfers between devices: 201 us -> 67.5 us
  starting transfers between devices: 0.24 us -> 44.4 us
  local copies, waits for them, and re-layouts: 32.2 us -> 4.31 us
  matrix products: 27.8 us -> 0 us
  Pallas kernels: 0 us -> 19.1 us
  between operations: 14.3 us -> 1.08 us
  other arithmetic: 0.91 us -> 10 us
    unnamed x10 -> x0, waiting for transfers between devices: 135 us -> none
    ppermute x0 -> x29, waiting for transfers between devices: none -> 67.5 us  [the longest x16 52.5 us: move(): lax.ppermute(x, 'wide', [(2 * s + c, 2 * d + c) for s, d in pairs for c i...]
    all_gather x2 -> x0, waiting for transfers between devices: 65.3 us -> none  [the longest x1 34.5 us: body(): lax.all_gather(w_value, 'wide', axis=0, tiled=True)]
    ppermute x0 -> x29, starting transfers between devices: none -> 44.4 us  [the longest x16 37.9 us: move(): lax.ppermute(x, 'wide', [(2 * s + c, 2 * d + c) for s, d in pairs for c i...]
    dot_general x14 -> x0, matrix products: 27.8 us -> none  [the longest x2 6.49 us: body(): jnp.dot(token_rows, full_value, preferred_element_type=jnp.float32)]
    pallas_call x0 -> x4, Pallas kernels: none -> 19.1 us  [the longest x1 6.98 us: body(): call(functools.partial(backward_kernel, planes), 'backward', [SMEM] + [AN...]
    unnamed x22 -> x14, local copies, waits for them, and re-layouts: 21 us -> 1.99 us
    slice x2 -> x0, local copies, waits for them, and re-layouts: 6.1 us -> none  [the longest x1 3.05 us: body(): upstream = cotangent[micro_index].reshape(token_count, model_width)]
  transfers between devices with their start and end apart: 6 -> 29, of which waited for: 5 -> 12; matrix products, arithmetic and copies ran while one was open for 20% -> 6% of each run, Pallas kernels for 0% -> 13%
where the time goes in v2:
time: 147 us; the launch traced here: 146 us
  waiting for transfers between devices  67.5 us (46%)
  starting transfers between devices  44.4 us (30%)
  Pallas kernels  19.1 us (13%)
  other arithmetic  10 us (7%)
  local copies, waits for them, and re-layouts  4.31 us (3%)
    ppermute x16, waiting for transfers between devices, move(): lax.ppermute(x, 'wide', [(2 * s + c, 2 * d + c) for s, d in pairs for c i...  52.5 us
    ppermute x16, starting transfers between devices, move(): lax.ppermute(x, 'wide', [(2 * s + c, 2 * d + c) for s, d in pairs for c i...  37.9 us
    ppermute x4, waiting for transfers between devices, flip(): return lax.ppermute(x, 'node', [(i, i ^ j) for i in range(n_node)])  13.7 us
    pallas_call x1, Pallas kernels, body(): call(functools.partial(backward_kernel, planes), 'backward', [SMEM] + [AN...  6.98 us
    pallas_call x1, Pallas kernels, body(): call(functools.partial(mixed_kernel, planes), 'mixed', [SMEM] + [ANY] * 4...  5.13 us
    ppermute x4, starting transfers between devices, flip(): return lax.ppermute(x, 'node', [(i, i ^ j) for i in range(n_node)])  4.94 us
    pallas_call x1, Pallas kernels, body(): call(grad_out_kernel, 'grad_out', [SMEM] + [ANY] * 2 + [VMEM] * 2, send_s...  4.58 us
    select_n x2, other arithmetic, gather_rest(): down = move(jnp.where(z == 1, across, u), [(3, 2), (2, 1), (1, 0)])  3.14 us
  transfers between devices with their start and end apart: 29, of which 12 were waited for; matrix products, arithmetic and copies ran while one was open for 6% of the time, Pallas kernels for 13%

profile of v2, /device:TPU:0, one launch (start us, length us, event | category | flops | bytes accessed | tf_op | source)
XLA Modules:
  0.0 146.4 jit_solution(11947796191211610198)
XLA Ops:
  0.6 1.1 constant_dynamic-slice_fusion.3
  1.7 0.5 collective-permute-start
  2.3 0.9 constant_dynamic-slice_fusion.2
  3.2 0.1 collective-permute-start.3
  3.3 1.3 collective-permute-done.3
  4.6 1.1 broadcast_select_fusion.5
  5.8 0.2 collective-permute-start.1
  6.0 0.4 collective-permute-start.10
  6.4 0.1 collective-permute-start.2
  6.6 4.0 %collective-permute-start.4 = (bf16[640,256]{1,0:T(8,128)(2,1)S(1)}, bf16[640,256]{1,0:T(8,128)(2,1)S(1)}, u32[]{:S(2)}, u32[]{:S(2)}) collective-permute-start(bf16[640,256]{1,0:T(8,128)(2,1)S(1)} %pad_maximum_fusion.3.rest_0_), channel_id=1, source_target_pairs={{0,16},{4,20},{8,24},{12,28},{16,0},{20,4},{24,8},{28,12},{1,17},{... | collective-permute-start | bytes 983048 | tf_op jit(solution)/shard_map/ppermute | solution.py:191
  10.5 1.3 collective-permute-start.11
  11.8 13.8 %collective-permute-done.4.rest_2_ = bf16[640,256]{1,0:T(8,128)(2,1)S(1)} collective-permute-done((bf16[640,256]{1,0:T(8,128)(2,1)S(1)}, bf16[640,256]{1,0:T(8,128)(2,1)S(1)}, u32[]{:S(2)}, u32[]{:S(2)}) %collective-permute-start.4) | collective-permute-done | bytes 327712 | tf_op jit(solution)/shard_map/ppermute | solution.py:191
  25.7 0.7 copy-done.4
  26.4 2.0 %broadcast_select_fusion = (bf16[640,256]{1,0:T(8,128)(2,1)}, bf16[640,256]{1,0:T(8,128)(2,1)}) fusion(bf16[640,256]{1,0:T(8,128)(2,1)} %copy-done.4, pred[]{:T(512)S(6)} %eq.14, bf16[320,256]{1,0:T(8,128)(2,1)S(1)} %get-tuple-element.63, bf16[320,256]{1,0:T(8,128)(2,1)} %copy-done.6, pred[]{:T(512)S(6)} %eq.13), kind=kLoop, calls=%fused_computation.27 | loop fusion | flops 983040 | bytes 1310722 | tf_op jit(solution)/shard_map/jit(_where)/select_n | solution.py:224
  28.4 1.3 collective-permute-start.13
  29.6 15.4 %collective-permute-done.6.rest_2_ = bf16[640,256]{1,0:T(8,128)(2,1)} collective-permute-done((bf16[640,256]{1,0:T(8,128)(2,1)S(1)}, bf16[640,256]{1,0:T(8,128)(2,1)}, u32[]{:S(2)}, u32[]{:S(2)}) %collective-permute-start.6) | collective-permute-done | bytes 327712 | tf_op jit(solution)/shard_map/ppermute | solution.py:191
  45.1 2.0 %collective-permute-start.12 = (bf16[640,256]{1,0:T(8,128)(2,1)}, bf16[640,256]{1,0:T(8,128)(2,1)}, u32[]{:S(2)}, u32[]{:S(2)}) collective-permute-start(bf16[640,256]{1,0:T(8,128)(2,1)} %get-tuple-element.56), channel_id=1, source_target_pairs={{0,8},{4,12},{8,16},{12,20},{16,24},{20,28},{1,9},{5,13},{9,17},{1... | collective-permute-start | bytes 983048 | tf_op jit(solution)/shard_map/ppermute | solution.py:191
  47.1 0.1 stack.78.idx
  47.2 0.1 stack.77.idx
  47.3 0.1 stack.72.idx
  47.4 1.2 broadcast_select_fusion.1
  48.6 1.3 collective-permute-start.5
  49.9 1.4 collective-permute-done.12
  51.3 1.3 collective-permute-start.8
  52.6 5.0 %collective-permute-start.7 = (bf16[640,256]{1,0:T(8,128)(2,1)S(1)}, bf16[640,256]{1,0:T(8,128)(2,1)S(1)}, u32[]{:S(2)}, u32[]{:S(2)}) collective-permute-start(bf16[640,256]{1,0:T(8,128)(2,1)S(1)} %get-tuple-element.58), channel_id=1, source_target_pairs={{0,8},{4,12},{8,16},{12,20},{16,24},{20,28},{1,9},{5,13},{9,17},{1... | collective-permute-start | bytes 983048 | tf_op jit(solution)/shard_map/ppermute | solution.py:191
  57.6 1.2 select_select_fusion
  58.9 1.2 copy-done.2
  60.2 7.0 %backward.1 = (bf16[2560,256]{1,0:T(8,128)(2,1)S(1)}, bf16[640,256]{1,0:T(8,128)(2,1)S(1)}, bf16[640,256]{1,0:T(8,128)(2,1)S(1)}, bf16[640,256]{1,0:T(8,128)(2,1...) custom-call(s32[10]{0:T(128)S(1)} %stack.77.idx, bf16[512,2560]{1,0:T(8,128)(2,1)S(1)} %bitcast.37, ...), custom_call_target="tpu_custom_call" | custom-call | flops 2684354560 | bytes 12582912 | tf_op jit(solution)/shard_map/backward/pallas_call | solution.py:306
  67.2 1.4 collective-permute-start.19
  68.6 4.9 %collective-permute-start.20 = (bf16[640,256]{1,0:T(8,128)(2,1)S(1)}, bf16[640,256]{1,0:T(8,128)(2,1)S(1)}, u32[]{:S(2)}, u32[]{:S(2)}) collective-permute-start(bf16[640,256]{1,0:T(8,128)(2,1)S(1)} %get-tuple-element.35), channel_id=1, source_target_pairs={{0,8},{4,12},{8,16},{12,20},{16,24},{20,28},{1,9},{5,13},{9,17},{1... | collective-permute-start | bytes 983048 | tf_op jit(solution)/shard_map/ppermute | solution.py:191
  73.5 0.1 collective-permute-start.14
  73.7 3.9 %collective-permute-start.21 = (bf16[640,256]{1,0:T(8,128)(2,1)S(1)}, bf16[640,256]{1,0:T(8,128)(2,1)S(1)}, u32[]{:S(2)}, u32[]{:S(2)}) collective-permute-start(bf16[640,256]{1,0:T(8,128)(2,1)S(1)} %get-tuple-element.36), channel_id=1, source_target_pairs={{0,8},{4,12},{24,16},{28,20},{1,9},{5,13},{25,17},{29,21},{2,10},{... | collective-permute-start | bytes 983048 | tf_op jit(solution)/shard_map/ppermute | solution.py:191
  77.7 5.1 %mixed.1 = (bf16[512,256]{1,0:T(8,128)(2,1)S(1)}, bf16[512,256]{1,0:T(8,128)(2,1)S(1)}) custom-call(s32[5]{0:T(128)S(1)} %stack.72.idx, bf16[512,2560]{1,0:T(8,128)(2,1)S(1)} %bitcast.35, bf16[512,2560]{1,0:T(8,128)(2,1)} %collective-permute-done.1.act_s, bf16[4,8,128,128]{3,2,1,0:T(8,128)(2,1)S(1)} %bitcast.41, ...), custom_call_target="tpu_custom_call" | custom-call | flops 1342177280 | bytes 12582912 | tf_op jit(solution)/shard_map/mixed/pallas_call | solution.py:317
  82.8 4.6 %grad_out.1 = (bf16[640,256]{1,0:T(8,128)(2,1)S(1)}, bf16[640,256]{1,0:T(8,128)(2,1)S(1)}, bf16[640,256]{1,0:T(8,128)(2,1)S(1)}, bf16[640,256]{1,0:T(8,128)(2,1)S(1)}, bf16[640,256]{1,0:T(8,128)(2,1)S(1)}) custom-call(s32[5]{0:T(128)S(1)} %stack.78.idx, bf16[512,2560]{1,0:T(8,128)(2,1)S(1)} %bitcast.38, bf16[512,2560]{1,0:T(8,128)(2,1)} %collective-permute-done.10.cot_s, ...), custom_call_target="tpu_custom_call" | custom-call | flops 1342177280 | bytes 12582912 | tf_op jit(solution)/shard_map/grad_out/pallas_call | solution.py:326
  87.4 1.3 collective-permute-start.24
  88.7 4.6 %collective-permute-start.25 = (bf16[640,256]{1,0:T(8,128)(2,1)S(1)}, bf16[640,256]{1,0:T(8,128)(2,1)S(1)}, u32[]{:S(2)}, u32[]{:S(2)}) collective-permute-start(bf16[640,256]{1,0:T(8,128)(2,1)S(1)} %get-tuple-element.40), channel_id=1, source_target_pairs={{0,8},{4,12},{8,16},{12,20},{16,24},{20,28},{1,9},{5,13},{9,17},{1... | collective-permute-start | bytes 983048 | tf_op jit(solution)/shard_map/ppermute | solution.py:191
  93.3 0.1 add_convert_fusion.1
  93.4 0.9 collective-permute-start.22
  94.4 0.1 pad_add_fusion.idx
  94.4 6.0 %collective-permute-done.24 = bf16[640,256]{1,0:T(8,128)(2,1)S(1)} collective-permute-done((bf16[640,256]{1,0:T(8,128)(2,1)S(1)}, bf16[640,256]{1,0:T(8,128)(2,1)S(1)}, u32[]{:S(2)}, u32[]{:S(2)}) %collective-permute-start.24) | collective-permute-done | bytes 327712 | tf_op jit(solution)/shard_map/ppermute | solution.py:191
  100.4 1.0 collective-permute-done.25
  101.3 4.6 %collective-permute-start.26 = (bf16[640,256]{1,0:T(8,128)(2,1)S(1)}, bf16[640,256]{1,0:T(8,128)(2,1)S(1)}, u32[]{:S(2)}, u32[]{:S(2)}) collective-permute-start(bf16[640,256]{1,0:T(8,128)(2,1)S(1)} %get-tuple-element.41), channel_id=1, source_target_pairs={{0,8},{4,12},{24,16},{28,20},{1,9},{5,13},{25,17},{29,21},{2,10},{... | collective-permute-start | bytes 983048 | tf_op jit(solution)/shard_map/ppermute | solution.py:191
  105.9 0.1 add_convert_fusion
  106.2 7.6 %collective-permute-done.22 = bf16[640,256]{1,0:T(8,128)(2,1)S(1)} collective-permute-done((bf16[640,256]{1,0:T(8,128)(2,1)S(1)}, bf16[640,256]{1,0:T(8,128)(2,1)S(1)}, u32[]{:S(2)}, u32[]{:S(2)}) %collective-permute-start.22) | collective-permute-done | bytes 327712 | tf_op jit(solution)/shard_map/ppermute | solution.py:191
  113.8 0.2 convert_add_fusion.1
  114.1 2.4 %terms.1 = (bf16[2,256,640]{2,1,0:T(8,128)(2,1)S(1)}, bf16[2,256,640]{2,1,0:T(8,128)(2,1)S(1)}, bf16[4,256,640]{2,1,0:T(8,128)(2,1)S(1)}) custom-call(s32[4]{0:T(128)S(1)} %pad_add_fusion.idx, bf16[512,256]{1,0:T(8,128)(2,1)S(1)} %get-tuple-element.26.mixed_o, bf16[512,256]{1,0:T(8,128)(2,1)S(1)} %collective-permute-done.9.mixed_r, ...), custom_call_target="tpu_custom_call" | custom-call | flops 1342177280 | bytes 12582912 | tf_op jit(solution)/shard_map/terms/pallas_call | solution.py:342
  116.5 1.3 collective-permute-start.15
  117.8 1.5 %collective-permute-start.17 = (bf16[2,256,640]{2,1,0:T(8,128)(2,1)S(1)}, bf16[2,256,640]{2,1,0:T(8,128)(2,1)S(1)}, u32[]{:S(2)}, u32[]{:S(2)}) collective-permute-start(bf16[2,256,640]{2,1,0:T(8,128)(2,1)S(1)} %get-tuple-element.32), channel_id=1, source_target_pairs={{0,2},{1,3},{2,0},{3,1},{4,6},{5,7},{6,4},{7,5},{8,10},{9,11},{10,... | collective-permute-start | bytes 1966088 | tf_op jit(solution)/shard_map/ppermute | solution.py:199
  119.3 7.2 %collective-permute-done.27 = bf16[640,256]{1,0:T(8,128)(2,1)S(1)} collective-permute-done((bf16[640,256]{1,0:T(8,128)(2,1)S(1)}, bf16[640,256]{1,0:T(8,128)(2,1)S(1)}, u32[]{:S(2)}, u32[]{:S(2)}) %collective-permute-start.27) | collective-permute-done | bytes 327712 | tf_op jit(solution)/shard_map/ppermute | solution.py:191
  126.6 0.2 convert_add_fusion
  127.0 0.9 pad_maximum_fusion.1
  127.9 0.2 convert_element_type.74
  128.1 5.6 %collective-permute-done.15 = bf16[2,256,640]{2,1,0:T(8,128)(2,1)S(1)} collective-permute-done((bf16[2,256,640]{2,1,0:T(8,128)(2,1)S(1)}, bf16[2,256,640]{2,1,0:T(8,128)(2,1)S(1)}, u32[]{:S(2)}, u32[]{:S(2)}) %collective-permute-start.15) | collective-permute-done | bytes 655392 | tf_op jit(solution)/shard_map/ppermute | solution.py:199
  133.7 0.1 convert_element_type.75
  133.8 0.9 collective-permute-done.17
  134.6 0.1 convert_element_type.79
  134.7 0.2 fusion.8
  134.9 1.6 %collective-permute-start.16 = (bf16[256,640]{1,0:T(8,128)(2,1)S(1)}, bf16[256,640]{1,0:T(8,128)(2,1)S(1)}, u32[]{:S(2)}, u32[]{:S(2)}) collective-permute-start(bf16[256,640]{1,0:T(8,128)(2,1)S(1)} %get-tuple-element.45), channel_id=1, source_target_pairs={{0,2},{1,3},{2,0},{3,1},{4,6},{5,7},{6,4},{7,5},{8,10},{9,11},{10,... | collective-permute-start | bytes 983048 | tf_op jit(solution)/shard_map/ppermute | solution.py:199
  136.5 0.5 collective-permute-start.18
  137.1 0.9 pad_maximum_fusion.2
  138.0 5.9 %collective-permute-done.16 = bf16[256,640]{1,0:T(8,128)(2,1)S(1)} collective-permute-done((bf16[256,640]{1,0:T(8,128)(2,1)S(1)}, bf16[256,640]{1,0:T(8,128)(2,1)S(1)}, u32[]{:S(2)}, u32[]{:S(2)}) %collective-permute-start.16) | collective-permute-done | bytes 327712 | tf_op jit(solution)/shard_map/ppermute | solution.py:199
  144.0 1.2 collective-permute-done.18
  145.2 0.2 fusion.7
  145.5 0.9 pad_maximum_fusion
  (41 shorter events, 0.6 us)
Async XLA Ops:
  0.6 5.2 %copy-start = (bf16[2,2,128,2560]{3,2,1,0:T(8,128)(2,1)S(1)}, bf16[2,2,128,2560]{3,2,1,0:T(8,128)(2,1)}, u32[]{:S(2)}) copy-start(bf16[2,2,128,2560]{3,2,1,0:T(8,128)(2,1)} %param.5) | copy-start | bytes 7864324
  1.7 1.6 %collective-permute-start = (bf16[320,256]{1,0:T(8,128)(2,1)S(1)}, bf16[320,256]{1,0:T(8,128)(2,1)S(1)}, u32[]{:S(2)}, u32[]{:S(2)}) collective-permute-start(bf16[320,256]{1,0:T(8,128)(2,1)S(1)} %constant_dynamic-slice_fusion.3), channel_id=1, source_target_pairs={{0,4},{4,0},{8,12},{12,8},{16,20},{20,16},{24,28},{28,24},{1,5},{5... | collective-permute-start | bytes 491528 | tf_op jit(solution)/shard_map/ppermute | solution.py:196
  3.2 1.5 collective-permute-start.3
  5.8 0.7 copy-start.6
  5.8 53.1 %collective-permute-start.1 = (bf16[512,2560]{1,0:T(8,128)(2,1)S(1)}, bf16[512,2560]{1,0:T(8,128)(2,1)}, u32[]{:S(2)}, u32[]{:S(2)}) collective-permute-start(bf16[512,2560]{1,0:T(8,128)(2,1)S(1)} %bitcast.33), channel_id=1, source_target_pairs={{0,4},{4,0},{8,12},{12,8},{16,20},{20,16},{24,28},{28,24},{1,5},{5... | collective-permute-start | bytes 7864328 | tf_op jit(solution)/shard_map/ppermute | solution.py:196
  6.0 52.9 %collective-permute-start.10 = (bf16[512,2560]{1,0:T(8,128)(2,1)}, bf16[512,2560]{1,0:T(8,128)(2,1)}, u32[]{:S(2)}, u32[]{:S(2)}) collective-permute-start(bf16[512,2560]{1,0:T(8,128)(2,1)} %bitcast.36), channel_id=1, source_target_pairs={{0,4},{4,0},{8,12},{12,8},{16,20},{20,16},{24,28},{28,24},{1,5},{5... | collective-permute-start | bytes 7864328 | tf_op jit(solution)/shard_map/ppermute | solution.py:196
  6.4 46.2 %collective-permute-start.2 = (bf16[4,8,128,128]{3,2,1,0:T(8,128)(2,1)}, bf16[4,8,128,128]{3,2,1,0:T(8,128)(2,1)}, u32[]{:S(2)}, u32[]{:S(2)}) collective-permute-start(bf16[4,8,128,128]{3,2,1,0:T(8,128)(2,1)} %bitcast.39), channel_id=1, source_target_pairs={{0,4},{4,0},{8,12},{12,8},{16,20},{20,16},{24,28},{28,24},{1,5},{5... | collective-permute-start | bytes 3145736 | tf_op jit(solution)/shard_map/ppermute | solution.py:196
  6.6 19.1 %collective-permute-start.4 = (bf16[640,256]{1,0:T(8,128)(2,1)S(1)}, bf16[640,256]{1,0:T(8,128)(2,1)S(1)}, u32[]{:S(2)}, u32[]{:S(2)}) collective-permute-start(bf16[640,256]{1,0:T(8,128)(2,1)S(1)} %pad_maximum_fusion.3.rest_0_), channel_id=1, source_target_pairs={{0,16},{4,20},{8,24},{12,28},{16,0},{20,4},{24,8},{28,12},{1,17},{... | collective-permute-start | bytes 983048 | tf_op jit(solution)/shard_map/ppermute | solution.py:191
  10.5 17.8 %collective-permute-start.11 = (bf16[640,256]{1,0:T(8,128)(2,1)S(1)}, bf16[640,256]{1,0:T(8,128)(2,1)}, u32[]{:S(2)}, u32[]{:S(2)}) collective-permute-start(bf16[640,256]{1,0:T(8,128)(2,1)S(1)} %pad_maximum_fusion.3.rest_0_), channel_id=1, source_target_pairs={{8,0},{12,4},{16,24},{20,28},{9,1},{13,5},{17,25},{21,29},{10,2},{... | collective-permute-start | bytes 983048 | tf_op jit(solution)/shard_map/ppermute | solution.py:191
  25.7 0.7 copy-start.4
  26.4 18.7 %collective-permute-start.6 = (bf16[640,256]{1,0:T(8,128)(2,1)S(1)}, bf16[640,256]{1,0:T(8,128)(2,1)}, u32[]{:S(2)}, u32[]{:S(2)}) collective-permute-start(bf16[640,256]{1,0:T(8,128)(2,1)S(1)} %pad_maximum_fusion.4.rest_0_), channel_id=1, source_target_pairs={{0,16},{4,20},{8,24},{12,28},{16,0},{20,4},{24,8},{28,12},{1,17},{... | collective-permute-start | bytes 983048 | tf_op jit(solution)/shard_map/ppermute | solution.py:191
  28.4 20.2 %collective-permute-start.13 = (bf16[640,256]{1,0:T(8,128)(2,1)}, bf16[640,256]{1,0:T(8,128)(2,1)}, u32[]{:S(2)}, u32[]{:S(2)}) collective-permute-start(bf16[640,256]{1,0:T(8,128)(2,1)} %get-tuple-element.55), channel_id=1, source_target_pairs={{24,16},{28,20},{16,8},{20,12},{8,0},{12,4},{25,17},{29,21},{17,9}... | collective-permute-start | bytes 983048 | tf_op jit(solution)/shard_map/ppermute | solution.py:191
  45.1 6.2 %collective-permute-start.12 = (bf16[640,256]{1,0:T(8,128)(2,1)}, bf16[640,256]{1,0:T(8,128)(2,1)}, u32[]{:S(2)}, u32[]{:S(2)}) collective-permute-start(bf16[640,256]{1,0:T(8,128)(2,1)} %get-tuple-element.56), channel_id=1, source_target_pairs={{0,8},{4,12},{8,16},{12,20},{16,24},{20,28},{1,9},{5,13},{9,17},{1... | collective-permute-start | bytes 983048 | tf_op jit(solution)/shard_map/ppermute | solution.py:191
  47.4 11.5 %copy-start.1 = (bf16[2,2,128,2560]{3,2,1,0:T(8,128)(2,1)S(1)}, bf16[2,2,128,2560]{3,2,1,0:T(8,128)(2,1)}, u32[]{:S(2)}) copy-start(bf16[2,2,128,2560]{3,2,1,0:T(8,128)(2,1)} %param.7) | copy-start | bytes 7864324
  47.4 11.5 %copy-start.5 = (bf16[640,256]{1,0:T(8,128)(2,1)S(1)}, bf16[640,256]{1,0:T(8,128)(2,1)}, u32[]{:S(2)}) copy-start(bf16[640,256]{1,0:T(8,128)(2,1)} %copy-done.4) | copy-start | bytes 983044
  48.6 25.0 %collective-permute-start.5 = (bf16[640,256]{1,0:T(8,128)(2,1)S(1)}, bf16[640,256]{1,0:T(8,128)(2,1)S(1)}, u32[]{:S(2)}, u32[]{:S(2)}) collective-permute-start(bf16[640,256]{1,0:T(8,128)(2,1)S(1)} %pad_maximum_fusion.4.rest_0_), channel_id=1, source_target_pairs={{8,0},{12,4},{16,24},{20,28},{9,1},{13,5},{17,25},{21,29},{10,2},{... | collective-permute-start | bytes 983048 | tf_op jit(solution)/shard_map/ppermute | solution.py:191
  51.3 22.3 %collective-permute-start.8 = (bf16[640,256]{1,0:T(8,128)(2,1)S(1)}, bf16[640,256]{1,0:T(8,128)(2,1)S(1)}, u32[]{:S(2)}, u32[]{:S(2)}) collective-permute-start(bf16[640,256]{1,0:T(8,128)(2,1)S(1)} %get-tuple-element.57), channel_id=1, source_target_pairs={{24,16},{28,20},{16,8},{20,12},{8,0},{12,4},{25,17},{29,21},{17,9}... | collective-permute-start | bytes 983048 | tf_op jit(solution)/shard_map/ppermute | solution.py:191
  52.6 21.0 %collective-permute-start.7 = (bf16[640,256]{1,0:T(8,128)(2,1)S(1)}, bf16[640,256]{1,0:T(8,128)(2,1)S(1)}, u32[]{:S(2)}, u32[]{:S(2)}) collective-permute-start(bf16[640,256]{1,0:T(8,128)(2,1)S(1)} %get-tuple-element.58), channel_id=1, source_target_pairs={{0,8},{4,12},{8,16},{12,20},{16,24},{20,28},{1,9},{5,13},{9,17},{1... | collective-permute-start | bytes 983048 | tf_op jit(solution)/shard_map/ppermute | solution.py:191
  58.9 1.2 copy-start.2
  67.1 10.5 %copy-start.3 = (bf16[2,2,8,128,128]{4,3,2,1,0:T(8,128)(2,1)S(1)}, bf16[2,2,8,128,128]{4,3,2,1,0:T(8,128)(2,1)}, u32[]{:S(2)}) copy-start(bf16[2,2,8,128,128]{4,3,2,1,0:T(8,128)(2,1)} %param.6) | copy-start | bytes 3145732
  67.2 21.5 %collective-permute-start.19 = (bf16[640,256]{1,0:T(8,128)(2,1)S(1)}, bf16[640,256]{1,0:T(8,128)(2,1)S(1)}, u32[]{:S(2)}, u32[]{:S(2)}) collective-permute-start(bf16[640,256]{1,0:T(8,128)(2,1)S(1)} %get-tuple-element.34), channel_id=1, source_target_pairs={{24,16},{28,20},{16,8},{20,12},{8,0},{12,4},{25,17},{29,21},{17,9}... | collective-permute-start | bytes 983048 | tf_op jit(solution)/shard_map/ppermute | solution.py:191
  68.6 24.7 %collective-permute-start.20 = (bf16[640,256]{1,0:T(8,128)(2,1)S(1)}, bf16[640,256]{1,0:T(8,128)(2,1)S(1)}, u32[]{:S(2)}, u32[]{:S(2)}) collective-permute-start(bf16[640,256]{1,0:T(8,128)(2,1)S(1)} %get-tuple-element.35), channel_id=1, source_target_pairs={{0,8},{4,12},{8,16},{12,20},{16,24},{20,28},{1,9},{5,13},{9,17},{1... | collective-permute-start | bytes 983048 | tf_op jit(solution)/shard_map/ppermute | solution.py:191
  73.5 40.6 %collective-permute-start.14 = (bf16[2560,256]{1,0:T(8,128)(2,1)S(1)}, bf16[2560,256]{1,0:T(8,128)(2,1)S(1)}, u32[]{:S(2)}, u32[]{:S(2)}) collective-permute-start(bf16[2560,256]{1,0:T(8,128)(2,1)S(1)} %get-tuple-element.29.w_o), channel_id=1, source_target_pairs={{0,4},{4,0},{8,12},{12,8},{16,20},{20,16},{24,28},{28,24},{1,5},{5... | collective-permute-start | bytes 3932168 | tf_op jit(solution)/shard_map/ppermute | solution.py:196
  73.7 32.4 %collective-permute-start.21 = (bf16[640,256]{1,0:T(8,128)(2,1)S(1)}, bf16[640,256]{1,0:T(8,128)(2,1)S(1)}, u32[]{:S(2)}, u32[]{:S(2)}) collective-permute-start(bf16[640,256]{1,0:T(8,128)(2,1)S(1)} %get-tuple-element.36), channel_id=1, source_target_pairs={{0,8},{4,12},{24,16},{28,20},{1,9},{5,13},{25,17},{29,21},{2,10},{... | collective-permute-start | bytes 983048 | tf_op jit(solution)/shard_map/ppermute | solution.py:191
  87.4 13.0 %collective-permute-start.24 = (bf16[640,256]{1,0:T(8,128)(2,1)S(1)}, bf16[640,256]{1,0:T(8,128)(2,1)S(1)}, u32[]{:S(2)}, u32[]{:S(2)}) collective-permute-start(bf16[640,256]{1,0:T(8,128)(2,1)S(1)} %get-tuple-element.39), channel_id=1, source_target_pairs={{24,16},{28,20},{16,8},{20,12},{8,0},{12,4},{25,17},{29,21},{17,9}... | collective-permute-start | bytes 983048 | tf_op jit(solution)/shard_map/ppermute | solution.py:191
  88.7 12.6 %collective-permute-start.25 = (bf16[640,256]{1,0:T(8,128)(2,1)S(1)}, bf16[640,256]{1,0:T(8,128)(2,1)S(1)}, u32[]{:S(2)}, u32[]{:S(2)}) collective-permute-start(bf16[640,256]{1,0:T(8,128)(2,1)S(1)} %get-tuple-element.40), channel_id=1, source_target_pairs={{0,8},{4,12},{8,16},{12,20},{16,24},{20,28},{1,9},{5,13},{9,17},{1... | collective-permute-start | bytes 983048 | tf_op jit(solution)/shard_map/ppermute | solution.py:191
  93.4 20.3 %collective-permute-start.22 = (bf16[640,256]{1,0:T(8,128)(2,1)S(1)}, bf16[640,256]{1,0:T(8,128)(2,1)S(1)}, u32[]{:S(2)}, u32[]{:S(2)}) collective-permute-start(bf16[640,256]{1,0:T(8,128)(2,1)S(1)} %add_convert_fusion.1), channel_id=1, source_target_pairs={{0,16},{4,20},{8,24},{12,28},{16,0},{20,4},{24,8},{28,12},{1,17},{... | collective-permute-start | bytes 983048 | tf_op jit(solution)/shard_map/ppermute | solution.py:191
  100.4 13.7 %collective-permute-start.9 = (bf16[512,256]{1,0:T(8,128)(2,1)S(1)}, bf16[512,256]{1,0:T(8,128)(2,1)S(1)}, u32[]{:S(2)}, u32[]{:S(2)}) collective-permute-start(bf16[512,256]{1,0:T(8,128)(2,1)S(1)} %get-tuple-element.27.mixed_s), channel_id=1, source_target_pairs={{0,4},{4,0},{8,12},{12,8},{16,20},{20,16},{24,28},{28,24},{1,5},{5... | collective-permute-start | bytes 786440 | tf_op jit(solution)/shard_map/ppermute | solution.py:196
  101.3 18.0 %collective-permute-start.26 = (bf16[640,256]{1,0:T(8,128)(2,1)S(1)}, bf16[640,256]{1,0:T(8,128)(2,1)S(1)}, u32[]{:S(2)}, u32[]{:S(2)}) collective-permute-start(bf16[640,256]{1,0:T(8,128)(2,1)S(1)} %get-tuple-element.41), channel_id=1, source_target_pairs={{0,8},{4,12},{24,16},{28,20},{1,9},{5,13},{25,17},{29,21},{2,10},{... | collective-permute-start | bytes 983048 | tf_op jit(solution)/shard_map/ppermute | solution.py:191
  106.1 20.5 %collective-permute-start.27 = (bf16[640,256]{1,0:T(8,128)(2,1)S(1)}, bf16[640,256]{1,0:T(8,128)(2,1)S(1)}, u32[]{:S(2)}, u32[]{:S(2)}) collective-permute-start(bf16[640,256]{1,0:T(8,128)(2,1)S(1)} %add_convert_fusion), channel_id=1, source_target_pairs={{0,16},{4,20},{8,24},{12,28},{16,0},{20,4},{24,8},{28,12},{1,17},{... | collective-permute-start | bytes 983048 | tf_op jit(solution)/shard_map/ppermute | solution.py:191
  114.0 12.9 %collective-permute-start.23 = (f32[320,256]{1,0:T(8,128)S(1)}, f32[320,256]{1,0:T(8,128)S(1)}, u32[]{:S(2)}, u32[]{:S(2)}) collective-permute-start(f32[320,256]{1,0:T(8,128)S(1)} %constant_dynamic-slice_fusion.1), channel_id=1, source_target_pairs={{0,4},{4,0},{8,12},{12,8},{16,20},{20,16},{24,28},{28,24},{1,5},{5... | collective-permute-start | bytes 983048 | tf_op jit(solution)/shard_map/ppermute | solution.py:196
  116.5 17.2 %collective-permute-start.15 = (bf16[2,256,640]{2,1,0:T(8,128)(2,1)S(1)}, bf16[2,256,640]{2,1,0:T(8,128)(2,1)S(1)}, u32[]{:S(2)}, u32[]{:S(2)}) collective-permute-start(bf16[2,256,640]{2,1,0:T(8,128)(2,1)S(1)} %get-tuple-element.31), channel_id=1, source_target_pairs={{0,1},{1,0},{2,3},{3,2},{4,5},{5,4},{6,7},{7,6},{8,9},{9,8},{10,11... | collective-permute-start | bytes 1966088 | tf_op jit(solution)/shard_map/ppermute | solution.py:199
  117.8 16.8 %collective-permute-start.17 = (bf16[2,256,640]{2,1,0:T(8,128)(2,1)S(1)}, bf16[2,256,640]{2,1,0:T(8,128)(2,1)S(1)}, u32[]{:S(2)}, u32[]{:S(2)}) collective-permute-start(bf16[2,256,640]{2,1,0:T(8,128)(2,1)S(1)} %get-tuple-element.32), channel_id=1, source_target_pairs={{0,2},{1,3},{2,0},{3,1},{4,6},{5,7},{6,4},{7,5},{8,10},{9,11},{10,... | collective-permute-start | bytes 1966088 | tf_op jit(solution)/shard_map/ppermute | solution.py:199
  126.8 10.3 %collective-permute-start.28 = (f32[320,256]{1,0:T(8,128)S(1)}, f32[320,256]{1,0:T(8,128)S(1)}, u32[]{:S(2)}, u32[]{:S(2)}) collective-permute-start(f32[320,256]{1,0:T(8,128)S(1)} %constant_dynamic-slice_fusion), channel_id=1, source_target_pairs={{0,4},{4,0},{8,12},{12,8},{16,20},{20,16},{24,28},{28,24},{1,5},{5... | collective-permute-start | bytes 983048 | tf_op jit(solution)/shard_map/ppermute | solution.py:196
  134.9 9.1 %collective-permute-start.16 = (bf16[256,640]{1,0:T(8,128)(2,1)S(1)}, bf16[256,640]{1,0:T(8,128)(2,1)S(1)}, u32[]{:S(2)}, u32[]{:S(2)}) collective-permute-start(bf16[256,640]{1,0:T(8,128)(2,1)S(1)} %get-tuple-element.45), channel_id=1, source_target_pairs={{0,2},{1,3},{2,0},{3,1},{4,6},{5,7},{6,4},{7,5},{8,10},{9,11},{10,... | collective-permute-start | bytes 983048 | tf_op jit(solution)/shard_map/ppermute | solution.py:199
  136.5 8.7 %collective-permute-start.18 = (bf16[256,640]{1,0:T(8,128)(2,1)S(1)}, bf16[256,640]{1,0:T(8,128)(2,1)S(1)}, u32[]{:S(2)}, u32[]{:S(2)}) collective-permute-start(bf16[256,640]{1,0:T(8,128)(2,1)S(1)} %get-tuple-element.46), channel_id=1, source_target_pairs={{0,1},{1,0},{2,3},{3,2},{4,5},{5,4},{6,7},{7,6},{8,9},{9,8},{10,11... | collective-permute-start | bytes 983048 | tf_op jit(solution)/shard_map/ppermute | solution.py:199

commit v3 on v2

--- a/solution.py
+++ b/solution.py
@@ -1,4 +1,5 @@
 import functools
+import math
 
 import jax
 import jax.numpy as jnp
@@ -25,7 +26,30 @@
 
 
 def rows_at(index, size):
-    return pl.ds(pl.multiple_of(index * size, 16), size)
+    return pl.ds(pl.multiple_of(index * size, math.gcd(size, 16)), size)
+
+
+def place(idx, slots, w_ref):
+    core = idx[0]
+    for j, slot in enumerate(slots):
+        depth = slot.shape[0] // 2
+
+        @pl.when(idx[2 + 2 * j] == 1)
+        def _(slot=slot, depth=depth, plane=idx[1 + 2 * j]):
+            mine, other = slot[:depth, :], slot[depth:, :]
+            low = jnp.where(core == 0, mine, other)
+            high = jnp.where(core == 0, other, mine)
+            w_ref[rows_at(plane, 2 * depth), :] = jnp.concatenate([low, high], axis=0)
+
+
+def hand_out(idx, base, grad_v, outs):
+    core = idx[0]
+    for i, out in enumerate(outs):
+        depth = out.shape[1]
+        block = grad_v[rows_at(idx[base + i], 2 * depth), :]
+        low, high = block[:depth], block[depth:]
+        out[0] = jnp.where(core == 0, low, high)
+        out[1] = jnp.where(core == 0, high, low)
 
 
 def gradient_rows(left, right_ref, rows_ref, step):
@@ -46,16 +70,14 @@
     tokens, cols = cot_o.shape[0], w_out.shape[1]
     groups, _, seq, _ = mix_o.shape
     heads = mix_v.shape[2]
-    depth = slots[0].shape[0]
-    here = pl.ds(idx[0], heads)
+    here = pl.ds(idx[0] * heads, heads)
     copies = begin(
         [(cot_o, cot_v.at[0]), (mix_o.at[:, here], mix_v.at[0])]
         + [(cot_s, cot_v.at[1]), (mix_s.at[:, here], mix_v.at[1])]
         + [(act_o, act_v.at[pl.ds(0, tokens)]), (act_s, act_v.at[pl.ds(tokens, tokens)])],
         sems,
     )
-    for j in range(n_slots):
-        w_out[rows_at(idx[1 + j], depth), :] = slots[j][...]
+    place(idx, slots, w_out)
     for half in range(2):
         copies[2 * half].wait()
         d_mixed = dot(cot_v[half], w_out[...])
@@ -82,23 +104,20 @@
     copies[4].wait()
     copies[5].wait()
     gradient_rows(left_v[...], act_v, grad_v, 640)
-    for i, out in enumerate(outs):
-        out[...] = grad_v[rows_at(idx[1 + n_slots + i], depth), :]
+    hand_out(idx, 1 + 2 * n_slots, grad_v, outs)
 
 
 def mixed_kernel(n_slots, idx, act_o, act_s, mix_o, mix_s, *rest):
     slots, (mixed_o, mixed_s, w_v, act_v, mix_v, sems) = rest[:n_slots], rest[n_slots:]
     groups, _, seq, _ = mix_o.shape
     heads = mix_v.shape[2]
-    depth = slots[0].shape[0]
-    here = pl.ds(idx[0], heads)
+    here = pl.ds(idx[0] * heads, heads)
     copies = begin(
         [(act_o, act_v.at[0]), (mix_o.at[:, here], mix_v.at[0])]
         + [(act_s, act_v.at[1]), (mix_s.at[:, here], mix_v.at[1])],
         sems,
     )
-    for j in range(n_slots):
-        w_v[rows_at(idx[1 + j], depth), :] = slots[j][...]
+    place(idx, slots, w_v)
     for half, out in enumerate((mixed_o, mixed_s)):
         copies[2 * half].wait()
         value = dot(act_v[half], w_v[...]).astype(BF16)
@@ -126,7 +145,6 @@
 def grad_out_kernel(idx, cot_o, cot_s, mixed_o, mixed_s, *rest):
     outs, (cot_v, left_v, grad_v, sems) = rest[:-4], rest[-4:]
     tokens, _ = cot_o.shape
-    depth = outs[0].shape[0]
     copies = begin(
         [(cot_o, cot_v.at[pl.ds(0, tokens)]), (cot_s, cot_v.at[pl.ds(tokens, tokens)])], sems
     )
@@ -135,8 +153,7 @@
     copies[0].wait()
     copies[1].wait()
     gradient_rows(left_v[...], cot_v, grad_v, 640)
-    for i, out in enumerate(outs):
-        out[...] = grad_v[rows_at(idx[i], depth), :]
+    hand_out(idx, 1, grad_v, outs)
 
 
 def terms_kernel(n_node, idx, mixed_o, mixed_r, w_o, w_r, *outs):
@@ -175,7 +192,7 @@
         out_shape=[jax.ShapeDtypeStruct(s, BF16) for s in out_shapes],
         scratch_shapes=scratch,
         compiler_params=pltpu.CompilerParams(vmem_limit_bytes=VMEM_LIMIT),
-        cost_estimate=pl.CostEstimate(flops=flops, bytes_accessed=12 << 20, transcendentals=0),
+        cost_estimate=pl.CostEstimate(flops=0, bytes_accessed=1024, transcendentals=0),
     )
 
 
@@ -198,33 +215,36 @@
     def flip(x, j):
         return lax.ppermute(x, "node", [(i, i ^ j) for i in range(n_node)])
 
-    def column_half(w, c):
-        cols = w.shape[1] // 2
-        mine = lax.dynamic_slice_in_dim(w, c * cols, cols, 1)
-        got = sibling(lax.dynamic_slice_in_dim(w, (1 - c) * cols, cols, 1))
-        low = jnp.where(c == 0, mine, got)
-        high = jnp.where(c == 0, got, mine)
-        return jnp.concatenate([low, high], axis=0)
+    def swap_halves(weights, c):
+        cols = weights[0].shape[1] // 2
+        low = jnp.stack([w[:, :cols] for w in weights])
+        high = jnp.stack([w[:, cols:] for w in weights])
+        got = sibling(jnp.where(c == 0, high, low))
+        mine = jnp.where(c == 0, low, high)
+        return [jnp.concatenate([mine[i], got[i]], axis=0) for i in range(len(weights))]
 
     def gather_first(u):
         if not line4:
-            return None
-        across = move(u, [(0, 2), (1, 3), (2, 0), (3, 1)])
-        ends = move(u, [(1, 0), (2, 3)])
-        return across, ends
-
-    def gather_rest(u, firsts, z):
+            return [move(u, [(s, (s - j) % planes) for s in range(planes)]) for j in range(1, planes)]
+        return [move(u, [(0, 2), (1, 3), (2, 0), (3, 1)]), move(u, [(1, 0), (2, 3)])]
+
+    def gather_rest(u, firsts):
         if not line4:
-            return [u] + [
-                move(u, [(s, (s - j) % planes) for s in range(planes)])
-                for j in range(1, planes)
-            ]
+            return [u, *firsts]
         across, ends = firsts
-        up = move(jnp.where(z == 2, across, u), [(0, 1), (1, 2), (2, 3)])
-        down = move(jnp.where(z == 1, across, u), [(3, 2), (2, 1), (1, 0)])
-        after_z = jnp.where(z == 0, ends, jnp.where(z == 3, up, down))
-        before_z = jnp.where(z == 0, down, jnp.where(z == 3, ends, up))
-        return [u, after_z, across, before_z]
+        up = move(u, [(0, 1), (1, 2)])
+        down = move(u, [(3, 2), (2, 1)])
+        on = move(across, [(2, 3), (1, 0)])
+        return [u, across, ends, on, up, down]
+
+    def slot_planes(z):
+        if not line4:
+            return [x for j in range(planes) for x in (lax.rem(z + j, planes), 1)]
+        edge = ((z == 0) | (z == 3)).astype(jnp.int32)
+        ends = jnp.where(z == 0, 1, 2)
+        on = jnp.where(z == 0, 3, 0)
+        up, down = jnp.maximum(z - 1, 0), jnp.minimum(z + 1, 3)
+        return [z, 1, lax.rem(z + 2, 4), 1, ends, edge, on, edge, up, 1 - edge, down, 1 - edge]
 
     def send_planes(z):
         if not line4:
@@ -234,32 +254,46 @@
         near = jnp.where(z == 0, 1, jnp.where(z == 3, 2, z))
         return [z, up, down, near, lax.rem(z + 2, 4)]
 
-    def scatter(blocks, z):
-        if not line4:
-            total = blocks[0].astype(F32)
-            for j in range(1, planes):
-                got = move(blocks[j], [(s, (s + j) % planes) for s in range(planes)])
-                total = total + got.astype(F32)
-            return total
-        own, up, down, near, far = blocks
-        up = move(up, [(0, 1), (1, 2), (2, 3)])
-        down = move(down, [(3, 2), (2, 1), (1, 0)])
-        near = move(near, [(0, 1), (3, 2)])
+    def scatter_first(blocks):
+        _, up, down, _, _ = blocks
+        return move(up, [(0, 1), (1, 2), (2, 3)]), move(down, [(3, 2), (2, 1), (1, 0)])
+
+    def scatter_far(blocks, firsts, z):
+        up, down = firsts
         add = jnp.where(z == 1, up, jnp.where(z == 2, down, jnp.zeros_like(up)))
-        far = move(
-            (far.astype(F32) + add.astype(F32)).astype(BF16),
-            [(0, 2), (1, 3), (2, 0), (3, 1)],
-        )
-        total = own.astype(F32) + jnp.where(z <= 1, down, up).astype(F32)
-        return total + near.astype(F32) + far.astype(F32)
-
-    def finish(total, c):
-        rows = total.shape[0] // 2
-        mine = lax.dynamic_slice_in_dim(total, c * rows, rows, 0)
-        got = sibling(lax.dynamic_slice_in_dim(total, (1 - c) * rows, rows, 0))
-        low = jnp.where(c == 0, mine, got)
-        high = jnp.where(c == 0, got, mine)
+        return (blocks[4].astype(F32) + add.astype(F32)).astype(BF16)
+
+    def scatter_near(blocks, firsts, z):
+        up, down = firsts
+        near = move(after(blocks[3], up, down), [(0, 1), (3, 2)])
+        total = blocks[0].astype(F32) + jnp.where(z <= 1, down, up).astype(F32)
+        return total + near.astype(F32)
+
+    def join(mine, other, c):
+        low = jnp.where(c == 0, mine, other)
+        high = jnp.where(c == 0, other, mine)
         return jnp.concatenate([low, high], axis=1)
+
+    def scatter_rest(blocks, firsts, far, z, c, last):
+        if last:
+            far_other = lax.ppermute(
+                far[1],
+                "wide",
+                [(2 * s + k, 2 * ((s + 2) % 4) + 1 - k) for s in range(4) for k in range(2)],
+            )
+            far_mine = move(far[0], [(s, (s + 2) % 4) for s in range(4)])
+            total = scatter_near(blocks, firsts, z)
+            other = sibling(total[1])
+            return join(total[0] + far_mine.astype(F32), other + far_other.astype(F32), c)
+        far = move(far, [(s, (s + 2) % 4) for s in range(4)])
+        return scatter_near(blocks, firsts, z) + far.astype(F32)
+
+    def scatter_ring(blocks, c):
+        total = blocks[0].astype(F32)
+        for j in range(1, planes):
+            got = move(blocks[j], [(s, (s + j) % planes) for s in range(planes)])
+            total = total + got.astype(F32)
+        return join(total[0], sibling(total[1]), c)
 
     def body(act_in, mixing, cotangent, w_value, w_out):
         wide = lax.axis_index("wide")
@@ -276,24 +310,23 @@
         mix = mixing.reshape(groups, 2 * heads, seq, seq)
         flops = 4 * tokens * width * cols
 
-        u_out = column_half(w_out, c)
-        u_value = column_half(w_value, c)
+        u_out, u_value = swap_halves([w_out, w_value], c)
         out_first = gather_first(u_out)
         cot_s = sibling(after(cot, u_out))
         mix_s = sibling(after(mix, u_out))
         act_s = sibling(after(act, u_out))
-        out_slots = gather_rest(u_out, out_first, z)
-        if line4:
-            u_value = after(u_value, out_first[0])
+        out_first = list(lax.optimization_barrier((*out_first, cot_s, mix_s, act_s)))
+        *out_first, cot_s, mix_s, act_s = out_first
+        out_slots = gather_rest(after(u_out, out_first[0]), out_first)
+        u_value = after(u_value, out_first[0])
         value_first = gather_first(u_value)
-        value_slots = gather_rest(u_value, value_first, z)
-
-        slot_planes = [lax.rem(z + j, planes) for j in range(planes)]
+
+        info = slot_planes(z)
         sends = send_planes(z)
-        first_head = c * heads
-        idx_back = jnp.stack([first_head, *slot_planes, *sends]).astype(jnp.int32)
-        idx_mixed = jnp.stack([first_head, *slot_planes]).astype(jnp.int32)
-        idx_send = jnp.stack(sends).astype(jnp.int32)
+        n_slots = len(out_slots)
+        idx_back = jnp.stack([c, *info, *sends]).astype(jnp.int32)
+        idx_mixed = jnp.stack([c, *info]).astype(jnp.int32)
+        idx_send = jnp.stack([c, *sends]).astype(jnp.int32)
         idx_node = jnp.stack([lax.bitwise_xor(n, jnp.int32(j)) for j in range(n_node)])
 
         mix_scratch = pltpu.VMEM((2, groups, heads, seq, seq), BF16)
@@ -301,23 +334,31 @@
         halves = pltpu.VMEM((2, tokens, width), BF16)
         left = pltpu.VMEM((cols, 2 * tokens), BF16)
         rows = pltpu.VMEM((width, cols), BF16)
-        send_shapes = [(depth, cols)] * len(sends)
+        send_shapes = [(2, depth // 2, cols)] * len(sends)
 
         w_full, *back_sends = call(
-            functools.partial(backward_kernel, planes),
+            functools.partial(backward_kernel, n_slots),
             "backward",
-            [SMEM] + [ANY] * 6 + [VMEM] * planes,
+            [SMEM] + [ANY] * 6 + [VMEM] * n_slots,
             [(width, cols)] + send_shapes,
             [halves, both, mix_scratch, left, rows, pltpu.SemaphoreType.DMA((6,))],
             2 * flops,
         )(idx_back, cot, cot_s, mix, mix_s, act, act_s, *out_slots)
-        w_full_s = sibling(w_full)
-        grad_value = scatter(back_sends, z)
+        if line4:
+            value_first = [after(x, back_sends[0]) for x in value_first]
+            value_slots = gather_rest(after(u_value, back_sends[0]), value_first)
+            back_firsts = scatter_first(back_sends)
+            far = scatter_far(back_sends, back_firsts, z)
+            value_slots = list(lax.optimization_barrier((*value_slots, far)))[:-1]
+            w_full_s = sibling(after(w_full, value_slots[0]))
+        else:
+            value_slots = gather_rest(u_value, value_first)
+            w_full_s = sibling(w_full)
 
         mixed_o, mixed_s = call(
-            functools.partial(mixed_kernel, planes),
+            functools.partial(mixed_kernel, n_slots),
             "mixed",
-            [SMEM] + [ANY] * 4 + [VMEM] * planes,
+            [SMEM] + [ANY] * 4 + [VMEM] * n_slots,
             [(tokens, cols)] * 2,
             [rows, halves, mix_scratch, pltpu.SemaphoreType.DMA((4,))],
             flops,
@@ -331,8 +372,6 @@
             [both, left, rows, pltpu.SemaphoreType.DMA((2,))],
             flops,
         )(idx_send, cot, cot_s, mixed_o, mixed_s)
-        grad_out = scatter(out_sends, z)
-
         part = width // n_node
         half = tokens // 2
         if n_node == 4:
@@ -347,6 +386,20 @@
             [],
             flops,
         )(idx_node, mixed_o, mixed_r, w_full, w_full_s)
+        if line4:
+            grad_value = scatter_rest(back_sends, back_firsts, far, z, c, False)
+            *out_sends, grad_value, mixed_r = lax.optimization_barrier(
+                (*out_sends, grad_value, mixed_r)
+            )
+            out_firsts = scatter_first(out_sends)
+            *out_firsts, _ = lax.optimization_barrier((*out_firsts, terms[0]))
+            out_far = scatter_far(out_sends, out_firsts, z)
+            grad_out = scatter_rest(out_sends, out_firsts, out_far, z, c, True)
+            grad_value = join(grad_value[0], sibling(grad_value[1]), c)
+        else:
+            grad_value = scatter_ring(back_sends, c)
+            grad_out = scatter_ring(out_sends, c)
+
         if n_node == 4:
             along_x, along_y, kept = terms
             kept = kept.astype(F32)
@@ -366,7 +419,7 @@
             for j in range(1, n_node):
                 layer_out = layer_out + flip(terms[j], j).astype(F32)
         layer_out = layer_out.astype(BF16).reshape(micro, images, seq, part)
-        return layer_out, finish(grad_value, c), finish(grad_out, c)
+        return layer_out, grad_value, grad_out
 
     return body
 

time: 147 us -> 158 us (1.075)
  local copies, waits for them, and re-layouts: 4.31 us -> 23.3 us
  waiting for transfers between devices: 67.5 us -> 49.2 us
  starting transfers between devices: 44.4 us -> 54.4 us
  Pallas kernels: 19.1 us -> 21.1 us
  other arithmetic: 10 us -> 8.37 us
    unnamed x14 -> x52, local copies, waits for them, and re-layouts: 1.99 us -> 21.7 us
    ppermute x16 -> x18, waiting for transfers between devices: 52.5 us -> 37.5 us  [move(): lax.ppermute(x, 'wide', [(2 * s + c, 2 * d + c) for s, d in pairs for c i...]
    ppermute x16 -> x18, starting transfers between devices: 37.9 us -> 47 us  [move(): lax.ppermute(x, 'wide', [(2 * s + c, 2 * d + c) for s, d in pairs for c i...]
    ppermute x4, waiting for transfers between devices: 13.7 us -> 7.82 us  [flip(): return lax.ppermute(x, 'node', [(i, i ^ j) for i in range(n_node)])]
    select_n x7 -> x3, other arithmetic: 5.65 us -> 0.2 us  [the longest x2 0.14 us: join(): low = jnp.where(c == 0, mine, other)]
    convert_element_type x2, other arithmetic: 0.29 us -> 3.16 us  [scatter_far(): return (blocks[4].astype(F32) + add.astype(F32)).astype(BF16)]
    ppermute x0 -> x1, waiting for transfers between devices: none -> 2.7 us  [scatter_rest(): lax.ppermute(far[1], 'wide', [(2 * s + k, 2 * ((s + 2) % 4) + 1 - k) for...]
    pallas_call x2, Pallas kernels: 12.1 us -> 14.4 us  [the longest x1 8.57 us: body(): call(functools.partial(backward_kernel, n_slots), 'backward', [SMEM] + [A...]
  transfers between devices with their start and end apart: 29 -> 31, of which waited for: 12 -> 15; matrix products, arithmetic and copies ran while one was open for 6% -> 5% of each run, Pallas kernels for 13% -> 13%
where the time goes in v3:
time: 158 us; the launch traced here: 157 us
  starting transfers between devices  54.4 us (34%)
  waiting for transfers between devices  49.2 us (31%)
  local copies, waits for them, and re-layouts  23.3 us (15%)
  Pallas kernels  21.1 us (13%)
  other arithmetic  8.37 us (5%)
    ppermute x18, starting transfers between devices, move(): lax.ppermute(x, 'wide', [(2 * s + c, 2 * d + c) for s, d in pairs for c i...  47 us
    ppermute x18, waiting for transfers between devices, move(): lax.ppermute(x, 'wide', [(2 * s + c, 2 * d + c) for s, d in pairs for c i...  37.5 us
    unnamed x52, local copies, waits for them, and re-layouts  21.7 us
    pallas_call x1, Pallas kernels, body(): call(functools.partial(backward_kernel, n_slots), 'backward', [SMEM] + [A...  8.57 us
    ppermute x4, waiting for transfers between devices, flip(): return lax.ppermute(x, 'node', [(i, i ^ j) for i in range(n_node)])  7.82 us
    pallas_call x1, Pallas kernels, body(): call(functools.partial(mixed_kernel, n_slots), 'mixed', [SMEM] + [ANY] *...  5.84 us
    ppermute x4, starting transfers between devices, flip(): return lax.ppermute(x, 'node', [(i, i ^ j) for i in range(n_node)])  5.2 us
    pallas_call x1, Pallas kernels, body(): call(functools.partial(terms_kernel, n_node), 'terms', [SMEM] + [VMEM] *...  3.56 us
  transfers between devices with their start and end apart: 31, of which 15 were waited for; matrix products, arithmetic and copies ran while one was open for 5% of the time, Pallas kernels for 13%

profile of v3, /device:TPU:0, one launch (start us, length us, event | category | flops | bytes accessed | tf_op | source)
XLA Modules:
  0.0 157.4 jit_solution(17866570066481373573)
XLA Ops:
  0.7 1.3 slice_bitcast_fusion.11
  2.6 1.2 collective-permute-done
  4.8 3.7 %collective-permute-start.1 = (bf16[640,256]{1,0:T(8,128)(2,1)S(1)}, bf16[640,256]{1,0:T(8,128)(2,1)}, u32[]{:S(2)}, u32[]{:S(2)}) collective-permute-start(bf16[640,256]{1,0:T(8,128)(2,1)S(1)} %pad_maximum_fusion.5.rest_0_), channel_id=1, source_target_pairs={{0,16},{4,20},{8,24},{12,28},{16,0},{20,4},{24,8},{28,12},{1,17},{... | collective-permute-start | bytes 983048 | tf_op jit(solution)/shard_map/ppermute | solution.py:208
  8.5 1.3 collective-permute-start.2
  9.8 14.2 %collective-permute-done.1.rest_1_ = bf16[640,256]{1,0:T(8,128)(2,1)} collective-permute-done((bf16[640,256]{1,0:T(8,128)(2,1)S(1)}, bf16[640,256]{1,0:T(8,128)(2,1)}, u32[]{:S(2)}, u32[]{:S(2)}) %collective-permute-start.1) | collective-permute-done | bytes 327712 | tf_op jit(solution)/shard_map/ppermute | solution.py:208
  24.0 2.0 %collective-permute-done.2.rest_2_ = bf16[640,256]{1,0:T(8,128)(2,1)S(1)} collective-permute-done((bf16[640,256]{1,0:T(8,128)(2,1)S(1)}, bf16[640,256]{1,0:T(8,128)(2,1)S(1)}, u32[]{:S(2)}, u32[]{:S(2)}) %collective-permute-start.2) | collective-permute-done | bytes 327712 | tf_op jit(solution)/shard_map/ppermute | solution.py:208
  26.0 0.7 copy-done.18
  26.7 1.0 copy-done.12
  27.7 1.5 copy-done.6
  29.2 1.5 copy-done.2
  30.7 1.5 collective-permute-start.7
  32.1 0.7 collective-permute-start.8
  32.8 1.3 collective-permute-start.6
  34.2 4.3 %collective-permute-start.9 = (bf16[640,256]{1,0:T(8,128)(2,1)S(1)}, bf16[640,256]{1,0:T(8,128)(2,1)}, u32[]{:S(2)}, u32[]{:S(2)}) collective-permute-start(bf16[640,256]{1,0:T(8,128)(2,1)S(1)} %pad_maximum_fusion.6.rest_0_), channel_id=1, source_target_pairs={{0,16},{4,20},{8,24},{12,28},{16,0},{20,4},{24,8},{28,12},{1,17},{... | collective-permute-start | bytes 983048 | tf_op jit(solution)/shard_map/ppermute | solution.py:208
  38.5 1.3 collective-permute-start.10
  40.3 0.7 copy-done.20
  41.0 0.7 copy-done.22
  41.7 5.5 %collective-permute-done.6.rest_3_ = bf16[640,256]{1,0:T(8,128)(2,1)S(1)} collective-permute-done((bf16[640,256]{1,0:T(8,128)(2,1)}, bf16[640,256]{1,0:T(8,128)(2,1)S(1)}, u32[]{:S(2)}, u32[]{:S(2)}) %collective-permute-start.6) | collective-permute-done | bytes 327712 | tf_op jit(solution)/shard_map/ppermute | solution.py:208
  47.2 0.7 copy-done.24
  47.9 1.7 %copy-done.4 = bf16[2,2,128,2560]{3,2,1,0:T(8,128)(2,1)S(1)} copy-done((bf16[2,2,128,2560]{3,2,1,0:T(8,128)(2,1)S(1)}, bf16[2,2,128,2560]{3,2,1,0:T(8,128)(2,1)}, u32[]{:S(2)}) %copy-start.4) | copy-done | bytes 2621464
  49.7 1.7 %copy-done.7 = bf16[512,2560]{1,0:T(8,128)(2,1)S(1)} copy-done((bf16[512,2560]{1,0:T(8,128)(2,1)S(1)}, bf16[512,2560]{1,0:T(8,128)(2,1)}, u32[]{:S(2)}) %copy-start.7) | copy-done | bytes 2621464
  51.4 1.2 copy-done.10
  52.6 1.2 copy-done.13
  53.9 1.0 copy-done.19
  54.8 1.0 copy-done.21
  55.8 1.0 copy-done.23
  56.8 1.0 copy-done.25
  57.8 8.6 %backward.1 = (bf16[2560,256]{1,0:T(8,128)(2,1)}, bf16[2,320,256]{2,1,0:T(8,128)(2,1)S(1)}, bf16[2,320,256]{2,1,0:T(8,128)(2,1)}, bf16[2,320,256]{2,1,0:T(8,128)...) custom-call(s32[18]{0:T(128)S(1)} %stack.123.idx, bf16[512,2560]{1,0:T(8,128)(2,1)S(1)} %bitcast.75, ...), custom_call_target="tpu_custom_call" | custom-call | bytes 1024 | tf_op jit(solution)/shard_map/backward/pallas_call | solution.py:339
  66.3 0.7 copy-done.15
  67.1 9.4 %collective-permute-start.14 = (bf16[2,320,256]{2,1,0:T(8,128)(2,1)}, bf16[2,320,256]{2,1,0:T(8,128)(2,1)}, u32[]{:S(2)}, u32[]{:S(2)}) collective-permute-start(bf16[2,320,256]{2,1,0:T(8,128)(2,1)} %get-tuple-element.64), channel_id=1, source_target_pairs={{0,8},{4,12},{8,16},{12,20},{16,24},{20,28},{1,9},{5,13},{9,17},{1... | collective-permute-start | bytes 983048 | tf_op jit(solution)/shard_map/ppermute | solution.py:208
  76.5 1.3 collective-permute-start.15
  77.8 1.3 collective-permute-start.11
  79.1 5.3 %collective-permute-start.12 = (bf16[640,256]{1,0:T(8,128)(2,1)S(1)}, bf16[640,256]{1,0:T(8,128)(2,1)}, u32[]{:S(2)}, u32[]{:S(2)}) collective-permute-start(bf16[640,256]{1,0:T(8,128)(2,1)S(1)} %pad_maximum_fusion.6.rest_0_), channel_id=1, source_target_pairs={{0,8},{4,12},{8,16},{12,20},{1,9},{5,13},{9,17},{13,21},{2,10},{6,... | collective-permute-start | bytes 983048 | tf_op jit(solution)/shard_map/ppermute | solution.py:208
  84.4 1.4 collective-permute-start.13
  85.8 1.8 %add_convert_fusion.1 = bf16[2,320,256]{2,1,0:T(8,128)(2,1)} fusion(bf16[2,320,256]{2,1,0:T(8,128)(2,1)} %copy-done.17, bf16[2,320,256]{2,1,0:T(8,128)(2,1)} %collective-permute-done.14, bf16[2,320,256]{2,1,0:T(8,128)(2,1)} %collective-permute-done.15, pred[]{:T(512)S(6)} %eq.14, pred[]{:T(512)S(6)} %eq.13), kind=kLoop, calls=%fused_computation.18 | loop fusion | flops 983040 | bytes 1310722 | tf_op jit(solution)/shard_map/convert_element_type | solution.py:264
  87.6 1.5 collective-permute-done.11.rest_3_
  89.2 6.3 %collective-permute-start.22 = (bf16[2,320,256]{2,1,0:T(8,128)(2,1)}, bf16[2,320,256]{2,1,0:T(8,128)(2,1)}, u32[]{:S(2)}, u32[]{:S(2)}) collective-permute-start(bf16[2,320,256]{2,1,0:T(8,128)(2,1)} %get-tuple-element.85), channel_id=1, source_target_pairs={{0,8},{4,12},{24,16},{28,20},{1,9},{5,13},{25,17},{29,21},{2,10},{... | collective-permute-start | bytes 983048 | tf_op jit(solution)/shard_map/ppermute | solution.py:208
  95.7 1.7 %copy-done.3 = bf16[512,2560]{1,0:T(8,128)(2,1)S(1)} copy-done((bf16[512,2560]{1,0:T(8,128)(2,1)S(1)}, bf16[512,2560]{1,0:T(8,128)(2,1)}, u32[]{:S(2)}) %copy-start.3) | copy-done | bytes 2621464
  97.4 1.2 copy-done.11
  98.7 1.2 copy-done.14
  99.9 5.8 %mixed.1 = (bf16[512,256]{1,0:T(8,128)(2,1)S(1)}, bf16[512,256]{1,0:T(8,128)(2,1)S(1)}) custom-call(s32[13]{0:T(128)S(1)} %stack.113.idx, bf16[512,2560]{1,0:T(8,128)(2,1)S(1)} %bitcast.73, bf16[512,2560]{1,0:T(8,128)(2,1)S(1)} %copy-done.3, bf16[4,8,128,128]{3,2,1,0:T(8,128)(2,1)S(1)} %bitcast.79, bf16[4,8,128,128]{3,2,1,0:T(8,128)(2,1)S(1)} %copy-done.14, ...), custom_call_target="tpu_custom_call" | custom-call | bytes 1024 | tf_op jit(solution)/shard_map/mixed/pallas_call | solution.py:358
  106.0 3.1 %grad_out.1 = (bf16[2,320,256]{2,1,0:T(8,128)(2,1)S(1)}, bf16[2,320,256]{2,1,0:T(8,128)(2,1)S(1)}, bf16[2,320,256]{2,1,0:T(8,128)(2,1)S(1)}, bf16[2,320,256]{2,1,0:T(8,128)(2,1)S(1)}, bf16[2,320,256]{2,1,0:T(8,128)(2,1)S(1)}) custom-call(s32[6]{0:T(128)S(1)} %stack.124.idx, bf16[512,2560]{1,0:T(8,128)(2,1)S(1)} %bitcast.76, bf16[512,2560]{1,0:T(8,128)(2,1)S(1)} %copy-done.8, ...), custom_call_target="tpu_custom_call" | custom-call | bytes 1024 | tf_op jit(solution)/shard_map/grad_out/pallas_call | solution.py:367
  109.2 4.4 %collective-permute-done.23 = bf16[2,320,256]{2,1,0:T(8,128)(2,1)} collective-permute-done((bf16[2,320,256]{2,1,0:T(8,128)(2,1)}, bf16[2,320,256]{2,1,0:T(8,128)(2,1)}, u32[]{:S(2)}, u32[]{:S(2)}) %collective-permute-start.23) | collective-permute-done | bytes 327712 | tf_op jit(solution)/shard_map/ppermute | solution.py:208
  113.6 1.4 convert_add_fusion.1
  115.0 2.0 %collective-permute-start.25 = (bf16[2,320,256]{2,1,0:T(8,128)(2,1)S(1)}, bf16[2,320,256]{2,1,0:T(8,128)(2,1)}, u32[]{:S(2)}, u32[]{:S(2)}) collective-permute-start(bf16[2,320,256]{2,1,0:T(8,128)(2,1)S(1)} %get-tuple-element.88), channel_id=1, source_target_pairs={{0,8},{4,12},{8,16},{12,20},{16,24},{20,28},{1,9},{5,13},{9,17},{1... | collective-permute-start | bytes 983048 | tf_op jit(solution)/shard_map/ppermute | solution.py:208
  117.0 1.5 collective-permute-start.26
  118.7 3.6 %terms.1 = (bf16[2,256,640]{2,1,0:T(8,128)(2,1)S(1)}, bf16[2,256,640]{2,1,0:T(8,128)(2,1)S(1)}, bf16[4,256,640]{2,1,0:T(8,128)(2,1)S(1)}) custom-call(s32[4]{0:T(128)S(1)} %pad_add_fusion.idx, bf16[512,256]{1,0:T(8,128)(2,1)S(1)} %get-tuple-element.72.mixed_o, bf16[512,256]{1,0:T(8,128)(2,1)S(1)} %collective-permute-done.16.mixed_r, ...), custom_call_target="tpu_custom_call" | custom-call | bytes 1024 | tf_op jit(solution)/shard_map/terms/pallas_call | solution.py:381
  122.2 0.8 collective-permute-done.25
  123.1 4.9 %collective-permute-done.26 = bf16[2,320,256]{2,1,0:T(8,128)(2,1)} collective-permute-done((bf16[2,320,256]{2,1,0:T(8,128)(2,1)S(1)}, bf16[2,320,256]{2,1,0:T(8,128)(2,1)}, u32[]{:S(2)}, u32[]{:S(2)}) %collective-permute-start.26) | collective-permute-done | bytes 327712 | tf_op jit(solution)/shard_map/ppermute | solution.py:208
  128.0 1.9 %collective-permute-start.27 = (bf16[2,320,256]{2,1,0:T(8,128)(2,1)S(1)}, bf16[2,320,256]{2,1,0:T(8,128)(2,1)S(1)}, u32[]{:S(2)}, u32[]{:S(2)}) collective-permute-start(bf16[2,320,256]{2,1,0:T(8,128)(2,1)S(1)} %get-tuple-element.93), channel_id=1, source_target_pairs={{0,8},{4,12},{24,16},{28,20},{1,9},{5,13},{25,17},{29,21},{2,10},{... | collective-permute-start | bytes 983048 | tf_op jit(solution)/shard_map/ppermute | solution.py:208
  130.1 0.9 pad_maximum_fusion.1
  131.0 1.5 collective-permute-start.18
  132.6 1.6 %collective-permute-start.20 = (bf16[2,256,640]{2,1,0:T(8,128)(2,1)S(1)}, bf16[2,256,640]{2,1,0:T(8,128)(2,1)S(1)}, u32[]{:S(2)}, u32[]{:S(2)}) collective-permute-start(bf16[2,256,640]{2,1,0:T(8,128)(2,1)S(1)} %get-tuple-element.78), channel_id=1, source_target_pairs={{0,2},{1,3},{2,0},{3,1},{4,6},{5,7},{6,4},{7,5},{8,10},{9,11},{10,... | collective-permute-start | bytes 1966088 | tf_op jit(solution)/shard_map/ppermute | solution.py:216
  134.2 1.4 collective-permute-done.27
  135.6 1.3 add_convert_fusion
  137.1 2.6 %collective-permute-start.28 = (bf16[320,256]{1,0:T(8,128)(2,1)S(1)}, bf16[320,256]{1,0:T(8,128)(2,1)S(1)}, u32[]{:S(2)}, u32[]{:S(2)}) collective-permute-start(bf16[320,256]{1,0:T(8,128)(2,1)S(1)} %get-tuple-element.107), channel_id=1, source_target_pairs={{0,16},{4,20},{8,24},{12,28},{16,0},{20,4},{24,8},{28,12},{1,17},{... | collective-permute-start | bytes 491528 | tf_op jit(solution)/shard_map/ppermute | solution.py:208
  139.9 6.0 %collective-permute-done.18 = bf16[2,256,640]{2,1,0:T(8,128)(2,1)S(1)} collective-permute-done((bf16[2,256,640]{2,1,0:T(8,128)(2,1)S(1)}, bf16[2,256,640]{2,1,0:T(8,128)(2,1)S(1)}, u32[]{:S(2)}, u32[]{:S(2)}) %collective-permute-start.18) | collective-permute-done | bytes 655392 | tf_op jit(solution)/shard_map/ppermute | solution.py:216
  145.9 1.4 collective-permute-done.20
  147.6 1.6 %collective-permute-start.19 = (bf16[256,640]{1,0:T(8,128)(2,1)S(1)}, bf16[256,640]{1,0:T(8,128)(2,1)S(1)}, u32[]{:S(2)}, u32[]{:S(2)}) collective-permute-start(bf16[256,640]{1,0:T(8,128)(2,1)S(1)} %get-tuple-element.97), channel_id=1, source_target_pairs={{0,2},{1,3},{2,0},{3,1},{4,6},{5,7},{6,4},{7,5},{8,10},{9,11},{10,... | collective-permute-start | bytes 983048 | tf_op jit(solution)/shard_map/ppermute | solution.py:216
  149.2 0.5 collective-permute-start.21
  149.7 2.3 %collective-permute-done.28 = bf16[320,256]{1,0:T(8,128)(2,1)S(1)} collective-permute-done((bf16[320,256]{1,0:T(8,128)(2,1)S(1)}, bf16[320,256]{1,0:T(8,128)(2,1)S(1)}, u32[]{:S(2)}, u32[]{:S(2)}) %collective-permute-start.28) | collective-permute-done | bytes 163872 | tf_op jit(solution)/shard_map/ppermute | solution.py:208
  152.0 2.7 %collective-permute-done.30 = bf16[320,256]{1,0:T(8,128)(2,1)S(1)} collective-permute-done((bf16[320,256]{1,0:T(8,128)(2,1)S(1)}, bf16[320,256]{1,0:T(8,128)(2,1)S(1)}, u32[]{:S(2)}, u32[]{:S(2)}) %collective-permute-start.30) | collective-permute-done | bytes 163872 | tf_op jit(solution)/shard_map/ppermute | solution.py:279
  154.8 0.9 pad_maximum_fusion.2
  156.5 0.9 pad_maximum_fusion
  (80 shorter events, 4.6 us)
Async XLA Ops:
  0.6 3.8 %copy-start.9 = (bf16[2,2,8,128,128]{4,3,2,1,0:T(8,128)(2,1)S(1)}, bf16[2,2,8,128,128]{4,3,2,1,0:T(8,128)(2,1)}, u32[]{:S(2)}) copy-start(bf16[2,2,8,128,128]{4,3,2,1,0:T(8,128)(2,1)} %param.6) | copy-start | bytes 3145732
  1.9 2.4 %copy-start = (bf16[2,2,128,2560]{3,2,1,0:T(8,128)(2,1)S(1)}, bf16[2,2,128,2560]{3,2,1,0:T(8,128)(2,1)}, u32[]{:S(2)}) copy-start(bf16[2,2,128,2560]{3,2,1,0:T(8,128)(2,1)} %param.5) | copy-start | bytes 7864324
  2.0 1.8 %collective-permute-start = (bf16[2,320,256]{2,1,0:T(8,128)(2,1)S(1)}, bf16[2,320,256]{2,1,0:T(8,128)(2,1)S(1)}, u32[]{:S(2)}, u32[]{:S(2)}) collective-permute-start(bf16[2,320,256]{2,1,0:T(8,128)(2,1)S(1)} %get-tuple-element.106), channel_id=1, source_target_pairs={{0,4},{4,0},{8,12},{12,8},{16,20},{20,16},{24,28},{28,24},{1,5},{5... | collective-permute-start | bytes 983048 | tf_op jit(solution)/shard_map/ppermute | solution.py:213
  3.9 23.9 %collective-permute-start.3 = (bf16[512,2560]{1,0:T(8,128)(2,1)}, bf16[512,2560]{1,0:T(8,128)(2,1)S(1)}, u32[]{:S(2)}, u32[]{:S(2)}) collective-permute-start(bf16[512,2560]{1,0:T(8,128)(2,1)} %bitcast.74), channel_id=1, source_target_pairs={{0,4},{4,0},{8,12},{12,8},{16,20},{20,16},{24,28},{28,24},{1,5},{5... | collective-permute-start | bytes 7864328 | tf_op jit(solution)/shard_map/ppermute | solution.py:213
  4.3 24.9 %collective-permute-start.5 = (bf16[512,2560]{1,0:T(8,128)(2,1)S(1)}, bf16[512,2560]{1,0:T(8,128)(2,1)S(1)}, u32[]{:S(2)}, u32[]{:S(2)}) collective-permute-start(bf16[512,2560]{1,0:T(8,128)(2,1)S(1)} %bitcast.72), channel_id=1, source_target_pairs={{0,4},{4,0},{8,12},{12,8},{16,20},{20,16},{24,28},{28,24},{1,5},{5... | collective-permute-start | bytes 7864328 | tf_op jit(solution)/shard_map/ppermute | solution.py:213
  4.4 22.3 %collective-permute-start.4 = (bf16[4,8,128,128]{3,2,1,0:T(8,128)(2,1)S(1)}, bf16[4,8,128,128]{3,2,1,0:T(8,128)(2,1)S(1)}, u32[]{:S(2)}, u32[]{:S(2)}) collective-permute-start(bf16[4,8,128,128]{3,2,1,0:T(8,128)(2,1)S(1)} %bitcast.77), channel_id=1, source_target_pairs={{0,4},{4,0},{8,12},{12,8},{16,20},{20,16},{24,28},{28,24},{1,5},{5... | collective-permute-start | bytes 3145736 | tf_op jit(solution)/shard_map/ppermute | solution.py:213
  4.8 19.2 %collective-permute-start.1 = (bf16[640,256]{1,0:T(8,128)(2,1)S(1)}, bf16[640,256]{1,0:T(8,128)(2,1)}, u32[]{:S(2)}, u32[]{:S(2)}) collective-permute-start(bf16[640,256]{1,0:T(8,128)(2,1)S(1)} %pad_maximum_fusion.5.rest_0_), channel_id=1, source_target_pairs={{0,16},{4,20},{8,24},{12,28},{16,0},{20,4},{24,8},{28,12},{1,17},{... | collective-permute-start | bytes 983048 | tf_op jit(solution)/shard_map/ppermute | solution.py:208
  8.5 17.4 %collective-permute-start.2 = (bf16[640,256]{1,0:T(8,128)(2,1)S(1)}, bf16[640,256]{1,0:T(8,128)(2,1)S(1)}, u32[]{:S(2)}, u32[]{:S(2)}) collective-permute-start(bf16[640,256]{1,0:T(8,128)(2,1)S(1)} %pad_maximum_fusion.5.rest_0_), channel_id=1, source_target_pairs={{8,0},{12,4},{16,24},{20,28},{9,1},{13,5},{17,25},{21,29},{10,2},{... | collective-permute-start | bytes 983048 | tf_op jit(solution)/shard_map/ppermute | solution.py:208
  26.0 0.7 copy-start.18
  26.7 1.0 copy-start.12
  27.7 1.5 copy-start.6
  29.2 1.5 copy-start.2
  30.7 9.6 %collective-permute-start.7 = (bf16[640,256]{1,0:T(8,128)(2,1)S(1)}, bf16[640,256]{1,0:T(8,128)(2,1)S(1)}, u32[]{:S(2)}, u32[]{:S(2)}) collective-permute-start(bf16[640,256]{1,0:T(8,128)(2,1)S(1)} %pad_maximum_fusion.5.rest_0_), channel_id=1, source_target_pairs={{0,8},{4,12},{8,16},{12,20},{1,9},{5,13},{9,17},{13,21},{2,10},{6,... | collective-permute-start | bytes 983048 | tf_op jit(solution)/shard_map/ppermute | solution.py:208
  32.1 8.9 %collective-permute-start.8 = (bf16[640,256]{1,0:T(8,128)(2,1)S(1)}, bf16[640,256]{1,0:T(8,128)(2,1)S(1)}, u32[]{:S(2)}, u32[]{:S(2)}) collective-permute-start(bf16[640,256]{1,0:T(8,128)(2,1)S(1)} %pad_maximum_fusion.5.rest_0_), channel_id=1, source_target_pairs={{24,16},{28,20},{16,8},{20,12},{25,17},{29,21},{17,9},{21,13},{26,... | collective-permute-start | bytes 983048 | tf_op jit(solution)/shard_map/ppermute | solution.py:208
  32.8 14.4 %collective-permute-start.6 = (bf16[640,256]{1,0:T(8,128)(2,1)}, bf16[640,256]{1,0:T(8,128)(2,1)S(1)}, u32[]{:S(2)}, u32[]{:S(2)}) collective-permute-start(bf16[640,256]{1,0:T(8,128)(2,1)} %collective-permute-done.1.rest_1_), channel_id=1, source_target_pairs={{16,24},{20,28},{8,0},{12,4},{17,25},{21,29},{9,1},{13,5},{18,26},... | collective-permute-start | bytes 983048 | tf_op jit(solution)/shard_map/ppermute | solution.py:208
  34.2 43.6 %collective-permute-start.9 = (bf16[640,256]{1,0:T(8,128)(2,1)S(1)}, bf16[640,256]{1,0:T(8,128)(2,1)}, u32[]{:S(2)}, u32[]{:S(2)}) collective-permute-start(bf16[640,256]{1,0:T(8,128)(2,1)S(1)} %pad_maximum_fusion.6.rest_0_), channel_id=1, source_target_pairs={{0,16},{4,20},{8,24},{12,28},{16,0},{20,4},{24,8},{28,12},{1,17},{... | collective-permute-start | bytes 983048 | tf_op jit(solution)/shard_map/ppermute | solution.py:208
  38.5 45.9 %collective-permute-start.10 = (bf16[640,256]{1,0:T(8,128)(2,1)S(1)}, bf16[640,256]{1,0:T(8,128)(2,1)}, u32[]{:S(2)}, u32[]{:S(2)}) collective-permute-start(bf16[640,256]{1,0:T(8,128)(2,1)S(1)} %pad_maximum_fusion.6.rest_0_), channel_id=1, source_target_pairs={{8,0},{12,4},{16,24},{20,28},{9,1},{13,5},{17,25},{21,29},{10,2},{... | collective-permute-start | bytes 983048 | tf_op jit(solution)/shard_map/ppermute | solution.py:208
  40.3 0.7 copy-start.20
  41.0 0.7 copy-start.22
  47.2 0.7 copy-start.24
  47.9 1.7 %copy-start.4 = (bf16[2,2,128,2560]{3,2,1,0:T(8,128)(2,1)S(1)}, bf16[2,2,128,2560]{3,2,1,0:T(8,128)(2,1)}, u32[]{:S(2)}) copy-start(bf16[2,2,128,2560]{3,2,1,0:T(8,128)(2,1)} %param.7) | copy-start | bytes 7864324
  49.7 1.7 %copy-start.7 = (bf16[512,2560]{1,0:T(8,128)(2,1)S(1)}, bf16[512,2560]{1,0:T(8,128)(2,1)}, u32[]{:S(2)}) copy-start(bf16[512,2560]{1,0:T(8,128)(2,1)} %copy-done.6) | copy-start | bytes 7864324
  51.4 1.2 copy-start.10
  52.6 1.2 copy-start.13
  53.9 1.0 copy-start.19
  54.8 1.0 copy-start.21
  55.8 1.0 copy-start.23
  56.8 1.0 copy-start.25
  57.8 37.9 %copy-start.1 = (bf16[2,2,128,2560]{3,2,1,0:T(8,128)(2,1)S(1)}, bf16[2,2,128,2560]{3,2,1,0:T(8,128)(2,1)}, u32[]{:S(2)}) copy-start(bf16[2,2,128,2560]{3,2,1,0:T(8,128)(2,1)} %param.5) | copy-start | bytes 7864324
  66.3 0.7 copy-start.15
  67.1 17.3 %copy-start.17 = (bf16[2,320,256]{2,1,0:T(8,128)(2,1)}, bf16[2,320,256]{2,1,0:T(8,128)(2,1)S(1)}, u32[]{:S(2)}) copy-start(bf16[2,320,256]{2,1,0:T(8,128)(2,1)S(1)} %get-tuple-element.63) | copy-start | bytes 983044
  67.1 18.7 %collective-permute-start.14 = (bf16[2,320,256]{2,1,0:T(8,128)(2,1)}, bf16[2,320,256]{2,1,0:T(8,128)(2,1)}, u32[]{:S(2)}, u32[]{:S(2)}) collective-permute-start(bf16[2,320,256]{2,1,0:T(8,128)(2,1)} %get-tuple-element.64), channel_id=1, source_target_pairs={{0,8},{4,12},{8,16},{12,20},{16,24},{20,28},{1,9},{5,13},{9,17},{1... | collective-permute-start | bytes 983048 | tf_op jit(solution)/shard_map/ppermute | solution.py:208
  76.5 9.3 %collective-permute-start.15 = (bf16[2,320,256]{2,1,0:T(8,128)(2,1)}, bf16[2,320,256]{2,1,0:T(8,128)(2,1)}, u32[]{:S(2)}, u32[]{:S(2)}) collective-permute-start(bf16[2,320,256]{2,1,0:T(8,128)(2,1)} %get-tuple-element.65), channel_id=1, source_target_pairs={{24,16},{28,20},{16,8},{20,12},{8,0},{12,4},{25,17},{29,21},{17,9}... | collective-permute-start | bytes 983048 | tf_op jit(solution)/shard_map/ppermute | solution.py:208
  77.8 11.4 %collective-permute-start.11 = (bf16[640,256]{1,0:T(8,128)(2,1)}, bf16[640,256]{1,0:T(8,128)(2,1)S(1)}, u32[]{:S(2)}, u32[]{:S(2)}) collective-permute-start(bf16[640,256]{1,0:T(8,128)(2,1)} %collective-permute-done.9.rest_1_), channel_id=1, source_target_pairs={{16,24},{20,28},{8,0},{12,4},{17,25},{21,29},{9,1},{13,5},{18,26},... | collective-permute-start | bytes 983048 | tf_op jit(solution)/shard_map/ppermute | solution.py:208
  79.1 10.1 %collective-permute-start.12 = (bf16[640,256]{1,0:T(8,128)(2,1)S(1)}, bf16[640,256]{1,0:T(8,128)(2,1)}, u32[]{:S(2)}, u32[]{:S(2)}) collective-permute-start(bf16[640,256]{1,0:T(8,128)(2,1)S(1)} %pad_maximum_fusion.6.rest_0_), channel_id=1, source_target_pairs={{0,8},{4,12},{8,16},{12,20},{1,9},{5,13},{9,17},{13,21},{2,10},{6,... | collective-permute-start | bytes 983048 | tf_op jit(solution)/shard_map/ppermute | solution.py:208
  84.4 4.8 %collective-permute-start.13 = (bf16[640,256]{1,0:T(8,128)(2,1)S(1)}, bf16[640,256]{1,0:T(8,128)(2,1)}, u32[]{:S(2)}, u32[]{:S(2)}) collective-permute-start(bf16[640,256]{1,0:T(8,128)(2,1)S(1)} %pad_maximum_fusion.6.rest_0_), channel_id=1, source_target_pairs={{24,16},{28,20},{16,8},{20,12},{25,17},{29,21},{17,9},{21,13},{26,... | collective-permute-start | bytes 983048 | tf_op jit(solution)/shard_map/ppermute | solution.py:208
  89.2 29.5 %collective-permute-start.17 = (bf16[2560,256]{1,0:T(8,128)(2,1)}, bf16[2560,256]{1,0:T(8,128)(2,1)}, u32[]{:S(2)}, u32[]{:S(2)}) collective-permute-start(bf16[2560,256]{1,0:T(8,128)(2,1)} %get-tuple-element.75.w_o), channel_id=1, source_target_pairs={{0,4},{4,0},{8,12},{12,8},{16,20},{20,16},{24,28},{28,24},{1,5},{5... | collective-permute-start | bytes 3932168 | tf_op jit(solution)/shard_map/ppermute | solution.py:213
  89.2 20.0 %collective-permute-start.22 = (bf16[2,320,256]{2,1,0:T(8,128)(2,1)}, bf16[2,320,256]{2,1,0:T(8,128)(2,1)}, u32[]{:S(2)}, u32[]{:S(2)}) collective-permute-start(bf16[2,320,256]{2,1,0:T(8,128)(2,1)} %get-tuple-element.85), channel_id=1, source_target_pairs={{0,8},{4,12},{24,16},{28,20},{1,9},{5,13},{25,17},{29,21},{2,10},{... | collective-permute-start | bytes 983048 | tf_op jit(solution)/shard_map/ppermute | solution.py:208
  95.5 18.1 %collective-permute-start.23 = (bf16[2,320,256]{2,1,0:T(8,128)(2,1)}, bf16[2,320,256]{2,1,0:T(8,128)(2,1)}, u32[]{:S(2)}, u32[]{:S(2)}) collective-permute-start(bf16[2,320,256]{2,1,0:T(8,128)(2,1)} %add_convert_fusion.1), channel_id=1, source_target_pairs={{0,16},{4,20},{8,24},{12,28},{16,0},{20,4},{24,8},{28,12},{1,17},{... | collective-permute-start | bytes 983048 | tf_op jit(solution)/shard_map/ppermute | solution.py:208
  95.7 1.7 %copy-start.3 = (bf16[512,2560]{1,0:T(8,128)(2,1)S(1)}, bf16[512,2560]{1,0:T(8,128)(2,1)}, u32[]{:S(2)}) copy-start(bf16[512,2560]{1,0:T(8,128)(2,1)} %copy-done.2) | copy-start | bytes 7864324
  97.4 1.2 copy-start.11
  98.7 1.2 copy-start.14
  99.9 6.1 %copy-start.5 = (bf16[2,2,128,2560]{3,2,1,0:T(8,128)(2,1)S(1)}, bf16[2,2,128,2560]{3,2,1,0:T(8,128)(2,1)}, u32[]{:S(2)}) copy-start(bf16[2,2,128,2560]{3,2,1,0:T(8,128)(2,1)} %param.7) | copy-start | bytes 7864324
  99.9 6.1 %copy-start.8 = (bf16[512,2560]{1,0:T(8,128)(2,1)S(1)}, bf16[512,2560]{1,0:T(8,128)(2,1)}, u32[]{:S(2)}) copy-start(bf16[512,2560]{1,0:T(8,128)(2,1)} %copy-done.6) | copy-start | bytes 7864324
  105.7 9.2 %collective-permute-start.16 = (bf16[512,256]{1,0:T(8,128)(2,1)S(1)}, bf16[512,256]{1,0:T(8,128)(2,1)S(1)}, u32[]{:S(2)}, u32[]{:S(2)}) collective-permute-start(bf16[512,256]{1,0:T(8,128)(2,1)S(1)} %get-tuple-element.73.mixed_s), channel_id=1, source_target_pairs={{0,4},{4,0},{8,12},{12,8},{16,20},{20,16},{24,28},{28,24},{1,5},{5... | collective-permute-start | bytes 786440 | tf_op jit(solution)/shard_map/ppermute | solution.py:213
  106.0 7.6 %copy-start.16 = (bf16[2,320,256]{2,1,0:T(8,128)(2,1)S(1)}, bf16[2,320,256]{2,1,0:T(8,128)(2,1)}, u32[]{:S(2)}) copy-start(bf16[2,320,256]{2,1,0:T(8,128)(2,1)} %copy-done.15) | copy-start | bytes 983044
  115.0 8.1 %collective-permute-start.25 = (bf16[2,320,256]{2,1,0:T(8,128)(2,1)S(1)}, bf16[2,320,256]{2,1,0:T(8,128)(2,1)}, u32[]{:S(2)}, u32[]{:S(2)}) collective-permute-start(bf16[2,320,256]{2,1,0:T(8,128)(2,1)S(1)} %get-tuple-element.88), channel_id=1, source_target_pairs={{0,8},{4,12},{8,16},{12,20},{16,24},{20,28},{1,9},{5,13},{9,17},{1... | collective-permute-start | bytes 983048 | tf_op jit(solution)/shard_map/ppermute | solution.py:208
  117.0 11.0 %collective-permute-start.26 = (bf16[2,320,256]{2,1,0:T(8,128)(2,1)S(1)}, bf16[2,320,256]{2,1,0:T(8,128)(2,1)}, u32[]{:S(2)}, u32[]{:S(2)}) collective-permute-start(bf16[2,320,256]{2,1,0:T(8,128)(2,1)S(1)} %get-tuple-element.89), channel_id=1, source_target_pairs={{24,16},{28,20},{16,8},{20,12},{8,0},{12,4},{25,17},{29,21},{17,9}... | collective-permute-start | bytes 983048 | tf_op jit(solution)/shard_map/ppermute | solution.py:208
  118.5 11.5 %collective-permute-start.24 = (f32[320,256]{1,0:T(8,128)S(1)}, f32[320,256]{1,0:T(8,128)S(1)}, u32[]{:S(2)}, u32[]{:S(2)}) collective-permute-start(f32[320,256]{1,0:T(8,128)S(1)} %slice_bitcast_fusion.2), channel_id=1, source_target_pairs={{0,4},{4,0},{8,12},{12,8},{16,20},{20,16},{24,28},{28,24},{1,5},{5... | collective-permute-start | bytes 983048 | tf_op jit(solution)/shard_map/ppermute | solution.py:213
  128.0 7.6 %collective-permute-start.27 = (bf16[2,320,256]{2,1,0:T(8,128)(2,1)S(1)}, bf16[2,320,256]{2,1,0:T(8,128)(2,1)S(1)}, u32[]{:S(2)}, u32[]{:S(2)}) collective-permute-start(bf16[2,320,256]{2,1,0:T(8,128)(2,1)S(1)} %get-tuple-element.93), channel_id=1, source_target_pairs={{0,8},{4,12},{24,16},{28,20},{1,9},{5,13},{25,17},{29,21},{2,10},{... | collective-permute-start | bytes 983048 | tf_op jit(solution)/shard_map/ppermute | solution.py:208
  131.0 14.9 %collective-permute-start.18 = (bf16[2,256,640]{2,1,0:T(8,128)(2,1)S(1)}, bf16[2,256,640]{2,1,0:T(8,128)(2,1)S(1)}, u32[]{:S(2)}, u32[]{:S(2)}) collective-permute-start(bf16[2,256,640]{2,1,0:T(8,128)(2,1)S(1)} %get-tuple-element.77), channel_id=1, source_target_pairs={{0,1},{1,0},{2,3},{3,2},{4,5},{5,4},{6,7},{7,6},{8,9},{9,8},{10,11... | collective-permute-start | bytes 1966088 | tf_op jit(solution)/shard_map/ppermute | solution.py:216
  132.6 14.7 %collective-permute-start.20 = (bf16[2,256,640]{2,1,0:T(8,128)(2,1)S(1)}, bf16[2,256,640]{2,1,0:T(8,128)(2,1)S(1)}, u32[]{:S(2)}, u32[]{:S(2)}) collective-permute-start(bf16[2,256,640]{2,1,0:T(8,128)(2,1)S(1)} %get-tuple-element.78), channel_id=1, source_target_pairs={{0,2},{1,3},{2,0},{3,1},{4,6},{5,7},{6,4},{7,5},{8,10},{9,11},{10,... | collective-permute-start | bytes 1966088 | tf_op jit(solution)/shard_map/ppermute | solution.py:216
  136.9 17.8 %collective-permute-start.29 = (f32[320,256]{1,0:T(8,128)S(1)}, f32[320,256]{1,0:T(8,128)S(1)}, u32[]{:S(2)}, u32[]{:S(2)}) collective-permute-start(f32[320,256]{1,0:T(8,128)S(1)} %slice_bitcast_fusion), channel_id=1, source_target_pairs={{0,4},{4,0},{8,12},{12,8},{16,20},{20,16},{24,28},{28,24},{1,5},{5... | collective-permute-start | bytes 983048 | tf_op jit(solution)/shard_map/ppermute | solution.py:213
  137.1 15.0 %collective-permute-start.28 = (bf16[320,256]{1,0:T(8,128)(2,1)S(1)}, bf16[320,256]{1,0:T(8,128)(2,1)S(1)}, u32[]{:S(2)}, u32[]{:S(2)}) collective-permute-start(bf16[320,256]{1,0:T(8,128)(2,1)S(1)} %get-tuple-element.107), channel_id=1, source_target_pairs={{0,16},{4,20},{8,24},{12,28},{16,0},{20,4},{24,8},{28,12},{1,17},{... | collective-permute-start | bytes 491528 | tf_op jit(solution)/shard_map/ppermute | solution.py:208
  139.6 15.1 %collective-permute-start.30 = (bf16[320,256]{1,0:T(8,128)(2,1)S(1)}, bf16[320,256]{1,0:T(8,128)(2,1)S(1)}, u32[]{:S(2)}, u32[]{:S(2)}) collective-permute-start(bf16[320,256]{1,0:T(8,128)(2,1)S(1)} %get-tuple-element.108), channel_id=1, source_target_pairs={{0,20},{4,16},{8,28},{12,24},{16,4},{20,0},{24,12},{28,8},{1,21},{... | collective-permute-start | bytes 491528 | tf_op jit(solution)/shard_map/ppermute | solution.py:279
  147.6 8.2 %collective-permute-start.19 = (bf16[256,640]{1,0:T(8,128)(2,1)S(1)}, bf16[256,640]{1,0:T(8,128)(2,1)S(1)}, u32[]{:S(2)}, u32[]{:S(2)}) collective-permute-start(bf16[256,640]{1,0:T(8,128)(2,1)S(1)} %get-tuple-element.97), channel_id=1, source_target_pairs={{0,2},{1,3},{2,0},{3,1},{4,6},{5,7},{6,4},{7,5},{8,10},{9,11},{10,... | collective-permute-start | bytes 983048 | tf_op jit(solution)/shard_map/ppermute | solution.py:216
  149.2 7.1 %collective-permute-start.21 = (bf16[256,640]{1,0:T(8,128)(2,1)S(1)}, bf16[256,640]{1,0:T(8,128)(2,1)S(1)}, u32[]{:S(2)}, u32[]{:S(2)}) collective-permute-start(bf16[256,640]{1,0:T(8,128)(2,1)S(1)} %get-tuple-element.98), channel_id=1, source_target_pairs={{0,1},{1,0},{2,3},{3,2},{4,5},{5,4},{6,7},{7,6},{8,9},{9,8},{10,11... | collective-permute-start | bytes 983048 | tf_op jit(solution)/shard_map/ppermute | solution.py:216

commit v4 on v3

--- a/solution.py
+++ b/solution.py
@@ -11,7 +11,7 @@
 HEAD_DIM = 64
 F32 = jnp.float32
 BF16 = jnp.bfloat16
-VMEM_LIMIT = 40 * 1024 * 1024
+VMEM_LIMIT = 56 * 1024 * 1024
 
 
 def dot(a, b, ca=1, cb=0):
@@ -192,7 +192,7 @@
         out_shape=[jax.ShapeDtypeStruct(s, BF16) for s in out_shapes],
         scratch_shapes=scratch,
         compiler_params=pltpu.CompilerParams(vmem_limit_bytes=VMEM_LIMIT),
-        cost_estimate=pl.CostEstimate(flops=0, bytes_accessed=1024, transcendentals=0),
+        cost_estimate=pl.CostEstimate(flops=flops, bytes_accessed=12 << 20, transcendentals=0),
     )
 
 

time: 158 us -> 148 us (0.937)
  local copies, waits for them, and re-layouts: 23.3 us -> 7.48 us
  Pallas kernels: 21.1 us -> 30 us
  other arithmetic: 8.37 us -> 6.6 us
    unnamed x52, local copies, waits for them, and re-layouts: 21.7 us -> 4.1 us
    ppermute x4, waiting for transfers between devices: 7.82 us -> 12 us  [flip(): return lax.ppermute(x, 'node', [(i, i ^ j) for i in range(n_node)])]
    ppermute x18, waiting for transfers between devices: 37.5 us -> 33.7 us  [move(): lax.ppermute(x, 'wide', [(2 * s + c, 2 * d + c) for s, d in pairs for c i...]
    pallas_call x1, Pallas kernels: 3.1 us -> 6.71 us  [body(): call(grad_out_kernel, 'grad_out', [SMEM] + [ANY] * 2 + [VMEM] * 2, send_s...]
    pallas_call x1, Pallas kernels: 5.84 us -> 7.79 us  [body(): call(functools.partial(mixed_kernel, n_slots), 'mixed', [SMEM] + [ANY] *...]
    ppermute x18, starting transfers between devices: 47 us -> 45.3 us  [move(): lax.ppermute(x, 'wide', [(2 * s + c, 2 * d + c) for s, d in pairs for c i...]
    pallas_call x1, Pallas kernels: 8.57 us -> 10.3 us  [body(): call(functools.partial(backward_kernel, n_slots), 'backward', [SMEM] + [A...]
    pallas_call x1, Pallas kernels: 3.56 us -> 5.2 us  [body(): call(functools.partial(terms_kernel, n_node), 'terms', [SMEM] + [VMEM] *...]
  transfers between devices with their start and end apart: 31 -> 31, of which waited for: 15 -> 15; matrix products, arithmetic and copies ran while one was open for 5% -> 5% of each run, Pallas kernels for 13% -> 20%
where the time goes in v4:
time: 148 us
  starting transfers between devices  52.9 us (36%)
  waiting for transfers between devices  49.6 us (34%)
  Pallas kernels  30 us (20%)
  local copies, waits for them, and re-layouts  7.48 us (5%)
  other arithmetic  6.6 us (4%)
    ppermute x18, starting transfers between devices, move(): lax.ppermute(x, 'wide', [(2 * s + c, 2 * d + c) for s, d in pairs for c i...  45.3 us
    ppermute x18, waiting for transfers between devices, move(): lax.ppermute(x, 'wide', [(2 * s + c, 2 * d + c) for s, d in pairs for c i...  33.7 us
    ppermute x4, waiting for transfers between devices, flip(): return lax.ppermute(x, 'node', [(i, i ^ j) for i in range(n_node)])  12 us
    pallas_call x1, Pallas kernels, body(): call(functools.partial(backward_kernel, n_slots), 'backward', [SMEM] + [A...  10.3 us
    pallas_call x1, Pallas kernels, body(): call(functools.partial(mixed_kernel, n_slots), 'mixed', [SMEM] + [ANY] *...  7.79 us
    pallas_call x1, Pallas kernels, body(): call(grad_out_kernel, 'grad_out', [SMEM] + [ANY] * 2 + [VMEM] * 2, send_s...  6.71 us
    ppermute x4, starting transfers between devices, flip(): return lax.ppermute(x, 'node', [(i, i ^ j) for i in range(n_node)])  5.24 us
    pallas_call x1, Pallas kernels, body(): call(functools.partial(terms_kernel, n_node), 'terms', [SMEM] + [VMEM] *...  5.2 us
  transfers between devices with their start and end apart: 31, of which 15 were waited for; matrix products, arithmetic and copies ran while one was open for 5% of the time, Pallas kernels for 20%

profile of v4, /device:TPU:0, one launch (start us, length us, event | category | flops | bytes accessed | tf_op | source)
XLA Modules:
  0.0 147.8 jit_solution(2395811169923920762)
XLA Ops:
  0.7 1.3 slice_bitcast_fusion.11
  2.0 0.5 collective-permute-start
  2.6 1.2 collective-permute-done
  3.9 0.4 collective-permute-start.3
  4.3 0.1 collective-permute-start.5
  4.4 0.4 collective-permute-start.4
  4.8 3.7 %collective-permute-start.1 = (bf16[640,256]{1,0:T(8,128)(2,1)S(1)}, bf16[640,256]{1,0:T(8,128)(2,1)}, u32[]{:S(2)}, u32[]{:S(2)}) collective-permute-start(bf16[640,256]{1,0:T(8,128)(2,1)S(1)} %pad_maximum_fusion.5.rest_0_), channel_id=1, source_target_pairs={{0,16},{4,20},{8,24},{12,28},{16,0},{20,4},{24,8},{28,12},{1,17},{... | collective-permute-start | bytes 983048 | tf_op jit(solution)/shard_map/ppermute | solution.py:208
  8.6 1.3 collective-permute-start.2
  9.8 14.2 %collective-permute-done.1.rest_1_ = bf16[640,256]{1,0:T(8,128)(2,1)} collective-permute-done((bf16[640,256]{1,0:T(8,128)(2,1)S(1)}, bf16[640,256]{1,0:T(8,128)(2,1)}, u32[]{:S(2)}, u32[]{:S(2)}) %collective-permute-start.1) | collective-permute-done | bytes 327712 | tf_op jit(solution)/shard_map/ppermute | solution.py:208
  24.0 2.0 %collective-permute-done.2.rest_2_ = bf16[640,256]{1,0:T(8,128)(2,1)S(1)} collective-permute-done((bf16[640,256]{1,0:T(8,128)(2,1)S(1)}, bf16[640,256]{1,0:T(8,128)(2,1)S(1)}, u32[]{:S(2)}, u32[]{:S(2)}) %collective-permute-start.2) | collective-permute-done | bytes 327712 | tf_op jit(solution)/shard_map/ppermute | solution.py:208
  26.0 2.3 %copy-done.1 = bf16[512,2560]{1,0:T(8,128)(2,1)} copy-done((bf16[512,2560]{1,0:T(8,128)(2,1)}, bf16[512,2560]{1,0:T(8,128)(2,1)S(1)}, u32[]{:S(2)}) %copy-start.1) | copy-done | bytes 2621464
  28.4 1.5 collective-permute-start.7
  29.9 0.7 collective-permute-start.8
  30.6 1.3 collective-permute-start.6
  31.9 0.7 stack.123.idx
  32.6 1.3 collective-permute-start.10
  33.9 4.3 %collective-permute-start.9 = (bf16[640,256]{1,0:T(8,128)(2,1)S(1)}, bf16[640,256]{1,0:T(8,128)(2,1)S(1)}, u32[]{:S(2)}, u32[]{:S(2)}) collective-permute-start(bf16[640,256]{1,0:T(8,128)(2,1)S(1)} %pad_maximum_fusion.6.rest_0_), channel_id=1, source_target_pairs={{0,16},{4,20},{8,24},{12,28},{16,0},{20,4},{24,8},{28,12},{1,17},{... | collective-permute-start | bytes 983048 | tf_op jit(solution)/shard_map/ppermute | solution.py:208
  38.3 6.4 %collective-permute-done.6.rest_3_ = bf16[640,256]{1,0:T(8,128)(2,1)S(1)} collective-permute-done((bf16[640,256]{1,0:T(8,128)(2,1)}, bf16[640,256]{1,0:T(8,128)(2,1)S(1)}, u32[]{:S(2)}, u32[]{:S(2)}) %collective-permute-start.6) | collective-permute-done | bytes 327712 | tf_op jit(solution)/shard_map/ppermute | solution.py:208
  44.7 0.7 copy-done.19
  45.4 10.3 %backward.1 = (bf16[2560,256]{1,0:T(8,128)(2,1)}, bf16[2,320,256]{2,1,0:T(8,128)(2,1)}, bf16[2,320,256]{2,1,0:T(8,128)(2,1)}, bf16[2,320,256]{2,1,0:T(8,128)(2,1...) custom-call(s32[18]{0:T(128)} %stack.123.idx, bf16[512,2560]{1,0:T(8,128)(2,1)} %bitcast.75, ...), custom_call_target="tpu_custom_call" | custom-call | flops 2684354560 | bytes 12582912 | tf_op jit(solution)/shard_map/backward/pallas_call | solution.py:339
  55.7 8.4 %collective-permute-start.14 = (bf16[2,320,256]{2,1,0:T(8,128)(2,1)}, bf16[2,320,256]{2,1,0:T(8,128)(2,1)S(1)}, u32[]{:S(2)}, u32[]{:S(2)}) collective-permute-start(bf16[2,320,256]{2,1,0:T(8,128)(2,1)} %get-tuple-element.64), channel_id=1, source_target_pairs={{0,8},{4,12},{8,16},{12,20},{16,24},{20,28},{1,9},{5,13},{9,17},{1... | collective-permute-start | bytes 983048 | tf_op jit(solution)/shard_map/ppermute | solution.py:208
  64.1 1.3 collective-permute-start.15
  65.4 1.3 collective-permute-start.11
  66.7 4.6 %collective-permute-start.12 = (bf16[640,256]{1,0:T(8,128)(2,1)S(1)}, bf16[640,256]{1,0:T(8,128)(2,1)S(1)}, u32[]{:S(2)}, u32[]{:S(2)}) collective-permute-start(bf16[640,256]{1,0:T(8,128)(2,1)S(1)} %pad_maximum_fusion.6.rest_0_), channel_id=1, source_target_pairs={{0,8},{4,12},{8,16},{12,20},{1,9},{5,13},{9,17},{13,21},{2,10},{6,... | collective-permute-start | bytes 983048 | tf_op jit(solution)/shard_map/ppermute | solution.py:208
  71.4 0.7 collective-permute-start.13
  72.1 1.2 collective-permute-done.15
  73.3 1.9 %add_convert_fusion.1 = bf16[2,320,256]{2,1,0:T(8,128)(2,1)} fusion(bf16[2,320,256]{2,1,0:T(8,128)(2,1)} %get-tuple-element.63, bf16[2,320,256]{2,1,0:T(8,128)(2,1)S(1)} %collective-permute-done.14, bf16[2,320,256]{2,1,0:T(8,128)(2,1)S(1)} %collective-permute-done.15, pred[]{:T(512)S(6)} %eq.14, pred[]{:T(512)S(6)} %eq.13), kind=kLoop, calls=%fused_computation.18 | loop fusion | flops 983040 | bytes 1310722 | tf_op jit(solution)/shard_map/convert_element_type | solution.py:264
  75.1 1.7 %collective-permute-done.11.rest_3_ = bf16[640,256]{1,0:T(8,128)(2,1)S(1)} collective-permute-done((bf16[640,256]{1,0:T(8,128)(2,1)S(1)}, bf16[640,256]{1,0:T(8,128)(2,1)S(1)}, u32[]{:S(2)}, u32[]{:S(2)}) %collective-permute-start.11) | collective-permute-done | bytes 327712 | tf_op jit(solution)/shard_map/ppermute | solution.py:208
  76.9 5.5 %collective-permute-start.22 = (bf16[2,320,256]{2,1,0:T(8,128)(2,1)}, bf16[2,320,256]{2,1,0:T(8,128)(2,1)S(1)}, u32[]{:S(2)}, u32[]{:S(2)}) collective-permute-start(bf16[2,320,256]{2,1,0:T(8,128)(2,1)} %get-tuple-element.85), channel_id=1, source_target_pairs={{0,8},{4,12},{24,16},{28,20},{1,9},{5,13},{25,17},{29,21},{2,10},{... | collective-permute-start | bytes 983048 | tf_op jit(solution)/shard_map/ppermute | solution.py:208
  82.5 0.7 stack.113.idx
  83.2 0.6 stack.124.idx
  83.8 7.8 %mixed.1 = (bf16[512,256]{1,0:T(8,128)(2,1)}, bf16[512,256]{1,0:T(8,128)(2,1)}) custom-call(s32[13]{0:T(128)} %stack.113.idx, bf16[512,2560]{1,0:T(8,128)(2,1)} %bitcast.72, bf16[512,2560]{1,0:T(8,128)(2,1)} %copy-done.1, bf16[4,8,128,128]{3,2,1,0:T(8,128)(2,1)} %bitcast.78, bf16[4,8,128,128]{3,2,1,0:T(8,128)(2,1)} %copy-done.4, bf16[640,256]{1,0:T(8,128)(2,1)} %copy-done.5, ...), custom_call_target="tpu_custom_call" | custom-call | flops 1342177280 | bytes 12582912 | tf_op jit(solution)/shard_map/mixed/pallas_call | solution.py:358
  91.6 0.3 collective-permute-start.16
  91.9 6.7 %grad_out.1 = (bf16[2,320,256]{2,1,0:T(8,128)(2,1)}, bf16[2,320,256]{2,1,0:T(8,128)(2,1)}, bf16[2,320,256]{2,1,0:T(8,128)(2,1)}, bf16[2,320,256]{2,1,0:T(8,128)(2,1)}, bf16[2,320,256]{2,1,0:T(8,128)(2,1)}) custom-call(s32[6]{0:T(128)} %stack.124.idx, bf16[512,2560]{1,0:T(8,128)(2,1)} %bitcast.76, bf16[512,2560]{1,0:T(8,128)(2,1)} %copy-done.2, ...), custom_call_target="tpu_custom_call" | custom-call | flops 1342177280 | bytes 12582912 | tf_op jit(solution)/shard_map/grad_out/pallas_call | solution.py:367
  98.6 1.8 %collective-permute-done.23 = bf16[2,320,256]{2,1,0:T(8,128)(2,1)S(1)} collective-permute-done((bf16[2,320,256]{2,1,0:T(8,128)(2,1)}, bf16[2,320,256]{2,1,0:T(8,128)(2,1)S(1)}, u32[]{:S(2)}, u32[]{:S(2)}) %collective-permute-start.23) | collective-permute-done | bytes 327712 | tf_op jit(solution)/shard_map/ppermute | solution.py:208
  100.4 0.2 convert_add_fusion.1
  100.7 1.6 %collective-permute-start.25 = (bf16[2,320,256]{2,1,0:T(8,128)(2,1)S(1)}, bf16[2,320,256]{2,1,0:T(8,128)(2,1)S(1)}, u32[]{:S(2)}, u32[]{:S(2)}) collective-permute-start(bf16[2,320,256]{2,1,0:T(8,128)(2,1)S(1)} %copy-done.24), channel_id=1, source_target_pairs={{0,8},{4,12},{8,16},{12,20},{16,24},{20,28},{1,9},{5,13},{9,17},{1... | collective-permute-start | bytes 983048 | tf_op jit(solution)/shard_map/ppermute | solution.py:208
  102.3 1.5 collective-permute-start.26
  103.8 0.3 collective-permute-start.24
  104.1 0.7 pad_add_fusion.idx
  104.8 5.2 %terms.1 = (bf16[2,256,640]{2,1,0:T(8,128)(2,1)}, bf16[2,256,640]{2,1,0:T(8,128)(2,1)}, bf16[4,256,640]{2,1,0:T(8,128)(2,1)}) custom-call(s32[4]{0:T(128)} %pad_add_fusion.idx, bf16[512,256]{1,0:T(8,128)(2,1)} %get-tuple-element.72.mixed_o, bf16[512,256]{1,0:T(8,128)(2,1)} %copy-done.25, bf16[2560,256]{1,0:T(8,128)(2,1)} %get-tuple-element.75.w_o, ...), custom_call_target="tpu_custom_call" | custom-call | flops 1342177280 | bytes 12582912 | tf_op jit(solution)/shard_map/terms/pallas_call | solution.py:381
  110.0 4.8 %collective-permute-done.26 = bf16[2,320,256]{2,1,0:T(8,128)(2,1)S(1)} collective-permute-done((bf16[2,320,256]{2,1,0:T(8,128)(2,1)S(1)}, bf16[2,320,256]{2,1,0:T(8,128)(2,1)S(1)}, u32[]{:S(2)}, u32[]{:S(2)}) %collective-permute-start.26) | collective-permute-done | bytes 327712 | tf_op jit(solution)/shard_map/ppermute | solution.py:208
  114.8 3.8 %collective-permute-start.27 = (bf16[2,320,256]{2,1,0:T(8,128)(2,1)S(1)}, bf16[2,320,256]{2,1,0:T(8,128)(2,1)S(1)}, u32[]{:S(2)}, u32[]{:S(2)}) collective-permute-start(bf16[2,320,256]{2,1,0:T(8,128)(2,1)S(1)} %copy-done.22), channel_id=1, source_target_pairs={{0,8},{4,12},{24,16},{28,20},{1,9},{5,13},{25,17},{29,21},{2,10},{... | collective-permute-start | bytes 983048 | tf_op jit(solution)/shard_map/ppermute | solution.py:208
  118.6 0.9 pad_maximum_fusion.1
  119.5 1.6 %collective-permute-start.18 = (bf16[2,256,640]{2,1,0:T(8,128)(2,1)S(1)}, bf16[2,256,640]{2,1,0:T(8,128)(2,1)S(1)}, u32[]{:S(2)}, u32[]{:S(2)}) collective-permute-start(bf16[2,256,640]{2,1,0:T(8,128)(2,1)S(1)} %copy-done.21), channel_id=1, source_target_pairs={{0,1},{1,0},{2,3},{3,2},{4,5},{5,4},{6,7},{7,6},{8,9},{9,8},{10,11... | collective-permute-start | bytes 1966088 | tf_op jit(solution)/shard_map/ppermute | solution.py:216
  121.2 0.2 convert_element_type.84
  121.3 0.9 copy-done.20
  122.2 1.5 %collective-permute-start.20 = (bf16[2,256,640]{2,1,0:T(8,128)(2,1)S(1)}, bf16[2,256,640]{2,1,0:T(8,128)(2,1)S(1)}, u32[]{:S(2)}, u32[]{:S(2)}) collective-permute-start(bf16[2,256,640]{2,1,0:T(8,128)(2,1)S(1)} %copy-done.20), channel_id=1, source_target_pairs={{0,2},{1,3},{2,0},{3,1},{4,6},{5,7},{6,4},{7,5},{8,10},{9,11},{10,... | collective-permute-start | bytes 1966088 | tf_op jit(solution)/shard_map/ppermute | solution.py:216
  123.8 1.3 collective-permute-done.27
  125.0 0.3 add_convert_fusion
  125.4 2.6 %collective-permute-start.28 = (bf16[320,256]{1,0:T(8,128)(2,1)S(1)}, bf16[320,256]{1,0:T(8,128)(2,1)S(1)}, u32[]{:S(2)}, u32[]{:S(2)}) collective-permute-start(bf16[320,256]{1,0:T(8,128)(2,1)S(1)} %get-tuple-element.107), channel_id=1, source_target_pairs={{0,16},{4,20},{8,24},{12,28},{16,0},{20,4},{24,8},{28,12},{1,17},{... | collective-permute-start | bytes 491528 | tf_op jit(solution)/shard_map/ppermute | solution.py:208
  128.0 0.2 collective-permute-start.30
  128.2 7.0 %collective-permute-done.18 = bf16[2,256,640]{2,1,0:T(8,128)(2,1)S(1)} collective-permute-done((bf16[2,256,640]{2,1,0:T(8,128)(2,1)S(1)}, bf16[2,256,640]{2,1,0:T(8,128)(2,1)S(1)}, u32[]{:S(2)}, u32[]{:S(2)}) %collective-permute-start.18) | collective-permute-done | bytes 655392 | tf_op jit(solution)/shard_map/ppermute | solution.py:216
  135.4 2.3 %collective-permute-done.20 = bf16[2,256,640]{2,1,0:T(8,128)(2,1)S(1)} collective-permute-done((bf16[2,256,640]{2,1,0:T(8,128)(2,1)S(1)}, bf16[2,256,640]{2,1,0:T(8,128)(2,1)S(1)}, u32[]{:S(2)}, u32[]{:S(2)}) %collective-permute-start.20) | collective-permute-done | bytes 655392 | tf_op jit(solution)/shard_map/ppermute | solution.py:216
  137.8 0.1 fusion.8
  137.9 1.6 %collective-permute-start.19 = (bf16[256,640]{1,0:T(8,128)(2,1)S(1)}, bf16[256,640]{1,0:T(8,128)(2,1)S(1)}, u32[]{:S(2)}, u32[]{:S(2)}) collective-permute-start(bf16[256,640]{1,0:T(8,128)(2,1)S(1)} %get-tuple-element.97), channel_id=1, source_target_pairs={{0,2},{1,3},{2,0},{3,1},{4,6},{5,7},{6,4},{7,5},{8,10},{9,11},{10,... | collective-permute-start | bytes 983048 | tf_op jit(solution)/shard_map/ppermute | solution.py:216
  139.5 0.5 collective-permute-start.21
  140.0 0.4 collective-permute-done.28
  140.4 2.7 %collective-permute-done.30 = bf16[320,256]{1,0:T(8,128)(2,1)S(1)} collective-permute-done((bf16[320,256]{1,0:T(8,128)(2,1)S(1)}, bf16[320,256]{1,0:T(8,128)(2,1)S(1)}, u32[]{:S(2)}, u32[]{:S(2)}) %collective-permute-start.30) | collective-permute-done | bytes 163872 | tf_op jit(solution)/shard_map/ppermute | solution.py:279
  143.2 0.9 pad_maximum_fusion.2
  144.1 1.4 collective-permute-done.19
  145.5 1.2 collective-permute-done.21
  146.7 0.2 fusion.7
  146.9 0.9 pad_maximum_fusion
  (80 shorter events, 0.9 us)
Async XLA Ops:
  0.6 3.8 %copy-start.3 = (bf16[2,2,8,128,128]{4,3,2,1,0:T(8,128)(2,1)S(1)}, bf16[2,2,8,128,128]{4,3,2,1,0:T(8,128)(2,1)}, u32[]{:S(2)}) copy-start(bf16[2,2,8,128,128]{4,3,2,1,0:T(8,128)(2,1)} %param.6) | copy-start | bytes 3145732
  1.9 2.4 %copy-start = (bf16[2,2,128,2560]{3,2,1,0:T(8,128)(2,1)S(1)}, bf16[2,2,128,2560]{3,2,1,0:T(8,128)(2,1)}, u32[]{:S(2)}) copy-start(bf16[2,2,128,2560]{3,2,1,0:T(8,128)(2,1)} %param.5) | copy-start | bytes 7864324
  2.0 1.8 %collective-permute-start = (bf16[2,320,256]{2,1,0:T(8,128)(2,1)S(1)}, bf16[2,320,256]{2,1,0:T(8,128)(2,1)S(1)}, u32[]{:S(2)}, u32[]{:S(2)}) collective-permute-start(bf16[2,320,256]{2,1,0:T(8,128)(2,1)S(1)} %get-tuple-element.106), channel_id=1, source_target_pairs={{0,4},{4,0},{8,12},{12,8},{16,20},{20,16},{24,28},{28,24},{1,5},{5... | collective-permute-start | bytes 983048 | tf_op jit(solution)/shard_map/ppermute | solution.py:213
  3.9 40.8 %copy-start.7 = (bf16[640,256]{1,0:T(8,128)(2,1)}, bf16[640,256]{1,0:T(8,128)(2,1)S(1)}, u32[]{:S(2)}) copy-start(bf16[640,256]{1,0:T(8,128)(2,1)S(1)} %pad_maximum_fusion.5.rest_0_) | copy-start | bytes 983044
  3.9 22.1 %collective-permute-start.3 = (bf16[512,2560]{1,0:T(8,128)(2,1)}, bf16[512,2560]{1,0:T(8,128)(2,1)S(1)}, u32[]{:S(2)}, u32[]{:S(2)}) collective-permute-start(bf16[512,2560]{1,0:T(8,128)(2,1)} %bitcast.74), channel_id=1, source_target_pairs={{0,4},{4,0},{8,12},{12,8},{16,20},{20,16},{24,28},{28,24},{1,5},{5... | collective-permute-start | bytes 7864328 | tf_op jit(solution)/shard_map/ppermute | solution.py:213
  4.3 21.7 %collective-permute-start.5 = (bf16[512,2560]{1,0:T(8,128)(2,1)S(1)}, bf16[512,2560]{1,0:T(8,128)(2,1)S(1)}, u32[]{:S(2)}, u32[]{:S(2)}) collective-permute-start(bf16[512,2560]{1,0:T(8,128)(2,1)S(1)} %bitcast.73), channel_id=1, source_target_pairs={{0,4},{4,0},{8,12},{12,8},{16,20},{20,16},{24,28},{28,24},{1,5},{5... | collective-permute-start | bytes 7864328 | tf_op jit(solution)/shard_map/ppermute | solution.py:213
  4.4 21.5 %collective-permute-start.4 = (bf16[4,8,128,128]{3,2,1,0:T(8,128)(2,1)S(1)}, bf16[4,8,128,128]{3,2,1,0:T(8,128)(2,1)S(1)}, u32[]{:S(2)}, u32[]{:S(2)}) collective-permute-start(bf16[4,8,128,128]{3,2,1,0:T(8,128)(2,1)S(1)} %bitcast.79), channel_id=1, source_target_pairs={{0,4},{4,0},{8,12},{12,8},{16,20},{20,16},{24,28},{28,24},{1,5},{5... | collective-permute-start | bytes 3145736 | tf_op jit(solution)/shard_map/ppermute | solution.py:213
  4.8 19.2 %collective-permute-start.1 = (bf16[640,256]{1,0:T(8,128)(2,1)S(1)}, bf16[640,256]{1,0:T(8,128)(2,1)}, u32[]{:S(2)}, u32[]{:S(2)}) collective-permute-start(bf16[640,256]{1,0:T(8,128)(2,1)S(1)} %pad_maximum_fusion.5.rest_0_), channel_id=1, source_target_pairs={{0,16},{4,20},{8,24},{12,28},{16,0},{20,4},{24,8},{28,12},{1,17},{... | collective-permute-start | bytes 983048 | tf_op jit(solution)/shard_map/ppermute | solution.py:208
  8.6 17.4 %collective-permute-start.2 = (bf16[640,256]{1,0:T(8,128)(2,1)S(1)}, bf16[640,256]{1,0:T(8,128)(2,1)S(1)}, u32[]{:S(2)}, u32[]{:S(2)}) collective-permute-start(bf16[640,256]{1,0:T(8,128)(2,1)S(1)} %pad_maximum_fusion.5.rest_0_), channel_id=1, source_target_pairs={{8,0},{12,4},{16,24},{20,28},{9,1},{13,5},{17,25},{21,29},{10,2},{... | collective-permute-start | bytes 983048 | tf_op jit(solution)/shard_map/ppermute | solution.py:208
  26.0 4.6 %copy-start.16 = (bf16[640,256]{1,0:T(8,128)(2,1)}, bf16[640,256]{1,0:T(8,128)(2,1)S(1)}, u32[]{:S(2)}) copy-start(bf16[640,256]{1,0:T(8,128)(2,1)S(1)} %collective-permute-done.2.rest_2_) | copy-start | bytes 983044
  26.0 4.6 %copy-start.4 = (bf16[4,8,128,128]{3,2,1,0:T(8,128)(2,1)}, bf16[4,8,128,128]{3,2,1,0:T(8,128)(2,1)S(1)}, u32[]{:S(2)}) copy-start(bf16[4,8,128,128]{3,2,1,0:T(8,128)(2,1)S(1)} %collective-permute-done.4.mix_s) | copy-start | bytes 3145732
  26.0 3.8 %copy-start.2 = (bf16[512,2560]{1,0:T(8,128)(2,1)}, bf16[512,2560]{1,0:T(8,128)(2,1)S(1)}, u32[]{:S(2)}) copy-start(bf16[512,2560]{1,0:T(8,128)(2,1)S(1)} %collective-permute-done.3.cot_s) | copy-start | bytes 7864324
  26.0 2.4 %copy-start.1 = (bf16[512,2560]{1,0:T(8,128)(2,1)}, bf16[512,2560]{1,0:T(8,128)(2,1)S(1)}, u32[]{:S(2)}) copy-start(bf16[512,2560]{1,0:T(8,128)(2,1)S(1)} %collective-permute-done.5.act_s) | copy-start | bytes 7864324
  28.4 9.9 %collective-permute-start.7 = (bf16[640,256]{1,0:T(8,128)(2,1)S(1)}, bf16[640,256]{1,0:T(8,128)(2,1)S(1)}, u32[]{:S(2)}, u32[]{:S(2)}) collective-permute-start(bf16[640,256]{1,0:T(8,128)(2,1)S(1)} %pad_maximum_fusion.5.rest_0_), channel_id=1, source_target_pairs={{0,8},{4,12},{8,16},{12,20},{1,9},{5,13},{9,17},{13,21},{2,10},{6,... | collective-permute-start | bytes 983048 | tf_op jit(solution)/shard_map/ppermute | solution.py:208
  29.9 8.4 %collective-permute-start.8 = (bf16[640,256]{1,0:T(8,128)(2,1)S(1)}, bf16[640,256]{1,0:T(8,128)(2,1)S(1)}, u32[]{:S(2)}, u32[]{:S(2)}) collective-permute-start(bf16[640,256]{1,0:T(8,128)(2,1)S(1)} %pad_maximum_fusion.5.rest_0_), channel_id=1, source_target_pairs={{24,16},{28,20},{16,8},{20,12},{25,17},{29,21},{17,9},{21,13},{26,... | collective-permute-start | bytes 983048 | tf_op jit(solution)/shard_map/ppermute | solution.py:208
  30.6 14.1 %collective-permute-start.6 = (bf16[640,256]{1,0:T(8,128)(2,1)}, bf16[640,256]{1,0:T(8,128)(2,1)S(1)}, u32[]{:S(2)}, u32[]{:S(2)}) collective-permute-start(bf16[640,256]{1,0:T(8,128)(2,1)} %collective-permute-done.1.rest_1_), channel_id=1, source_target_pairs={{16,24},{20,28},{8,0},{12,4},{17,25},{21,29},{9,1},{13,5},{18,26},... | collective-permute-start | bytes 983048 | tf_op jit(solution)/shard_map/ppermute | solution.py:208
  32.6 38.7 %copy-start.5 = (bf16[640,256]{1,0:T(8,128)(2,1)}, bf16[640,256]{1,0:T(8,128)(2,1)S(1)}, u32[]{:S(2)}) copy-start(bf16[640,256]{1,0:T(8,128)(2,1)S(1)} %pad_maximum_fusion.6.rest_0_) | copy-start | bytes 983044
  32.6 38.7 %collective-permute-start.10 = (bf16[640,256]{1,0:T(8,128)(2,1)S(1)}, bf16[640,256]{1,0:T(8,128)(2,1)S(1)}, u32[]{:S(2)}, u32[]{:S(2)}) collective-permute-start(bf16[640,256]{1,0:T(8,128)(2,1)S(1)} %pad_maximum_fusion.6.rest_0_), channel_id=1, source_target_pairs={{8,0},{12,4},{16,24},{20,28},{9,1},{13,5},{17,25},{21,29},{10,2},{... | collective-permute-start | bytes 983048 | tf_op jit(solution)/shard_map/ppermute | solution.py:208
  33.9 31.5 %collective-permute-start.9 = (bf16[640,256]{1,0:T(8,128)(2,1)S(1)}, bf16[640,256]{1,0:T(8,128)(2,1)S(1)}, u32[]{:S(2)}, u32[]{:S(2)}) collective-permute-start(bf16[640,256]{1,0:T(8,128)(2,1)S(1)} %pad_maximum_fusion.6.rest_0_), channel_id=1, source_target_pairs={{0,16},{4,20},{8,24},{12,28},{16,0},{20,4},{24,8},{28,12},{1,17},{... | collective-permute-start | bytes 983048 | tf_op jit(solution)/shard_map/ppermute | solution.py:208
  38.2 6.4 %copy-start.17 = (bf16[640,256]{1,0:T(8,128)(2,1)}, bf16[640,256]{1,0:T(8,128)(2,1)S(1)}, u32[]{:S(2)}) copy-start(bf16[640,256]{1,0:T(8,128)(2,1)S(1)} %collective-permute-done.7.rest_4_) | copy-start | bytes 983044
  38.2 6.4 %copy-start.18 = (bf16[640,256]{1,0:T(8,128)(2,1)}, bf16[640,256]{1,0:T(8,128)(2,1)S(1)}, u32[]{:S(2)}) copy-start(bf16[640,256]{1,0:T(8,128)(2,1)S(1)} %collective-permute-done.8.rest_5_) | copy-start | bytes 983044
  44.7 0.8 copy-start.19
  55.7 16.3 %collective-permute-start.14 = (bf16[2,320,256]{2,1,0:T(8,128)(2,1)}, bf16[2,320,256]{2,1,0:T(8,128)(2,1)S(1)}, u32[]{:S(2)}, u32[]{:S(2)}) collective-permute-start(bf16[2,320,256]{2,1,0:T(8,128)(2,1)} %get-tuple-element.64), channel_id=1, source_target_pairs={{0,8},{4,12},{8,16},{12,20},{16,24},{20,28},{1,9},{5,13},{9,17},{1... | collective-permute-start | bytes 983048 | tf_op jit(solution)/shard_map/ppermute | solution.py:208
  64.1 9.2 %collective-permute-start.15 = (bf16[2,320,256]{2,1,0:T(8,128)(2,1)}, bf16[2,320,256]{2,1,0:T(8,128)(2,1)S(1)}, u32[]{:S(2)}, u32[]{:S(2)}) collective-permute-start(bf16[2,320,256]{2,1,0:T(8,128)(2,1)} %get-tuple-element.65), channel_id=1, source_target_pairs={{24,16},{28,20},{16,8},{20,12},{8,0},{12,4},{25,17},{29,21},{17,9}... | collective-permute-start | bytes 983048 | tf_op jit(solution)/shard_map/ppermute | solution.py:208
  65.4 18.4 %copy-start.9 = (bf16[640,256]{1,0:T(8,128)(2,1)}, bf16[640,256]{1,0:T(8,128)(2,1)S(1)}, u32[]{:S(2)}) copy-start(bf16[640,256]{1,0:T(8,128)(2,1)S(1)} %collective-permute-done.9.rest_1_) | copy-start | bytes 983044
  65.4 11.4 %collective-permute-start.11 = (bf16[640,256]{1,0:T(8,128)(2,1)S(1)}, bf16[640,256]{1,0:T(8,128)(2,1)S(1)}, u32[]{:S(2)}, u32[]{:S(2)}) collective-permute-start(bf16[640,256]{1,0:T(8,128)(2,1)S(1)} %collective-permute-done.9.rest_1_), channel_id=1, source_target_pairs={{16,24},{20,28},{8,0},{12,4},{17,25},{21,29},{9,1},{13,5},{18,26},... | collective-permute-start | bytes 983048 | tf_op jit(solution)/shard_map/ppermute | solution.py:208
  66.7 10.1 %collective-permute-start.12 = (bf16[640,256]{1,0:T(8,128)(2,1)S(1)}, bf16[640,256]{1,0:T(8,128)(2,1)S(1)}, u32[]{:S(2)}, u32[]{:S(2)}) collective-permute-start(bf16[640,256]{1,0:T(8,128)(2,1)S(1)} %pad_maximum_fusion.6.rest_0_), channel_id=1, source_target_pairs={{0,8},{4,12},{8,16},{12,20},{1,9},{5,13},{9,17},{13,21},{2,10},{6,... | collective-permute-start | bytes 983048 | tf_op jit(solution)/shard_map/ppermute | solution.py:208
  71.3 12.5 %copy-start.8 = (bf16[640,256]{1,0:T(8,128)(2,1)}, bf16[640,256]{1,0:T(8,128)(2,1)S(1)}, u32[]{:S(2)}) copy-start(bf16[640,256]{1,0:T(8,128)(2,1)S(1)} %collective-permute-done.10.rest_2_) | copy-start | bytes 983044
  71.4 5.5 %collective-permute-start.13 = (bf16[640,256]{1,0:T(8,128)(2,1)S(1)}, bf16[640,256]{1,0:T(8,128)(2,1)S(1)}, u32[]{:S(2)}, u32[]{:S(2)}) collective-permute-start(bf16[640,256]{1,0:T(8,128)(2,1)S(1)} %pad_maximum_fusion.6.rest_0_), channel_id=1, source_target_pairs={{24,16},{28,20},{16,8},{20,12},{25,17},{29,21},{17,9},{21,13},{26,... | collective-permute-start | bytes 983048 | tf_op jit(solution)/shard_map/ppermute | solution.py:208
  76.8 7.0 %copy-start.10 = (bf16[640,256]{1,0:T(8,128)(2,1)}, bf16[640,256]{1,0:T(8,128)(2,1)S(1)}, u32[]{:S(2)}) copy-start(bf16[640,256]{1,0:T(8,128)(2,1)S(1)} %collective-permute-done.11.rest_3_) | copy-start | bytes 983044
  76.8 7.0 %copy-start.11 = (bf16[640,256]{1,0:T(8,128)(2,1)}, bf16[640,256]{1,0:T(8,128)(2,1)S(1)}, u32[]{:S(2)}) copy-start(bf16[640,256]{1,0:T(8,128)(2,1)S(1)} %collective-permute-done.12.rest_4_) | copy-start | bytes 983044
  76.8 7.0 %copy-start.12 = (bf16[640,256]{1,0:T(8,128)(2,1)}, bf16[640,256]{1,0:T(8,128)(2,1)S(1)}, u32[]{:S(2)}) copy-start(bf16[640,256]{1,0:T(8,128)(2,1)S(1)} %collective-permute-done.13.rest_5_) | copy-start | bytes 983044
  76.8 27.9 %collective-permute-start.17 = (bf16[2560,256]{1,0:T(8,128)(2,1)}, bf16[2560,256]{1,0:T(8,128)(2,1)}, u32[]{:S(2)}, u32[]{:S(2)}) collective-permute-start(bf16[2560,256]{1,0:T(8,128)(2,1)} %get-tuple-element.75.w_o), channel_id=1, source_target_pairs={{0,4},{4,0},{8,12},{12,8},{16,20},{20,16},{24,28},{28,24},{1,5},{5... | collective-permute-start | bytes 3932168 | tf_op jit(solution)/shard_map/ppermute | solution.py:213
  76.9 21.7 %collective-permute-start.22 = (bf16[2,320,256]{2,1,0:T(8,128)(2,1)}, bf16[2,320,256]{2,1,0:T(8,128)(2,1)S(1)}, u32[]{:S(2)}, u32[]{:S(2)}) collective-permute-start(bf16[2,320,256]{2,1,0:T(8,128)(2,1)} %get-tuple-element.85), channel_id=1, source_target_pairs={{0,8},{4,12},{24,16},{28,20},{1,9},{5,13},{25,17},{29,21},{2,10},{... | collective-permute-start | bytes 983048 | tf_op jit(solution)/shard_map/ppermute | solution.py:208
  82.4 18.0 %collective-permute-start.23 = (bf16[2,320,256]{2,1,0:T(8,128)(2,1)}, bf16[2,320,256]{2,1,0:T(8,128)(2,1)S(1)}, u32[]{:S(2)}, u32[]{:S(2)}) collective-permute-start(bf16[2,320,256]{2,1,0:T(8,128)(2,1)} %add_convert_fusion.1), channel_id=1, source_target_pairs={{0,16},{4,20},{8,24},{12,28},{16,0},{20,4},{24,8},{28,12},{1,17},{... | collective-permute-start | bytes 983048 | tf_op jit(solution)/shard_map/ppermute | solution.py:208
  91.6 9.0 %collective-permute-start.16 = (bf16[512,256]{1,0:T(8,128)(2,1)}, bf16[512,256]{1,0:T(8,128)(2,1)S(1)}, u32[]{:S(2)}, u32[]{:S(2)}) collective-permute-start(bf16[512,256]{1,0:T(8,128)(2,1)} %get-tuple-element.73.mixed_s), channel_id=1, source_target_pairs={{0,4},{4,0},{8,12},{12,8},{16,20},{20,16},{24,28},{28,24},{1,5},{5... | collective-permute-start | bytes 786440 | tf_op jit(solution)/shard_map/ppermute | solution.py:213
  91.9 8.5 %copy-start.13 = (bf16[2,320,256]{2,1,0:T(8,128)(2,1)S(1)}, bf16[2,320,256]{2,1,0:T(8,128)(2,1)}, u32[]{:S(2)}) copy-start(bf16[2,320,256]{2,1,0:T(8,128)(2,1)} %get-tuple-element.59) | copy-start | bytes 983044
  98.6 2.0 %copy-start.24 = (bf16[2,320,256]{2,1,0:T(8,128)(2,1)S(1)}, bf16[2,320,256]{2,1,0:T(8,128)(2,1)}, u32[]{:S(2)}) copy-start(bf16[2,320,256]{2,1,0:T(8,128)(2,1)} %get-tuple-element.88) | copy-start | bytes 983044
  98.6 3.7 %copy-start.23 = (bf16[2,320,256]{2,1,0:T(8,128)(2,1)S(1)}, bf16[2,320,256]{2,1,0:T(8,128)(2,1)}, u32[]{:S(2)}) copy-start(bf16[2,320,256]{2,1,0:T(8,128)(2,1)} %get-tuple-element.89) | copy-start | bytes 983044
  100.7 4.1 %copy-start.25 = (bf16[512,256]{1,0:T(8,128)(2,1)}, bf16[512,256]{1,0:T(8,128)(2,1)S(1)}, u32[]{:S(2)}) copy-start(bf16[512,256]{1,0:T(8,128)(2,1)S(1)} %collective-permute-done.16.mixed_r) | copy-start | bytes 786436
  100.7 9.3 %collective-permute-start.25 = (bf16[2,320,256]{2,1,0:T(8,128)(2,1)S(1)}, bf16[2,320,256]{2,1,0:T(8,128)(2,1)S(1)}, u32[]{:S(2)}, u32[]{:S(2)}) collective-permute-start(bf16[2,320,256]{2,1,0:T(8,128)(2,1)S(1)} %copy-done.24), channel_id=1, source_target_pairs={{0,8},{4,12},{8,16},{12,20},{16,24},{20,28},{1,9},{5,13},{9,17},{1... | collective-permute-start | bytes 983048 | tf_op jit(solution)/shard_map/ppermute | solution.py:208
  102.3 12.5 %collective-permute-start.26 = (bf16[2,320,256]{2,1,0:T(8,128)(2,1)S(1)}, bf16[2,320,256]{2,1,0:T(8,128)(2,1)S(1)}, u32[]{:S(2)}, u32[]{:S(2)}) collective-permute-start(bf16[2,320,256]{2,1,0:T(8,128)(2,1)S(1)} %copy-done.23), channel_id=1, source_target_pairs={{24,16},{28,20},{16,8},{20,12},{8,0},{12,4},{25,17},{29,21},{17,9}... | collective-permute-start | bytes 983048 | tf_op jit(solution)/shard_map/ppermute | solution.py:208
  103.8 14.7 %collective-permute-start.24 = (f32[320,256]{1,0:T(8,128)S(1)}, f32[320,256]{1,0:T(8,128)S(1)}, u32[]{:S(2)}, u32[]{:S(2)}) collective-permute-start(f32[320,256]{1,0:T(8,128)S(1)} %slice_bitcast_fusion.2), channel_id=1, source_target_pairs={{0,4},{4,0},{8,12},{12,8},{16,20},{20,16},{24,28},{28,24},{1,5},{5... | collective-permute-start | bytes 983048 | tf_op jit(solution)/shard_map/ppermute | solution.py:213
  104.7 10.0 %copy-start.22 = (bf16[2,320,256]{2,1,0:T(8,128)(2,1)S(1)}, bf16[2,320,256]{2,1,0:T(8,128)(2,1)}, u32[]{:S(2)}) copy-start(bf16[2,320,256]{2,1,0:T(8,128)(2,1)} %get-tuple-element.93) | copy-start | bytes 983044
  114.8 4.8 %copy-start.21 = (bf16[2,256,640]{2,1,0:T(8,128)(2,1)S(1)}, bf16[2,256,640]{2,1,0:T(8,128)(2,1)}, u32[]{:S(2)}) copy-start(bf16[2,256,640]{2,1,0:T(8,128)(2,1)} %get-tuple-element.77) | copy-start | bytes 1966084
  114.8 6.4 %copy-start.6 = (bf16[4,256,640]{2,1,0:T(8,128)(2,1)S(1)}, bf16[4,256,640]{2,1,0:T(8,128)(2,1)}, u32[]{:S(2)}) copy-start(bf16[4,256,640]{2,1,0:T(8,128)(2,1)} %get-tuple-element.76) | copy-start | bytes 3932164
  114.8 10.3 %collective-permute-start.27 = (bf16[2,320,256]{2,1,0:T(8,128)(2,1)S(1)}, bf16[2,320,256]{2,1,0:T(8,128)(2,1)S(1)}, u32[]{:S(2)}, u32[]{:S(2)}) collective-permute-start(bf16[2,320,256]{2,1,0:T(8,128)(2,1)S(1)} %copy-done.22), channel_id=1, source_target_pairs={{0,8},{4,12},{24,16},{28,20},{1,9},{5,13},{25,17},{29,21},{2,10},{... | collective-permute-start | bytes 983048 | tf_op jit(solution)/shard_map/ppermute | solution.py:208
  119.5 15.7 %collective-permute-start.18 = (bf16[2,256,640]{2,1,0:T(8,128)(2,1)S(1)}, bf16[2,256,640]{2,1,0:T(8,128)(2,1)S(1)}, u32[]{:S(2)}, u32[]{:S(2)}) collective-permute-start(bf16[2,256,640]{2,1,0:T(8,128)(2,1)S(1)} %copy-done.21), channel_id=1, source_target_pairs={{0,1},{1,0},{2,3},{3,2},{4,5},{5,4},{6,7},{7,6},{8,9},{9,8},{10,11... | collective-permute-start | bytes 1966088 | tf_op jit(solution)/shard_map/ppermute | solution.py:216
  121.1 1.1 copy-start.20
  121.1 3.9 %copy-start.14 = (bf16[2,320,256]{2,1,0:T(8,128)(2,1)S(1)}, bf16[2,320,256]{2,1,0:T(8,128)(2,1)}, u32[]{:S(2)}) copy-start(bf16[2,320,256]{2,1,0:T(8,128)(2,1)} %get-tuple-element.87) | copy-start | bytes 983044
  121.1 3.9 %copy-start.15 = (bf16[2,320,256]{2,1,0:T(8,128)(2,1)S(1)}, bf16[2,320,256]{2,1,0:T(8,128)(2,1)}, u32[]{:S(2)}) copy-start(bf16[2,320,256]{2,1,0:T(8,128)(2,1)} %get-tuple-element.94) | copy-start | bytes 983044
  122.2 15.5 %collective-permute-start.20 = (bf16[2,256,640]{2,1,0:T(8,128)(2,1)S(1)}, bf16[2,256,640]{2,1,0:T(8,128)(2,1)S(1)}, u32[]{:S(2)}, u32[]{:S(2)}) collective-permute-start(bf16[2,256,640]{2,1,0:T(8,128)(2,1)S(1)} %copy-done.20), channel_id=1, source_target_pairs={{0,2},{1,3},{2,0},{3,1},{4,6},{5,7},{6,4},{7,5},{8,10},{9,11},{10,... | collective-permute-start | bytes 1966088 | tf_op jit(solution)/shard_map/ppermute | solution.py:216
  125.3 17.8 %collective-permute-start.29 = (f32[320,256]{1,0:T(8,128)S(1)}, f32[320,256]{1,0:T(8,128)S(1)}, u32[]{:S(2)}, u32[]{:S(2)}) collective-permute-start(f32[320,256]{1,0:T(8,128)S(1)} %slice_bitcast_fusion), channel_id=1, source_target_pairs={{0,4},{4,0},{8,12},{12,8},{16,20},{20,16},{24,28},{28,24},{1,5},{5... | collective-permute-start | bytes 983048 | tf_op jit(solution)/shard_map/ppermute | solution.py:213
  125.4 15.0 %collective-permute-start.28 = (bf16[320,256]{1,0:T(8,128)(2,1)S(1)}, bf16[320,256]{1,0:T(8,128)(2,1)S(1)}, u32[]{:S(2)}, u32[]{:S(2)}) collective-permute-start(bf16[320,256]{1,0:T(8,128)(2,1)S(1)} %get-tuple-element.107), channel_id=1, source_target_pairs={{0,16},{4,20},{8,24},{12,28},{16,0},{20,4},{24,8},{28,12},{1,17},{... | collective-permute-start | bytes 491528 | tf_op jit(solution)/shard_map/ppermute | solution.py:208
  128.0 15.1 %collective-permute-start.30 = (bf16[320,256]{1,0:T(8,128)(2,1)S(1)}, bf16[320,256]{1,0:T(8,128)(2,1)S(1)}, u32[]{:S(2)}, u32[]{:S(2)}) collective-permute-start(bf16[320,256]{1,0:T(8,128)(2,1)S(1)} %get-tuple-element.108), channel_id=1, source_target_pairs={{0,20},{4,16},{8,28},{12,24},{16,4},{20,0},{24,12},{28,8},{1,21},{... | collective-permute-start | bytes 491528 | tf_op jit(solution)/shard_map/ppermute | solution.py:279
  137.9 7.6 %collective-permute-start.19 = (bf16[256,640]{1,0:T(8,128)(2,1)S(1)}, bf16[256,640]{1,0:T(8,128)(2,1)S(1)}, u32[]{:S(2)}, u32[]{:S(2)}) collective-permute-start(bf16[256,640]{1,0:T(8,128)(2,1)S(1)} %get-tuple-element.97), channel_id=1, source_target_pairs={{0,2},{1,3},{2,0},{3,1},{4,6},{5,7},{6,4},{7,5},{8,10},{9,11},{10,... | collective-permute-start | bytes 983048 | tf_op jit(solution)/shard_map/ppermute | solution.py:216
  139.5 7.2 %collective-permute-start.21 = (bf16[256,640]{1,0:T(8,128)(2,1)S(1)}, bf16[256,640]{1,0:T(8,128)(2,1)S(1)}, u32[]{:S(2)}, u32[]{:S(2)}) collective-permute-start(bf16[256,640]{1,0:T(8,128)(2,1)S(1)} %get-tuple-element.98), channel_id=1, source_target_pairs={{0,1},{1,0},{2,3},{3,2},{4,5},{5,4},{6,7},{7,6},{8,9},{9,8},{10,11... | collective-permute-start | bytes 983048 | tf_op jit(solution)/shard_map/ppermute | solution.py:216

commit v5 on v4

--- a/solution.py
+++ b/solution.py
@@ -11,7 +11,7 @@
 HEAD_DIM = 64
 F32 = jnp.float32
 BF16 = jnp.bfloat16
-VMEM_LIMIT = 56 * 1024 * 1024
+VMEM_LIMIT = 24 * 1024 * 1024
 
 
 def dot(a, b, ca=1, cb=0):
@@ -63,18 +63,14 @@
     return [(h, min(2, heads - h)) for h in range(0, heads, 2)]
 
 
-def backward_kernel(n_slots, idx, cot_o, cot_s, mix_o, mix_s, act_o, act_s, *rest):
-    slots, rest = rest[:n_slots], rest[n_slots:]
-    w_out, rest = rest[0], rest[1:]
-    outs, (cot_v, act_v, mix_v, left_v, grad_v, sems) = rest[:-6], rest[-6:]
-    tokens, cols = cot_o.shape[0], w_out.shape[1]
+def d_value_kernel(n_slots, idx, cot_o, cot_s, mix_o, mix_s, *rest):
+    slots, (w_out, left_v, cot_v, mix_v, sems) = rest[:n_slots], rest[n_slots:]
     groups, _, seq, _ = mix_o.shape
     heads = mix_v.shape[2]
     here = pl.ds(idx[0] * heads, heads)
     copies = begin(
         [(cot_o, cot_v.at[0]), (mix_o.at[:, here], mix_v.at[0])]
-        + [(cot_s, cot_v.at[1]), (mix_s.at[:, here], mix_v.at[1])]
-        + [(act_o, act_v.at[pl.ds(0, tokens)]), (act_s, act_v.at[pl.ds(tokens, tokens)])],
+        + [(cot_s, cot_v.at[1]), (mix_s.at[:, here], mix_v.at[1])],
         sems,
     )
     place(idx, slots, w_out)
@@ -101,10 +97,19 @@
                 left_v[h * HEAD_DIM : (h + n) * HEAD_DIM, at : at + seq] = dot(
                     part, weights
                 ).astype(BF16)
-    copies[4].wait()
-    copies[5].wait()
-    gradient_rows(left_v[...], act_v, grad_v, 640)
-    hand_out(idx, 1 + 2 * n_slots, grad_v, outs)
+
+
+def gradient_kernel(idx, right_o, right_s, left_ref, *rest):
+    outs, (right_v, grad_v, sems) = rest[:-3], rest[-3:]
+    tokens, _ = right_o.shape
+    copies = begin(
+        [(right_o, right_v.at[pl.ds(0, tokens)]), (right_s, right_v.at[pl.ds(tokens, tokens)])],
+        sems,
+    )
+    copies[0].wait()
+    copies[1].wait()
+    gradient_rows(left_ref[...], right_v, grad_v, 640)
+    hand_out(idx, 1, grad_v, outs)
 
 
 def mixed_kernel(n_slots, idx, act_o, act_s, mix_o, mix_s, *rest):
@@ -178,7 +183,7 @@
             along_x[1], along_y[1] = first, second
 
 
-ANY = pl.BlockSpec(memory_space=pl.ANY)
+ANY = pl.BlockSpec(memory_space=pltpu.HBM)
 SMEM = pl.BlockSpec(memory_space=pltpu.SMEM)
 VMEM = pl.BlockSpec(memory_space=pltpu.VMEM)
 
@@ -223,70 +228,60 @@
         mine = jnp.where(c == 0, low, high)
         return [jnp.concatenate([mine[i], got[i]], axis=0) for i in range(len(weights))]
 
-    def gather_first(u):
-        if not line4:
-            return [move(u, [(s, (s - j) % planes) for s in range(planes)]) for j in range(1, planes)]
-        return [move(u, [(0, 2), (1, 3), (2, 0), (3, 1)]), move(u, [(1, 0), (2, 3)])]
-
-    def gather_rest(u, firsts):
-        if not line4:
-            return [u, *firsts]
-        across, ends = firsts
-        up = move(u, [(0, 1), (1, 2)])
-        down = move(u, [(3, 2), (2, 1)])
-        on = move(across, [(2, 3), (1, 0)])
-        return [u, across, ends, on, up, down]
+    right = [[(s, s + 1) for s in range(planes - 1)][k:] for k in range(planes)]
+    left = [[(s + 1, s) for s in reversed(range(planes - 1))][k:] for k in range(planes)]
+
+    def gather_ring(u):
+        return [u] + [
+            move(u, [(s, (s - j) % planes) for s in range(planes)]) for j in range(1, planes)
+        ]
+
+    def gather_step(u, k):
+        return move(u[0], right[k]), move(u[1], left[k])
+
+    def gather_last(second, z):
+        return move(jnp.where(z == 2, *second), right[2] + left[2])
 
     def slot_planes(z):
         if not line4:
             return [x for j in range(planes) for x in (lax.rem(z + j, planes), 1)]
-        edge = ((z == 0) | (z == 3)).astype(jnp.int32)
-        ends = jnp.where(z == 0, 1, 2)
-        on = jnp.where(z == 0, 3, 0)
-        up, down = jnp.maximum(z - 1, 0), jnp.minimum(z + 1, 3)
-        return [z, 1, lax.rem(z + 2, 4), 1, ends, edge, on, edge, up, 1 - edge, down, 1 - edge]
+        last = jnp.where(z == 0, 3, 0)
+        return [
+            *(z, 1, jnp.maximum(z - 1, 0), z >= 1, jnp.minimum(z + 1, 3), z <= 2),
+            *(jnp.maximum(z - 2, 0), z >= 2, jnp.minimum(z + 2, 3), z <= 1),
+            *(last, (z == 0) | (z == 3)),
+        ]
 
     def send_planes(z):
         if not line4:
             return [lax.rem(z + j, planes) for j in range(planes)]
-        up = jnp.where(z == 0, 3, jnp.minimum(z + 1, 3))
-        down = jnp.where(z == 3, 0, jnp.maximum(z - 1, 0))
-        near = jnp.where(z == 0, 1, jnp.where(z == 3, 2, z))
-        return [z, up, down, near, lax.rem(z + 2, 4)]
+        across = jnp.where(z == 0, 3, 0)
+        return [z, jnp.minimum(z + 1, 3), jnp.maximum(z - 1, 0), lax.rem(z + 2, 4), across]
+
+    def added(block, got):
+        return (block.astype(F32) + got.astype(F32)).astype(BF16)
 
     def scatter_first(blocks):
-        _, up, down, _, _ = blocks
-        return move(up, [(0, 1), (1, 2), (2, 3)]), move(down, [(3, 2), (2, 1), (1, 0)])
-
-    def scatter_far(blocks, firsts, z):
-        up, down = firsts
-        add = jnp.where(z == 1, up, jnp.where(z == 2, down, jnp.zeros_like(up)))
-        return (blocks[4].astype(F32) + add.astype(F32)).astype(BF16)
-
-    def scatter_near(blocks, firsts, z):
-        up, down = firsts
-        near = move(after(blocks[3], up, down), [(0, 1), (3, 2)])
-        total = blocks[0].astype(F32) + jnp.where(z <= 1, down, up).astype(F32)
-        return total + near.astype(F32)
+        return move(blocks[4], [(0, 1), (3, 2)])
+
+    def scatter_second(blocks, first):
+        far = added(blocks[3], first)
+        return move(far, [(0, 1), (1, 2)]), move(far, [(3, 2), (2, 1)])
+
+    def scatter_sums(blocks, second):
+        return added(blocks[1], second[0]), added(blocks[2], second[1])
+
+    def scatter_third(sums):
+        return move(sums[0], right[0]), move(sums[1], left[0])
+
+    def scatter_end(blocks, third, c):
+        total = blocks[0].astype(F32) + third[0].astype(F32) + third[1].astype(F32)
+        return join(total[0], sibling(total[1]), c)
 
     def join(mine, other, c):
         low = jnp.where(c == 0, mine, other)
         high = jnp.where(c == 0, other, mine)
         return jnp.concatenate([low, high], axis=1)
-
-    def scatter_rest(blocks, firsts, far, z, c, last):
-        if last:
-            far_other = lax.ppermute(
-                far[1],
-                "wide",
-                [(2 * s + k, 2 * ((s + 2) % 4) + 1 - k) for s in range(4) for k in range(2)],
-            )
-            far_mine = move(far[0], [(s, (s + 2) % 4) for s in range(4)])
-            total = scatter_near(blocks, firsts, z)
-            other = sibling(total[1])
-            return join(total[0] + far_mine.astype(F32), other + far_other.astype(F32), c)
-        far = move(far, [(s, (s + 2) % 4) for s in range(4)])
-        return scatter_near(blocks, firsts, z) + far.astype(F32)
 
     def scatter_ring(blocks, c):
         total = blocks[0].astype(F32)
@@ -311,49 +306,33 @@
         flops = 4 * tokens * width * cols
 
         u_out, u_value = swap_halves([w_out, w_value], c)
-        out_first = gather_first(u_out)
-        cot_s = sibling(after(cot, u_out))
-        mix_s = sibling(after(mix, u_out))
-        act_s = sibling(after(act, u_out))
-        out_first = list(lax.optimization_barrier((*out_first, cot_s, mix_s, act_s)))
-        *out_first, cot_s, mix_s, act_s = out_first
-        out_slots = gather_rest(after(u_out, out_first[0]), out_first)
-        u_value = after(u_value, out_first[0])
-        value_first = gather_first(u_value)
+        act_s, mix_s, cot_s = (sibling(after(x, u_value)) for x in (act, mix, cot))
+        if line4:
+            v1 = gather_step((u_value, u_value), 0)
+            v2 = gather_step(v1, 1)
+            v2, act_s, mix_s, cot_s = lax.optimization_barrier((v2, act_s, mix_s, cot_s))
+            v3 = gather_last(v2, z)
+            u_out = after(u_out, *v2)
+            o1 = gather_step((u_out, u_out), 0)
+            value_slots, o1 = lax.optimization_barrier(([u_value, *v1, *v2, v3], o1))
+            o2 = gather_step(o1, 1)
+        else:
+            value_slots = gather_ring(u_value)
+            out_slots = gather_ring(u_out)
 
         info = slot_planes(z)
         sends = send_planes(z)
-        n_slots = len(out_slots)
-        idx_back = jnp.stack([c, *info, *sends]).astype(jnp.int32)
-        idx_mixed = jnp.stack([c, *info]).astype(jnp.int32)
-        idx_send = jnp.stack([c, *sends]).astype(jnp.int32)
+        n_slots = len(value_slots)
+        idx_slots = jnp.stack([jnp.int32(x) for x in (c, *info)])
+        idx_send = jnp.stack([jnp.int32(x) for x in (c, *sends)])
         idx_node = jnp.stack([lax.bitwise_xor(n, jnp.int32(j)) for j in range(n_node)])
 
         mix_scratch = pltpu.VMEM((2, groups, heads, seq, seq), BF16)
         both = pltpu.VMEM((2 * tokens, width), BF16)
         halves = pltpu.VMEM((2, tokens, width), BF16)
-        left = pltpu.VMEM((cols, 2 * tokens), BF16)
+        left_tokens = pltpu.VMEM((cols, 2 * tokens), BF16)
         rows = pltpu.VMEM((width, cols), BF16)
         send_shapes = [(2, depth // 2, cols)] * len(sends)
-
-        w_full, *back_sends = call(
-            functools.partial(backward_kernel, n_slots),
-            "backward",
-            [SMEM] + [ANY] * 6 + [VMEM] * n_slots,
-            [(width, cols)] + send_shapes,
-            [halves, both, mix_scratch, left, rows, pltpu.SemaphoreType.DMA((6,))],
-            2 * flops,
-        )(idx_back, cot, cot_s, mix, mix_s, act, act_s, *out_slots)
-        if line4:
-            value_first = [after(x, back_sends[0]) for x in value_first]
-            value_slots = gather_rest(after(u_value, back_sends[0]), value_first)
-            back_firsts = scatter_first(back_sends)
-            far = scatter_far(back_sends, back_firsts, z)
-            value_slots = list(lax.optimization_barrier((*value_slots, far)))[:-1]
-            w_full_s = sibling(after(w_full, value_slots[0]))
-        else:
-            value_slots = gather_rest(u_value, value_first)
-            w_full_s = sibling(w_full)
 
         mixed_o, mixed_s = call(
             functools.partial(mixed_kernel, n_slots),
@@ -362,16 +341,50 @@
             [(tokens, cols)] * 2,
             [rows, halves, mix_scratch, pltpu.SemaphoreType.DMA((4,))],
             flops,
-        )(idx_mixed, act, act_s, mix, mix_s, *value_slots)
+        )(idx_slots, act, act_s, mix, mix_s, *value_slots)
         mixed_r = sibling(mixed_s)
+        if line4:
+            (mixed_o, mixed_s, mixed_r), o2 = lax.optimization_barrier(
+                ((mixed_o, mixed_s, mixed_r), o2)
+            )
+            out_slots = [u_out, *o1, *o2, gather_last(o2, z)]
         out_sends = call(
             grad_out_kernel,
             "grad_out",
             [SMEM] + [ANY] * 2 + [VMEM] * 2,
             send_shapes,
-            [both, left, rows, pltpu.SemaphoreType.DMA((2,))],
+            [both, left_tokens, rows, pltpu.SemaphoreType.DMA((2,))],
             flops,
         )(idx_send, cot, cot_s, mixed_o, mixed_s)
+        if line4:
+            out_slots, out_sends = lax.optimization_barrier((out_slots, out_sends))
+        w_full, left = call(
+            functools.partial(d_value_kernel, n_slots),
+            "d_value",
+            [SMEM] + [ANY] * 4 + [VMEM] * n_slots,
+            [(width, cols), (cols, 2 * tokens)],
+            [halves, mix_scratch, pltpu.SemaphoreType.DMA((4,))],
+            flops,
+        )(idx_slots, cot, cot_s, mix, mix_s, *out_slots)
+        w_full_s = sibling(w_full)
+        if line4:
+            out_first = scatter_first(out_sends)
+            left, out_first = lax.optimization_barrier((left, out_first))
+            out_second = scatter_second(out_sends, out_first)
+        back_sends = call(
+            gradient_kernel,
+            "grad_value",
+            [SMEM] + [ANY] * 2 + [VMEM],
+            send_shapes,
+            [both, rows, pltpu.SemaphoreType.DMA((2,))],
+            flops,
+        )(idx_send, act, act_s, left)
+        if line4:
+            back_first = scatter_first(back_sends)
+            out_sums = scatter_sums(out_sends, out_second)
+            w_full_s, out_sums = lax.optimization_barrier((w_full_s, out_sums))
+            out_third = scatter_third(out_sums)
+
         part = width // n_node
         half = tokens // 2
         if n_node == 4:
@@ -386,20 +399,16 @@
             [],
             flops,
         )(idx_node, mixed_o, mixed_r, w_full, w_full_s)
-        if line4:
-            grad_value = scatter_rest(back_sends, back_firsts, far, z, c, False)
-            *out_sends, grad_value, mixed_r = lax.optimization_barrier(
-                (*out_sends, grad_value, mixed_r)
-            )
-            out_firsts = scatter_first(out_sends)
-            *out_firsts, _ = lax.optimization_barrier((*out_firsts, terms[0]))
-            out_far = scatter_far(out_sends, out_firsts, z)
-            grad_out = scatter_rest(out_sends, out_firsts, out_far, z, c, True)
-            grad_value = join(grad_value[0], sibling(grad_value[1]), c)
+
+        if line4:
+            back_first = after(back_first, terms[0])
+            back_second = scatter_second(back_sends, back_first)
+            back_third = scatter_third(scatter_sums(back_sends, back_second))
+            grad_out = scatter_end(out_sends, out_third, c)
+            grad_value = scatter_end(back_sends, back_third, c)
         else:
             grad_value = scatter_ring(back_sends, c)
             grad_out = scatter_ring(out_sends, c)
-
         if n_node == 4:
             along_x, along_y, kept = terms
             kept = kept.astype(F32)

time: 148 us -> 151 us (1.020)
  local copies, waits for them, and re-layouts: 7.48 us -> 14.4 us
  starting transfers between devices: 52.9 us -> 59.4 us
  Pallas kernels: 30 us -> 23.6 us
  waiting for transfers between devices: 49.6 us -> 44.8 us
    unnamed x52 -> x44, local copies, waits for them, and re-layouts: 4.1 us -> 11.4 us
    ppermute x18 -> x20, starting transfers between devices: 45.3 us -> 52.4 us  [move(): lax.ppermute(x, 'wide', [(2 * s + c, 2 * d + c) for s, d in pairs for c i...]
    ppermute x4, waiting for transfers between devices: 12 us -> 9.2 us  [flip(): return lax.ppermute(x, 'node', [(i, i ^ j) for i in range(n_node)])]
    ppermute x1 -> x0, waiting for transfers between devices: 2.7 us -> none  [scatter_rest(): lax.ppermute(far[1], 'wide', [(2 * s + k, 2 * ((s + 2) % 4) + 1 - k) for...]
    pallas_call x1, Pallas kernels: 7.79 us -> 5.34 us  [body(): call(functools.partial(mixed_kernel, n_slots), 'mixed', [SMEM] + [ANY] *...]
    pallas_call x1, Pallas kernels: 6.71 us -> 4.59 us  [body(): call(grad_out_kernel, 'grad_out', [SMEM] + [ANY] * 2 + [VMEM] * 2, send_s...]
    pallas_call x1, Pallas kernels: 5.2 us -> 3.16 us  [body(): call(functools.partial(terms_kernel, n_node), 'terms', [SMEM] + [VMEM] *...]
    another operation x3 -> x2, local copies, waits for them, and re-layouts: 1.98 us -> 0.17 us  [the longest x1 0.09 us: body(): idx_slots = jnp.stack([jnp.int32(x) for x in (c, *info)])]
  transfers between devices with their start and end apart: 31 -> 32, of which waited for: 15 -> 15; matrix products, arithmetic and copies ran while one was open for 5% -> 3% of each run, Pallas kernels for 20% -> 16%
where the time goes in v5:
time: 151 us; the launch traced here: 150 us
  starting transfers between devices  59.4 us (39%)
  waiting for transfers between devices  44.8 us (30%)
  Pallas kernels  23.6 us (16%)
  local copies, waits for them, and re-layouts  14.4 us (10%)
  other arithmetic  6.97 us (5%)
    ppermute x20, starting transfers between devices, move(): lax.ppermute(x, 'wide', [(2 * s + c, 2 * d + c) for s, d in pairs for c i...  52.4 us
    ppermute x20, waiting for transfers between devices, move(): lax.ppermute(x, 'wide', [(2 * s + c, 2 * d + c) for s, d in pairs for c i...  32.8 us
    unnamed x44, local copies, waits for them, and re-layouts  11.4 us
    ppermute x4, waiting for transfers between devices, flip(): return lax.ppermute(x, 'node', [(i, i ^ j) for i in range(n_node)])  9.2 us
    pallas_call x1, Pallas kernels, body(): call(functools.partial(d_value_kernel, n_slots), 'd_value', [SMEM] + [ANY...  6.08 us
    pallas_call x1, Pallas kernels, body(): call(functools.partial(mixed_kernel, n_slots), 'mixed', [SMEM] + [ANY] *...  5.34 us
    ppermute x4, starting transfers between devices, flip(): return lax.ppermute(x, 'node', [(i, i ^ j) for i in range(n_node)])  5.26 us
    pallas_call x1, Pallas kernels, body(): call(grad_out_kernel, 'grad_out', [SMEM] + [ANY] * 2 + [VMEM] * 2, send_s...  4.59 us
  transfers between devices with their start and end apart: 32, of which 15 were waited for; matrix products, arithmetic and copies ran while one was open for 3% of the time, Pallas kernels for 16%

profile of v5, /device:TPU:0, one launch (start us, length us, event | category | flops | bytes accessed | tf_op | source)
XLA Modules:
  0.0 150.3 jit_solution(9547556108063551735)
XLA Ops:
  0.6 1.0 slice_bitcast_fusion.10
  1.7 1.0 slice_bitcast_fusion.11
  3.3 1.2 collective-permute-done
  4.5 0.7 slice_bitcast_fusion.4
  6.2 1.3 collective-permute-start.3
  7.5 6.0 %collective-permute-start.1 = (bf16[640,256]{1,0:T(8,128)(2,1)S(1)}, bf16[640,256]{1,0:T(8,128)(2,1)}, u32[]{:S(2)}, u32[]{:S(2)}) collective-permute-start(bf16[640,256]{1,0:T(8,128)(2,1)S(1)} %pad_maximum_fusion.5.rest_0_), channel_id=1, source_target_pairs={{0,8},{4,12},{8,16},{12,20},{16,24},{20,28},{1,9},{5,13},{9,17},{1... | collective-permute-start | bytes 983048 | tf_op jit(solution)/shard_map/ppermute | solution.py:213
  13.5 0.7 copy-done.7
  14.2 4.9 %collective-permute-done.3.rest_2_ = bf16[640,256]{1,0:T(8,128)(2,1)} collective-permute-done((bf16[640,256]{1,0:T(8,128)(2,1)S(1)}, bf16[640,256]{1,0:T(8,128)(2,1)}, u32[]{:S(2)}, u32[]{:S(2)}) %collective-permute-start.3) | collective-permute-done | bytes 327712 | tf_op jit(solution)/shard_map/ppermute | solution.py:213
  19.2 1.3 collective-permute-start.4
  20.5 0.7 collective-permute-start.2
  21.2 1.7 %pad_maximum_fusion.6.rest_0_ = bf16[640,256]{1,0:T(8,128)(2,1)} fusion(bf16[320,256]{1,0:T(8,128)(2,1)} %get-tuple-element.127, bf16[320,256]{1,0:T(8,128)(2,1)S(1)} %get-tuple-element.125), kind=kLoop, calls=%fused_computation.32 | loop fusion | flops 655360 | bytes 655360 | tf_op jit(solution)/shard_map/concatenate | solution.py:229
  22.8 7.8 %collective-permute-done.4.rest_4_ = bf16[640,256]{1,0:T(8,128)(2,1)S(1)} collective-permute-done((bf16[640,256]{1,0:T(8,128)(2,1)}, bf16[640,256]{1,0:T(8,128)(2,1)S(1)}, u32[]{:S(2)}, u32[]{:S(2)}) %collective-permute-start.4) | collective-permute-done | bytes 327712 | tf_op jit(solution)/shard_map/ppermute | solution.py:213
  30.7 0.8 broadcast_select_fusion.1
  31.4 1.3 collective-permute-start.8
  32.7 1.3 collective-permute-start.10
  34.0 6.8 %collective-permute-start.9 = (bf16[640,256]{1,0:T(8,128)(2,1)}, bf16[640,256]{1,0:T(8,128)(2,1)}, u32[]{:S(2)}, u32[]{:S(2)}) collective-permute-start(bf16[640,256]{1,0:T(8,128)(2,1)} %pad_maximum_fusion.6.rest_0_), channel_id=1, source_target_pairs={{0,8},{4,12},{8,16},{12,20},{16,24},{20,28},{1,9},{5,13},{9,17},{1... | collective-permute-start | bytes 983048 | tf_op jit(solution)/shard_map/ppermute | solution.py:213
  40.9 3.5 %collective-permute-done.8.rest_5_ = bf16[640,256]{1,0:T(8,128)(2,1)} collective-permute-done((bf16[640,256]{1,0:T(8,128)(2,1)}, bf16[640,256]{1,0:T(8,128)(2,1)}, u32[]{:S(2)}, u32[]{:S(2)}) %collective-permute-start.8) | collective-permute-done | bytes 327712 | tf_op jit(solution)/shard_map/ppermute | solution.py:213
  44.4 4.8 %collective-permute-done.10.rest_2_ = bf16[640,256]{1,0:T(8,128)(2,1)} collective-permute-done((bf16[640,256]{1,0:T(8,128)(2,1)}, bf16[640,256]{1,0:T(8,128)(2,1)}, u32[]{:S(2)}, u32[]{:S(2)}) %collective-permute-start.10) | collective-permute-done | bytes 327712 | tf_op jit(solution)/shard_map/ppermute | solution.py:213
  49.2 0.7 collective-permute-start.12
  49.9 1.3 collective-permute-start.13
  51.2 1.7 %copy-done.1 = bf16[2,2,128,2560]{3,2,1,0:T(8,128)(2,1)S(1)} copy-done((bf16[2,2,128,2560]{3,2,1,0:T(8,128)(2,1)S(1)}, bf16[2,2,128,2560]{3,2,1,0:T(8,128)(2,1)}, u32[]{:S(2)}) %copy-start.1) | copy-done | bytes 2621464
  52.9 1.0 copy-done.8
  53.9 5.3 %mixed.1 = (bf16[512,256]{1,0:T(8,128)(2,1)S(1)}, bf16[512,256]{1,0:T(8,128)(2,1)S(1)}) custom-call(s32[13]{0:T(128)S(1)} %stack.120.idx, bf16[512,2560]{1,0:T(8,128)(2,1)S(1)} %bitcast.73, bf16[512,2560]{1,0:T(8,128)(2,1)} %collective-permute-done.5.act_s.right_s, bf16[4,8,128,128]{3,2,1,0:T(8,128)(2,1)} %bitcast.23.mix_o, ...), custom_call_target="tpu_custom_call" | custom-call | flops 1342177280 | bytes 12582912 | tf_op jit(solution)/shard_map/mixed/pallas_call | solution.py:337
  59.4 1.5 %collective-permute-done.11.mixed_r = bf16[512,256]{1,0:T(8,128)(2,1)S(1)} collective-permute-done((bf16[512,256]{1,0:T(8,128)(2,1)S(1)}, bf16[512,256]{1,0:T(8,128)(2,1)S(1)}, u32[]{:S(2)}, u32[]{:S(2)}) %collective-permute-start.11) | collective-permute-done | bytes 262176 | tf_op jit(solution)/shard_map/ppermute | solution.py:218
  60.9 0.7 copy-done.20
  61.6 0.8 collective-permute-done.13.rest_4_
  62.4 0.7 copy-done.5
  63.1 0.7 copy-done.3
  63.8 1.3 collective-permute-start.14
  65.2 1.0 copy-done.16
  66.1 0.9 copy-done.19
  67.1 4.6 %grad_out.1 = (bf16[2,320,256]{2,1,0:T(8,128)(2,1)S(1)}, bf16[2,320,256]{2,1,0:T(8,128)(2,1)S(1)}, bf16[2,320,256]{2,1,0:T(8,128)(2,1)S(1)}, bf16[2,320,256]{2,1,0:T(8,128)(2,1)S(1)}, bf16[2,320,256]{2,1,0:T(8,128)(2,1)S(1)}) custom-call(s32[6]{0:T(128)S(1)} %stack.128.idx, bf16[512,2560]{1,0:T(8,128)(2,1)S(1)} %bitcast.70, ...), custom_call_target="tpu_custom_call" | custom-call | flops 1342177280 | bytes 12582912 | tf_op jit(solution)/shard_map/grad_out/pallas_call | solution.py:351
  71.7 0.7 copy-done.9
  72.4 0.7 copy-done.11
  73.1 0.7 copy-done.13
  73.9 4.4 %collective-permute-done.14.rest_5_ = bf16[640,256]{1,0:T(8,128)(2,1)S(1)} collective-permute-done((bf16[640,256]{1,0:T(8,128)(2,1)S(1)}, bf16[640,256]{1,0:T(8,128)(2,1)S(1)}, u32[]{:S(2)}, u32[]{:S(2)}) %collective-permute-start.14) | collective-permute-done | bytes 327712 | tf_op jit(solution)/shard_map/ppermute | solution.py:213
  78.2 2.7 %collective-permute-start.16 = (bf16[2,320,256]{2,1,0:T(8,128)(2,1)S(1)}, bf16[2,320,256]{2,1,0:T(8,128)(2,1)S(1)}, u32[]{:S(2)}, u32[]{:S(2)}) collective-permute-start(bf16[2,320,256]{2,1,0:T(8,128)(2,1)S(1)} %get-tuple-element.98), channel_id=1, source_target_pairs={{0,8},{4,12},{24,16},{28,20},{1,9},{5,13},{25,17},{29,21},{2,10},{... | collective-permute-start | bytes 983048 | tf_op jit(solution)/shard_map/ppermute | solution.py:213
  81.0 6.1 %d_value.1 = (bf16[2560,256]{1,0:T(8,128)(2,1)}, bf16[256,1024]{1,0:T(8,128)(2,1)S(1)}) custom-call(s32[13]{0:T(128)S(1)} %stack.120.idx, bf16[512,2560]{1,0:T(8,128)(2,1)S(1)} %bitcast.71, bf16[512,2560]{1,0:T(8,128)(2,1)} %collective-permute-done.7.cot_s, bf16[4,8,128,128]{3,2,1,0:T(8,128)(2,1)} %bitcast.23.mix_o, ...), custom_call_target="tpu_custom_call" | custom-call | flops 1342177280 | bytes 12582912 | tf_op jit(solution)/shard_map/d_value/pallas_call | solution.py:361
  87.2 1.0 collective-permute-done.16
  88.3 0.7 collective-permute-start.18
  89.1 5.0 %collective-permute-start.17 = (bf16[2,320,256]{2,1,0:T(8,128)(2,1)S(1)}, bf16[2,320,256]{2,1,0:T(8,128)(2,1)S(1)}, u32[]{:S(2)}, u32[]{:S(2)}) collective-permute-start(bf16[2,320,256]{2,1,0:T(8,128)(2,1)S(1)} %add_convert_fusion.5), channel_id=1, source_target_pairs={{0,8},{4,12},{8,16},{12,20},{1,9},{5,13},{9,17},{13,21},{2,10},{6,... | collective-permute-start | bytes 983048 | tf_op jit(solution)/shard_map/ppermute | solution.py:213
  94.1 1.7 %copy-done.2 = bf16[2,2,128,2560]{3,2,1,0:T(8,128)(2,1)S(1)} copy-done((bf16[2,2,128,2560]{3,2,1,0:T(8,128)(2,1)S(1)}, bf16[2,2,128,2560]{3,2,1,0:T(8,128)(2,1)}, u32[]{:S(2)}) %copy-start.2) | copy-done | bytes 2621464
  95.8 4.5 %grad_value.1 = (bf16[2,320,256]{2,1,0:T(8,128)(2,1)S(1)}, bf16[2,320,256]{2,1,0:T(8,128)(2,1)S(1)}, bf16[2,320,256]{2,1,0:T(8,128)(2,1)S(1)}, bf16[2,320,256]{2,1,0:T(8,128)(2,1)S(1)}, bf16[2,320,256]{2,1,0:T(8,128)(2,1)S(1)}) custom-call(s32[6]{0:T(128)S(1)} %stack.128.idx, bf16[512,2560]{1,0:T(8,128)(2,1)S(1)} %bitcast.74, ...), custom_call_target="tpu_custom_call" | custom-call | flops 1342177280 | bytes 12582912 | tf_op jit(solution)/shard_map/grad_value/pallas_call | solution.py:374
  100.3 4.9 %collective-permute-start.23 = (bf16[2,320,256]{2,1,0:T(8,128)(2,1)S(1)}, bf16[2,320,256]{2,1,0:T(8,128)(2,1)S(1)}, u32[]{:S(2)}, u32[]{:S(2)}) collective-permute-start(bf16[2,320,256]{2,1,0:T(8,128)(2,1)S(1)} %get-tuple-element.109), channel_id=1, source_target_pairs={{0,8},{4,12},{24,16},{28,20},{1,9},{5,13},{25,17},{29,21},{2,10},{... | collective-permute-start | bytes 983048 | tf_op jit(solution)/shard_map/ppermute | solution.py:213
  105.5 3.2 %terms.1 = (bf16[2,256,640]{2,1,0:T(8,128)(2,1)S(1)}, bf16[2,256,640]{2,1,0:T(8,128)(2,1)S(1)}, bf16[4,256,640]{2,1,0:T(8,128)(2,1)S(1)}) custom-call(s32[4]{0:T(128)S(1)} %pad_add_fusion.idx, bf16[512,256]{1,0:T(8,128)(2,1)S(1)} %copy-done.17, bf16[512,256]{1,0:T(8,128)(2,1)S(1)} %copy-done.21, bf16[2560,256]{1,0:T(8,128)(2,1)} %get-tuple-element.94.w_o, ...), custom_call_target="tpu_custom_call" | custom-call | flops 1342177280 | bytes 12582912 | tf_op jit(solution)/shard_map/terms/pallas_call | solution.py:394
  108.6 2.5 %collective-permute-done.23 = bf16[2,320,256]{2,1,0:T(8,128)(2,1)S(1)} collective-permute-done((bf16[2,320,256]{2,1,0:T(8,128)(2,1)S(1)}, bf16[2,320,256]{2,1,0:T(8,128)(2,1)S(1)}, u32[]{:S(2)}, u32[]{:S(2)}) %collective-permute-start.23) | collective-permute-done | bytes 327712 | tf_op jit(solution)/shard_map/ppermute | solution.py:213
  111.2 0.7 collective-permute-start.26
  111.9 5.0 %collective-permute-start.24 = (bf16[2,320,256]{2,1,0:T(8,128)(2,1)S(1)}, bf16[2,320,256]{2,1,0:T(8,128)(2,1)S(1)}, u32[]{:S(2)}, u32[]{:S(2)}) collective-permute-start(bf16[2,320,256]{2,1,0:T(8,128)(2,1)S(1)} %add_convert_fusion.2), channel_id=1, source_target_pairs={{0,8},{4,12},{8,16},{12,20},{1,9},{5,13},{9,17},{13,21},{2,10},{6,... | collective-permute-start | bytes 983048 | tf_op jit(solution)/shard_map/ppermute | solution.py:213
  117.0 1.6 %collective-permute-start.19 = (bf16[2,256,640]{2,1,0:T(8,128)(2,1)S(1)}, bf16[2,256,640]{2,1,0:T(8,128)(2,1)S(1)}, u32[]{:S(2)}, u32[]{:S(2)}) collective-permute-start(bf16[2,256,640]{2,1,0:T(8,128)(2,1)S(1)} %get-tuple-element.103), channel_id=1, source_target_pairs={{0,1},{1,0},{2,3},{3,2},{4,5},{5,4},{6,7},{7,6},{8,9},{9,8},{10,11... | collective-permute-start | bytes 1966088 | tf_op jit(solution)/shard_map/ppermute | solution.py:221
  118.5 4.5 %collective-permute-start.29 = (bf16[2,320,256]{2,1,0:T(8,128)(2,1)S(1)}, bf16[2,320,256]{2,1,0:T(8,128)(2,1)S(1)}, u32[]{:S(2)}, u32[]{:S(2)}) collective-permute-start(bf16[2,320,256]{2,1,0:T(8,128)(2,1)S(1)} %add_convert_fusion.4), channel_id=1, source_target_pairs={{0,8},{4,12},{8,16},{12,20},{16,24},{20,28},{1,9},{5,13},{9,17},{1... | collective-permute-start | bytes 983048 | tf_op jit(solution)/shard_map/ppermute | solution.py:213
  123.1 1.3 collective-permute-start.30
  124.6 1.6 %collective-permute-start.21 = (bf16[2,256,640]{2,1,0:T(8,128)(2,1)S(1)}, bf16[2,256,640]{2,1,0:T(8,128)(2,1)S(1)}, u32[]{:S(2)}, u32[]{:S(2)}) collective-permute-start(bf16[2,256,640]{2,1,0:T(8,128)(2,1)S(1)} %get-tuple-element.104), channel_id=1, source_target_pairs={{0,2},{1,3},{2,0},{3,1},{4,6},{5,7},{6,4},{7,5},{8,10},{9,11},{10,... | collective-permute-start | bytes 1966088 | tf_op jit(solution)/shard_map/ppermute | solution.py:221
  126.2 1.3 collective-permute-start.27
  127.6 1.5 %collective-permute-done.29 = bf16[2,320,256]{2,1,0:T(8,128)(2,1)S(1)} collective-permute-done((bf16[2,320,256]{2,1,0:T(8,128)(2,1)S(1)}, bf16[2,320,256]{2,1,0:T(8,128)(2,1)S(1)}, u32[]{:S(2)}, u32[]{:S(2)}) %collective-permute-start.29) | collective-permute-done | bytes 327712 | tf_op jit(solution)/shard_map/ppermute | solution.py:213
  129.2 4.4 %collective-permute-start.25 = (bf16[2,320,256]{2,1,0:T(8,128)(2,1)S(1)}, bf16[2,320,256]{2,1,0:T(8,128)(2,1)S(1)}, u32[]{:S(2)}, u32[]{:S(2)}) collective-permute-start(bf16[2,320,256]{2,1,0:T(8,128)(2,1)S(1)} %add_convert_fusion.1), channel_id=1, source_target_pairs={{0,8},{4,12},{8,16},{12,20},{16,24},{20,28},{1,9},{5,13},{9,17},{1... | collective-permute-start | bytes 983048 | tf_op jit(solution)/shard_map/ppermute | solution.py:213
  133.6 1.5 collective-permute-done.30
  135.3 2.9 %collective-permute-done.21 = bf16[2,256,640]{2,1,0:T(8,128)(2,1)S(1)} collective-permute-done((bf16[2,256,640]{2,1,0:T(8,128)(2,1)S(1)}, bf16[2,256,640]{2,1,0:T(8,128)(2,1)S(1)}, u32[]{:S(2)}, u32[]{:S(2)}) %collective-permute-start.21) | collective-permute-done | bytes 655392 | tf_op jit(solution)/shard_map/ppermute | solution.py:221
  138.6 1.6 %collective-permute-start.20 = (bf16[256,640]{1,0:T(8,128)(2,1)S(1)}, bf16[256,640]{1,0:T(8,128)(2,1)S(1)}, u32[]{:S(2)}, u32[]{:S(2)}) collective-permute-start(bf16[256,640]{1,0:T(8,128)(2,1)S(1)} %get-tuple-element.117), channel_id=1, source_target_pairs={{0,2},{1,3},{2,0},{3,1},{4,6},{5,7},{6,4},{7,5},{8,10},{9,11},{10,... | collective-permute-start | bytes 983048 | tf_op jit(solution)/shard_map/ppermute | solution.py:221
  140.2 0.5 collective-permute-start.22
  141.0 4.9 %collective-permute-done.20 = bf16[256,640]{1,0:T(8,128)(2,1)S(1)} collective-permute-done((bf16[256,640]{1,0:T(8,128)(2,1)S(1)}, bf16[256,640]{1,0:T(8,128)(2,1)S(1)}, u32[]{:S(2)}, u32[]{:S(2)}) %collective-permute-start.20) | collective-permute-done | bytes 327712 | tf_op jit(solution)/shard_map/ppermute | solution.py:221
  145.8 1.4 collective-permute-done.22
  147.5 0.9 pad_maximum_fusion
  148.5 0.9 pad_maximum_fusion.1
  149.4 0.9 pad_maximum_fusion.2
  (80 shorter events, 3.9 us)
Async XLA Ops:
  2.7 3.0 %copy-start = (bf16[2,2,128,2560]{3,2,1,0:T(8,128)(2,1)S(1)}, bf16[2,2,128,2560]{3,2,1,0:T(8,128)(2,1)}, u32[]{:S(2)}) copy-start(bf16[2,2,128,2560]{3,2,1,0:T(8,128)(2,1)} %param.7) | copy-start | bytes 7864324
  2.8 1.8 %collective-permute-start = (bf16[2,320,256]{2,1,0:T(8,128)(2,1)S(1)}, bf16[2,320,256]{2,1,0:T(8,128)(2,1)S(1)}, u32[]{:S(2)}, u32[]{:S(2)}) collective-permute-start(bf16[2,320,256]{2,1,0:T(8,128)(2,1)S(1)} %get-tuple-element.124), channel_id=1, source_target_pairs={{0,4},{4,0},{8,12},{12,8},{16,20},{20,16},{24,28},{28,24},{1,5},{5... | collective-permute-start | bytes 983048 | tf_op jit(solution)/shard_map/ppermute | solution.py:218
  5.3 25.4 %collective-permute-start.5 = (bf16[512,2560]{1,0:T(8,128)(2,1)}, bf16[512,2560]{1,0:T(8,128)(2,1)}, u32[]{:S(2)}, u32[]{:S(2)}) collective-permute-start(bf16[512,2560]{1,0:T(8,128)(2,1)} %bitcast.72), channel_id=1, source_target_pairs={{0,4},{4,0},{8,12},{12,8},{16,20},{20,16},{24,28},{28,24},{1,5},{5... | collective-permute-start | bytes 7864328 | tf_op jit(solution)/shard_map/ppermute | solution.py:218
  5.7 25.0 %collective-permute-start.7 = (bf16[512,2560]{1,0:T(8,128)(2,1)S(1)}, bf16[512,2560]{1,0:T(8,128)(2,1)}, u32[]{:S(2)}, u32[]{:S(2)}) collective-permute-start(bf16[512,2560]{1,0:T(8,128)(2,1)S(1)} %bitcast.69), channel_id=1, source_target_pairs={{0,4},{4,0},{8,12},{12,8},{16,20},{20,16},{24,28},{28,24},{1,5},{5... | collective-permute-start | bytes 7864328 | tf_op jit(solution)/shard_map/ppermute | solution.py:218
  5.8 24.8 %collective-permute-start.6 = (bf16[4,8,128,128]{3,2,1,0:T(8,128)(2,1)}, bf16[4,8,128,128]{3,2,1,0:T(8,128)(2,1)}, u32[]{:S(2)}, u32[]{:S(2)}) collective-permute-start(bf16[4,8,128,128]{3,2,1,0:T(8,128)(2,1)} %bitcast.23.mix_o), channel_id=1, source_target_pairs={{0,4},{4,0},{8,12},{12,8},{16,20},{20,16},{24,28},{28,24},{1,5},{5... | collective-permute-start | bytes 3145736 | tf_op jit(solution)/shard_map/ppermute | solution.py:218
  6.2 13.0 %collective-permute-start.3 = (bf16[640,256]{1,0:T(8,128)(2,1)S(1)}, bf16[640,256]{1,0:T(8,128)(2,1)}, u32[]{:S(2)}, u32[]{:S(2)}) collective-permute-start(bf16[640,256]{1,0:T(8,128)(2,1)S(1)} %pad_maximum_fusion.5.rest_0_), channel_id=1, source_target_pairs={{24,16},{28,20},{16,8},{20,12},{8,0},{12,4},{25,17},{29,21},{17,9}... | collective-permute-start | bytes 983048 | tf_op jit(solution)/shard_map/ppermute | solution.py:213
  7.5 13.0 %collective-permute-start.1 = (bf16[640,256]{1,0:T(8,128)(2,1)S(1)}, bf16[640,256]{1,0:T(8,128)(2,1)}, u32[]{:S(2)}, u32[]{:S(2)}) collective-permute-start(bf16[640,256]{1,0:T(8,128)(2,1)S(1)} %pad_maximum_fusion.5.rest_0_), channel_id=1, source_target_pairs={{0,8},{4,12},{8,16},{12,20},{16,24},{20,28},{1,9},{5,13},{9,17},{1... | collective-permute-start | bytes 983048 | tf_op jit(solution)/shard_map/ppermute | solution.py:213
  13.5 0.7 copy-start.7
  19.2 11.5 %collective-permute-start.4 = (bf16[640,256]{1,0:T(8,128)(2,1)}, bf16[640,256]{1,0:T(8,128)(2,1)S(1)}, u32[]{:S(2)}, u32[]{:S(2)}) collective-permute-start(bf16[640,256]{1,0:T(8,128)(2,1)} %collective-permute-done.3.rest_2_), channel_id=1, source_target_pairs={{16,8},{20,12},{8,0},{12,4},{17,9},{21,13},{9,1},{13,5},{18,10},{2... | collective-permute-start | bytes 983048 | tf_op jit(solution)/shard_map/ppermute | solution.py:213
  20.5 10.2 %collective-permute-start.2 = (bf16[640,256]{1,0:T(8,128)(2,1)}, bf16[640,256]{1,0:T(8,128)(2,1)S(1)}, u32[]{:S(2)}, u32[]{:S(2)}) collective-permute-start(bf16[640,256]{1,0:T(8,128)(2,1)} %collective-permute-done.1.rest_1_), channel_id=1, source_target_pairs={{8,16},{12,20},{16,24},{20,28},{9,17},{13,21},{17,25},{21,29},{10,... | collective-permute-start | bytes 983048 | tf_op jit(solution)/shard_map/ppermute | solution.py:213
  31.4 13.0 %collective-permute-start.8 = (bf16[640,256]{1,0:T(8,128)(2,1)}, bf16[640,256]{1,0:T(8,128)(2,1)}, u32[]{:S(2)}, u32[]{:S(2)}) collective-permute-start(bf16[640,256]{1,0:T(8,128)(2,1)} %broadcast_select_fusion.1), channel_id=1, source_target_pairs={{16,24},{20,28},{8,0},{12,4},{17,25},{21,29},{9,1},{13,5},{18,26},... | collective-permute-start | bytes 983048 | tf_op jit(solution)/shard_map/ppermute | solution.py:213
  32.7 16.5 %collective-permute-start.10 = (bf16[640,256]{1,0:T(8,128)(2,1)}, bf16[640,256]{1,0:T(8,128)(2,1)}, u32[]{:S(2)}, u32[]{:S(2)}) collective-permute-start(bf16[640,256]{1,0:T(8,128)(2,1)} %pad_maximum_fusion.6.rest_0_), channel_id=1, source_target_pairs={{24,16},{28,20},{16,8},{20,12},{8,0},{12,4},{25,17},{29,21},{17,9}... | collective-permute-start | bytes 983048 | tf_op jit(solution)/shard_map/ppermute | solution.py:213
  34.0 15.2 %collective-permute-start.9 = (bf16[640,256]{1,0:T(8,128)(2,1)}, bf16[640,256]{1,0:T(8,128)(2,1)}, u32[]{:S(2)}, u32[]{:S(2)}) collective-permute-start(bf16[640,256]{1,0:T(8,128)(2,1)} %pad_maximum_fusion.6.rest_0_), channel_id=1, source_target_pairs={{0,8},{4,12},{8,16},{12,20},{16,24},{20,28},{1,9},{5,13},{9,17},{1... | collective-permute-start | bytes 983048 | tf_op jit(solution)/shard_map/ppermute | solution.py:213
  49.2 12.4 %collective-permute-start.12 = (bf16[640,256]{1,0:T(8,128)(2,1)}, bf16[640,256]{1,0:T(8,128)(2,1)S(1)}, u32[]{:S(2)}, u32[]{:S(2)}) collective-permute-start(bf16[640,256]{1,0:T(8,128)(2,1)} %collective-permute-done.9.rest_1_), channel_id=1, source_target_pairs={{8,16},{12,20},{16,24},{20,28},{9,17},{13,21},{17,25},{21,29},{10,... | collective-permute-start | bytes 983048 | tf_op jit(solution)/shard_map/ppermute | solution.py:213
  49.9 12.4 %collective-permute-start.13 = (bf16[640,256]{1,0:T(8,128)(2,1)}, bf16[640,256]{1,0:T(8,128)(2,1)S(1)}, u32[]{:S(2)}, u32[]{:S(2)}) collective-permute-start(bf16[640,256]{1,0:T(8,128)(2,1)} %collective-permute-done.10.rest_2_), channel_id=1, source_target_pairs={{16,8},{20,12},{8,0},{12,4},{17,9},{21,13},{9,1},{13,5},{18,10},{2... | collective-permute-start | bytes 983048 | tf_op jit(solution)/shard_map/ppermute | solution.py:213
  51.2 1.7 %copy-start.1 = (bf16[2,2,128,2560]{3,2,1,0:T(8,128)(2,1)S(1)}, bf16[2,2,128,2560]{3,2,1,0:T(8,128)(2,1)}, u32[]{:S(2)}) copy-start(bf16[2,2,128,2560]{3,2,1,0:T(8,128)(2,1)} %param.5) | copy-start | bytes 7864324
  52.9 1.0 copy-start.8
  59.3 3.1 %copy-start.15 = (bf16[512,256]{1,0:T(8,128)(2,1)}, bf16[512,256]{1,0:T(8,128)(2,1)S(1)}, u32[]{:S(2)}) copy-start(bf16[512,256]{1,0:T(8,128)(2,1)S(1)} %get-tuple-element.77.mixed_o) | copy-start | bytes 786436
  59.3 3.1 %copy-start.18 = (bf16[512,256]{1,0:T(8,128)(2,1)}, bf16[512,256]{1,0:T(8,128)(2,1)S(1)}, u32[]{:S(2)}) copy-start(bf16[512,256]{1,0:T(8,128)(2,1)S(1)} %get-tuple-element.82.mixed_s) | copy-start | bytes 786436
  59.3 1.6 %collective-permute-start.11 = (bf16[512,256]{1,0:T(8,128)(2,1)S(1)}, bf16[512,256]{1,0:T(8,128)(2,1)S(1)}, u32[]{:S(2)}, u32[]{:S(2)}) collective-permute-start(bf16[512,256]{1,0:T(8,128)(2,1)S(1)} %get-tuple-element.82.mixed_s), channel_id=1, source_target_pairs={{0,4},{4,0},{8,12},{12,8},{16,20},{20,16},{24,28},{28,24},{1,5},{5... | collective-permute-start | bytes 786440 | tf_op jit(solution)/shard_map/ppermute | solution.py:218
  60.9 0.7 copy-start.20
  62.3 0.7 copy-start.5
  63.1 0.7 copy-start.3
  63.8 14.4 %collective-permute-start.14 = (bf16[640,256]{1,0:T(8,128)(2,1)S(1)}, bf16[640,256]{1,0:T(8,128)(2,1)S(1)}, u32[]{:S(2)}, u32[]{:S(2)}) collective-permute-start(bf16[640,256]{1,0:T(8,128)(2,1)S(1)} %broadcast_select_fusion), channel_id=1, source_target_pairs={{16,24},{20,28},{8,0},{12,4},{17,25},{21,29},{9,1},{13,5},{18,26},... | collective-permute-start | bytes 983048 | tf_op jit(solution)/shard_map/ppermute | solution.py:213
  65.2 1.0 copy-start.16
  66.1 0.9 copy-start.19
  67.1 13.9 %copy-start.4 = (bf16[640,256]{1,0:T(8,128)(2,1)S(1)}, bf16[640,256]{1,0:T(8,128)(2,1)}, u32[]{:S(2)}) copy-start(bf16[640,256]{1,0:T(8,128)(2,1)} %copy-done.3) | copy-start | bytes 983044
  67.1 13.9 %copy-start.6 = (bf16[640,256]{1,0:T(8,128)(2,1)S(1)}, bf16[640,256]{1,0:T(8,128)(2,1)}, u32[]{:S(2)}) copy-start(bf16[640,256]{1,0:T(8,128)(2,1)} %copy-done.5) | copy-start | bytes 983044
  71.7 0.7 copy-start.9
  72.4 0.7 copy-start.11
  73.1 0.7 copy-start.13
  78.2 10.0 %collective-permute-start.16 = (bf16[2,320,256]{2,1,0:T(8,128)(2,1)S(1)}, bf16[2,320,256]{2,1,0:T(8,128)(2,1)S(1)}, u32[]{:S(2)}, u32[]{:S(2)}) collective-permute-start(bf16[2,320,256]{2,1,0:T(8,128)(2,1)S(1)} %get-tuple-element.98), channel_id=1, source_target_pairs={{0,8},{4,12},{24,16},{28,20},{1,9},{5,13},{25,17},{29,21},{2,10},{... | collective-permute-start | bytes 983048 | tf_op jit(solution)/shard_map/ppermute | solution.py:213
  87.1 18.3 %collective-permute-start.15 = (bf16[2560,256]{1,0:T(8,128)(2,1)}, bf16[2560,256]{1,0:T(8,128)(2,1)S(1)}, u32[]{:S(2)}, u32[]{:S(2)}) collective-permute-start(bf16[2560,256]{1,0:T(8,128)(2,1)} %get-tuple-element.94.w_o), channel_id=1, source_target_pairs={{0,4},{4,0},{8,12},{12,8},{16,20},{20,16},{24,28},{28,24},{1,5},{5... | collective-permute-start | bytes 3932168 | tf_op jit(solution)/shard_map/ppermute | solution.py:218
  88.3 16.9 %collective-permute-start.18 = (bf16[2,320,256]{2,1,0:T(8,128)(2,1)S(1)}, bf16[2,320,256]{2,1,0:T(8,128)(2,1)S(1)}, u32[]{:S(2)}, u32[]{:S(2)}) collective-permute-start(bf16[2,320,256]{2,1,0:T(8,128)(2,1)S(1)} %add_convert_fusion.5), channel_id=1, source_target_pairs={{24,16},{28,20},{16,8},{20,12},{25,17},{29,21},{17,9},{21,13},{26,... | collective-permute-start | bytes 983048 | tf_op jit(solution)/shard_map/ppermute | solution.py:213
  89.1 16.3 %collective-permute-start.17 = (bf16[2,320,256]{2,1,0:T(8,128)(2,1)S(1)}, bf16[2,320,256]{2,1,0:T(8,128)(2,1)S(1)}, u32[]{:S(2)}, u32[]{:S(2)}) collective-permute-start(bf16[2,320,256]{2,1,0:T(8,128)(2,1)S(1)} %add_convert_fusion.5), channel_id=1, source_target_pairs={{0,8},{4,12},{8,16},{12,20},{1,9},{5,13},{9,17},{13,21},{2,10},{6,... | collective-permute-start | bytes 983048 | tf_op jit(solution)/shard_map/ppermute | solution.py:213
  94.1 1.7 %copy-start.2 = (bf16[2,2,128,2560]{3,2,1,0:T(8,128)(2,1)S(1)}, bf16[2,2,128,2560]{3,2,1,0:T(8,128)(2,1)}, u32[]{:S(2)}) copy-start(bf16[2,2,128,2560]{3,2,1,0:T(8,128)(2,1)} %param.5) | copy-start | bytes 7864324
  95.8 9.4 %copy-start.14 = (bf16[2,320,256]{2,1,0:T(8,128)(2,1)S(1)}, bf16[2,320,256]{2,1,0:T(8,128)(2,1)}, u32[]{:S(2)}) copy-start(bf16[2,320,256]{2,1,0:T(8,128)(2,1)} %copy-done.13) | copy-start | bytes 983044
  95.8 9.5 %copy-start.12 = (bf16[2,320,256]{2,1,0:T(8,128)(2,1)S(1)}, bf16[2,320,256]{2,1,0:T(8,128)(2,1)}, u32[]{:S(2)}) copy-start(bf16[2,320,256]{2,1,0:T(8,128)(2,1)} %copy-done.11) | copy-start | bytes 983044
  100.3 5.1 %copy-start.17 = (bf16[512,256]{1,0:T(8,128)(2,1)S(1)}, bf16[512,256]{1,0:T(8,128)(2,1)}, u32[]{:S(2)}) copy-start(bf16[512,256]{1,0:T(8,128)(2,1)} %copy-done.15) | copy-start | bytes 786436
  100.3 5.1 %copy-start.21 = (bf16[512,256]{1,0:T(8,128)(2,1)S(1)}, bf16[512,256]{1,0:T(8,128)(2,1)}, u32[]{:S(2)}) copy-start(bf16[512,256]{1,0:T(8,128)(2,1)} %copy-done.20) | copy-start | bytes 786436
  100.3 10.8 %collective-permute-start.23 = (bf16[2,320,256]{2,1,0:T(8,128)(2,1)S(1)}, bf16[2,320,256]{2,1,0:T(8,128)(2,1)S(1)}, u32[]{:S(2)}, u32[]{:S(2)}) collective-permute-start(bf16[2,320,256]{2,1,0:T(8,128)(2,1)S(1)} %get-tuple-element.109), channel_id=1, source_target_pairs={{0,8},{4,12},{24,16},{28,20},{1,9},{5,13},{25,17},{29,21},{2,10},{... | collective-permute-start | bytes 983048 | tf_op jit(solution)/shard_map/ppermute | solution.py:213
  111.2 13.3 %collective-permute-start.26 = (bf16[2,320,256]{2,1,0:T(8,128)(2,1)S(1)}, bf16[2,320,256]{2,1,0:T(8,128)(2,1)S(1)}, u32[]{:S(2)}, u32[]{:S(2)}) collective-permute-start(bf16[2,320,256]{2,1,0:T(8,128)(2,1)S(1)} %add_convert_fusion.2), channel_id=1, source_target_pairs={{24,16},{28,20},{16,8},{20,12},{25,17},{29,21},{17,9},{21,13},{26,... | collective-permute-start | bytes 983048 | tf_op jit(solution)/shard_map/ppermute | solution.py:213
  111.9 14.3 %collective-permute-start.24 = (bf16[2,320,256]{2,1,0:T(8,128)(2,1)S(1)}, bf16[2,320,256]{2,1,0:T(8,128)(2,1)S(1)}, u32[]{:S(2)}, u32[]{:S(2)}) collective-permute-start(bf16[2,320,256]{2,1,0:T(8,128)(2,1)S(1)} %add_convert_fusion.2), channel_id=1, source_target_pairs={{0,8},{4,12},{8,16},{12,20},{1,9},{5,13},{9,17},{13,21},{2,10},{6,... | collective-permute-start | bytes 983048 | tf_op jit(solution)/shard_map/ppermute | solution.py:213
  117.0 21.4 %collective-permute-start.19 = (bf16[2,256,640]{2,1,0:T(8,128)(2,1)S(1)}, bf16[2,256,640]{2,1,0:T(8,128)(2,1)S(1)}, u32[]{:S(2)}, u32[]{:S(2)}) collective-permute-start(bf16[2,256,640]{2,1,0:T(8,128)(2,1)S(1)} %get-tuple-element.103), channel_id=1, source_target_pairs={{0,1},{1,0},{2,3},{3,2},{4,5},{5,4},{6,7},{7,6},{8,9},{9,8},{10,11... | collective-permute-start | bytes 1966088 | tf_op jit(solution)/shard_map/ppermute | solution.py:221
  118.5 10.7 %collective-permute-start.29 = (bf16[2,320,256]{2,1,0:T(8,128)(2,1)S(1)}, bf16[2,320,256]{2,1,0:T(8,128)(2,1)S(1)}, u32[]{:S(2)}, u32[]{:S(2)}) collective-permute-start(bf16[2,320,256]{2,1,0:T(8,128)(2,1)S(1)} %add_convert_fusion.4), channel_id=1, source_target_pairs={{0,8},{4,12},{8,16},{12,20},{16,24},{20,28},{1,9},{5,13},{9,17},{1... | collective-permute-start | bytes 983048 | tf_op jit(solution)/shard_map/ppermute | solution.py:213
  123.1 12.0 %collective-permute-start.30 = (bf16[2,320,256]{2,1,0:T(8,128)(2,1)S(1)}, bf16[2,320,256]{2,1,0:T(8,128)(2,1)S(1)}, u32[]{:S(2)}, u32[]{:S(2)}) collective-permute-start(bf16[2,320,256]{2,1,0:T(8,128)(2,1)S(1)} %add_convert_fusion.3), channel_id=1, source_target_pairs={{24,16},{28,20},{16,8},{20,12},{8,0},{12,4},{25,17},{29,21},{17,9}... | collective-permute-start | bytes 983048 | tf_op jit(solution)/shard_map/ppermute | solution.py:213
  124.5 10.5 %copy-start.10 = (bf16[2,320,256]{2,1,0:T(8,128)(2,1)S(1)}, bf16[2,320,256]{2,1,0:T(8,128)(2,1)}, u32[]{:S(2)}) copy-start(bf16[2,320,256]{2,1,0:T(8,128)(2,1)} %copy-done.9) | copy-start | bytes 983044
  124.6 13.7 %collective-permute-start.21 = (bf16[2,256,640]{2,1,0:T(8,128)(2,1)S(1)}, bf16[2,256,640]{2,1,0:T(8,128)(2,1)S(1)}, u32[]{:S(2)}, u32[]{:S(2)}) collective-permute-start(bf16[2,256,640]{2,1,0:T(8,128)(2,1)S(1)} %get-tuple-element.104), channel_id=1, source_target_pairs={{0,2},{1,3},{2,0},{3,1},{4,6},{5,7},{6,4},{7,5},{8,10},{9,11},{10,... | collective-permute-start | bytes 1966088 | tf_op jit(solution)/shard_map/ppermute | solution.py:221
  126.2 14.5 %collective-permute-start.27 = (bf16[2,320,256]{2,1,0:T(8,128)(2,1)S(1)}, bf16[2,320,256]{2,1,0:T(8,128)(2,1)S(1)}, u32[]{:S(2)}, u32[]{:S(2)}) collective-permute-start(bf16[2,320,256]{2,1,0:T(8,128)(2,1)S(1)} %add_convert_fusion), channel_id=1, source_target_pairs={{24,16},{28,20},{16,8},{20,12},{8,0},{12,4},{25,17},{29,21},{17,9}... | collective-permute-start | bytes 983048 | tf_op jit(solution)/shard_map/ppermute | solution.py:213
  129.2 11.5 %collective-permute-start.25 = (bf16[2,320,256]{2,1,0:T(8,128)(2,1)S(1)}, bf16[2,320,256]{2,1,0:T(8,128)(2,1)S(1)}, u32[]{:S(2)}, u32[]{:S(2)}) collective-permute-start(bf16[2,320,256]{2,1,0:T(8,128)(2,1)S(1)} %add_convert_fusion.1), channel_id=1, source_target_pairs={{0,8},{4,12},{8,16},{12,20},{16,24},{20,28},{1,9},{5,13},{9,17},{1... | collective-permute-start | bytes 983048 | tf_op jit(solution)/shard_map/ppermute | solution.py:213
  135.2 13.1 %collective-permute-start.31 = (f32[320,256]{1,0:T(8,128)S(1)}, f32[320,256]{1,0:T(8,128)S(1)}, u32[]{:S(2)}, u32[]{:S(2)}) collective-permute-start(f32[320,256]{1,0:T(8,128)S(1)} %slice_bitcast_fusion), channel_id=1, source_target_pairs={{0,4},{4,0},{8,12},{12,8},{16,20},{20,16},{24,28},{28,24},{1,5},{5... | collective-permute-start | bytes 983048 | tf_op jit(solution)/shard_map/ppermute | solution.py:218
  138.6 7.3 %collective-permute-start.20 = (bf16[256,640]{1,0:T(8,128)(2,1)S(1)}, bf16[256,640]{1,0:T(8,128)(2,1)S(1)}, u32[]{:S(2)}, u32[]{:S(2)}) collective-permute-start(bf16[256,640]{1,0:T(8,128)(2,1)S(1)} %get-tuple-element.117), channel_id=1, source_target_pairs={{0,2},{1,3},{2,0},{3,1},{4,6},{5,7},{6,4},{7,5},{8,10},{9,11},{10,... | collective-permute-start | bytes 983048 | tf_op jit(solution)/shard_map/ppermute | solution.py:221
  140.2 7.1 %collective-permute-start.22 = (bf16[256,640]{1,0:T(8,128)(2,1)S(1)}, bf16[256,640]{1,0:T(8,128)(2,1)S(1)}, u32[]{:S(2)}, u32[]{:S(2)}) collective-permute-start(bf16[256,640]{1,0:T(8,128)(2,1)S(1)} %get-tuple-element.118), channel_id=1, source_target_pairs={{0,1},{1,0},{2,3},{3,2},{4,5},{5,4},{6,7},{7,6},{8,9},{9,8},{10,11... | collective-permute-start | bytes 983048 | tf_op jit(solution)/shard_map/ppermute | solution.py:221
  140.9 7.5 %collective-permute-start.28 = (f32[320,256]{1,0:T(8,128)S(1)}, f32[320,256]{1,0:T(8,128)S(1)}, u32[]{:S(2)}, u32[]{:S(2)}) collective-permute-start(f32[320,256]{1,0:T(8,128)S(1)} %slice_bitcast_fusion.2), channel_id=1, source_target_pairs={{0,4},{4,0},{8,12},{12,8},{16,20},{20,16},{24,28},{28,24},{1,5},{5... | collective-permute-start | bytes 983048 | tf_op jit(solution)/shard_map/ppermute | solution.py:218

commit v6 on v5

--- a/solution.py
+++ b/solution.py
@@ -11,7 +11,7 @@
 HEAD_DIM = 64
 F32 = jnp.float32
 BF16 = jnp.bfloat16
-VMEM_LIMIT = 24 * 1024 * 1024
+VMEM_LIMIT = 40 * 1024 * 1024
 
 
 def dot(a, b, ca=1, cb=0):
@@ -32,11 +32,11 @@
 def place(idx, slots, w_ref):
     core = idx[0]
     for j, slot in enumerate(slots):
-        depth = slot.shape[0] // 2
+        depth = slot.shape[1]
 
         @pl.when(idx[2 + 2 * j] == 1)
         def _(slot=slot, depth=depth, plane=idx[1 + 2 * j]):
-            mine, other = slot[:depth, :], slot[depth:, :]
+            mine, other = slot[0], slot[1]
             low = jnp.where(core == 0, mine, other)
             high = jnp.where(core == 0, other, mine)
             w_ref[rows_at(plane, 2 * depth), :] = jnp.concatenate([low, high], axis=0)
@@ -63,8 +63,8 @@
     return [(h, min(2, heads - h)) for h in range(0, heads, 2)]
 
 
-def d_value_kernel(n_slots, idx, cot_o, cot_s, mix_o, mix_s, *rest):
-    slots, (w_out, left_v, cot_v, mix_v, sems) = rest[:n_slots], rest[n_slots:]
+def d_value_kernel(n_slots, n_ties, idx, cot_o, cot_s, mix_o, mix_s, *rest):
+    slots, (w_out, left_v, cot_v, mix_v, sems) = rest[:n_slots], rest[n_slots + n_ties :]
     groups, _, seq, _ = mix_o.shape
     heads = mix_v.shape[2]
     here = pl.ds(idx[0] * heads, heads)
@@ -99,8 +99,8 @@
                 ).astype(BF16)
 
 
-def gradient_kernel(idx, right_o, right_s, left_ref, *rest):
-    outs, (right_v, grad_v, sems) = rest[:-3], rest[-3:]
+def gradient_kernel(n_ties, idx, right_o, right_s, left_ref, *rest):
+    outs, (right_v, grad_v, sems) = rest[n_ties:-3], rest[-3:]
     tokens, _ = right_o.shape
     copies = begin(
         [(right_o, right_v.at[pl.ds(0, tokens)]), (right_s, right_v.at[pl.ds(tokens, tokens)])],
@@ -112,8 +112,8 @@
     hand_out(idx, 1, grad_v, outs)
 
 
-def mixed_kernel(n_slots, idx, act_o, act_s, mix_o, mix_s, *rest):
-    slots, (mixed_o, mixed_s, w_v, act_v, mix_v, sems) = rest[:n_slots], rest[n_slots:]
+def mixed_kernel(n_slots, n_ties, idx, act_o, act_s, mix_o, mix_s, *rest):
+    slots, (mixed_o, mixed_s, w_v, act_v, mix_v, sems) = rest[:n_slots], rest[n_slots + n_ties :]
     groups, _, seq, _ = mix_o.shape
     heads = mix_v.shape[2]
     here = pl.ds(idx[0] * heads, heads)
@@ -147,7 +147,8 @@
                 ).astype(BF16)
 
 
-def grad_out_kernel(idx, cot_o, cot_s, mixed_o, mixed_s, *rest):
+def grad_out_kernel(n_pass, n_ties, idx, cot_o, cot_s, mixed_o, mixed_s, *rest):
+    passed, rest = rest[:n_pass], rest[n_pass + n_ties :]
     outs, (cot_v, left_v, grad_v, sems) = rest[:-4], rest[-4:]
     tokens, _ = cot_o.shape
     copies = begin(
@@ -159,9 +160,15 @@
     copies[1].wait()
     gradient_rows(left_v[...], cot_v, grad_v, 640)
     hand_out(idx, 1, grad_v, outs)
-
-
-def terms_kernel(n_node, idx, mixed_o, mixed_r, w_o, w_r, *outs):
+    for j, block in enumerate(passed):
+
+        @pl.when(idx[1 + len(outs) + j] == 1)
+        def _(block=block):
+            outs[-1][...] = block[...]
+
+
+def terms_kernel(n_node, n_ties, idx, mixed_o, mixed_r, w_o, w_r, *rest):
+    outs = rest[n_ties:]
     depth = w_o.shape[0] // n_node
     half = mixed_o.shape[0] // 2
     for j in range(n_node):
@@ -184,8 +191,14 @@
 
 
 ANY = pl.BlockSpec(memory_space=pltpu.HBM)
+TIE = pl.BlockSpec(memory_space=pl.ANY)
 SMEM = pl.BlockSpec(memory_space=pltpu.SMEM)
 VMEM = pl.BlockSpec(memory_space=pltpu.VMEM)
+
+
+def select_kernel(take, first, second, *rest):
+    out = rest[-1]
+    out[...] = jnp.where(take[0] == 1, first[...], second[...])
 
 
 def call(kernel, name, in_specs, out_shapes, scratch, flops):
@@ -201,10 +214,6 @@
     )
 
 
-def after(x, *others):
-    return lax.optimization_barrier((x, *others))[0]
-
-
 def make_body(n_wide, n_node):
     planes = n_wide // 2
     line4 = planes == 4
@@ -212,6 +221,14 @@
     def move(x, pairs):
         return lax.ppermute(
             x, "wide", [(2 * s + c, 2 * d + c) for s, d in pairs for c in range(2)]
+        )
+
+    def apart(ahead, back, pairs):
+        mirror = [(planes - 1 - s, planes - 1 - d) for s, d in pairs]
+        lines = (pairs, mirror), (mirror, pairs)
+        return tuple(
+            lax.ppermute(x, "wide", [(2 * s + c, 2 * d + c) for c in range(2) for s, d in line[c]])
+            for x, line in zip((ahead, back), lines)
         )
 
     def sibling(x):
@@ -226,53 +243,44 @@
         high = jnp.stack([w[:, cols:] for w in weights])
         got = sibling(jnp.where(c == 0, high, low))
         mine = jnp.where(c == 0, low, high)
-        return [jnp.concatenate([mine[i], got[i]], axis=0) for i in range(len(weights))]
-
-    right = [[(s, s + 1) for s in range(planes - 1)][k:] for k in range(planes)]
-    left = [[(s + 1, s) for s in reversed(range(planes - 1))][k:] for k in range(planes)]
+        return got, [jnp.stack([mine[i], got[i]]) for i in range(len(weights))]
+
+    line = [(s, s + 1) for s in range(planes - 1)]
 
     def gather_ring(u):
         return [u] + [
             move(u, [(s, (s - j) % planes) for s in range(planes)]) for j in range(1, planes)
         ]
 
-    def gather_step(u, k):
-        return move(u[0], right[k]), move(u[1], left[k])
-
-    def gather_last(second, z):
-        return move(jnp.where(z == 2, *second), right[2] + left[2])
-
-    def slot_planes(z):
+    def slot_planes(z, d):
         if not line4:
             return [x for j in range(planes) for x in (lax.rem(z + j, planes), 1)]
-        last = jnp.where(z == 0, 3, 0)
-        return [
-            *(z, 1, jnp.maximum(z - 1, 0), z >= 1, jnp.minimum(z + 1, 3), z <= 2),
-            *(jnp.maximum(z - 2, 0), z >= 2, jnp.minimum(z + 2, 3), z <= 1),
-            *(last, (z == 0) | (z == 3)),
-        ]
-
-    def send_planes(z):
+        found = [z, 1]
+        for plane in (z - d, z + d, z - 2 * d, z + 2 * d):
+            found += [jnp.clip(plane, 0, 3), (plane >= 0) & (plane <= 3)]
+        return found + [3 - z, (z == 0) | (z == 3)]
+
+    def send_planes(z, d):
         if not line4:
             return [lax.rem(z + j, planes) for j in range(planes)]
-        across = jnp.where(z == 0, 3, 0)
-        return [z, jnp.minimum(z + 1, 3), jnp.maximum(z - 1, 0), lax.rem(z + 2, 4), across]
+        near = [jnp.clip(plane, 0, 3) for plane in (z + d, z - d)]
+        return [z, *near, lax.rem(z + 2, 4), 3 - z]
 
     def added(block, got):
         return (block.astype(F32) + got.astype(F32)).astype(BF16)
 
-    def scatter_first(blocks):
-        return move(blocks[4], [(0, 1), (3, 2)])
-
-    def scatter_second(blocks, first):
-        far = added(blocks[3], first)
-        return move(far, [(0, 1), (1, 2)]), move(far, [(3, 2), (2, 1)])
+    def scatter_far(blocks, first, z):
+        inside = (z == 1) | (z == 2)
+        return added(blocks[3], jnp.where(inside, first, jnp.zeros_like(first)))
+
+    def scatter_second(far):
+        return apart(far, far, line[:2])
 
     def scatter_sums(blocks, second):
         return added(blocks[1], second[0]), added(blocks[2], second[1])
 
     def scatter_third(sums):
-        return move(sums[0], right[0]), move(sums[1], left[0])
+        return apart(*sums, line)
 
     def scatter_end(blocks, third, c):
         total = blocks[0].astype(F32) + third[0].astype(F32) + third[1].astype(F32)
@@ -305,86 +313,87 @@
         mix = mixing.reshape(groups, 2 * heads, seq, seq)
         flops = 4 * tokens * width * cols
 
-        u_out, u_value = swap_halves([w_out, w_value], c)
-        act_s, mix_s, cot_s = (sibling(after(x, u_value)) for x in (act, mix, cot))
-        if line4:
-            v1 = gather_step((u_value, u_value), 0)
-            v2 = gather_step(v1, 1)
-            v2, act_s, mix_s, cot_s = lax.optimization_barrier((v2, act_s, mix_s, cot_s))
-            v3 = gather_last(v2, z)
-            u_out = after(u_out, *v2)
-            o1 = gather_step((u_out, u_out), 0)
-            value_slots, o1 = lax.optimization_barrier(([u_value, *v1, *v2, v3], o1))
-            o2 = gather_step(o1, 1)
-        else:
-            value_slots = gather_ring(u_value)
-            out_slots = gather_ring(u_out)
-
-        info = slot_planes(z)
-        sends = send_planes(z)
-        n_slots = len(value_slots)
-        idx_slots = jnp.stack([jnp.int32(x) for x in (c, *info)])
-        idx_send = jnp.stack([jnp.int32(x) for x in (c, *sends)])
-        idx_node = jnp.stack([lax.bitwise_xor(n, jnp.int32(j)) for j in range(n_node)])
+        got, (u_out, u_value) = swap_halves([w_out, w_value], c)
+        act_s, mix_s, cot_s = (
+            sibling(lax.optimization_barrier((x, got))[0]) for x in (act, mix, cot)
+        )
+
+        d = 1 - 2 * c
+        info = slot_planes(z, d)
+        sends = send_planes(z, d)
+        pack = lambda *values: jnp.stack([jnp.int32(x) for x in values])
+        idx_slots = pack(c, *info)
+        idx_send = pack(c, *sends)
+        idx_node = pack(*[lax.bitwise_xor(n, jnp.int32(j)) for j in range(n_node)])
 
         mix_scratch = pltpu.VMEM((2, groups, heads, seq, seq), BF16)
         both = pltpu.VMEM((2 * tokens, width), BF16)
         halves = pltpu.VMEM((2, tokens, width), BF16)
         left_tokens = pltpu.VMEM((cols, 2 * tokens), BF16)
         rows = pltpu.VMEM((width, cols), BF16)
-        send_shapes = [(2, depth // 2, cols)] * len(sends)
+        block = (2, depth // 2, cols)
+        send_shapes = [block] * len(sends)
+
+        ties, passed = [], []
+        if line4:
+            along = jnp.where(c == 0, z == 2, z == 1)
+            v1 = apart(u_value, u_value, line)
+            v2 = apart(*v1, line[1:])
+            forward = call(
+                select_kernel,
+                "forward",
+                [SMEM] + [VMEM] * 2 + [TIE] * 3,
+                [block],
+                [],
+                0,
+            )(pack(along), *v2, act_s, mix_s, cot_s)[0]
+            v3 = move(forward, [(2, 3), (1, 0)])
+            value_slots = [u_value, *v1, *v2, v3]
+            o1 = apart(u_out, u_out, line)
+            o2 = apart(*o1, line[1:])
+            ties = [*o1]
+            passed = [*o2]
+            idx_pass = pack(c, *sends, (1 - along) & (z % 3 != 0), along)
+        else:
+            value_slots = gather_ring(u_value)
+            out_slots = gather_ring(u_out)
+            idx_pass = idx_send
+        n_slots = len(value_slots)
 
         mixed_o, mixed_s = call(
-            functools.partial(mixed_kernel, n_slots),
+            functools.partial(mixed_kernel, n_slots, len(ties)),
             "mixed",
-            [SMEM] + [ANY] * 4 + [VMEM] * n_slots,
+            [SMEM] + [ANY] * 4 + [VMEM] * n_slots + [TIE] * len(ties),
             [(tokens, cols)] * 2,
             [rows, halves, mix_scratch, pltpu.SemaphoreType.DMA((4,))],
             flops,
-        )(idx_slots, act, act_s, mix, mix_s, *value_slots)
+        )(idx_slots, act, act_s, mix, mix_s, *value_slots, *ties)
         mixed_r = sibling(mixed_s)
-        if line4:
-            (mixed_o, mixed_s, mixed_r), o2 = lax.optimization_barrier(
-                ((mixed_o, mixed_s, mixed_r), o2)
-            )
-            out_slots = [u_out, *o1, *o2, gather_last(o2, z)]
         out_sends = call(
-            grad_out_kernel,
+            functools.partial(grad_out_kernel, len(passed), 1),
             "grad_out",
-            [SMEM] + [ANY] * 2 + [VMEM] * 2,
+            [SMEM] + [ANY] * 2 + [VMEM] * (2 + len(passed)) + [TIE],
             send_shapes,
             [both, left_tokens, rows, pltpu.SemaphoreType.DMA((2,))],
             flops,
-        )(idx_send, cot, cot_s, mixed_o, mixed_s)
+        )(idx_pass, cot, cot_s, mixed_o, mixed_s, *reversed(passed), mixed_r)
         if line4:
-            out_slots, out_sends = lax.optimization_barrier((out_slots, out_sends))
+            swapped = move(out_sends[4], [(0, 1), (1, 0), (2, 3), (3, 2)])
+            out_slots = [u_out, *o1, *o2, swapped]
+            far = scatter_far(out_sends, swapped, z)
+            out_second = scatter_second(far)
+            ties = [far]
+        else:
+            ties = [out_sends[0]]
         w_full, left = call(
-            functools.partial(d_value_kernel, n_slots),
+            functools.partial(d_value_kernel, n_slots, len(ties)),
             "d_value",
-            [SMEM] + [ANY] * 4 + [VMEM] * n_slots,
+            [SMEM] + [ANY] * 4 + [VMEM] * n_slots + [TIE] * len(ties),
             [(width, cols), (cols, 2 * tokens)],
             [halves, mix_scratch, pltpu.SemaphoreType.DMA((4,))],
             flops,
-        )(idx_slots, cot, cot_s, mix, mix_s, *out_slots)
+        )(idx_slots, cot, cot_s, mix, mix_s, *out_slots, *ties)
         w_full_s = sibling(w_full)
-        if line4:
-            out_first = scatter_first(out_sends)
-            left, out_first = lax.optimization_barrier((left, out_first))
-            out_second = scatter_second(out_sends, out_first)
-        back_sends = call(
-            gradient_kernel,
-            "grad_value",
-            [SMEM] + [ANY] * 2 + [VMEM],
-            send_shapes,
-            [both, rows, pltpu.SemaphoreType.DMA((2,))],
-            flops,
-        )(idx_send, act, act_s, left)
-        if line4:
-            back_first = scatter_first(back_sends)
-            out_sums = scatter_sums(out_sends, out_second)
-            w_full_s, out_sums = lax.optimization_barrier((w_full_s, out_sums))
-            out_third = scatter_third(out_sums)
-
         part = width // n_node
         half = tokens // 2
         if n_node == 4:
@@ -392,7 +401,7 @@
         else:
             term_shapes = [(tokens, part)] * n_node
         terms = call(
-            functools.partial(terms_kernel, n_node),
+            functools.partial(terms_kernel, n_node, 0),
             "terms",
             [SMEM] + [VMEM] * 4,
             term_shapes,
@@ -400,9 +409,22 @@
             flops,
         )(idx_node, mixed_o, mixed_r, w_full, w_full_s)
 
+        ties = [terms[0]]
         if line4:
-            back_first = after(back_first, terms[0])
-            back_second = scatter_second(back_sends, back_first)
+            out_sums = scatter_sums(out_sends, out_second)
+            out_third = scatter_third(out_sums)
+            ties += out_sums
+        back_sends = call(
+            functools.partial(gradient_kernel, len(ties)),
+            "grad_value",
+            [SMEM] + [ANY] * 2 + [VMEM] + [TIE] * len(ties),
+            send_shapes,
+            [both, rows, pltpu.SemaphoreType.DMA((2,))],
+            flops,
+        )(idx_send, act, act_s, left, *ties)
+        if line4:
+            back_first = move(back_sends[4], [(0, 1), (3, 2)])
+            back_second = scatter_second(scatter_far(back_sends, back_first, z))
             back_third = scatter_third(scatter_sums(back_sends, back_second))
             grad_out = scatter_end(out_sends, out_third, c)
             grad_value = scatter_end(back_sends, back_third, c)

time: 151 us -> 161 us (1.066)
  waiting for transfers between devices: 44.8 us -> 52.8 us
  starting transfers between devices: 59.4 us -> 52.4 us
  Pallas kernels: 23.6 us -> 30.2 us
  other arithmetic: 6.97 us -> 9.9 us
    ppermute x20 -> x3, starting transfers between devices: 52.4 us -> 5.76 us  [move(): lax.ppermute(x, 'wide', [(2 * s + c, 2 * d + c) for s, d in pairs for c i...]
    ppermute x0 -> x16, starting transfers between devices: none -> 39.8 us  [apart(): lax.ppermute(x, 'wide', [(2 * s + c, 2 * d + c) for c in range(2) for s,...]
    ppermute x0 -> x16, waiting for transfers between devices: none -> 19.3 us  [apart(): lax.ppermute(x, 'wide', [(2 * s + c, 2 * d + c) for c in range(2) for s,...]
    ppermute x20 -> x3, waiting for transfers between devices: 32.8 us -> 19.4 us  [move(): lax.ppermute(x, 'wide', [(2 * s + c, 2 * d + c) for s, d in pairs for c i...]
    pallas_call x5 -> x6, Pallas kernels: 23.6 us -> 30.2 us  [the longest x1 7.59 us: body(): call(functools.partial(d_value_kernel, n_slots, len(ties)), 'd_value', [S...]
    convert_element_type x6, other arithmetic: 0.51 us -> 4.18 us  [added(): return (block.astype(F32) + got.astype(F32)).astype(BF16)]
    ppermute x4, waiting for transfers between devices: 9.2 us -> 11 us  [flip(): return lax.ppermute(x, 'node', [(i, i ^ j) for i in range(n_node)])]
    another operation x2 -> x4, other arithmetic: 0.32 us -> 2.04 us  [the longest x2 1.71 us: swap_halves(): return (got, [jnp.stack([mine[i], got[i]]) for i in range(len(weights))])]
  transfers between devices with their start and end apart: 32 -> 31, of which waited for: 15 -> 15; matrix products, arithmetic and copies ran while one was open for 3% -> 4% of each run, Pallas kernels for 16% -> 5%
where the time goes in v6:
time: 161 us; the launch traced here: 160 us
  waiting for transfers between devices  52.8 us (33%)
  starting transfers between devices  52.4 us (33%)
  Pallas kernels  30.2 us (19%)
  local copies, waits for them, and re-layouts  13.8 us (9%)
  other arithmetic  9.9 us (6%)
    ppermute x16, starting transfers between devices, apart(): lax.ppermute(x, 'wide', [(2 * s + c, 2 * d + c) for c in range(2) for s,...  39.8 us
    ppermute x3, waiting for transfers between devices, move(): lax.ppermute(x, 'wide', [(2 * s + c, 2 * d + c) for s, d in pairs for c i...  19.4 us
    ppermute x16, waiting for transfers between devices, apart(): lax.ppermute(x, 'wide', [(2 * s + c, 2 * d + c) for c in range(2) for s,...  19.3 us
    ppermute x4, waiting for transfers between devices, flip(): return lax.ppermute(x, 'node', [(i, i ^ j) for i in range(n_node)])  11 us
    unnamed x30, local copies, waits for them, and re-layouts  10.7 us
    pallas_call x1, Pallas kernels, body(): call(functools.partial(d_value_kernel, n_slots, len(ties)), 'd_value', [S...  7.59 us
    pallas_call x1, Pallas kernels, body(): call(functools.partial(mixed_kernel, n_slots, len(ties)), 'mixed', [SMEM]...  7.46 us
    pallas_call x1, Pallas kernels, body(): call(functools.partial(grad_out_kernel, len(passed), 1), 'grad_out', [SME...  6.44 us
  transfers between devices with their start and end apart: 31, of which 15 were waited for; matrix products, arithmetic and copies ran while one was open for 4% of the time, Pallas kernels for 5%

profile of v6, /device:TPU:0, one launch (start us, length us, event | category | flops | bytes accessed | tf_op | source)
XLA Modules:
  0.0 160.3 jit_solution(7934951218441987564)
XLA Ops:
  0.6 1.0 slice_bitcast_fusion.6
  1.7 1.0 slice_bitcast_fusion.7
  3.3 1.3 collective-permute-done
  5.4 0.7 fusion.15
  6.2 1.3 collective-permute-start.4
  7.5 6.0 %collective-permute-start.3 = (bf16[2,320,256]{2,1,0:T(8,128)(2,1)S(1)}, bf16[2,320,256]{2,1,0:T(8,128)(2,1)}, u32[]{:S(2)}, u32[]{:S(2)}) collective-permute-start(bf16[2,320,256]{2,1,0:T(8,128)(2,1)S(1)} %pad_maximum_fusion.5.rest_0_), channel_id=1, source_target_pairs={{0,8},{8,16},{16,24},{28,20},{20,12},{12,4},{1,9},{9,17},{17,25},{... | collective-permute-start | bytes 983048 | tf_op jit(solution)/shard_map/ppermute | solution.py:230
  13.4 0.7 copy-done.6
  14.2 1.8 %collective-permute-done.4.rest_2_ = bf16[2,320,256]{2,1,0:T(8,128)(2,1)} collective-permute-done((bf16[2,320,256]{2,1,0:T(8,128)(2,1)S(1)}, bf16[2,320,256]{2,1,0:T(8,128)(2,1)}, u32[]{:S(2)}, u32[]{:S(2)}) %collective-permute-start.4) | collective-permute-done | bytes 327712 | tf_op jit(solution)/shard_map/ppermute | solution.py:230
  15.9 1.3 collective-permute-start.6
  17.2 1.1 collective-permute-done.3.rest_1_
  19.0 1.7 %pad_maximum_fusion.6.rest_0_ = bf16[2,320,256]{2,1,0:T(8,128)(2,1)} fusion(bf16[1,320,256]{2,1,0:T(8,128)(2,1)} %get-tuple-element.55, bf16[1,320,256]{2,1,0:T(8,128)(2,1)S(1)} %get-tuple-element.53), kind=kLoop, calls=%fused_computation.32 | loop fusion | flops 163840 | bytes 655360 | tf_op jit(solution)/shard_map/stack | solution.py:246
  20.7 6.9 %collective-permute-done.6.second.rest_4_ = bf16[2,320,256]{2,1,0:T(8,128)(2,1)S(1)} collective-permute-done((bf16[2,320,256]{2,1,0:T(8,128)(2,1)}, bf16[2,320,256]{2,1,0:T(8,128)(2,1)S(1)}, u32[]{:S(2)}, u32[]{:S(2)}) %collective-permute-start.6) | collective-permute-done | bytes 327712 | tf_op jit(solution)/shard_map/ppermute | solution.py:230
  27.6 0.7 copy-done
  28.3 1.3 collective-permute-start.10
  29.6 0.7 copy-done.3
  30.3 4.8 %collective-permute-start.9 = (bf16[2,320,256]{2,1,0:T(8,128)(2,1)}, bf16[2,320,256]{2,1,0:T(8,128)(2,1)S(1)}, u32[]{:S(2)}, u32[]{:S(2)}) collective-permute-start(bf16[2,320,256]{2,1,0:T(8,128)(2,1)} %pad_maximum_fusion.6.rest_0_), channel_id=1, source_target_pairs={{0,8},{8,16},{16,24},{28,20},{20,12},{12,4},{1,9},{9,17},{17,25},{... | collective-permute-start | bytes 983048 | tf_op jit(solution)/shard_map/ppermute | solution.py:230
  35.2 1.0 copy-done.1
  36.1 1.0 copy-done.4
  37.1 0.8 forward.1
  37.9 1.3 collective-permute-start.8
  39.3 1.2 collective-permute-done.10.rest_7_.rest_2_
  40.5 1.3 collective-permute-start.13
  41.8 1.4 collective-permute-start.12
  43.2 7.4 %collective-permute-done.8.rest_5_ = bf16[2,320,256]{2,1,0:T(8,128)(2,1)} collective-permute-done((bf16[2,320,256]{2,1,0:T(8,128)(2,1)}, bf16[2,320,256]{2,1,0:T(8,128)(2,1)}, u32[]{:S(2)}, u32[]{:S(2)}) %collective-permute-start.8) | collective-permute-done | bytes 327712 | tf_op jit(solution)/shard_map/ppermute | solution.py:222
  50.6 1.0 copy-done.2
  51.6 1.0 copy-done.5
  52.6 1.0 copy-done.7
  53.5 7.5 %mixed.1 = (bf16[512,256]{1,0:T(8,128)(2,1)S(1)}, bf16[512,256]{1,0:T(8,128)(2,1)}) custom-call(s32[13]{0:T(128)S(1)} %stack.142.idx, bf16[512,2560]{1,0:T(8,128)(2,1)} %bitcast.16.act_o.right_o, bf16[512,2560]{1,0:T(8,128)(2,1)S(1)} %collective-permute-done.1.rest_0_.act_s.right_s, bf16[4,8,128,128]{3,2,1,0:T(8,128)(2,1)} %bitcast.21.mix_o, ...), custom_call_target="tpu_custom_call" | custom-call | flops 1342177280 | bytes 12582912 | tf_op jit(solution)/shard_map/mixed/pallas_call | solution.py:363
  61.2 1.7 %collective-permute-done.11.rest_2_.mixed_r = bf16[512,256]{1,0:T(8,128)(2,1)} collective-permute-done((bf16[512,256]{1,0:T(8,128)(2,1)}, bf16[512,256]{1,0:T(8,128)(2,1)}, u32[]{:S(2)}, u32[]{:S(2)}) %collective-permute-start.11) | collective-permute-done | bytes 262176 | tf_op jit(solution)/shard_map/ppermute | solution.py:235
  63.0 6.4 %grad_out.1 = (bf16[2,320,256]{2,1,0:T(8,128)(2,1)S(1)}, bf16[2,320,256]{2,1,0:T(8,128)(2,1)S(1)}, bf16[2,320,256]{2,1,0:T(8,128)(2,1)S(1)}, bf16[2,320,256]{2,1,0:T(8,128)(2,1)S(1)}, bf16[2,320,256]{2,1,0:T(8,128)(2,1)}) custom-call(s32[8]{0:T(128)S(1)} %stack.154.idx, bf16[512,2560]{1,0:T(8,128)(2,1)} %bitcast.23.cot_o, ...), custom_call_target="tpu_custom_call" | custom-call | flops 1342177280 | bytes 12582912 | tf_op jit(solution)/shard_map/grad_out/pallas_call | solution.py:372
  69.4 0.7 copy-done.10
  70.1 0.7 copy-done.11
  70.9 0.7 copy-done.13
  71.6 0.7 copy-done.14
  72.3 10.1 %collective-permute-done.14.rest_5_ = bf16[2,320,256]{2,1,0:T(8,128)(2,1)} collective-permute-done((bf16[2,320,256]{2,1,0:T(8,128)(2,1)}, bf16[2,320,256]{2,1,0:T(8,128)(2,1)}, u32[]{:S(2)}, u32[]{:S(2)}) %collective-permute-start.14) | collective-permute-done | bytes 327712 | tf_op jit(solution)/shard_map/ppermute | solution.py:222
  82.4 1.8 %add_convert_fusion.5.rest_6_ = bf16[2,320,256]{2,1,0:T(8,128)(2,1)} fusion(bf16[2,320,256]{2,1,0:T(8,128)(2,1)} %copy-done.10, bf16[2,320,256]{2,1,0:T(8,128)(2,1)} %collective-permute-done.14.rest_5_, pred[]{:T(512)S(6)} %or.8), kind=kLoop, calls=%fused_computation.22 | loop fusion | flops 819200 | bytes 983041 | tf_op jit(solution)/shard_map/convert_element_type | solution.py:270
  84.2 7.6 %d_value.1 = (bf16[2560,256]{1,0:T(8,128)(2,1)}, bf16[256,1024]{1,0:T(8,128)(2,1)S(1)}) custom-call(s32[13]{0:T(128)S(1)} %stack.142.idx, bf16[512,2560]{1,0:T(8,128)(2,1)} %bitcast.23.cot_o, bf16[512,2560]{1,0:T(8,128)(2,1)} %collective-permute-done.7.rest_2_.cot_s, bf16[4,8,128,128]{3,2,1,0:T(8,128)(2,1)} %bitcast.21.mix_o, ...), custom_call_target="tpu_custom_call" | custom-call | flops 1342177280 | bytes 12582912 | tf_op jit(solution)/shard_map/d_value/pallas_call | solution.py:388
  91.8 0.8 copy-done.8
  92.6 0.7 collective-permute-start.21
  93.4 2.9 %collective-permute-start.20 = (bf16[2,320,256]{2,1,0:T(8,128)(2,1)}, bf16[2,320,256]{2,1,0:T(8,128)(2,1)S(1)}, u32[]{:S(2)}, u32[]{:S(2)}) collective-permute-start(bf16[2,320,256]{2,1,0:T(8,128)(2,1)} %add_convert_fusion.5.rest_6_), channel_id=1, source_target_pairs={{0,8},{8,16},{28,20},{20,12},{1,9},{9,17},{29,21},{21,13},{2,10},{... | collective-permute-start | bytes 983048 | tf_op jit(solution)/shard_map/ppermute | solution.py:230
  96.4 1.1 add_convert_fusion.3.rest_2_
  97.4 5.4 %collective-permute-done.20 = bf16[2,320,256]{2,1,0:T(8,128)(2,1)S(1)} collective-permute-done((bf16[2,320,256]{2,1,0:T(8,128)(2,1)}, bf16[2,320,256]{2,1,0:T(8,128)(2,1)S(1)}, u32[]{:S(2)}, u32[]{:S(2)}) %collective-permute-start.20) | collective-permute-done | bytes 327712 | tf_op jit(solution)/shard_map/ppermute | solution.py:230
  102.8 1.1 add_convert_fusion.4.rest_1_
  103.9 3.7 %terms.1 = (bf16[2,256,640]{2,1,0:T(8,128)(2,1)S(1)}, bf16[2,256,640]{2,1,0:T(8,128)(2,1)S(1)}, bf16[4,256,640]{2,1,0:T(8,128)(2,1)S(1)}) custom-call(s32[4]{0:T(128)S(1)} %pad_add_fusion.idx, bf16[512,256]{1,0:T(8,128)(2,1)S(1)} %get-tuple-element.26.mixed_o, bf16[512,256]{1,0:T(8,128)(2,1)} %collective-permute-done.11.rest_2_.mixed_r, ...), custom_call_target="tpu_custom_call" | custom-call | flops 1342177280 | bytes 12582912 | tf_op jit(solution)/shard_map/terms/pallas_call | solution.py:403
  107.6 4.3 %grad_value.1 = (bf16[2,320,256]{2,1,0:T(8,128)(2,1)S(1)}, bf16[2,320,256]{2,1,0:T(8,128)(2,1)S(1)}, bf16[2,320,256]{2,1,0:T(8,128)(2,1)S(1)}, bf16[2,320,256]{2,1,0:T(8,128)(2,1)S(1)}, bf16[2,320,256]{2,1,0:T(8,128)(2,1)S(1)}) custom-call(s32[6]{0:T(128)S(1)} %stack.155.idx, bf16[512,2560]{1,0:T(8,128)(2,1)} %bitcast.16.act_o.right_o, ...), custom_call_target="tpu_custom_call" | custom-call | flops 1342177280 | bytes 12582912 | tf_op jit(solution)/shard_map/grad_value/pallas_call | solution.py:417
  111.9 4.5 %collective-permute-start.22 = (bf16[2,320,256]{2,1,0:T(8,128)(2,1)S(1)}, bf16[2,320,256]{2,1,0:T(8,128)(2,1)S(1)}, u32[]{:S(2)}, u32[]{:S(2)}) collective-permute-start(bf16[2,320,256]{2,1,0:T(8,128)(2,1)S(1)} %get-tuple-element.40), channel_id=1, source_target_pairs={{0,8},{4,12},{24,16},{28,20},{1,9},{5,13},{25,17},{29,21},{2,10},{... | collective-permute-start | bytes 983048 | tf_op jit(solution)/shard_map/ppermute | solution.py:222
  116.4 1.3 collective-permute-start.29
  117.7 4.6 %collective-permute-start.28 = (bf16[2,320,256]{2,1,0:T(8,128)(2,1)S(1)}, bf16[2,320,256]{2,1,0:T(8,128)(2,1)S(1)}, u32[]{:S(2)}, u32[]{:S(2)}) collective-permute-start(bf16[2,320,256]{2,1,0:T(8,128)(2,1)S(1)} %add_convert_fusion.4.rest_1_), channel_id=1, source_target_pairs={{0,8},{8,16},{16,24},{28,20},{20,12},{12,4},{1,9},{9,17},{17,25},{... | collective-permute-start | bytes 983048 | tf_op jit(solution)/shard_map/ppermute | solution.py:230
  122.3 2.0 %collective-permute-done.22 = bf16[2,320,256]{2,1,0:T(8,128)(2,1)S(1)} collective-permute-done((bf16[2,320,256]{2,1,0:T(8,128)(2,1)S(1)}, bf16[2,320,256]{2,1,0:T(8,128)(2,1)S(1)}, u32[]{:S(2)}, u32[]{:S(2)}) %collective-permute-start.22) | collective-permute-done | bytes 327712 | tf_op jit(solution)/shard_map/ppermute | solution.py:222
  124.3 0.7 collective-permute-start.25
  125.0 5.0 %collective-permute-start.23 = (bf16[2,320,256]{2,1,0:T(8,128)(2,1)S(1)}, bf16[2,320,256]{2,1,0:T(8,128)(2,1)S(1)}, u32[]{:S(2)}, u32[]{:S(2)}) collective-permute-start(bf16[2,320,256]{2,1,0:T(8,128)(2,1)S(1)} %add_convert_fusion.2), channel_id=1, source_target_pairs={{0,8},{8,16},{28,20},{20,12},{1,9},{9,17},{29,21},{21,13},{2,10},{... | collective-permute-start | bytes 983048 | tf_op jit(solution)/shard_map/ppermute | solution.py:230
  130.1 1.2 collective-permute-done.28
  131.4 1.6 collective-permute-start.16
  132.9 1.5 collective-permute-start.18
  134.5 1.3 collective-permute-start.26
  135.8 1.8 %collective-permute-done.23 = bf16[2,320,256]{2,1,0:T(8,128)(2,1)S(1)} collective-permute-done((bf16[2,320,256]{2,1,0:T(8,128)(2,1)S(1)}, bf16[2,320,256]{2,1,0:T(8,128)(2,1)S(1)}, u32[]{:S(2)}, u32[]{:S(2)}) %collective-permute-start.23) | collective-permute-done | bytes 327712 | tf_op jit(solution)/shard_map/ppermute | solution.py:230
  137.7 5.4 %collective-permute-start.24 = (bf16[2,320,256]{2,1,0:T(8,128)(2,1)S(1)}, bf16[2,320,256]{2,1,0:T(8,128)(2,1)S(1)}, u32[]{:S(2)}, u32[]{:S(2)}) collective-permute-start(bf16[2,320,256]{2,1,0:T(8,128)(2,1)S(1)} %add_convert_fusion.1), channel_id=1, source_target_pairs={{0,8},{8,16},{16,24},{28,20},{20,12},{12,4},{1,9},{9,17},{17,25},{... | collective-permute-start | bytes 983048 | tf_op jit(solution)/shard_map/ppermute | solution.py:230
  143.4 4.7 %collective-permute-done.18 = bf16[2,256,640]{2,1,0:T(8,128)(2,1)S(1)} collective-permute-done((bf16[2,256,640]{2,1,0:T(8,128)(2,1)S(1)}, bf16[2,256,640]{2,1,0:T(8,128)(2,1)S(1)}, u32[]{:S(2)}, u32[]{:S(2)}) %collective-permute-start.18) | collective-permute-done | bytes 655392 | tf_op jit(solution)/shard_map/ppermute | solution.py:238
  148.5 1.6 collective-permute-start.17
  150.9 5.0 %collective-permute-done.17 = bf16[256,640]{1,0:T(8,128)(2,1)S(1)} collective-permute-done((bf16[256,640]{1,0:T(8,128)(2,1)S(1)}, bf16[256,640]{1,0:T(8,128)(2,1)S(1)}, u32[]{:S(2)}, u32[]{:S(2)}) %collective-permute-start.17) | collective-permute-done | bytes 327712 | tf_op jit(solution)/shard_map/ppermute | solution.py:238
  155.8 1.3 collective-permute-done.19
  157.4 0.9 pad_maximum_fusion
  158.4 0.9 pad_maximum_fusion.1
  159.4 0.9 pad_maximum_fusion.2
  (64 shorter events, 4.8 us)
Async XLA Ops:
  2.8 1.8 %collective-permute-start = (bf16[2,320,256]{2,1,0:T(8,128)(2,1)S(1)}, bf16[2,320,256]{2,1,0:T(8,128)(2,1)S(1)}, u32[]{:S(2)}, u32[]{:S(2)}) collective-permute-start(bf16[2,320,256]{2,1,0:T(8,128)(2,1)S(1)} %get-tuple-element.52), channel_id=1, source_target_pairs={{0,4},{4,0},{8,12},{12,8},{16,20},{20,16},{24,28},{28,24},{1,5},{5... | collective-permute-start | bytes 983048 | tf_op jit(solution)/shard_map/ppermute | solution.py:235
  4.5 30.6 %collective-permute-start.1 = (bf16[512,2560]{1,0:T(8,128)(2,1)}, bf16[512,2560]{1,0:T(8,128)(2,1)S(1)}, u32[]{:S(2)}, u32[]{:S(2)}) collective-permute-start(bf16[512,2560]{1,0:T(8,128)(2,1)} %bitcast.16.act_o.right_o), channel_id=1, source_target_pairs={{0,4},{4,0},{8,12},{12,8},{16,20},{20,16},{24,28},{28,24},{1,5},{5... | collective-permute-start | bytes 7864328 | tf_op jit(solution)/shard_map/ppermute | solution.py:235
  4.9 30.3 %collective-permute-start.7 = (bf16[512,2560]{1,0:T(8,128)(2,1)}, bf16[512,2560]{1,0:T(8,128)(2,1)}, u32[]{:S(2)}, u32[]{:S(2)}) collective-permute-start(bf16[512,2560]{1,0:T(8,128)(2,1)} %bitcast.23.cot_o), channel_id=1, source_target_pairs={{0,4},{4,0},{8,12},{12,8},{16,20},{20,16},{24,28},{28,24},{1,5},{5... | collective-permute-start | bytes 7864328 | tf_op jit(solution)/shard_map/ppermute | solution.py:235
  5.0 30.1 %collective-permute-start.2 = (bf16[4,8,128,128]{3,2,1,0:T(8,128)(2,1)}, bf16[4,8,128,128]{3,2,1,0:T(8,128)(2,1)}, u32[]{:S(2)}, u32[]{:S(2)}) collective-permute-start(bf16[4,8,128,128]{3,2,1,0:T(8,128)(2,1)} %bitcast.21.mix_o), channel_id=1, source_target_pairs={{0,4},{4,0},{8,12},{12,8},{16,20},{20,16},{24,28},{28,24},{1,5},{5... | collective-permute-start | bytes 3145736 | tf_op jit(solution)/shard_map/ppermute | solution.py:235
  6.2 9.8 %collective-permute-start.4 = (bf16[2,320,256]{2,1,0:T(8,128)(2,1)S(1)}, bf16[2,320,256]{2,1,0:T(8,128)(2,1)}, u32[]{:S(2)}, u32[]{:S(2)}) collective-permute-start(bf16[2,320,256]{2,1,0:T(8,128)(2,1)S(1)} %pad_maximum_fusion.5.rest_0_), channel_id=1, source_target_pairs={{24,16},{16,8},{8,0},{4,12},{12,20},{20,28},{25,17},{17,9},{9,1},{... | collective-permute-start | bytes 983048 | tf_op jit(solution)/shard_map/ppermute | solution.py:230
  7.5 10.8 %collective-permute-start.3 = (bf16[2,320,256]{2,1,0:T(8,128)(2,1)S(1)}, bf16[2,320,256]{2,1,0:T(8,128)(2,1)}, u32[]{:S(2)}, u32[]{:S(2)}) collective-permute-start(bf16[2,320,256]{2,1,0:T(8,128)(2,1)S(1)} %pad_maximum_fusion.5.rest_0_), channel_id=1, source_target_pairs={{0,8},{8,16},{16,24},{28,20},{20,12},{12,4},{1,9},{9,17},{17,25},{... | collective-permute-start | bytes 983048 | tf_op jit(solution)/shard_map/ppermute | solution.py:230
  13.4 0.7 copy-start.6
  15.9 11.6 %collective-permute-start.6 = (bf16[2,320,256]{2,1,0:T(8,128)(2,1)}, bf16[2,320,256]{2,1,0:T(8,128)(2,1)S(1)}, u32[]{:S(2)}, u32[]{:S(2)}) collective-permute-start(bf16[2,320,256]{2,1,0:T(8,128)(2,1)} %collective-permute-done.4.rest_2_), channel_id=1, source_target_pairs={{16,8},{8,0},{12,20},{20,28},{17,9},{9,1},{13,21},{21,29},{18,10},... | collective-permute-start | bytes 983048 | tf_op jit(solution)/shard_map/ppermute | solution.py:230
  18.3 11.3 %collective-permute-start.5 = (bf16[2,320,256]{2,1,0:T(8,128)(2,1)}, bf16[2,320,256]{2,1,0:T(8,128)(2,1)S(1)}, u32[]{:S(2)}, u32[]{:S(2)}) collective-permute-start(bf16[2,320,256]{2,1,0:T(8,128)(2,1)} %collective-permute-done.3.rest_1_), channel_id=1, source_target_pairs={{8,16},{16,24},{20,12},{12,4},{9,17},{17,25},{21,13},{13,5},{10,18... | collective-permute-start | bytes 983048 | tf_op jit(solution)/shard_map/ppermute | solution.py:230
  27.5 0.7 copy-start
  28.3 12.3 %collective-permute-start.10 = (bf16[2,320,256]{2,1,0:T(8,128)(2,1)}, bf16[2,320,256]{2,1,0:T(8,128)(2,1)S(1)}, u32[]{:S(2)}, u32[]{:S(2)}) collective-permute-start(bf16[2,320,256]{2,1,0:T(8,128)(2,1)} %pad_maximum_fusion.6.rest_0_), channel_id=1, source_target_pairs={{24,16},{16,8},{8,0},{4,12},{12,20},{20,28},{25,17},{17,9},{9,1},{... | collective-permute-start | bytes 983048 | tf_op jit(solution)/shard_map/ppermute | solution.py:230
  29.6 0.7 copy-start.3
  30.3 11.5 %collective-permute-start.9 = (bf16[2,320,256]{2,1,0:T(8,128)(2,1)}, bf16[2,320,256]{2,1,0:T(8,128)(2,1)S(1)}, u32[]{:S(2)}, u32[]{:S(2)}) collective-permute-start(bf16[2,320,256]{2,1,0:T(8,128)(2,1)} %pad_maximum_fusion.6.rest_0_), channel_id=1, source_target_pairs={{0,8},{8,16},{16,24},{28,20},{20,12},{12,4},{1,9},{9,17},{17,25},{... | collective-permute-start | bytes 983048 | tf_op jit(solution)/shard_map/ppermute | solution.py:230
  35.2 1.0 copy-start.1
  36.1 1.0 copy-start.4
  37.9 12.7 %collective-permute-start.8 = (bf16[2,320,256]{2,1,0:T(8,128)(2,1)}, bf16[2,320,256]{2,1,0:T(8,128)(2,1)}, u32[]{:S(2)}, u32[]{:S(2)}) collective-permute-start(bf16[2,320,256]{2,1,0:T(8,128)(2,1)} %forward.1), channel_id=1, source_target_pairs={{16,24},{20,28},{8,0},{12,4},{17,25},{21,29},{9,1},{13,5},{18,26},... | collective-permute-start | bytes 983048 | tf_op jit(solution)/shard_map/ppermute | solution.py:222
  40.5 20.7 %collective-permute-start.13 = (bf16[2,320,256]{2,1,0:T(8,128)(2,1)S(1)}, bf16[2,320,256]{2,1,0:T(8,128)(2,1)}, u32[]{:S(2)}, u32[]{:S(2)}) collective-permute-start(bf16[2,320,256]{2,1,0:T(8,128)(2,1)S(1)} %collective-permute-done.10.rest_7_.rest_2_), channel_id=1, source_target_pairs={{16,8},{8,0},{12,20},{20,28},{17,9},{9,1},{13,21},{21,29},{18,10},... | collective-permute-start | bytes 983048 | tf_op jit(solution)/shard_map/ppermute | solution.py:230
  41.8 19.4 %collective-permute-start.12 = (bf16[2,320,256]{2,1,0:T(8,128)(2,1)S(1)}, bf16[2,320,256]{2,1,0:T(8,128)(2,1)}, u32[]{:S(2)}, u32[]{:S(2)}) collective-permute-start(bf16[2,320,256]{2,1,0:T(8,128)(2,1)S(1)} %collective-permute-done.9.rest_6_.rest_1_), channel_id=1, source_target_pairs={{8,16},{16,24},{20,12},{12,4},{9,17},{17,25},{21,13},{13,5},{10,18... | collective-permute-start | bytes 983048 | tf_op jit(solution)/shard_map/ppermute | solution.py:230
  50.6 1.0 copy-start.2
  51.6 1.0 copy-start.5
  52.6 1.0 copy-start.7
  61.0 1.9 %collective-permute-start.11 = (bf16[512,256]{1,0:T(8,128)(2,1)}, bf16[512,256]{1,0:T(8,128)(2,1)}, u32[]{:S(2)}, u32[]{:S(2)}) collective-permute-start(bf16[512,256]{1,0:T(8,128)(2,1)} %get-tuple-element.27.mixed_s), channel_id=1, source_target_pairs={{0,4},{4,0},{8,12},{12,8},{16,20},{20,16},{24,28},{28,24},{1,5},{5... | collective-permute-start | bytes 786440 | tf_op jit(solution)/shard_map/ppermute | solution.py:235
  69.4 0.7 copy-start.10
  70.1 0.7 copy-start.11
  70.9 0.7 copy-start.13
  71.6 0.7 copy-start.14
  72.3 10.1 %collective-permute-start.14 = (bf16[2,320,256]{2,1,0:T(8,128)(2,1)}, bf16[2,320,256]{2,1,0:T(8,128)(2,1)}, u32[]{:S(2)}, u32[]{:S(2)}) collective-permute-start(bf16[2,320,256]{2,1,0:T(8,128)(2,1)} %get-tuple-element.28), channel_id=1, source_target_pairs={{0,8},{4,12},{8,0},{12,4},{16,24},{20,28},{24,16},{28,20},{1,9},{5... | collective-permute-start | bytes 983048 | tf_op jit(solution)/shard_map/ppermute | solution.py:222
  91.8 0.8 copy-start.8
  92.6 11.3 %collective-permute-start.15 = (bf16[2560,256]{1,0:T(8,128)(2,1)}, bf16[2560,256]{1,0:T(8,128)(2,1)}, u32[]{:S(2)}, u32[]{:S(2)}) collective-permute-start(bf16[2560,256]{1,0:T(8,128)(2,1)} %get-tuple-element.30.w_o), channel_id=1, source_target_pairs={{0,4},{4,0},{8,12},{12,8},{16,20},{20,16},{24,28},{28,24},{1,5},{5... | collective-permute-start | bytes 3932168 | tf_op jit(solution)/shard_map/ppermute | solution.py:235
  92.6 3.8 %collective-permute-start.21 = (bf16[2,320,256]{2,1,0:T(8,128)(2,1)}, bf16[2,320,256]{2,1,0:T(8,128)(2,1)S(1)}, u32[]{:S(2)}, u32[]{:S(2)}) collective-permute-start(bf16[2,320,256]{2,1,0:T(8,128)(2,1)} %add_convert_fusion.5.rest_6_), channel_id=1, source_target_pairs={{24,16},{16,8},{4,12},{12,20},{25,17},{17,9},{5,13},{13,21},{26,18... | collective-permute-start | bytes 983048 | tf_op jit(solution)/shard_map/ppermute | solution.py:230
  93.4 9.4 %collective-permute-start.20 = (bf16[2,320,256]{2,1,0:T(8,128)(2,1)}, bf16[2,320,256]{2,1,0:T(8,128)(2,1)S(1)}, u32[]{:S(2)}, u32[]{:S(2)}) collective-permute-start(bf16[2,320,256]{2,1,0:T(8,128)(2,1)} %add_convert_fusion.5.rest_6_), channel_id=1, source_target_pairs={{0,8},{8,16},{28,20},{20,12},{1,9},{9,17},{29,21},{21,13},{2,10},{... | collective-permute-start | bytes 983048 | tf_op jit(solution)/shard_map/ppermute | solution.py:230
  103.9 3.7 %copy-start.9 = (bf16[256,1024]{1,0:T(8,128)(2,1)S(1)}, bf16[256,1024]{1,0:T(8,128)(2,1)}, u32[]{:S(2)}) copy-start(bf16[256,1024]{1,0:T(8,128)(2,1)} %copy-done.8) | copy-start | bytes 1572868
  107.6 23.7 %copy-start.12 = (bf16[2,320,256]{2,1,0:T(8,128)(2,1)S(1)}, bf16[2,320,256]{2,1,0:T(8,128)(2,1)}, u32[]{:S(2)}) copy-start(bf16[2,320,256]{2,1,0:T(8,128)(2,1)} %copy-done.11) | copy-start | bytes 983044
  111.9 12.3 %collective-permute-start.22 = (bf16[2,320,256]{2,1,0:T(8,128)(2,1)S(1)}, bf16[2,320,256]{2,1,0:T(8,128)(2,1)S(1)}, u32[]{:S(2)}, u32[]{:S(2)}) collective-permute-start(bf16[2,320,256]{2,1,0:T(8,128)(2,1)S(1)} %get-tuple-element.40), channel_id=1, source_target_pairs={{0,8},{4,12},{24,16},{28,20},{1,9},{5,13},{25,17},{29,21},{2,10},{... | collective-permute-start | bytes 983048 | tf_op jit(solution)/shard_map/ppermute | solution.py:222
  116.4 13.7 %collective-permute-start.29 = (bf16[2,320,256]{2,1,0:T(8,128)(2,1)S(1)}, bf16[2,320,256]{2,1,0:T(8,128)(2,1)S(1)}, u32[]{:S(2)}, u32[]{:S(2)}) collective-permute-start(bf16[2,320,256]{2,1,0:T(8,128)(2,1)S(1)} %add_convert_fusion.3.rest_2_), channel_id=1, source_target_pairs={{24,16},{16,8},{8,0},{4,12},{12,20},{20,28},{25,17},{17,9},{9,1},{... | collective-permute-start | bytes 983048 | tf_op jit(solution)/shard_map/ppermute | solution.py:230
  117.7 13.6 %collective-permute-start.28 = (bf16[2,320,256]{2,1,0:T(8,128)(2,1)S(1)}, bf16[2,320,256]{2,1,0:T(8,128)(2,1)S(1)}, u32[]{:S(2)}, u32[]{:S(2)}) collective-permute-start(bf16[2,320,256]{2,1,0:T(8,128)(2,1)S(1)} %add_convert_fusion.4.rest_1_), channel_id=1, source_target_pairs={{0,8},{8,16},{16,24},{28,20},{20,12},{12,4},{1,9},{9,17},{17,25},{... | collective-permute-start | bytes 983048 | tf_op jit(solution)/shard_map/ppermute | solution.py:230
  124.3 10.1 %collective-permute-start.25 = (bf16[2,320,256]{2,1,0:T(8,128)(2,1)S(1)}, bf16[2,320,256]{2,1,0:T(8,128)(2,1)S(1)}, u32[]{:S(2)}, u32[]{:S(2)}) collective-permute-start(bf16[2,320,256]{2,1,0:T(8,128)(2,1)S(1)} %add_convert_fusion.2), channel_id=1, source_target_pairs={{24,16},{16,8},{4,12},{12,20},{25,17},{17,9},{5,13},{13,21},{26,18... | collective-permute-start | bytes 983048 | tf_op jit(solution)/shard_map/ppermute | solution.py:230
  125.0 12.6 %collective-permute-start.23 = (bf16[2,320,256]{2,1,0:T(8,128)(2,1)S(1)}, bf16[2,320,256]{2,1,0:T(8,128)(2,1)S(1)}, u32[]{:S(2)}, u32[]{:S(2)}) collective-permute-start(bf16[2,320,256]{2,1,0:T(8,128)(2,1)S(1)} %add_convert_fusion.2), channel_id=1, source_target_pairs={{0,8},{8,16},{28,20},{20,12},{1,9},{9,17},{29,21},{21,13},{2,10},{... | collective-permute-start | bytes 983048 | tf_op jit(solution)/shard_map/ppermute | solution.py:230
  131.4 16.8 %collective-permute-start.16 = (bf16[2,256,640]{2,1,0:T(8,128)(2,1)S(1)}, bf16[2,256,640]{2,1,0:T(8,128)(2,1)S(1)}, u32[]{:S(2)}, u32[]{:S(2)}) collective-permute-start(bf16[2,256,640]{2,1,0:T(8,128)(2,1)S(1)} %get-tuple-element.32.rest_0_), channel_id=1, source_target_pairs={{0,1},{1,0},{2,3},{3,2},{4,5},{5,4},{6,7},{7,6},{8,9},{9,8},{10,11... | collective-permute-start | bytes 1966088 | tf_op jit(solution)/shard_map/ppermute | solution.py:238
  132.9 15.2 %collective-permute-start.18 = (bf16[2,256,640]{2,1,0:T(8,128)(2,1)S(1)}, bf16[2,256,640]{2,1,0:T(8,128)(2,1)S(1)}, u32[]{:S(2)}, u32[]{:S(2)}) collective-permute-start(bf16[2,256,640]{2,1,0:T(8,128)(2,1)S(1)} %get-tuple-element.33), channel_id=1, source_target_pairs={{0,2},{1,3},{2,0},{3,1},{4,6},{5,7},{6,4},{7,5},{8,10},{9,11},{10,... | collective-permute-start | bytes 1966088 | tf_op jit(solution)/shard_map/ppermute | solution.py:238
  134.5 16.1 %collective-permute-start.26 = (bf16[2,320,256]{2,1,0:T(8,128)(2,1)S(1)}, bf16[2,320,256]{2,1,0:T(8,128)(2,1)S(1)}, u32[]{:S(2)}, u32[]{:S(2)}) collective-permute-start(bf16[2,320,256]{2,1,0:T(8,128)(2,1)S(1)} %add_convert_fusion), channel_id=1, source_target_pairs={{24,16},{16,8},{8,0},{4,12},{12,20},{20,28},{25,17},{17,9},{9,1},{... | collective-permute-start | bytes 983048 | tf_op jit(solution)/shard_map/ppermute | solution.py:230
  137.7 12.9 %collective-permute-start.24 = (bf16[2,320,256]{2,1,0:T(8,128)(2,1)S(1)}, bf16[2,320,256]{2,1,0:T(8,128)(2,1)S(1)}, u32[]{:S(2)}, u32[]{:S(2)}) collective-permute-start(bf16[2,320,256]{2,1,0:T(8,128)(2,1)S(1)} %add_convert_fusion.1), channel_id=1, source_target_pairs={{0,8},{8,16},{16,24},{28,20},{20,12},{12,4},{1,9},{9,17},{17,25},{... | collective-permute-start | bytes 983048 | tf_op jit(solution)/shard_map/ppermute | solution.py:230
  143.2 15.2 %collective-permute-start.30 = (f32[320,256]{1,0:T(8,128)S(1)}, f32[320,256]{1,0:T(8,128)S(1)}, u32[]{:S(2)}, u32[]{:S(2)}) collective-permute-start(f32[320,256]{1,0:T(8,128)S(1)} %slice_bitcast_fusion), channel_id=1, source_target_pairs={{0,4},{4,0},{8,12},{12,8},{16,20},{20,16},{24,28},{28,24},{1,5},{5... | collective-permute-start | bytes 983048 | tf_op jit(solution)/shard_map/ppermute | solution.py:235
  148.5 7.3 %collective-permute-start.17 = (bf16[256,640]{1,0:T(8,128)(2,1)S(1)}, bf16[256,640]{1,0:T(8,128)(2,1)S(1)}, u32[]{:S(2)}, u32[]{:S(2)}) collective-permute-start(bf16[256,640]{1,0:T(8,128)(2,1)S(1)} %get-tuple-element.45), channel_id=1, source_target_pairs={{0,2},{1,3},{2,0},{3,1},{4,6},{5,7},{6,4},{7,5},{8,10},{9,11},{10,... | collective-permute-start | bytes 983048 | tf_op jit(solution)/shard_map/ppermute | solution.py:238
  150.1 7.1 %collective-permute-start.19 = (bf16[256,640]{1,0:T(8,128)(2,1)S(1)}, bf16[256,640]{1,0:T(8,128)(2,1)S(1)}, u32[]{:S(2)}, u32[]{:S(2)}) collective-permute-start(bf16[256,640]{1,0:T(8,128)(2,1)S(1)} %get-tuple-element.46), channel_id=1, source_target_pairs={{0,1},{1,0},{2,3},{3,2},{4,5},{5,4},{6,7},{7,6},{8,9},{9,8},{10,11... | collective-permute-start | bytes 983048 | tf_op jit(solution)/shard_map/ppermute | solution.py:238
  150.8 7.5 %collective-permute-start.27 = (f32[320,256]{1,0:T(8,128)S(1)}, f32[320,256]{1,0:T(8,128)S(1)}, u32[]{:S(2)}, u32[]{:S(2)}) collective-permute-start(f32[320,256]{1,0:T(8,128)S(1)} %slice_bitcast_fusion.2), channel_id=1, source_target_pairs={{0,4},{4,0},{8,12},{12,8},{16,20},{20,16},{24,28},{28,24},{1,5},{5... | collective-permute-start | bytes 983048 | tf_op jit(solution)/shard_map/ppermute | solution.py:235

commit v7 on v5

--- a/solution.py
+++ b/solution.py
@@ -11,7 +11,7 @@
 HEAD_DIM = 64
 F32 = jnp.float32
 BF16 = jnp.bfloat16
-VMEM_LIMIT = 24 * 1024 * 1024
+VMEM_LIMIT = 20 * 1024 * 1024
 
 
 def dot(a, b, ca=1, cb=0):
@@ -32,11 +32,11 @@
 def place(idx, slots, w_ref):
     core = idx[0]
     for j, slot in enumerate(slots):
-        depth = slot.shape[0] // 2
+        depth = slot.shape[1]
 
         @pl.when(idx[2 + 2 * j] == 1)
         def _(slot=slot, depth=depth, plane=idx[1 + 2 * j]):
-            mine, other = slot[:depth, :], slot[depth:, :]
+            mine, other = slot[0], slot[1]
             low = jnp.where(core == 0, mine, other)
             high = jnp.where(core == 0, other, mine)
             w_ref[rows_at(plane, 2 * depth), :] = jnp.concatenate([low, high], axis=0)
@@ -201,10 +201,6 @@
     )
 
 
-def after(x, *others):
-    return lax.optimization_barrier((x, *others))[0]
-
-
 def make_body(n_wide, n_node):
     planes = n_wide // 2
     line4 = planes == 4
@@ -213,6 +209,9 @@
         return lax.ppermute(
             x, "wide", [(2 * s + c, 2 * d + c) for s, d in pairs for c in range(2)]
         )
+
+    outer, middle = [(0, 1), (1, 0), (2, 3), (3, 2)], [(1, 2), (2, 1)]
+    outward, inward = [(1, 0), (2, 3)], [(0, 1), (3, 2)]
 
     def sibling(x):
         return lax.ppermute(x, "wide", [(i, i ^ 1) for i in range(n_wide)])
@@ -226,56 +225,48 @@
         high = jnp.stack([w[:, cols:] for w in weights])
         got = sibling(jnp.where(c == 0, high, low))
         mine = jnp.where(c == 0, low, high)
-        return [jnp.concatenate([mine[i], got[i]], axis=0) for i in range(len(weights))]
-
-    right = [[(s, s + 1) for s in range(planes - 1)][k:] for k in range(planes)]
-    left = [[(s + 1, s) for s in reversed(range(planes - 1))][k:] for k in range(planes)]
+        return got, [jnp.stack([mine[i], got[i]]) for i in range(len(weights))]
 
     def gather_ring(u):
         return [u] + [
             move(u, [(s, (s - j) % planes) for s in range(planes)]) for j in range(1, planes)
         ]
 
-    def gather_step(u, k):
-        return move(u[0], right[k]), move(u[1], left[k])
-
-    def gather_last(second, z):
-        return move(jnp.where(z == 2, *second), right[2] + left[2])
-
     def slot_planes(z):
         if not line4:
             return [x for j in range(planes) for x in (lax.rem(z + j, planes), 1)]
-        last = jnp.where(z == 0, 3, 0)
-        return [
-            *(z, 1, jnp.maximum(z - 1, 0), z >= 1, jnp.minimum(z + 1, 3), z <= 2),
-            *(jnp.maximum(z - 2, 0), z >= 2, jnp.minimum(z + 2, 3), z <= 1),
-            *(last, (z == 0) | (z == 3)),
-        ]
+        beside = lax.bitwise_xor(z, 1)
+        inside = (z == 1) | (z == 2)
+        found = [z, 1, beside, 1, 3 - z, inside, 3 - beside, inside]
+        return found + [3 - beside, ~inside, 3 - z, ~inside]
 
     def send_planes(z):
         if not line4:
             return [lax.rem(z + j, planes) for j in range(planes)]
-        across = jnp.where(z == 0, 3, 0)
-        return [z, jnp.minimum(z + 1, 3), jnp.maximum(z - 1, 0), lax.rem(z + 2, 4), across]
+        beside = lax.bitwise_xor(z, 1)
+        return [z, beside, 3 - z, 3 - beside]
 
     def added(block, got):
         return (block.astype(F32) + got.astype(F32)).astype(BF16)
 
-    def scatter_first(blocks):
-        return move(blocks[4], [(0, 1), (3, 2)])
-
-    def scatter_second(blocks, first):
-        far = added(blocks[3], first)
-        return move(far, [(0, 1), (1, 2)]), move(far, [(3, 2), (2, 1)])
-
-    def scatter_sums(blocks, second):
-        return added(blocks[1], second[0]), added(blocks[2], second[1])
-
-    def scatter_third(sums):
-        return move(sums[0], right[0]), move(sums[1], left[0])
-
-    def scatter_end(blocks, third, c):
-        total = blocks[0].astype(F32) + third[0].astype(F32) + third[1].astype(F32)
+    def hold(x, *others):
+        for y in others:
+            x = jnp.where(jnp.isnan(y[(0,) * y.ndim]), jnp.zeros_like(x), x)
+        return x
+
+    def scatter_first(blocks, first):
+        return added(blocks[3], first), move(blocks[3], inward)
+
+    def scatter_sums(blocks, second, crossed):
+        return added(blocks[2], second), added(blocks[1], crossed)
+
+    def scatter_last(sums):
+        return move(sums[0], middle), move(sums[1], outer)
+
+    def scatter_end(own, got, c):
+        total = own.astype(F32)
+        for part in got:
+            total = total + part.astype(F32)
         return join(total[0], sibling(total[1]), c)
 
     def join(mine, other, c):
@@ -305,34 +296,41 @@
         mix = mixing.reshape(groups, 2 * heads, seq, seq)
         flops = 4 * tokens * width * cols
 
-        u_out, u_value = swap_halves([w_out, w_value], c)
-        act_s, mix_s, cot_s = (sibling(after(x, u_value)) for x in (act, mix, cot))
-        if line4:
-            v1 = gather_step((u_value, u_value), 0)
-            v2 = gather_step(v1, 1)
-            v2, act_s, mix_s, cot_s = lax.optimization_barrier((v2, act_s, mix_s, cot_s))
-            v3 = gather_last(v2, z)
-            u_out = after(u_out, *v2)
-            o1 = gather_step((u_out, u_out), 0)
-            value_slots, o1 = lax.optimization_barrier(([u_value, *v1, *v2, v3], o1))
-            o2 = gather_step(o1, 1)
-        else:
-            value_slots = gather_ring(u_value)
-            out_slots = gather_ring(u_out)
+        got, (u_out, u_value) = swap_halves([w_out, w_value], c)
+        act_s, mix_s, cot_s = (
+            sibling(lax.optimization_barrier((x, got))[0]) for x in (act, mix, cot)
+        )
 
         info = slot_planes(z)
         sends = send_planes(z)
-        n_slots = len(value_slots)
-        idx_slots = jnp.stack([jnp.int32(x) for x in (c, *info)])
-        idx_send = jnp.stack([jnp.int32(x) for x in (c, *sends)])
-        idx_node = jnp.stack([lax.bitwise_xor(n, jnp.int32(j)) for j in range(n_node)])
+        pack = lambda *values: jnp.stack([jnp.int32(x) for x in values])
+        idx_slots = pack(c, *info)
+        idx_send = pack(c, *sends)
+        idx_node = pack(*[lax.bitwise_xor(n, jnp.int32(j)) for j in range(n_node)])
 
         mix_scratch = pltpu.VMEM((2, groups, heads, seq, seq), BF16)
         both = pltpu.VMEM((2 * tokens, width), BF16)
         halves = pltpu.VMEM((2, tokens, width), BF16)
         left_tokens = pltpu.VMEM((cols, 2 * tokens), BF16)
         rows = pltpu.VMEM((width, cols), BF16)
-        send_shapes = [(2, depth // 2, cols)] * len(sends)
+        block = (2, depth // 2, cols)
+        send_shapes = [block] * len(sends)
+
+        if line4:
+            v_outer, v_middle = move(u_value, outer), move(u_value, middle)
+            v_cross = move(v_outer, middle)
+            v_out = move(v_middle, outward)
+            v_last = move(v_cross, outward)
+            value_slots = [u_value, v_outer, v_middle, v_cross, v_out, v_last]
+            swaps = act_s, mix_s, cot_s
+            o_outer = move(hold(u_out, v_out, *swaps), outer)
+            o_middle = move(hold(u_out, v_cross, *swaps), middle)
+            o_cross = move(o_outer, middle)
+            o_out = move(o_middle, outward)
+        else:
+            value_slots = gather_ring(u_value)
+            out_slots = gather_ring(u_out)
+        n_slots = len(value_slots)
 
         mixed_o, mixed_s = call(
             functools.partial(mixed_kernel, n_slots),
@@ -343,11 +341,7 @@
             flops,
         )(idx_slots, act, act_s, mix, mix_s, *value_slots)
         mixed_r = sibling(mixed_s)
-        if line4:
-            (mixed_o, mixed_s, mixed_r), o2 = lax.optimization_barrier(
-                ((mixed_o, mixed_s, mixed_r), o2)
-            )
-            out_slots = [u_out, *o1, *o2, gather_last(o2, z)]
+        idx_out = hold(idx_send, o_outer, o_middle, mixed_r) if line4 else idx_send
         out_sends = call(
             grad_out_kernel,
             "grad_out",
@@ -355,9 +349,16 @@
             send_shapes,
             [both, left_tokens, rows, pltpu.SemaphoreType.DMA((2,))],
             flops,
-        )(idx_send, cot, cot_s, mixed_o, mixed_s)
+        )(idx_out, cot, cot_s, mixed_o, mixed_s)
         if line4:
-            out_slots, out_sends = lax.optimization_barrier((out_slots, out_sends))
+            inside = (z == 1) | (z == 2)
+            swapped = move(hold(jnp.where(inside, o_cross, out_sends[2]), o_out), outer)
+            out_slots = [u_out, o_outer, o_middle, o_cross, o_out, swapped]
+            out_crossing, out_second = scatter_first(out_sends, swapped)
+            out_crossed = move(out_crossing, middle)
+            idx_value = hold(idx_slots, out_crossing)
+        else:
+            idx_value = idx_slots
         w_full, left = call(
             functools.partial(d_value_kernel, n_slots),
             "d_value",
@@ -365,26 +366,8 @@
             [(width, cols), (cols, 2 * tokens)],
             [halves, mix_scratch, pltpu.SemaphoreType.DMA((4,))],
             flops,
-        )(idx_slots, cot, cot_s, mix, mix_s, *out_slots)
+        )(idx_value, cot, cot_s, mix, mix_s, *out_slots)
         w_full_s = sibling(w_full)
-        if line4:
-            out_first = scatter_first(out_sends)
-            left, out_first = lax.optimization_barrier((left, out_first))
-            out_second = scatter_second(out_sends, out_first)
-        back_sends = call(
-            gradient_kernel,
-            "grad_value",
-            [SMEM] + [ANY] * 2 + [VMEM],
-            send_shapes,
-            [both, rows, pltpu.SemaphoreType.DMA((2,))],
-            flops,
-        )(idx_send, act, act_s, left)
-        if line4:
-            back_first = scatter_first(back_sends)
-            out_sums = scatter_sums(out_sends, out_second)
-            w_full_s, out_sums = lax.optimization_barrier((w_full_s, out_sums))
-            out_third = scatter_third(out_sums)
-
         part = width // n_node
         half = tokens // 2
         if n_node == 4:
@@ -401,14 +384,20 @@
         )(idx_node, mixed_o, mixed_r, w_full, w_full_s)
 
         if line4:
-            back_first = after(back_first, terms[0])
-            back_second = scatter_second(back_sends, back_first)
-            back_third = scatter_third(scatter_sums(back_sends, back_second))
-            grad_out = scatter_end(out_sends, out_third, c)
-            grad_value = scatter_end(back_sends, back_third, c)
-        else:
-            grad_value = scatter_ring(back_sends, c)
-            grad_out = scatter_ring(out_sends, c)
+            out_sums = scatter_sums(out_sends, out_second, out_crossed)
+            out_got = scatter_last(out_sums)
+            idx_back = hold(idx_send, *out_sums, terms[0])
+        else:
+            idx_back = idx_send
+        back_sends = call(
+            gradient_kernel,
+            "grad_value",
+            [SMEM] + [ANY] * 2 + [VMEM],
+            send_shapes,
+            [both, rows, pltpu.SemaphoreType.DMA((2,))],
+            flops,
+        )(idx_back, act, act_s, left)
+
         if n_node == 4:
             along_x, along_y, kept = terms
             kept = kept.astype(F32)
@@ -416,6 +405,7 @@
             got_y = flip(along_y, 2).astype(F32)
             last_y = flip((kept[1] + got_x[1]).astype(BF16), 2)
             last_x = flip((kept[3] + got_y[1]).astype(BF16), 1)
+            early = got_x, got_y
             layer_out = jnp.concatenate(
                 [
                     kept[0] + got_x[0] + last_y.astype(F32),
@@ -424,10 +414,20 @@
                 axis=0,
             )
         else:
-            layer_out = terms[0].astype(F32)
+            early, layer_out = terms, terms[0].astype(F32)
             for j in range(1, n_node):
                 layer_out = layer_out + flip(terms[j], j).astype(F32)
         layer_out = layer_out.astype(BF16).reshape(micro, images, seq, part)
+        if line4:
+            first = move(back_sends[2], inward)
+            crossing, second = scatter_first(back_sends, first)
+            crossed = move(hold(crossing, *early), middle)
+            got = scatter_last(scatter_sums(back_sends, second, crossed))
+            grad_value = scatter_end(back_sends[0], got, c)
+            grad_out = scatter_end(out_sends[0], out_got, c)
+        else:
+            grad_value = scatter_ring(back_sends, c)
+            grad_out = scatter_ring(out_sends, c)
         return layer_out, grad_value, grad_out
 
     return body

time: 151 us -> 179 us (1.19)
  between operations: 1.23 us -> 20.7 us
  starting transfers between devices: 59.4 us -> 45.3 us
  local copies, waits for them, and re-layouts: 14.4 us -> 25.7 us
  waiting for transfers between devices: 44.8 us -> 52.4 us
    slice x0 -> x17, local copies, waits for them, and re-layouts: none -> 13.2 us  [the longest x15 12.5 us: hold(): x = jnp.where(jnp.isnan(y[(0,) * y.ndim]), jnp.zeros_like(x), x)]
    ppermute x20 -> x19, starting transfers between devices: 52.4 us -> 39.4 us  [move(): lax.ppermute(x, 'wide', [(2 * s + c, 2 * d + c) for s, d in pairs for c i...]
    ppermute x20 -> x19, waiting for transfers between devices: 32.8 us -> 41.3 us  [move(): lax.ppermute(x, 'wide', [(2 * s + c, 2 * d + c) for s, d in pairs for c i...]
    another operation x2 -> x4, other arithmetic: 0.32 us -> 2.22 us  [the longest x2 1.9 us: swap_halves(): return (got, [jnp.stack([mine[i], got[i]]) for i in range(len(weights))])]
    convert_element_type x6 -> x5, other arithmetic: 0.51 us -> 2.36 us  [added(): return (block.astype(F32) + got.astype(F32)).astype(BF16)]
    unnamed x44 -> x38, local copies, waits for them, and re-layouts: 11.4 us -> 10.1 us
  transfers between devices with their start and end apart: 32 -> 31, of which waited for: 15 -> 13; matrix products, arithmetic and copies ran while one was open for 3% -> 9% of each run, Pallas kernels for 16% -> 9%
where the time goes in v7:
time: 179 us; the launch traced here: 178 us
  waiting for transfers between devices  52.4 us (29%)
  starting transfers between devices  45.3 us (25%)
  local copies, waits for them, and re-layouts  25.7 us (14%)
  Pallas kernels  25.3 us (14%)
  between operations  20.7 us (12%)
  other arithmetic  8.43 us (5%)
    ppermute x19, waiting for transfers between devices, move(): lax.ppermute(x, 'wide', [(2 * s + c, 2 * d + c) for s, d in pairs for c i...  41.3 us
    ppermute x19, starting transfers between devices, move(): lax.ppermute(x, 'wide', [(2 * s + c, 2 * d + c) for s, d in pairs for c i...  39.4 us
    slice x15, local copies, waits for them, and re-layouts, hold(): x = jnp.where(jnp.isnan(y[(0,) * y.ndim]), jnp.zeros_like(x), x)  12.5 us
    unnamed x38, local copies, waits for them, and re-layouts  10.1 us
    ppermute x4, waiting for transfers between devices, flip(): return lax.ppermute(x, 'node', [(i, i ^ j) for i in range(n_node)])  8.23 us
    pallas_call x1, Pallas kernels, body(): call(functools.partial(mixed_kernel, n_slots), 'mixed', [SMEM] + [ANY] *...  6.08 us
    pallas_call x1, Pallas kernels, body(): call(functools.partial(d_value_kernel, n_slots), 'd_value', [SMEM] + [ANY...  6.03 us
    pallas_call x1, Pallas kernels, body(): call(grad_out_kernel, 'grad_out', [SMEM] + [ANY] * 2 + [VMEM] * 2, send_s...  5.61 us
  transfers between devices with their start and end apart: 31, of which 13 were waited for; matrix products, arithmetic and copies ran while one was open for 9% of the time, Pallas kernels for 9%

profile of v7, /device:TPU:0, one launch (start us, length us, event | category | flops | bytes accessed | tf_op | source)
XLA Modules:
  0.0 177.9 jit_solution(17698080358774673680)
XLA Ops:
  0.7 1.2 slice_bitcast_fusion.7
  1.8 1.0 slice_bitcast_fusion.6
  3.4 1.3 collective-permute-done
  5.7 0.7 fusion.17
  6.4 2.8 %collective-permute-start.3 = (bf16[2,320,256]{2,1,0:T(8,128)(2,1)S(1)}, bf16[2,320,256]{2,1,0:T(8,128)(2,1)S(1)}, u32[]{:S(2)}, u32[]{:S(2)}) collective-permute-start(bf16[2,320,256]{2,1,0:T(8,128)(2,1)S(1)} %pad_maximum_fusion.5.rest_0_), channel_id=1, source_target_pairs={{0,8},{4,12},{8,0},{12,4},{16,24},{20,28},{24,16},{28,20},{1,9},{5... | collective-permute-start | bytes 983048 | tf_op jit(solution)/shard_map/ppermute | solution.py:209
  9.2 0.7 collective-permute-start.4
  9.9 7.6 %collective-permute-done.3.rest_1_ = bf16[2,320,256]{2,1,0:T(8,128)(2,1)S(1)} collective-permute-done((bf16[2,320,256]{2,1,0:T(8,128)(2,1)S(1)}, bf16[2,320,256]{2,1,0:T(8,128)(2,1)S(1)}, u32[]{:S(2)}, u32[]{:S(2)}) %collective-permute-start.3) | collective-permute-done | bytes 327712 | tf_op jit(solution)/shard_map/ppermute | solution.py:209
  17.4 1.4 collective-permute-start.5
  18.8 0.7 copy-done.7
  19.5 1.3 collective-permute-start.6
  20.8 0.7 copy-done.9
  21.6 1.3 collective-permute-start.7
  23.0 1.3 slice.149
  25.6 6.8 %collective-permute-done.6.rest_4_ = bf16[2,320,256]{2,1,0:T(8,128)(2,1)} collective-permute-done((bf16[2,320,256]{2,1,0:T(8,128)(2,1)S(1)}, bf16[2,320,256]{2,1,0:T(8,128)(2,1)}, u32[]{:S(2)}, u32[]{:S(2)}) %collective-permute-start.6) | collective-permute-done | bytes 327712 | tf_op jit(solution)/shard_map/ppermute | solution.py:209
  32.3 1.2 slice.153
  34.8 1.2 slice.147
  37.3 1.2 slice.146
  39.8 1.2 slice.148
  42.3 1.9 %pad_maximum_fusion.6 = (bf16[2,320,256]{2,1,0:T(8,128)(2,1)S(1)}, bf16[2,320,256]{2,1,0:T(8,128)(2,1)}, bf16[2,320,256]{2,1,0:T(8,128)(2,1)}) fusion(bf16[1,320,256]{2,1,0:T(8,128)(2,1)} %get-tuple-element.54, bf16[1,320,256]{2,1,0:T(8,128)(2,1)S(1)} %get-tuple-element.52, pred[]{:T(512)} %bitcast.22, pred[]{:T(512)} %bitcast.21, pred[]{:T(512)} %bitcast.20, ...), kind=kLoop, calls=%fused_computation.34 | loop fusion | flops 1474560 | bytes 1310725 | tf_op jit(solution)/shard_map/stack | solution.py:228
  44.1 1.4 collective-permute-start.10
  45.5 4.9 %collective-permute-start.11 = (bf16[2,320,256]{2,1,0:T(8,128)(2,1)}, bf16[2,320,256]{2,1,0:T(8,128)(2,1)}, u32[]{:S(2)}, u32[]{:S(2)}) collective-permute-start(bf16[2,320,256]{2,1,0:T(8,128)(2,1)} %get-tuple-element.51), channel_id=1, source_target_pairs={{0,8},{4,12},{8,0},{12,4},{16,24},{20,28},{24,16},{28,20},{1,9},{5... | collective-permute-start | bytes 983048 | tf_op jit(solution)/shard_map/ppermute | solution.py:209
  50.4 1.7 copy-done.1
  52.2 1.0 copy-done.8
  53.1 1.0 copy-done.10
  54.1 6.1 %mixed.1 = (bf16[512,256]{1,0:T(8,128)(2,1)S(1)}, bf16[512,256]{1,0:T(8,128)(2,1)}) custom-call(s32[13]{0:T(128)S(1)} %stack.95.idx, bf16[512,2560]{1,0:T(8,128)(2,1)S(1)} %bitcast.74, bf16[512,2560]{1,0:T(8,128)(2,1)} %collective-permute-done.1.act_s.right_s, bf16[4,8,128,128]{3,2,1,0:T(8,128)(2,1)S(1)} %bitcast.77, ...), custom_call_target="tpu_custom_call" | custom-call | flops 1342177280 | bytes 12582912 | tf_op jit(solution)/shard_map/mixed/pallas_call | solution.py:335
  60.4 1.6 collective-permute-done.8.mixed_r
  62.5 0.7 copy-done.16
  64.5 1.2 slice.152
  67.0 1.2 slice.154
  69.5 1.3 collective-permute-start.12
  70.8 0.7 collective-permute-start.13
  71.5 5.6 %grad_out.1 = (bf16[2,320,256]{2,1,0:T(8,128)(2,1)S(1)}, bf16[2,320,256]{2,1,0:T(8,128)(2,1)S(1)}, bf16[2,320,256]{2,1,0:T(8,128)(2,1)S(1)}, bf16[2,320,256]{2,1,0:T(8,128)(2,1)}) custom-call(s32[5]{0:T(128)S(1)} %broadcast_select_fusion.8.idx, bf16[512,2560]{1,0:T(8,128)(2,1)S(1)} %bitcast.71, bf16[512,2560]{1,0:T(8,128)(2,1)} %collective-permute-done.9.cot_s, ...), custom_call_target="tpu_custom_call" | custom-call | flops 1342177280 | bytes 12582912 | tf_op jit(solution)/shard_map/grad_out/pallas_call | solution.py:345
  77.2 0.7 copy-done.13
  77.9 3.5 %collective-permute-done.12.rest_4_ = bf16[2,320,256]{2,1,0:T(8,128)(2,1)S(1)} collective-permute-done((bf16[2,320,256]{2,1,0:T(8,128)(2,1)}, bf16[2,320,256]{2,1,0:T(8,128)(2,1)S(1)}, u32[]{:S(2)}, u32[]{:S(2)}) %collective-permute-start.12) | collective-permute-done | bytes 327712 | tf_op jit(solution)/shard_map/ppermute | solution.py:209
  83.3 1.9 %collective-permute-start.14 = (bf16[2,320,256]{2,1,0:T(8,128)(2,1)S(1)}, bf16[2,320,256]{2,1,0:T(8,128)(2,1)S(1)}, u32[]{:S(2)}, u32[]{:S(2)}) collective-permute-start(bf16[2,320,256]{2,1,0:T(8,128)(2,1)S(1)} %select_select_fusion), channel_id=1, source_target_pairs={{0,8},{4,12},{8,0},{12,4},{16,24},{20,28},{24,16},{28,20},{1,9},{5... | collective-permute-start | bytes 983048 | tf_op jit(solution)/shard_map/ppermute | solution.py:209
  85.2 7.1 %collective-permute-done.14.rest_5_ = bf16[2,320,256]{2,1,0:T(8,128)(2,1)S(1)} collective-permute-done((bf16[2,320,256]{2,1,0:T(8,128)(2,1)S(1)}, bf16[2,320,256]{2,1,0:T(8,128)(2,1)S(1)}, u32[]{:S(2)}, u32[]{:S(2)}) %collective-permute-start.14) | collective-permute-done | bytes 327712 | tf_op jit(solution)/shard_map/ppermute | solution.py:209
  92.2 1.1 add_convert_fusion.5
  95.2 6.0 %d_value.1 = (bf16[2560,256]{1,0:T(8,128)(2,1)}, bf16[256,1024]{1,0:T(8,128)(2,1)S(1)}) custom-call(s32[13]{0:T(128)S(1)} %broadcast_select_fusion.5.idx, bf16[512,2560]{1,0:T(8,128)(2,1)S(1)} %bitcast.72, bf16[512,2560]{1,0:T(8,128)(2,1)} %collective-permute-done.9.cot_s, bf16[4,8,128,128]{3,2,1,0:T(8,128)(2,1)S(1)} %bitcast.78, ...), custom_call_target="tpu_custom_call" | custom-call | flops 1342177280 | bytes 12582912 | tf_op jit(solution)/shard_map/d_value/pallas_call | solution.py:362
  101.3 0.8 copy-done.5
  102.1 3.6 %collective-permute-start.21 = (bf16[2,320,256]{2,1,0:T(8,128)(2,1)}, bf16[2,320,256]{2,1,0:T(8,128)(2,1)S(1)}, u32[]{:S(2)}, u32[]{:S(2)}) collective-permute-start(bf16[2,320,256]{2,1,0:T(8,128)(2,1)} %get-tuple-element.26), channel_id=1, source_target_pairs={{0,8},{4,12},{24,16},{28,20},{1,9},{5,13},{25,17},{29,21},{2,10},{... | collective-permute-start | bytes 983048 | tf_op jit(solution)/shard_map/ppermute | solution.py:209
  105.7 0.9 collective-permute-start.20
  106.6 6.8 %collective-permute-done.21 = bf16[2,320,256]{2,1,0:T(8,128)(2,1)S(1)} collective-permute-done((bf16[2,320,256]{2,1,0:T(8,128)(2,1)}, bf16[2,320,256]{2,1,0:T(8,128)(2,1)S(1)}, u32[]{:S(2)}, u32[]{:S(2)}) %collective-permute-start.21) | collective-permute-done | bytes 327712 | tf_op jit(solution)/shard_map/ppermute | solution.py:209
  115.3 1.1 add_convert_fusion.4
  118.3 1.1 copy-done.14
  119.3 1.6 copy-done.15
  120.9 3.2 %terms.1 = (bf16[2,256,640]{2,1,0:T(8,128)(2,1)S(1)}, bf16[2,256,640]{2,1,0:T(8,128)(2,1)S(1)}, bf16[4,256,640]{2,1,0:T(8,128)(2,1)S(1)}) custom-call(s32[4]{0:T(128)S(1)} %pad_add_fusion.idx, bf16[512,256]{1,0:T(8,128)(2,1)S(1)} %get-tuple-element.23.mixed_o, bf16[512,256]{1,0:T(8,128)(2,1)S(1)} %copy-done.17, bf16[2560,256]{1,0:T(8,128)(2,1)} %get-tuple-element.28.w_o, ...), custom_call_target="tpu_custom_call" | custom-call | flops 1342177280 | bytes 12582912 | tf_op jit(solution)/shard_map/terms/pallas_call | solution.py:377
  124.6 1.5 collective-permute-start.16
  127.4 1.6 collective-permute-start.18
  129.0 4.4 %grad_value.1 = (bf16[2,320,256]{2,1,0:T(8,128)(2,1)S(1)}, bf16[2,320,256]{2,1,0:T(8,128)(2,1)S(1)}, bf16[2,320,256]{2,1,0:T(8,128)(2,1)S(1)}, bf16[2,320,256]{2,1,0:T(8,128)(2,1)S(1)}) custom-call(s32[5]{0:T(128)S(1)} %broadcast_select_fusion.4.idx, bf16[512,2560]{1,0:T(8,128)(2,1)S(1)} %bitcast.75, bf16[512,2560]{1,0:T(8,128)(2,1)} %collective-permute-done.1.act_s.right_s, ...), custom_call_target="tpu_custom_call" | custom-call | flops 1342177280 | bytes 12582912 | tf_op jit(solution)/shard_map/grad_value/pallas_call | solution.py:392
  133.5 4.3 %collective-permute-start.24 = (bf16[2,320,256]{2,1,0:T(8,128)(2,1)S(1)}, bf16[2,320,256]{2,1,0:T(8,128)(2,1)S(1)}, u32[]{:S(2)}, u32[]{:S(2)}) collective-permute-start(bf16[2,320,256]{2,1,0:T(8,128)(2,1)S(1)} %get-tuple-element.35), channel_id=1, source_target_pairs={{0,8},{4,12},{24,16},{28,20},{1,9},{5,13},{25,17},{29,21},{2,10},{... | collective-permute-start | bytes 983048 | tf_op jit(solution)/shard_map/ppermute | solution.py:209
  137.8 0.7 collective-permute-start.28
  138.5 1.8 %collective-permute-start.29 = (bf16[2,320,256]{2,1,0:T(8,128)(2,1)S(1)}, bf16[2,320,256]{2,1,0:T(8,128)(2,1)S(1)}, u32[]{:S(2)}, u32[]{:S(2)}) collective-permute-start(bf16[2,320,256]{2,1,0:T(8,128)(2,1)S(1)} %add_convert_fusion.4), channel_id=1, source_target_pairs={{0,8},{4,12},{8,0},{12,4},{16,24},{20,28},{24,16},{28,20},{1,9},{5... | collective-permute-start | bytes 983048 | tf_op jit(solution)/shard_map/ppermute | solution.py:209
  140.3 3.1 %collective-permute-done.18 = bf16[2,256,640]{2,1,0:T(8,128)(2,1)S(1)} collective-permute-done((bf16[2,256,640]{2,1,0:T(8,128)(2,1)S(1)}, bf16[2,256,640]{2,1,0:T(8,128)(2,1)S(1)}, u32[]{:S(2)}, u32[]{:S(2)}) %collective-permute-start.18) | collective-permute-done | bytes 655392 | tf_op jit(solution)/shard_map/ppermute | solution.py:220
  143.4 4.3 %collective-permute-start.22 = (bf16[2,320,256]{2,1,0:T(8,128)(2,1)S(1)}, bf16[2,320,256]{2,1,0:T(8,128)(2,1)S(1)}, u32[]{:S(2)}, u32[]{:S(2)}) collective-permute-start(bf16[2,320,256]{2,1,0:T(8,128)(2,1)S(1)} %get-tuple-element.36), channel_id=1, source_target_pairs={{0,8},{4,12},{24,16},{28,20},{1,9},{5,13},{25,17},{29,21},{2,10},{... | collective-permute-start | bytes 983048 | tf_op jit(solution)/shard_map/ppermute | solution.py:209
  151.5 0.7 collective-permute-start.25
  152.2 0.8 collective-permute-done.29
  153.1 4.9 %collective-permute-done.22 = bf16[2,320,256]{2,1,0:T(8,128)(2,1)S(1)} collective-permute-done((bf16[2,320,256]{2,1,0:T(8,128)(2,1)S(1)}, bf16[2,320,256]{2,1,0:T(8,128)(2,1)S(1)}, u32[]{:S(2)}, u32[]{:S(2)}) %collective-permute-start.22) | collective-permute-done | bytes 327712 | tf_op jit(solution)/shard_map/ppermute | solution.py:209
  158.0 0.7 collective-permute-start.23
  158.8 4.9 %collective-permute-start.26 = (bf16[2,320,256]{2,1,0:T(8,128)(2,1)S(1)}, bf16[2,320,256]{2,1,0:T(8,128)(2,1)S(1)}, u32[]{:S(2)}, u32[]{:S(2)}) collective-permute-start(bf16[2,320,256]{2,1,0:T(8,128)(2,1)S(1)} %add_convert_fusion), channel_id=1, source_target_pairs={{0,8},{4,12},{8,0},{12,4},{16,24},{20,28},{24,16},{28,20},{1,9},{5... | collective-permute-start | bytes 983048 | tf_op jit(solution)/shard_map/ppermute | solution.py:209
  165.5 3.9 %collective-permute-done.26 = bf16[2,320,256]{2,1,0:T(8,128)(2,1)S(1)} collective-permute-done((bf16[2,320,256]{2,1,0:T(8,128)(2,1)S(1)}, bf16[2,320,256]{2,1,0:T(8,128)(2,1)S(1)}, u32[]{:S(2)}, u32[]{:S(2)}) %collective-permute-start.26) | collective-permute-done | bytes 327712 | tf_op jit(solution)/shard_map/ppermute | solution.py:209
  169.6 4.9 %collective-permute-done.17 = bf16[256,640]{1,0:T(8,128)(2,1)S(1)} collective-permute-done((bf16[256,640]{1,0:T(8,128)(2,1)S(1)}, bf16[256,640]{1,0:T(8,128)(2,1)S(1)}, u32[]{:S(2)}, u32[]{:S(2)}) %collective-permute-start.17) | collective-permute-done | bytes 327712 | tf_op jit(solution)/shard_map/ppermute | solution.py:220
  175.0 0.9 pad_maximum_fusion
  176.0 0.9 pad_maximum_fusion.2
  176.9 0.9 pad_maximum_fusion.1
  (89 shorter events, 9.2 us)
Async XLA Ops:
  0.6 4.1 %copy-start = (bf16[2,2,128,2560]{3,2,1,0:T(8,128)(2,1)S(1)}, bf16[2,2,128,2560]{3,2,1,0:T(8,128)(2,1)}, u32[]{:S(2)}) copy-start(bf16[2,2,128,2560]{3,2,1,0:T(8,128)(2,1)} %param.7) | copy-start | bytes 7864324
  2.9 1.8 collective-permute-start
  4.7 32.6 %collective-permute-start.9 = (bf16[512,2560]{1,0:T(8,128)(2,1)S(1)}, bf16[512,2560]{1,0:T(8,128)(2,1)}, u32[]{:S(2)}, u32[]{:S(2)}) collective-permute-start(bf16[512,2560]{1,0:T(8,128)(2,1)S(1)} %bitcast.70), channel_id=1, source_target_pairs={{0,4},{4,0},{8,12},{12,8},{16,20},{20,16},{24,28},{28,24},{1,5},{5... | collective-permute-start | bytes 7864328 | tf_op jit(solution)/shard_map/ppermute | solution.py:217
  5.1 34.7 %collective-permute-start.1 = (bf16[512,2560]{1,0:T(8,128)(2,1)}, bf16[512,2560]{1,0:T(8,128)(2,1)}, u32[]{:S(2)}, u32[]{:S(2)}) collective-permute-start(bf16[512,2560]{1,0:T(8,128)(2,1)} %bitcast.73), channel_id=1, source_target_pairs={{0,4},{4,0},{8,12},{12,8},{16,20},{20,16},{24,28},{28,24},{1,5},{5... | collective-permute-start | bytes 7864328 | tf_op jit(solution)/shard_map/ppermute | solution.py:217
  5.2 29.6 %collective-permute-start.2 = (bf16[4,8,128,128]{3,2,1,0:T(8,128)(2,1)}, bf16[4,8,128,128]{3,2,1,0:T(8,128)(2,1)}, u32[]{:S(2)}, u32[]{:S(2)}) collective-permute-start(bf16[4,8,128,128]{3,2,1,0:T(8,128)(2,1)} %bitcast.76), channel_id=1, source_target_pairs={{0,4},{4,0},{8,12},{12,8},{16,20},{20,16},{24,28},{28,24},{1,5},{5... | collective-permute-start | bytes 3145736 | tf_op jit(solution)/shard_map/ppermute | solution.py:217
  6.4 11.0 %collective-permute-start.3 = (bf16[2,320,256]{2,1,0:T(8,128)(2,1)S(1)}, bf16[2,320,256]{2,1,0:T(8,128)(2,1)S(1)}, u32[]{:S(2)}, u32[]{:S(2)}) collective-permute-start(bf16[2,320,256]{2,1,0:T(8,128)(2,1)S(1)} %pad_maximum_fusion.5.rest_0_), channel_id=1, source_target_pairs={{0,8},{4,12},{8,0},{12,4},{16,24},{20,28},{24,16},{28,20},{1,9},{5... | collective-permute-start | bytes 983048 | tf_op jit(solution)/shard_map/ppermute | solution.py:209
  9.2 10.4 %collective-permute-start.4 = (bf16[2,320,256]{2,1,0:T(8,128)(2,1)S(1)}, bf16[2,320,256]{2,1,0:T(8,128)(2,1)S(1)}, u32[]{:S(2)}, u32[]{:S(2)}) collective-permute-start(bf16[2,320,256]{2,1,0:T(8,128)(2,1)S(1)} %pad_maximum_fusion.5.rest_0_), channel_id=1, source_target_pairs={{8,16},{12,20},{16,8},{20,12},{9,17},{13,21},{17,9},{21,13},{10,18... | collective-permute-start | bytes 983048 | tf_op jit(solution)/shard_map/ppermute | solution.py:209
  17.4 4.1 %collective-permute-start.5 = (bf16[2,320,256]{2,1,0:T(8,128)(2,1)S(1)}, bf16[2,320,256]{2,1,0:T(8,128)(2,1)}, u32[]{:S(2)}, u32[]{:S(2)}) collective-permute-start(bf16[2,320,256]{2,1,0:T(8,128)(2,1)S(1)} %collective-permute-done.3.rest_1_), channel_id=1, source_target_pairs={{8,16},{12,20},{16,8},{20,12},{9,17},{13,21},{17,9},{21,13},{10,18... | collective-permute-start | bytes 983048 | tf_op jit(solution)/shard_map/ppermute | solution.py:209
  18.8 0.7 copy-start.7
  19.5 12.8 %collective-permute-start.6 = (bf16[2,320,256]{2,1,0:T(8,128)(2,1)S(1)}, bf16[2,320,256]{2,1,0:T(8,128)(2,1)}, u32[]{:S(2)}, u32[]{:S(2)}) collective-permute-start(bf16[2,320,256]{2,1,0:T(8,128)(2,1)S(1)} %collective-permute-done.4.rest_2_), channel_id=1, source_target_pairs={{8,0},{12,4},{16,24},{20,28},{9,1},{13,5},{17,25},{21,29},{10,2},{... | collective-permute-start | bytes 983048 | tf_op jit(solution)/shard_map/ppermute | solution.py:209
  20.8 0.7 copy-start.9
  21.6 28.9 %collective-permute-start.7 = (bf16[2,320,256]{2,1,0:T(8,128)(2,1)}, bf16[2,320,256]{2,1,0:T(8,128)(2,1)}, u32[]{:S(2)}, u32[]{:S(2)}) collective-permute-start(bf16[2,320,256]{2,1,0:T(8,128)(2,1)} %collective-permute-done.5.rest_3_), channel_id=1, source_target_pairs={{8,0},{12,4},{16,24},{20,28},{9,1},{13,5},{17,25},{21,29},{10,2},{... | collective-permute-start | bytes 983048 | tf_op jit(solution)/shard_map/ppermute | solution.py:209
  23.0 27.5 %copy-start.3 = (bf16[2,2,8,128,128]{4,3,2,1,0:T(8,128)(2,1)S(1)}, bf16[2,2,8,128,128]{4,3,2,1,0:T(8,128)(2,1)}, u32[]{:S(2)}) copy-start(bf16[2,2,8,128,128]{4,3,2,1,0:T(8,128)(2,1)} %param.6) | copy-start | bytes 3145732
  44.1 20.4 %collective-permute-start.10 = (bf16[2,320,256]{2,1,0:T(8,128)(2,1)}, bf16[2,320,256]{2,1,0:T(8,128)(2,1)}, u32[]{:S(2)}, u32[]{:S(2)}) collective-permute-start(bf16[2,320,256]{2,1,0:T(8,128)(2,1)} %get-tuple-element.50), channel_id=1, source_target_pairs={{8,16},{12,20},{16,8},{20,12},{9,17},{13,21},{17,9},{21,13},{10,18... | collective-permute-start | bytes 983048 | tf_op jit(solution)/shard_map/ppermute | solution.py:209
  45.5 21.5 %collective-permute-start.11 = (bf16[2,320,256]{2,1,0:T(8,128)(2,1)}, bf16[2,320,256]{2,1,0:T(8,128)(2,1)}, u32[]{:S(2)}, u32[]{:S(2)}) collective-permute-start(bf16[2,320,256]{2,1,0:T(8,128)(2,1)} %get-tuple-element.51), channel_id=1, source_target_pairs={{0,8},{4,12},{8,0},{12,4},{16,24},{20,28},{24,16},{28,20},{1,9},{5... | collective-permute-start | bytes 983048 | tf_op jit(solution)/shard_map/ppermute | solution.py:209
  50.4 1.7 copy-start.1
  52.2 1.0 copy-start.8
  53.1 1.0 copy-start.10
  60.2 1.8 %collective-permute-start.8 = (bf16[512,256]{1,0:T(8,128)(2,1)}, bf16[512,256]{1,0:T(8,128)(2,1)S(1)}, u32[]{:S(2)}, u32[]{:S(2)}) collective-permute-start(bf16[512,256]{1,0:T(8,128)(2,1)} %get-tuple-element.24.mixed_s), channel_id=1, source_target_pairs={{0,4},{4,0},{8,12},{12,8},{16,20},{20,16},{24,28},{28,24},{1,5},{5... | collective-permute-start | bytes 786440 | tf_op jit(solution)/shard_map/ppermute | solution.py:217
  62.5 0.7 copy-start.16
  69.5 11.9 %collective-permute-start.12 = (bf16[2,320,256]{2,1,0:T(8,128)(2,1)}, bf16[2,320,256]{2,1,0:T(8,128)(2,1)S(1)}, u32[]{:S(2)}, u32[]{:S(2)}) collective-permute-start(bf16[2,320,256]{2,1,0:T(8,128)(2,1)} %collective-permute-done.10.rest_2_), channel_id=1, source_target_pairs={{8,0},{12,4},{16,24},{20,28},{9,1},{13,5},{17,25},{21,29},{10,2},{... | collective-permute-start | bytes 983048 | tf_op jit(solution)/shard_map/ppermute | solution.py:209
  70.8 12.4 %collective-permute-start.13 = (bf16[2,320,256]{2,1,0:T(8,128)(2,1)}, bf16[2,320,256]{2,1,0:T(8,128)(2,1)S(1)}, u32[]{:S(2)}, u32[]{:S(2)}) collective-permute-start(bf16[2,320,256]{2,1,0:T(8,128)(2,1)} %collective-permute-done.11.rest_1_), channel_id=1, source_target_pairs={{8,16},{12,20},{16,8},{20,12},{9,17},{13,21},{17,9},{21,13},{10,18... | collective-permute-start | bytes 983048 | tf_op jit(solution)/shard_map/ppermute | solution.py:209
  77.1 0.7 copy-start.13
  77.9 17.3 %copy-start.11 = (bf16[2,320,256]{2,1,0:T(8,128)(2,1)}, bf16[2,320,256]{2,1,0:T(8,128)(2,1)S(1)}, u32[]{:S(2)}) copy-start(bf16[2,320,256]{2,1,0:T(8,128)(2,1)S(1)} %get-tuple-element.38) | copy-start | bytes 983044
  77.9 17.3 %copy-start.4 = (bf16[2,2,8,128,128]{4,3,2,1,0:T(8,128)(2,1)S(1)}, bf16[2,2,8,128,128]{4,3,2,1,0:T(8,128)(2,1)}, u32[]{:S(2)}) copy-start(bf16[2,2,8,128,128]{4,3,2,1,0:T(8,128)(2,1)} %param.6) | copy-start | bytes 3145732
  83.3 9.0 %collective-permute-start.14 = (bf16[2,320,256]{2,1,0:T(8,128)(2,1)S(1)}, bf16[2,320,256]{2,1,0:T(8,128)(2,1)S(1)}, u32[]{:S(2)}, u32[]{:S(2)}) collective-permute-start(bf16[2,320,256]{2,1,0:T(8,128)(2,1)S(1)} %select_select_fusion), channel_id=1, source_target_pairs={{0,8},{4,12},{8,0},{12,4},{16,24},{20,28},{24,16},{28,20},{1,9},{5... | collective-permute-start | bytes 983048 | tf_op jit(solution)/shard_map/ppermute | solution.py:209
  93.3 1.9 %copy-start.18 = (bf16[2,320,256]{2,1,0:T(8,128)(2,1)}, bf16[2,320,256]{2,1,0:T(8,128)(2,1)S(1)}, u32[]{:S(2)}) copy-start(bf16[2,320,256]{2,1,0:T(8,128)(2,1)S(1)} %add_convert_fusion.5) | copy-start | bytes 983044
  101.3 0.8 copy-start.5
  102.0 17.3 %copy-start.17 = (bf16[512,256]{1,0:T(8,128)(2,1)S(1)}, bf16[512,256]{1,0:T(8,128)(2,1)}, u32[]{:S(2)}) copy-start(bf16[512,256]{1,0:T(8,128)(2,1)} %copy-done.16) | copy-start | bytes 786436
  102.0 16.2 %collective-permute-start.15 = (bf16[2560,256]{1,0:T(8,128)(2,1)}, bf16[2560,256]{1,0:T(8,128)(2,1)S(1)}, u32[]{:S(2)}, u32[]{:S(2)}) collective-permute-start(bf16[2560,256]{1,0:T(8,128)(2,1)} %get-tuple-element.28.w_o), channel_id=1, source_target_pairs={{0,4},{4,0},{8,12},{12,8},{16,20},{20,16},{24,28},{28,24},{1,5},{5... | collective-permute-start | bytes 3932168 | tf_op jit(solution)/shard_map/ppermute | solution.py:217
  102.1 11.4 %collective-permute-start.21 = (bf16[2,320,256]{2,1,0:T(8,128)(2,1)}, bf16[2,320,256]{2,1,0:T(8,128)(2,1)S(1)}, u32[]{:S(2)}, u32[]{:S(2)}) collective-permute-start(bf16[2,320,256]{2,1,0:T(8,128)(2,1)} %get-tuple-element.26), channel_id=1, source_target_pairs={{0,8},{4,12},{24,16},{28,20},{1,9},{5,13},{25,17},{29,21},{2,10},{... | collective-permute-start | bytes 983048 | tf_op jit(solution)/shard_map/ppermute | solution.py:209
  105.7 9.7 %collective-permute-start.20 = (bf16[2,320,256]{2,1,0:T(8,128)(2,1)}, bf16[2,320,256]{2,1,0:T(8,128)(2,1)S(1)}, u32[]{:S(2)}, u32[]{:S(2)}) collective-permute-start(bf16[2,320,256]{2,1,0:T(8,128)(2,1)} %copy-done.18), channel_id=1, source_target_pairs={{8,16},{12,20},{16,8},{20,12},{9,17},{13,21},{17,9},{21,13},{10,18... | collective-permute-start | bytes 983048 | tf_op jit(solution)/shard_map/ppermute | solution.py:209
  118.2 10.8 %copy-start.2 = (bf16[2,2,128,2560]{3,2,1,0:T(8,128)(2,1)S(1)}, bf16[2,2,128,2560]{3,2,1,0:T(8,128)(2,1)}, u32[]{:S(2)}) copy-start(bf16[2,2,128,2560]{3,2,1,0:T(8,128)(2,1)} %param.5) | copy-start | bytes 7864324
  118.2 10.8 %copy-start.6 = (bf16[256,1024]{1,0:T(8,128)(2,1)S(1)}, bf16[256,1024]{1,0:T(8,128)(2,1)}, u32[]{:S(2)}) copy-start(bf16[256,1024]{1,0:T(8,128)(2,1)} %copy-done.5) | copy-start | bytes 1572868
  118.2 1.1 copy-start.14
  119.3 1.6 copy-start.15
  124.6 24.9 %collective-permute-start.16 = (bf16[2,256,640]{2,1,0:T(8,128)(2,1)S(1)}, bf16[2,256,640]{2,1,0:T(8,128)(2,1)S(1)}, u32[]{:S(2)}, u32[]{:S(2)}) collective-permute-start(bf16[2,256,640]{2,1,0:T(8,128)(2,1)S(1)} %get-tuple-element.30), channel_id=1, source_target_pairs={{0,1},{1,0},{2,3},{3,2},{4,5},{5,4},{6,7},{7,6},{8,9},{9,8},{10,11... | collective-permute-start | bytes 1966088 | tf_op jit(solution)/shard_map/ppermute | solution.py:220
  127.4 16.0 %collective-permute-start.18 = (bf16[2,256,640]{2,1,0:T(8,128)(2,1)S(1)}, bf16[2,256,640]{2,1,0:T(8,128)(2,1)S(1)}, u32[]{:S(2)}, u32[]{:S(2)}) collective-permute-start(bf16[2,256,640]{2,1,0:T(8,128)(2,1)S(1)} %get-tuple-element.31), channel_id=1, source_target_pairs={{0,2},{1,3},{2,0},{3,1},{4,6},{5,7},{6,4},{7,5},{8,10},{9,11},{10,... | collective-permute-start | bytes 1966088 | tf_op jit(solution)/shard_map/ppermute | solution.py:220
  129.0 23.9 %copy-start.12 = (bf16[2,320,256]{2,1,0:T(8,128)(2,1)S(1)}, bf16[2,320,256]{2,1,0:T(8,128)(2,1)}, u32[]{:S(2)}) copy-start(bf16[2,320,256]{2,1,0:T(8,128)(2,1)} %copy-done.11) | copy-start | bytes 983044
  133.5 17.9 %collective-permute-start.24 = (bf16[2,320,256]{2,1,0:T(8,128)(2,1)S(1)}, bf16[2,320,256]{2,1,0:T(8,128)(2,1)S(1)}, u32[]{:S(2)}, u32[]{:S(2)}) collective-permute-start(bf16[2,320,256]{2,1,0:T(8,128)(2,1)S(1)} %get-tuple-element.35), channel_id=1, source_target_pairs={{0,8},{4,12},{24,16},{28,20},{1,9},{5,13},{25,17},{29,21},{2,10},{... | collective-permute-start | bytes 983048 | tf_op jit(solution)/shard_map/ppermute | solution.py:209
  137.8 14.4 %collective-permute-start.28 = (bf16[2,320,256]{2,1,0:T(8,128)(2,1)S(1)}, bf16[2,320,256]{2,1,0:T(8,128)(2,1)S(1)}, u32[]{:S(2)}, u32[]{:S(2)}) collective-permute-start(bf16[2,320,256]{2,1,0:T(8,128)(2,1)S(1)} %add_convert_fusion.3), channel_id=1, source_target_pairs={{8,16},{12,20},{16,8},{20,12},{9,17},{13,21},{17,9},{21,13},{10,18... | collective-permute-start | bytes 983048 | tf_op jit(solution)/shard_map/ppermute | solution.py:209
  138.5 14.5 %collective-permute-start.29 = (bf16[2,320,256]{2,1,0:T(8,128)(2,1)S(1)}, bf16[2,320,256]{2,1,0:T(8,128)(2,1)S(1)}, u32[]{:S(2)}, u32[]{:S(2)}) collective-permute-start(bf16[2,320,256]{2,1,0:T(8,128)(2,1)S(1)} %add_convert_fusion.4), channel_id=1, source_target_pairs={{0,8},{4,12},{8,0},{12,4},{16,24},{20,28},{24,16},{28,20},{1,9},{5... | collective-permute-start | bytes 983048 | tf_op jit(solution)/shard_map/ppermute | solution.py:209
  143.4 14.5 %collective-permute-start.22 = (bf16[2,320,256]{2,1,0:T(8,128)(2,1)S(1)}, bf16[2,320,256]{2,1,0:T(8,128)(2,1)S(1)}, u32[]{:S(2)}, u32[]{:S(2)}) collective-permute-start(bf16[2,320,256]{2,1,0:T(8,128)(2,1)S(1)} %get-tuple-element.36), channel_id=1, source_target_pairs={{0,8},{4,12},{24,16},{28,20},{1,9},{5,13},{25,17},{29,21},{2,10},{... | collective-permute-start | bytes 983048 | tf_op jit(solution)/shard_map/ppermute | solution.py:209
  151.5 7.2 %collective-permute-start.25 = (bf16[2,320,256]{2,1,0:T(8,128)(2,1)S(1)}, bf16[2,320,256]{2,1,0:T(8,128)(2,1)S(1)}, u32[]{:S(2)}, u32[]{:S(2)}) collective-permute-start(bf16[2,320,256]{2,1,0:T(8,128)(2,1)S(1)} %fusion.9), channel_id=1, source_target_pairs={{8,16},{12,20},{16,8},{20,12},{9,17},{13,21},{17,9},{21,13},{10,18... | collective-permute-start | bytes 983048 | tf_op jit(solution)/shard_map/ppermute | solution.py:209
  158.0 7.5 %collective-permute-start.23 = (bf16[2,320,256]{2,1,0:T(8,128)(2,1)S(1)}, bf16[2,320,256]{2,1,0:T(8,128)(2,1)S(1)}, u32[]{:S(2)}, u32[]{:S(2)}) collective-permute-start(bf16[2,320,256]{2,1,0:T(8,128)(2,1)S(1)} %add_convert_fusion.2), channel_id=1, source_target_pairs={{8,16},{12,20},{16,8},{20,12},{9,17},{13,21},{17,9},{21,13},{10,18... | collective-permute-start | bytes 983048 | tf_op jit(solution)/shard_map/ppermute | solution.py:209
  158.8 10.6 %collective-permute-start.26 = (bf16[2,320,256]{2,1,0:T(8,128)(2,1)S(1)}, bf16[2,320,256]{2,1,0:T(8,128)(2,1)S(1)}, u32[]{:S(2)}, u32[]{:S(2)}) collective-permute-start(bf16[2,320,256]{2,1,0:T(8,128)(2,1)S(1)} %add_convert_fusion), channel_id=1, source_target_pairs={{0,8},{4,12},{8,0},{12,4},{16,24},{20,28},{24,16},{28,20},{1,9},{5... | collective-permute-start | bytes 983048 | tf_op jit(solution)/shard_map/ppermute | solution.py:209
  163.8 12.1 %collective-permute-start.30 = (f32[320,256]{1,0:T(8,128)S(1)}, f32[320,256]{1,0:T(8,128)S(1)}, u32[]{:S(2)}, u32[]{:S(2)}) collective-permute-start(f32[320,256]{1,0:T(8,128)S(1)} %slice_bitcast_fusion), channel_id=1, source_target_pairs={{0,4},{4,0},{8,12},{12,8},{16,20},{20,16},{24,28},{28,24},{1,5},{5... | collective-permute-start | bytes 983048 | tf_op jit(solution)/shard_map/ppermute | solution.py:217
  164.4 10.2 %collective-permute-start.17 = (bf16[256,640]{1,0:T(8,128)(2,1)S(1)}, bf16[256,640]{1,0:T(8,128)(2,1)S(1)}, u32[]{:S(2)}, u32[]{:S(2)}) collective-permute-start(bf16[256,640]{1,0:T(8,128)(2,1)S(1)} %get-tuple-element.41), channel_id=1, source_target_pairs={{0,2},{1,3},{2,0},{3,1},{4,6},{5,7},{6,4},{7,5},{8,10},{9,11},{10,... | collective-permute-start | bytes 983048 | tf_op jit(solution)/shard_map/ppermute | solution.py:220
  164.9 9.8 %collective-permute-start.19 = (bf16[256,640]{1,0:T(8,128)(2,1)S(1)}, bf16[256,640]{1,0:T(8,128)(2,1)S(1)}, u32[]{:S(2)}, u32[]{:S(2)}) collective-permute-start(bf16[256,640]{1,0:T(8,128)(2,1)S(1)} %get-tuple-element.42), channel_id=1, source_target_pairs={{0,1},{1,0},{2,3},{3,2},{4,5},{5,4},{6,7},{7,6},{8,9},{9,8},{10,11... | collective-permute-start | bytes 983048 | tf_op jit(solution)/shard_map/ppermute | solution.py:220
  169.6 6.3 %collective-permute-start.27 = (f32[320,256]{1,0:T(8,128)S(1)}, f32[320,256]{1,0:T(8,128)S(1)}, u32[]{:S(2)}, u32[]{:S(2)}) collective-permute-start(f32[320,256]{1,0:T(8,128)S(1)} %slice_bitcast_fusion.2), channel_id=1, source_target_pairs={{0,4},{4,0},{8,12},{12,8},{16,20},{20,16},{24,28},{28,24},{1,5},{5... | collective-permute-start | bytes 983048 | tf_op jit(solution)/shard_map/ppermute | solution.py:217

commit v8 on v7

--- a/solution.py
+++ b/solution.py
@@ -11,7 +11,7 @@
 HEAD_DIM = 64
 F32 = jnp.float32
 BF16 = jnp.bfloat16
-VMEM_LIMIT = 20 * 1024 * 1024
+VMEM_LIMIT = 40 * 1024 * 1024
 
 
 def dot(a, b, ca=1, cb=0):
@@ -33,13 +33,10 @@
     core = idx[0]
     for j, slot in enumerate(slots):
         depth = slot.shape[1]
-
-        @pl.when(idx[2 + 2 * j] == 1)
-        def _(slot=slot, depth=depth, plane=idx[1 + 2 * j]):
-            mine, other = slot[0], slot[1]
-            low = jnp.where(core == 0, mine, other)
-            high = jnp.where(core == 0, other, mine)
-            w_ref[rows_at(plane, 2 * depth), :] = jnp.concatenate([low, high], axis=0)
+        mine, other = slot[0], slot[1]
+        low = jnp.where(core == 0, mine, other)
+        high = jnp.where(core == 0, other, mine)
+        w_ref[rows_at(idx[1 + j], 2 * depth), :] = jnp.concatenate([low, high], axis=0)
 
 
 def hand_out(idx, base, grad_v, outs):
@@ -63,14 +60,19 @@
     return [(h, min(2, heads - h)) for h in range(0, heads, 2)]
 
 
-def d_value_kernel(n_slots, idx, cot_o, cot_s, mix_o, mix_s, *rest):
-    slots, (w_out, left_v, cot_v, mix_v, sems) = rest[:n_slots], rest[n_slots:]
+def backward_kernel(n_slots, idx, unread, token, cot_o, cot_s, mix_o, mix_s, act_o, act_s, *rest):
+    del unread, token
+    slots, rest = rest[:n_slots], rest[n_slots:]
+    w_out, rest = rest[0], rest[1:]
+    outs, (cot_v, act_v, mix_v, left_v, grad_v, sems) = rest[:-6], rest[-6:]
+    tokens, cols = cot_o.shape[0], w_out.shape[1]
     groups, _, seq, _ = mix_o.shape
     heads = mix_v.shape[2]
     here = pl.ds(idx[0] * heads, heads)
     copies = begin(
         [(cot_o, cot_v.at[0]), (mix_o.at[:, here], mix_v.at[0])]
-        + [(cot_s, cot_v.at[1]), (mix_s.at[:, here], mix_v.at[1])],
+        + [(cot_s, cot_v.at[1]), (mix_s.at[:, here], mix_v.at[1])]
+        + [(act_o, act_v.at[pl.ds(0, tokens)]), (act_s, act_v.at[pl.ds(tokens, tokens)])],
         sems,
     )
     place(idx, slots, w_out)
@@ -97,18 +99,9 @@
                 left_v[h * HEAD_DIM : (h + n) * HEAD_DIM, at : at + seq] = dot(
                     part, weights
                 ).astype(BF16)
-
-
-def gradient_kernel(idx, right_o, right_s, left_ref, *rest):
-    outs, (right_v, grad_v, sems) = rest[:-3], rest[-3:]
-    tokens, _ = right_o.shape
-    copies = begin(
-        [(right_o, right_v.at[pl.ds(0, tokens)]), (right_s, right_v.at[pl.ds(tokens, tokens)])],
-        sems,
-    )
-    copies[0].wait()
-    copies[1].wait()
-    gradient_rows(left_ref[...], right_v, grad_v, 640)
+    copies[4].wait()
+    copies[5].wait()
+    gradient_rows(left_v[...], act_v, grad_v, 640)
     hand_out(idx, 1, grad_v, outs)
 
 
@@ -147,8 +140,10 @@
                 ).astype(BF16)
 
 
-def grad_out_kernel(idx, cot_o, cot_s, mixed_o, mixed_s, *rest):
+def grad_out_kernel(idx, cot_o, cot_s, mixed_o, mixed_s, unread, token, *rest):
+    del unread
     outs, (cot_v, left_v, grad_v, sems) = rest[:-4], rest[-4:]
+    token[...] = jnp.zeros_like(token)
     tokens, _ = cot_o.shape
     copies = begin(
         [(cot_o, cot_v.at[pl.ds(0, tokens)]), (cot_s, cot_v.at[pl.ds(tokens, tokens)])], sems
@@ -161,7 +156,13 @@
     hand_out(idx, 1, grad_v, outs)
 
 
-def terms_kernel(n_node, idx, mixed_o, mixed_r, w_o, w_r, *outs):
+def sum_kernel(token, block, got, out):
+    del token
+    out[...] = (block[...].astype(F32) + got[...].astype(F32)).astype(BF16)
+
+
+def terms_kernel(n_node, idx, mixed_o, mixed_r, w_o, w_r, token, *outs):
+    token[...] = jnp.zeros_like(token)
     depth = w_o.shape[0] // n_node
     half = mixed_o.shape[0] // 2
     for j in range(n_node):
@@ -183,7 +184,7 @@
             along_x[1], along_y[1] = first, second
 
 
-ANY = pl.BlockSpec(memory_space=pltpu.HBM)
+ANY = pl.BlockSpec(memory_space=pl.ANY)
 SMEM = pl.BlockSpec(memory_space=pltpu.SMEM)
 VMEM = pl.BlockSpec(memory_space=pltpu.VMEM)
 
@@ -210,8 +211,8 @@
             x, "wide", [(2 * s + c, 2 * d + c) for s, d in pairs for c in range(2)]
         )
 
-    outer, middle = [(0, 1), (1, 0), (2, 3), (3, 2)], [(1, 2), (2, 1)]
-    outward, inward = [(1, 0), (2, 3)], [(0, 1), (3, 2)]
+    def swap(x, j):
+        return move(x, [(s, s ^ j) for s in range(planes)])
 
     def sibling(x):
         return lax.ppermute(x, "wide", [(i, i ^ 1) for i in range(n_wide)])
@@ -219,49 +220,40 @@
     def flip(x, j):
         return lax.ppermute(x, "node", [(i, i ^ j) for i in range(n_node)])
 
-    def swap_halves(weights, c):
-        cols = weights[0].shape[1] // 2
-        low = jnp.stack([w[:, :cols] for w in weights])
-        high = jnp.stack([w[:, cols:] for w in weights])
+    def swap_cores(w_out, w_value, act, mix, cot, c):
+        cols = w_out.shape[1] // 2
+        low = jnp.stack([w_out[:, :cols], w_value[:, :cols]])
+        high = jnp.stack([w_out[:, cols:], w_value[:, cols:]])
         got = sibling(jnp.where(c == 0, high, low))
+        got, act, mix, cot = lax.optimization_barrier((got, act, mix, cot))
         mine = jnp.where(c == 0, low, high)
-        return got, [jnp.stack([mine[i], got[i]]) for i in range(len(weights))]
+        u_out, u_value = (jnp.stack([mine[i], got[i]]) for i in range(2))
+        return u_out, u_value, sibling(act), sibling(mix), sibling(cot)
 
     def gather_ring(u):
         return [u] + [
             move(u, [(s, (s - j) % planes) for s in range(planes)]) for j in range(1, planes)
         ]
 
-    def slot_planes(z):
-        if not line4:
-            return [x for j in range(planes) for x in (lax.rem(z + j, planes), 1)]
-        beside = lax.bitwise_xor(z, 1)
-        inside = (z == 1) | (z == 2)
-        found = [z, 1, beside, 1, 3 - z, inside, 3 - beside, inside]
-        return found + [3 - beside, ~inside, 3 - z, ~inside]
-
-    def send_planes(z):
-        if not line4:
-            return [lax.rem(z + j, planes) for j in range(planes)]
-        beside = lax.bitwise_xor(z, 1)
-        return [z, beside, 3 - z, 3 - beside]
+    def planes_of(z):
+        if line4:
+            return [lax.bitwise_xor(z, jnp.int32(j)) for j in range(4)]
+        return [lax.rem(z + j, planes) for j in range(planes)]
 
     def added(block, got):
         return (block.astype(F32) + got.astype(F32)).astype(BF16)
 
-    def hold(x, *others):
-        for y in others:
-            x = jnp.where(jnp.isnan(y[(0,) * y.ndim]), jnp.zeros_like(x), x)
-        return x
-
-    def scatter_first(blocks, first):
-        return added(blocks[3], first), move(blocks[3], inward)
-
-    def scatter_sums(blocks, second, crossed):
-        return added(blocks[2], second), added(blocks[1], crossed)
-
-    def scatter_last(sums):
-        return move(sums[0], middle), move(sums[1], outer)
+    def gather(u):
+        if not line4:
+            return gather_ring(u)
+        far = swap(u, 2)
+        return [u, swap(u, 1), far, swap(far, 1)]
+
+    def scatter(blocks, passed, c, add=added):
+        if not line4:
+            return scatter_ring(blocks, c)
+        far = swap(add(blocks[2], passed), 2)
+        return scatter_end(blocks[0], (swap(blocks[1], 1), far), c)
 
     def scatter_end(own, got, c):
         total = own.astype(F32)
@@ -296,16 +288,11 @@
         mix = mixing.reshape(groups, 2 * heads, seq, seq)
         flops = 4 * tokens * width * cols
 
-        got, (u_out, u_value) = swap_halves([w_out, w_value], c)
-        act_s, mix_s, cot_s = (
-            sibling(lax.optimization_barrier((x, got))[0]) for x in (act, mix, cot)
-        )
-
-        info = slot_planes(z)
-        sends = send_planes(z)
+        u_out, u_value, act_s, mix_s, cot_s = swap_cores(w_out, w_value, act, mix, cot, c)
+        value_slots, out_slots = gather(u_value), gather(u_out)
+        n_slots = len(out_slots)
         pack = lambda *values: jnp.stack([jnp.int32(x) for x in values])
-        idx_slots = pack(c, *info)
-        idx_send = pack(c, *sends)
+        idx = pack(c, *planes_of(z))
         idx_node = pack(*[lax.bitwise_xor(n, jnp.int32(j)) for j in range(n_node)])
 
         mix_scratch = pltpu.VMEM((2, groups, heads, seq, seq), BF16)
@@ -314,23 +301,7 @@
         left_tokens = pltpu.VMEM((cols, 2 * tokens), BF16)
         rows = pltpu.VMEM((width, cols), BF16)
         block = (2, depth // 2, cols)
-        send_shapes = [block] * len(sends)
-
-        if line4:
-            v_outer, v_middle = move(u_value, outer), move(u_value, middle)
-            v_cross = move(v_outer, middle)
-            v_out = move(v_middle, outward)
-            v_last = move(v_cross, outward)
-            value_slots = [u_value, v_outer, v_middle, v_cross, v_out, v_last]
-            swaps = act_s, mix_s, cot_s
-            o_outer = move(hold(u_out, v_out, *swaps), outer)
-            o_middle = move(hold(u_out, v_cross, *swaps), middle)
-            o_cross = move(o_outer, middle)
-            o_out = move(o_middle, outward)
-        else:
-            value_slots = gather_ring(u_value)
-            out_slots = gather_ring(u_out)
-        n_slots = len(value_slots)
+        send_shapes = [block] * n_slots
 
         mixed_o, mixed_s = call(
             functools.partial(mixed_kernel, n_slots),
@@ -339,65 +310,48 @@
             [(tokens, cols)] * 2,
             [rows, halves, mix_scratch, pltpu.SemaphoreType.DMA((4,))],
             flops,
-        )(idx_slots, act, act_s, mix, mix_s, *value_slots)
+        )(idx, act, act_s, mix, mix_s, *value_slots)
         mixed_r = sibling(mixed_s)
-        idx_out = hold(idx_send, o_outer, o_middle, mixed_r) if line4 else idx_send
-        out_sends = call(
+        token, *out_sends = call(
             grad_out_kernel,
             "grad_out",
-            [SMEM] + [ANY] * 2 + [VMEM] * 2,
-            send_shapes,
+            [SMEM] + [ANY] * 2 + [VMEM] * 2 + [ANY],
+            [(16, 128)] + send_shapes,
             [both, left_tokens, rows, pltpu.SemaphoreType.DMA((2,))],
             flops,
-        )(idx_out, cot, cot_s, mixed_o, mixed_s)
-        if line4:
-            inside = (z == 1) | (z == 2)
-            swapped = move(hold(jnp.where(inside, o_cross, out_sends[2]), o_out), outer)
-            out_slots = [u_out, o_outer, o_middle, o_cross, o_out, swapped]
-            out_crossing, out_second = scatter_first(out_sends, swapped)
-            out_crossed = move(out_crossing, middle)
-            idx_value = hold(idx_slots, out_crossing)
-        else:
-            idx_value = idx_slots
-        w_full, left = call(
-            functools.partial(d_value_kernel, n_slots),
-            "d_value",
-            [SMEM] + [ANY] * 4 + [VMEM] * n_slots,
-            [(width, cols), (cols, 2 * tokens)],
-            [halves, mix_scratch, pltpu.SemaphoreType.DMA((4,))],
-            flops,
-        )(idx_value, cot, cot_s, mix, mix_s, *out_slots)
+        )(idx, cot, cot_s, mixed_o, mixed_s, mixed_r)
+        out_passed = swap(out_sends[3], 1) if line4 else token
+        grad_out = scatter(out_sends, out_passed, c)
+        w_full, *back_sends = call(
+            functools.partial(backward_kernel, n_slots),
+            "backward",
+            [SMEM, ANY, VMEM] + [ANY] * 6 + [VMEM] * n_slots,
+            [(width, cols)] + send_shapes,
+            [halves, both, mix_scratch, left_tokens, rows, pltpu.SemaphoreType.DMA((6,))],
+            2 * flops,
+        )(idx, out_passed, token, cot, cot_s, mix, mix_s, act, act_s, *out_slots)
         w_full_s = sibling(w_full)
+        back_passed = swap(back_sends[3], 1) if line4 else token
+
         part = width // n_node
         half = tokens // 2
         if n_node == 4:
             term_shapes = [(2, half, part), (2, half, part), (4, half, part)]
         else:
             term_shapes = [(tokens, part)] * n_node
-        terms = call(
+        token, *terms = call(
             functools.partial(terms_kernel, n_node),
             "terms",
             [SMEM] + [VMEM] * 4,
-            term_shapes,
+            [(16, 128)] + term_shapes,
             [],
             flops,
         )(idx_node, mixed_o, mixed_r, w_full, w_full_s)
 
-        if line4:
-            out_sums = scatter_sums(out_sends, out_second, out_crossed)
-            out_got = scatter_last(out_sums)
-            idx_back = hold(idx_send, *out_sums, terms[0])
-        else:
-            idx_back = idx_send
-        back_sends = call(
-            gradient_kernel,
-            "grad_value",
-            [SMEM] + [ANY] * 2 + [VMEM],
-            send_shapes,
-            [both, rows, pltpu.SemaphoreType.DMA((2,))],
-            flops,
-        )(idx_back, act, act_s, left)
-
+        def add_after_terms(a, b):
+            return call(sum_kernel, "sum", [VMEM] * 3, [block], [], 0)(token, a, b)[0]
+
+        grad_value = scatter(back_sends, back_passed, c, add_after_terms)
         if n_node == 4:
             along_x, along_y, kept = terms
             kept = kept.astype(F32)
@@ -405,7 +359,6 @@
             got_y = flip(along_y, 2).astype(F32)
             last_y = flip((kept[1] + got_x[1]).astype(BF16), 2)
             last_x = flip((kept[3] + got_y[1]).astype(BF16), 1)
-            early = got_x, got_y
             layer_out = jnp.concatenate(
                 [
                     kept[0] + got_x[0] + last_y.astype(F32),
@@ -414,20 +367,10 @@
                 axis=0,
             )
         else:
-            early, layer_out = terms, terms[0].astype(F32)
+            layer_out = terms[0].astype(F32)
             for j in range(1, n_node):
                 layer_out = layer_out + flip(terms[j], j).astype(F32)
         layer_out = layer_out.astype(BF16).reshape(micro, images, seq, part)
-        if line4:
-            first = move(back_sends[2], inward)
-            crossing, second = scatter_first(back_sends, first)
-            crossed = move(hold(crossing, *early), middle)
-            got = scatter_last(scatter_sums(back_sends, second, crossed))
-            grad_value = scatter_end(back_sends[0], got, c)
-            grad_out = scatter_end(out_sends[0], out_got, c)
-        else:
-            grad_value = scatter_ring(back_sends, c)
-            grad_out = scatter_ring(out_sends, c)
         return layer_out, grad_value, grad_out
 
     return body

time: 179 us -> 134 us (0.75)
  waiting for transfers between devices: 52.4 us -> 76.3 us
  starting transfers between devices: 45.3 us -> 24.5 us
  local copies, waits for them, and re-layouts: 25.7 us -> 5.24 us
  between operations: 20.7 us -> 0.91 us
  Pallas kernels: 25.3 us -> 21.5 us
  other arithmetic: 8.43 us -> 5.69 us
    ppermute x19 -> x12, waiting for transfers between devices: 41.3 us -> 68.6 us  [move(): lax.ppermute(x, 'wide', [(2 * s + c, 2 * d + c) for s, d in pairs for c i...]
    ppermute x19 -> x12, starting transfers between devices: 39.4 us -> 16.8 us  [move(): lax.ppermute(x, 'wide', [(2 * s + c, 2 * d + c) for s, d in pairs for c i...]
    slice x17 -> x2, local copies, waits for them, and re-layouts: 13.2 us -> 0.71 us  [swap_cores(): u_out, u_value = (jnp.stack([mine[i], got[i]]) for i in range(2))]
    unnamed x38 -> x18, local copies, waits for them, and re-layouts: 10.1 us -> 2.21 us
    pallas_call x3, Pallas kernels: 16.1 us -> 13.1 us  [the longest x1 7.7 us: body(): call(functools.partial(backward_kernel, n_slots), 'backward', [SMEM, ANY,...]
    ppermute x4, waiting for transfers between devices: 8.23 us -> 6.4 us  [flip(): return lax.ppermute(x, 'node', [(i, i ^ j) for i in range(n_node)])]
  transfers between devices with their start and end apart: 31 -> 24, of which waited for: 13 -> 11; matrix products, arithmetic and copies ran while one was open for 9% -> 4% of each run, Pallas kernels for 9% -> 10%
where the time goes in v8:
time: 134 us
  waiting for transfers between devices  76.3 us (57%)
  starting transfers between devices  24.5 us (18%)
  Pallas kernels  21.5 us (16%)
  other arithmetic  5.69 us (4%)
  local copies, waits for them, and re-layouts  5.24 us (4%)
    ppermute x12, waiting for transfers between devices, move(): lax.ppermute(x, 'wide', [(2 * s + c, 2 * d + c) for s, d in pairs for c i...  68.6 us
    ppermute x12, starting transfers between devices, move(): lax.ppermute(x, 'wide', [(2 * s + c, 2 * d + c) for s, d in pairs for c i...  16.8 us
    pallas_call x1, Pallas kernels, body(): call(functools.partial(backward_kernel, n_slots), 'backward', [SMEM, ANY,...  7.7 us
    ppermute x4, waiting for transfers between devices, flip(): return lax.ppermute(x, 'node', [(i, i ^ j) for i in range(n_node)])  6.4 us
    ppermute x4, starting transfers between devices, flip(): return lax.ppermute(x, 'node', [(i, i ^ j) for i in range(n_node)])  5.96 us
    pallas_call x1, Pallas kernels, body(): call(grad_out_kernel, 'grad_out', [SMEM] + [ANY] * 2 + [VMEM] * 2 + [ANY]...  5.29 us
    pallas_call x1, Pallas kernels, body(): call(functools.partial(mixed_kernel, n_slots), 'mixed', [SMEM] + [ANY] *...  5.22 us
    pallas_call x1, Pallas kernels, body(): call(functools.partial(terms_kernel, n_node), 'terms', [SMEM] + [VMEM] *...  3.16 us
  transfers between devices with their start and end apart: 24, of which 11 were waited for; matrix products, arithmetic and copies ran while one was open for 4% of the time, Pallas kernels for 10%

profile of v8, /device:TPU:0, one launch (start us, length us, event | category | flops | bytes accessed | tf_op | source)
XLA Modules:
  0.0 134.0 jit_solution(2165171594954559929)
XLA Ops:
  0.6 1.2 slice_bitcast_fusion.6
  1.8 1.0 slice_bitcast_fusion.7
  2.8 0.1 broadcast_select_fusion
  2.9 0.5 collective-permute-start
  3.4 1.3 collective-permute-done
  4.7 0.4 collective-permute-start.1
  5.1 0.1 collective-permute-start.7
  5.2 0.4 collective-permute-start.2
  5.6 0.7 fusion.15
  6.3 3.8 %collective-permute-start.4 = (bf16[2,320,256]{2,1,0:T(8,128)(2,1)S(1)}, bf16[2,320,256]{2,1,0:T(8,128)(2,1)S(1)}, u32[]{:S(2)}, u32[]{:S(2)}) collective-permute-start(bf16[2,320,256]{2,1,0:T(8,128)(2,1)S(1)} %pad_maximum_fusion.5.rest_0_), channel_id=1, source_target_pairs={{0,16},{4,20},{8,24},{12,28},{16,0},{20,4},{24,8},{28,12},{1,17},{... | collective-permute-start | bytes 983048 | tf_op jit(solution)/shard_map/ppermute | solution.py:210
  10.1 1.6 %collective-permute-start.3 = (bf16[2,320,256]{2,1,0:T(8,128)(2,1)S(1)}, bf16[2,320,256]{2,1,0:T(8,128)(2,1)}, u32[]{:S(2)}, u32[]{:S(2)}) collective-permute-start(bf16[2,320,256]{2,1,0:T(8,128)(2,1)S(1)} %pad_maximum_fusion.5.rest_0_), channel_id=1, source_target_pairs={{0,8},{4,12},{8,0},{12,4},{16,24},{20,28},{24,16},{28,20},{1,9},{5... | collective-permute-start | bytes 983048 | tf_op jit(solution)/shard_map/ppermute | solution.py:210
  11.7 13.8 %collective-permute-done.4.rest_2_ = bf16[2,320,256]{2,1,0:T(8,128)(2,1)S(1)} collective-permute-done((bf16[2,320,256]{2,1,0:T(8,128)(2,1)S(1)}, bf16[2,320,256]{2,1,0:T(8,128)(2,1)S(1)}, u32[]{:S(2)}, u32[]{:S(2)}) %collective-permute-start.4) | collective-permute-done | bytes 327712 | tf_op jit(solution)/shard_map/ppermute | solution.py:210
  25.5 0.6 collective-permute-start.5
  26.1 0.1 stack.67.idx
  26.2 0.9 pad_maximum_fusion.6.rest_0_
  27.2 0.0 copy-start.1
  27.2 3.4 %collective-permute-start.10 = (bf16[2,320,256]{2,1,0:T(8,128)(2,1)S(1)}, bf16[2,320,256]{2,1,0:T(8,128)(2,1)S(1)}, u32[]{:S(2)}, u32[]{:S(2)}) collective-permute-start(bf16[2,320,256]{2,1,0:T(8,128)(2,1)S(1)} %pad_maximum_fusion.6.rest_0_), channel_id=1, source_target_pairs={{0,16},{4,20},{8,24},{12,28},{16,0},{20,4},{24,8},{28,12},{1,17},{... | collective-permute-start | bytes 983048 | tf_op jit(solution)/shard_map/ppermute | solution.py:210
  30.6 10.0 %collective-permute-done.5.rest_3_ = bf16[2,320,256]{2,1,0:T(8,128)(2,1)} collective-permute-done((bf16[2,320,256]{2,1,0:T(8,128)(2,1)S(1)}, bf16[2,320,256]{2,1,0:T(8,128)(2,1)}, u32[]{:S(2)}, u32[]{:S(2)}) %collective-permute-start.5) | collective-permute-done | bytes 327712 | tf_op jit(solution)/shard_map/ppermute | solution.py:210
  40.6 1.2 copy-done.2
  41.8 5.2 %mixed.1 = (bf16[512,256]{1,0:T(8,128)(2,1)S(1)}, bf16[512,256]{1,0:T(8,128)(2,1)S(1)}) custom-call(s32[5]{0:T(128)S(1)} %stack.67.idx, bf16[512,2560]{1,0:T(8,128)(2,1)S(1)} %bitcast.54, bf16[512,2560]{1,0:T(8,128)(2,1)} %collective-permute-done.1.act_s, bf16[4,8,128,128]{3,2,1,0:T(8,128)(2,1)S(1)} %bitcast.60, ...), custom_call_target="tpu_custom_call" | custom-call | flops 1342177280 | bytes 12582912 | tf_op jit(solution)/shard_map/mixed/pallas_call | solution.py:306
  47.1 0.1 collective-permute-start.6
  47.2 0.1 collective-permute-start.9
  47.2 2.0 %collective-permute-start.11 = (bf16[2,320,256]{2,1,0:T(8,128)(2,1)S(1)}, bf16[2,320,256]{2,1,0:T(8,128)(2,1)S(1)}, u32[]{:S(2)}, u32[]{:S(2)}) collective-permute-start(bf16[2,320,256]{2,1,0:T(8,128)(2,1)S(1)} %collective-permute-done.10.rest_2_), channel_id=1, source_target_pairs={{0,8},{4,12},{8,0},{12,4},{16,24},{20,28},{24,16},{28,20},{1,9},{5... | collective-permute-start | bytes 983048 | tf_op jit(solution)/shard_map/ppermute | solution.py:210
  49.3 0.0 copy-start.3
  49.3 5.3 %grad_out.1 = (bf16[16,128]{1,0:T(8,128)(2,1)S(1)}, bf16[2,320,256]{2,1,0:T(8,128)(2,1)S(1)}, bf16[2,320,256]{2,1,0:T(8,128)(2,1)}, bf16[2,320,256]{2,1,0:T(8,128)(2,1)S(1)}, bf16[2,320,256]{2,1,0:T(8,128)(2,1)S(1)}) custom-call(s32[5]{0:T(128)S(1)} %stack.67.idx, bf16[512,2560]{1,0:T(8,128)(2,1)S(1)} %bitcast.57, ...), custom_call_target="tpu_custom_call" | custom-call | flops 1342177280 | bytes 12582912 | tf_op jit(solution)/shard_map/grad_out/pallas_call | solution.py:315
  54.6 0.2 collective-permute-start.8
  54.8 3.0 %collective-permute-done.9.rest_1_ = bf16[2,320,256]{2,1,0:T(8,128)(2,1)S(1)} collective-permute-done((bf16[2,320,256]{2,1,0:T(8,128)(2,1)S(1)}, bf16[2,320,256]{2,1,0:T(8,128)(2,1)S(1)}, u32[]{:S(2)}, u32[]{:S(2)}) %collective-permute-start.9) | collective-permute-done | bytes 327712 | tf_op jit(solution)/shard_map/ppermute | solution.py:210
  57.7 7.0 %collective-permute-done.11.rest_3_ = bf16[2,320,256]{2,1,0:T(8,128)(2,1)S(1)} collective-permute-done((bf16[2,320,256]{2,1,0:T(8,128)(2,1)S(1)}, bf16[2,320,256]{2,1,0:T(8,128)(2,1)S(1)}, u32[]{:S(2)}, u32[]{:S(2)}) %collective-permute-start.11) | collective-permute-done | bytes 327712 | tf_op jit(solution)/shard_map/ppermute | solution.py:210
  64.8 6.6 %collective-permute-done.8.unread = bf16[2,320,256]{2,1,0:T(8,128)(2,1)S(1)} collective-permute-done((bf16[2,320,256]{2,1,0:T(8,128)(2,1)S(1)}, bf16[2,320,256]{2,1,0:T(8,128)(2,1)S(1)}, u32[]{:S(2)}, u32[]{:S(2)}) %collective-permute-start.8) | collective-permute-done | bytes 327712 | tf_op jit(solution)/shard_map/ppermute | solution.py:210
  71.3 7.7 %backward.1 = (bf16[2560,256]{1,0:T(8,128)(2,1)}, bf16[2,320,256]{2,1,0:T(8,128)(2,1)S(1)}, bf16[2,320,256]{2,1,0:T(8,128)(2,1)S(1)}, bf16[2,320,256]{2,1,0:T(8,128)(2,1)S(1)}, bf16[2,320,256]{2,1,0:T(8,128)(2,1)}) custom-call(s32[5]{0:T(128)S(1)} %stack.67.idx, bf16[2,320,256]{2,1,0:T(8,128)(2,1)S(1)} %collective-permute-done.8.unread, ...), custom_call_target="tpu_custom_call" | custom-call | flops 2684354560 | bytes 12582912 | tf_op jit(solution)/shard_map/backward/pallas_call | solution.py:325
  79.0 0.0 copy-start.4
  79.1 0.1 collective-permute-start.12
  79.1 0.3 collective-permute-start.21
  79.5 1.8 %collective-permute-start.18 = (bf16[2,320,256]{2,1,0:T(8,128)(2,1)}, bf16[2,320,256]{2,1,0:T(8,128)(2,1)S(1)}, u32[]{:S(2)}, u32[]{:S(2)}) collective-permute-start(bf16[2,320,256]{2,1,0:T(8,128)(2,1)} %get-tuple-element.39), channel_id=1, source_target_pairs={{0,8},{4,12},{8,0},{12,4},{16,24},{20,28},{24,16},{28,20},{1,9},{5... | collective-permute-start | bytes 983048 | tf_op jit(solution)/shard_map/ppermute | solution.py:210
  81.2 0.8 add_convert_fusion
  82.0 0.9 collective-permute-start.22
  83.0 0.1 pad_add_fusion.idx
  83.0 1.8 %collective-permute-start.17 = (bf16[2,320,256]{2,1,0:T(8,128)(2,1)}, bf16[2,320,256]{2,1,0:T(8,128)(2,1)S(1)}, u32[]{:S(2)}, u32[]{:S(2)}) collective-permute-start(bf16[2,320,256]{2,1,0:T(8,128)(2,1)} %copy-done.8), channel_id=1, source_target_pairs={{0,8},{4,12},{8,0},{12,4},{16,24},{20,28},{24,16},{28,20},{1,9},{5... | collective-permute-start | bytes 983048 | tf_op jit(solution)/shard_map/ppermute | solution.py:210
  84.8 0.9 copy-done.7
  85.8 3.2 %terms.1 = (bf16[16,128]{1,0:T(8,128)(2,1)S(1)}, bf16[2,256,640]{2,1,0:T(8,128)(2,1)S(1)}, bf16[2,256,640]{2,1,0:T(8,128)(2,1)S(1)}, bf16[4,256,640]{2,1,0:T(8,128)(2,1)S(1)}) custom-call(s32[4]{0:T(128)S(1)} %pad_add_fusion.idx, bf16[512,256]{1,0:T(8,128)(2,1)S(1)} %get-tuple-element.26.mixed_o, bf16[512,256]{1,0:T(8,128)(2,1)S(1)} %copy-done.7, ...), custom_call_target="tpu_custom_call" | custom-call | flops 1342177280 | bytes 12582912 | tf_op jit(solution)/shard_map/terms/pallas_call | solution.py:342
  88.9 15.0 %collective-permute-done.18.got = bf16[2,320,256]{2,1,0:T(8,128)(2,1)S(1)} collective-permute-done((bf16[2,320,256]{2,1,0:T(8,128)(2,1)}, bf16[2,320,256]{2,1,0:T(8,128)(2,1)S(1)}, u32[]{:S(2)}, u32[]{:S(2)}) %collective-permute-start.18) | collective-permute-done | bytes 327712 | tf_op jit(solution)/shard_map/ppermute | solution.py:210
  104.0 0.1 sum.1
  104.1 0.4 collective-permute-start.19
  104.4 0.1 convert_add_fusion
  104.5 1.6 %collective-permute-start.13 = (bf16[2,256,640]{2,1,0:T(8,128)(2,1)S(1)}, bf16[2,256,640]{2,1,0:T(8,128)(2,1)S(1)}, u32[]{:S(2)}, u32[]{:S(2)}) collective-permute-start(bf16[2,256,640]{2,1,0:T(8,128)(2,1)S(1)} %get-tuple-element.33), channel_id=1, source_target_pairs={{0,1},{1,0},{2,3},{3,2},{4,5},{5,4},{6,7},{7,6},{8,9},{9,8},{10,11... | collective-permute-start | bytes 1966088 | tf_op jit(solution)/shard_map/ppermute | solution.py:221
  106.1 1.5 %collective-permute-start.15 = (bf16[2,256,640]{2,1,0:T(8,128)(2,1)S(1)}, bf16[2,256,640]{2,1,0:T(8,128)(2,1)S(1)}, u32[]{:S(2)}, u32[]{:S(2)}) collective-permute-start(bf16[2,256,640]{2,1,0:T(8,128)(2,1)S(1)} %get-tuple-element.34), channel_id=1, source_target_pairs={{0,2},{1,3},{2,0},{3,1},{4,6},{5,7},{6,4},{7,5},{8,10},{9,11},{10,... | collective-permute-start | bytes 1966088 | tf_op jit(solution)/shard_map/ppermute | solution.py:221
  107.7 0.1 collective-permute-start.23
  107.7 7.0 %collective-permute-done.17 = bf16[2,320,256]{2,1,0:T(8,128)(2,1)S(1)} collective-permute-done((bf16[2,320,256]{2,1,0:T(8,128)(2,1)}, bf16[2,320,256]{2,1,0:T(8,128)(2,1)S(1)}, u32[]{:S(2)}, u32[]{:S(2)}) %collective-permute-start.17) | collective-permute-done | bytes 327712 | tf_op jit(solution)/shard_map/ppermute | solution.py:210
  114.7 6.2 %collective-permute-done.19 = bf16[2,320,256]{2,1,0:T(8,128)(2,1)S(1)} collective-permute-done((bf16[2,320,256]{2,1,0:T(8,128)(2,1)S(1)}, bf16[2,320,256]{2,1,0:T(8,128)(2,1)S(1)}, u32[]{:S(2)}, u32[]{:S(2)}) %collective-permute-start.19) | collective-permute-done | bytes 327712 | tf_op jit(solution)/shard_map/ppermute | solution.py:210
  120.9 0.1 convert_add_fusion.1
  121.1 0.1 collective-permute-start.20
  121.1 0.2 convert_element_type.59
  121.3 0.1 convert_element_type.60
  121.4 0.1 convert_element_type.64
  121.5 0.1 fusion.8
  121.7 1.5 %collective-permute-start.14 = (bf16[256,640]{1,0:T(8,128)(2,1)S(1)}, bf16[256,640]{1,0:T(8,128)(2,1)S(1)}, u32[]{:S(2)}, u32[]{:S(2)}) collective-permute-start(bf16[256,640]{1,0:T(8,128)(2,1)S(1)} %get-tuple-element.45), channel_id=1, source_target_pairs={{0,2},{1,3},{2,0},{3,1},{4,6},{5,7},{6,4},{7,5},{8,10},{9,11},{10,... | collective-permute-start | bytes 983048 | tf_op jit(solution)/shard_map/ppermute | solution.py:221
  123.2 1.3 %collective-permute-start.16 = (bf16[256,640]{1,0:T(8,128)(2,1)S(1)}, bf16[256,640]{1,0:T(8,128)(2,1)S(1)}, u32[]{:S(2)}, u32[]{:S(2)}) collective-permute-start(bf16[256,640]{1,0:T(8,128)(2,1)S(1)} %get-tuple-element.46), channel_id=1, source_target_pairs={{0,1},{1,0},{2,3},{3,2},{4,5},{5,4},{6,7},{7,6},{8,9},{9,8},{10,11... | collective-permute-start | bytes 983048 | tf_op jit(solution)/shard_map/ppermute | solution.py:221
  124.6 0.1 fusion.11
  124.7 0.9 pad_maximum_fusion.1
  125.6 0.9 pad_maximum_fusion.2
  126.5 5.3 %collective-permute-done.14 = bf16[256,640]{1,0:T(8,128)(2,1)S(1)} collective-permute-done((bf16[256,640]{1,0:T(8,128)(2,1)S(1)}, bf16[256,640]{1,0:T(8,128)(2,1)S(1)}, u32[]{:S(2)}, u32[]{:S(2)}) %collective-permute-start.14) | collective-permute-done | bytes 327712 | tf_op jit(solution)/shard_map/ppermute | solution.py:221
  131.8 1.1 collective-permute-done.16
  132.9 0.2 fusion.7
  133.1 0.9 pad_maximum_fusion
  (30 shorter events, 0.2 us)
Async XLA Ops:
  0.6 4.1 %copy-start = (bf16[2,2,128,2560]{3,2,1,0:T(8,128)(2,1)S(1)}, bf16[2,2,128,2560]{3,2,1,0:T(8,128)(2,1)}, u32[]{:S(2)}) copy-start(bf16[2,2,128,2560]{3,2,1,0:T(8,128)(2,1)} %param.5) | copy-start | bytes 7864324
  2.9 1.8 %collective-permute-start = (bf16[2,320,256]{2,1,0:T(8,128)(2,1)S(1)}, bf16[2,320,256]{2,1,0:T(8,128)(2,1)S(1)}, u32[]{:S(2)}, u32[]{:S(2)}) collective-permute-start(bf16[2,320,256]{2,1,0:T(8,128)(2,1)S(1)} %get-tuple-element.52), channel_id=1, source_target_pairs={{0,4},{4,0},{8,12},{12,8},{16,20},{20,16},{24,28},{28,24},{1,5},{5... | collective-permute-start | bytes 983048 | tf_op jit(solution)/shard_map/ppermute | solution.py:218
  4.7 35.9 %collective-permute-start.1 = (bf16[512,2560]{1,0:T(8,128)(2,1)S(1)}, bf16[512,2560]{1,0:T(8,128)(2,1)}, u32[]{:S(2)}, u32[]{:S(2)}) collective-permute-start(bf16[512,2560]{1,0:T(8,128)(2,1)S(1)} %bitcast.53), channel_id=1, source_target_pairs={{0,4},{4,0},{8,12},{12,8},{16,20},{20,16},{24,28},{28,24},{1,5},{5... | collective-permute-start | bytes 7864328 | tf_op jit(solution)/shard_map/ppermute | solution.py:218
  5.1 44.2 %collective-permute-start.7 = (bf16[512,2560]{1,0:T(8,128)(2,1)}, bf16[512,2560]{1,0:T(8,128)(2,1)}, u32[]{:S(2)}, u32[]{:S(2)}) collective-permute-start(bf16[512,2560]{1,0:T(8,128)(2,1)} %bitcast.56), channel_id=1, source_target_pairs={{0,4},{4,0},{8,12},{12,8},{16,20},{20,16},{24,28},{28,24},{1,5},{5... | collective-permute-start | bytes 7864328 | tf_op jit(solution)/shard_map/ppermute | solution.py:218
  5.2 35.4 %collective-permute-start.2 = (bf16[4,8,128,128]{3,2,1,0:T(8,128)(2,1)}, bf16[4,8,128,128]{3,2,1,0:T(8,128)(2,1)}, u32[]{:S(2)}, u32[]{:S(2)}) collective-permute-start(bf16[4,8,128,128]{3,2,1,0:T(8,128)(2,1)} %bitcast.59), channel_id=1, source_target_pairs={{0,4},{4,0},{8,12},{12,8},{16,20},{20,16},{24,28},{28,24},{1,5},{5... | collective-permute-start | bytes 3145736 | tf_op jit(solution)/shard_map/ppermute | solution.py:218
  6.3 19.2 %collective-permute-start.4 = (bf16[2,320,256]{2,1,0:T(8,128)(2,1)S(1)}, bf16[2,320,256]{2,1,0:T(8,128)(2,1)S(1)}, u32[]{:S(2)}, u32[]{:S(2)}) collective-permute-start(bf16[2,320,256]{2,1,0:T(8,128)(2,1)S(1)} %pad_maximum_fusion.5.rest_0_), channel_id=1, source_target_pairs={{0,16},{4,20},{8,24},{12,28},{16,0},{20,4},{24,8},{28,12},{1,17},{... | collective-permute-start | bytes 983048 | tf_op jit(solution)/shard_map/ppermute | solution.py:210
  10.1 17.1 %collective-permute-start.3 = (bf16[2,320,256]{2,1,0:T(8,128)(2,1)S(1)}, bf16[2,320,256]{2,1,0:T(8,128)(2,1)}, u32[]{:S(2)}, u32[]{:S(2)}) collective-permute-start(bf16[2,320,256]{2,1,0:T(8,128)(2,1)S(1)} %pad_maximum_fusion.5.rest_0_), channel_id=1, source_target_pairs={{0,8},{4,12},{8,0},{12,4},{16,24},{20,28},{24,16},{28,20},{1,9},{5... | collective-permute-start | bytes 983048 | tf_op jit(solution)/shard_map/ppermute | solution.py:210
  25.5 15.1 %collective-permute-start.5 = (bf16[2,320,256]{2,1,0:T(8,128)(2,1)S(1)}, bf16[2,320,256]{2,1,0:T(8,128)(2,1)}, u32[]{:S(2)}, u32[]{:S(2)}) collective-permute-start(bf16[2,320,256]{2,1,0:T(8,128)(2,1)S(1)} %collective-permute-done.4.rest_2_), channel_id=1, source_target_pairs={{0,8},{4,12},{8,0},{12,4},{16,24},{20,28},{24,16},{28,20},{1,9},{5... | collective-permute-start | bytes 983048 | tf_op jit(solution)/shard_map/ppermute | solution.py:210
  27.2 22.1 %copy-start.1 = (bf16[2,2,128,2560]{3,2,1,0:T(8,128)(2,1)S(1)}, bf16[2,2,128,2560]{3,2,1,0:T(8,128)(2,1)}, u32[]{:S(2)}) copy-start(bf16[2,2,128,2560]{3,2,1,0:T(8,128)(2,1)} %param.7) | copy-start | bytes 7864324
  27.2 20.1 %collective-permute-start.10 = (bf16[2,320,256]{2,1,0:T(8,128)(2,1)S(1)}, bf16[2,320,256]{2,1,0:T(8,128)(2,1)S(1)}, u32[]{:S(2)}, u32[]{:S(2)}) collective-permute-start(bf16[2,320,256]{2,1,0:T(8,128)(2,1)S(1)} %pad_maximum_fusion.6.rest_0_), channel_id=1, source_target_pairs={{0,16},{4,20},{8,24},{12,28},{16,0},{20,4},{24,8},{28,12},{1,17},{... | collective-permute-start | bytes 983048 | tf_op jit(solution)/shard_map/ppermute | solution.py:210
  40.6 1.2 copy-start.2
  47.1 2.2 %collective-permute-start.6 = (bf16[512,256]{1,0:T(8,128)(2,1)S(1)}, bf16[512,256]{1,0:T(8,128)(2,1)S(1)}, u32[]{:S(2)}, u32[]{:S(2)}) collective-permute-start(bf16[512,256]{1,0:T(8,128)(2,1)S(1)} %get-tuple-element.27.mixed_s), channel_id=1, source_target_pairs={{0,4},{4,0},{8,12},{12,8},{16,20},{20,16},{24,28},{28,24},{1,5},{5... | collective-permute-start | bytes 786440 | tf_op jit(solution)/shard_map/ppermute | solution.py:218
  47.2 10.6 %collective-permute-start.9 = (bf16[2,320,256]{2,1,0:T(8,128)(2,1)S(1)}, bf16[2,320,256]{2,1,0:T(8,128)(2,1)S(1)}, u32[]{:S(2)}, u32[]{:S(2)}) collective-permute-start(bf16[2,320,256]{2,1,0:T(8,128)(2,1)S(1)} %pad_maximum_fusion.6.rest_0_), channel_id=1, source_target_pairs={{0,8},{4,12},{8,0},{12,4},{16,24},{20,28},{24,16},{28,20},{1,9},{5... | collective-permute-start | bytes 983048 | tf_op jit(solution)/shard_map/ppermute | solution.py:210
  47.2 17.5 %collective-permute-start.11 = (bf16[2,320,256]{2,1,0:T(8,128)(2,1)S(1)}, bf16[2,320,256]{2,1,0:T(8,128)(2,1)S(1)}, u32[]{:S(2)}, u32[]{:S(2)}) collective-permute-start(bf16[2,320,256]{2,1,0:T(8,128)(2,1)S(1)} %collective-permute-done.10.rest_2_), channel_id=1, source_target_pairs={{0,8},{4,12},{8,0},{12,4},{16,24},{20,28},{24,16},{28,20},{1,9},{5... | collective-permute-start | bytes 983048 | tf_op jit(solution)/shard_map/ppermute | solution.py:210
  49.3 5.3 %copy-start.6 = (bf16[512,256]{1,0:T(8,128)(2,1)}, bf16[512,256]{1,0:T(8,128)(2,1)S(1)}, u32[]{:S(2)}) copy-start(bf16[512,256]{1,0:T(8,128)(2,1)S(1)} %collective-permute-done.6.unread.mixed_r) | copy-start | bytes 786436
  49.3 22.1 %copy-start.3 = (bf16[2,2,8,128,128]{4,3,2,1,0:T(8,128)(2,1)S(1)}, bf16[2,2,8,128,128]{4,3,2,1,0:T(8,128)(2,1)}, u32[]{:S(2)}) copy-start(bf16[2,2,8,128,128]{4,3,2,1,0:T(8,128)(2,1)} %param.6) | copy-start | bytes 3145732
  54.6 16.7 %collective-permute-start.8 = (bf16[2,320,256]{2,1,0:T(8,128)(2,1)S(1)}, bf16[2,320,256]{2,1,0:T(8,128)(2,1)S(1)}, u32[]{:S(2)}, u32[]{:S(2)}) collective-permute-start(bf16[2,320,256]{2,1,0:T(8,128)(2,1)S(1)} %get-tuple-element.29), channel_id=1, source_target_pairs={{0,8},{4,12},{8,0},{12,4},{16,24},{20,28},{24,16},{28,20},{1,9},{5... | collective-permute-start | bytes 983048 | tf_op jit(solution)/shard_map/ppermute | solution.py:210
  79.0 3.0 %copy-start.4 = (bf16[2,320,256]{2,1,0:T(8,128)(2,1)}, bf16[2,320,256]{2,1,0:T(8,128)(2,1)S(1)}, u32[]{:S(2)}) copy-start(bf16[2,320,256]{2,1,0:T(8,128)(2,1)S(1)} %get-tuple-element.38.block) | copy-start | bytes 983044
  79.1 3.0 %copy-start.8 = (bf16[2,320,256]{2,1,0:T(8,128)(2,1)}, bf16[2,320,256]{2,1,0:T(8,128)(2,1)S(1)}, u32[]{:S(2)}) copy-start(bf16[2,320,256]{2,1,0:T(8,128)(2,1)S(1)} %get-tuple-element.36) | copy-start | bytes 983044
  79.1 5.8 %collective-permute-start.12 = (bf16[2560,256]{1,0:T(8,128)(2,1)}, bf16[2560,256]{1,0:T(8,128)(2,1)S(1)}, u32[]{:S(2)}, u32[]{:S(2)}) collective-permute-start(bf16[2560,256]{1,0:T(8,128)(2,1)} %get-tuple-element.31.w_o), channel_id=1, source_target_pairs={{0,4},{4,0},{8,12},{12,8},{16,20},{20,16},{24,28},{28,24},{1,5},{5... | collective-permute-start | bytes 3932168 | tf_op jit(solution)/shard_map/ppermute | solution.py:218
  79.1 25.3 %collective-permute-start.21 = (bf16[2,320,256]{2,1,0:T(8,128)(2,1)}, bf16[2,320,256]{2,1,0:T(8,128)(2,1)S(1)}, u32[]{:S(2)}, u32[]{:S(2)}) collective-permute-start(bf16[2,320,256]{2,1,0:T(8,128)(2,1)} %get-tuple-element.41), channel_id=1, source_target_pairs={{0,8},{4,12},{8,0},{12,4},{16,24},{20,28},{24,16},{28,20},{1,9},{5... | collective-permute-start | bytes 983048 | tf_op jit(solution)/shard_map/ppermute | solution.py:210
  79.5 24.5 %collective-permute-start.18 = (bf16[2,320,256]{2,1,0:T(8,128)(2,1)}, bf16[2,320,256]{2,1,0:T(8,128)(2,1)S(1)}, u32[]{:S(2)}, u32[]{:S(2)}) collective-permute-start(bf16[2,320,256]{2,1,0:T(8,128)(2,1)} %get-tuple-element.39), channel_id=1, source_target_pairs={{0,8},{4,12},{8,0},{12,4},{16,24},{20,28},{24,16},{28,20},{1,9},{5... | collective-permute-start | bytes 983048 | tf_op jit(solution)/shard_map/ppermute | solution.py:210
  82.0 22.4 %collective-permute-start.22 = (bf16[2,320,256]{2,1,0:T(8,128)(2,1)}, bf16[2,320,256]{2,1,0:T(8,128)(2,1)S(1)}, u32[]{:S(2)}, u32[]{:S(2)}) collective-permute-start(bf16[2,320,256]{2,1,0:T(8,128)(2,1)} %add_convert_fusion), channel_id=1, source_target_pairs={{0,16},{4,20},{8,24},{12,28},{16,0},{20,4},{24,8},{28,12},{1,17},{... | collective-permute-start | bytes 983048 | tf_op jit(solution)/shard_map/ppermute | solution.py:210
  83.0 20.9 %copy-start.5 = (bf16[2,320,256]{2,1,0:T(8,128)(2,1)S(1)}, bf16[2,320,256]{2,1,0:T(8,128)(2,1)}, u32[]{:S(2)}) copy-start(bf16[2,320,256]{2,1,0:T(8,128)(2,1)} %copy-done.4) | copy-start | bytes 983044
  83.0 31.6 %collective-permute-start.17 = (bf16[2,320,256]{2,1,0:T(8,128)(2,1)}, bf16[2,320,256]{2,1,0:T(8,128)(2,1)S(1)}, u32[]{:S(2)}, u32[]{:S(2)}) collective-permute-start(bf16[2,320,256]{2,1,0:T(8,128)(2,1)} %copy-done.8), channel_id=1, source_target_pairs={{0,8},{4,12},{8,0},{12,4},{16,24},{20,28},{24,16},{28,20},{1,9},{5... | collective-permute-start | bytes 983048 | tf_op jit(solution)/shard_map/ppermute | solution.py:210
  84.8 1.0 copy-start.7
  104.1 16.9 %collective-permute-start.19 = (bf16[2,320,256]{2,1,0:T(8,128)(2,1)S(1)}, bf16[2,320,256]{2,1,0:T(8,128)(2,1)S(1)}, u32[]{:S(2)}, u32[]{:S(2)}) collective-permute-start(bf16[2,320,256]{2,1,0:T(8,128)(2,1)S(1)} %sum.1), channel_id=1, source_target_pairs={{0,16},{4,20},{8,24},{12,28},{16,0},{20,4},{24,8},{28,12},{1,17},{... | collective-permute-start | bytes 983048 | tf_op jit(solution)/shard_map/ppermute | solution.py:210
  104.5 16.8 %collective-permute-start.13 = (bf16[2,256,640]{2,1,0:T(8,128)(2,1)S(1)}, bf16[2,256,640]{2,1,0:T(8,128)(2,1)S(1)}, u32[]{:S(2)}, u32[]{:S(2)}) collective-permute-start(bf16[2,256,640]{2,1,0:T(8,128)(2,1)S(1)} %get-tuple-element.33), channel_id=1, source_target_pairs={{0,1},{1,0},{2,3},{3,2},{4,5},{5,4},{6,7},{7,6},{8,9},{9,8},{10,11... | collective-permute-start | bytes 1966088 | tf_op jit(solution)/shard_map/ppermute | solution.py:221
  106.1 15.3 %collective-permute-start.15 = (bf16[2,256,640]{2,1,0:T(8,128)(2,1)S(1)}, bf16[2,256,640]{2,1,0:T(8,128)(2,1)S(1)}, u32[]{:S(2)}, u32[]{:S(2)}) collective-permute-start(bf16[2,256,640]{2,1,0:T(8,128)(2,1)S(1)} %get-tuple-element.34), channel_id=1, source_target_pairs={{0,2},{1,3},{2,0},{3,1},{4,6},{5,7},{6,4},{7,5},{8,10},{9,11},{10,... | collective-permute-start | bytes 1966088 | tf_op jit(solution)/shard_map/ppermute | solution.py:221
  107.7 16.9 %collective-permute-start.23 = (f32[320,256]{1,0:T(8,128)S(1)}, f32[320,256]{1,0:T(8,128)S(1)}, u32[]{:S(2)}, u32[]{:S(2)}) collective-permute-start(f32[320,256]{1,0:T(8,128)S(1)} %slice_bitcast_fusion), channel_id=1, source_target_pairs={{0,4},{4,0},{8,12},{12,8},{16,20},{20,16},{24,28},{28,24},{1,5},{5... | collective-permute-start | bytes 983048 | tf_op jit(solution)/shard_map/ppermute | solution.py:218
  121.1 3.5 %collective-permute-start.20 = (f32[320,256]{1,0:T(8,128)S(1)}, f32[320,256]{1,0:T(8,128)S(1)}, u32[]{:S(2)}, u32[]{:S(2)}) collective-permute-start(f32[320,256]{1,0:T(8,128)S(1)} %slice_bitcast_fusion.2), channel_id=1, source_target_pairs={{0,4},{4,0},{8,12},{12,8},{16,20},{20,16},{24,28},{28,24},{1,5},{5... | collective-permute-start | bytes 983048 | tf_op jit(solution)/shard_map/ppermute | solution.py:218
  121.7 10.2 %collective-permute-start.14 = (bf16[256,640]{1,0:T(8,128)(2,1)S(1)}, bf16[256,640]{1,0:T(8,128)(2,1)S(1)}, u32[]{:S(2)}, u32[]{:S(2)}) collective-permute-start(bf16[256,640]{1,0:T(8,128)(2,1)S(1)} %get-tuple-element.45), channel_id=1, source_target_pairs={{0,2},{1,3},{2,0},{3,1},{4,6},{5,7},{6,4},{7,5},{8,10},{9,11},{10,... | collective-permute-start | bytes 983048 | tf_op jit(solution)/shard_map/ppermute | solution.py:221
  123.2 9.7 %collective-permute-start.16 = (bf16[256,640]{1,0:T(8,128)(2,1)S(1)}, bf16[256,640]{1,0:T(8,128)(2,1)S(1)}, u32[]{:S(2)}, u32[]{:S(2)}) collective-permute-start(bf16[256,640]{1,0:T(8,128)(2,1)S(1)} %get-tuple-element.46), channel_id=1, source_target_pairs={{0,1},{1,0},{2,3},{3,2},{4,5},{5,4},{6,7},{7,6},{8,9},{9,8},{10,11... | collective-permute-start | bytes 983048 | tf_op jit(solution)/shard_map/ppermute | solution.py:221

commit v9 on v8

--- a/solution.py
+++ b/solution.py
@@ -29,9 +29,10 @@
     return pl.ds(pl.multiple_of(index * size, math.gcd(size, 16)), size)
 
 
-def place(idx, slots, w_ref):
+def place(idx, slots, which, w_ref):
     core = idx[0]
     for j, slot in enumerate(slots):
+        slot = slot if len(slot.shape) == 3 else slot.at[which]
         depth = slot.shape[1]
         mine, other = slot[0], slot[1]
         low = jnp.where(core == 0, mine, other)
@@ -60,22 +61,20 @@
     return [(h, min(2, heads - h)) for h in range(0, heads, 2)]
 
 
-def backward_kernel(n_slots, idx, unread, token, cot_o, cot_s, mix_o, mix_s, act_o, act_s, *rest):
-    del unread, token
-    slots, rest = rest[:n_slots], rest[n_slots:]
-    w_out, rest = rest[0], rest[1:]
-    outs, (cot_v, act_v, mix_v, left_v, grad_v, sems) = rest[:-6], rest[-6:]
-    tokens, cols = cot_o.shape[0], w_out.shape[1]
+def assemble_kernel(idx, token, *rest):
+    del token
+    place(idx, rest[:-1], 1, rest[-1])
+
+
+def d_value_kernel(idx, cot_o, cot_s, mix_o, mix_s, w_out, left_v, cot_v, mix_v, sems):
     groups, _, seq, _ = mix_o.shape
     heads = mix_v.shape[2]
     here = pl.ds(idx[0] * heads, heads)
     copies = begin(
         [(cot_o, cot_v.at[0]), (mix_o.at[:, here], mix_v.at[0])]
-        + [(cot_s, cot_v.at[1]), (mix_s.at[:, here], mix_v.at[1])]
-        + [(act_o, act_v.at[pl.ds(0, tokens)]), (act_s, act_v.at[pl.ds(tokens, tokens)])],
+        + [(cot_s, cot_v.at[1]), (mix_s.at[:, here], mix_v.at[1])],
         sems,
     )
-    place(idx, slots, w_out)
     for half in range(2):
         copies[2 * half].wait()
         d_mixed = dot(cot_v[half], w_out[...])
@@ -99,10 +98,23 @@
                 left_v[h * HEAD_DIM : (h + n) * HEAD_DIM, at : at + seq] = dot(
                     part, weights
                 ).astype(BF16)
-    copies[4].wait()
-    copies[5].wait()
-    gradient_rows(left_v[...], act_v, grad_v, 640)
-    hand_out(idx, 1, grad_v, outs)
+
+
+def gradient_kernel(n_near, idx, token, unread, right_o, right_s, left_ref, *rest):
+    del token, unread
+    others, rest = rest[:n_near], rest[n_near:]
+    outs, (right_v, grad_v, sems) = rest[:-3], rest[-3:]
+    tokens, _ = right_o.shape
+    copies = begin(
+        [(right_o, right_v.at[pl.ds(0, tokens)]), (right_s, right_v.at[pl.ds(tokens, tokens)])],
+        sems,
+    )
+    copies[0].wait()
+    copies[1].wait()
+    gradient_rows(left_ref[...], right_v, grad_v, 640)
+    for other in others:
+        outs[1][1] = other[...]
+    hand_out(idx, 1, grad_v, [outs[0], outs[1].at[0], *outs[2:]] if n_near else outs)
 
 
 def mixed_kernel(n_slots, idx, act_o, act_s, mix_o, mix_s, *rest):
@@ -115,7 +127,7 @@
         + [(act_s, act_v.at[1]), (mix_s.at[:, here], mix_v.at[1])],
         sems,
     )
-    place(idx, slots, w_v)
+    place(idx, slots, 0, w_v)
     for half, out in enumerate((mixed_o, mixed_s)):
         copies[2 * half].wait()
         value = dot(act_v[half], w_v[...]).astype(BF16)
@@ -156,8 +168,8 @@
     hand_out(idx, 1, grad_v, outs)
 
 
-def sum_kernel(token, block, got, out):
-    del token
+def sum_kernel(unread, block, got, out):
+    del unread
     out[...] = (block[...].astype(F32) + got[...].astype(F32)).astype(BF16)
 
 
@@ -243,17 +255,15 @@
     def added(block, got):
         return (block.astype(F32) + got.astype(F32)).astype(BF16)
 
-    def gather(u):
+    def gather_two(u_value, u_out):
         if not line4:
-            return gather_ring(u)
-        far = swap(u, 2)
-        return [u, swap(u, 1), far, swap(far, 1)]
-
-    def scatter(blocks, passed, c, add=added):
-        if not line4:
-            return scatter_ring(blocks, c)
-        far = swap(add(blocks[2], passed), 2)
-        return scatter_end(blocks[0], (swap(blocks[1], 1), far), c)
+            return gather_ring(u_value), gather_ring(u_out)
+        beside = swap(jnp.stack([u_value, u_out]), 1)
+        far_value, far_out = swap(u_value, 2), swap(u_out, 2)
+        return (
+            [u_value, beside, far_value, swap(far_value, 1)],
+            [u_out, beside, far_out, swap(far_out, 1)],
+        )
 
     def scatter_end(own, got, c):
         total = own.astype(F32)
@@ -289,7 +299,7 @@
         flops = 4 * tokens * width * cols
 
         u_out, u_value, act_s, mix_s, cot_s = swap_cores(w_out, w_value, act, mix, cot, c)
-        value_slots, out_slots = gather(u_value), gather(u_out)
+        value_slots, out_slots = gather_two(u_value, u_out)
         n_slots = len(out_slots)
         pack = lambda *values: jnp.stack([jnp.int32(x) for x in values])
         idx = pack(c, *planes_of(z))
@@ -321,18 +331,30 @@
             flops,
         )(idx, cot, cot_s, mixed_o, mixed_s, mixed_r)
         out_passed = swap(out_sends[3], 1) if line4 else token
-        grad_out = scatter(out_sends, out_passed, c)
-        w_full, *back_sends = call(
-            functools.partial(backward_kernel, n_slots),
-            "backward",
-            [SMEM, ANY, VMEM] + [ANY] * 6 + [VMEM] * n_slots,
-            [(width, cols)] + send_shapes,
-            [halves, both, mix_scratch, left_tokens, rows, pltpu.SemaphoreType.DMA((6,))],
-            2 * flops,
-        )(idx, out_passed, token, cot, cot_s, mix, mix_s, act, act_s, *out_slots)
+        w_full = call(
+            assemble_kernel,
+            "assemble",
+            [SMEM, ANY] + [VMEM] * n_slots,
+            [(width, cols)],
+            [],
+            0,
+        )(idx, token, *out_slots)[0]
         w_full_s = sibling(w_full)
-        back_passed = swap(back_sends[3], 1) if line4 else token
-
+        left = call(
+            d_value_kernel,
+            "d_value",
+            [SMEM] + [ANY] * 4 + [VMEM],
+            [(cols, 2 * tokens)],
+            [halves, mix_scratch, pltpu.SemaphoreType.DMA((4,))],
+            flops,
+        )(idx, cot, cot_s, mix, mix_s, w_full)[0]
+        if line4:
+            out_onward = added(out_sends[2], out_passed)
+            out_far = swap(out_onward, 2)
+            others = [out_sends[1]]
+            back_shapes = [block, (2, *block), block, block]
+        else:
+            out_onward, others, back_shapes = token, [], send_shapes
         part = width // n_node
         half = tokens // 2
         if n_node == 4:
@@ -348,10 +370,26 @@
             flops,
         )(idx_node, mixed_o, mixed_r, w_full, w_full_s)
 
-        def add_after_terms(a, b):
-            return call(sum_kernel, "sum", [VMEM] * 3, [block], [], 0)(token, a, b)[0]
-
-        grad_value = scatter(back_sends, back_passed, c, add_after_terms)
+        back_sends = call(
+            functools.partial(gradient_kernel, len(others)),
+            "grad_value",
+            [SMEM] + [ANY] * 4 + [VMEM] * (1 + len(others)),
+            back_shapes,
+            [both, rows, pltpu.SemaphoreType.DMA((2,))],
+            flops,
+        )(idx, token, out_onward, act, act_s, left, *others)
+        if line4:
+            near = swap(back_sends[1], 1)
+            back_passed = swap(back_sends[3], 1)
+            onward = call(sum_kernel, "sum", [ANY] + [VMEM] * 2, [block], [], 0)(
+                out_far, back_sends[2], back_passed
+            )[0]
+            grad_out = scatter_end(out_sends[0], (near[1], out_far), c)
+            grad_value = scatter_end(back_sends[0], (near[0], swap(onward, 2)), c)
+        else:
+            grad_value = scatter_ring(back_sends, c)
+            grad_out = scatter_ring(out_sends, c)
+
         if n_node == 4:
             along_x, along_y, kept = terms
             kept = kept.astype(F32)

time: 134 us -> 131 us (0.978)
  waiting for transfers between devices: 76.3 us -> 71.2 us
  Pallas kernels: 21.5 us -> 25.8 us
  starting transfers between devices: 24.5 us -> 20.8 us
  local copies, waits for them, and re-layouts: 5.24 us -> 6.74 us
    ppermute x4, waiting for transfers between devices: 6.4 us -> 0.01 us  [flip(): return lax.ppermute(x, 'node', [(i, i ^ j) for i in range(n_node)])]
    pallas_call x2 -> x4, Pallas kernels: 7.78 us -> 12.3 us  [the longest x1 5.53 us: body(): call(d_value_kernel, 'd_value', [SMEM] + [ANY] * 4 + [VMEM], [(cols, 2 *...]
    unnamed x18 -> x32, local copies, waits for them, and re-layouts: 2.21 us -> 5.22 us
    ppermute x12 -> x10, starting transfers between devices: 16.8 us -> 14.4 us  [move(): lax.ppermute(x, 'wide', [(2 * s + c, 2 * d + c) for s, d in pairs for c i...]
    ppermute x4, starting transfers between devices: 5.96 us -> 4.19 us  [flip(): return lax.ppermute(x, 'node', [(i, i ^ j) for i in range(n_node)])]
    ppermute x8, waiting for transfers between devices: 1.27 us -> 2.69 us  [sibling(): return lax.ppermute(x, 'wide', [(i, i ^ 1) for i in range(n_wide)])]
    ppermute x12 -> x10, waiting for transfers between devices: 68.6 us -> 68.5 us  [move(): lax.ppermute(x, 'wide', [(2 * s + c, 2 * d + c) for s, d in pairs for c i...]
  transfers between devices with their start and end apart: 24 -> 22, of which waited for: 11 -> 8; matrix products, arithmetic and copies ran while one was open for 4% -> 3% of each run, Pallas kernels for 10% -> 18%
where the time goes in v9:
time: 131 us
  waiting for transfers between devices  71.2 us (54%)
  Pallas kernels  25.8 us (20%)
  starting transfers between devices  20.8 us (16%)
  local copies, waits for them, and re-layouts  6.74 us (5%)
  other arithmetic  4.95 us (4%)
    ppermute x10, waiting for transfers between devices, move(): lax.ppermute(x, 'wide', [(2 * s + c, 2 * d + c) for s, d in pairs for c i...  68.5 us
    ppermute x10, starting transfers between devices, move(): lax.ppermute(x, 'wide', [(2 * s + c, 2 * d + c) for s, d in pairs for c i...  14.4 us
    pallas_call x1, Pallas kernels, body(): call(d_value_kernel, 'd_value', [SMEM] + [ANY] * 4 + [VMEM], [(cols, 2 *...  5.53 us
    pallas_call x1, Pallas kernels, body(): call(functools.partial(mixed_kernel, n_slots), 'mixed', [SMEM] + [ANY] *...  5.23 us
    unnamed x32, local copies, waits for them, and re-layouts  5.22 us
    pallas_call x1, Pallas kernels, body(): call(grad_out_kernel, 'grad_out', [SMEM] + [ANY] * 2 + [VMEM] * 2 + [ANY]...  4.56 us
    pallas_call x1, Pallas kernels, body(): call(functools.partial(gradient_kernel, len(others)), 'grad_value', [SMEM...  4.46 us
    ppermute x4, starting transfers between devices, flip(): return lax.ppermute(x, 'node', [(i, i ^ j) for i in range(n_node)])  4.19 us
  transfers between devices with their start and end apart: 22, of which 8 were waited for; matrix products, arithmetic and copies ran while one was open for 3% of the time, Pallas kernels for 18%

profile of v9, /device:TPU:0, one launch (start us, length us, event | category | flops | bytes accessed | tf_op | source)
XLA Modules:
  0.0 130.6 jit_solution(5189842554646540880)
XLA Ops:
  0.7 1.3 %slice_bitcast_fusion.8 = (bf16[1,320,256]{2,1,0:T(8,128)(2,1)S(1)}, bf16[1,320,256]{2,1,0:T(8,128)(2,1)S(1)}, bf16[1,320,256]{2,1,0:T(8,128)(2,1)S(1)}, bf16[1,320,256]{2,1,0:T(8,128)(2,1)S(1)}) fusion(bf16[320,512]{1,0:T(8,128)(2,1)} %param.8, bf16[320,512]{1,0:T(8,128)(2,1)} %param.9), kind=kLoop, calls=%fused_computation.41 | loop fusion | bytes 1310720 | tf_op jit(solution)/shard_map/stack | solution.py:238
  2.0 0.1 broadcast_select_fusion
  2.1 0.5 collective-permute-start
  2.6 1.3 collective-permute-done
  3.8 0.4 collective-permute-start.1
  4.2 0.1 collective-permute-start.7
  4.4 0.4 collective-permute-start.2
  4.8 0.8 pad_maximum_fusion.7
  5.7 0.0 copy-start.5
  5.7 0.1 pad_maximum_fusion
  5.7 2.8 %collective-permute-start.3 = (bf16[2,2,320,256]{3,2,1,0:T(8,128)(2,1)S(1)}, bf16[2,2,320,256]{3,2,1,0:T(8,128)(2,1)S(1)}, u32[]{:S(2)}, u32[]{:S(2)}) collective-permute-start(bf16[2,2,320,256]{3,2,1,0:T(8,128)(2,1)S(1)} %pad_maximum_fusion), channel_id=1, source_target_pairs={{0,8},{4,12},{8,0},{12,4},{16,24},{20,28},{24,16},{28,20},{1,9},{5... | collective-permute-start | bytes 1966088 | tf_op jit(solution)/shard_map/ppermute | solution.py:222
  8.5 2.6 %collective-permute-start.4 = (bf16[2,320,256]{2,1,0:T(8,128)(2,1)S(1)}, bf16[2,320,256]{2,1,0:T(8,128)(2,1)}, u32[]{:S(2)}, u32[]{:S(2)}) collective-permute-start(bf16[2,320,256]{2,1,0:T(8,128)(2,1)S(1)} %get-tuple-element.56.rest_0_), channel_id=1, source_target_pairs={{0,16},{4,20},{8,24},{12,28},{16,0},{20,4},{24,8},{28,12},{1,17},{... | collective-permute-start | bytes 983048 | tf_op jit(solution)/shard_map/ppermute | solution.py:222
  11.1 18.9 %collective-permute-done.4.rest_2_ = bf16[2,320,256]{2,1,0:T(8,128)(2,1)} collective-permute-done((bf16[2,320,256]{2,1,0:T(8,128)(2,1)S(1)}, bf16[2,320,256]{2,1,0:T(8,128)(2,1)}, u32[]{:S(2)}, u32[]{:S(2)}) %collective-permute-start.4) | collective-permute-done | bytes 327712 | tf_op jit(solution)/shard_map/ppermute | solution.py:222
  30.1 3.6 %collective-permute-start.5 = (bf16[2,320,256]{2,1,0:T(8,128)(2,1)}, bf16[2,320,256]{2,1,0:T(8,128)(2,1)}, u32[]{:S(2)}, u32[]{:S(2)}) collective-permute-start(bf16[2,320,256]{2,1,0:T(8,128)(2,1)} %collective-permute-done.4.rest_2_), channel_id=1, source_target_pairs={{0,8},{4,12},{8,0},{12,4},{16,24},{20,28},{24,16},{28,20},{1,9},{5... | collective-permute-start | bytes 983048 | tf_op jit(solution)/shard_map/ppermute | solution.py:222
  33.7 0.0 collective-permute-start.8
  33.7 0.1 stack.76.idx
  33.8 13.4 %collective-permute-done.5.rest_3_ = bf16[2,320,256]{2,1,0:T(8,128)(2,1)} collective-permute-done((bf16[2,320,256]{2,1,0:T(8,128)(2,1)}, bf16[2,320,256]{2,1,0:T(8,128)(2,1)}, u32[]{:S(2)}, u32[]{:S(2)}) %collective-permute-start.5) | collective-permute-done | bytes 327712 | tf_op jit(solution)/shard_map/ppermute | solution.py:222
  47.2 0.0 collective-permute-done.2.mix_s
  47.2 0.0 collective-permute-done.1.act_s.right_s
  47.2 1.7 %copy-done.1 = bf16[2,2,128,2560]{3,2,1,0:T(8,128)(2,1)S(1)} copy-done((bf16[2,2,128,2560]{3,2,1,0:T(8,128)(2,1)S(1)}, bf16[2,2,128,2560]{3,2,1,0:T(8,128)(2,1)}, u32[]{:S(2)}) %copy-start.1) | copy-done | bytes 2621464
  48.9 1.2 copy-done.3
  50.2 1.0 copy-done.6
  51.1 5.2 %mixed.1 = (bf16[512,256]{1,0:T(8,128)(2,1)S(1)}, bf16[512,256]{1,0:T(8,128)(2,1)S(1)}) custom-call(s32[5]{0:T(128)S(1)} %stack.76.idx, bf16[512,2560]{1,0:T(8,128)(2,1)S(1)} %bitcast.71, bf16[512,2560]{1,0:T(8,128)(2,1)} %collective-permute-done.1.act_s.right_s, bf16[4,8,128,128]{3,2,1,0:T(8,128)(2,1)S(1)} %bitcast.74, ...), custom_call_target="tpu_custom_call" | custom-call | flops 1342177280 | bytes 12582912 | tf_op jit(solution)/shard_map/mixed/pallas_call | solution.py:316
  56.4 0.1 collective-permute-start.6
  56.5 0.1 collective-permute-start.9
  56.6 1.4 %collective-permute-done.6.unread.mixed_r = bf16[512,256]{1,0:T(8,128)(2,1)S(1)} collective-permute-done((bf16[512,256]{1,0:T(8,128)(2,1)S(1)}, bf16[512,256]{1,0:T(8,128)(2,1)S(1)}, u32[]{:S(2)}, u32[]{:S(2)}) %collective-permute-start.6) | collective-permute-done | bytes 262176 | tf_op jit(solution)/shard_map/ppermute | solution.py:230
  58.0 4.6 %grad_out.1 = (bf16[16,128]{1,0:T(8,128)(2,1)S(1)}, bf16[2,320,256]{2,1,0:T(8,128)(2,1)S(1)}, bf16[2,320,256]{2,1,0:T(8,128)(2,1)S(1)}, bf16[2,320,256]{2,1,0:T(8,128)(2,1)S(1)}, bf16[2,320,256]{2,1,0:T(8,128)(2,1)S(1)}) custom-call(s32[5]{0:T(128)S(1)} %stack.76.idx, bf16[512,2560]{1,0:T(8,128)(2,1)S(1)} %bitcast.68, ...), custom_call_target="tpu_custom_call" | custom-call | flops 1342177280 | bytes 12582912 | tf_op jit(solution)/shard_map/grad_out/pallas_call | solution.py:325
  62.6 0.0 copy-start.11
  62.6 0.0 copy-start.15
  62.6 4.2 %collective-permute-done.9.rest_3_ = bf16[2,320,256]{2,1,0:T(8,128)(2,1)S(1)} collective-permute-done((bf16[2,320,256]{2,1,0:T(8,128)(2,1)}, bf16[2,320,256]{2,1,0:T(8,128)(2,1)S(1)}, u32[]{:S(2)}, u32[]{:S(2)}) %collective-permute-start.9) | collective-permute-done | bytes 327712 | tf_op jit(solution)/shard_map/ppermute | solution.py:222
  66.8 2.3 %assemble.1.w_o.w_out = bf16[2560,256]{1,0:T(8,128)(2,1)} custom-call(s32[5]{0:T(128)S(1)} %stack.76.idx, bf16[16,128]{1,0:T(8,128)(2,1)S(1)} %get-tuple-element.28.token, bf16[2,320,256]{2,1,0:T(8,128)(2,1)} %get-tuple-element.53.rest_0_, bf16[2,2,320,256]{3,2,1,0:T(8,128)(2,1)S(1)} %collective-permute-done.3.rest_1_, ...), custom_call_target="tpu_custom_call" | custom-call | bytes 12582912 | tf_op jit(solution)/shard_map/assemble/pallas_call | solution.py:334
  69.1 0.1 collective-permute-start.10
  69.2 0.3 collective-permute-start.15
  69.5 0.1 pad_add_fusion.idx
  69.6 1.2 copy-done.4
  70.8 5.5 %d_value.1.left_ref = bf16[256,1024]{1,0:T(8,128)(2,1)S(1)} custom-call(s32[5]{0:T(128)S(1)} %stack.76.idx, bf16[512,2560]{1,0:T(8,128)(2,1)S(1)} %bitcast.69, bf16[512,2560]{1,0:T(8,128)(2,1)} %collective-permute-done.7.cot_s, bf16[4,8,128,128]{3,2,1,0:T(8,128)(2,1)S(1)} %bitcast.75, bf16[4,8,128,128]{3,2,1,0:T(8,128)(2,1)} %collective-permute-done.2.mix_s, ...), custom_call_target="tpu_custom_call" | custom-call | flops 1342177280 | bytes 12582912 | tf_op jit(solution)/shard_map/d_value/pallas_call | solution.py:343
  76.4 0.0 copy-start.12
  76.4 0.0 copy-start.2
  76.4 3.7 %terms.1 = (bf16[16,128]{1,0:T(8,128)(2,1)S(1)}, bf16[2,256,640]{2,1,0:T(8,128)(2,1)S(1)}, bf16[2,256,640]{2,1,0:T(8,128)(2,1)S(1)}, bf16[4,256,640]{2,1,0:T(8,128)(2,1)S(1)}) custom-call(s32[4]{0:T(128)S(1)} %pad_add_fusion.idx, bf16[512,256]{1,0:T(8,128)(2,1)S(1)} %get-tuple-element.25.mixed_o, bf16[512,256]{1,0:T(8,128)(2,1)S(1)} %copy-done.14, ...), custom_call_target="tpu_custom_call" | custom-call | flops 1342177280 | bytes 12582912 | tf_op jit(solution)/shard_map/terms/pallas_call | solution.py:364
  80.1 1.6 %collective-permute-start.11 = (bf16[2,256,640]{2,1,0:T(8,128)(2,1)S(1)}, bf16[2,256,640]{2,1,0:T(8,128)(2,1)S(1)}, u32[]{:S(2)}, u32[]{:S(2)}) collective-permute-start(bf16[2,256,640]{2,1,0:T(8,128)(2,1)S(1)} %get-tuple-element.30), channel_id=1, source_target_pairs={{0,1},{1,0},{2,3},{3,2},{4,5},{5,4},{6,7},{7,6},{8,9},{9,8},{10,11... | collective-permute-start | bytes 1966088 | tf_op jit(solution)/shard_map/ppermute | solution.py:233
  81.7 1.5 %collective-permute-start.13 = (bf16[2,256,640]{2,1,0:T(8,128)(2,1)S(1)}, bf16[2,256,640]{2,1,0:T(8,128)(2,1)S(1)}, u32[]{:S(2)}, u32[]{:S(2)}) collective-permute-start(bf16[2,256,640]{2,1,0:T(8,128)(2,1)S(1)} %get-tuple-element.31), channel_id=1, source_target_pairs={{0,2},{1,3},{2,0},{3,1},{4,6},{5,7},{6,4},{7,5},{8,10},{9,11},{10,... | collective-permute-start | bytes 1966088 | tf_op jit(solution)/shard_map/ppermute | solution.py:233
  83.2 0.1 add_convert_fusion.unread
  83.3 2.8 %collective-permute-start.17 = (bf16[2,320,256]{2,1,0:T(8,128)(2,1)S(1)}, bf16[2,320,256]{2,1,0:T(8,128)(2,1)S(1)}, u32[]{:S(2)}, u32[]{:S(2)}) collective-permute-start(bf16[2,320,256]{2,1,0:T(8,128)(2,1)S(1)} %add_convert_fusion.unread), channel_id=1, source_target_pairs={{0,16},{4,20},{8,24},{12,28},{16,0},{20,4},{24,8},{28,12},{1,17},{... | collective-permute-start | bytes 983048 | tf_op jit(solution)/shard_map/ppermute | solution.py:222
  86.1 4.5 %grad_value.1 = (bf16[2,320,256]{2,1,0:T(8,128)(2,1)S(1)}, bf16[2,2,320,256]{3,2,1,0:T(8,128)(2,1)S(1)}, bf16[2,320,256]{2,1,0:T(8,128)(2,1)S(1)}, bf16[2,320,256]{2,1,0:T(8,128)(2,1)S(1)}) custom-call(s32[5]{0:T(128)S(1)} %stack.76.idx, bf16[16,128]{1,0:T(8,128)(2,1)S(1)} %get-tuple-element.32.token, bf16[2,320,256]{2,1,0:T(8,128)(2,1)S(1)} %add_convert_fusion.unread, ...), custom_call_target="tpu_custom_call" | custom-call | flops 1342177280 | bytes 12582912 | tf_op jit(solution)/shard_map/grad_value/pallas_call | solution.py:373
  90.6 0.3 collective-permute-start.18
  90.9 1.8 %collective-permute-start.16 = (bf16[2,2,320,256]{3,2,1,0:T(8,128)(2,1)S(1)}, bf16[2,2,320,256]{3,2,1,0:T(8,128)(2,1)S(1)}, u32[]{:S(2)}, u32[]{:S(2)}) collective-permute-start(bf16[2,2,320,256]{3,2,1,0:T(8,128)(2,1)S(1)} %get-tuple-element.37), channel_id=1, source_target_pairs={{0,8},{4,12},{8,0},{12,4},{16,24},{20,28},{24,16},{28,20},{1,9},{5... | collective-permute-start | bytes 1966088 | tf_op jit(solution)/shard_map/ppermute | solution.py:222
  92.7 8.0 %collective-permute-done.17.unread = bf16[2,320,256]{2,1,0:T(8,128)(2,1)S(1)} collective-permute-done((bf16[2,320,256]{2,1,0:T(8,128)(2,1)S(1)}, bf16[2,320,256]{2,1,0:T(8,128)(2,1)S(1)}, u32[]{:S(2)}, u32[]{:S(2)}) %collective-permute-start.17) | collective-permute-done | bytes 327712 | tf_op jit(solution)/shard_map/ppermute | solution.py:222
  100.7 6.1 %collective-permute-done.18.got = bf16[2,320,256]{2,1,0:T(8,128)(2,1)S(1)} collective-permute-done((bf16[2,320,256]{2,1,0:T(8,128)(2,1)S(1)}, bf16[2,320,256]{2,1,0:T(8,128)(2,1)S(1)}, u32[]{:S(2)}, u32[]{:S(2)}) %collective-permute-start.18) | collective-permute-done | bytes 327712 | tf_op jit(solution)/shard_map/ppermute | solution.py:222
  106.8 0.1 sum.1
  106.9 0.1 collective-permute-start.19
  106.9 0.2 convert_element_type.65
  107.1 0.1 convert_element_type.66
  107.2 0.1 convert_element_type.70
  107.4 0.2 fusion.10
  107.5 0.6 collective-permute-start.12
  108.1 0.5 collective-permute-start.14
  108.6 17.9 %collective-permute-done.16 = bf16[2,2,320,256]{3,2,1,0:T(8,128)(2,1)S(1)} collective-permute-done((bf16[2,2,320,256]{3,2,1,0:T(8,128)(2,1)S(1)}, bf16[2,2,320,256]{3,2,1,0:T(8,128)(2,1)S(1)}, u32[]{:S(2)}, u32[]{:S(2)}) %collective-permute-start.16) | collective-permute-done | bytes 655392 | tf_op jit(solution)/shard_map/ppermute | solution.py:222
  126.5 0.2 fusion.8
  126.8 0.1 collective-permute-start.21
  126.9 0.6 collective-permute-start.20
  127.5 0.2 fusion.7
  127.7 0.9 pad_maximum_fusion.1
  128.7 0.9 pad_maximum_fusion.3
  129.7 0.9 pad_maximum_fusion.2
  (42 shorter events, 0.3 us)
Async XLA Ops:
  0.6 3.6 %copy-start = (bf16[2,2,128,2560]{3,2,1,0:T(8,128)(2,1)S(1)}, bf16[2,2,128,2560]{3,2,1,0:T(8,128)(2,1)}, u32[]{:S(2)}) copy-start(bf16[2,2,128,2560]{3,2,1,0:T(8,128)(2,1)} %param.7) | copy-start | bytes 7864324
  2.1 1.8 %collective-permute-start = (bf16[2,320,256]{2,1,0:T(8,128)(2,1)S(1)}, bf16[2,320,256]{2,1,0:T(8,128)(2,1)S(1)}, u32[]{:S(2)}, u32[]{:S(2)}) collective-permute-start(bf16[2,320,256]{2,1,0:T(8,128)(2,1)S(1)} %get-tuple-element.52), channel_id=1, source_target_pairs={{0,4},{4,0},{8,12},{12,8},{16,20},{20,16},{24,28},{28,24},{1,5},{5... | collective-permute-start | bytes 983048 | tf_op jit(solution)/shard_map/ppermute | solution.py:230
  3.8 43.4 %collective-permute-start.1 = (bf16[512,2560]{1,0:T(8,128)(2,1)}, bf16[512,2560]{1,0:T(8,128)(2,1)}, u32[]{:S(2)}, u32[]{:S(2)}) collective-permute-start(bf16[512,2560]{1,0:T(8,128)(2,1)} %bitcast.70), channel_id=1, source_target_pairs={{0,4},{4,0},{8,12},{12,8},{16,20},{20,16},{24,28},{28,24},{1,5},{5... | collective-permute-start | bytes 7864328 | tf_op jit(solution)/shard_map/ppermute | solution.py:230
  4.2 52.3 %collective-permute-start.7 = (bf16[512,2560]{1,0:T(8,128)(2,1)S(1)}, bf16[512,2560]{1,0:T(8,128)(2,1)}, u32[]{:S(2)}, u32[]{:S(2)}) collective-permute-start(bf16[512,2560]{1,0:T(8,128)(2,1)S(1)} %bitcast.67), channel_id=1, source_target_pairs={{0,4},{4,0},{8,12},{12,8},{16,20},{20,16},{24,28},{28,24},{1,5},{5... | collective-permute-start | bytes 7864328 | tf_op jit(solution)/shard_map/ppermute | solution.py:230
  4.4 42.8 %collective-permute-start.2 = (bf16[4,8,128,128]{3,2,1,0:T(8,128)(2,1)}, bf16[4,8,128,128]{3,2,1,0:T(8,128)(2,1)}, u32[]{:S(2)}, u32[]{:S(2)}) collective-permute-start(bf16[4,8,128,128]{3,2,1,0:T(8,128)(2,1)} %bitcast.73), channel_id=1, source_target_pairs={{0,4},{4,0},{8,12},{12,8},{16,20},{20,16},{24,28},{28,24},{1,5},{5... | collective-permute-start | bytes 3145736 | tf_op jit(solution)/shard_map/ppermute | solution.py:230
  5.7 28.0 %copy-start.5 = (bf16[2,320,256]{2,1,0:T(8,128)(2,1)}, bf16[2,320,256]{2,1,0:T(8,128)(2,1)S(1)}, u32[]{:S(2)}) copy-start(bf16[2,320,256]{2,1,0:T(8,128)(2,1)S(1)} %get-tuple-element.56.rest_0_) | copy-start | bytes 983044
  5.7 27.9 %collective-permute-start.3 = (bf16[2,2,320,256]{3,2,1,0:T(8,128)(2,1)S(1)}, bf16[2,2,320,256]{3,2,1,0:T(8,128)(2,1)S(1)}, u32[]{:S(2)}, u32[]{:S(2)}) collective-permute-start(bf16[2,2,320,256]{3,2,1,0:T(8,128)(2,1)S(1)} %pad_maximum_fusion), channel_id=1, source_target_pairs={{0,8},{4,12},{8,0},{12,4},{16,24},{20,28},{24,16},{28,20},{1,9},{5... | collective-permute-start | bytes 1966088 | tf_op jit(solution)/shard_map/ppermute | solution.py:222
  8.5 21.5 %collective-permute-start.4 = (bf16[2,320,256]{2,1,0:T(8,128)(2,1)S(1)}, bf16[2,320,256]{2,1,0:T(8,128)(2,1)}, u32[]{:S(2)}, u32[]{:S(2)}) collective-permute-start(bf16[2,320,256]{2,1,0:T(8,128)(2,1)S(1)} %get-tuple-element.56.rest_0_), channel_id=1, source_target_pairs={{0,16},{4,20},{8,24},{12,28},{16,0},{20,4},{24,8},{28,12},{1,17},{... | collective-permute-start | bytes 983048 | tf_op jit(solution)/shard_map/ppermute | solution.py:222
  30.1 17.1 %collective-permute-start.5 = (bf16[2,320,256]{2,1,0:T(8,128)(2,1)}, bf16[2,320,256]{2,1,0:T(8,128)(2,1)}, u32[]{:S(2)}, u32[]{:S(2)}) collective-permute-start(bf16[2,320,256]{2,1,0:T(8,128)(2,1)} %collective-permute-done.4.rest_2_), channel_id=1, source_target_pairs={{0,8},{4,12},{8,0},{12,4},{16,24},{20,28},{24,16},{28,20},{1,9},{5... | collective-permute-start | bytes 983048 | tf_op jit(solution)/shard_map/ppermute | solution.py:222
  33.7 22.8 %collective-permute-start.8 = (bf16[2,320,256]{2,1,0:T(8,128)(2,1)}, bf16[2,320,256]{2,1,0:T(8,128)(2,1)}, u32[]{:S(2)}, u32[]{:S(2)}) collective-permute-start(bf16[2,320,256]{2,1,0:T(8,128)(2,1)} %get-tuple-element.53.rest_0_), channel_id=1, source_target_pairs={{0,16},{4,20},{8,24},{12,28},{16,0},{20,4},{24,8},{28,12},{1,17},{... | collective-permute-start | bytes 983048 | tf_op jit(solution)/shard_map/ppermute | solution.py:222
  47.2 1.7 %copy-start.1 = (bf16[2,2,128,2560]{3,2,1,0:T(8,128)(2,1)S(1)}, bf16[2,2,128,2560]{3,2,1,0:T(8,128)(2,1)}, u32[]{:S(2)}) copy-start(bf16[2,2,128,2560]{3,2,1,0:T(8,128)(2,1)} %param.5) | copy-start | bytes 7864324
  48.9 1.2 copy-start.3
  50.2 1.0 copy-start.6
  56.4 1.6 %collective-permute-start.6 = (bf16[512,256]{1,0:T(8,128)(2,1)S(1)}, bf16[512,256]{1,0:T(8,128)(2,1)S(1)}, u32[]{:S(2)}, u32[]{:S(2)}) collective-permute-start(bf16[512,256]{1,0:T(8,128)(2,1)S(1)} %get-tuple-element.26.mixed_s), channel_id=1, source_target_pairs={{0,4},{4,0},{8,12},{12,8},{16,20},{20,16},{24,28},{28,24},{1,5},{5... | collective-permute-start | bytes 786440 | tf_op jit(solution)/shard_map/ppermute | solution.py:230
  56.5 10.3 %collective-permute-start.9 = (bf16[2,320,256]{2,1,0:T(8,128)(2,1)}, bf16[2,320,256]{2,1,0:T(8,128)(2,1)S(1)}, u32[]{:S(2)}, u32[]{:S(2)}) collective-permute-start(bf16[2,320,256]{2,1,0:T(8,128)(2,1)} %collective-permute-done.8.rest_2_), channel_id=1, source_target_pairs={{0,8},{4,12},{8,0},{12,4},{16,24},{20,28},{24,16},{28,20},{1,9},{5... | collective-permute-start | bytes 983048 | tf_op jit(solution)/shard_map/ppermute | solution.py:222
  58.0 4.6 %copy-start.13 = (bf16[512,256]{1,0:T(8,128)(2,1)}, bf16[512,256]{1,0:T(8,128)(2,1)S(1)}, u32[]{:S(2)}) copy-start(bf16[512,256]{1,0:T(8,128)(2,1)S(1)} %collective-permute-done.6.unread.mixed_r) | copy-start | bytes 786436
  62.6 6.5 %copy-start.7 = (bf16[2,320,256]{2,1,0:T(8,128)(2,1)}, bf16[2,320,256]{2,1,0:T(8,128)(2,1)S(1)}, u32[]{:S(2)}) copy-start(bf16[2,320,256]{2,1,0:T(8,128)(2,1)S(1)} %get-tuple-element.35.rest_0_) | copy-start | bytes 983044
  62.6 6.5 %copy-start.9 = (bf16[2,320,256]{2,1,0:T(8,128)(2,1)}, bf16[2,320,256]{2,1,0:T(8,128)(2,1)S(1)}, u32[]{:S(2)}) copy-start(bf16[2,320,256]{2,1,0:T(8,128)(2,1)S(1)} %get-tuple-element.40) | copy-start | bytes 983044
  62.6 6.5 %copy-start.11 = (bf16[2,320,256]{2,1,0:T(8,128)(2,1)}, bf16[2,320,256]{2,1,0:T(8,128)(2,1)S(1)}, u32[]{:S(2)}) copy-start(bf16[2,320,256]{2,1,0:T(8,128)(2,1)S(1)} %get-tuple-element.33) | copy-start | bytes 983044
  62.6 6.5 %copy-start.15 = (bf16[2,320,256]{2,1,0:T(8,128)(2,1)}, bf16[2,320,256]{2,1,0:T(8,128)(2,1)S(1)}, u32[]{:S(2)}) copy-start(bf16[2,320,256]{2,1,0:T(8,128)(2,1)S(1)} %get-tuple-element.34) | copy-start | bytes 983044
  69.1 7.3 %collective-permute-start.10 = (bf16[2560,256]{1,0:T(8,128)(2,1)}, bf16[2560,256]{1,0:T(8,128)(2,1)}, u32[]{:S(2)}, u32[]{:S(2)}) collective-permute-start(bf16[2560,256]{1,0:T(8,128)(2,1)} %assemble.1.w_o.w_out), channel_id=1, source_target_pairs={{0,4},{4,0},{8,12},{12,8},{16,20},{20,16},{24,28},{28,24},{1,5},{5... | collective-permute-start | bytes 3932168 | tf_op jit(solution)/shard_map/ppermute | solution.py:230
  69.2 14.0 %collective-permute-start.15 = (bf16[2,320,256]{2,1,0:T(8,128)(2,1)}, bf16[2,320,256]{2,1,0:T(8,128)(2,1)S(1)}, u32[]{:S(2)}, u32[]{:S(2)}) collective-permute-start(bf16[2,320,256]{2,1,0:T(8,128)(2,1)} %copy-done.15), channel_id=1, source_target_pairs={{0,8},{4,12},{8,0},{12,4},{16,24},{20,28},{24,16},{28,20},{1,9},{5... | collective-permute-start | bytes 983048 | tf_op jit(solution)/shard_map/ppermute | solution.py:222
  69.6 1.2 copy-start.4
  70.8 5.6 %copy-start.14 = (bf16[512,256]{1,0:T(8,128)(2,1)S(1)}, bf16[512,256]{1,0:T(8,128)(2,1)}, u32[]{:S(2)}) copy-start(bf16[512,256]{1,0:T(8,128)(2,1)} %copy-done.13) | copy-start | bytes 786436
  76.4 6.8 %copy-start.12 = (bf16[2,320,256]{2,1,0:T(8,128)(2,1)S(1)}, bf16[2,320,256]{2,1,0:T(8,128)(2,1)}, u32[]{:S(2)}) copy-start(bf16[2,320,256]{2,1,0:T(8,128)(2,1)} %copy-done.11) | copy-start | bytes 983044
  76.4 9.8 %copy-start.8 = (bf16[2,320,256]{2,1,0:T(8,128)(2,1)S(1)}, bf16[2,320,256]{2,1,0:T(8,128)(2,1)}, u32[]{:S(2)}) copy-start(bf16[2,320,256]{2,1,0:T(8,128)(2,1)} %copy-done.7) | copy-start | bytes 983044
  76.4 9.7 %copy-start.2 = (bf16[2,2,128,2560]{3,2,1,0:T(8,128)(2,1)S(1)}, bf16[2,2,128,2560]{3,2,1,0:T(8,128)(2,1)}, u32[]{:S(2)}) copy-start(bf16[2,2,128,2560]{3,2,1,0:T(8,128)(2,1)} %param.5) | copy-start | bytes 7864324
  80.1 27.0 %collective-permute-start.11 = (bf16[2,256,640]{2,1,0:T(8,128)(2,1)S(1)}, bf16[2,256,640]{2,1,0:T(8,128)(2,1)S(1)}, u32[]{:S(2)}, u32[]{:S(2)}) collective-permute-start(bf16[2,256,640]{2,1,0:T(8,128)(2,1)S(1)} %get-tuple-element.30), channel_id=1, source_target_pairs={{0,1},{1,0},{2,3},{3,2},{4,5},{5,4},{6,7},{7,6},{8,9},{9,8},{10,11... | collective-permute-start | bytes 1966088 | tf_op jit(solution)/shard_map/ppermute | solution.py:233
  81.7 25.6 %collective-permute-start.13 = (bf16[2,256,640]{2,1,0:T(8,128)(2,1)S(1)}, bf16[2,256,640]{2,1,0:T(8,128)(2,1)S(1)}, u32[]{:S(2)}, u32[]{:S(2)}) collective-permute-start(bf16[2,256,640]{2,1,0:T(8,128)(2,1)S(1)} %get-tuple-element.31), channel_id=1, source_target_pairs={{0,2},{1,3},{2,0},{3,1},{4,6},{5,7},{6,4},{7,5},{8,10},{9,11},{10,... | collective-permute-start | bytes 1966088 | tf_op jit(solution)/shard_map/ppermute | solution.py:233
  83.3 17.4 %collective-permute-start.17 = (bf16[2,320,256]{2,1,0:T(8,128)(2,1)S(1)}, bf16[2,320,256]{2,1,0:T(8,128)(2,1)S(1)}, u32[]{:S(2)}, u32[]{:S(2)}) collective-permute-start(bf16[2,320,256]{2,1,0:T(8,128)(2,1)S(1)} %add_convert_fusion.unread), channel_id=1, source_target_pairs={{0,16},{4,20},{8,24},{12,28},{16,0},{20,4},{24,8},{28,12},{1,17},{... | collective-permute-start | bytes 983048 | tf_op jit(solution)/shard_map/ppermute | solution.py:222
  90.6 16.2 %collective-permute-start.18 = (bf16[2,320,256]{2,1,0:T(8,128)(2,1)S(1)}, bf16[2,320,256]{2,1,0:T(8,128)(2,1)S(1)}, u32[]{:S(2)}, u32[]{:S(2)}) collective-permute-start(bf16[2,320,256]{2,1,0:T(8,128)(2,1)S(1)} %get-tuple-element.39), channel_id=1, source_target_pairs={{0,8},{4,12},{8,0},{12,4},{16,24},{20,28},{24,16},{28,20},{1,9},{5... | collective-permute-start | bytes 983048 | tf_op jit(solution)/shard_map/ppermute | solution.py:222
  90.9 35.6 %collective-permute-start.16 = (bf16[2,2,320,256]{3,2,1,0:T(8,128)(2,1)S(1)}, bf16[2,2,320,256]{3,2,1,0:T(8,128)(2,1)S(1)}, u32[]{:S(2)}, u32[]{:S(2)}) collective-permute-start(bf16[2,2,320,256]{3,2,1,0:T(8,128)(2,1)S(1)} %get-tuple-element.37), channel_id=1, source_target_pairs={{0,8},{4,12},{8,0},{12,4},{16,24},{20,28},{24,16},{28,20},{1,9},{5... | collective-permute-start | bytes 1966088 | tf_op jit(solution)/shard_map/ppermute | solution.py:222
  106.9 19.7 %collective-permute-start.19 = (bf16[2,320,256]{2,1,0:T(8,128)(2,1)S(1)}, bf16[2,320,256]{2,1,0:T(8,128)(2,1)S(1)}, u32[]{:S(2)}, u32[]{:S(2)}) collective-permute-start(bf16[2,320,256]{2,1,0:T(8,128)(2,1)S(1)} %sum.1), channel_id=1, source_target_pairs={{0,16},{4,20},{8,24},{12,28},{16,0},{20,4},{24,8},{28,12},{1,17},{... | collective-permute-start | bytes 983048 | tf_op jit(solution)/shard_map/ppermute | solution.py:222
  107.3 19.2 %copy-start.10 = (bf16[2,320,256]{2,1,0:T(8,128)(2,1)S(1)}, bf16[2,320,256]{2,1,0:T(8,128)(2,1)}, u32[]{:S(2)}) copy-start(bf16[2,320,256]{2,1,0:T(8,128)(2,1)} %copy-done.9) | copy-start | bytes 983044
  107.5 19.9 %collective-permute-start.12 = (bf16[256,640]{1,0:T(8,128)(2,1)S(1)}, bf16[256,640]{1,0:T(8,128)(2,1)S(1)}, u32[]{:S(2)}, u32[]{:S(2)}) collective-permute-start(bf16[256,640]{1,0:T(8,128)(2,1)S(1)} %get-tuple-element.43), channel_id=1, source_target_pairs={{0,2},{1,3},{2,0},{3,1},{4,6},{5,7},{6,4},{7,5},{8,10},{9,11},{10,... | collective-permute-start | bytes 983048 | tf_op jit(solution)/shard_map/ppermute | solution.py:233
  108.1 19.4 %collective-permute-start.14 = (bf16[256,640]{1,0:T(8,128)(2,1)S(1)}, bf16[256,640]{1,0:T(8,128)(2,1)S(1)}, u32[]{:S(2)}, u32[]{:S(2)}) collective-permute-start(bf16[256,640]{1,0:T(8,128)(2,1)S(1)} %get-tuple-element.44), channel_id=1, source_target_pairs={{0,1},{1,0},{2,3},{3,2},{4,5},{5,4},{6,7},{7,6},{8,9},{9,8},{10,11... | collective-permute-start | bytes 983048 | tf_op jit(solution)/shard_map/ppermute | solution.py:233
  126.8 1.8 %collective-permute-start.21 = (f32[320,256]{1,0:T(8,128)S(1)}, f32[320,256]{1,0:T(8,128)S(1)}, u32[]{:S(2)}, u32[]{:S(2)}) collective-permute-start(f32[320,256]{1,0:T(8,128)S(1)} %slice_bitcast_fusion), channel_id=1, source_target_pairs={{0,4},{4,0},{8,12},{12,8},{16,20},{20,16},{24,28},{28,24},{1,5},{5... | collective-permute-start | bytes 983048 | tf_op jit(solution)/shard_map/ppermute | solution.py:230
  126.9 2.7 %collective-permute-start.20 = (f32[320,256]{1,0:T(8,128)S(1)}, f32[320,256]{1,0:T(8,128)S(1)}, u32[]{:S(2)}, u32[]{:S(2)}) collective-permute-start(f32[320,256]{1,0:T(8,128)S(1)} %slice_bitcast_fusion.3), channel_id=1, source_target_pairs={{0,4},{4,0},{8,12},{12,8},{16,20},{20,16},{24,28},{28,24},{1,5},{5... | collective-permute-start | bytes 983048 | tf_op jit(solution)/shard_map/ppermute | solution.py:230

commit v10 on v9

--- a/solution.py
+++ b/solution.py
@@ -100,9 +100,8 @@
                 ).astype(BF16)
 
 
-def gradient_kernel(n_near, idx, token, unread, right_o, right_s, left_ref, *rest):
+def gradient_kernel(idx, token, unread, right_o, right_s, left_ref, *rest):
     del token, unread
-    others, rest = rest[:n_near], rest[n_near:]
     outs, (right_v, grad_v, sems) = rest[:-3], rest[-3:]
     tokens, _ = right_o.shape
     copies = begin(
@@ -112,9 +111,7 @@
     copies[0].wait()
     copies[1].wait()
     gradient_rows(left_ref[...], right_v, grad_v, 640)
-    for other in others:
-        outs[1][1] = other[...]
-    hand_out(idx, 1, grad_v, [outs[0], outs[1].at[0], *outs[2:]] if n_near else outs)
+    hand_out(idx, 1, grad_v, outs)
 
 
 def mixed_kernel(n_slots, idx, act_o, act_s, mix_o, mix_s, *rest):
@@ -152,8 +149,8 @@
                 ).astype(BF16)
 
 
-def grad_out_kernel(idx, cot_o, cot_s, mixed_o, mixed_s, unread, token, *rest):
-    del unread
+def grad_out_kernel(n_unread, idx, cot_o, cot_s, mixed_o, mixed_s, *rest):
+    token, *rest = rest[n_unread:]
     outs, (cot_v, left_v, grad_v, sems) = rest[:-4], rest[-4:]
     token[...] = jnp.zeros_like(token)
     tokens, _ = cot_o.shape
@@ -168,9 +165,15 @@
     hand_out(idx, 1, grad_v, outs)
 
 
-def sum_kernel(unread, block, got, out):
+def release_kernel(unread, block, out):
     del unread
-    out[...] = (block[...].astype(F32) + got[...].astype(F32)).astype(BF16)
+    out[...] = block[...]
+
+
+def sum_kernel(block, got, beside, own, near, far, onward, beside_out, total):
+    onward[...] = (block[...].astype(F32) + got[...].astype(F32)).astype(BF16)
+    beside_out[...] = beside[...]
+    total[...] = own[...].astype(F32) + near[...].astype(F32) + far[...].astype(F32)
 
 
 def terms_kernel(n_node, idx, mixed_o, mixed_r, w_o, w_r, token, *outs):
@@ -201,13 +204,15 @@
 VMEM = pl.BlockSpec(memory_space=pltpu.VMEM)
 
 
-def call(kernel, name, in_specs, out_shapes, scratch, flops):
+def call(kernel, name, in_specs, out_shapes, scratch, flops, kinds=None):
     return pl.pallas_call(
         kernel,
         name=name,
         in_specs=in_specs,
         out_specs=[VMEM] * len(out_shapes),
-        out_shape=[jax.ShapeDtypeStruct(s, BF16) for s in out_shapes],
+        out_shape=[
+            jax.ShapeDtypeStruct(s, k) for s, k in zip(out_shapes, kinds or [BF16] * len(out_shapes))
+        ],
         scratch_shapes=scratch,
         compiler_params=pltpu.CompilerParams(vmem_limit_bytes=VMEM_LIMIT),
         cost_estimate=pl.CostEstimate(flops=flops, bytes_accessed=12 << 20, transcendentals=0),
@@ -255,15 +260,9 @@
     def added(block, got):
         return (block.astype(F32) + got.astype(F32)).astype(BF16)
 
-    def gather_two(u_value, u_out):
-        if not line4:
-            return gather_ring(u_value), gather_ring(u_out)
-        beside = swap(jnp.stack([u_value, u_out]), 1)
-        far_value, far_out = swap(u_value, 2), swap(u_out, 2)
-        return (
-            [u_value, beside, far_value, swap(far_value, 1)],
-            [u_out, beside, far_out, swap(far_out, 1)],
-        )
+    def gather_steps(u):
+        far = swap(u, 2)
+        return [u, swap(u, 1), far, swap(far, 1)]
 
     def scatter_end(own, got, c):
         total = own.astype(F32)
@@ -299,7 +298,15 @@
         flops = 4 * tokens * width * cols
 
         u_out, u_value, act_s, mix_s, cot_s = swap_cores(w_out, w_value, act, mix, cot, c)
-        value_slots, out_slots = gather_two(u_value, u_out)
+        block = u_out.shape
+        if line4:
+            value_slots = gather_steps(u_value)
+            u_out = call(release_kernel, "release", [ANY, VMEM], [block], [], 0)(
+                value_slots[3], u_out
+            )[0]
+            out_slots = gather_steps(u_out)
+        else:
+            value_slots, out_slots = gather_ring(u_value), gather_ring(u_out)
         n_slots = len(out_slots)
         pack = lambda *values: jnp.stack([jnp.int32(x) for x in values])
         idx = pack(c, *planes_of(z))
@@ -310,7 +317,6 @@
         halves = pltpu.VMEM((2, tokens, width), BF16)
         left_tokens = pltpu.VMEM((cols, 2 * tokens), BF16)
         rows = pltpu.VMEM((width, cols), BF16)
-        block = (2, depth // 2, cols)
         send_shapes = [block] * n_slots
 
         mixed_o, mixed_s = call(
@@ -322,14 +328,15 @@
             flops,
         )(idx, act, act_s, mix, mix_s, *value_slots)
         mixed_r = sibling(mixed_s)
+        unread = [mixed_r, *(out_slots[1:3] if line4 else [])]
         token, *out_sends = call(
-            grad_out_kernel,
+            functools.partial(grad_out_kernel, len(unread)),
             "grad_out",
-            [SMEM] + [ANY] * 2 + [VMEM] * 2 + [ANY],
+            [SMEM] + [ANY] * 2 + [VMEM] * 2 + [ANY] * len(unread),
             [(16, 128)] + send_shapes,
             [both, left_tokens, rows, pltpu.SemaphoreType.DMA((2,))],
             flops,
-        )(idx, cot, cot_s, mixed_o, mixed_s, mixed_r)
+        )(idx, cot, cot_s, mixed_o, mixed_s, *unread)
         out_passed = swap(out_sends[3], 1) if line4 else token
         w_full = call(
             assemble_kernel,
@@ -351,10 +358,9 @@
         if line4:
             out_onward = added(out_sends[2], out_passed)
             out_far = swap(out_onward, 2)
-            others = [out_sends[1]]
-            back_shapes = [block, (2, *block), block, block]
-        else:
-            out_onward, others, back_shapes = token, [], send_shapes
+            out_near = swap(out_sends[1], 1)
+        else:
+            out_onward = token
         part = width // n_node
         half = tokens // 2
         if n_node == 4:
@@ -371,21 +377,21 @@
         )(idx_node, mixed_o, mixed_r, w_full, w_full_s)
 
         back_sends = call(
-            functools.partial(gradient_kernel, len(others)),
+            gradient_kernel,
             "grad_value",
-            [SMEM] + [ANY] * 4 + [VMEM] * (1 + len(others)),
-            back_shapes,
+            [SMEM] + [ANY] * 4 + [VMEM],
+            send_shapes,
             [both, rows, pltpu.SemaphoreType.DMA((2,))],
             flops,
-        )(idx, token, out_onward, act, act_s, left, *others)
+        )(idx, token, out_onward, act, act_s, left)
         if line4:
-            near = swap(back_sends[1], 1)
             back_passed = swap(back_sends[3], 1)
-            onward = call(sum_kernel, "sum", [ANY] + [VMEM] * 2, [block], [], 0)(
-                out_far, back_sends[2], back_passed
-            )[0]
-            grad_out = scatter_end(out_sends[0], (near[1], out_far), c)
-            grad_value = scatter_end(back_sends[0], (near[0], swap(onward, 2)), c)
+            onward, beside, out_total = call(
+                sum_kernel, "sum", [VMEM] * 6, [block] * 3, [], 0, [BF16, BF16, F32]
+            )(back_sends[2], back_passed, back_sends[1], out_sends[0], out_near, out_far)
+            back_far, back_near = swap(onward, 2), swap(beside, 1)
+            grad_out = join(out_total[0], sibling(out_total[1]), c)
+            grad_value = scatter_end(back_sends[0], (back_near, back_far), c)
         else:
             grad_value = scatter_ring(back_sends, c)
             grad_out = scatter_ring(out_sends, c)

time: 131 us -> 125 us (0.954)
  waiting for transfers between devices: 71.2 us -> 61.7 us
  starting transfers between devices: 20.8 us -> 23.5 us
    ppermute x10 -> x12, waiting for transfers between devices: 68.5 us -> 60.4 us  [move(): lax.ppermute(x, 'wide', [(2 * s + c, 2 * d + c) for s, d in pairs for c i...]
    ppermute x10 -> x12, starting transfers between devices: 14.4 us -> 17.1 us  [move(): lax.ppermute(x, 'wide', [(2 * s + c, 2 * d + c) for s, d in pairs for c i...]
    pallas_call x3 -> x4, Pallas kernels: 9.1 us -> 10.7 us  [the longest x1 5.29 us: body(): call(functools.partial(grad_out_kernel, len(unread)), 'grad_out', [SMEM]...]
    ppermute x8, waiting for transfers between devices: 2.69 us -> 1.27 us  [sibling(): return lax.ppermute(x, 'wide', [(i, i ^ 1) for i in range(n_wide)])]
    unnamed x32 -> x20, local copies, waits for them, and re-layouts: 5.22 us -> 5.18 us
  transfers between devices with their start and end apart: 22 -> 24, of which waited for: 8 -> 10; matrix products, arithmetic and copies ran while one was open for 3% -> 3% of each run, Pallas kernels for 18% -> 20%
where the time goes in v10:
time: 125 us
  waiting for transfers between devices  61.7 us (49%)
  Pallas kernels  27.1 us (22%)
  starting transfers between devices  23.5 us (19%)
  local copies, waits for them, and re-layouts  6.7 us (5%)
  other arithmetic  4.94 us (4%)
    ppermute x12, waiting for transfers between devices, move(): lax.ppermute(x, 'wide', [(2 * s + c, 2 * d + c) for s, d in pairs for c i...  60.4 us
    ppermute x12, starting transfers between devices, move(): lax.ppermute(x, 'wide', [(2 * s + c, 2 * d + c) for s, d in pairs for c i...  17.1 us
    pallas_call x1, Pallas kernels, body(): call(d_value_kernel, 'd_value', [SMEM] + [ANY] * 4 + [VMEM], [(cols, 2 *...  5.53 us
    pallas_call x1, Pallas kernels, body(): call(functools.partial(grad_out_kernel, len(unread)), 'grad_out', [SMEM]...  5.29 us
    unnamed x20, local copies, waits for them, and re-layouts  5.18 us
    pallas_call x1, Pallas kernels, body(): call(functools.partial(mixed_kernel, n_slots), 'mixed', [SMEM] + [ANY] *...  5.12 us
    ppermute x4, starting transfers between devices, flip(): return lax.ppermute(x, 'node', [(i, i ^ j) for i in range(n_node)])  4.68 us
    pallas_call x1, Pallas kernels, body(): call(gradient_kernel, 'grad_value', [SMEM] + [ANY] * 4 + [VMEM], send_sha...  4.44 us
  transfers between devices with their start and end apart: 24, of which 10 were waited for; matrix products, arithmetic and copies ran while one was open for 3% of the time, Pallas kernels for 20%

profile of v10, /device:TPU:0, one launch (start us, length us, event | category | flops | bytes accessed | tf_op | source)
XLA Modules:
  0.0 124.9 jit_solution(16358841592907062663)
XLA Ops:
  0.7 1.3 %slice_bitcast_fusion.5 = (bf16[1,320,256]{2,1,0:T(8,128)(2,1)S(1)}, bf16[1,320,256]{2,1,0:T(8,128)(2,1)S(1)}, bf16[1,320,256]{2,1,0:T(8,128)(2,1)S(1)}, bf16[1,320,256]{2,1,0:T(8,128)(2,1)S(1)}) fusion(bf16[320,512]{1,0:T(8,128)(2,1)} %param.8, bf16[320,512]{1,0:T(8,128)(2,1)} %param.9), kind=kLoop, calls=%fused_computation.34 | loop fusion | bytes 1310720 | tf_op jit(solution)/shard_map/stack | solution.py:243
  2.0 0.1 broadcast_select_fusion
  2.1 0.5 collective-permute-start
  2.6 1.3 %collective-permute-done = bf16[2,320,256]{2,1,0:T(8,128)(2,1)S(1)} collective-permute-done((bf16[2,320,256]{2,1,0:T(8,128)(2,1)S(1)}, bf16[2,320,256]{2,1,0:T(8,128)(2,1)S(1)}, u32[]{:S(2)}, u32[]{:S(2)}) %collective-permute-start) | collective-permute-done | bytes 327712 | tf_op jit(solution)/shard_map/ppermute | solution.py:235
  3.8 0.4 collective-permute-start.1
  4.2 0.1 collective-permute-start.7
  4.4 0.4 collective-permute-start.2
  4.9 3.8 %collective-permute-start.4 = (bf16[2,320,256]{2,1,0:T(8,128)(2,1)S(1)}, bf16[2,320,256]{2,1,0:T(8,128)(2,1)S(1)}, u32[]{:S(2)}, u32[]{:S(2)}) collective-permute-start(bf16[2,320,256]{2,1,0:T(8,128)(2,1)S(1)} %pad_maximum_fusion.5.rest_0_), channel_id=1, source_target_pairs={{0,16},{4,20},{8,24},{12,28},{16,0},{20,4},{24,8},{28,12},{1,17},{... | collective-permute-start | bytes 983048 | tf_op jit(solution)/shard_map/ppermute | solution.py:227
  8.7 15.3 %collective-permute-done.4.rest_2_ = bf16[2,320,256]{2,1,0:T(8,128)(2,1)S(1)} collective-permute-done((bf16[2,320,256]{2,1,0:T(8,128)(2,1)S(1)}, bf16[2,320,256]{2,1,0:T(8,128)(2,1)S(1)}, u32[]{:S(2)}, u32[]{:S(2)}) %collective-permute-start.4) | collective-permute-done | bytes 327712 | tf_op jit(solution)/shard_map/ppermute | solution.py:227
  23.9 0.7 collective-permute-start.5
  24.7 1.3 %collective-permute-start.3 = (bf16[2,320,256]{2,1,0:T(8,128)(2,1)S(1)}, bf16[2,320,256]{2,1,0:T(8,128)(2,1)}, u32[]{:S(2)}, u32[]{:S(2)}) collective-permute-start(bf16[2,320,256]{2,1,0:T(8,128)(2,1)S(1)} %pad_maximum_fusion.5.rest_0_), channel_id=1, source_target_pairs={{0,8},{4,12},{8,0},{12,4},{16,24},{20,28},{24,16},{28,20},{1,9},{5... | collective-permute-start | bytes 983048 | tf_op jit(solution)/shard_map/ppermute | solution.py:227
  26.0 8.5 %collective-permute-done.5.rest_3_.unread = bf16[2,320,256]{2,1,0:T(8,128)(2,1)S(1)} collective-permute-done((bf16[2,320,256]{2,1,0:T(8,128)(2,1)S(1)}, bf16[2,320,256]{2,1,0:T(8,128)(2,1)S(1)}, u32[]{:S(2)}, u32[]{:S(2)}) %collective-permute-start.5) | collective-permute-done | bytes 327712 | tf_op jit(solution)/shard_map/ppermute | solution.py:227
  34.6 0.7 release.1.rest_0_
  35.3 2.0 %collective-permute-start.9 = (bf16[2,320,256]{2,1,0:T(8,128)(2,1)}, bf16[2,320,256]{2,1,0:T(8,128)(2,1)}, u32[]{:S(2)}, u32[]{:S(2)}) collective-permute-start(bf16[2,320,256]{2,1,0:T(8,128)(2,1)} %release.1.rest_0_), channel_id=1, source_target_pairs={{0,16},{4,20},{8,24},{12,28},{16,0},{20,4},{24,8},{28,12},{1,17},{... | collective-permute-start | bytes 983048 | tf_op jit(solution)/shard_map/ppermute | solution.py:227
  37.3 0.1 stack.67.idx
  37.4 8.3 %collective-permute-done.3.rest_1_ = bf16[2,320,256]{2,1,0:T(8,128)(2,1)} collective-permute-done((bf16[2,320,256]{2,1,0:T(8,128)(2,1)S(1)}, bf16[2,320,256]{2,1,0:T(8,128)(2,1)}, u32[]{:S(2)}, u32[]{:S(2)}) %collective-permute-start.3) | collective-permute-done | bytes 327712 | tf_op jit(solution)/shard_map/ppermute | solution.py:227
  45.7 0.0 collective-permute-done.1.act_s.right_s
  45.7 0.0 copy-start.1
  45.7 1.7 %copy-done.1 = bf16[2,2,128,2560]{3,2,1,0:T(8,128)(2,1)S(1)} copy-done((bf16[2,2,128,2560]{3,2,1,0:T(8,128)(2,1)S(1)}, bf16[2,2,128,2560]{3,2,1,0:T(8,128)(2,1)}, u32[]{:S(2)}) %copy-start.1) | copy-done | bytes 2621464
  47.4 1.2 copy-done.3
  48.6 1.0 copy-done.6
  49.6 5.1 %mixed.1 = (bf16[512,256]{1,0:T(8,128)(2,1)S(1)}, bf16[512,256]{1,0:T(8,128)(2,1)S(1)}) custom-call(s32[5]{0:T(128)S(1)} %stack.67.idx, bf16[512,2560]{1,0:T(8,128)(2,1)S(1)} %bitcast.54, bf16[512,2560]{1,0:T(8,128)(2,1)} %collective-permute-done.1.act_s.right_s, bf16[4,8,128,128]{3,2,1,0:T(8,128)(2,1)S(1)} %bitcast.57, ...), custom_call_target="tpu_custom_call" | custom-call | flops 1342177280 | bytes 12582912 | tf_op jit(solution)/shard_map/mixed/pallas_call | solution.py:322
  54.7 0.1 collective-permute-start.6
  54.8 0.0 collective-permute-done.9.rest_2_
  54.8 2.1 %collective-permute-start.10 = (bf16[2,320,256]{2,1,0:T(8,128)(2,1)}, bf16[2,320,256]{2,1,0:T(8,128)(2,1)S(1)}, u32[]{:S(2)}, u32[]{:S(2)}) collective-permute-start(bf16[2,320,256]{2,1,0:T(8,128)(2,1)} %collective-permute-done.9.rest_2_), channel_id=1, source_target_pairs={{0,8},{4,12},{8,0},{12,4},{16,24},{20,28},{24,16},{28,20},{1,9},{5... | collective-permute-start | bytes 983048 | tf_op jit(solution)/shard_map/ppermute | solution.py:227
  56.9 0.0 collective-permute-done.8.rest_1_
  56.9 5.3 %grad_out.1 = (bf16[16,128]{1,0:T(8,128)(2,1)S(1)}, bf16[2,320,256]{2,1,0:T(8,128)(2,1)S(1)}, bf16[2,320,256]{2,1,0:T(8,128)(2,1)S(1)}, bf16[2,320,256]{2,1,0:T(8,128)(2,1)S(1)}, bf16[2,320,256]{2,1,0:T(8,128)(2,1)}) custom-call(s32[5]{0:T(128)S(1)} %stack.67.idx, bf16[512,2560]{1,0:T(8,128)(2,1)S(1)} %bitcast.51, ...), custom_call_target="tpu_custom_call" | custom-call | flops 1342177280 | bytes 12582912 | tf_op jit(solution)/shard_map/grad_out/pallas_call | solution.py:332
  62.3 0.0 copy-start.9
  62.3 3.2 %collective-permute-done.10.rest_3_ = bf16[2,320,256]{2,1,0:T(8,128)(2,1)S(1)} collective-permute-done((bf16[2,320,256]{2,1,0:T(8,128)(2,1)}, bf16[2,320,256]{2,1,0:T(8,128)(2,1)S(1)}, u32[]{:S(2)}, u32[]{:S(2)}) %collective-permute-start.10) | collective-permute-done | bytes 327712 | tf_op jit(solution)/shard_map/ppermute | solution.py:227
  65.4 2.3 %assemble.1.w_o.w_out = bf16[2560,256]{1,0:T(8,128)(2,1)} custom-call(s32[5]{0:T(128)S(1)} %stack.67.idx, bf16[16,128]{1,0:T(8,128)(2,1)S(1)} %get-tuple-element.31.token, bf16[2,320,256]{2,1,0:T(8,128)(2,1)} %release.1.rest_0_, bf16[2,320,256]{2,1,0:T(8,128)(2,1)S(1)} %collective-permute-done.8.rest_1_, ...), custom_call_target="tpu_custom_call" | custom-call | bytes 12582912 | tf_op jit(solution)/shard_map/assemble/pallas_call | solution.py:341
  67.7 1.8 %collective-permute-start.16 = (bf16[2,320,256]{2,1,0:T(8,128)(2,1)}, bf16[2,320,256]{2,1,0:T(8,128)(2,1)}, u32[]{:S(2)}, u32[]{:S(2)}) collective-permute-start(bf16[2,320,256]{2,1,0:T(8,128)(2,1)} %get-tuple-element.37), channel_id=1, source_target_pairs={{0,8},{4,12},{8,0},{12,4},{16,24},{20,28},{24,16},{28,20},{1,9},{5... | collective-permute-start | bytes 983048 | tf_op jit(solution)/shard_map/ppermute | solution.py:227
  69.5 0.1 pad_add_fusion.idx
  69.5 0.3 collective-permute-start.18
  69.8 1.2 copy-done.4
  71.0 5.5 %d_value.1.left_ref = bf16[256,1024]{1,0:T(8,128)(2,1)S(1)} custom-call(s32[5]{0:T(128)S(1)} %stack.67.idx, bf16[512,2560]{1,0:T(8,128)(2,1)S(1)} %bitcast.52, bf16[512,2560]{1,0:T(8,128)(2,1)} %collective-permute-done.7.cot_s, bf16[4,8,128,128]{3,2,1,0:T(8,128)(2,1)S(1)} %bitcast.58, bf16[4,8,128,128]{3,2,1,0:T(8,128)(2,1)} %collective-permute-done.2.mix_s, ...), custom_call_target="tpu_custom_call" | custom-call | flops 1342177280 | bytes 12582912 | tf_op jit(solution)/shard_map/d_value/pallas_call | solution.py:350
  76.6 2.0 %collective-permute-done.16 = bf16[2,320,256]{2,1,0:T(8,128)(2,1)} collective-permute-done((bf16[2,320,256]{2,1,0:T(8,128)(2,1)}, bf16[2,320,256]{2,1,0:T(8,128)(2,1)}, u32[]{:S(2)}, u32[]{:S(2)}) %collective-permute-start.16) | collective-permute-done | bytes 327712 | tf_op jit(solution)/shard_map/ppermute | solution.py:227
  78.5 1.1 add_convert_fusion.unread
  79.6 0.0 copy-start.2
  79.6 1.4 %collective-permute-start.19 = (bf16[2,320,256]{2,1,0:T(8,128)(2,1)S(1)}, bf16[2,320,256]{2,1,0:T(8,128)(2,1)S(1)}, u32[]{:S(2)}, u32[]{:S(2)}) collective-permute-start(bf16[2,320,256]{2,1,0:T(8,128)(2,1)S(1)} %add_convert_fusion.unread), channel_id=1, source_target_pairs={{0,16},{4,20},{8,24},{12,28},{16,0},{20,4},{24,8},{28,12},{1,17},{... | collective-permute-start | bytes 983048 | tf_op jit(solution)/shard_map/ppermute | solution.py:227
  81.0 3.6 %terms.1 = (bf16[16,128]{1,0:T(8,128)(2,1)S(1)}, bf16[2,256,640]{2,1,0:T(8,128)(2,1)S(1)}, bf16[2,256,640]{2,1,0:T(8,128)(2,1)S(1)}, bf16[4,256,640]{2,1,0:T(8,128)(2,1)S(1)}) custom-call(s32[4]{0:T(128)S(1)} %pad_add_fusion.idx, bf16[512,256]{1,0:T(8,128)(2,1)S(1)} %get-tuple-element.28.mixed_o, bf16[512,256]{1,0:T(8,128)(2,1)S(1)} %copy-done.8, ...), custom_call_target="tpu_custom_call" | custom-call | flops 1342177280 | bytes 12582912 | tf_op jit(solution)/shard_map/terms/pallas_call | solution.py:370
  84.6 1.6 %collective-permute-start.12 = (bf16[2,256,640]{2,1,0:T(8,128)(2,1)S(1)}, bf16[2,256,640]{2,1,0:T(8,128)(2,1)S(1)}, u32[]{:S(2)}, u32[]{:S(2)}) collective-permute-start(bf16[2,256,640]{2,1,0:T(8,128)(2,1)S(1)} %get-tuple-element.33), channel_id=1, source_target_pairs={{0,1},{1,0},{2,3},{3,2},{4,5},{5,4},{6,7},{7,6},{8,9},{9,8},{10,11... | collective-permute-start | bytes 1966088 | tf_op jit(solution)/shard_map/ppermute | solution.py:238
  86.1 1.5 %collective-permute-start.14 = (bf16[2,256,640]{2,1,0:T(8,128)(2,1)S(1)}, bf16[2,256,640]{2,1,0:T(8,128)(2,1)S(1)}, u32[]{:S(2)}, u32[]{:S(2)}) collective-permute-start(bf16[2,256,640]{2,1,0:T(8,128)(2,1)S(1)} %get-tuple-element.34), channel_id=1, source_target_pairs={{0,2},{1,3},{2,0},{3,1},{4,6},{5,7},{6,4},{7,5},{8,10},{9,11},{10,... | collective-permute-start | bytes 1966088 | tf_op jit(solution)/shard_map/ppermute | solution.py:238
  87.6 4.4 %grad_value.1 = (bf16[2,320,256]{2,1,0:T(8,128)(2,1)S(1)}, bf16[2,320,256]{2,1,0:T(8,128)(2,1)S(1)}, bf16[2,320,256]{2,1,0:T(8,128)(2,1)S(1)}, bf16[2,320,256]{2,1,0:T(8,128)(2,1)S(1)}) custom-call(s32[5]{0:T(128)S(1)} %stack.67.idx, bf16[16,128]{1,0:T(8,128)(2,1)S(1)} %get-tuple-element.35.token, bf16[2,320,256]{2,1,0:T(8,128)(2,1)S(1)} %add_convert_fusion.unread, ...), custom_call_target="tpu_custom_call" | custom-call | flops 1342177280 | bytes 12582912 | tf_op jit(solution)/shard_map/grad_value/pallas_call | solution.py:379
  92.1 1.3 %collective-permute-start.17 = (bf16[2,320,256]{2,1,0:T(8,128)(2,1)S(1)}, bf16[2,320,256]{2,1,0:T(8,128)(2,1)S(1)}, u32[]{:S(2)}, u32[]{:S(2)}) collective-permute-start(bf16[2,320,256]{2,1,0:T(8,128)(2,1)S(1)} %get-tuple-element.40), channel_id=1, source_target_pairs={{0,8},{4,12},{8,0},{12,4},{16,24},{20,28},{24,16},{28,20},{1,9},{5... | collective-permute-start | bytes 983048 | tf_op jit(solution)/shard_map/ppermute | solution.py:227
  93.3 0.2 convert_element_type.50
  93.5 3.2 %collective-permute-done.19.far = bf16[2,320,256]{2,1,0:T(8,128)(2,1)S(1)} collective-permute-done((bf16[2,320,256]{2,1,0:T(8,128)(2,1)S(1)}, bf16[2,320,256]{2,1,0:T(8,128)(2,1)S(1)}, u32[]{:S(2)}, u32[]{:S(2)}) %collective-permute-start.19) | collective-permute-done | bytes 327712 | tf_op jit(solution)/shard_map/ppermute | solution.py:227
  96.7 6.9 %collective-permute-done.17.got = bf16[2,320,256]{2,1,0:T(8,128)(2,1)S(1)} collective-permute-done((bf16[2,320,256]{2,1,0:T(8,128)(2,1)S(1)}, bf16[2,320,256]{2,1,0:T(8,128)(2,1)S(1)}, u32[]{:S(2)}, u32[]{:S(2)}) %collective-permute-start.17) | collective-permute-done | bytes 327712 | tf_op jit(solution)/shard_map/ppermute | solution.py:227
  103.6 0.2 sum.1
  103.8 0.1 collective-permute-start.20
  103.9 2.5 %collective-permute-start.21 = (bf16[2,320,256]{2,1,0:T(8,128)(2,1)S(1)}, bf16[2,320,256]{2,1,0:T(8,128)(2,1)S(1)}, u32[]{:S(2)}, u32[]{:S(2)}) collective-permute-start(bf16[2,320,256]{2,1,0:T(8,128)(2,1)S(1)} %get-tuple-element.45), channel_id=1, source_target_pairs={{0,16},{4,20},{8,24},{12,28},{16,0},{20,4},{24,8},{28,12},{1,17},{... | collective-permute-start | bytes 983048 | tf_op jit(solution)/shard_map/ppermute | solution.py:227
  106.4 0.1 collective-permute-start.23
  106.5 0.1 convert_element_type.51
  106.6 0.1 convert_element_type.55
  106.7 0.1 fusion.8
  106.8 0.9 collective-permute-start.13
  107.7 0.7 collective-permute-start.15
  108.5 11.4 %collective-permute-done.20 = bf16[2,320,256]{2,1,0:T(8,128)(2,1)S(1)} collective-permute-done((bf16[2,320,256]{2,1,0:T(8,128)(2,1)S(1)}, bf16[2,320,256]{2,1,0:T(8,128)(2,1)S(1)}, u32[]{:S(2)}, u32[]{:S(2)}) %collective-permute-start.20) | collective-permute-done | bytes 327712 | tf_op jit(solution)/shard_map/ppermute | solution.py:227
  119.8 1.8 %collective-permute-done.21 = bf16[2,320,256]{2,1,0:T(8,128)(2,1)S(1)} collective-permute-done((bf16[2,320,256]{2,1,0:T(8,128)(2,1)S(1)}, bf16[2,320,256]{2,1,0:T(8,128)(2,1)S(1)}, u32[]{:S(2)}, u32[]{:S(2)}) %collective-permute-start.21) | collective-permute-done | bytes 327712 | tf_op jit(solution)/shard_map/ppermute | solution.py:227
  121.6 0.1 convert_add_fusion
  121.7 0.1 collective-permute-start.22
  121.9 0.9 pad_maximum_fusion.2
  122.8 0.2 fusion.7
  123.0 0.9 pad_maximum_fusion
  124.0 0.9 pad_maximum_fusion.1
  (34 shorter events, 0.3 us)
Async XLA Ops:
  0.6 3.6 %copy-start = (bf16[2,2,128,2560]{3,2,1,0:T(8,128)(2,1)S(1)}, bf16[2,2,128,2560]{3,2,1,0:T(8,128)(2,1)}, u32[]{:S(2)}) copy-start(bf16[2,2,128,2560]{3,2,1,0:T(8,128)(2,1)} %param.7) | copy-start | bytes 7864324
  2.1 1.8 %collective-permute-start = (bf16[2,320,256]{2,1,0:T(8,128)(2,1)S(1)}, bf16[2,320,256]{2,1,0:T(8,128)(2,1)S(1)}, u32[]{:S(2)}, u32[]{:S(2)}) collective-permute-start(bf16[2,320,256]{2,1,0:T(8,128)(2,1)S(1)} %get-tuple-element.56), channel_id=1, source_target_pairs={{0,4},{4,0},{8,12},{12,8},{16,20},{20,16},{24,28},{28,24},{1,5},{5... | collective-permute-start | bytes 983048 | tf_op jit(solution)/shard_map/ppermute | solution.py:235
  3.8 41.8 %collective-permute-start.1 = (bf16[512,2560]{1,0:T(8,128)(2,1)}, bf16[512,2560]{1,0:T(8,128)(2,1)}, u32[]{:S(2)}, u32[]{:S(2)}) collective-permute-start(bf16[512,2560]{1,0:T(8,128)(2,1)} %bitcast.53), channel_id=1, source_target_pairs={{0,4},{4,0},{8,12},{12,8},{16,20},{20,16},{24,28},{28,24},{1,5},{5... | collective-permute-start | bytes 7864328 | tf_op jit(solution)/shard_map/ppermute | solution.py:235
  4.2 52.7 %collective-permute-start.7 = (bf16[512,2560]{1,0:T(8,128)(2,1)S(1)}, bf16[512,2560]{1,0:T(8,128)(2,1)}, u32[]{:S(2)}, u32[]{:S(2)}) collective-permute-start(bf16[512,2560]{1,0:T(8,128)(2,1)S(1)} %bitcast.50), channel_id=1, source_target_pairs={{0,4},{4,0},{8,12},{12,8},{16,20},{20,16},{24,28},{28,24},{1,5},{5... | collective-permute-start | bytes 7864328 | tf_op jit(solution)/shard_map/ppermute | solution.py:235
  4.4 41.3 %collective-permute-start.2 = (bf16[4,8,128,128]{3,2,1,0:T(8,128)(2,1)}, bf16[4,8,128,128]{3,2,1,0:T(8,128)(2,1)}, u32[]{:S(2)}, u32[]{:S(2)}) collective-permute-start(bf16[4,8,128,128]{3,2,1,0:T(8,128)(2,1)} %bitcast.56), channel_id=1, source_target_pairs={{0,4},{4,0},{8,12},{12,8},{16,20},{20,16},{24,28},{28,24},{1,5},{5... | collective-permute-start | bytes 3145736 | tf_op jit(solution)/shard_map/ppermute | solution.py:235
  4.9 19.1 %collective-permute-start.4 = (bf16[2,320,256]{2,1,0:T(8,128)(2,1)S(1)}, bf16[2,320,256]{2,1,0:T(8,128)(2,1)S(1)}, u32[]{:S(2)}, u32[]{:S(2)}) collective-permute-start(bf16[2,320,256]{2,1,0:T(8,128)(2,1)S(1)} %pad_maximum_fusion.5.rest_0_), channel_id=1, source_target_pairs={{0,16},{4,20},{8,24},{12,28},{16,0},{20,4},{24,8},{28,12},{1,17},{... | collective-permute-start | bytes 983048 | tf_op jit(solution)/shard_map/ppermute | solution.py:227
  23.9 11.4 %copy-start.5 = (bf16[2,320,256]{2,1,0:T(8,128)(2,1)}, bf16[2,320,256]{2,1,0:T(8,128)(2,1)S(1)}, u32[]{:S(2)}) copy-start(bf16[2,320,256]{2,1,0:T(8,128)(2,1)S(1)} %collective-permute-done.4.rest_2_) | copy-start | bytes 983044
  23.9 10.6 %collective-permute-start.5 = (bf16[2,320,256]{2,1,0:T(8,128)(2,1)S(1)}, bf16[2,320,256]{2,1,0:T(8,128)(2,1)S(1)}, u32[]{:S(2)}, u32[]{:S(2)}) collective-permute-start(bf16[2,320,256]{2,1,0:T(8,128)(2,1)S(1)} %collective-permute-done.4.rest_2_), channel_id=1, source_target_pairs={{0,8},{4,12},{8,0},{12,4},{16,24},{20,28},{24,16},{28,20},{1,9},{5... | collective-permute-start | bytes 983048 | tf_op jit(solution)/shard_map/ppermute | solution.py:227
  24.7 21.0 %collective-permute-start.3 = (bf16[2,320,256]{2,1,0:T(8,128)(2,1)S(1)}, bf16[2,320,256]{2,1,0:T(8,128)(2,1)}, u32[]{:S(2)}, u32[]{:S(2)}) collective-permute-start(bf16[2,320,256]{2,1,0:T(8,128)(2,1)S(1)} %pad_maximum_fusion.5.rest_0_), channel_id=1, source_target_pairs={{0,8},{4,12},{8,0},{12,4},{16,24},{20,28},{24,16},{28,20},{1,9},{5... | collective-permute-start | bytes 983048 | tf_op jit(solution)/shard_map/ppermute | solution.py:227
  35.3 19.5 %collective-permute-start.9 = (bf16[2,320,256]{2,1,0:T(8,128)(2,1)}, bf16[2,320,256]{2,1,0:T(8,128)(2,1)}, u32[]{:S(2)}, u32[]{:S(2)}) collective-permute-start(bf16[2,320,256]{2,1,0:T(8,128)(2,1)} %release.1.rest_0_), channel_id=1, source_target_pairs={{0,16},{4,20},{8,24},{12,28},{16,0},{20,4},{24,8},{28,12},{1,17},{... | collective-permute-start | bytes 983048 | tf_op jit(solution)/shard_map/ppermute | solution.py:227
  45.7 11.3 %collective-permute-start.8 = (bf16[2,320,256]{2,1,0:T(8,128)(2,1)}, bf16[2,320,256]{2,1,0:T(8,128)(2,1)S(1)}, u32[]{:S(2)}, u32[]{:S(2)}) collective-permute-start(bf16[2,320,256]{2,1,0:T(8,128)(2,1)} %release.1.rest_0_), channel_id=1, source_target_pairs={{0,8},{4,12},{8,0},{12,4},{16,24},{20,28},{24,16},{28,20},{1,9},{5... | collective-permute-start | bytes 983048 | tf_op jit(solution)/shard_map/ppermute | solution.py:227
  45.7 1.7 %copy-start.1 = (bf16[2,2,128,2560]{3,2,1,0:T(8,128)(2,1)S(1)}, bf16[2,2,128,2560]{3,2,1,0:T(8,128)(2,1)}, u32[]{:S(2)}) copy-start(bf16[2,2,128,2560]{3,2,1,0:T(8,128)(2,1)} %param.5) | copy-start | bytes 7864324
  47.4 1.2 copy-start.3
  48.6 1.0 copy-start.6
  54.7 2.2 %collective-permute-start.6 = (bf16[512,256]{1,0:T(8,128)(2,1)S(1)}, bf16[512,256]{1,0:T(8,128)(2,1)S(1)}, u32[]{:S(2)}, u32[]{:S(2)}) collective-permute-start(bf16[512,256]{1,0:T(8,128)(2,1)S(1)} %get-tuple-element.29.mixed_s), channel_id=1, source_target_pairs={{0,4},{4,0},{8,12},{12,8},{16,20},{20,16},{24,28},{28,24},{1,5},{5... | collective-permute-start | bytes 786440 | tf_op jit(solution)/shard_map/ppermute | solution.py:235
  54.8 10.6 %collective-permute-start.10 = (bf16[2,320,256]{2,1,0:T(8,128)(2,1)}, bf16[2,320,256]{2,1,0:T(8,128)(2,1)S(1)}, u32[]{:S(2)}, u32[]{:S(2)}) collective-permute-start(bf16[2,320,256]{2,1,0:T(8,128)(2,1)} %collective-permute-done.9.rest_2_), channel_id=1, source_target_pairs={{0,8},{4,12},{8,0},{12,4},{16,24},{20,28},{24,16},{28,20},{1,9},{5... | collective-permute-start | bytes 983048 | tf_op jit(solution)/shard_map/ppermute | solution.py:227
  56.9 5.3 %copy-start.7 = (bf16[512,256]{1,0:T(8,128)(2,1)}, bf16[512,256]{1,0:T(8,128)(2,1)S(1)}, u32[]{:S(2)}) copy-start(bf16[512,256]{1,0:T(8,128)(2,1)S(1)} %collective-permute-done.6.rest_0_.mixed_r) | copy-start | bytes 786436
  62.3 5.5 %copy-start.9 = (bf16[2,320,256]{2,1,0:T(8,128)(2,1)}, bf16[2,320,256]{2,1,0:T(8,128)(2,1)S(1)}, u32[]{:S(2)}) copy-start(bf16[2,320,256]{2,1,0:T(8,128)(2,1)S(1)} %get-tuple-element.43) | copy-start | bytes 983044
  67.7 13.3 %collective-permute-start.11 = (bf16[2560,256]{1,0:T(8,128)(2,1)}, bf16[2560,256]{1,0:T(8,128)(2,1)}, u32[]{:S(2)}, u32[]{:S(2)}) collective-permute-start(bf16[2560,256]{1,0:T(8,128)(2,1)} %assemble.1.w_o.w_out), channel_id=1, source_target_pairs={{0,4},{4,0},{8,12},{12,8},{16,20},{20,16},{24,28},{28,24},{1,5},{5... | collective-permute-start | bytes 3932168 | tf_op jit(solution)/shard_map/ppermute | solution.py:235
  67.7 10.8 %collective-permute-start.16 = (bf16[2,320,256]{2,1,0:T(8,128)(2,1)}, bf16[2,320,256]{2,1,0:T(8,128)(2,1)}, u32[]{:S(2)}, u32[]{:S(2)}) collective-permute-start(bf16[2,320,256]{2,1,0:T(8,128)(2,1)} %get-tuple-element.37), channel_id=1, source_target_pairs={{0,8},{4,12},{8,0},{12,4},{16,24},{20,28},{24,16},{28,20},{1,9},{5... | collective-permute-start | bytes 983048 | tf_op jit(solution)/shard_map/ppermute | solution.py:227
  69.5 24.0 %collective-permute-start.18 = (bf16[2,320,256]{2,1,0:T(8,128)(2,1)}, bf16[2,320,256]{2,1,0:T(8,128)(2,1)S(1)}, u32[]{:S(2)}, u32[]{:S(2)}) collective-permute-start(bf16[2,320,256]{2,1,0:T(8,128)(2,1)} %copy-done.9), channel_id=1, source_target_pairs={{0,8},{4,12},{8,0},{12,4},{16,24},{20,28},{24,16},{28,20},{1,9},{5... | collective-permute-start | bytes 983048 | tf_op jit(solution)/shard_map/ppermute | solution.py:227
  69.8 1.2 copy-start.4
  71.0 10.0 %copy-start.8 = (bf16[512,256]{1,0:T(8,128)(2,1)S(1)}, bf16[512,256]{1,0:T(8,128)(2,1)}, u32[]{:S(2)}) copy-start(bf16[512,256]{1,0:T(8,128)(2,1)} %copy-done.7) | copy-start | bytes 786436
  79.6 8.0 %copy-start.2 = (bf16[2,2,128,2560]{3,2,1,0:T(8,128)(2,1)S(1)}, bf16[2,2,128,2560]{3,2,1,0:T(8,128)(2,1)}, u32[]{:S(2)}) copy-start(bf16[2,2,128,2560]{3,2,1,0:T(8,128)(2,1)} %param.5) | copy-start | bytes 7864324
  79.6 17.1 %collective-permute-start.19 = (bf16[2,320,256]{2,1,0:T(8,128)(2,1)S(1)}, bf16[2,320,256]{2,1,0:T(8,128)(2,1)S(1)}, u32[]{:S(2)}, u32[]{:S(2)}) collective-permute-start(bf16[2,320,256]{2,1,0:T(8,128)(2,1)S(1)} %add_convert_fusion.unread), channel_id=1, source_target_pairs={{0,16},{4,20},{8,24},{12,28},{16,0},{20,4},{24,8},{28,12},{1,17},{... | collective-permute-start | bytes 983048 | tf_op jit(solution)/shard_map/ppermute | solution.py:227
  84.6 21.9 %collective-permute-start.12 = (bf16[2,256,640]{2,1,0:T(8,128)(2,1)S(1)}, bf16[2,256,640]{2,1,0:T(8,128)(2,1)S(1)}, u32[]{:S(2)}, u32[]{:S(2)}) collective-permute-start(bf16[2,256,640]{2,1,0:T(8,128)(2,1)S(1)} %get-tuple-element.33), channel_id=1, source_target_pairs={{0,1},{1,0},{2,3},{3,2},{4,5},{5,4},{6,7},{7,6},{8,9},{9,8},{10,11... | collective-permute-start | bytes 1966088 | tf_op jit(solution)/shard_map/ppermute | solution.py:238
  86.1 20.5 %collective-permute-start.14 = (bf16[2,256,640]{2,1,0:T(8,128)(2,1)S(1)}, bf16[2,256,640]{2,1,0:T(8,128)(2,1)S(1)}, u32[]{:S(2)}, u32[]{:S(2)}) collective-permute-start(bf16[2,256,640]{2,1,0:T(8,128)(2,1)S(1)} %get-tuple-element.34), channel_id=1, source_target_pairs={{0,2},{1,3},{2,0},{3,1},{4,6},{5,7},{6,4},{7,5},{8,10},{9,11},{10,... | collective-permute-start | bytes 1966088 | tf_op jit(solution)/shard_map/ppermute | solution.py:238
  92.1 11.6 %collective-permute-start.17 = (bf16[2,320,256]{2,1,0:T(8,128)(2,1)S(1)}, bf16[2,320,256]{2,1,0:T(8,128)(2,1)S(1)}, u32[]{:S(2)}, u32[]{:S(2)}) collective-permute-start(bf16[2,320,256]{2,1,0:T(8,128)(2,1)S(1)} %get-tuple-element.40), channel_id=1, source_target_pairs={{0,8},{4,12},{8,0},{12,4},{16,24},{20,28},{24,16},{28,20},{1,9},{5... | collective-permute-start | bytes 983048 | tf_op jit(solution)/shard_map/ppermute | solution.py:227
  103.8 16.0 %collective-permute-start.20 = (bf16[2,320,256]{2,1,0:T(8,128)(2,1)S(1)}, bf16[2,320,256]{2,1,0:T(8,128)(2,1)S(1)}, u32[]{:S(2)}, u32[]{:S(2)}) collective-permute-start(bf16[2,320,256]{2,1,0:T(8,128)(2,1)S(1)} %get-tuple-element.44), channel_id=1, source_target_pairs={{0,8},{4,12},{8,0},{12,4},{16,24},{20,28},{24,16},{28,20},{1,9},{5... | collective-permute-start | bytes 983048 | tf_op jit(solution)/shard_map/ppermute | solution.py:227
  103.9 17.7 %collective-permute-start.21 = (bf16[2,320,256]{2,1,0:T(8,128)(2,1)S(1)}, bf16[2,320,256]{2,1,0:T(8,128)(2,1)S(1)}, u32[]{:S(2)}, u32[]{:S(2)}) collective-permute-start(bf16[2,320,256]{2,1,0:T(8,128)(2,1)S(1)} %get-tuple-element.45), channel_id=1, source_target_pairs={{0,16},{4,20},{8,24},{12,28},{16,0},{20,4},{24,8},{28,12},{1,17},{... | collective-permute-start | bytes 983048 | tf_op jit(solution)/shard_map/ppermute | solution.py:227
  106.4 15.4 %collective-permute-start.23 = (f32[320,256]{1,0:T(8,128)S(1)}, f32[320,256]{1,0:T(8,128)S(1)}, u32[]{:S(2)}, u32[]{:S(2)}) collective-permute-start(f32[320,256]{1,0:T(8,128)S(1)} %slice_bitcast_fusion.2), channel_id=1, source_target_pairs={{0,4},{4,0},{8,12},{12,8},{16,20},{20,16},{24,28},{28,24},{1,5},{5... | collective-permute-start | bytes 983048 | tf_op jit(solution)/shard_map/ppermute | solution.py:235
  106.8 16.0 %collective-permute-start.13 = (bf16[256,640]{1,0:T(8,128)(2,1)S(1)}, bf16[256,640]{1,0:T(8,128)(2,1)S(1)}, u32[]{:S(2)}, u32[]{:S(2)}) collective-permute-start(bf16[256,640]{1,0:T(8,128)(2,1)S(1)} %get-tuple-element.49), channel_id=1, source_target_pairs={{0,2},{1,3},{2,0},{3,1},{4,6},{5,7},{6,4},{7,5},{8,10},{9,11},{10,... | collective-permute-start | bytes 983048 | tf_op jit(solution)/shard_map/ppermute | solution.py:238
  107.7 15.1 %collective-permute-start.15 = (bf16[256,640]{1,0:T(8,128)(2,1)S(1)}, bf16[256,640]{1,0:T(8,128)(2,1)S(1)}, u32[]{:S(2)}, u32[]{:S(2)}) collective-permute-start(bf16[256,640]{1,0:T(8,128)(2,1)S(1)} %get-tuple-element.50), channel_id=1, source_target_pairs={{0,1},{1,0},{2,3},{3,2},{4,5},{5,4},{6,7},{7,6},{8,9},{9,8},{10,11... | collective-permute-start | bytes 983048 | tf_op jit(solution)/shard_map/ppermute | solution.py:238
  121.7 2.2 %collective-permute-start.22 = (f32[320,256]{1,0:T(8,128)S(1)}, f32[320,256]{1,0:T(8,128)S(1)}, u32[]{:S(2)}, u32[]{:S(2)}) collective-permute-start(f32[320,256]{1,0:T(8,128)S(1)} %slice_bitcast_fusion), channel_id=1, source_target_pairs={{0,4},{4,0},{8,12},{12,8},{16,20},{20,16},{24,28},{28,24},{1,5},{5... | collective-permute-start | bytes 983048 | tf_op jit(solution)/shard_map/ppermute | solution.py:235

commit v11 on v10

--- a/solution.py
+++ b/solution.py
@@ -18,6 +18,10 @@
     return lax.dot_general(a, b, (((ca,), (cb,)), ((), ())), preferred_element_type=F32)
 
 
+def begin_slots(slots, slots_v, sems):
+    return begin([(slot, slots_v.at[j]) for j, slot in enumerate(slots)], sems)
+
+
 def begin(pairs, sems):
     copies = [pltpu.make_async_copy(s, d, sems.at[i]) for i, (s, d) in enumerate(pairs)]
     for copy in copies:
@@ -29,12 +33,11 @@
     return pl.ds(pl.multiple_of(index * size, math.gcd(size, 16)), size)
 
 
-def place(idx, slots, which, w_ref):
+def place(idx, slots_v, w_ref):
     core = idx[0]
-    for j, slot in enumerate(slots):
-        slot = slot if len(slot.shape) == 3 else slot.at[which]
-        depth = slot.shape[1]
-        mine, other = slot[0], slot[1]
+    for j in range(slots_v.shape[0]):
+        depth = slots_v.shape[2]
+        mine, other = slots_v[j, 0], slots_v[j, 1]
         low = jnp.where(core == 0, mine, other)
         high = jnp.where(core == 0, other, mine)
         w_ref[rows_at(idx[1 + j], 2 * depth), :] = jnp.concatenate([low, high], axis=0)
@@ -63,7 +66,10 @@
 
 def assemble_kernel(idx, token, *rest):
     del token
-    place(idx, rest[:-1], 1, rest[-1])
+    slots, (w_out, slots_v, sems) = rest[:-3], rest[-3:]
+    for copy in begin_slots(slots, slots_v, sems):
+        copy.wait()
+    place(idx, slots_v, w_out)
 
 
 def d_value_kernel(idx, cot_o, cot_s, mix_o, mix_s, w_out, left_v, cot_v, mix_v, sems):
@@ -115,16 +121,20 @@
 
 
 def mixed_kernel(n_slots, idx, act_o, act_s, mix_o, mix_s, *rest):
-    slots, (mixed_o, mixed_s, w_v, act_v, mix_v, sems) = rest[:n_slots], rest[n_slots:]
+    slots, rest = rest[:n_slots], rest[n_slots:]
+    mixed_o, mixed_s, w_v, act_v, mix_v, sems, slots_v, slot_sems = rest
     groups, _, seq, _ = mix_o.shape
     heads = mix_v.shape[2]
     here = pl.ds(idx[0] * heads, heads)
+    slot_copies = begin_slots(slots, slots_v, slot_sems)
     copies = begin(
         [(act_o, act_v.at[0]), (mix_o.at[:, here], mix_v.at[0])]
         + [(act_s, act_v.at[1]), (mix_s.at[:, here], mix_v.at[1])],
         sems,
     )
-    place(idx, slots, 0, w_v)
+    for copy in slot_copies:
+        copy.wait()
+    place(idx, slots_v, w_v)
     for half, out in enumerate((mixed_o, mixed_s)):
         copies[2 * half].wait()
         value = dot(act_v[half], w_v[...]).astype(BF16)
@@ -204,7 +214,7 @@
 VMEM = pl.BlockSpec(memory_space=pltpu.VMEM)
 
 
-def call(kernel, name, in_specs, out_shapes, scratch, flops, kinds=None):
+def call(kernel, name, in_specs, out_shapes, scratch, flops, size=1 << 20, kinds=None):
     return pl.pallas_call(
         kernel,
         name=name,
@@ -215,7 +225,7 @@
         ],
         scratch_shapes=scratch,
         compiler_params=pltpu.CompilerParams(vmem_limit_bytes=VMEM_LIMIT),
-        cost_estimate=pl.CostEstimate(flops=flops, bytes_accessed=12 << 20, transcendentals=0),
+        cost_estimate=pl.CostEstimate(flops=flops, bytes_accessed=size, transcendentals=0),
     )
 
 
@@ -259,10 +269,6 @@
 
     def added(block, got):
         return (block.astype(F32) + got.astype(F32)).astype(BF16)
-
-    def gather_steps(u):
-        far = swap(u, 2)
-        return [u, swap(u, 1), far, swap(far, 1)]
 
     def scatter_end(own, got, c):
         total = own.astype(F32)
@@ -300,11 +306,14 @@
         u_out, u_value, act_s, mix_s, cot_s = swap_cores(w_out, w_value, act, mix, cot, c)
         block = u_out.shape
         if line4:
-            value_slots = gather_steps(u_value)
+            far, near = swap(u_value, 2), swap(u_value, 1)
+            far = call(release_kernel, "relay", [ANY, VMEM], [block], [], 0)(near, far)[0]
+            value_slots = [u_value, near, far, swap(far, 1)]
             u_out = call(release_kernel, "release", [ANY, VMEM], [block], [], 0)(
                 value_slots[3], u_out
             )[0]
-            out_slots = gather_steps(u_out)
+            far = swap(u_out, 2)
+            out_slots = [u_out, swap(u_out, 1), far, swap(far, 1)]
         else:
             value_slots, out_slots = gather_ring(u_value), gather_ring(u_out)
         n_slots = len(out_slots)
@@ -319,13 +328,18 @@
         rows = pltpu.VMEM((width, cols), BF16)
         send_shapes = [block] * n_slots
 
+        slots_scratch = [
+            pltpu.VMEM((n_slots, *block), BF16),
+            pltpu.SemaphoreType.DMA((n_slots,)),
+        ]
         mixed_o, mixed_s = call(
             functools.partial(mixed_kernel, n_slots),
             "mixed",
-            [SMEM] + [ANY] * 4 + [VMEM] * n_slots,
+            [SMEM] + [ANY] * (4 + n_slots),
             [(tokens, cols)] * 2,
-            [rows, halves, mix_scratch, pltpu.SemaphoreType.DMA((4,))],
+            [rows, halves, mix_scratch, pltpu.SemaphoreType.DMA((4,)), *slots_scratch],
             flops,
+            2 * (2 * act.size + mix.size + width * cols + 2 * tokens * cols),
         )(idx, act, act_s, mix, mix_s, *value_slots)
         mixed_r = sibling(mixed_s)
         unread = [mixed_r, *(out_slots[1:3] if line4 else [])]
@@ -336,15 +350,17 @@
             [(16, 128)] + send_shapes,
             [both, left_tokens, rows, pltpu.SemaphoreType.DMA((2,))],
             flops,
+            2 * (2 * cot.size + 2 * tokens * cols + width * cols),
         )(idx, cot, cot_s, mixed_o, mixed_s, *unread)
         out_passed = swap(out_sends[3], 1) if line4 else token
         w_full = call(
             assemble_kernel,
             "assemble",
-            [SMEM, ANY] + [VMEM] * n_slots,
+            [SMEM] + [ANY] * (1 + n_slots),
             [(width, cols)],
-            [],
+            slots_scratch,
             0,
+            4 * width * cols,
         )(idx, token, *out_slots)[0]
         w_full_s = sibling(w_full)
         left = call(
@@ -354,6 +370,7 @@
             [(cols, 2 * tokens)],
             [halves, mix_scratch, pltpu.SemaphoreType.DMA((4,))],
             flops,
+            2 * (2 * cot.size + mix.size + width * cols + 2 * tokens * cols),
         )(idx, cot, cot_s, mix, mix_s, w_full)[0]
         if line4:
             out_onward = added(out_sends[2], out_passed)
@@ -374,6 +391,7 @@
             [(16, 128)] + term_shapes,
             [],
             flops,
+            2 * (2 * tokens * cols + 2 * width * cols + tokens * width),
         )(idx_node, mixed_o, mixed_r, w_full, w_full_s)
 
         back_sends = call(
@@ -383,11 +401,12 @@
             send_shapes,
             [both, rows, pltpu.SemaphoreType.DMA((2,))],
             flops,
+            2 * (2 * act.size + 2 * tokens * cols + width * cols),
         )(idx, token, out_onward, act, act_s, left)
         if line4:
             back_passed = swap(back_sends[3], 1)
             onward, beside, out_total = call(
-                sum_kernel, "sum", [VMEM] * 6, [block] * 3, [], 0, [BF16, BF16, F32]
+                sum_kernel, "sum", [VMEM] * 6, [block] * 3, [], 0, kinds=[BF16, BF16, F32]
             )(back_sends[2], back_passed, back_sends[1], out_sends[0], out_near, out_far)
             back_far, back_near = swap(onward, 2), swap(beside, 1)
             grad_out = join(out_total[0], sibling(out_total[1]), c)

time: 125 us -> 122 us (0.976)
  waiting for transfers between devices: 61.7 us -> 49.5 us
  starting transfers between devices: 23.5 us -> 29.5 us
  local copies, waits for them, and re-layouts: 6.7 us -> 9.12 us
    ppermute x12, waiting for transfers between devices: 60.4 us -> 48.2 us  [move(): lax.ppermute(x, 'wide', [(2 * s + c, 2 * d + c) for s, d in pairs for c i...]
    ppermute x12, starting transfers between devices: 17.1 us -> 22.4 us  [move(): lax.ppermute(x, 'wide', [(2 * s + c, 2 * d + c) for s, d in pairs for c i...]
    unnamed x20 -> x24, local copies, waits for them, and re-layouts: 5.18 us -> 7.6 us
    pallas_call x2 -> x3, Pallas kernels: 2.46 us -> 3.09 us  [the longest x1 2.88 us: body(): call(assemble_kernel, 'assemble', [SMEM] + [ANY] * (1 + n_slots), [(width...]
  transfers between devices with their start and end apart: 24 -> 24, of which waited for: 10 -> 11; matrix products, arithmetic and copies ran while one was open for 3% -> 3% of each run, Pallas kernels for 20% -> 20%
where the time goes in v11:
time: 122 us
  waiting for transfers between devices  49.5 us (41%)
  starting transfers between devices  29.5 us (24%)
  Pallas kernels  27.8 us (23%)
  local copies, waits for them, and re-layouts  9.12 us (7%)
  other arithmetic  5.03 us (4%)
    ppermute x12, waiting for transfers between devices, move(): lax.ppermute(x, 'wide', [(2 * s + c, 2 * d + c) for s, d in pairs for c i...  48.2 us
    ppermute x12, starting transfers between devices, move(): lax.ppermute(x, 'wide', [(2 * s + c, 2 * d + c) for s, d in pairs for c i...  22.4 us
    unnamed x24, local copies, waits for them, and re-layouts  7.6 us
    pallas_call x1, Pallas kernels, body(): call(d_value_kernel, 'd_value', [SMEM] + [ANY] * 4 + [VMEM], [(cols, 2 *...  5.53 us
    ppermute x4, starting transfers between devices, flip(): return lax.ppermute(x, 'node', [(i, i ^ j) for i in range(n_node)])  5.34 us
    pallas_call x1, Pallas kernels, body(): call(functools.partial(grad_out_kernel, len(unread)), 'grad_out', [SMEM]...  5.29 us
    pallas_call x1, Pallas kernels, body(): call(functools.partial(mixed_kernel, n_slots), 'mixed', [SMEM] + [ANY] *...  5.14 us
    pallas_call x1, Pallas kernels, body(): call(gradient_kernel, 'grad_value', [SMEM] + [ANY] * 4 + [VMEM], send_sha...  4.44 us
  transfers between devices with their start and end apart: 24, of which 11 were waited for; matrix products, arithmetic and copies ran while one was open for 3% of the time, Pallas kernels for 20%

profile of v11, /device:TPU:0, one launch (start us, length us, event | category | flops | bytes accessed | tf_op | source)
XLA Modules:
  0.0 121.9 jit_solution(18148038333736372587)
XLA Ops:
  0.7 1.3 %slice_bitcast_fusion.5 = (bf16[1,320,256]{2,1,0:T(8,128)(2,1)S(1)}, bf16[1,320,256]{2,1,0:T(8,128)(2,1)S(1)}, bf16[1,320,256]{2,1,0:T(8,128)(2,1)S(1)}, bf16[1,320,256]{2,1,0:T(8,128)(2,1)S(1)}) fusion(bf16[320,512]{1,0:T(8,128)(2,1)} %param.8, bf16[320,512]{1,0:T(8,128)(2,1)} %param.9), kind=kLoop, calls=%fused_computation.34 | loop fusion | bytes 1310720 | tf_op jit(solution)/shard_map/stack | solution.py:253
  2.0 0.1 broadcast_select_fusion
  2.1 0.5 collective-permute-start
  2.6 1.3 %collective-permute-done = bf16[2,320,256]{2,1,0:T(8,128)(2,1)S(1)} collective-permute-done((bf16[2,320,256]{2,1,0:T(8,128)(2,1)S(1)}, bf16[2,320,256]{2,1,0:T(8,128)(2,1)S(1)}, u32[]{:S(2)}, u32[]{:S(2)}) %collective-permute-start) | collective-permute-done | bytes 327712 | tf_op jit(solution)/shard_map/ppermute | solution.py:245
  3.8 0.4 collective-permute-start.1
  4.2 0.1 collective-permute-start.7
  4.4 0.4 collective-permute-start.2
  4.9 2.8 %collective-permute-start.3 = (bf16[2,320,256]{2,1,0:T(8,128)(2,1)S(1)}, bf16[2,320,256]{2,1,0:T(8,128)(2,1)S(1)}, u32[]{:S(2)}, u32[]{:S(2)}) collective-permute-start(bf16[2,320,256]{2,1,0:T(8,128)(2,1)S(1)} %pad_maximum_fusion.5.rest_0_), channel_id=1, source_target_pairs={{0,8},{4,12},{8,0},{12,4},{16,24},{20,28},{24,16},{28,20},{1,9},{5... | collective-permute-start | bytes 983048 | tf_op jit(solution)/shard_map/ppermute | solution.py:237
  7.7 2.6 %collective-permute-start.4 = (bf16[2,320,256]{2,1,0:T(8,128)(2,1)S(1)}, bf16[2,320,256]{2,1,0:T(8,128)(2,1)S(1)}, u32[]{:S(2)}, u32[]{:S(2)}) collective-permute-start(bf16[2,320,256]{2,1,0:T(8,128)(2,1)S(1)} %pad_maximum_fusion.5.rest_0_), channel_id=1, source_target_pairs={{0,16},{4,20},{8,24},{12,28},{16,0},{20,4},{24,8},{28,12},{1,17},{... | collective-permute-start | bytes 983048 | tf_op jit(solution)/shard_map/ppermute | solution.py:237
  10.3 12.6 %collective-permute-done.3.unread.rest_1_ = bf16[2,320,256]{2,1,0:T(8,128)(2,1)S(1)} collective-permute-done((bf16[2,320,256]{2,1,0:T(8,128)(2,1)S(1)}, bf16[2,320,256]{2,1,0:T(8,128)(2,1)S(1)}, u32[]{:S(2)}, u32[]{:S(2)}) %collective-permute-start.3) | collective-permute-done | bytes 327712 | tf_op jit(solution)/shard_map/ppermute | solution.py:237
  22.8 2.5 %collective-permute-done.4.block = bf16[2,320,256]{2,1,0:T(8,128)(2,1)S(1)} collective-permute-done((bf16[2,320,256]{2,1,0:T(8,128)(2,1)S(1)}, bf16[2,320,256]{2,1,0:T(8,128)(2,1)S(1)}, u32[]{:S(2)}, u32[]{:S(2)}) %collective-permute-start.4) | collective-permute-done | bytes 327712 | tf_op jit(solution)/shard_map/ppermute | solution.py:237
  25.4 0.5 collective-permute-start.5
  25.9 0.7 copy-done.5
  26.6 6.6 %collective-permute-done.5.rest_3_.unread = bf16[2,320,256]{2,1,0:T(8,128)(2,1)S(1)} collective-permute-done((bf16[2,320,256]{2,1,0:T(8,128)(2,1)S(1)}, bf16[2,320,256]{2,1,0:T(8,128)(2,1)S(1)}, u32[]{:S(2)}, u32[]{:S(2)}) %collective-permute-start.5) | collective-permute-done | bytes 327712 | tf_op jit(solution)/shard_map/ppermute | solution.py:237
  33.3 0.7 release.1.rest_0_
  34.0 0.7 copy-done.7
  34.7 2.3 %collective-permute-start.9 = (bf16[2,320,256]{2,1,0:T(8,128)(2,1)}, bf16[2,320,256]{2,1,0:T(8,128)(2,1)}, u32[]{:S(2)}, u32[]{:S(2)}) collective-permute-start(bf16[2,320,256]{2,1,0:T(8,128)(2,1)} %release.1.rest_0_), channel_id=1, source_target_pairs={{0,16},{4,20},{8,24},{12,28},{16,0},{20,4},{24,8},{28,12},{1,17},{... | collective-permute-start | bytes 983048 | tf_op jit(solution)/shard_map/ppermute | solution.py:237
  37.1 0.1 stack.67.idx
  37.1 1.7 %collective-permute-start.8 = (bf16[2,320,256]{2,1,0:T(8,128)(2,1)}, bf16[2,320,256]{2,1,0:T(8,128)(2,1)S(1)}, u32[]{:S(2)}, u32[]{:S(2)}) collective-permute-start(bf16[2,320,256]{2,1,0:T(8,128)(2,1)} %release.1.rest_0_), channel_id=1, source_target_pairs={{0,8},{4,12},{8,0},{12,4},{16,24},{20,28},{24,16},{28,20},{1,9},{5... | collective-permute-start | bytes 983048 | tf_op jit(solution)/shard_map/ppermute | solution.py:237
  38.9 1.7 %copy-done.1 = bf16[2,2,128,2560]{3,2,1,0:T(8,128)(2,1)S(1)} copy-done((bf16[2,2,128,2560]{3,2,1,0:T(8,128)(2,1)S(1)}, bf16[2,2,128,2560]{3,2,1,0:T(8,128)(2,1)}, u32[]{:S(2)}) %copy-start.1) | copy-done | bytes 2621464
  40.6 1.2 %copy-done.3 = bf16[2,2,8,128,128]{4,3,2,1,0:T(8,128)(2,1)S(1)} copy-done((bf16[2,2,8,128,128]{4,3,2,1,0:T(8,128)(2,1)S(1)}, bf16[2,2,8,128,128]{4,3,2,1,0:T(8,128)(2,1)}, u32[]{:S(2)}) %copy-start.3) | copy-done | bytes 1048600
  41.9 1.0 copy-done.6
  42.8 1.0 copy-done.8
  43.8 5.1 %mixed.1 = (bf16[512,256]{1,0:T(8,128)(2,1)S(1)}, bf16[512,256]{1,0:T(8,128)(2,1)S(1)}) custom-call(s32[5]{0:T(128)S(1)} %stack.67.idx, bf16[512,2560]{1,0:T(8,128)(2,1)S(1)} %bitcast.54, bf16[512,2560]{1,0:T(8,128)(2,1)} %collective-permute-done.1.act_s.right_s, bf16[4,8,128,128]{3,2,1,0:T(8,128)(2,1)S(1)} %bitcast.57, ...), custom_call_target="tpu_custom_call" | custom-call | flops 1342177280 | bytes 8126464 | tf_op jit(solution)/shard_map/mixed/pallas_call | solution.py:335
  48.9 0.1 collective-permute-start.6
  49.0 1.9 %collective-permute-done.9.rest_2_ = bf16[2,320,256]{2,1,0:T(8,128)(2,1)} collective-permute-done((bf16[2,320,256]{2,1,0:T(8,128)(2,1)}, bf16[2,320,256]{2,1,0:T(8,128)(2,1)}, u32[]{:S(2)}, u32[]{:S(2)}) %collective-permute-start.9) | collective-permute-done | bytes 327712 | tf_op jit(solution)/shard_map/ppermute | solution.py:237
  50.9 0.7 collective-permute-start.10
  51.6 5.3 %grad_out.1 = (bf16[16,128]{1,0:T(8,128)(2,1)S(1)}, bf16[2,320,256]{2,1,0:T(8,128)(2,1)S(1)}, bf16[2,320,256]{2,1,0:T(8,128)(2,1)S(1)}, bf16[2,320,256]{2,1,0:T(8,128)(2,1)S(1)}, bf16[2,320,256]{2,1,0:T(8,128)(2,1)}) custom-call(s32[5]{0:T(128)S(1)} %stack.67.idx, bf16[512,2560]{1,0:T(8,128)(2,1)S(1)} %bitcast.51, ...), custom_call_target="tpu_custom_call" | custom-call | flops 1342177280 | bytes 7077888 | tf_op jit(solution)/shard_map/grad_out/pallas_call | solution.py:346
  56.9 2.7 %collective-permute-done.10.rest_3_ = bf16[2,320,256]{2,1,0:T(8,128)(2,1)S(1)} collective-permute-done((bf16[2,320,256]{2,1,0:T(8,128)(2,1)}, bf16[2,320,256]{2,1,0:T(8,128)(2,1)S(1)}, u32[]{:S(2)}, u32[]{:S(2)}) %collective-permute-start.10) | collective-permute-done | bytes 327712 | tf_op jit(solution)/shard_map/ppermute | solution.py:237
  59.7 2.9 %assemble.1.w_o.w_out = bf16[2560,256]{1,0:T(8,128)(2,1)} custom-call(s32[5]{0:T(128)S(1)} %stack.67.idx, bf16[16,128]{1,0:T(8,128)(2,1)S(1)} %get-tuple-element.31.token, bf16[2,320,256]{2,1,0:T(8,128)(2,1)} %release.1.rest_0_, bf16[2,320,256]{2,1,0:T(8,128)(2,1)S(1)} %collective-permute-done.8.rest_1_, ...), custom_call_target="tpu_custom_call" | custom-call | bytes 2621440 | tf_op jit(solution)/shard_map/assemble/pallas_call | solution.py:356
  62.6 0.1 collective-permute-start.11
  62.6 1.8 %collective-permute-start.16 = (bf16[2,320,256]{2,1,0:T(8,128)(2,1)}, bf16[2,320,256]{2,1,0:T(8,128)(2,1)}, u32[]{:S(2)}, u32[]{:S(2)}) collective-permute-start(bf16[2,320,256]{2,1,0:T(8,128)(2,1)} %get-tuple-element.37), channel_id=1, source_target_pairs={{0,8},{4,12},{8,0},{12,4},{16,24},{20,28},{24,16},{28,20},{1,9},{5... | collective-permute-start | bytes 983048 | tf_op jit(solution)/shard_map/ppermute | solution.py:237
  64.5 0.1 pad_add_fusion.idx
  64.5 0.3 collective-permute-start.18
  64.8 1.2 %copy-done.4 = bf16[2,2,8,128,128]{4,3,2,1,0:T(8,128)(2,1)S(1)} copy-done((bf16[2,2,8,128,128]{4,3,2,1,0:T(8,128)(2,1)S(1)}, bf16[2,2,8,128,128]{4,3,2,1,0:T(8,128)(2,1)}, u32[]{:S(2)}) %copy-start.4) | copy-done | bytes 1048600
  66.0 5.5 %d_value.1.left_ref = bf16[256,1024]{1,0:T(8,128)(2,1)S(1)} custom-call(s32[5]{0:T(128)S(1)} %stack.67.idx, bf16[512,2560]{1,0:T(8,128)(2,1)S(1)} %bitcast.52, bf16[512,2560]{1,0:T(8,128)(2,1)} %collective-permute-done.7.cot_s, bf16[4,8,128,128]{3,2,1,0:T(8,128)(2,1)S(1)} %bitcast.58, bf16[4,8,128,128]{3,2,1,0:T(8,128)(2,1)} %collective-permute-done.2.mix_s, ...), custom_call_target="tpu_custom_call" | custom-call | flops 1342177280 | bytes 8126464 | tf_op jit(solution)/shard_map/d_value/pallas_call | solution.py:366
  71.6 2.0 %collective-permute-done.16 = bf16[2,320,256]{2,1,0:T(8,128)(2,1)} collective-permute-done((bf16[2,320,256]{2,1,0:T(8,128)(2,1)}, bf16[2,320,256]{2,1,0:T(8,128)(2,1)}, u32[]{:S(2)}, u32[]{:S(2)}) %collective-permute-start.16) | collective-permute-done | bytes 327712 | tf_op jit(solution)/shard_map/ppermute | solution.py:237
  73.5 1.1 add_convert_fusion.unread
  74.6 3.4 %collective-permute-start.19 = (bf16[2,320,256]{2,1,0:T(8,128)(2,1)S(1)}, bf16[2,320,256]{2,1,0:T(8,128)(2,1)S(1)}, u32[]{:S(2)}, u32[]{:S(2)}) collective-permute-start(bf16[2,320,256]{2,1,0:T(8,128)(2,1)S(1)} %add_convert_fusion.unread), channel_id=1, source_target_pairs={{0,16},{4,20},{8,24},{12,28},{16,0},{20,4},{24,8},{28,12},{1,17},{... | collective-permute-start | bytes 983048 | tf_op jit(solution)/shard_map/ppermute | solution.py:237
  78.1 3.6 %terms.1 = (bf16[16,128]{1,0:T(8,128)(2,1)S(1)}, bf16[2,256,640]{2,1,0:T(8,128)(2,1)S(1)}, bf16[2,256,640]{2,1,0:T(8,128)(2,1)S(1)}, bf16[4,256,640]{2,1,0:T(8,128)(2,1)S(1)}) custom-call(s32[4]{0:T(128)S(1)} %pad_add_fusion.idx, bf16[512,256]{1,0:T(8,128)(2,1)S(1)} %get-tuple-element.28.mixed_o, bf16[512,256]{1,0:T(8,128)(2,1)S(1)} %copy-done.10, ...), custom_call_target="tpu_custom_call" | custom-call | flops 1342177280 | bytes 5767168 | tf_op jit(solution)/shard_map/terms/pallas_call | solution.py:387
  81.6 1.6 %collective-permute-start.12 = (bf16[2,256,640]{2,1,0:T(8,128)(2,1)S(1)}, bf16[2,256,640]{2,1,0:T(8,128)(2,1)S(1)}, u32[]{:S(2)}, u32[]{:S(2)}) collective-permute-start(bf16[2,256,640]{2,1,0:T(8,128)(2,1)S(1)} %get-tuple-element.33), channel_id=1, source_target_pairs={{0,1},{1,0},{2,3},{3,2},{4,5},{5,4},{6,7},{7,6},{8,9},{9,8},{10,11... | collective-permute-start | bytes 1966088 | tf_op jit(solution)/shard_map/ppermute | solution.py:248
  83.2 1.5 %collective-permute-start.14 = (bf16[2,256,640]{2,1,0:T(8,128)(2,1)S(1)}, bf16[2,256,640]{2,1,0:T(8,128)(2,1)S(1)}, u32[]{:S(2)}, u32[]{:S(2)}) collective-permute-start(bf16[2,256,640]{2,1,0:T(8,128)(2,1)S(1)} %get-tuple-element.34), channel_id=1, source_target_pairs={{0,2},{1,3},{2,0},{3,1},{4,6},{5,7},{6,4},{7,5},{8,10},{9,11},{10,... | collective-permute-start | bytes 1966088 | tf_op jit(solution)/shard_map/ppermute | solution.py:248
  84.7 4.4 %grad_value.1 = (bf16[2,320,256]{2,1,0:T(8,128)(2,1)S(1)}, bf16[2,320,256]{2,1,0:T(8,128)(2,1)S(1)}, bf16[2,320,256]{2,1,0:T(8,128)(2,1)S(1)}, bf16[2,320,256]{2,1,0:T(8,128)(2,1)S(1)}) custom-call(s32[5]{0:T(128)S(1)} %stack.67.idx, bf16[16,128]{1,0:T(8,128)(2,1)S(1)} %get-tuple-element.35.token, bf16[2,320,256]{2,1,0:T(8,128)(2,1)S(1)} %add_convert_fusion.unread, ...), custom_call_target="tpu_custom_call" | custom-call | flops 1342177280 | bytes 7077888 | tf_op jit(solution)/shard_map/grad_value/pallas_call | solution.py:397
  89.2 1.8 %collective-permute-start.17 = (bf16[2,320,256]{2,1,0:T(8,128)(2,1)S(1)}, bf16[2,320,256]{2,1,0:T(8,128)(2,1)S(1)}, u32[]{:S(2)}, u32[]{:S(2)}) collective-permute-start(bf16[2,320,256]{2,1,0:T(8,128)(2,1)S(1)} %get-tuple-element.40), channel_id=1, source_target_pairs={{0,8},{4,12},{8,0},{12,4},{16,24},{20,28},{24,16},{28,20},{1,9},{5... | collective-permute-start | bytes 983048 | tf_op jit(solution)/shard_map/ppermute | solution.py:237
  91.0 0.2 convert_element_type.50
  91.1 1.2 collective-permute-done.19.far
  92.3 6.9 %collective-permute-done.17.got = bf16[2,320,256]{2,1,0:T(8,128)(2,1)S(1)} collective-permute-done((bf16[2,320,256]{2,1,0:T(8,128)(2,1)S(1)}, bf16[2,320,256]{2,1,0:T(8,128)(2,1)S(1)}, u32[]{:S(2)}, u32[]{:S(2)}) %collective-permute-start.17) | collective-permute-done | bytes 327712 | tf_op jit(solution)/shard_map/ppermute | solution.py:237
  99.2 0.2 sum.1
  99.4 0.1 collective-permute-start.20
  99.5 4.4 %collective-permute-start.21 = (bf16[2,320,256]{2,1,0:T(8,128)(2,1)S(1)}, bf16[2,320,256]{2,1,0:T(8,128)(2,1)S(1)}, u32[]{:S(2)}, u32[]{:S(2)}) collective-permute-start(bf16[2,320,256]{2,1,0:T(8,128)(2,1)S(1)} %get-tuple-element.45), channel_id=1, source_target_pairs={{0,16},{4,20},{8,24},{12,28},{16,0},{20,4},{24,8},{28,12},{1,17},{... | collective-permute-start | bytes 983048 | tf_op jit(solution)/shard_map/ppermute | solution.py:237
  103.9 0.1 collective-permute-start.23
  104.0 0.1 convert_element_type.51
  104.1 0.1 convert_element_type.55
  104.2 0.2 fusion.8
  104.4 1.6 %collective-permute-start.13 = (bf16[256,640]{1,0:T(8,128)(2,1)S(1)}, bf16[256,640]{1,0:T(8,128)(2,1)S(1)}, u32[]{:S(2)}, u32[]{:S(2)}) collective-permute-start(bf16[256,640]{1,0:T(8,128)(2,1)S(1)} %get-tuple-element.49), channel_id=1, source_target_pairs={{0,2},{1,3},{2,0},{3,1},{4,6},{5,7},{6,4},{7,5},{8,10},{9,11},{10,... | collective-permute-start | bytes 983048 | tf_op jit(solution)/shard_map/ppermute | solution.py:248
  106.0 0.7 collective-permute-start.15
  106.6 8.7 %collective-permute-done.20 = bf16[2,320,256]{2,1,0:T(8,128)(2,1)S(1)} collective-permute-done((bf16[2,320,256]{2,1,0:T(8,128)(2,1)S(1)}, bf16[2,320,256]{2,1,0:T(8,128)(2,1)S(1)}, u32[]{:S(2)}, u32[]{:S(2)}) %collective-permute-start.20) | collective-permute-done | bytes 327712 | tf_op jit(solution)/shard_map/ppermute | solution.py:237
  115.4 3.2 %collective-permute-done.21 = bf16[2,320,256]{2,1,0:T(8,128)(2,1)S(1)} collective-permute-done((bf16[2,320,256]{2,1,0:T(8,128)(2,1)S(1)}, bf16[2,320,256]{2,1,0:T(8,128)(2,1)S(1)}, u32[]{:S(2)}, u32[]{:S(2)}) %collective-permute-start.21) | collective-permute-done | bytes 327712 | tf_op jit(solution)/shard_map/ppermute | solution.py:237
  118.5 0.1 convert_add_fusion
  118.7 0.1 collective-permute-start.22
  118.9 0.9 pad_maximum_fusion.2
  119.8 0.3 fusion.7
  120.1 0.9 pad_maximum_fusion
  121.0 0.9 pad_maximum_fusion.1
  (39 shorter events, 0.3 us)
Async XLA Ops:
  0.6 3.6 %copy-start = (bf16[2,2,128,2560]{3,2,1,0:T(8,128)(2,1)S(1)}, bf16[2,2,128,2560]{3,2,1,0:T(8,128)(2,1)}, u32[]{:S(2)}) copy-start(bf16[2,2,128,2560]{3,2,1,0:T(8,128)(2,1)} %param.7) | copy-start | bytes 7864324
  2.1 1.8 %collective-permute-start = (bf16[2,320,256]{2,1,0:T(8,128)(2,1)S(1)}, bf16[2,320,256]{2,1,0:T(8,128)(2,1)S(1)}, u32[]{:S(2)}, u32[]{:S(2)}) collective-permute-start(bf16[2,320,256]{2,1,0:T(8,128)(2,1)S(1)} %get-tuple-element.56), channel_id=1, source_target_pairs={{0,4},{4,0},{8,12},{12,8},{16,20},{20,16},{24,28},{28,24},{1,5},{5... | collective-permute-start | bytes 983048 | tf_op jit(solution)/shard_map/ppermute | solution.py:245
  3.8 35.0 %collective-permute-start.1 = (bf16[512,2560]{1,0:T(8,128)(2,1)}, bf16[512,2560]{1,0:T(8,128)(2,1)}, u32[]{:S(2)}, u32[]{:S(2)}) collective-permute-start(bf16[512,2560]{1,0:T(8,128)(2,1)} %bitcast.53), channel_id=1, source_target_pairs={{0,4},{4,0},{8,12},{12,8},{16,20},{20,16},{24,28},{28,24},{1,5},{5... | collective-permute-start | bytes 7864328 | tf_op jit(solution)/shard_map/ppermute | solution.py:245
  4.2 47.4 %collective-permute-start.7 = (bf16[512,2560]{1,0:T(8,128)(2,1)S(1)}, bf16[512,2560]{1,0:T(8,128)(2,1)}, u32[]{:S(2)}, u32[]{:S(2)}) collective-permute-start(bf16[512,2560]{1,0:T(8,128)(2,1)S(1)} %bitcast.50), channel_id=1, source_target_pairs={{0,4},{4,0},{8,12},{12,8},{16,20},{20,16},{24,28},{28,24},{1,5},{5... | collective-permute-start | bytes 7864328 | tf_op jit(solution)/shard_map/ppermute | solution.py:245
  4.4 34.5 %collective-permute-start.2 = (bf16[4,8,128,128]{3,2,1,0:T(8,128)(2,1)}, bf16[4,8,128,128]{3,2,1,0:T(8,128)(2,1)}, u32[]{:S(2)}, u32[]{:S(2)}) collective-permute-start(bf16[4,8,128,128]{3,2,1,0:T(8,128)(2,1)} %bitcast.56), channel_id=1, source_target_pairs={{0,4},{4,0},{8,12},{12,8},{16,20},{20,16},{24,28},{28,24},{1,5},{5... | collective-permute-start | bytes 3145736 | tf_op jit(solution)/shard_map/ppermute | solution.py:245
  4.9 17.9 %collective-permute-start.3 = (bf16[2,320,256]{2,1,0:T(8,128)(2,1)S(1)}, bf16[2,320,256]{2,1,0:T(8,128)(2,1)S(1)}, u32[]{:S(2)}, u32[]{:S(2)}) collective-permute-start(bf16[2,320,256]{2,1,0:T(8,128)(2,1)S(1)} %pad_maximum_fusion.5.rest_0_), channel_id=1, source_target_pairs={{0,8},{4,12},{8,0},{12,4},{16,24},{20,28},{24,16},{28,20},{1,9},{5... | collective-permute-start | bytes 983048 | tf_op jit(solution)/shard_map/ppermute | solution.py:237
  7.7 17.7 %collective-permute-start.4 = (bf16[2,320,256]{2,1,0:T(8,128)(2,1)S(1)}, bf16[2,320,256]{2,1,0:T(8,128)(2,1)S(1)}, u32[]{:S(2)}, u32[]{:S(2)}) collective-permute-start(bf16[2,320,256]{2,1,0:T(8,128)(2,1)S(1)} %pad_maximum_fusion.5.rest_0_), channel_id=1, source_target_pairs={{0,16},{4,20},{8,24},{12,28},{16,0},{20,4},{24,8},{28,12},{1,17},{... | collective-permute-start | bytes 983048 | tf_op jit(solution)/shard_map/ppermute | solution.py:237
  25.4 7.9 %collective-permute-start.5 = (bf16[2,320,256]{2,1,0:T(8,128)(2,1)S(1)}, bf16[2,320,256]{2,1,0:T(8,128)(2,1)S(1)}, u32[]{:S(2)}, u32[]{:S(2)}) collective-permute-start(bf16[2,320,256]{2,1,0:T(8,128)(2,1)S(1)} %relay.1.rest_2_), channel_id=1, source_target_pairs={{0,8},{4,12},{8,0},{12,4},{16,24},{20,28},{24,16},{28,20},{1,9},{5... | collective-permute-start | bytes 983048 | tf_op jit(solution)/shard_map/ppermute | solution.py:237
  25.9 0.7 copy-start.5
  34.0 0.7 copy-start.7
  34.7 16.1 %collective-permute-start.9 = (bf16[2,320,256]{2,1,0:T(8,128)(2,1)}, bf16[2,320,256]{2,1,0:T(8,128)(2,1)}, u32[]{:S(2)}, u32[]{:S(2)}) collective-permute-start(bf16[2,320,256]{2,1,0:T(8,128)(2,1)} %release.1.rest_0_), channel_id=1, source_target_pairs={{0,16},{4,20},{8,24},{12,28},{16,0},{20,4},{24,8},{28,12},{1,17},{... | collective-permute-start | bytes 983048 | tf_op jit(solution)/shard_map/ppermute | solution.py:237
  37.1 14.4 %collective-permute-start.8 = (bf16[2,320,256]{2,1,0:T(8,128)(2,1)}, bf16[2,320,256]{2,1,0:T(8,128)(2,1)S(1)}, u32[]{:S(2)}, u32[]{:S(2)}) collective-permute-start(bf16[2,320,256]{2,1,0:T(8,128)(2,1)} %release.1.rest_0_), channel_id=1, source_target_pairs={{0,8},{4,12},{8,0},{12,4},{16,24},{20,28},{24,16},{28,20},{1,9},{5... | collective-permute-start | bytes 983048 | tf_op jit(solution)/shard_map/ppermute | solution.py:237
  38.9 1.7 %copy-start.1 = (bf16[2,2,128,2560]{3,2,1,0:T(8,128)(2,1)S(1)}, bf16[2,2,128,2560]{3,2,1,0:T(8,128)(2,1)}, u32[]{:S(2)}) copy-start(bf16[2,2,128,2560]{3,2,1,0:T(8,128)(2,1)} %param.5) | copy-start | bytes 7864324
  40.6 1.2 %copy-start.3 = (bf16[2,2,8,128,128]{4,3,2,1,0:T(8,128)(2,1)S(1)}, bf16[2,2,8,128,128]{4,3,2,1,0:T(8,128)(2,1)}, u32[]{:S(2)}) copy-start(bf16[2,2,8,128,128]{4,3,2,1,0:T(8,128)(2,1)} %param.6) | copy-start | bytes 3145732
  41.9 1.0 copy-start.6
  42.8 1.0 copy-start.8
  48.9 2.6 %collective-permute-start.6 = (bf16[512,256]{1,0:T(8,128)(2,1)S(1)}, bf16[512,256]{1,0:T(8,128)(2,1)S(1)}, u32[]{:S(2)}, u32[]{:S(2)}) collective-permute-start(bf16[512,256]{1,0:T(8,128)(2,1)S(1)} %get-tuple-element.29.mixed_s), channel_id=1, source_target_pairs={{0,4},{4,0},{8,12},{12,8},{16,20},{20,16},{24,28},{28,24},{1,5},{5... | collective-permute-start | bytes 786440 | tf_op jit(solution)/shard_map/ppermute | solution.py:245
  50.9 8.8 %collective-permute-start.10 = (bf16[2,320,256]{2,1,0:T(8,128)(2,1)}, bf16[2,320,256]{2,1,0:T(8,128)(2,1)S(1)}, u32[]{:S(2)}, u32[]{:S(2)}) collective-permute-start(bf16[2,320,256]{2,1,0:T(8,128)(2,1)} %collective-permute-done.9.rest_2_), channel_id=1, source_target_pairs={{0,8},{4,12},{8,0},{12,4},{16,24},{20,28},{24,16},{28,20},{1,9},{5... | collective-permute-start | bytes 983048 | tf_op jit(solution)/shard_map/ppermute | solution.py:237
  51.6 5.3 %copy-start.9 = (bf16[512,256]{1,0:T(8,128)(2,1)}, bf16[512,256]{1,0:T(8,128)(2,1)S(1)}, u32[]{:S(2)}) copy-start(bf16[512,256]{1,0:T(8,128)(2,1)S(1)} %collective-permute-done.6.rest_0_.mixed_r) | copy-start | bytes 786436
  56.9 5.6 %copy-start.11 = (bf16[2,320,256]{2,1,0:T(8,128)(2,1)}, bf16[2,320,256]{2,1,0:T(8,128)(2,1)S(1)}, u32[]{:S(2)}) copy-start(bf16[2,320,256]{2,1,0:T(8,128)(2,1)S(1)} %get-tuple-element.43) | copy-start | bytes 983044
  62.6 15.5 %collective-permute-start.11 = (bf16[2560,256]{1,0:T(8,128)(2,1)}, bf16[2560,256]{1,0:T(8,128)(2,1)}, u32[]{:S(2)}, u32[]{:S(2)}) collective-permute-start(bf16[2560,256]{1,0:T(8,128)(2,1)} %assemble.1.w_o.w_out), channel_id=1, source_target_pairs={{0,4},{4,0},{8,12},{12,8},{16,20},{20,16},{24,28},{28,24},{1,5},{5... | collective-permute-start | bytes 3932168 | tf_op jit(solution)/shard_map/ppermute | solution.py:245
  62.6 10.9 %collective-permute-start.16 = (bf16[2,320,256]{2,1,0:T(8,128)(2,1)}, bf16[2,320,256]{2,1,0:T(8,128)(2,1)}, u32[]{:S(2)}, u32[]{:S(2)}) collective-permute-start(bf16[2,320,256]{2,1,0:T(8,128)(2,1)} %get-tuple-element.37), channel_id=1, source_target_pairs={{0,8},{4,12},{8,0},{12,4},{16,24},{20,28},{24,16},{28,20},{1,9},{5... | collective-permute-start | bytes 983048 | tf_op jit(solution)/shard_map/ppermute | solution.py:237
  64.5 26.6 %collective-permute-start.18 = (bf16[2,320,256]{2,1,0:T(8,128)(2,1)}, bf16[2,320,256]{2,1,0:T(8,128)(2,1)S(1)}, u32[]{:S(2)}, u32[]{:S(2)}) collective-permute-start(bf16[2,320,256]{2,1,0:T(8,128)(2,1)} %copy-done.11), channel_id=1, source_target_pairs={{0,8},{4,12},{8,0},{12,4},{16,24},{20,28},{24,16},{28,20},{1,9},{5... | collective-permute-start | bytes 983048 | tf_op jit(solution)/shard_map/ppermute | solution.py:237
  64.8 1.2 %copy-start.4 = (bf16[2,2,8,128,128]{4,3,2,1,0:T(8,128)(2,1)S(1)}, bf16[2,2,8,128,128]{4,3,2,1,0:T(8,128)(2,1)}, u32[]{:S(2)}) copy-start(bf16[2,2,8,128,128]{4,3,2,1,0:T(8,128)(2,1)} %param.6) | copy-start | bytes 3145732
  66.0 12.0 %copy-start.10 = (bf16[512,256]{1,0:T(8,128)(2,1)S(1)}, bf16[512,256]{1,0:T(8,128)(2,1)}, u32[]{:S(2)}) copy-start(bf16[512,256]{1,0:T(8,128)(2,1)} %copy-done.9) | copy-start | bytes 786436
  74.6 10.1 %copy-start.2 = (bf16[2,2,128,2560]{3,2,1,0:T(8,128)(2,1)S(1)}, bf16[2,2,128,2560]{3,2,1,0:T(8,128)(2,1)}, u32[]{:S(2)}) copy-start(bf16[2,2,128,2560]{3,2,1,0:T(8,128)(2,1)} %param.5) | copy-start | bytes 7864324
  74.6 17.7 %collective-permute-start.19 = (bf16[2,320,256]{2,1,0:T(8,128)(2,1)S(1)}, bf16[2,320,256]{2,1,0:T(8,128)(2,1)S(1)}, u32[]{:S(2)}, u32[]{:S(2)}) collective-permute-start(bf16[2,320,256]{2,1,0:T(8,128)(2,1)S(1)} %add_convert_fusion.unread), channel_id=1, source_target_pairs={{0,16},{4,20},{8,24},{12,28},{16,0},{20,4},{24,8},{28,12},{1,17},{... | collective-permute-start | bytes 983048 | tf_op jit(solution)/shard_map/ppermute | solution.py:237
  81.6 22.4 %collective-permute-start.12 = (bf16[2,256,640]{2,1,0:T(8,128)(2,1)S(1)}, bf16[2,256,640]{2,1,0:T(8,128)(2,1)S(1)}, u32[]{:S(2)}, u32[]{:S(2)}) collective-permute-start(bf16[2,256,640]{2,1,0:T(8,128)(2,1)S(1)} %get-tuple-element.33), channel_id=1, source_target_pairs={{0,1},{1,0},{2,3},{3,2},{4,5},{5,4},{6,7},{7,6},{8,9},{9,8},{10,11... | collective-permute-start | bytes 1966088 | tf_op jit(solution)/shard_map/ppermute | solution.py:248
  83.2 20.9 %collective-permute-start.14 = (bf16[2,256,640]{2,1,0:T(8,128)(2,1)S(1)}, bf16[2,256,640]{2,1,0:T(8,128)(2,1)S(1)}, u32[]{:S(2)}, u32[]{:S(2)}) collective-permute-start(bf16[2,256,640]{2,1,0:T(8,128)(2,1)S(1)} %get-tuple-element.34), channel_id=1, source_target_pairs={{0,2},{1,3},{2,0},{3,1},{4,6},{5,7},{6,4},{7,5},{8,10},{9,11},{10,... | collective-permute-start | bytes 1966088 | tf_op jit(solution)/shard_map/ppermute | solution.py:248
  89.2 10.1 %collective-permute-start.17 = (bf16[2,320,256]{2,1,0:T(8,128)(2,1)S(1)}, bf16[2,320,256]{2,1,0:T(8,128)(2,1)S(1)}, u32[]{:S(2)}, u32[]{:S(2)}) collective-permute-start(bf16[2,320,256]{2,1,0:T(8,128)(2,1)S(1)} %get-tuple-element.40), channel_id=1, source_target_pairs={{0,8},{4,12},{8,0},{12,4},{16,24},{20,28},{24,16},{28,20},{1,9},{5... | collective-permute-start | bytes 983048 | tf_op jit(solution)/shard_map/ppermute | solution.py:237
  99.4 16.0 %collective-permute-start.20 = (bf16[2,320,256]{2,1,0:T(8,128)(2,1)S(1)}, bf16[2,320,256]{2,1,0:T(8,128)(2,1)S(1)}, u32[]{:S(2)}, u32[]{:S(2)}) collective-permute-start(bf16[2,320,256]{2,1,0:T(8,128)(2,1)S(1)} %get-tuple-element.44), channel_id=1, source_target_pairs={{0,8},{4,12},{8,0},{12,4},{16,24},{20,28},{24,16},{28,20},{1,9},{5... | collective-permute-start | bytes 983048 | tf_op jit(solution)/shard_map/ppermute | solution.py:237
  99.5 19.0 %collective-permute-start.21 = (bf16[2,320,256]{2,1,0:T(8,128)(2,1)S(1)}, bf16[2,320,256]{2,1,0:T(8,128)(2,1)S(1)}, u32[]{:S(2)}, u32[]{:S(2)}) collective-permute-start(bf16[2,320,256]{2,1,0:T(8,128)(2,1)S(1)} %get-tuple-element.45), channel_id=1, source_target_pairs={{0,16},{4,20},{8,24},{12,28},{16,0},{20,4},{24,8},{28,12},{1,17},{... | collective-permute-start | bytes 983048 | tf_op jit(solution)/shard_map/ppermute | solution.py:237
  103.9 14.9 %collective-permute-start.23 = (f32[320,256]{1,0:T(8,128)S(1)}, f32[320,256]{1,0:T(8,128)S(1)}, u32[]{:S(2)}, u32[]{:S(2)}) collective-permute-start(f32[320,256]{1,0:T(8,128)S(1)} %slice_bitcast_fusion.2), channel_id=1, source_target_pairs={{0,4},{4,0},{8,12},{12,8},{16,20},{20,16},{24,28},{28,24},{1,5},{5... | collective-permute-start | bytes 983048 | tf_op jit(solution)/shard_map/ppermute | solution.py:245
  104.4 15.4 %collective-permute-start.13 = (bf16[256,640]{1,0:T(8,128)(2,1)S(1)}, bf16[256,640]{1,0:T(8,128)(2,1)S(1)}, u32[]{:S(2)}, u32[]{:S(2)}) collective-permute-start(bf16[256,640]{1,0:T(8,128)(2,1)S(1)} %get-tuple-element.49), channel_id=1, source_target_pairs={{0,2},{1,3},{2,0},{3,1},{4,6},{5,7},{6,4},{7,5},{8,10},{9,11},{10,... | collective-permute-start | bytes 983048 | tf_op jit(solution)/shard_map/ppermute | solution.py:248
  106.0 13.8 %collective-permute-start.15 = (bf16[256,640]{1,0:T(8,128)(2,1)S(1)}, bf16[256,640]{1,0:T(8,128)(2,1)S(1)}, u32[]{:S(2)}, u32[]{:S(2)}) collective-permute-start(bf16[256,640]{1,0:T(8,128)(2,1)S(1)} %get-tuple-element.50), channel_id=1, source_target_pairs={{0,1},{1,0},{2,3},{3,2},{4,5},{5,4},{6,7},{7,6},{8,9},{9,8},{10,11... | collective-permute-start | bytes 983048 | tf_op jit(solution)/shard_map/ppermute | solution.py:248
  118.7 2.2 %collective-permute-start.22 = (f32[320,256]{1,0:T(8,128)S(1)}, f32[320,256]{1,0:T(8,128)S(1)}, u32[]{:S(2)}, u32[]{:S(2)}) collective-permute-start(f32[320,256]{1,0:T(8,128)S(1)} %slice_bitcast_fusion), channel_id=1, source_target_pairs={{0,4},{4,0},{8,12},{12,8},{16,20},{20,16},{24,28},{28,24},{1,5},{5... | collective-permute-start | bytes 983048 | tf_op jit(solution)/shard_map/ppermute | solution.py:245

commit v12 on v11

--- a/solution.py
+++ b/solution.py
@@ -11,7 +11,6 @@
 HEAD_DIM = 64
 F32 = jnp.float32
 BF16 = jnp.bfloat16
-VMEM_LIMIT = 40 * 1024 * 1024
 
 
 def dot(a, b, ca=1, cb=0):
@@ -175,9 +174,10 @@
     hand_out(idx, 1, grad_v, outs)
 
 
-def release_kernel(unread, block, out):
+def relay_kernel(unread, first, second, first_out, second_out):
     del unread
-    out[...] = block[...]
+    first_out[...] = first[...]
+    second_out[...] = second[...]
 
 
 def sum_kernel(block, got, beside, own, near, far, onward, beside_out, total):
@@ -214,7 +214,7 @@
 VMEM = pl.BlockSpec(memory_space=pltpu.VMEM)
 
 
-def call(kernel, name, in_specs, out_shapes, scratch, flops, size=1 << 20, kinds=None):
+def call(kernel, name, in_specs, out_shapes, scratch, flops, size=1 << 20, kinds=None, vmem=40):
     return pl.pallas_call(
         kernel,
         name=name,
@@ -224,7 +224,7 @@
             jax.ShapeDtypeStruct(s, k) for s, k in zip(out_shapes, kinds or [BF16] * len(out_shapes))
         ],
         scratch_shapes=scratch,
-        compiler_params=pltpu.CompilerParams(vmem_limit_bytes=VMEM_LIMIT),
+        compiler_params=pltpu.CompilerParams(vmem_limit_bytes=vmem << 20),
         cost_estimate=pl.CostEstimate(flops=flops, bytes_accessed=size, transcendentals=0),
     )
 
@@ -307,11 +307,10 @@
         block = u_out.shape
         if line4:
             far, near = swap(u_value, 2), swap(u_value, 1)
-            far = call(release_kernel, "relay", [ANY, VMEM], [block], [], 0)(near, far)[0]
+            far, u_out = call(relay_kernel, "relay", [ANY, VMEM, VMEM], [block] * 2, [], 0)(
+                near, far, u_out
+            )
             value_slots = [u_value, near, far, swap(far, 1)]
-            u_out = call(release_kernel, "release", [ANY, VMEM], [block], [], 0)(
-                value_slots[3], u_out
-            )[0]
             far = swap(u_out, 2)
             out_slots = [u_out, swap(u_out, 1), far, swap(far, 1)]
         else:
@@ -340,6 +339,7 @@
             [rows, halves, mix_scratch, pltpu.SemaphoreType.DMA((4,)), *slots_scratch],
             flops,
             2 * (2 * act.size + mix.size + width * cols + 2 * tokens * cols),
+            vmem=60,
         )(idx, act, act_s, mix, mix_s, *value_slots)
         mixed_r = sibling(mixed_s)
         unread = [mixed_r, *(out_slots[1:3] if line4 else [])]

time: 122 us -> 119 us (0.975)
  local copies, waits for them, and re-layouts: 9.12 us -> 5.25 us
  starting transfers between devices: 29.5 us -> 26 us
  Pallas kernels: 27.8 us -> 31.1 us
  waiting for transfers between devices: 49.5 us -> 51 us
    unnamed x24, local copies, waits for them, and re-layouts: 7.6 us -> 3.16 us
    pallas_call x1, Pallas kernels: 5.14 us -> 8.29 us  [body(): call(functools.partial(mixed_kernel, n_slots), 'mixed', [SMEM] + [ANY] *...]
    ppermute x12, starting transfers between devices: 22.4 us -> 20.2 us  [move(): lax.ppermute(x, 'wide', [(2 * s + c, 2 * d + c) for s, d in pairs for c i...]
    ppermute x12, waiting for transfers between devices: 48.2 us -> 49.7 us  [move(): lax.ppermute(x, 'wide', [(2 * s + c, 2 * d + c) for s, d in pairs for c i...]
  transfers between devices with their start and end apart: 24 -> 24, of which waited for: 11 -> 10; matrix products, arithmetic and copies ran while one was open for 3% -> 3% of each run, Pallas kernels for 20% -> 24%
where the time goes in v12:
time: 119 us; the launch traced here: 118 us
  waiting for transfers between devices  51 us (43%)
  Pallas kernels  31.1 us (26%)
  starting transfers between devices  26 us (22%)
  local copies, waits for them, and re-layouts  5.25 us (4%)
  other arithmetic  3.99 us (3%)
    ppermute x12, waiting for transfers between devices, move(): lax.ppermute(x, 'wide', [(2 * s + c, 2 * d + c) for s, d in pairs for c i...  49.7 us
    ppermute x12, starting transfers between devices, move(): lax.ppermute(x, 'wide', [(2 * s + c, 2 * d + c) for s, d in pairs for c i...  20.2 us
    pallas_call x1, Pallas kernels, body(): call(functools.partial(mixed_kernel, n_slots), 'mixed', [SMEM] + [ANY] *...  8.29 us
    pallas_call x1, Pallas kernels, body(): call(d_value_kernel, 'd_value', [SMEM] + [ANY] * 4 + [VMEM], [(cols, 2 *...  5.53 us
    pallas_call x1, Pallas kernels, body(): call(functools.partial(grad_out_kernel, len(unread)), 'grad_out', [SMEM]...  5.47 us
    pallas_call x1, Pallas kernels, body(): call(gradient_kernel, 'grad_value', [SMEM] + [ANY] * 4 + [VMEM], send_sha...  4.44 us
    ppermute x4, starting transfers between devices, flip(): return lax.ppermute(x, 'node', [(i, i ^ j) for i in range(n_node)])  4.17 us
    pallas_call x1, Pallas kernels, body(): call(functools.partial(terms_kernel, n_node), 'terms', [SMEM] + [VMEM] *...  3.55 us
  transfers between devices with their start and end apart: 24, of which 10 were waited for; matrix products, arithmetic and copies ran while one was open for 3% of the time, Pallas kernels for 24%

profile of v12, /device:TPU:0, one launch (start us, length us, event | category | flops | bytes accessed | tf_op | source)
XLA Modules:
  0.0 118.4 jit_solution(16153692379430561455)
XLA Ops:
  0.7 1.3 %slice_bitcast_fusion.5 = (bf16[1,320,256]{2,1,0:T(8,128)(2,1)S(1)}, bf16[1,320,256]{2,1,0:T(8,128)(2,1)S(1)}, bf16[1,320,256]{2,1,0:T(8,128)(2,1)S(1)}, bf16[1,320,256]{2,1,0:T(8,128)(2,1)S(1)}) fusion(bf16[320,512]{1,0:T(8,128)(2,1)} %param.8, bf16[320,512]{1,0:T(8,128)(2,1)} %param.9), kind=kLoop, calls=%fused_computation.34 | loop fusion | bytes 1310720 | tf_op jit(solution)/shard_map/stack | solution.py:253
  2.0 0.1 broadcast_select_fusion
  2.1 0.5 collective-permute-start
  2.6 1.3 %collective-permute-done = bf16[2,320,256]{2,1,0:T(8,128)(2,1)S(1)} collective-permute-done((bf16[2,320,256]{2,1,0:T(8,128)(2,1)S(1)}, bf16[2,320,256]{2,1,0:T(8,128)(2,1)S(1)}, u32[]{:S(2)}, u32[]{:S(2)}) %collective-permute-start) | collective-permute-done | bytes 327712 | tf_op jit(solution)/shard_map/ppermute | solution.py:245
  3.8 0.4 collective-permute-start.1
  4.2 0.1 collective-permute-start.7
  4.4 0.4 collective-permute-start.2
  4.8 0.0 copy-start.11
  4.8 2.8 %collective-permute-start.3 = (bf16[2,320,256]{2,1,0:T(8,128)(2,1)S(1)}, bf16[2,320,256]{2,1,0:T(8,128)(2,1)S(1)}, u32[]{:S(2)}, u32[]{:S(2)}) collective-permute-start(bf16[2,320,256]{2,1,0:T(8,128)(2,1)S(1)} %pad_maximum_fusion.5.rest_0_), channel_id=1, source_target_pairs={{0,8},{4,12},{8,0},{12,4},{16,24},{20,28},{24,16},{28,20},{1,9},{5... | collective-permute-start | bytes 983048 | tf_op jit(solution)/shard_map/ppermute | solution.py:237
  7.6 2.6 %collective-permute-start.4 = (bf16[2,320,256]{2,1,0:T(8,128)(2,1)S(1)}, bf16[2,320,256]{2,1,0:T(8,128)(2,1)S(1)}, u32[]{:S(2)}, u32[]{:S(2)}) collective-permute-start(bf16[2,320,256]{2,1,0:T(8,128)(2,1)S(1)} %pad_maximum_fusion.5.rest_0_), channel_id=1, source_target_pairs={{0,16},{4,20},{8,24},{12,28},{16,0},{20,4},{24,8},{28,12},{1,17},{... | collective-permute-start | bytes 983048 | tf_op jit(solution)/shard_map/ppermute | solution.py:237
  10.3 12.5 %collective-permute-done.3.unread.rest_1_ = bf16[2,320,256]{2,1,0:T(8,128)(2,1)S(1)} collective-permute-done((bf16[2,320,256]{2,1,0:T(8,128)(2,1)S(1)}, bf16[2,320,256]{2,1,0:T(8,128)(2,1)S(1)}, u32[]{:S(2)}, u32[]{:S(2)}) %collective-permute-start.3) | collective-permute-done | bytes 327712 | tf_op jit(solution)/shard_map/ppermute | solution.py:237
  22.8 2.5 %collective-permute-done.4.first = bf16[2,320,256]{2,1,0:T(8,128)(2,1)S(1)} collective-permute-done((bf16[2,320,256]{2,1,0:T(8,128)(2,1)S(1)}, bf16[2,320,256]{2,1,0:T(8,128)(2,1)S(1)}, u32[]{:S(2)}, u32[]{:S(2)}) %collective-permute-start.4) | collective-permute-done | bytes 327712 | tf_op jit(solution)/shard_map/ppermute | solution.py:237
  25.3 0.9 relay.1
  26.2 0.4 collective-permute-start.5
  26.6 2.6 %collective-permute-start.9 = (bf16[2,320,256]{2,1,0:T(8,128)(2,1)}, bf16[2,320,256]{2,1,0:T(8,128)(2,1)S(1)}, u32[]{:S(2)}, u32[]{:S(2)}) collective-permute-start(bf16[2,320,256]{2,1,0:T(8,128)(2,1)} %get-tuple-element.34.rest_0_), channel_id=1, source_target_pairs={{0,16},{4,20},{8,24},{12,28},{16,0},{20,4},{24,8},{28,12},{1,17},{... | collective-permute-start | bytes 983048 | tf_op jit(solution)/shard_map/ppermute | solution.py:237
  29.2 0.7 stack.67.idx
  29.9 10.9 %collective-permute-done.5.rest_3_ = bf16[2,320,256]{2,1,0:T(8,128)(2,1)} collective-permute-done((bf16[2,320,256]{2,1,0:T(8,128)(2,1)}, bf16[2,320,256]{2,1,0:T(8,128)(2,1)}, u32[]{:S(2)}, u32[]{:S(2)}) %collective-permute-start.5) | collective-permute-done | bytes 327712 | tf_op jit(solution)/shard_map/ppermute | solution.py:237
  40.8 0.0 collective-permute-start.8
  40.8 0.0 collective-permute-done.2.mix_s
  40.8 8.3 %mixed.1 = (bf16[512,256]{1,0:T(8,128)(2,1)}, bf16[512,256]{1,0:T(8,128)(2,1)}) custom-call(s32[5]{0:T(128)} %stack.67.idx, bf16[512,2560]{1,0:T(8,128)(2,1)} %bitcast.54, bf16[512,2560]{1,0:T(8,128)(2,1)} %collective-permute-done.1.act_s.right_s, bf16[4,8,128,128]{3,2,1,0:T(8,128)(2,1)} %bitcast.57, bf16[4,8,128,128]{3,2,1,0:T(8,128)(2,1)} %collective-permute-done.2.mix_s, ...), custom_call_target="tpu_custom_call" | custom-call | flops 1342177280 | bytes 8126464 | tf_op jit(solution)/shard_map/mixed/pallas_call | solution.py:334
  49.1 0.1 collective-permute-start.6
  49.2 2.1 %collective-permute-start.10 = (bf16[2,320,256]{2,1,0:T(8,128)(2,1)S(1)}, bf16[2,320,256]{2,1,0:T(8,128)(2,1)S(1)}, u32[]{:S(2)}, u32[]{:S(2)}) collective-permute-start(bf16[2,320,256]{2,1,0:T(8,128)(2,1)S(1)} %collective-permute-done.9.rest_2_), channel_id=1, source_target_pairs={{0,8},{4,12},{8,0},{12,4},{16,24},{20,28},{24,16},{28,20},{1,9},{5... | collective-permute-start | bytes 983048 | tf_op jit(solution)/shard_map/ppermute | solution.py:237
  51.3 0.9 copy-done.6
  52.2 0.9 copy-done.8
  53.2 5.5 %grad_out.1 = (bf16[16,128]{1,0:T(8,128)(2,1)S(1)}, bf16[2,320,256]{2,1,0:T(8,128)(2,1)S(1)}, bf16[2,320,256]{2,1,0:T(8,128)(2,1)S(1)}, bf16[2,320,256]{2,1,0:T(8,128)(2,1)S(1)}, bf16[2,320,256]{2,1,0:T(8,128)(2,1)}) custom-call(s32[5]{0:T(128)S(1)} %copy-done.9, bf16[512,2560]{1,0:T(8,128)(2,1)S(1)} %bitcast.51, ...), custom_call_target="tpu_custom_call" | custom-call | flops 1342177280 | bytes 7077888 | tf_op jit(solution)/shard_map/grad_out/pallas_call | solution.py:346
  58.7 0.0 copy-start.4
  58.7 0.0 copy-start.10
  58.7 0.9 collective-permute-done.10.rest_3_
  59.6 2.7 %assemble.1.w_o.w_out = bf16[2560,256]{1,0:T(8,128)(2,1)} custom-call(s32[5]{0:T(128)S(1)} %copy-done.9, bf16[16,128]{1,0:T(8,128)(2,1)S(1)} %get-tuple-element.35.token, bf16[2,320,256]{2,1,0:T(8,128)(2,1)} %get-tuple-element.34.rest_0_, bf16[2,320,256]{2,1,0:T(8,128)(2,1)S(1)} %collective-permute-done.8.rest_1_, ...), custom_call_target="tpu_custom_call" | custom-call | bytes 2621440 | tf_op jit(solution)/shard_map/assemble/pallas_call | solution.py:356
  62.3 0.1 collective-permute-start.11
  62.4 1.8 %collective-permute-start.16 = (bf16[2,320,256]{2,1,0:T(8,128)(2,1)}, bf16[2,320,256]{2,1,0:T(8,128)(2,1)S(1)}, u32[]{:S(2)}, u32[]{:S(2)}) collective-permute-start(bf16[2,320,256]{2,1,0:T(8,128)(2,1)} %get-tuple-element.41), channel_id=1, source_target_pairs={{0,8},{4,12},{8,0},{12,4},{16,24},{20,28},{24,16},{28,20},{1,9},{5... | collective-permute-start | bytes 983048 | tf_op jit(solution)/shard_map/ppermute | solution.py:237
  64.2 0.1 pad_add_fusion.idx
  64.3 0.3 collective-permute-start.18
  64.6 1.2 %copy-done.2 = bf16[2,2,8,128,128]{4,3,2,1,0:T(8,128)(2,1)S(1)} copy-done((bf16[2,2,8,128,128]{4,3,2,1,0:T(8,128)(2,1)S(1)}, bf16[2,2,8,128,128]{4,3,2,1,0:T(8,128)(2,1)}, u32[]{:S(2)}) %copy-start.2) | copy-done | bytes 1048600
  65.8 5.5 %d_value.1.left_ref = bf16[256,1024]{1,0:T(8,128)(2,1)S(1)} custom-call(s32[5]{0:T(128)S(1)} %copy-done.9, bf16[512,2560]{1,0:T(8,128)(2,1)S(1)} %bitcast.52, bf16[512,2560]{1,0:T(8,128)(2,1)} %collective-permute-done.7.cot_s, bf16[4,8,128,128]{3,2,1,0:T(8,128)(2,1)S(1)} %bitcast.58, bf16[4,8,128,128]{3,2,1,0:T(8,128)(2,1)} %collective-permute-done.2.mix_s, ...), custom_call_target="tpu_custom_call" | custom-call | flops 1342177280 | bytes 8126464 | tf_op jit(solution)/shard_map/d_value/pallas_call | solution.py:366
  71.4 1.9 %collective-permute-done.16 = bf16[2,320,256]{2,1,0:T(8,128)(2,1)S(1)} collective-permute-done((bf16[2,320,256]{2,1,0:T(8,128)(2,1)}, bf16[2,320,256]{2,1,0:T(8,128)(2,1)S(1)}, u32[]{:S(2)}, u32[]{:S(2)}) %collective-permute-start.16) | collective-permute-done | bytes 327712 | tf_op jit(solution)/shard_map/ppermute | solution.py:237
  73.2 0.1 add_convert_fusion.unread
  73.3 0.0 copy-start.1
  73.3 4.1 %collective-permute-start.19 = (bf16[2,320,256]{2,1,0:T(8,128)(2,1)S(1)}, bf16[2,320,256]{2,1,0:T(8,128)(2,1)S(1)}, u32[]{:S(2)}, u32[]{:S(2)}) collective-permute-start(bf16[2,320,256]{2,1,0:T(8,128)(2,1)S(1)} %add_convert_fusion.unread), channel_id=1, source_target_pairs={{0,16},{4,20},{8,24},{12,28},{16,0},{20,4},{24,8},{28,12},{1,17},{... | collective-permute-start | bytes 983048 | tf_op jit(solution)/shard_map/ppermute | solution.py:237
  77.4 3.6 %terms.1 = (bf16[16,128]{1,0:T(8,128)(2,1)S(1)}, bf16[2,256,640]{2,1,0:T(8,128)(2,1)S(1)}, bf16[2,256,640]{2,1,0:T(8,128)(2,1)S(1)}, bf16[4,256,640]{2,1,0:T(8,128)(2,1)S(1)}) custom-call(s32[4]{0:T(128)S(1)} %pad_add_fusion.idx, bf16[512,256]{1,0:T(8,128)(2,1)S(1)} %copy-done.7, bf16[512,256]{1,0:T(8,128)(2,1)S(1)} %collective-permute-done.6.rest_0_.mixed_r, ...), custom_call_target="tpu_custom_call" | custom-call | flops 1342177280 | bytes 5767168 | tf_op jit(solution)/shard_map/terms/pallas_call | solution.py:387
  81.0 1.6 %collective-permute-start.12 = (bf16[2,256,640]{2,1,0:T(8,128)(2,1)S(1)}, bf16[2,256,640]{2,1,0:T(8,128)(2,1)S(1)}, u32[]{:S(2)}, u32[]{:S(2)}) collective-permute-start(bf16[2,256,640]{2,1,0:T(8,128)(2,1)S(1)} %get-tuple-element.37), channel_id=1, source_target_pairs={{0,1},{1,0},{2,3},{3,2},{4,5},{5,4},{6,7},{7,6},{8,9},{9,8},{10,11... | collective-permute-start | bytes 1966088 | tf_op jit(solution)/shard_map/ppermute | solution.py:248
  82.6 1.5 %collective-permute-start.14 = (bf16[2,256,640]{2,1,0:T(8,128)(2,1)S(1)}, bf16[2,256,640]{2,1,0:T(8,128)(2,1)S(1)}, u32[]{:S(2)}, u32[]{:S(2)}) collective-permute-start(bf16[2,256,640]{2,1,0:T(8,128)(2,1)S(1)} %get-tuple-element.38), channel_id=1, source_target_pairs={{0,2},{1,3},{2,0},{3,1},{4,6},{5,7},{6,4},{7,5},{8,10},{9,11},{10,... | collective-permute-start | bytes 1966088 | tf_op jit(solution)/shard_map/ppermute | solution.py:248
  84.1 4.4 %grad_value.1 = (bf16[2,320,256]{2,1,0:T(8,128)(2,1)S(1)}, bf16[2,320,256]{2,1,0:T(8,128)(2,1)S(1)}, bf16[2,320,256]{2,1,0:T(8,128)(2,1)S(1)}, bf16[2,320,256]{2,1,0:T(8,128)(2,1)S(1)}) custom-call(s32[5]{0:T(128)S(1)} %copy-done.9, bf16[16,128]{1,0:T(8,128)(2,1)S(1)} %get-tuple-element.39.token, bf16[2,320,256]{2,1,0:T(8,128)(2,1)S(1)} %add_convert_fusion.unread, ...), custom_call_target="tpu_custom_call" | custom-call | flops 1342177280 | bytes 7077888 | tf_op jit(solution)/shard_map/grad_value/pallas_call | solution.py:397
  88.5 0.3 collective-permute-start.17
  88.9 0.2 convert_element_type.50
  89.0 2.7 %collective-permute-done.19.far = bf16[2,320,256]{2,1,0:T(8,128)(2,1)S(1)} collective-permute-done((bf16[2,320,256]{2,1,0:T(8,128)(2,1)S(1)}, bf16[2,320,256]{2,1,0:T(8,128)(2,1)S(1)}, u32[]{:S(2)}, u32[]{:S(2)}) %collective-permute-start.19) | collective-permute-done | bytes 327712 | tf_op jit(solution)/shard_map/ppermute | solution.py:237
  91.7 6.1 %collective-permute-done.17.got = bf16[2,320,256]{2,1,0:T(8,128)(2,1)S(1)} collective-permute-done((bf16[2,320,256]{2,1,0:T(8,128)(2,1)S(1)}, bf16[2,320,256]{2,1,0:T(8,128)(2,1)S(1)}, u32[]{:S(2)}, u32[]{:S(2)}) %collective-permute-start.17) | collective-permute-done | bytes 327712 | tf_op jit(solution)/shard_map/ppermute | solution.py:237
  97.8 0.2 sum.1
  98.0 0.1 collective-permute-start.20
  98.0 3.0 %collective-permute-start.21 = (bf16[2,320,256]{2,1,0:T(8,128)(2,1)S(1)}, bf16[2,320,256]{2,1,0:T(8,128)(2,1)S(1)}, u32[]{:S(2)}, u32[]{:S(2)}) collective-permute-start(bf16[2,320,256]{2,1,0:T(8,128)(2,1)S(1)} %get-tuple-element.49), channel_id=1, source_target_pairs={{0,16},{4,20},{8,24},{12,28},{16,0},{20,4},{24,8},{28,12},{1,17},{... | collective-permute-start | bytes 983048 | tf_op jit(solution)/shard_map/ppermute | solution.py:237
  101.1 0.1 collective-permute-start.23
  101.2 0.1 convert_element_type.51
  101.3 0.1 convert_element_type.55
  101.4 0.1 fusion.8
  101.5 0.6 collective-permute-start.13
  102.1 0.5 collective-permute-start.15
  102.6 10.4 %collective-permute-done.20 = bf16[2,320,256]{2,1,0:T(8,128)(2,1)S(1)} collective-permute-done((bf16[2,320,256]{2,1,0:T(8,128)(2,1)S(1)}, bf16[2,320,256]{2,1,0:T(8,128)(2,1)S(1)}, u32[]{:S(2)}, u32[]{:S(2)}) %collective-permute-start.20) | collective-permute-done | bytes 327712 | tf_op jit(solution)/shard_map/ppermute | solution.py:237
  113.1 1.9 %collective-permute-done.21 = bf16[2,320,256]{2,1,0:T(8,128)(2,1)S(1)} collective-permute-done((bf16[2,320,256]{2,1,0:T(8,128)(2,1)S(1)}, bf16[2,320,256]{2,1,0:T(8,128)(2,1)S(1)}, u32[]{:S(2)}, u32[]{:S(2)}) %collective-permute-start.21) | collective-permute-done | bytes 327712 | tf_op jit(solution)/shard_map/ppermute | solution.py:237
  115.0 0.1 convert_add_fusion
  115.2 0.1 collective-permute-start.22
  115.3 0.9 pad_maximum_fusion.2
  116.2 0.2 fusion.7
  116.5 0.9 pad_maximum_fusion
  117.4 0.9 pad_maximum_fusion.1
  (38 shorter events, 0.3 us)
Async XLA Ops:
  0.6 3.6 %copy-start = (bf16[2,2,128,2560]{3,2,1,0:T(8,128)(2,1)S(1)}, bf16[2,2,128,2560]{3,2,1,0:T(8,128)(2,1)}, u32[]{:S(2)}) copy-start(bf16[2,2,128,2560]{3,2,1,0:T(8,128)(2,1)} %param.7) | copy-start | bytes 7864324
  2.1 1.8 %collective-permute-start = (bf16[2,320,256]{2,1,0:T(8,128)(2,1)S(1)}, bf16[2,320,256]{2,1,0:T(8,128)(2,1)S(1)}, u32[]{:S(2)}, u32[]{:S(2)}) collective-permute-start(bf16[2,320,256]{2,1,0:T(8,128)(2,1)S(1)} %get-tuple-element.60), channel_id=1, source_target_pairs={{0,4},{4,0},{8,12},{12,8},{16,20},{20,16},{24,28},{28,24},{1,5},{5... | collective-permute-start | bytes 983048 | tf_op jit(solution)/shard_map/ppermute | solution.py:245
  3.8 36.9 %collective-permute-start.1 = (bf16[512,2560]{1,0:T(8,128)(2,1)}, bf16[512,2560]{1,0:T(8,128)(2,1)}, u32[]{:S(2)}, u32[]{:S(2)}) collective-permute-start(bf16[512,2560]{1,0:T(8,128)(2,1)} %bitcast.53), channel_id=1, source_target_pairs={{0,4},{4,0},{8,12},{12,8},{16,20},{20,16},{24,28},{28,24},{1,5},{5... | collective-permute-start | bytes 7864328 | tf_op jit(solution)/shard_map/ppermute | solution.py:245
  4.2 47.1 %collective-permute-start.7 = (bf16[512,2560]{1,0:T(8,128)(2,1)S(1)}, bf16[512,2560]{1,0:T(8,128)(2,1)}, u32[]{:S(2)}, u32[]{:S(2)}) collective-permute-start(bf16[512,2560]{1,0:T(8,128)(2,1)S(1)} %bitcast.50), channel_id=1, source_target_pairs={{0,4},{4,0},{8,12},{12,8},{16,20},{20,16},{24,28},{28,24},{1,5},{5... | collective-permute-start | bytes 7864328 | tf_op jit(solution)/shard_map/ppermute | solution.py:245
  4.4 36.4 %collective-permute-start.2 = (bf16[4,8,128,128]{3,2,1,0:T(8,128)(2,1)}, bf16[4,8,128,128]{3,2,1,0:T(8,128)(2,1)}, u32[]{:S(2)}, u32[]{:S(2)}) collective-permute-start(bf16[4,8,128,128]{3,2,1,0:T(8,128)(2,1)} %bitcast.56), channel_id=1, source_target_pairs={{0,4},{4,0},{8,12},{12,8},{16,20},{20,16},{24,28},{28,24},{1,5},{5... | collective-permute-start | bytes 3145736 | tf_op jit(solution)/shard_map/ppermute | solution.py:245
  4.8 17.9 %copy-start.11 = (bf16[2,320,256]{2,1,0:T(8,128)(2,1)}, bf16[2,320,256]{2,1,0:T(8,128)(2,1)S(1)}, u32[]{:S(2)}) copy-start(bf16[2,320,256]{2,1,0:T(8,128)(2,1)S(1)} %pad_maximum_fusion.5.rest_0_) | copy-start | bytes 983044
  4.8 17.9 %collective-permute-start.3 = (bf16[2,320,256]{2,1,0:T(8,128)(2,1)S(1)}, bf16[2,320,256]{2,1,0:T(8,128)(2,1)S(1)}, u32[]{:S(2)}, u32[]{:S(2)}) collective-permute-start(bf16[2,320,256]{2,1,0:T(8,128)(2,1)S(1)} %pad_maximum_fusion.5.rest_0_), channel_id=1, source_target_pairs={{0,8},{4,12},{8,0},{12,4},{16,24},{20,28},{24,16},{28,20},{1,9},{5... | collective-permute-start | bytes 983048 | tf_op jit(solution)/shard_map/ppermute | solution.py:237
  7.6 17.7 %collective-permute-start.4 = (bf16[2,320,256]{2,1,0:T(8,128)(2,1)S(1)}, bf16[2,320,256]{2,1,0:T(8,128)(2,1)S(1)}, u32[]{:S(2)}, u32[]{:S(2)}) collective-permute-start(bf16[2,320,256]{2,1,0:T(8,128)(2,1)S(1)} %pad_maximum_fusion.5.rest_0_), channel_id=1, source_target_pairs={{0,16},{4,20},{8,24},{12,28},{16,0},{20,4},{24,8},{28,12},{1,17},{... | collective-permute-start | bytes 983048 | tf_op jit(solution)/shard_map/ppermute | solution.py:237
  22.8 18.0 %copy-start.3 = (bf16[2,320,256]{2,1,0:T(8,128)(2,1)}, bf16[2,320,256]{2,1,0:T(8,128)(2,1)S(1)}, u32[]{:S(2)}) copy-start(bf16[2,320,256]{2,1,0:T(8,128)(2,1)S(1)} %collective-permute-done.3.unread.rest_1_) | copy-start | bytes 983044
  26.2 14.6 %collective-permute-start.5 = (bf16[2,320,256]{2,1,0:T(8,128)(2,1)}, bf16[2,320,256]{2,1,0:T(8,128)(2,1)}, u32[]{:S(2)}, u32[]{:S(2)}) collective-permute-start(bf16[2,320,256]{2,1,0:T(8,128)(2,1)} %get-tuple-element.30.rest_2_), channel_id=1, source_target_pairs={{0,8},{4,12},{8,0},{12,4},{16,24},{20,28},{24,16},{28,20},{1,9},{5... | collective-permute-start | bytes 983048 | tf_op jit(solution)/shard_map/ppermute | solution.py:237
  26.6 22.6 %collective-permute-start.9 = (bf16[2,320,256]{2,1,0:T(8,128)(2,1)}, bf16[2,320,256]{2,1,0:T(8,128)(2,1)S(1)}, u32[]{:S(2)}, u32[]{:S(2)}) collective-permute-start(bf16[2,320,256]{2,1,0:T(8,128)(2,1)} %get-tuple-element.34.rest_0_), channel_id=1, source_target_pairs={{0,16},{4,20},{8,24},{12,28},{16,0},{20,4},{24,8},{28,12},{1,17},{... | collective-permute-start | bytes 983048 | tf_op jit(solution)/shard_map/ppermute | solution.py:237
  29.9 21.4 %copy-start.9 = (s32[5]{0:T(128)S(1)}, s32[5]{0:T(128)}, u32[]{:S(2)}) copy-start(s32[5]{0:T(128)} %stack.67.idx) | copy-start | bytes 64
  40.8 10.5 %collective-permute-start.8 = (bf16[2,320,256]{2,1,0:T(8,128)(2,1)}, bf16[2,320,256]{2,1,0:T(8,128)(2,1)S(1)}, u32[]{:S(2)}, u32[]{:S(2)}) collective-permute-start(bf16[2,320,256]{2,1,0:T(8,128)(2,1)} %get-tuple-element.34.rest_0_), channel_id=1, source_target_pairs={{0,8},{4,12},{8,0},{12,4},{16,24},{20,28},{24,16},{28,20},{1,9},{5... | collective-permute-start | bytes 983048 | tf_op jit(solution)/shard_map/ppermute | solution.py:237
  49.1 2.2 %collective-permute-start.6 = (bf16[512,256]{1,0:T(8,128)(2,1)}, bf16[512,256]{1,0:T(8,128)(2,1)S(1)}, u32[]{:S(2)}, u32[]{:S(2)}) collective-permute-start(bf16[512,256]{1,0:T(8,128)(2,1)} %get-tuple-element.32.mixed_s), channel_id=1, source_target_pairs={{0,4},{4,0},{8,12},{12,8},{16,20},{20,16},{24,28},{28,24},{1,5},{5... | collective-permute-start | bytes 786440 | tf_op jit(solution)/shard_map/ppermute | solution.py:245
  49.2 10.4 %collective-permute-start.10 = (bf16[2,320,256]{2,1,0:T(8,128)(2,1)S(1)}, bf16[2,320,256]{2,1,0:T(8,128)(2,1)S(1)}, u32[]{:S(2)}, u32[]{:S(2)}) collective-permute-start(bf16[2,320,256]{2,1,0:T(8,128)(2,1)S(1)} %collective-permute-done.9.rest_2_), channel_id=1, source_target_pairs={{0,8},{4,12},{8,0},{12,4},{16,24},{20,28},{24,16},{28,20},{1,9},{5... | collective-permute-start | bytes 983048 | tf_op jit(solution)/shard_map/ppermute | solution.py:237
  51.3 1.0 copy-start.6
  52.2 0.9 copy-start.8
  58.7 3.7 %copy-start.4 = (bf16[2,320,256]{2,1,0:T(8,128)(2,1)}, bf16[2,320,256]{2,1,0:T(8,128)(2,1)S(1)}, u32[]{:S(2)}) copy-start(bf16[2,320,256]{2,1,0:T(8,128)(2,1)S(1)} %get-tuple-element.46.own) | copy-start | bytes 983044
  58.7 3.7 %copy-start.10 = (bf16[2,320,256]{2,1,0:T(8,128)(2,1)}, bf16[2,320,256]{2,1,0:T(8,128)(2,1)S(1)}, u32[]{:S(2)}) copy-start(bf16[2,320,256]{2,1,0:T(8,128)(2,1)S(1)} %get-tuple-element.47) | copy-start | bytes 983044
  62.3 15.1 %collective-permute-start.11 = (bf16[2560,256]{1,0:T(8,128)(2,1)}, bf16[2560,256]{1,0:T(8,128)(2,1)}, u32[]{:S(2)}, u32[]{:S(2)}) collective-permute-start(bf16[2560,256]{1,0:T(8,128)(2,1)} %assemble.1.w_o.w_out), channel_id=1, source_target_pairs={{0,4},{4,0},{8,12},{12,8},{16,20},{20,16},{24,28},{28,24},{1,5},{5... | collective-permute-start | bytes 3932168 | tf_op jit(solution)/shard_map/ppermute | solution.py:245
  62.4 10.8 %collective-permute-start.16 = (bf16[2,320,256]{2,1,0:T(8,128)(2,1)}, bf16[2,320,256]{2,1,0:T(8,128)(2,1)S(1)}, u32[]{:S(2)}, u32[]{:S(2)}) collective-permute-start(bf16[2,320,256]{2,1,0:T(8,128)(2,1)} %get-tuple-element.41), channel_id=1, source_target_pairs={{0,8},{4,12},{8,0},{12,4},{16,24},{20,28},{24,16},{28,20},{1,9},{5... | collective-permute-start | bytes 983048 | tf_op jit(solution)/shard_map/ppermute | solution.py:237
  64.3 24.7 %collective-permute-start.18 = (bf16[2,320,256]{2,1,0:T(8,128)(2,1)}, bf16[2,320,256]{2,1,0:T(8,128)(2,1)S(1)}, u32[]{:S(2)}, u32[]{:S(2)}) collective-permute-start(bf16[2,320,256]{2,1,0:T(8,128)(2,1)} %copy-done.10), channel_id=1, source_target_pairs={{0,8},{4,12},{8,0},{12,4},{16,24},{20,28},{24,16},{28,20},{1,9},{5... | collective-permute-start | bytes 983048 | tf_op jit(solution)/shard_map/ppermute | solution.py:237
  64.6 1.2 %copy-start.2 = (bf16[2,2,8,128,128]{4,3,2,1,0:T(8,128)(2,1)S(1)}, bf16[2,2,8,128,128]{4,3,2,1,0:T(8,128)(2,1)}, u32[]{:S(2)}) copy-start(bf16[2,2,8,128,128]{4,3,2,1,0:T(8,128)(2,1)} %param.6) | copy-start | bytes 3145732
  65.8 11.6 %copy-start.7 = (bf16[512,256]{1,0:T(8,128)(2,1)S(1)}, bf16[512,256]{1,0:T(8,128)(2,1)}, u32[]{:S(2)}) copy-start(bf16[512,256]{1,0:T(8,128)(2,1)} %get-tuple-element.31.mixed_o) | copy-start | bytes 786436
  73.3 10.8 %copy-start.1 = (bf16[2,2,128,2560]{3,2,1,0:T(8,128)(2,1)S(1)}, bf16[2,2,128,2560]{3,2,1,0:T(8,128)(2,1)}, u32[]{:S(2)}) copy-start(bf16[2,2,128,2560]{3,2,1,0:T(8,128)(2,1)} %param.5) | copy-start | bytes 7864324
  73.3 18.4 %collective-permute-start.19 = (bf16[2,320,256]{2,1,0:T(8,128)(2,1)S(1)}, bf16[2,320,256]{2,1,0:T(8,128)(2,1)S(1)}, u32[]{:S(2)}, u32[]{:S(2)}) collective-permute-start(bf16[2,320,256]{2,1,0:T(8,128)(2,1)S(1)} %add_convert_fusion.unread), channel_id=1, source_target_pairs={{0,16},{4,20},{8,24},{12,28},{16,0},{20,4},{24,8},{28,12},{1,17},{... | collective-permute-start | bytes 983048 | tf_op jit(solution)/shard_map/ppermute | solution.py:237
  81.0 20.2 %collective-permute-start.12 = (bf16[2,256,640]{2,1,0:T(8,128)(2,1)S(1)}, bf16[2,256,640]{2,1,0:T(8,128)(2,1)S(1)}, u32[]{:S(2)}, u32[]{:S(2)}) collective-permute-start(bf16[2,256,640]{2,1,0:T(8,128)(2,1)S(1)} %get-tuple-element.37), channel_id=1, source_target_pairs={{0,1},{1,0},{2,3},{3,2},{4,5},{5,4},{6,7},{7,6},{8,9},{9,8},{10,11... | collective-permute-start | bytes 1966088 | tf_op jit(solution)/shard_map/ppermute | solution.py:248
  82.6 18.7 %collective-permute-start.14 = (bf16[2,256,640]{2,1,0:T(8,128)(2,1)S(1)}, bf16[2,256,640]{2,1,0:T(8,128)(2,1)S(1)}, u32[]{:S(2)}, u32[]{:S(2)}) collective-permute-start(bf16[2,256,640]{2,1,0:T(8,128)(2,1)S(1)} %get-tuple-element.38), channel_id=1, source_target_pairs={{0,2},{1,3},{2,0},{3,1},{4,6},{5,7},{6,4},{7,5},{8,10},{9,11},{10,... | collective-permute-start | bytes 1966088 | tf_op jit(solution)/shard_map/ppermute | solution.py:248
  88.5 9.2 %collective-permute-start.17 = (bf16[2,320,256]{2,1,0:T(8,128)(2,1)S(1)}, bf16[2,320,256]{2,1,0:T(8,128)(2,1)S(1)}, u32[]{:S(2)}, u32[]{:S(2)}) collective-permute-start(bf16[2,320,256]{2,1,0:T(8,128)(2,1)S(1)} %get-tuple-element.44), channel_id=1, source_target_pairs={{0,8},{4,12},{8,0},{12,4},{16,24},{20,28},{24,16},{28,20},{1,9},{5... | collective-permute-start | bytes 983048 | tf_op jit(solution)/shard_map/ppermute | solution.py:237
  88.9 8.9 %copy-start.5 = (bf16[2,320,256]{2,1,0:T(8,128)(2,1)S(1)}, bf16[2,320,256]{2,1,0:T(8,128)(2,1)}, u32[]{:S(2)}) copy-start(bf16[2,320,256]{2,1,0:T(8,128)(2,1)} %copy-done.4) | copy-start | bytes 983044
  98.0 15.1 %collective-permute-start.20 = (bf16[2,320,256]{2,1,0:T(8,128)(2,1)S(1)}, bf16[2,320,256]{2,1,0:T(8,128)(2,1)S(1)}, u32[]{:S(2)}, u32[]{:S(2)}) collective-permute-start(bf16[2,320,256]{2,1,0:T(8,128)(2,1)S(1)} %get-tuple-element.48), channel_id=1, source_target_pairs={{0,8},{4,12},{8,0},{12,4},{16,24},{20,28},{24,16},{28,20},{1,9},{5... | collective-permute-start | bytes 983048 | tf_op jit(solution)/shard_map/ppermute | solution.py:237
  98.0 17.0 %collective-permute-start.21 = (bf16[2,320,256]{2,1,0:T(8,128)(2,1)S(1)}, bf16[2,320,256]{2,1,0:T(8,128)(2,1)S(1)}, u32[]{:S(2)}, u32[]{:S(2)}) collective-permute-start(bf16[2,320,256]{2,1,0:T(8,128)(2,1)S(1)} %get-tuple-element.49), channel_id=1, source_target_pairs={{0,16},{4,20},{8,24},{12,28},{16,0},{20,4},{24,8},{28,12},{1,17},{... | collective-permute-start | bytes 983048 | tf_op jit(solution)/shard_map/ppermute | solution.py:237
  101.1 14.1 %collective-permute-start.23 = (f32[320,256]{1,0:T(8,128)S(1)}, f32[320,256]{1,0:T(8,128)S(1)}, u32[]{:S(2)}, u32[]{:S(2)}) collective-permute-start(f32[320,256]{1,0:T(8,128)S(1)} %slice_bitcast_fusion.2), channel_id=1, source_target_pairs={{0,4},{4,0},{8,12},{12,8},{16,20},{20,16},{24,28},{28,24},{1,5},{5... | collective-permute-start | bytes 983048 | tf_op jit(solution)/shard_map/ppermute | solution.py:245
  101.5 14.7 %collective-permute-start.13 = (bf16[256,640]{1,0:T(8,128)(2,1)S(1)}, bf16[256,640]{1,0:T(8,128)(2,1)S(1)}, u32[]{:S(2)}, u32[]{:S(2)}) collective-permute-start(bf16[256,640]{1,0:T(8,128)(2,1)S(1)} %get-tuple-element.53), channel_id=1, source_target_pairs={{0,2},{1,3},{2,0},{3,1},{4,6},{5,7},{6,4},{7,5},{8,10},{9,11},{10,... | collective-permute-start | bytes 983048 | tf_op jit(solution)/shard_map/ppermute | solution.py:248
  102.1 14.1 %collective-permute-start.15 = (bf16[256,640]{1,0:T(8,128)(2,1)S(1)}, bf16[256,640]{1,0:T(8,128)(2,1)S(1)}, u32[]{:S(2)}, u32[]{:S(2)}) collective-permute-start(bf16[256,640]{1,0:T(8,128)(2,1)S(1)} %get-tuple-element.54), channel_id=1, source_target_pairs={{0,1},{1,0},{2,3},{3,2},{4,5},{5,4},{6,7},{7,6},{8,9},{9,8},{10,11... | collective-permute-start | bytes 983048 | tf_op jit(solution)/shard_map/ppermute | solution.py:248
  115.2 2.2 %collective-permute-start.22 = (f32[320,256]{1,0:T(8,128)S(1)}, f32[320,256]{1,0:T(8,128)S(1)}, u32[]{:S(2)}, u32[]{:S(2)}) collective-permute-start(f32[320,256]{1,0:T(8,128)S(1)} %slice_bitcast_fusion), channel_id=1, source_target_pairs={{0,4},{4,0},{8,12},{12,8},{16,20},{20,16},{24,28},{28,24},{1,5},{5... | collective-permute-start | bytes 983048 | tf_op jit(solution)/shard_map/ppermute | solution.py:245

commit v13 on v12

--- a/solution.py
+++ b/solution.py
@@ -32,14 +32,9 @@
     return pl.ds(pl.multiple_of(index * size, math.gcd(size, 16)), size)
 
 
-def place(idx, slots_v, w_ref):
-    core = idx[0]
+def place(idx, core, slots_v, w_ref):
     for j in range(slots_v.shape[0]):
-        depth = slots_v.shape[2]
-        mine, other = slots_v[j, 0], slots_v[j, 1]
-        low = jnp.where(core == 0, mine, other)
-        high = jnp.where(core == 0, other, mine)
-        w_ref[rows_at(idx[1 + j], 2 * depth), :] = jnp.concatenate([low, high], axis=0)
+        w_ref[rows_at(idx[1 + j], 2 * slots_v.shape[2]), :] = whole(core, slots_v[j])
 
 
 def hand_out(idx, base, grad_v, outs):
@@ -63,17 +58,110 @@
     return [(h, min(2, heads - h)) for h in range(0, heads, 2)]
 
 
-def assemble_kernel(idx, token, *rest):
-    del token
-    slots, (w_out, slots_v, sems) = rest[:-3], rest[-3:]
-    for copy in begin_slots(slots, slots_v, sems):
+def whole(core, slot):
+    mine, other = slot[0], slot[1]
+    low = jnp.where(core == 0, mine, other)
+    high = jnp.where(core == 0, other, mine)
+    return jnp.concatenate([low, high], axis=0)
+
+
+def part_kernel(n_slots, idx, x_o, x_s, mix_o, mix_s, *rest):
+    slots, rest = rest[:n_slots], rest[n_slots:]
+    part, last, weights, w_v, x_v, slots_v, x_sems, sems, slot_sems = rest
+    heads, depth = weights.shape[2], last.shape[2]
+    here = pl.ds(idx[0] * heads, heads)
+    missing = idx[1 + n_slots]
+    columns = pl.ds(pl.multiple_of(missing * depth, 128), depth)
+    copies = begin_slots(slots, slots_v, slot_sems)
+    halves = begin([(x_o, x_v.at[0]), (x_s, x_v.at[1])], x_sems)
+    later = begin(
+        [(x_o.at[:, columns], last.at[0]), (x_s.at[:, columns], last.at[1])]
+        + [(mix_o.at[:, here], weights.at[0]), (mix_s.at[:, here], weights.at[1])],
+        sems,
+    )
+    for copy in copies:
         copy.wait()
-    place(idx, slots_v, w_out)
+    place(idx, idx[0], slots_v, w_v)
+    w_v[rows_at(missing, depth), :] = jnp.zeros((depth, w_v.shape[1]), BF16)
+    for half in range(2):
+        halves[half].wait()
+        part[half] = dot(x_v[half], w_v[...])
+    for copy in later:
+        copy.wait()
+
+
+def mix_values(value, weights, out):
+    groups, heads, seq, _ = weights.shape
+    for g in range(groups):
+        for h, n in head_pairs(heads):
+            part = value[g * seq : (g + 1) * seq, h * HEAD_DIM : (h + n) * HEAD_DIM]
+            both = weights[g, h]
+            if n == 2:
+                lane = lax.broadcasted_iota(jnp.int32, part.shape, 1)
+                zero = jnp.zeros_like(part)
+                part = jnp.concatenate(
+                    [
+                        jnp.where(lane < HEAD_DIM, part, zero),
+                        jnp.where(lane < HEAD_DIM, zero, part),
+                    ],
+                    axis=0,
+                )
+                both = jnp.concatenate([both, weights[g, h + 1]], axis=1)
+            out[g * seq : (g + 1) * seq, h * HEAD_DIM : (h + n) * HEAD_DIM] = dot(
+                both, part
+            ).astype(BF16)
+
+
+def mix_back(d_mixed, weights, left_v, start):
+    groups, heads, seq, _ = weights.shape
+    for g in range(groups):
+        turned = d_mixed[g * seq : (g + 1) * seq, :].T.astype(BF16)
+        at = start + g * seq
+        for h, n in head_pairs(heads):
+            part = turned[h * HEAD_DIM : (h + n) * HEAD_DIM, :]
+            if n == 2:
+                row = lax.broadcasted_iota(jnp.int32, part.shape, 0)
+                zero = jnp.zeros_like(part)
+                part = jnp.concatenate(
+                    [
+                        jnp.where(row < HEAD_DIM, part, zero),
+                        jnp.where(row < HEAD_DIM, zero, part),
+                    ],
+                    axis=1,
+                )
+            both = weights[g, h : h + n].reshape(n * seq, seq)
+            left_v[h * HEAD_DIM : (h + n) * HEAD_DIM, at : at + seq] = dot(part, both).astype(BF16)
+
+
+def mixed_rest_kernel(idx, part, last, weights, slot, mixed_o, mixed_s):
+    w_last = whole(idx[0], slot)
+    for half, out in enumerate((mixed_o, mixed_s)):
+        value = (part[half] + dot(last[half], w_last)).astype(BF16)
+        mix_values(value, weights.at[half], out)
+
+
+def d_value_rest_kernel(idx, part, last, weights, slot, left_v, slot_out):
+    slot_out[...] = slot[...]
+    w_last = whole(idx[0], slot)
+    tokens = part.shape[1]
+    for half in range(2):
+        mix_back(part[half] + dot(last[half], w_last), weights.at[half], left_v, half * tokens)
+
+
+def assemble_kernel(n_slots, idx, unread, *rest):
+    del unread
+    slots, (w_out, slots_v, sems) = rest[:n_slots], rest[n_slots:]
+    copies = begin_slots(slots, slots_v, sems)
+    planes, depth = idx.shape[0] - 1, 2 * slots_v.shape[2]
+    for j in range(n_slots, planes):
+        w_out[rows_at(idx[1 + j], depth), :] = jnp.zeros((depth, w_out.shape[1]), BF16)
+    for copy in copies:
+        copy.wait()
+    place(idx, idx[0], slots_v, w_out)
 
 
 def d_value_kernel(idx, cot_o, cot_s, mix_o, mix_s, w_out, left_v, cot_v, mix_v, sems):
-    groups, _, seq, _ = mix_o.shape
-    heads = mix_v.shape[2]
+    tokens, heads = cot_o.shape[0], mix_v.shape[2]
     here = pl.ds(idx[0] * heads, heads)
     copies = begin(
         [(cot_o, cot_v.at[0]), (mix_o.at[:, here], mix_v.at[0])]
@@ -84,25 +172,7 @@
         copies[2 * half].wait()
         d_mixed = dot(cot_v[half], w_out[...])
         copies[2 * half + 1].wait()
-        for g in range(groups):
-            turned = d_mixed[g * seq : (g + 1) * seq, :].T.astype(BF16)
-            at = (half * groups + g) * seq
-            for h, n in head_pairs(heads):
-                part = turned[h * HEAD_DIM : (h + n) * HEAD_DIM, :]
-                if n == 2:
-                    row = lax.broadcasted_iota(jnp.int32, part.shape, 0)
-                    zero = jnp.zeros_like(part)
-                    part = jnp.concatenate(
-                        [
-                            jnp.where(row < HEAD_DIM, part, zero),
-                            jnp.where(row < HEAD_DIM, zero, part),
-                        ],
-                        axis=1,
-                    )
-                weights = mix_v[half, g, h : h + n].reshape(n * seq, seq)
-                left_v[h * HEAD_DIM : (h + n) * HEAD_DIM, at : at + seq] = dot(
-                    part, weights
-                ).astype(BF16)
+        mix_back(d_mixed, mix_v.at[half], left_v, half * tokens)
 
 
 def gradient_kernel(idx, token, unread, right_o, right_s, left_ref, *rest):
@@ -122,7 +192,6 @@
 def mixed_kernel(n_slots, idx, act_o, act_s, mix_o, mix_s, *rest):
     slots, rest = rest[:n_slots], rest[n_slots:]
     mixed_o, mixed_s, w_v, act_v, mix_v, sems, slots_v, slot_sems = rest
-    groups, _, seq, _ = mix_o.shape
     heads = mix_v.shape[2]
     here = pl.ds(idx[0] * heads, heads)
     slot_copies = begin_slots(slots, slots_v, slot_sems)
@@ -133,45 +202,45 @@
     )
     for copy in slot_copies:
         copy.wait()
-    place(idx, slots_v, w_v)
+    place(idx, idx[0], slots_v, w_v)
     for half, out in enumerate((mixed_o, mixed_s)):
         copies[2 * half].wait()
         value = dot(act_v[half], w_v[...]).astype(BF16)
         copies[2 * half + 1].wait()
-        for g in range(groups):
-            for h, n in head_pairs(heads):
-                part = value[g * seq : (g + 1) * seq, h * HEAD_DIM : (h + n) * HEAD_DIM]
-                weights = mix_v[half, g, h]
-                if n == 2:
-                    lane = lax.broadcasted_iota(jnp.int32, part.shape, 1)
-                    zero = jnp.zeros_like(part)
-                    part = jnp.concatenate(
-                        [
-                            jnp.where(lane < HEAD_DIM, part, zero),
-                            jnp.where(lane < HEAD_DIM, zero, part),
-                        ],
-                        axis=0,
-                    )
-                    weights = jnp.concatenate([weights, mix_v[half, g, h + 1]], axis=1)
-                out[g * seq : (g + 1) * seq, h * HEAD_DIM : (h + n) * HEAD_DIM] = dot(
-                    weights, part
-                ).astype(BF16)
-
-
-def grad_out_kernel(n_unread, idx, cot_o, cot_s, mixed_o, mixed_s, *rest):
-    token, *rest = rest[n_unread:]
-    outs, (cot_v, left_v, grad_v, sems) = rest[:-4], rest[-4:]
-    token[...] = jnp.zeros_like(token)
+        mix_values(value, mix_v.at[half], out)
+
+
+def grad_out_kernel(idx, cot_o, cot_s, mixed_o, mixed_s, w_out, unread, *rest):
+    del unread
+    *outs, cot_v, left_v, grad_v, sems, last_sems = rest
+    part = last = None
+    if w_out is not None:
+        part, last, *outs = outs
     tokens, _ = cot_o.shape
     copies = begin(
         [(cot_o, cot_v.at[pl.ds(0, tokens)]), (cot_s, cot_v.at[pl.ds(tokens, tokens)])], sems
     )
+    if w_out is not None:
+        depth = last.shape[2]
+        columns = pl.ds(pl.multiple_of(idx[idx.shape[0] - 1] * depth, 128), depth)
+        later = begin(
+            [(cot_o.at[:, columns], last.at[0]), (cot_s.at[:, columns], last.at[1])], last_sems
+        )
     left_v[:, :tokens] = mixed_o[...].astype(F32).T.astype(BF16)
     left_v[:, tokens:] = mixed_s[...].astype(F32).T.astype(BF16)
     copies[0].wait()
     copies[1].wait()
     gradient_rows(left_v[...], cot_v, grad_v, 640)
     hand_out(idx, 1, grad_v, outs)
+    if w_out is not None:
+        for half in range(2):
+            part[half] = dot(cot_v[half * tokens : (half + 1) * tokens, :], w_out[...])
+        for copy in later:
+            copy.wait()
+
+
+def grad_out_only_kernel(idx, cot_o, cot_s, mixed_o, mixed_s, unread, *rest):
+    grad_out_kernel(idx, cot_o, cot_s, mixed_o, mixed_s, None, unread, *rest)
 
 
 def relay_kernel(unread, first, second, first_out, second_out):
@@ -186,18 +255,26 @@
     total[...] = own[...].astype(F32) + near[...].astype(F32) + far[...].astype(F32)
 
 
-def terms_kernel(n_node, idx, mixed_o, mixed_r, w_o, w_r, token, *outs):
-    token[...] = jnp.zeros_like(token)
+def terms_kernel(n_node, idx, mixed_o, mixed_r, w_o, w_r, *outs):
     depth = w_o.shape[0] // n_node
-    half = mixed_o.shape[0] // 2
     for j in range(n_node):
         rows = rows_at(idx[j], depth)
         term = dot(mixed_o[...], w_o[rows, :], 1, 1) + dot(mixed_r[...], w_r[rows, :], 1, 1)
+        outs[j][...] = term.astype(BF16)
+
+
+def terms_line_kernel(idx_node, idx, mixed_o, mixed_r, w_o, w_r, slot, slot_r, *outs):
+    token, along_x, along_y, kept = outs
+    token[...] = jnp.zeros_like(token)
+    core, missing = idx[0], idx[4]
+    last_o, last_r = whole(core, slot), whole(1 - core, slot_r)
+    half = mixed_o.shape[0] // 2
+    for j in range(4):
+        rows = rows_at(idx_node[j], last_o.shape[0])
+        here = idx_node[j] == missing
+        term = dot(mixed_o[...], jnp.where(here, last_o, w_o[rows, :]), 1, 1)
+        term += dot(mixed_r[...], jnp.where(here, last_r, w_r[rows, :]), 1, 1)
         term = term.astype(BF16)
-        if n_node != 4:
-            outs[j][...] = term
-            continue
-        along_x, along_y, kept = outs
         first, second = term[:half], term[half:]
         if j == 0:
             kept[0], kept[2] = first, second
@@ -231,7 +308,7 @@
 
 def make_body(n_wide, n_node):
     planes = n_wide // 2
-    line4 = planes == 4
+    line4 = planes == 4 and n_node == 4
 
     def move(x, pairs):
         return lax.ppermute(
@@ -331,47 +408,106 @@
             pltpu.VMEM((n_slots, *block), BF16),
             pltpu.SemaphoreType.DMA((n_slots,)),
         ]
-        mixed_o, mixed_s = call(
-            functools.partial(mixed_kernel, n_slots),
-            "mixed",
-            [SMEM] + [ANY] * (4 + n_slots),
-            [(tokens, cols)] * 2,
-            [rows, halves, mix_scratch, pltpu.SemaphoreType.DMA((4,)), *slots_scratch],
-            flops,
-            2 * (2 * act.size + mix.size + width * cols + 2 * tokens * cols),
-            vmem=60,
-        )(idx, act, act_s, mix, mix_s, *value_slots)
+        part_shapes = [(2, tokens, cols), (2, tokens, depth)]
+        if line4:
+            ahead = call(
+                functools.partial(part_kernel, n_slots - 1),
+                "value_ahead",
+                [SMEM] + [ANY] * (3 + n_slots),
+                [*part_shapes, (2, groups, heads, seq, seq)],
+                [
+                    *(rows, halves, pltpu.VMEM((n_slots - 1, *block), BF16)),
+                    *(pltpu.SemaphoreType.DMA((k,)) for k in (2, 4, n_slots - 1)),
+                ],
+                flops,
+                2 * (3 * act.size + mix.size + width * cols + 4 * tokens * cols),
+                kinds=[F32, BF16, BF16],
+            )(idx, act, act_s, mix, mix_s, *value_slots[:-1])
+            mixed_o, mixed_s = call(
+                mixed_rest_kernel,
+                "mixed",
+                [SMEM] + [VMEM] * 4,
+                [(tokens, cols)] * 2,
+                [],
+                flops // 4,
+                2 * (2 * tokens * depth + mix.size + 6 * tokens * cols),
+            )(idx, *ahead, value_slots[-1])
+        else:
+            mixed_o, mixed_s = call(
+                functools.partial(mixed_kernel, n_slots),
+                "mixed",
+                [SMEM] + [ANY] * (4 + n_slots),
+                [(tokens, cols)] * 2,
+                [rows, halves, mix_scratch, pltpu.SemaphoreType.DMA((4,)), *slots_scratch],
+                flops,
+                2 * (2 * act.size + mix.size + width * cols + 2 * tokens * cols),
+                )(idx, act, act_s, mix, mix_s, *value_slots)
         mixed_r = sibling(mixed_s)
-        unread = [mixed_r, *(out_slots[1:3] if line4 else [])]
-        token, *out_sends = call(
-            functools.partial(grad_out_kernel, len(unread)),
-            "grad_out",
-            [SMEM] + [ANY] * 2 + [VMEM] * 2 + [ANY] * len(unread),
-            [(16, 128)] + send_shapes,
-            [both, left_tokens, rows, pltpu.SemaphoreType.DMA((2,))],
-            flops,
-            2 * (2 * cot.size + 2 * tokens * cols + width * cols),
-        )(idx, cot, cot_s, mixed_o, mixed_s, *unread)
-        out_passed = swap(out_sends[3], 1) if line4 else token
-        w_full = call(
-            assemble_kernel,
-            "assemble",
-            [SMEM] + [ANY] * (1 + n_slots),
-            [(width, cols)],
-            slots_scratch,
-            0,
-            4 * width * cols,
-        )(idx, token, *out_slots)[0]
-        w_full_s = sibling(w_full)
-        left = call(
-            d_value_kernel,
-            "d_value",
-            [SMEM] + [ANY] * 4 + [VMEM],
-            [(cols, 2 * tokens)],
-            [halves, mix_scratch, pltpu.SemaphoreType.DMA((4,))],
-            flops,
-            2 * (2 * cot.size + mix.size + width * cols + 2 * tokens * cols),
-        )(idx, cot, cot_s, mix, mix_s, w_full)[0]
+        grad_scratch = [both, left_tokens, rows] + [pltpu.SemaphoreType.DMA((2,))] * 2
+        size = 2 * (3 * cot.size + 6 * tokens * cols + 2 * width * cols)
+        if line4:
+            w_part = call(
+                functools.partial(assemble_kernel, n_slots - 1),
+                "assemble",
+                [SMEM] + [ANY] * n_slots,
+                [(width, cols)],
+                [pltpu.VMEM((n_slots - 1, *block), BF16), pltpu.SemaphoreType.DMA((n_slots - 1,))],
+                0,
+                4 * width * cols,
+            )(idx, mixed_s, *out_slots[:-1])[0]
+            w_part_s = sibling(w_part)
+            *rest, w_mix = ahead
+            part, last, *out_sends = call(
+                grad_out_kernel,
+                "grad_out",
+                [SMEM] + [ANY] * 2 + [VMEM] * 3 + [ANY],
+                part_shapes + send_shapes,
+                grad_scratch,
+                2 * flops,
+                size,
+                kinds=[F32] + [BF16] * (1 + n_slots),
+            )(idx, cot, cot_s, mixed_o, mixed_s, w_part, mixed_r)
+            out_passed = swap(out_sends[3], 1)
+            left, last_block = call(
+                d_value_rest_kernel,
+                "d_value",
+                [SMEM] + [VMEM] * 4,
+                [(cols, 2 * tokens), block],
+                [],
+                flops // 4,
+                2 * (2 * tokens * depth + mix.size + 6 * tokens * cols),
+            )(idx, part, last, w_mix, out_slots[-1])
+            last_s = sibling(last_block)
+        else:
+            out_sends = call(
+                grad_out_only_kernel,
+                "grad_out",
+                [SMEM] + [ANY] * 2 + [VMEM] * 2 + [ANY],
+                send_shapes,
+                grad_scratch,
+                flops,
+                size,
+            )(idx, cot, cot_s, mixed_o, mixed_s, mixed_r)
+            w_full = call(
+                functools.partial(assemble_kernel, n_slots),
+                "assemble",
+                [SMEM] + [ANY] * (1 + n_slots),
+                [(width, cols)],
+                slots_scratch,
+                0,
+                4 * width * cols,
+            )(idx, mixed_s, *out_slots)[0]
+            left = call(
+                d_value_kernel,
+                "d_value",
+                [SMEM] + [ANY] * 4 + [VMEM],
+                [(cols, 2 * tokens)],
+                [halves, mix_scratch, pltpu.SemaphoreType.DMA((4,))],
+                flops,
+                2 * (2 * cot.size + mix.size + width * cols + 2 * tokens * cols),
+            )(idx, cot, cot_s, mix, mix_s, w_full)[0]
+            w_full_s = sibling(w_full)
+            token = left
         if line4:
             out_onward = added(out_sends[2], out_passed)
             out_far = swap(out_onward, 2)
@@ -380,19 +516,27 @@
             out_onward = token
         part = width // n_node
         half = tokens // 2
-        if n_node == 4:
-            term_shapes = [(2, half, part), (2, half, part), (4, half, part)]
-        else:
-            term_shapes = [(tokens, part)] * n_node
-        token, *terms = call(
-            functools.partial(terms_kernel, n_node),
-            "terms",
-            [SMEM] + [VMEM] * 4,
-            [(16, 128)] + term_shapes,
-            [],
-            flops,
-            2 * (2 * tokens * cols + 2 * width * cols + tokens * width),
-        )(idx_node, mixed_o, mixed_r, w_full, w_full_s)
+        size = 2 * (2 * tokens * cols + 2 * width * cols + tokens * width)
+        if line4:
+            token, *terms = call(
+                terms_line_kernel,
+                "terms",
+                [SMEM] * 2 + [VMEM] * 6,
+                [(16, 128), (2, half, part), (2, half, part), (4, half, part)],
+                [],
+                flops,
+                size,
+            )(idx_node, idx, mixed_o, mixed_r, w_part, w_part_s, last_block, last_s)
+        else:
+            terms = call(
+                functools.partial(terms_kernel, n_node),
+                "terms",
+                [SMEM] + [VMEM] * 4,
+                [(tokens, part)] * n_node,
+                [],
+                flops,
+                size,
+            )(idx_node, mixed_o, mixed_r, w_full, w_full_s)
 
         back_sends = call(
             gradient_kernel,
@@ -415,7 +559,7 @@
             grad_value = scatter_ring(back_sends, c)
             grad_out = scatter_ring(out_sends, c)
 
-        if n_node == 4:
+        if line4:
             along_x, along_y, kept = terms
             kept = kept.astype(F32)
             got_x = flip(along_x, 1).astype(F32)

time: 119 us -> 123 us (1.034)
  local copies, waits for them, and re-layouts: 5.25 us -> 11.5 us
  waiting for transfers between devices: 51 us -> 47.6 us
  starting transfers between devices: 26 us -> 27.7 us
  Pallas kernels: 31.1 us -> 29.7 us
    unnamed x24 -> x30, local copies, waits for them, and re-layouts: 3.16 us -> 10 us
    ppermute x12, waiting for transfers between devices: 49.7 us -> 46.1 us  [move(): lax.ppermute(x, 'wide', [(2 * s + c, 2 * d + c) for s, d in pairs for c i...]
    pallas_call x5 -> x6, Pallas kernels: 25.6 us -> 24 us  [the longest x1 7.3 us: body(): call(grad_out_kernel, 'grad_out', [SMEM] + [ANY] * 2 + [VMEM] * 3 + [ANY]...]
  transfers between devices with their start and end apart: 24 -> 25, of which waited for: 10 -> 11; matrix products, arithmetic and copies ran while one was open for 3% -> 3% of each run, Pallas kernels for 24% -> 24%
where the time goes in v13:
time: 123 us; the launch traced here: 122 us
  waiting for transfers between devices  47.6 us (39%)
  Pallas kernels  29.7 us (24%)
  starting transfers between devices  27.7 us (23%)
  local copies, waits for them, and re-layouts  11.5 us (9%)
  other arithmetic  5.02 us (4%)
    ppermute x12, waiting for transfers between devices, move(): lax.ppermute(x, 'wide', [(2 * s + c, 2 * d + c) for s, d in pairs for c i...  46.1 us
    ppermute x12, starting transfers between devices, move(): lax.ppermute(x, 'wide', [(2 * s + c, 2 * d + c) for s, d in pairs for c i...  20.9 us
    unnamed x30, local copies, waits for them, and re-layouts  10 us
    pallas_call x1, Pallas kernels, body(): call(grad_out_kernel, 'grad_out', [SMEM] + [ANY] * 2 + [VMEM] * 3 + [ANY]...  7.3 us
    pallas_call x1, Pallas kernels, body(): call(functools.partial(part_kernel, n_slots - 1), 'value_ahead', [SMEM] +...  4.9 us
    pallas_call x1, Pallas kernels, body(): call(gradient_kernel, 'grad_value', [SMEM] + [ANY] * 4 + [VMEM], send_sha...  4.63 us
    ppermute x4, starting transfers between devices, flip(): return lax.ppermute(x, 'node', [(i, i ^ j) for i in range(n_node)])  4.53 us
    pallas_call x1, Pallas kernels, body(): call(terms_line_kernel, 'terms', [SMEM] * 2 + [VMEM] * 6, [(16, 128), (2,...  3.6 us
  transfers between devices with their start and end apart: 25, of which 11 were waited for; matrix products, arithmetic and copies ran while one was open for 3% of the time, Pallas kernels for 24%

profile of v13, /device:TPU:0, one launch (start us, length us, event | category | flops | bytes accessed | tf_op | source)
XLA Modules:
  0.0 122.5 jit_solution(5287752378363607859)
XLA Ops:
  0.7 1.3 %slice_bitcast_fusion.5 = (bf16[1,320,256]{2,1,0:T(8,128)(2,1)S(1)}, bf16[1,320,256]{2,1,0:T(8,128)(2,1)S(1)}, bf16[1,320,256]{2,1,0:T(8,128)(2,1)S(1)}, bf16[1,320,256]{2,1,0:T(8,128)(2,1)S(1)}) fusion(bf16[320,512]{1,0:T(8,128)(2,1)} %param.8, bf16[320,512]{1,0:T(8,128)(2,1)} %param.9), kind=kLoop, calls=%fused_computation.34 | loop fusion | bytes 1310720 | tf_op jit(solution)/shard_map/stack | solution.py:330
  2.1 0.5 collective-permute-start
  2.6 1.3 %collective-permute-done = bf16[2,320,256]{2,1,0:T(8,128)(2,1)S(1)} collective-permute-done((bf16[2,320,256]{2,1,0:T(8,128)(2,1)S(1)}, bf16[2,320,256]{2,1,0:T(8,128)(2,1)S(1)}, u32[]{:S(2)}, u32[]{:S(2)}) %collective-permute-start) | collective-permute-done | bytes 327712 | tf_op jit(solution)/shard_map/ppermute | solution.py:322
  3.8 0.4 collective-permute-start.1
  4.2 0.1 collective-permute-start.10
  4.4 0.4 collective-permute-start.2
  4.8 2.8 %collective-permute-start.3 = (bf16[2,320,256]{2,1,0:T(8,128)(2,1)S(1)}, bf16[2,320,256]{2,1,0:T(8,128)(2,1)S(1)}, u32[]{:S(2)}, u32[]{:S(2)}) collective-permute-start(bf16[2,320,256]{2,1,0:T(8,128)(2,1)S(1)} %pad_maximum_fusion.5.rest_0_), channel_id=1, source_target_pairs={{0,8},{4,12},{8,0},{12,4},{16,24},{20,28},{24,16},{28,20},{1,9},{5... | collective-permute-start | bytes 983048 | tf_op jit(solution)/shard_map/ppermute | solution.py:314
  7.6 2.6 %collective-permute-start.4 = (bf16[2,320,256]{2,1,0:T(8,128)(2,1)S(1)}, bf16[2,320,256]{2,1,0:T(8,128)(2,1)S(1)}, u32[]{:S(2)}, u32[]{:S(2)}) collective-permute-start(bf16[2,320,256]{2,1,0:T(8,128)(2,1)S(1)} %pad_maximum_fusion.5.rest_0_), channel_id=1, source_target_pairs={{0,16},{4,20},{8,24},{12,28},{16,0},{20,4},{24,8},{28,12},{1,17},{... | collective-permute-start | bytes 983048 | tf_op jit(solution)/shard_map/ppermute | solution.py:314
  10.2 12.5 %collective-permute-done.3.unread.rest_1_ = bf16[2,320,256]{2,1,0:T(8,128)(2,1)S(1)} collective-permute-done((bf16[2,320,256]{2,1,0:T(8,128)(2,1)S(1)}, bf16[2,320,256]{2,1,0:T(8,128)(2,1)S(1)}, u32[]{:S(2)}, u32[]{:S(2)}) %collective-permute-start.3) | collective-permute-done | bytes 327712 | tf_op jit(solution)/shard_map/ppermute | solution.py:314
  22.8 2.5 %collective-permute-done.4.first = bf16[2,320,256]{2,1,0:T(8,128)(2,1)S(1)} collective-permute-done((bf16[2,320,256]{2,1,0:T(8,128)(2,1)S(1)}, bf16[2,320,256]{2,1,0:T(8,128)(2,1)S(1)}, u32[]{:S(2)}, u32[]{:S(2)}) %collective-permute-start.4) | collective-permute-done | bytes 327712 | tf_op jit(solution)/shard_map/ppermute | solution.py:314
  25.3 0.9 relay.1
  26.2 0.4 collective-permute-start.5
  26.6 1.6 %collective-permute-start.7 = (bf16[2,320,256]{2,1,0:T(8,128)(2,1)}, bf16[2,320,256]{2,1,0:T(8,128)(2,1)}, u32[]{:S(2)}, u32[]{:S(2)}) collective-permute-start(bf16[2,320,256]{2,1,0:T(8,128)(2,1)} %get-tuple-element.42.rest_0_), channel_id=1, source_target_pairs={{0,8},{4,12},{8,0},{12,4},{16,24},{20,28},{24,16},{28,20},{1,9},{5... | collective-permute-start | bytes 983048 | tf_op jit(solution)/shard_map/ppermute | solution.py:314
  28.2 1.0 copy-done.8
  29.2 1.0 collective-permute-start.8
  30.2 0.1 stack.67.idx
  30.3 1.2 copy-done.7
  31.5 1.2 copy-done.9
  32.8 4.9 %value_ahead.1 = (f32[2,512,256]{2,1,0:T(8,128)S(1)}, bf16[2,512,640]{2,1,0:T(8,128)(2,1)S(1)}, bf16[2,4,4,128,128]{4,3,2,1,0:T(8,128)(2,1)S(1)}) custom-call(s32[5]{0:T(128)S(1)} %stack.67.idx, bf16[512,2560]{1,0:T(8,128)(2,1)S(1)} %bitcast.51, bf16[512,2560]{1,0:T(8,128)(2,1)} %collective-permute-done.1.x_s.right_s, bf16[4,8,128,128]{3,2,1,0:T(8,128)(2,1)S(1)} %bitcast.54, ...), custom_call_target="tpu_custom_call" | custom-call | flops 1342177280 | bytes 11272192 | tf_op jit(solution)/shard_map/value_ahead/pallas_call | solution.py:413
  37.7 6.5 %collective-permute-done.5.slot = bf16[2,320,256]{2,1,0:T(8,128)(2,1)} collective-permute-done((bf16[2,320,256]{2,1,0:T(8,128)(2,1)}, bf16[2,320,256]{2,1,0:T(8,128)(2,1)}, u32[]{:S(2)}, u32[]{:S(2)}) %collective-permute-start.5) | collective-permute-done | bytes 327712 | tf_op jit(solution)/shard_map/ppermute | solution.py:314
  44.1 2.7 %mixed.1 = (bf16[512,256]{1,0:T(8,128)(2,1)S(1)}, bf16[512,256]{1,0:T(8,128)(2,1)S(1)}) custom-call(s32[5]{0:T(128)S(1)} %stack.67.idx, f32[2,512,256]{2,1,0:T(8,128)S(1)} %get-tuple-element.37.part, bf16[2,512,640]{2,1,0:T(8,128)(2,1)S(1)} %get-tuple-element.38.last, bf16[2,4,4,128,128]{4,3,2,1,0:T(8,128)(2,1)S(1)} %get-tuple-element.39.weights, ...), custom_call_target="tpu_custom_call" | custom-call | flops 335544320 | bytes 3932160 | tf_op jit(solution)/shard_map/mixed/pallas_call | solution.py:426
  46.8 1.5 %collective-permute-done.7.rest_1_ = bf16[2,320,256]{2,1,0:T(8,128)(2,1)} collective-permute-done((bf16[2,320,256]{2,1,0:T(8,128)(2,1)}, bf16[2,320,256]{2,1,0:T(8,128)(2,1)}, u32[]{:S(2)}, u32[]{:S(2)}) %collective-permute-start.7) | collective-permute-done | bytes 327712 | tf_op jit(solution)/shard_map/ppermute | solution.py:314
  48.3 2.9 %assemble.1.w_out.w_o = bf16[2560,256]{1,0:T(8,128)(2,1)} custom-call(s32[5]{0:T(128)S(1)} %stack.67.idx, bf16[512,256]{1,0:T(8,128)(2,1)S(1)} %get-tuple-element.41.unread.mixed_s, bf16[2,320,256]{2,1,0:T(8,128)(2,1)} %get-tuple-element.42.rest_0_, bf16[2,320,256]{2,1,0:T(8,128)(2,1)} %collective-permute-done.7.rest_1_, ...), custom_call_target="tpu_custom_call" | custom-call | bytes 2621440 | tf_op jit(solution)/shard_map/assemble/pallas_call | solution.py:449
  51.2 0.1 collective-permute-start.9
  51.3 0.5 collective-permute-start.6
  51.8 2.3 %collective-permute-start.11 = (bf16[2,320,256]{2,1,0:T(8,128)(2,1)}, bf16[2,320,256]{2,1,0:T(8,128)(2,1)}, u32[]{:S(2)}, u32[]{:S(2)}) collective-permute-start(bf16[2,320,256]{2,1,0:T(8,128)(2,1)} %collective-permute-done.8.rest_2_), channel_id=1, source_target_pairs={{0,8},{4,12},{8,0},{12,4},{16,24},{20,28},{24,16},{28,20},{1,9},{5... | collective-permute-start | bytes 983048 | tf_op jit(solution)/shard_map/ppermute | solution.py:314
  54.1 0.2 collective-permute-done.6.unread.mixed_r
  54.3 7.3 %grad_out.1 = (f32[2,512,256]{2,1,0:T(8,128)S(1)}, bf16[2,512,640]{2,1,0:T(8,128)(2,1)S(1)}, bf16[2,320,256]{2,1,0:T(8,128)(2,1)S(1)}, bf16[2,320,256]{2,1,0:T(8...) custom-call(s32[5]{0:T(128)S(1)} %stack.67.idx, bf16[512,2560]{1,0:T(8,128)(2,1)S(1)} %bitcast.56, ...), custom_call_target="tpu_custom_call" | custom-call | flops 2684354560 | bytes 12058624 | tf_op jit(solution)/shard_map/grad_out/pallas_call | solution.py:460
  61.7 1.1 copy-done.3
  62.7 1.0 copy-done.5
  63.8 0.7 copy-done.11
  64.5 2.3 %collective-permute-start.17 = (bf16[2,320,256]{2,1,0:T(8,128)(2,1)}, bf16[2,320,256]{2,1,0:T(8,128)(2,1)}, u32[]{:S(2)}, u32[]{:S(2)}) collective-permute-start(bf16[2,320,256]{2,1,0:T(8,128)(2,1)} %get-tuple-element.52), channel_id=1, source_target_pairs={{0,8},{4,12},{8,0},{12,4},{16,24},{20,28},{24,16},{28,20},{1,9},{5... | collective-permute-start | bytes 983048 | tf_op jit(solution)/shard_map/ppermute | solution.py:314
  66.8 1.2 copy-done.2
  68.0 1.3 %copy-done.4 = bf16[2,512,640]{2,1,0:T(8,128)(2,1)S(1)} copy-done((bf16[2,512,640]{2,1,0:T(8,128)(2,1)S(1)}, bf16[2,512,640]{2,1,0:T(8,128)(2,1)}, u32[]{:S(2)}) %copy-start.4) | copy-done | bytes 1310744
  69.4 1.2 copy-done.6
  70.6 2.7 %d_value.1 = (bf16[256,1024]{1,0:T(8,128)(2,1)S(1)}, bf16[2,320,256]{2,1,0:T(8,128)(2,1)S(1)}) custom-call(s32[5]{0:T(128)S(1)} %stack.67.idx, f32[2,512,256]{2,1,0:T(8,128)S(1)} %copy-done.6, bf16[2,512,640]{2,1,0:T(8,128)(2,1)S(1)} %copy-done.4, bf16[2,4,4,128,128]{4,3,2,1,0:T(8,128)(2,1)S(1)} %copy-done.2, bf16[2,320,256]{2,1,0:T(8,128)(2,1)} %collective-permute-done.11.slot), custom_call_target="tpu_custom_call" | custom-call | flops 335544320 | bytes 3932160 | tf_op jit(solution)/shard_map/d_value/pallas_call | solution.py:471
  73.3 0.1 collective-permute-start.12
  73.4 0.1 pad_add_fusion.idx_node
  73.5 0.3 collective-permute-start.19
  73.8 1.6 %collective-permute-done.17 = bf16[2,320,256]{2,1,0:T(8,128)(2,1)} collective-permute-done((bf16[2,320,256]{2,1,0:T(8,128)(2,1)}, bf16[2,320,256]{2,1,0:T(8,128)(2,1)}, u32[]{:S(2)}, u32[]{:S(2)}) %collective-permute-start.17) | collective-permute-done | bytes 327712 | tf_op jit(solution)/shard_map/ppermute | solution.py:314
  75.4 1.1 add_convert_fusion.unread
  76.4 2.1 %collective-permute-start.20 = (bf16[2,320,256]{2,1,0:T(8,128)(2,1)S(1)}, bf16[2,320,256]{2,1,0:T(8,128)(2,1)S(1)}, u32[]{:S(2)}, u32[]{:S(2)}) collective-permute-start(bf16[2,320,256]{2,1,0:T(8,128)(2,1)S(1)} %add_convert_fusion.unread), channel_id=1, source_target_pairs={{0,16},{4,20},{8,24},{12,28},{16,0},{20,4},{24,8},{28,12},{1,17},{... | collective-permute-start | bytes 983048 | tf_op jit(solution)/shard_map/ppermute | solution.py:314
  78.6 3.6 %terms.1 = (bf16[16,128]{1,0:T(8,128)(2,1)S(1)}, bf16[2,256,640]{2,1,0:T(8,128)(2,1)S(1)}, bf16[2,256,640]{2,1,0:T(8,128)(2,1)S(1)}, bf16[4,256,640]{2,1,0:T(8,128)(2,1)S(1)}) custom-call(s32[4]{0:T(128)S(1)} %pad_add_fusion.idx_node, s32[5]{0:T(128)S(1)} %stack.67.idx, bf16[512,256]{1,0:T(8,128)(2,1)S(1)} %get-tuple-element.40.mixed_o, ...), custom_call_target="tpu_custom_call" | custom-call | flops 1342177280 | bytes 5767168 | tf_op jit(solution)/shard_map/terms/pallas_call | solution.py:521
  82.2 1.6 %collective-permute-start.13 = (bf16[2,256,640]{2,1,0:T(8,128)(2,1)S(1)}, bf16[2,256,640]{2,1,0:T(8,128)(2,1)S(1)}, u32[]{:S(2)}, u32[]{:S(2)}) collective-permute-start(bf16[2,256,640]{2,1,0:T(8,128)(2,1)S(1)} %get-tuple-element.48), channel_id=1, source_target_pairs={{0,1},{1,0},{2,3},{3,2},{4,5},{5,4},{6,7},{7,6},{8,9},{9,8},{10,11... | collective-permute-start | bytes 1966088 | tf_op jit(solution)/shard_map/ppermute | solution.py:325
  83.7 1.5 %collective-permute-start.15 = (bf16[2,256,640]{2,1,0:T(8,128)(2,1)S(1)}, bf16[2,256,640]{2,1,0:T(8,128)(2,1)S(1)}, u32[]{:S(2)}, u32[]{:S(2)}) collective-permute-start(bf16[2,256,640]{2,1,0:T(8,128)(2,1)S(1)} %get-tuple-element.49), channel_id=1, source_target_pairs={{0,2},{1,3},{2,0},{3,1},{4,6},{5,7},{6,4},{7,5},{8,10},{9,11},{10,... | collective-permute-start | bytes 1966088 | tf_op jit(solution)/shard_map/ppermute | solution.py:325
  85.2 4.6 %grad_value.1 = (bf16[2,320,256]{2,1,0:T(8,128)(2,1)S(1)}, bf16[2,320,256]{2,1,0:T(8,128)(2,1)S(1)}, bf16[2,320,256]{2,1,0:T(8,128)(2,1)S(1)}, bf16[2,320,256]{2,1,0:T(8,128)(2,1)S(1)}) custom-call(s32[5]{0:T(128)S(1)} %stack.67.idx, bf16[16,128]{1,0:T(8,128)(2,1)S(1)} %get-tuple-element.50.token, bf16[2,320,256]{2,1,0:T(8,128)(2,1)S(1)} %add_convert_fusion.unread, ...), custom_call_target="tpu_custom_call" | custom-call | flops 1342177280 | bytes 7077888 | tf_op jit(solution)/shard_map/grad_value/pallas_call | solution.py:541
  89.9 1.5 %collective-permute-start.18 = (bf16[2,320,256]{2,1,0:T(8,128)(2,1)S(1)}, bf16[2,320,256]{2,1,0:T(8,128)(2,1)S(1)}, u32[]{:S(2)}, u32[]{:S(2)}) collective-permute-start(bf16[2,320,256]{2,1,0:T(8,128)(2,1)S(1)} %get-tuple-element.56), channel_id=1, source_target_pairs={{0,8},{4,12},{8,0},{12,4},{16,24},{20,28},{24,16},{28,20},{1,9},{5... | collective-permute-start | bytes 983048 | tf_op jit(solution)/shard_map/ppermute | solution.py:314
  91.4 0.2 convert_element_type.50
  91.6 2.4 %collective-permute-done.20.far = bf16[2,320,256]{2,1,0:T(8,128)(2,1)S(1)} collective-permute-done((bf16[2,320,256]{2,1,0:T(8,128)(2,1)S(1)}, bf16[2,320,256]{2,1,0:T(8,128)(2,1)S(1)}, u32[]{:S(2)}, u32[]{:S(2)}) %collective-permute-start.20) | collective-permute-done | bytes 327712 | tf_op jit(solution)/shard_map/ppermute | solution.py:314
  94.0 6.3 %collective-permute-done.18.got = bf16[2,320,256]{2,1,0:T(8,128)(2,1)S(1)} collective-permute-done((bf16[2,320,256]{2,1,0:T(8,128)(2,1)S(1)}, bf16[2,320,256]{2,1,0:T(8,128)(2,1)S(1)}, u32[]{:S(2)}, u32[]{:S(2)}) %collective-permute-start.18) | collective-permute-done | bytes 327712 | tf_op jit(solution)/shard_map/ppermute | solution.py:314
  100.3 0.2 sum.1
  100.5 3.8 %collective-permute-start.22 = (bf16[2,320,256]{2,1,0:T(8,128)(2,1)S(1)}, bf16[2,320,256]{2,1,0:T(8,128)(2,1)S(1)}, u32[]{:S(2)}, u32[]{:S(2)}) collective-permute-start(bf16[2,320,256]{2,1,0:T(8,128)(2,1)S(1)} %get-tuple-element.61), channel_id=1, source_target_pairs={{0,16},{4,20},{8,24},{12,28},{16,0},{20,4},{24,8},{28,12},{1,17},{... | collective-permute-start | bytes 983048 | tf_op jit(solution)/shard_map/ppermute | solution.py:314
  104.5 0.1 convert_element_type.51
  104.6 0.1 convert_element_type.55
  104.7 0.2 fusion.8
  104.9 0.9 collective-permute-start.14
  105.8 0.5 collective-permute-start.16
  106.3 9.9 %collective-permute-done.21 = bf16[2,320,256]{2,1,0:T(8,128)(2,1)S(1)} collective-permute-done((bf16[2,320,256]{2,1,0:T(8,128)(2,1)S(1)}, bf16[2,320,256]{2,1,0:T(8,128)(2,1)S(1)}, u32[]{:S(2)}, u32[]{:S(2)}) %collective-permute-start.21) | collective-permute-done | bytes 327712 | tf_op jit(solution)/shard_map/ppermute | solution.py:314
  116.3 2.8 %collective-permute-done.22 = bf16[2,320,256]{2,1,0:T(8,128)(2,1)S(1)} collective-permute-done((bf16[2,320,256]{2,1,0:T(8,128)(2,1)S(1)}, bf16[2,320,256]{2,1,0:T(8,128)(2,1)S(1)}, u32[]{:S(2)}, u32[]{:S(2)}) %collective-permute-start.22) | collective-permute-done | bytes 327712 | tf_op jit(solution)/shard_map/ppermute | solution.py:314
  119.1 0.1 convert_add_fusion
  119.4 0.9 pad_maximum_fusion.2
  120.3 0.3 fusion.7
  120.6 0.9 pad_maximum_fusion
  121.5 0.9 pad_maximum_fusion.1
  (47 shorter events, 0.6 us)
Async XLA Ops:
  0.6 3.2 %copy-start = (bf16[2,2,128,2560]{3,2,1,0:T(8,128)(2,1)S(1)}, bf16[2,2,128,2560]{3,2,1,0:T(8,128)(2,1)}, u32[]{:S(2)}) copy-start(bf16[2,2,128,2560]{3,2,1,0:T(8,128)(2,1)} %param.5) | copy-start | bytes 7864324
  2.1 1.8 %collective-permute-start = (bf16[2,320,256]{2,1,0:T(8,128)(2,1)S(1)}, bf16[2,320,256]{2,1,0:T(8,128)(2,1)S(1)}, u32[]{:S(2)}, u32[]{:S(2)}) collective-permute-start(bf16[2,320,256]{2,1,0:T(8,128)(2,1)S(1)} %get-tuple-element.72), channel_id=1, source_target_pairs={{0,4},{4,0},{8,12},{12,8},{16,20},{20,16},{24,28},{28,24},{1,5},{5... | collective-permute-start | bytes 983048 | tf_op jit(solution)/shard_map/ppermute | solution.py:322
  3.8 26.5 %collective-permute-start.1 = (bf16[512,2560]{1,0:T(8,128)(2,1)S(1)}, bf16[512,2560]{1,0:T(8,128)(2,1)}, u32[]{:S(2)}, u32[]{:S(2)}) collective-permute-start(bf16[512,2560]{1,0:T(8,128)(2,1)S(1)} %bitcast.50), channel_id=1, source_target_pairs={{0,4},{4,0},{8,12},{12,8},{16,20},{20,16},{24,28},{28,24},{1,5},{5... | collective-permute-start | bytes 7864328 | tf_op jit(solution)/shard_map/ppermute | solution.py:322
  4.2 49.9 %collective-permute-start.10 = (bf16[512,2560]{1,0:T(8,128)(2,1)}, bf16[512,2560]{1,0:T(8,128)(2,1)}, u32[]{:S(2)}, u32[]{:S(2)}) collective-permute-start(bf16[512,2560]{1,0:T(8,128)(2,1)} %bitcast.55), channel_id=1, source_target_pairs={{0,4},{4,0},{8,12},{12,8},{16,20},{20,16},{24,28},{28,24},{1,5},{5... | collective-permute-start | bytes 7864328 | tf_op jit(solution)/shard_map/ppermute | solution.py:322
  4.4 23.8 %collective-permute-start.2 = (bf16[4,8,128,128]{3,2,1,0:T(8,128)(2,1)}, bf16[4,8,128,128]{3,2,1,0:T(8,128)(2,1)S(1)}, u32[]{:S(2)}, u32[]{:S(2)}) collective-permute-start(bf16[4,8,128,128]{3,2,1,0:T(8,128)(2,1)} %bitcast.53), channel_id=1, source_target_pairs={{0,4},{4,0},{8,12},{12,8},{16,20},{20,16},{24,28},{28,24},{1,5},{5... | collective-permute-start | bytes 3145736 | tf_op jit(solution)/shard_map/ppermute | solution.py:322
  4.8 17.9 %collective-permute-start.3 = (bf16[2,320,256]{2,1,0:T(8,128)(2,1)S(1)}, bf16[2,320,256]{2,1,0:T(8,128)(2,1)S(1)}, u32[]{:S(2)}, u32[]{:S(2)}) collective-permute-start(bf16[2,320,256]{2,1,0:T(8,128)(2,1)S(1)} %pad_maximum_fusion.5.rest_0_), channel_id=1, source_target_pairs={{0,8},{4,12},{8,0},{12,4},{16,24},{20,28},{24,16},{28,20},{1,9},{5... | collective-permute-start | bytes 983048 | tf_op jit(solution)/shard_map/ppermute | solution.py:314
  7.6 17.7 %collective-permute-start.4 = (bf16[2,320,256]{2,1,0:T(8,128)(2,1)S(1)}, bf16[2,320,256]{2,1,0:T(8,128)(2,1)S(1)}, u32[]{:S(2)}, u32[]{:S(2)}) collective-permute-start(bf16[2,320,256]{2,1,0:T(8,128)(2,1)S(1)} %pad_maximum_fusion.5.rest_0_), channel_id=1, source_target_pairs={{0,16},{4,20},{8,24},{12,28},{16,0},{20,4},{24,8},{28,12},{1,17},{... | collective-permute-start | bytes 983048 | tf_op jit(solution)/shard_map/ppermute | solution.py:314
  26.2 18.0 %collective-permute-start.5 = (bf16[2,320,256]{2,1,0:T(8,128)(2,1)}, bf16[2,320,256]{2,1,0:T(8,128)(2,1)}, u32[]{:S(2)}, u32[]{:S(2)}) collective-permute-start(bf16[2,320,256]{2,1,0:T(8,128)(2,1)} %get-tuple-element.36.rest_2_), channel_id=1, source_target_pairs={{0,8},{4,12},{8,0},{12,4},{16,24},{20,28},{24,16},{28,20},{1,9},{5... | collective-permute-start | bytes 983048 | tf_op jit(solution)/shard_map/ppermute | solution.py:314
  26.6 21.7 %collective-permute-start.7 = (bf16[2,320,256]{2,1,0:T(8,128)(2,1)}, bf16[2,320,256]{2,1,0:T(8,128)(2,1)}, u32[]{:S(2)}, u32[]{:S(2)}) collective-permute-start(bf16[2,320,256]{2,1,0:T(8,128)(2,1)} %get-tuple-element.42.rest_0_), channel_id=1, source_target_pairs={{0,8},{4,12},{8,0},{12,4},{16,24},{20,28},{24,16},{28,20},{1,9},{5... | collective-permute-start | bytes 983048 | tf_op jit(solution)/shard_map/ppermute | solution.py:314
  28.2 1.0 copy-start.8
  29.2 19.2 %collective-permute-start.8 = (bf16[2,320,256]{2,1,0:T(8,128)(2,1)}, bf16[2,320,256]{2,1,0:T(8,128)(2,1)}, u32[]{:S(2)}, u32[]{:S(2)}) collective-permute-start(bf16[2,320,256]{2,1,0:T(8,128)(2,1)} %get-tuple-element.42.rest_0_), channel_id=1, source_target_pairs={{0,16},{4,20},{8,24},{12,28},{16,0},{20,4},{24,8},{28,12},{1,17},{... | collective-permute-start | bytes 983048 | tf_op jit(solution)/shard_map/ppermute | solution.py:314
  30.3 1.2 %copy-start.7 = (bf16[2,2,8,128,128]{4,3,2,1,0:T(8,128)(2,1)S(1)}, bf16[2,2,8,128,128]{4,3,2,1,0:T(8,128)(2,1)}, u32[]{:S(2)}) copy-start(bf16[2,2,8,128,128]{4,3,2,1,0:T(8,128)(2,1)} %param.6) | copy-start | bytes 3145732
  31.5 1.2 %copy-start.9 = (bf16[4,8,128,128]{3,2,1,0:T(8,128)(2,1)S(1)}, bf16[4,8,128,128]{3,2,1,0:T(8,128)(2,1)}, u32[]{:S(2)}) copy-start(bf16[4,8,128,128]{3,2,1,0:T(8,128)(2,1)} %copy-done.8) | copy-start | bytes 3145732
  37.7 9.2 %copy-start.1 = (bf16[2,4,4,128,128]{4,3,2,1,0:T(8,128)(2,1)}, bf16[2,4,4,128,128]{4,3,2,1,0:T(8,128)(2,1)S(1)}, u32[]{:S(2)}) copy-start(bf16[2,4,4,128,128]{4,3,2,1,0:T(8,128)(2,1)S(1)} %get-tuple-element.39.weights) | copy-start | bytes 3145732
  44.1 10.2 %copy-start.10 = (bf16[2,2,128,2560]{3,2,1,0:T(8,128)(2,1)S(1)}, bf16[2,2,128,2560]{3,2,1,0:T(8,128)(2,1)}, u32[]{:S(2)}) copy-start(bf16[2,2,128,2560]{3,2,1,0:T(8,128)(2,1)} %param.7) | copy-start | bytes 7864324
  51.2 27.3 %collective-permute-start.9 = (bf16[2560,256]{1,0:T(8,128)(2,1)}, bf16[2560,256]{1,0:T(8,128)(2,1)}, u32[]{:S(2)}, u32[]{:S(2)}) collective-permute-start(bf16[2560,256]{1,0:T(8,128)(2,1)} %assemble.1.w_out.w_o), channel_id=1, source_target_pairs={{0,4},{4,0},{8,12},{12,8},{16,20},{20,16},{24,28},{28,24},{1,5},{5... | collective-permute-start | bytes 3932168 | tf_op jit(solution)/shard_map/ppermute | solution.py:322
  51.3 3.0 %collective-permute-start.6 = (bf16[512,256]{1,0:T(8,128)(2,1)S(1)}, bf16[512,256]{1,0:T(8,128)(2,1)S(1)}, u32[]{:S(2)}, u32[]{:S(2)}) collective-permute-start(bf16[512,256]{1,0:T(8,128)(2,1)S(1)} %get-tuple-element.41.unread.mixed_s), channel_id=1, source_target_pairs={{0,4},{4,0},{8,12},{12,8},{16,20},{20,16},{24,28},{28,24},{1,5},{5... | collective-permute-start | bytes 786440 | tf_op jit(solution)/shard_map/ppermute | solution.py:322
  51.8 15.0 %collective-permute-start.11 = (bf16[2,320,256]{2,1,0:T(8,128)(2,1)}, bf16[2,320,256]{2,1,0:T(8,128)(2,1)}, u32[]{:S(2)}, u32[]{:S(2)}) collective-permute-start(bf16[2,320,256]{2,1,0:T(8,128)(2,1)} %collective-permute-done.8.rest_2_), channel_id=1, source_target_pairs={{0,8},{4,12},{8,0},{12,4},{16,24},{20,28},{24,16},{28,20},{1,9},{5... | collective-permute-start | bytes 983048 | tf_op jit(solution)/shard_map/ppermute | solution.py:314
  54.3 7.3 %copy-start.13 = (bf16[512,256]{1,0:T(8,128)(2,1)}, bf16[512,256]{1,0:T(8,128)(2,1)S(1)}, u32[]{:S(2)}) copy-start(bf16[512,256]{1,0:T(8,128)(2,1)S(1)} %collective-permute-done.6.unread.mixed_r) | copy-start | bytes 786436
  61.7 1.1 copy-start.3
  62.7 1.0 copy-start.5
  63.7 0.7 copy-start.11
  64.5 10.9 %collective-permute-start.17 = (bf16[2,320,256]{2,1,0:T(8,128)(2,1)}, bf16[2,320,256]{2,1,0:T(8,128)(2,1)}, u32[]{:S(2)}, u32[]{:S(2)}) collective-permute-start(bf16[2,320,256]{2,1,0:T(8,128)(2,1)} %get-tuple-element.52), channel_id=1, source_target_pairs={{0,8},{4,12},{8,0},{12,4},{16,24},{20,28},{24,16},{28,20},{1,9},{5... | collective-permute-start | bytes 983048 | tf_op jit(solution)/shard_map/ppermute | solution.py:314
  66.8 1.2 %copy-start.2 = (bf16[2,4,4,128,128]{4,3,2,1,0:T(8,128)(2,1)S(1)}, bf16[2,4,4,128,128]{4,3,2,1,0:T(8,128)(2,1)}, u32[]{:S(2)}) copy-start(bf16[2,4,4,128,128]{4,3,2,1,0:T(8,128)(2,1)} %copy-done.1) | copy-start | bytes 3145732
  68.0 1.3 %copy-start.4 = (bf16[2,512,640]{2,1,0:T(8,128)(2,1)S(1)}, bf16[2,512,640]{2,1,0:T(8,128)(2,1)}, u32[]{:S(2)}) copy-start(bf16[2,512,640]{2,1,0:T(8,128)(2,1)} %copy-done.3) | copy-start | bytes 3932164
  69.4 1.2 %copy-start.6 = (f32[2,512,256]{2,1,0:T(8,128)S(1)}, f32[2,512,256]{2,1,0:T(8,128)}, u32[]{:S(2)}) copy-start(f32[2,512,256]{2,1,0:T(8,128)} %copy-done.5) | copy-start | bytes 3145732
  70.6 2.9 %copy-start.12 = (bf16[2,320,256]{2,1,0:T(8,128)(2,1)S(1)}, bf16[2,320,256]{2,1,0:T(8,128)(2,1)}, u32[]{:S(2)}) copy-start(bf16[2,320,256]{2,1,0:T(8,128)(2,1)} %copy-done.11) | copy-start | bytes 983044
  70.6 8.0 %copy-start.14 = (bf16[512,256]{1,0:T(8,128)(2,1)S(1)}, bf16[512,256]{1,0:T(8,128)(2,1)}, u32[]{:S(2)}) copy-start(bf16[512,256]{1,0:T(8,128)(2,1)} %copy-done.13) | copy-start | bytes 786436
  73.3 5.3 %collective-permute-start.12 = (bf16[2,320,256]{2,1,0:T(8,128)(2,1)S(1)}, bf16[2,320,256]{2,1,0:T(8,128)(2,1)S(1)}, u32[]{:S(2)}, u32[]{:S(2)}) collective-permute-start(bf16[2,320,256]{2,1,0:T(8,128)(2,1)S(1)} %get-tuple-element.46.slot), channel_id=1, source_target_pairs={{0,4},{4,0},{8,12},{12,8},{16,20},{20,16},{24,28},{28,24},{1,5},{5... | collective-permute-start | bytes 983048 | tf_op jit(solution)/shard_map/ppermute | solution.py:322
  73.5 18.1 %collective-permute-start.19 = (bf16[2,320,256]{2,1,0:T(8,128)(2,1)S(1)}, bf16[2,320,256]{2,1,0:T(8,128)(2,1)S(1)}, u32[]{:S(2)}, u32[]{:S(2)}) collective-permute-start(bf16[2,320,256]{2,1,0:T(8,128)(2,1)S(1)} %copy-done.12), channel_id=1, source_target_pairs={{0,8},{4,12},{8,0},{12,4},{16,24},{20,28},{24,16},{28,20},{1,9},{5... | collective-permute-start | bytes 983048 | tf_op jit(solution)/shard_map/ppermute | solution.py:314
  76.4 17.5 %collective-permute-start.20 = (bf16[2,320,256]{2,1,0:T(8,128)(2,1)S(1)}, bf16[2,320,256]{2,1,0:T(8,128)(2,1)S(1)}, u32[]{:S(2)}, u32[]{:S(2)}) collective-permute-start(bf16[2,320,256]{2,1,0:T(8,128)(2,1)S(1)} %add_convert_fusion.unread), channel_id=1, source_target_pairs={{0,16},{4,20},{8,24},{12,28},{16,0},{20,4},{24,8},{28,12},{1,17},{... | collective-permute-start | bytes 983048 | tf_op jit(solution)/shard_map/ppermute | solution.py:314
  82.2 22.3 %collective-permute-start.13 = (bf16[2,256,640]{2,1,0:T(8,128)(2,1)S(1)}, bf16[2,256,640]{2,1,0:T(8,128)(2,1)S(1)}, u32[]{:S(2)}, u32[]{:S(2)}) collective-permute-start(bf16[2,256,640]{2,1,0:T(8,128)(2,1)S(1)} %get-tuple-element.48), channel_id=1, source_target_pairs={{0,1},{1,0},{2,3},{3,2},{4,5},{5,4},{6,7},{7,6},{8,9},{9,8},{10,11... | collective-permute-start | bytes 1966088 | tf_op jit(solution)/shard_map/ppermute | solution.py:325
  83.7 20.9 %collective-permute-start.15 = (bf16[2,256,640]{2,1,0:T(8,128)(2,1)S(1)}, bf16[2,256,640]{2,1,0:T(8,128)(2,1)S(1)}, u32[]{:S(2)}, u32[]{:S(2)}) collective-permute-start(bf16[2,256,640]{2,1,0:T(8,128)(2,1)S(1)} %get-tuple-element.49), channel_id=1, source_target_pairs={{0,2},{1,3},{2,0},{3,1},{4,6},{5,7},{6,4},{7,5},{8,10},{9,11},{10,... | collective-permute-start | bytes 1966088 | tf_op jit(solution)/shard_map/ppermute | solution.py:325
  89.9 10.4 %collective-permute-start.18 = (bf16[2,320,256]{2,1,0:T(8,128)(2,1)S(1)}, bf16[2,320,256]{2,1,0:T(8,128)(2,1)S(1)}, u32[]{:S(2)}, u32[]{:S(2)}) collective-permute-start(bf16[2,320,256]{2,1,0:T(8,128)(2,1)S(1)} %get-tuple-element.56), channel_id=1, source_target_pairs={{0,8},{4,12},{8,0},{12,4},{16,24},{20,28},{24,16},{28,20},{1,9},{5... | collective-permute-start | bytes 983048 | tf_op jit(solution)/shard_map/ppermute | solution.py:314
  100.5 15.8 %collective-permute-start.21 = (bf16[2,320,256]{2,1,0:T(8,128)(2,1)S(1)}, bf16[2,320,256]{2,1,0:T(8,128)(2,1)S(1)}, u32[]{:S(2)}, u32[]{:S(2)}) collective-permute-start(bf16[2,320,256]{2,1,0:T(8,128)(2,1)S(1)} %get-tuple-element.60), channel_id=1, source_target_pairs={{0,8},{4,12},{8,0},{12,4},{16,24},{20,28},{24,16},{28,20},{1,9},{5... | collective-permute-start | bytes 983048 | tf_op jit(solution)/shard_map/ppermute | solution.py:314
  100.5 18.5 %collective-permute-start.22 = (bf16[2,320,256]{2,1,0:T(8,128)(2,1)S(1)}, bf16[2,320,256]{2,1,0:T(8,128)(2,1)S(1)}, u32[]{:S(2)}, u32[]{:S(2)}) collective-permute-start(bf16[2,320,256]{2,1,0:T(8,128)(2,1)S(1)} %get-tuple-element.61), channel_id=1, source_target_pairs={{0,16},{4,20},{8,24},{12,28},{16,0},{20,4},{24,8},{28,12},{1,17},{... | collective-permute-start | bytes 983048 | tf_op jit(solution)/shard_map/ppermute | solution.py:314
  104.4 14.9 %collective-permute-start.24 = (f32[320,256]{1,0:T(8,128)S(1)}, f32[320,256]{1,0:T(8,128)S(1)}, u32[]{:S(2)}, u32[]{:S(2)}) collective-permute-start(f32[320,256]{1,0:T(8,128)S(1)} %slice_bitcast_fusion.2), channel_id=1, source_target_pairs={{0,4},{4,0},{8,12},{12,8},{16,20},{20,16},{24,28},{28,24},{1,5},{5... | collective-permute-start | bytes 983048 | tf_op jit(solution)/shard_map/ppermute | solution.py:322
  104.9 15.4 %collective-permute-start.14 = (bf16[256,640]{1,0:T(8,128)(2,1)S(1)}, bf16[256,640]{1,0:T(8,128)(2,1)S(1)}, u32[]{:S(2)}, u32[]{:S(2)}) collective-permute-start(bf16[256,640]{1,0:T(8,128)(2,1)S(1)} %get-tuple-element.65), channel_id=1, source_target_pairs={{0,2},{1,3},{2,0},{3,1},{4,6},{5,7},{6,4},{7,5},{8,10},{9,11},{10,... | collective-permute-start | bytes 983048 | tf_op jit(solution)/shard_map/ppermute | solution.py:325
  105.8 14.5 %collective-permute-start.16 = (bf16[256,640]{1,0:T(8,128)(2,1)S(1)}, bf16[256,640]{1,0:T(8,128)(2,1)S(1)}, u32[]{:S(2)}, u32[]{:S(2)}) collective-permute-start(bf16[256,640]{1,0:T(8,128)(2,1)S(1)} %get-tuple-element.66), channel_id=1, source_target_pairs={{0,1},{1,0},{2,3},{3,2},{4,5},{5,4},{6,7},{7,6},{8,9},{9,8},{10,11... | collective-permute-start | bytes 983048 | tf_op jit(solution)/shard_map/ppermute | solution.py:325
  119.2 2.2 %collective-permute-start.23 = (f32[320,256]{1,0:T(8,128)S(1)}, f32[320,256]{1,0:T(8,128)S(1)}, u32[]{:S(2)}, u32[]{:S(2)}) collective-permute-start(f32[320,256]{1,0:T(8,128)S(1)} %slice_bitcast_fusion), channel_id=1, source_target_pairs={{0,4},{4,0},{8,12},{12,8},{16,20},{20,16},{24,28},{28,24},{1,5},{5... | collective-permute-start | bytes 983048 | tf_op jit(solution)/shard_map/ppermute | solution.py:322

commit v14 on v13

--- a/solution.py
+++ b/solution.py
@@ -291,7 +291,7 @@
 VMEM = pl.BlockSpec(memory_space=pltpu.VMEM)
 
 
-def call(kernel, name, in_specs, out_shapes, scratch, flops, size=1 << 20, kinds=None, vmem=40):
+def call(kernel, name, in_specs, out_shapes, scratch, flops, size=1 << 20, kinds=None, vmem=24):
     return pl.pallas_call(
         kernel,
         name=name,
@@ -384,7 +384,7 @@
         block = u_out.shape
         if line4:
             far, near = swap(u_value, 2), swap(u_value, 1)
-            far, u_out = call(relay_kernel, "relay", [ANY, VMEM, VMEM], [block] * 2, [], 0)(
+            far, u_out = call(relay_kernel, "relay", [ANY, VMEM, VMEM], [block] * 2, [], 0, vmem=8)(
                 near, far, u_out
             )
             value_slots = [u_value, near, far, swap(far, 1)]
@@ -431,6 +431,7 @@
                 [],
                 flops // 4,
                 2 * (2 * tokens * depth + mix.size + 6 * tokens * cols),
+                vmem=16,
             )(idx, *ahead, value_slots[-1])
         else:
             mixed_o, mixed_s = call(
@@ -454,7 +455,7 @@
                 [pltpu.VMEM((n_slots - 1, *block), BF16), pltpu.SemaphoreType.DMA((n_slots - 1,))],
                 0,
                 4 * width * cols,
-            )(idx, mixed_s, *out_slots[:-1])[0]
+            )(idx, mixed_r, *out_slots[:-1])[0]
             w_part_s = sibling(w_part)
             *rest, w_mix = ahead
             part, last, *out_sends = call(
@@ -476,6 +477,7 @@
                 [],
                 flops // 4,
                 2 * (2 * tokens * depth + mix.size + 6 * tokens * cols),
+                vmem=16,
             )(idx, part, last, w_mix, out_slots[-1])
             last_s = sibling(last_block)
         else:
@@ -550,7 +552,7 @@
         if line4:
             back_passed = swap(back_sends[3], 1)
             onward, beside, out_total = call(
-                sum_kernel, "sum", [VMEM] * 6, [block] * 3, [], 0, kinds=[BF16, BF16, F32]
+                sum_kernel, "sum", [VMEM] * 6, [block] * 3, [], 0, kinds=[BF16, BF16, F32], vmem=8
             )(back_sends[2], back_passed, back_sends[1], out_sends[0], out_near, out_far)
             back_far, back_near = swap(onward, 2), swap(beside, 1)
             grad_out = join(out_total[0], sibling(out_total[1]), c)

time: 123 us -> 121 us (0.984)
  starting transfers between devices: 27.7 us -> 23.1 us
  waiting for transfers between devices: 47.6 us -> 51.6 us
  local copies, waits for them, and re-layouts: 11.5 us -> 10.1 us
    ppermute x12, waiting for transfers between devices: 46.1 us -> 50.3 us  [move(): lax.ppermute(x, 'wide', [(2 * s + c, 2 * d + c) for s, d in pairs for c i...]
    ppermute x12, starting transfers between devices: 20.9 us -> 16.9 us  [move(): lax.ppermute(x, 'wide', [(2 * s + c, 2 * d + c) for s, d in pairs for c i...]
    unnamed x30, local copies, waits for them, and re-layouts: 10 us -> 8.55 us
  transfers between devices with their start and end apart: 25 -> 25, of which waited for: 11 -> 11; matrix products, arithmetic and copies ran while one was open for 3% -> 3% of each run, Pallas kernels for 24% -> 25%
where the time goes in v14:
time: 121 us; the launch traced here: 120 us
  waiting for transfers between devices  51.6 us (43%)
  Pallas kernels  29.5 us (24%)
  starting transfers between devices  23.1 us (19%)
  local copies, waits for them, and re-layouts  10.1 us (8%)
  other arithmetic  4.87 us (4%)
    ppermute x12, waiting for transfers between devices, move(): lax.ppermute(x, 'wide', [(2 * s + c, 2 * d + c) for s, d in pairs for c i...  50.3 us
    ppermute x12, starting transfers between devices, move(): lax.ppermute(x, 'wide', [(2 * s + c, 2 * d + c) for s, d in pairs for c i...  16.9 us
    unnamed x30, local copies, waits for them, and re-layouts  8.55 us
    pallas_call x1, Pallas kernels, body(): call(grad_out_kernel, 'grad_out', [SMEM] + [ANY] * 2 + [VMEM] * 3 + [ANY]...  7.2 us
    pallas_call x1, Pallas kernels, body(): call(functools.partial(part_kernel, n_slots - 1), 'value_ahead', [SMEM] +...  4.9 us
    pallas_call x1, Pallas kernels, body(): call(gradient_kernel, 'grad_value', [SMEM] + [ANY] * 4 + [VMEM], send_sha...  4.62 us
    ppermute x4, starting transfers between devices, flip(): return lax.ppermute(x, 'node', [(i, i ^ j) for i in range(n_node)])  4.18 us
    pallas_call x1, Pallas kernels, body(): call(terms_line_kernel, 'terms', [SMEM] * 2 + [VMEM] * 6, [(16, 128), (2,...  3.58 us
  transfers between devices with their start and end apart: 25, of which 11 were waited for; matrix products, arithmetic and copies ran while one was open for 3% of the time, Pallas kernels for 25%

profile of v14, /device:TPU:0, one launch (start us, length us, event | category | flops | bytes accessed | tf_op | source)
XLA Modules:
  0.0 120.0 jit_solution(6083342945776352065)
XLA Ops:
  0.7 1.3 %slice_bitcast_fusion.5 = (bf16[1,320,256]{2,1,0:T(8,128)(2,1)S(1)}, bf16[1,320,256]{2,1,0:T(8,128)(2,1)S(1)}, bf16[1,320,256]{2,1,0:T(8,128)(2,1)S(1)}, bf16[1,320,256]{2,1,0:T(8,128)(2,1)S(1)}) fusion(bf16[320,512]{1,0:T(8,128)(2,1)} %param.8, bf16[320,512]{1,0:T(8,128)(2,1)} %param.9), kind=kLoop, calls=%fused_computation.34 | loop fusion | bytes 1310720 | tf_op jit(solution)/shard_map/stack | solution.py:330
  2.1 0.5 collective-permute-start
  2.6 1.3 %collective-permute-done = bf16[2,320,256]{2,1,0:T(8,128)(2,1)S(1)} collective-permute-done((bf16[2,320,256]{2,1,0:T(8,128)(2,1)S(1)}, bf16[2,320,256]{2,1,0:T(8,128)(2,1)S(1)}, u32[]{:S(2)}, u32[]{:S(2)}) %collective-permute-start) | collective-permute-done | bytes 327712 | tf_op jit(solution)/shard_map/ppermute | solution.py:322
  3.8 0.4 collective-permute-start.1
  4.2 0.1 collective-permute-start.10
  4.4 0.4 collective-permute-start.2
  4.8 2.8 %collective-permute-start.3 = (bf16[2,320,256]{2,1,0:T(8,128)(2,1)S(1)}, bf16[2,320,256]{2,1,0:T(8,128)(2,1)S(1)}, u32[]{:S(2)}, u32[]{:S(2)}) collective-permute-start(bf16[2,320,256]{2,1,0:T(8,128)(2,1)S(1)} %pad_maximum_fusion.5.rest_0_), channel_id=1, source_target_pairs={{0,8},{4,12},{8,0},{12,4},{16,24},{20,28},{24,16},{28,20},{1,9},{5... | collective-permute-start | bytes 983048 | tf_op jit(solution)/shard_map/ppermute | solution.py:314
  7.6 2.6 %collective-permute-start.4 = (bf16[2,320,256]{2,1,0:T(8,128)(2,1)S(1)}, bf16[2,320,256]{2,1,0:T(8,128)(2,1)S(1)}, u32[]{:S(2)}, u32[]{:S(2)}) collective-permute-start(bf16[2,320,256]{2,1,0:T(8,128)(2,1)S(1)} %pad_maximum_fusion.5.rest_0_), channel_id=1, source_target_pairs={{0,16},{4,20},{8,24},{12,28},{16,0},{20,4},{24,8},{28,12},{1,17},{... | collective-permute-start | bytes 983048 | tf_op jit(solution)/shard_map/ppermute | solution.py:314
  10.2 12.5 %collective-permute-done.3.unread.rest_1_ = bf16[2,320,256]{2,1,0:T(8,128)(2,1)S(1)} collective-permute-done((bf16[2,320,256]{2,1,0:T(8,128)(2,1)S(1)}, bf16[2,320,256]{2,1,0:T(8,128)(2,1)S(1)}, u32[]{:S(2)}, u32[]{:S(2)}) %collective-permute-start.3) | collective-permute-done | bytes 327712 | tf_op jit(solution)/shard_map/ppermute | solution.py:314
  22.8 2.5 %collective-permute-done.4.first = bf16[2,320,256]{2,1,0:T(8,128)(2,1)S(1)} collective-permute-done((bf16[2,320,256]{2,1,0:T(8,128)(2,1)S(1)}, bf16[2,320,256]{2,1,0:T(8,128)(2,1)S(1)}, u32[]{:S(2)}, u32[]{:S(2)}) %collective-permute-start.4) | collective-permute-done | bytes 327712 | tf_op jit(solution)/shard_map/ppermute | solution.py:314
  25.3 0.8 relay.1
  26.1 0.7 copy-done.8
  26.8 0.4 collective-permute-start.5
  27.2 0.1 stack.67.idx
  27.3 1.6 %collective-permute-start.7 = (bf16[2,320,256]{2,1,0:T(8,128)(2,1)}, bf16[2,320,256]{2,1,0:T(8,128)(2,1)S(1)}, u32[]{:S(2)}, u32[]{:S(2)}) collective-permute-start(bf16[2,320,256]{2,1,0:T(8,128)(2,1)} %copy-done.8), channel_id=1, source_target_pairs={{0,8},{4,12},{8,0},{12,4},{16,24},{20,28},{24,16},{28,20},{1,9},{5... | collective-permute-start | bytes 983048 | tf_op jit(solution)/shard_map/ppermute | solution.py:314
  28.9 1.1 collective-permute-start.8
  30.0 1.2 %copy-done.7 = bf16[2,2,8,128,128]{4,3,2,1,0:T(8,128)(2,1)S(1)} copy-done((bf16[2,2,8,128,128]{4,3,2,1,0:T(8,128)(2,1)S(1)}, bf16[2,2,8,128,128]{4,3,2,1,0:T(8,128)(2,1)}, u32[]{:S(2)}) %copy-start.7) | copy-done | bytes 1048600
  31.2 4.9 %value_ahead.1 = (f32[2,512,256]{2,1,0:T(8,128)S(1)}, bf16[2,512,640]{2,1,0:T(8,128)(2,1)S(1)}, bf16[2,4,4,128,128]{4,3,2,1,0:T(8,128)(2,1)S(1)}) custom-call(s32[5]{0:T(128)S(1)} %stack.67.idx, bf16[512,2560]{1,0:T(8,128)(2,1)S(1)} %bitcast.51, bf16[512,2560]{1,0:T(8,128)(2,1)} %collective-permute-done.1.x_s.right_s, bf16[4,8,128,128]{3,2,1,0:T(8,128)(2,1)S(1)} %bitcast.54, ...), custom_call_target="tpu_custom_call" | custom-call | flops 1342177280 | bytes 11272192 | tf_op jit(solution)/shard_map/value_ahead/pallas_call | solution.py:413
  36.1 8.5 %collective-permute-done.5.slot = bf16[2,320,256]{2,1,0:T(8,128)(2,1)} collective-permute-done((bf16[2,320,256]{2,1,0:T(8,128)(2,1)}, bf16[2,320,256]{2,1,0:T(8,128)(2,1)}, u32[]{:S(2)}, u32[]{:S(2)}) %collective-permute-start.5) | collective-permute-done | bytes 327712 | tf_op jit(solution)/shard_map/ppermute | solution.py:314
  44.6 2.7 %mixed.1 = (bf16[512,256]{1,0:T(8,128)(2,1)S(1)}, bf16[512,256]{1,0:T(8,128)(2,1)S(1)}) custom-call(s32[5]{0:T(128)S(1)} %stack.67.idx, f32[2,512,256]{2,1,0:T(8,128)S(1)} %get-tuple-element.37.part, bf16[2,512,640]{2,1,0:T(8,128)(2,1)S(1)} %get-tuple-element.38.last, bf16[2,4,4,128,128]{4,3,2,1,0:T(8,128)(2,1)S(1)} %get-tuple-element.39.weights, ...), custom_call_target="tpu_custom_call" | custom-call | flops 335544320 | bytes 3932160 | tf_op jit(solution)/shard_map/mixed/pallas_call | solution.py:426
  47.3 0.1 collective-permute-start.6
  47.4 1.5 %collective-permute-done.7.rest_1_ = bf16[2,320,256]{2,1,0:T(8,128)(2,1)S(1)} collective-permute-done((bf16[2,320,256]{2,1,0:T(8,128)(2,1)}, bf16[2,320,256]{2,1,0:T(8,128)(2,1)S(1)}, u32[]{:S(2)}, u32[]{:S(2)}) %collective-permute-start.7) | collective-permute-done | bytes 327712 | tf_op jit(solution)/shard_map/ppermute | solution.py:314
  48.9 2.9 %assemble.1.w_out.w_o = bf16[2560,256]{1,0:T(8,128)(2,1)} custom-call(s32[5]{0:T(128)S(1)} %stack.67.idx, bf16[512,256]{1,0:T(8,128)(2,1)S(1)} %collective-permute-done.6.unread.mixed_r, bf16[2,320,256]{2,1,0:T(8,128)(2,1)S(1)} %copy-done.9, bf16[2,320,256]{2,1,0:T(8,128)(2,1)S(1)} %collective-permute-done.7.rest_1_, ...), custom_call_target="tpu_custom_call" | custom-call | bytes 2621440 | tf_op jit(solution)/shard_map/assemble/pallas_call | solution.py:450
  51.8 0.2 collective-permute-start.9
  52.0 2.3 %collective-permute-start.11 = (bf16[2,320,256]{2,1,0:T(8,128)(2,1)}, bf16[2,320,256]{2,1,0:T(8,128)(2,1)}, u32[]{:S(2)}, u32[]{:S(2)}) collective-permute-start(bf16[2,320,256]{2,1,0:T(8,128)(2,1)} %collective-permute-done.8.rest_2_), channel_id=1, source_target_pairs={{0,8},{4,12},{8,0},{12,4},{16,24},{20,28},{24,16},{28,20},{1,9},{5... | collective-permute-start | bytes 983048 | tf_op jit(solution)/shard_map/ppermute | solution.py:314
  54.3 7.2 %grad_out.1 = (f32[2,512,256]{2,1,0:T(8,128)S(1)}, bf16[2,512,640]{2,1,0:T(8,128)(2,1)S(1)}, bf16[2,320,256]{2,1,0:T(8,128)(2,1)S(1)}, bf16[2,320,256]{2,1,0:T(8...) custom-call(s32[5]{0:T(128)S(1)} %stack.67.idx, bf16[512,2560]{1,0:T(8,128)(2,1)S(1)} %bitcast.56, ...), custom_call_target="tpu_custom_call" | custom-call | flops 2684354560 | bytes 12058624 | tf_op jit(solution)/shard_map/grad_out/pallas_call | solution.py:461
  61.6 1.1 copy-done.3
  62.6 1.0 copy-done.5
  63.6 0.7 copy-done.11
  64.4 1.2 %copy-done.2 = bf16[2,4,4,128,128]{4,3,2,1,0:T(8,128)(2,1)S(1)} copy-done((bf16[2,4,4,128,128]{4,3,2,1,0:T(8,128)(2,1)S(1)}, bf16[2,4,4,128,128]{4,3,2,1,0:T(8,128)(2,1)}, u32[]{:S(2)}) %copy-start.2) | copy-done | bytes 1048600
  65.6 1.3 %copy-done.4 = bf16[2,512,640]{2,1,0:T(8,128)(2,1)S(1)} copy-done((bf16[2,512,640]{2,1,0:T(8,128)(2,1)S(1)}, bf16[2,512,640]{2,1,0:T(8,128)(2,1)}, u32[]{:S(2)}) %copy-start.4) | copy-done | bytes 1310744
  66.9 1.2 %copy-done.6 = f32[2,512,256]{2,1,0:T(8,128)S(1)} copy-done((f32[2,512,256]{2,1,0:T(8,128)S(1)}, f32[2,512,256]{2,1,0:T(8,128)}, u32[]{:S(2)}) %copy-start.6) | copy-done | bytes 1048600
  68.2 2.7 %d_value.1 = (bf16[256,1024]{1,0:T(8,128)(2,1)S(1)}, bf16[2,320,256]{2,1,0:T(8,128)(2,1)S(1)}) custom-call(s32[5]{0:T(128)S(1)} %stack.67.idx, f32[2,512,256]{2,1,0:T(8,128)S(1)} %copy-done.6, bf16[2,512,640]{2,1,0:T(8,128)(2,1)S(1)} %copy-done.4, bf16[2,4,4,128,128]{4,3,2,1,0:T(8,128)(2,1)S(1)} %copy-done.2, bf16[2,320,256]{2,1,0:T(8,128)(2,1)} %collective-permute-done.11.slot), custom_call_target="tpu_custom_call" | custom-call | flops 335544320 | bytes 3932160 | tf_op jit(solution)/shard_map/d_value/pallas_call | solution.py:472
  70.8 0.2 collective-permute-start.12
  71.1 0.1 pad_add_fusion.idx_node
  71.1 1.9 %collective-permute-start.19 = (bf16[2,320,256]{2,1,0:T(8,128)(2,1)S(1)}, bf16[2,320,256]{2,1,0:T(8,128)(2,1)S(1)}, u32[]{:S(2)}, u32[]{:S(2)}) collective-permute-start(bf16[2,320,256]{2,1,0:T(8,128)(2,1)S(1)} %copy-done.12), channel_id=1, source_target_pairs={{0,8},{4,12},{8,0},{12,4},{16,24},{20,28},{24,16},{28,20},{1,9},{5... | collective-permute-start | bytes 983048 | tf_op jit(solution)/shard_map/ppermute | solution.py:314
  73.0 1.4 %collective-permute-done.17 = bf16[2,320,256]{2,1,0:T(8,128)(2,1)} collective-permute-done((bf16[2,320,256]{2,1,0:T(8,128)(2,1)}, bf16[2,320,256]{2,1,0:T(8,128)(2,1)}, u32[]{:S(2)}, u32[]{:S(2)}) %collective-permute-start.17) | collective-permute-done | bytes 327712 | tf_op jit(solution)/shard_map/ppermute | solution.py:314
  74.5 1.1 add_convert_fusion.unread
  75.5 1.7 %collective-permute-start.20 = (bf16[2,320,256]{2,1,0:T(8,128)(2,1)S(1)}, bf16[2,320,256]{2,1,0:T(8,128)(2,1)S(1)}, u32[]{:S(2)}, u32[]{:S(2)}) collective-permute-start(bf16[2,320,256]{2,1,0:T(8,128)(2,1)S(1)} %add_convert_fusion.unread), channel_id=1, source_target_pairs={{0,16},{4,20},{8,24},{12,28},{16,0},{20,4},{24,8},{28,12},{1,17},{... | collective-permute-start | bytes 983048 | tf_op jit(solution)/shard_map/ppermute | solution.py:314
  77.2 3.6 %terms.1 = (bf16[16,128]{1,0:T(8,128)(2,1)S(1)}, bf16[2,256,640]{2,1,0:T(8,128)(2,1)S(1)}, bf16[2,256,640]{2,1,0:T(8,128)(2,1)S(1)}, bf16[4,256,640]{2,1,0:T(8,128)(2,1)S(1)}) custom-call(s32[4]{0:T(128)S(1)} %pad_add_fusion.idx_node, s32[5]{0:T(128)S(1)} %stack.67.idx, bf16[512,256]{1,0:T(8,128)(2,1)S(1)} %copy-done.14, ...), custom_call_target="tpu_custom_call" | custom-call | flops 1342177280 | bytes 5767168 | tf_op jit(solution)/shard_map/terms/pallas_call | solution.py:523
  80.8 1.6 %collective-permute-start.13 = (bf16[2,256,640]{2,1,0:T(8,128)(2,1)S(1)}, bf16[2,256,640]{2,1,0:T(8,128)(2,1)S(1)}, u32[]{:S(2)}, u32[]{:S(2)}) collective-permute-start(bf16[2,256,640]{2,1,0:T(8,128)(2,1)S(1)} %get-tuple-element.48), channel_id=1, source_target_pairs={{0,1},{1,0},{2,3},{3,2},{4,5},{5,4},{6,7},{7,6},{8,9},{9,8},{10,11... | collective-permute-start | bytes 1966088 | tf_op jit(solution)/shard_map/ppermute | solution.py:325
  82.4 1.5 %collective-permute-start.15 = (bf16[2,256,640]{2,1,0:T(8,128)(2,1)S(1)}, bf16[2,256,640]{2,1,0:T(8,128)(2,1)S(1)}, u32[]{:S(2)}, u32[]{:S(2)}) collective-permute-start(bf16[2,256,640]{2,1,0:T(8,128)(2,1)S(1)} %get-tuple-element.49), channel_id=1, source_target_pairs={{0,2},{1,3},{2,0},{3,1},{4,6},{5,7},{6,4},{7,5},{8,10},{9,11},{10,... | collective-permute-start | bytes 1966088 | tf_op jit(solution)/shard_map/ppermute | solution.py:325
  83.9 4.6 %grad_value.1 = (bf16[2,320,256]{2,1,0:T(8,128)(2,1)S(1)}, bf16[2,320,256]{2,1,0:T(8,128)(2,1)S(1)}, bf16[2,320,256]{2,1,0:T(8,128)(2,1)S(1)}, bf16[2,320,256]{2,1,0:T(8,128)(2,1)S(1)}) custom-call(s32[5]{0:T(128)S(1)} %stack.67.idx, bf16[16,128]{1,0:T(8,128)(2,1)S(1)} %get-tuple-element.50.token, bf16[2,320,256]{2,1,0:T(8,128)(2,1)S(1)} %add_convert_fusion.unread, ...), custom_call_target="tpu_custom_call" | custom-call | flops 1342177280 | bytes 7077888 | tf_op jit(solution)/shard_map/grad_value/pallas_call | solution.py:543
  88.5 0.8 collective-permute-start.18
  89.3 0.2 convert_element_type.50
  89.5 3.1 %collective-permute-done.20.far = bf16[2,320,256]{2,1,0:T(8,128)(2,1)S(1)} collective-permute-done((bf16[2,320,256]{2,1,0:T(8,128)(2,1)S(1)}, bf16[2,320,256]{2,1,0:T(8,128)(2,1)S(1)}, u32[]{:S(2)}, u32[]{:S(2)}) %collective-permute-start.20) | collective-permute-done | bytes 327712 | tf_op jit(solution)/shard_map/ppermute | solution.py:314
  92.6 6.6 %collective-permute-done.18.got = bf16[2,320,256]{2,1,0:T(8,128)(2,1)S(1)} collective-permute-done((bf16[2,320,256]{2,1,0:T(8,128)(2,1)S(1)}, bf16[2,320,256]{2,1,0:T(8,128)(2,1)S(1)}, u32[]{:S(2)}, u32[]{:S(2)}) %collective-permute-start.18) | collective-permute-done | bytes 327712 | tf_op jit(solution)/shard_map/ppermute | solution.py:314
  99.2 0.2 sum.1
  99.4 0.1 collective-permute-start.21
  99.5 1.6 %collective-permute-start.22 = (bf16[2,320,256]{2,1,0:T(8,128)(2,1)S(1)}, bf16[2,320,256]{2,1,0:T(8,128)(2,1)S(1)}, u32[]{:S(2)}, u32[]{:S(2)}) collective-permute-start(bf16[2,320,256]{2,1,0:T(8,128)(2,1)S(1)} %get-tuple-element.61), channel_id=1, source_target_pairs={{0,16},{4,20},{8,24},{12,28},{16,0},{20,4},{24,8},{28,12},{1,17},{... | collective-permute-start | bytes 983048 | tf_op jit(solution)/shard_map/ppermute | solution.py:314
  101.1 0.1 collective-permute-start.24
  101.2 0.1 convert_element_type.51
  101.3 0.1 convert_element_type.55
  101.4 0.1 fusion.8
  101.5 0.6 collective-permute-start.14
  102.1 0.5 collective-permute-start.16
  102.7 10.7 %collective-permute-done.21 = bf16[2,320,256]{2,1,0:T(8,128)(2,1)S(1)} collective-permute-done((bf16[2,320,256]{2,1,0:T(8,128)(2,1)S(1)}, bf16[2,320,256]{2,1,0:T(8,128)(2,1)S(1)}, u32[]{:S(2)}, u32[]{:S(2)}) %collective-permute-start.21) | collective-permute-done | bytes 327712 | tf_op jit(solution)/shard_map/ppermute | solution.py:314
  113.4 3.4 %collective-permute-done.22 = bf16[2,320,256]{2,1,0:T(8,128)(2,1)S(1)} collective-permute-done((bf16[2,320,256]{2,1,0:T(8,128)(2,1)S(1)}, bf16[2,320,256]{2,1,0:T(8,128)(2,1)S(1)}, u32[]{:S(2)}, u32[]{:S(2)}) %collective-permute-start.22) | collective-permute-done | bytes 327712 | tf_op jit(solution)/shard_map/ppermute | solution.py:314
  116.8 0.1 convert_add_fusion
  116.9 0.1 collective-permute-start.23
  117.1 0.9 pad_maximum_fusion.2
  118.0 0.2 fusion.7
  118.2 0.9 pad_maximum_fusion
  119.1 0.9 pad_maximum_fusion.1
  (47 shorter events, 0.5 us)
Async XLA Ops:
  0.6 3.2 %copy-start = (bf16[2,2,128,2560]{3,2,1,0:T(8,128)(2,1)S(1)}, bf16[2,2,128,2560]{3,2,1,0:T(8,128)(2,1)}, u32[]{:S(2)}) copy-start(bf16[2,2,128,2560]{3,2,1,0:T(8,128)(2,1)} %param.5) | copy-start | bytes 7864324
  2.1 1.8 %collective-permute-start = (bf16[2,320,256]{2,1,0:T(8,128)(2,1)S(1)}, bf16[2,320,256]{2,1,0:T(8,128)(2,1)S(1)}, u32[]{:S(2)}, u32[]{:S(2)}) collective-permute-start(bf16[2,320,256]{2,1,0:T(8,128)(2,1)S(1)} %get-tuple-element.72), channel_id=1, source_target_pairs={{0,4},{4,0},{8,12},{12,8},{16,20},{20,16},{24,28},{28,24},{1,5},{5... | collective-permute-start | bytes 983048 | tf_op jit(solution)/shard_map/ppermute | solution.py:322
  3.8 26.1 %collective-permute-start.1 = (bf16[512,2560]{1,0:T(8,128)(2,1)S(1)}, bf16[512,2560]{1,0:T(8,128)(2,1)}, u32[]{:S(2)}, u32[]{:S(2)}) collective-permute-start(bf16[512,2560]{1,0:T(8,128)(2,1)S(1)} %bitcast.50), channel_id=1, source_target_pairs={{0,4},{4,0},{8,12},{12,8},{16,20},{20,16},{24,28},{28,24},{1,5},{5... | collective-permute-start | bytes 7864328 | tf_op jit(solution)/shard_map/ppermute | solution.py:322
  4.2 50.1 %collective-permute-start.10 = (bf16[512,2560]{1,0:T(8,128)(2,1)}, bf16[512,2560]{1,0:T(8,128)(2,1)}, u32[]{:S(2)}, u32[]{:S(2)}) collective-permute-start(bf16[512,2560]{1,0:T(8,128)(2,1)} %bitcast.55), channel_id=1, source_target_pairs={{0,4},{4,0},{8,12},{12,8},{16,20},{20,16},{24,28},{28,24},{1,5},{5... | collective-permute-start | bytes 7864328 | tf_op jit(solution)/shard_map/ppermute | solution.py:322
  4.4 24.5 %collective-permute-start.2 = (bf16[4,8,128,128]{3,2,1,0:T(8,128)(2,1)}, bf16[4,8,128,128]{3,2,1,0:T(8,128)(2,1)}, u32[]{:S(2)}, u32[]{:S(2)}) collective-permute-start(bf16[4,8,128,128]{3,2,1,0:T(8,128)(2,1)} %bitcast.53), channel_id=1, source_target_pairs={{0,4},{4,0},{8,12},{12,8},{16,20},{20,16},{24,28},{28,24},{1,5},{5... | collective-permute-start | bytes 3145736 | tf_op jit(solution)/shard_map/ppermute | solution.py:322
  4.8 17.9 %collective-permute-start.3 = (bf16[2,320,256]{2,1,0:T(8,128)(2,1)S(1)}, bf16[2,320,256]{2,1,0:T(8,128)(2,1)S(1)}, u32[]{:S(2)}, u32[]{:S(2)}) collective-permute-start(bf16[2,320,256]{2,1,0:T(8,128)(2,1)S(1)} %pad_maximum_fusion.5.rest_0_), channel_id=1, source_target_pairs={{0,8},{4,12},{8,0},{12,4},{16,24},{20,28},{24,16},{28,20},{1,9},{5... | collective-permute-start | bytes 983048 | tf_op jit(solution)/shard_map/ppermute | solution.py:314
  7.6 17.7 %collective-permute-start.4 = (bf16[2,320,256]{2,1,0:T(8,128)(2,1)S(1)}, bf16[2,320,256]{2,1,0:T(8,128)(2,1)S(1)}, u32[]{:S(2)}, u32[]{:S(2)}) collective-permute-start(bf16[2,320,256]{2,1,0:T(8,128)(2,1)S(1)} %pad_maximum_fusion.5.rest_0_), channel_id=1, source_target_pairs={{0,16},{4,20},{8,24},{12,28},{16,0},{20,4},{24,8},{28,12},{1,17},{... | collective-permute-start | bytes 983048 | tf_op jit(solution)/shard_map/ppermute | solution.py:314
  26.1 0.7 copy-start.8
  26.8 17.9 %collective-permute-start.5 = (bf16[2,320,256]{2,1,0:T(8,128)(2,1)}, bf16[2,320,256]{2,1,0:T(8,128)(2,1)}, u32[]{:S(2)}, u32[]{:S(2)}) collective-permute-start(bf16[2,320,256]{2,1,0:T(8,128)(2,1)} %get-tuple-element.36.rest_2_), channel_id=1, source_target_pairs={{0,8},{4,12},{8,0},{12,4},{16,24},{20,28},{24,16},{28,20},{1,9},{5... | collective-permute-start | bytes 983048 | tf_op jit(solution)/shard_map/ppermute | solution.py:314
  27.3 21.5 %collective-permute-start.7 = (bf16[2,320,256]{2,1,0:T(8,128)(2,1)}, bf16[2,320,256]{2,1,0:T(8,128)(2,1)S(1)}, u32[]{:S(2)}, u32[]{:S(2)}) collective-permute-start(bf16[2,320,256]{2,1,0:T(8,128)(2,1)} %copy-done.8), channel_id=1, source_target_pairs={{0,8},{4,12},{8,0},{12,4},{16,24},{20,28},{24,16},{28,20},{1,9},{5... | collective-permute-start | bytes 983048 | tf_op jit(solution)/shard_map/ppermute | solution.py:314
  28.9 20.0 %collective-permute-start.8 = (bf16[2,320,256]{2,1,0:T(8,128)(2,1)}, bf16[2,320,256]{2,1,0:T(8,128)(2,1)}, u32[]{:S(2)}, u32[]{:S(2)}) collective-permute-start(bf16[2,320,256]{2,1,0:T(8,128)(2,1)} %copy-done.8), channel_id=1, source_target_pairs={{0,16},{4,20},{8,24},{12,28},{16,0},{20,4},{24,8},{28,12},{1,17},{... | collective-permute-start | bytes 983048 | tf_op jit(solution)/shard_map/ppermute | solution.py:314
  30.0 1.2 %copy-start.7 = (bf16[2,2,8,128,128]{4,3,2,1,0:T(8,128)(2,1)S(1)}, bf16[2,2,8,128,128]{4,3,2,1,0:T(8,128)(2,1)}, u32[]{:S(2)}) copy-start(bf16[2,2,8,128,128]{4,3,2,1,0:T(8,128)(2,1)} %param.6) | copy-start | bytes 3145732
  36.1 11.2 %copy-start.1 = (bf16[2,4,4,128,128]{4,3,2,1,0:T(8,128)(2,1)}, bf16[2,4,4,128,128]{4,3,2,1,0:T(8,128)(2,1)S(1)}, u32[]{:S(2)}) copy-start(bf16[2,4,4,128,128]{4,3,2,1,0:T(8,128)(2,1)S(1)} %get-tuple-element.39.weights) | copy-start | bytes 3145732
  44.6 4.3 %copy-start.9 = (bf16[2,320,256]{2,1,0:T(8,128)(2,1)S(1)}, bf16[2,320,256]{2,1,0:T(8,128)(2,1)}, u32[]{:S(2)}) copy-start(bf16[2,320,256]{2,1,0:T(8,128)(2,1)} %copy-done.8) | copy-start | bytes 983044
  44.6 9.7 %copy-start.10 = (bf16[2,2,128,2560]{3,2,1,0:T(8,128)(2,1)S(1)}, bf16[2,2,128,2560]{3,2,1,0:T(8,128)(2,1)}, u32[]{:S(2)}) copy-start(bf16[2,2,128,2560]{3,2,1,0:T(8,128)(2,1)} %param.7) | copy-start | bytes 7864324
  47.3 14.2 %copy-start.13 = (bf16[512,256]{1,0:T(8,128)(2,1)}, bf16[512,256]{1,0:T(8,128)(2,1)S(1)}, u32[]{:S(2)}) copy-start(bf16[512,256]{1,0:T(8,128)(2,1)S(1)} %get-tuple-element.40.mixed_o) | copy-start | bytes 786436
  47.3 1.6 %collective-permute-start.6 = (bf16[512,256]{1,0:T(8,128)(2,1)S(1)}, bf16[512,256]{1,0:T(8,128)(2,1)S(1)}, u32[]{:S(2)}, u32[]{:S(2)}) collective-permute-start(bf16[512,256]{1,0:T(8,128)(2,1)S(1)} %get-tuple-element.41.mixed_s), channel_id=1, source_target_pairs={{0,4},{4,0},{8,12},{12,8},{16,20},{20,16},{24,28},{28,24},{1,5},{5... | collective-permute-start | bytes 786440 | tf_op jit(solution)/shard_map/ppermute | solution.py:322
  51.8 25.4 %collective-permute-start.9 = (bf16[2560,256]{1,0:T(8,128)(2,1)}, bf16[2560,256]{1,0:T(8,128)(2,1)}, u32[]{:S(2)}, u32[]{:S(2)}) collective-permute-start(bf16[2560,256]{1,0:T(8,128)(2,1)} %assemble.1.w_out.w_o), channel_id=1, source_target_pairs={{0,4},{4,0},{8,12},{12,8},{16,20},{20,16},{24,28},{28,24},{1,5},{5... | collective-permute-start | bytes 3932168 | tf_op jit(solution)/shard_map/ppermute | solution.py:322
  52.0 12.4 %collective-permute-start.11 = (bf16[2,320,256]{2,1,0:T(8,128)(2,1)}, bf16[2,320,256]{2,1,0:T(8,128)(2,1)}, u32[]{:S(2)}, u32[]{:S(2)}) collective-permute-start(bf16[2,320,256]{2,1,0:T(8,128)(2,1)} %collective-permute-done.8.rest_2_), channel_id=1, source_target_pairs={{0,8},{4,12},{8,0},{12,4},{16,24},{20,28},{24,16},{28,20},{1,9},{5... | collective-permute-start | bytes 983048 | tf_op jit(solution)/shard_map/ppermute | solution.py:314
  61.6 1.1 copy-start.3
  62.6 1.0 copy-start.5
  63.6 0.7 copy-start.11
  64.4 10.1 %collective-permute-start.17 = (bf16[2,320,256]{2,1,0:T(8,128)(2,1)}, bf16[2,320,256]{2,1,0:T(8,128)(2,1)}, u32[]{:S(2)}, u32[]{:S(2)}) collective-permute-start(bf16[2,320,256]{2,1,0:T(8,128)(2,1)} %get-tuple-element.52), channel_id=1, source_target_pairs={{0,8},{4,12},{8,0},{12,4},{16,24},{20,28},{24,16},{28,20},{1,9},{5... | collective-permute-start | bytes 983048 | tf_op jit(solution)/shard_map/ppermute | solution.py:314
  64.4 1.2 %copy-start.2 = (bf16[2,4,4,128,128]{4,3,2,1,0:T(8,128)(2,1)S(1)}, bf16[2,4,4,128,128]{4,3,2,1,0:T(8,128)(2,1)}, u32[]{:S(2)}) copy-start(bf16[2,4,4,128,128]{4,3,2,1,0:T(8,128)(2,1)} %copy-done.1) | copy-start | bytes 3145732
  65.6 1.3 %copy-start.4 = (bf16[2,512,640]{2,1,0:T(8,128)(2,1)S(1)}, bf16[2,512,640]{2,1,0:T(8,128)(2,1)}, u32[]{:S(2)}) copy-start(bf16[2,512,640]{2,1,0:T(8,128)(2,1)} %copy-done.3) | copy-start | bytes 3932164
  66.9 1.2 %copy-start.6 = (f32[2,512,256]{2,1,0:T(8,128)S(1)}, f32[2,512,256]{2,1,0:T(8,128)}, u32[]{:S(2)}) copy-start(f32[2,512,256]{2,1,0:T(8,128)} %copy-done.5) | copy-start | bytes 3145732
  68.2 3.0 %copy-start.12 = (bf16[2,320,256]{2,1,0:T(8,128)(2,1)S(1)}, bf16[2,320,256]{2,1,0:T(8,128)(2,1)}, u32[]{:S(2)}) copy-start(bf16[2,320,256]{2,1,0:T(8,128)(2,1)} %copy-done.11) | copy-start | bytes 983044
  68.2 9.1 %copy-start.14 = (bf16[512,256]{1,0:T(8,128)(2,1)S(1)}, bf16[512,256]{1,0:T(8,128)(2,1)}, u32[]{:S(2)}) copy-start(bf16[512,256]{1,0:T(8,128)(2,1)} %copy-done.13) | copy-start | bytes 786436
  70.8 6.4 %collective-permute-start.12 = (bf16[2,320,256]{2,1,0:T(8,128)(2,1)S(1)}, bf16[2,320,256]{2,1,0:T(8,128)(2,1)S(1)}, u32[]{:S(2)}, u32[]{:S(2)}) collective-permute-start(bf16[2,320,256]{2,1,0:T(8,128)(2,1)S(1)} %get-tuple-element.46.slot), channel_id=1, source_target_pairs={{0,4},{4,0},{8,12},{12,8},{16,20},{20,16},{24,28},{28,24},{1,5},{5... | collective-permute-start | bytes 983048 | tf_op jit(solution)/shard_map/ppermute | solution.py:322
  71.1 18.3 %collective-permute-start.19 = (bf16[2,320,256]{2,1,0:T(8,128)(2,1)S(1)}, bf16[2,320,256]{2,1,0:T(8,128)(2,1)S(1)}, u32[]{:S(2)}, u32[]{:S(2)}) collective-permute-start(bf16[2,320,256]{2,1,0:T(8,128)(2,1)S(1)} %copy-done.12), channel_id=1, source_target_pairs={{0,8},{4,12},{8,0},{12,4},{16,24},{20,28},{24,16},{28,20},{1,9},{5... | collective-permute-start | bytes 983048 | tf_op jit(solution)/shard_map/ppermute | solution.py:314
  75.5 17.1 %collective-permute-start.20 = (bf16[2,320,256]{2,1,0:T(8,128)(2,1)S(1)}, bf16[2,320,256]{2,1,0:T(8,128)(2,1)S(1)}, u32[]{:S(2)}, u32[]{:S(2)}) collective-permute-start(bf16[2,320,256]{2,1,0:T(8,128)(2,1)S(1)} %add_convert_fusion.unread), channel_id=1, source_target_pairs={{0,16},{4,20},{8,24},{12,28},{16,0},{20,4},{24,8},{28,12},{1,17},{... | collective-permute-start | bytes 983048 | tf_op jit(solution)/shard_map/ppermute | solution.py:314
  80.8 20.4 %collective-permute-start.13 = (bf16[2,256,640]{2,1,0:T(8,128)(2,1)S(1)}, bf16[2,256,640]{2,1,0:T(8,128)(2,1)S(1)}, u32[]{:S(2)}, u32[]{:S(2)}) collective-permute-start(bf16[2,256,640]{2,1,0:T(8,128)(2,1)S(1)} %get-tuple-element.48), channel_id=1, source_target_pairs={{0,1},{1,0},{2,3},{3,2},{4,5},{5,4},{6,7},{7,6},{8,9},{9,8},{10,11... | collective-permute-start | bytes 1966088 | tf_op jit(solution)/shard_map/ppermute | solution.py:325
  82.4 18.9 %collective-permute-start.15 = (bf16[2,256,640]{2,1,0:T(8,128)(2,1)S(1)}, bf16[2,256,640]{2,1,0:T(8,128)(2,1)S(1)}, u32[]{:S(2)}, u32[]{:S(2)}) collective-permute-start(bf16[2,256,640]{2,1,0:T(8,128)(2,1)S(1)} %get-tuple-element.49), channel_id=1, source_target_pairs={{0,2},{1,3},{2,0},{3,1},{4,6},{5,7},{6,4},{7,5},{8,10},{9,11},{10,... | collective-permute-start | bytes 1966088 | tf_op jit(solution)/shard_map/ppermute | solution.py:325
  88.5 10.7 %collective-permute-start.18 = (bf16[2,320,256]{2,1,0:T(8,128)(2,1)S(1)}, bf16[2,320,256]{2,1,0:T(8,128)(2,1)S(1)}, u32[]{:S(2)}, u32[]{:S(2)}) collective-permute-start(bf16[2,320,256]{2,1,0:T(8,128)(2,1)S(1)} %get-tuple-element.56), channel_id=1, source_target_pairs={{0,8},{4,12},{8,0},{12,4},{16,24},{20,28},{24,16},{28,20},{1,9},{5... | collective-permute-start | bytes 983048 | tf_op jit(solution)/shard_map/ppermute | solution.py:314
  99.4 14.0 %collective-permute-start.21 = (bf16[2,320,256]{2,1,0:T(8,128)(2,1)S(1)}, bf16[2,320,256]{2,1,0:T(8,128)(2,1)S(1)}, u32[]{:S(2)}, u32[]{:S(2)}) collective-permute-start(bf16[2,320,256]{2,1,0:T(8,128)(2,1)S(1)} %get-tuple-element.60), channel_id=1, source_target_pairs={{0,8},{4,12},{8,0},{12,4},{16,24},{20,28},{24,16},{28,20},{1,9},{5... | collective-permute-start | bytes 983048 | tf_op jit(solution)/shard_map/ppermute | solution.py:314
  99.5 17.3 %collective-permute-start.22 = (bf16[2,320,256]{2,1,0:T(8,128)(2,1)S(1)}, bf16[2,320,256]{2,1,0:T(8,128)(2,1)S(1)}, u32[]{:S(2)}, u32[]{:S(2)}) collective-permute-start(bf16[2,320,256]{2,1,0:T(8,128)(2,1)S(1)} %get-tuple-element.61), channel_id=1, source_target_pairs={{0,16},{4,20},{8,24},{12,28},{16,0},{20,4},{24,8},{28,12},{1,17},{... | collective-permute-start | bytes 983048 | tf_op jit(solution)/shard_map/ppermute | solution.py:314
  101.1 15.9 %collective-permute-start.24 = (f32[320,256]{1,0:T(8,128)S(1)}, f32[320,256]{1,0:T(8,128)S(1)}, u32[]{:S(2)}, u32[]{:S(2)}) collective-permute-start(f32[320,256]{1,0:T(8,128)S(1)} %slice_bitcast_fusion.2), channel_id=1, source_target_pairs={{0,4},{4,0},{8,12},{12,8},{16,20},{20,16},{24,28},{28,24},{1,5},{5... | collective-permute-start | bytes 983048 | tf_op jit(solution)/shard_map/ppermute | solution.py:322
  101.5 16.4 %collective-permute-start.14 = (bf16[256,640]{1,0:T(8,128)(2,1)S(1)}, bf16[256,640]{1,0:T(8,128)(2,1)S(1)}, u32[]{:S(2)}, u32[]{:S(2)}) collective-permute-start(bf16[256,640]{1,0:T(8,128)(2,1)S(1)} %get-tuple-element.65), channel_id=1, source_target_pairs={{0,2},{1,3},{2,0},{3,1},{4,6},{5,7},{6,4},{7,5},{8,10},{9,11},{10,... | collective-permute-start | bytes 983048 | tf_op jit(solution)/shard_map/ppermute | solution.py:325
  102.1 15.9 %collective-permute-start.16 = (bf16[256,640]{1,0:T(8,128)(2,1)S(1)}, bf16[256,640]{1,0:T(8,128)(2,1)S(1)}, u32[]{:S(2)}, u32[]{:S(2)}) collective-permute-start(bf16[256,640]{1,0:T(8,128)(2,1)S(1)} %get-tuple-element.66), channel_id=1, source_target_pairs={{0,1},{1,0},{2,3},{3,2},{4,5},{5,4},{6,7},{7,6},{8,9},{9,8},{10,11... | collective-permute-start | bytes 983048 | tf_op jit(solution)/shard_map/ppermute | solution.py:325
  116.9 2.1 %collective-permute-start.23 = (f32[320,256]{1,0:T(8,128)S(1)}, f32[320,256]{1,0:T(8,128)S(1)}, u32[]{:S(2)}, u32[]{:S(2)}) collective-permute-start(f32[320,256]{1,0:T(8,128)S(1)} %slice_bitcast_fusion), channel_id=1, source_target_pairs={{0,4},{4,0},{8,12},{12,8},{16,20},{20,16},{24,28},{28,24},{1,5},{5... | collective-permute-start | bytes 983048 | tf_op jit(solution)/shard_map/ppermute | solution.py:322

commit v15 on v14

--- a/solution.py
+++ b/solution.py
@@ -140,34 +140,21 @@
         mix_values(value, weights.at[half], out)
 
 
-def d_value_rest_kernel(idx, part, last, weights, slot, left_v, slot_out):
-    slot_out[...] = slot[...]
-    w_last = whole(idx[0], slot)
-    tokens = part.shape[1]
-    for half in range(2):
-        mix_back(part[half] + dot(last[half], w_last), weights.at[half], left_v, half * tokens)
-
-
-def assemble_kernel(n_slots, idx, unread, *rest):
-    del unread
-    slots, (w_out, slots_v, sems) = rest[:n_slots], rest[n_slots:]
-    copies = begin_slots(slots, slots_v, sems)
-    planes, depth = idx.shape[0] - 1, 2 * slots_v.shape[2]
-    for j in range(n_slots, planes):
-        w_out[rows_at(idx[1 + j], depth), :] = jnp.zeros((depth, w_out.shape[1]), BF16)
-    for copy in copies:
-        copy.wait()
-    place(idx, idx[0], slots_v, w_out)
-
-
-def d_value_kernel(idx, cot_o, cot_s, mix_o, mix_s, w_out, left_v, cot_v, mix_v, sems):
+def d_value_kernel(n_slots, idx, token, cot_o, cot_s, mix_o, mix_s, *rest):
+    del token
+    slots, rest = rest[:n_slots], rest[n_slots:]
+    left_v, w_out, cot_v, mix_v, sems, slots_v, slot_sems = rest
     tokens, heads = cot_o.shape[0], mix_v.shape[2]
     here = pl.ds(idx[0] * heads, heads)
+    slot_copies = begin_slots(slots, slots_v, slot_sems)
     copies = begin(
         [(cot_o, cot_v.at[0]), (mix_o.at[:, here], mix_v.at[0])]
         + [(cot_s, cot_v.at[1]), (mix_s.at[:, here], mix_v.at[1])],
         sems,
     )
+    for copy in slot_copies:
+        copy.wait()
+    place(idx, idx[0], slots_v, w_out)
     for half in range(2):
         copies[2 * half].wait()
         d_mixed = dot(cot_v[half], w_out[...])
@@ -210,37 +197,19 @@
         mix_values(value, mix_v.at[half], out)
 
 
-def grad_out_kernel(idx, cot_o, cot_s, mixed_o, mixed_s, w_out, unread, *rest):
-    del unread
-    *outs, cot_v, left_v, grad_v, sems, last_sems = rest
-    part = last = None
-    if w_out is not None:
-        part, last, *outs = outs
+def grad_out_kernel(n_unread, idx, cot_o, cot_s, mixed_o, mixed_s, *rest):
+    token, *outs, cot_v, left_v, grad_v, sems = rest[n_unread:]
+    token[...] = jnp.zeros_like(token)
     tokens, _ = cot_o.shape
     copies = begin(
         [(cot_o, cot_v.at[pl.ds(0, tokens)]), (cot_s, cot_v.at[pl.ds(tokens, tokens)])], sems
     )
-    if w_out is not None:
-        depth = last.shape[2]
-        columns = pl.ds(pl.multiple_of(idx[idx.shape[0] - 1] * depth, 128), depth)
-        later = begin(
-            [(cot_o.at[:, columns], last.at[0]), (cot_s.at[:, columns], last.at[1])], last_sems
-        )
     left_v[:, :tokens] = mixed_o[...].astype(F32).T.astype(BF16)
     left_v[:, tokens:] = mixed_s[...].astype(F32).T.astype(BF16)
     copies[0].wait()
     copies[1].wait()
     gradient_rows(left_v[...], cot_v, grad_v, 640)
     hand_out(idx, 1, grad_v, outs)
-    if w_out is not None:
-        for half in range(2):
-            part[half] = dot(cot_v[half * tokens : (half + 1) * tokens, :], w_out[...])
-        for copy in later:
-            copy.wait()
-
-
-def grad_out_only_kernel(idx, cot_o, cot_s, mixed_o, mixed_s, unread, *rest):
-    grad_out_kernel(idx, cot_o, cot_s, mixed_o, mixed_s, None, unread, *rest)
 
 
 def relay_kernel(unread, first, second, first_out, second_out):
@@ -255,26 +224,18 @@
     total[...] = own[...].astype(F32) + near[...].astype(F32) + far[...].astype(F32)
 
 
-def terms_kernel(n_node, idx, mixed_o, mixed_r, w_o, w_r, *outs):
+def terms_kernel(n_node, idx, mixed_o, mixed_r, w_o, w_r, token, *outs):
+    token[...] = jnp.zeros_like(token)
     depth = w_o.shape[0] // n_node
+    half = mixed_o.shape[0] // 2
     for j in range(n_node):
         rows = rows_at(idx[j], depth)
         term = dot(mixed_o[...], w_o[rows, :], 1, 1) + dot(mixed_r[...], w_r[rows, :], 1, 1)
-        outs[j][...] = term.astype(BF16)
-
-
-def terms_line_kernel(idx_node, idx, mixed_o, mixed_r, w_o, w_r, slot, slot_r, *outs):
-    token, along_x, along_y, kept = outs
-    token[...] = jnp.zeros_like(token)
-    core, missing = idx[0], idx[4]
-    last_o, last_r = whole(core, slot), whole(1 - core, slot_r)
-    half = mixed_o.shape[0] // 2
-    for j in range(4):
-        rows = rows_at(idx_node[j], last_o.shape[0])
-        here = idx_node[j] == missing
-        term = dot(mixed_o[...], jnp.where(here, last_o, w_o[rows, :]), 1, 1)
-        term += dot(mixed_r[...], jnp.where(here, last_r, w_r[rows, :]), 1, 1)
         term = term.astype(BF16)
+        if n_node != 4:
+            outs[j][...] = term
+            continue
+        along_x, along_y, kept = outs
         first, second = term[:half], term[half:]
         if j == 0:
             kept[0], kept[2] = first, second
@@ -444,102 +405,48 @@
                 2 * (2 * act.size + mix.size + width * cols + 2 * tokens * cols),
                 )(idx, act, act_s, mix, mix_s, *value_slots)
         mixed_r = sibling(mixed_s)
-        grad_scratch = [both, left_tokens, rows] + [pltpu.SemaphoreType.DMA((2,))] * 2
-        size = 2 * (3 * cot.size + 6 * tokens * cols + 2 * width * cols)
-        if line4:
-            w_part = call(
-                functools.partial(assemble_kernel, n_slots - 1),
-                "assemble",
-                [SMEM] + [ANY] * n_slots,
-                [(width, cols)],
-                [pltpu.VMEM((n_slots - 1, *block), BF16), pltpu.SemaphoreType.DMA((n_slots - 1,))],
-                0,
-                4 * width * cols,
-            )(idx, mixed_r, *out_slots[:-1])[0]
-            w_part_s = sibling(w_part)
-            *rest, w_mix = ahead
-            part, last, *out_sends = call(
-                grad_out_kernel,
-                "grad_out",
-                [SMEM] + [ANY] * 2 + [VMEM] * 3 + [ANY],
-                part_shapes + send_shapes,
-                grad_scratch,
-                2 * flops,
-                size,
-                kinds=[F32] + [BF16] * (1 + n_slots),
-            )(idx, cot, cot_s, mixed_o, mixed_s, w_part, mixed_r)
-            out_passed = swap(out_sends[3], 1)
-            left, last_block = call(
-                d_value_rest_kernel,
-                "d_value",
-                [SMEM] + [VMEM] * 4,
-                [(cols, 2 * tokens), block],
-                [],
-                flops // 4,
-                2 * (2 * tokens * depth + mix.size + 6 * tokens * cols),
-                vmem=16,
-            )(idx, part, last, w_mix, out_slots[-1])
-            last_s = sibling(last_block)
-        else:
-            out_sends = call(
-                grad_out_only_kernel,
-                "grad_out",
-                [SMEM] + [ANY] * 2 + [VMEM] * 2 + [ANY],
-                send_shapes,
-                grad_scratch,
-                flops,
-                size,
-            )(idx, cot, cot_s, mixed_o, mixed_s, mixed_r)
-            w_full = call(
-                functools.partial(assemble_kernel, n_slots),
-                "assemble",
-                [SMEM] + [ANY] * (1 + n_slots),
-                [(width, cols)],
-                slots_scratch,
-                0,
-                4 * width * cols,
-            )(idx, mixed_s, *out_slots)[0]
-            left = call(
-                d_value_kernel,
-                "d_value",
-                [SMEM] + [ANY] * 4 + [VMEM],
-                [(cols, 2 * tokens)],
-                [halves, mix_scratch, pltpu.SemaphoreType.DMA((4,))],
-                flops,
-                2 * (2 * cot.size + mix.size + width * cols + 2 * tokens * cols),
-            )(idx, cot, cot_s, mix, mix_s, w_full)[0]
-            w_full_s = sibling(w_full)
-            token = left
+        unread = [mixed_r, *(out_slots[1:3] if line4 else [])]
+        token, *out_sends = call(
+            functools.partial(grad_out_kernel, len(unread)),
+            "grad_out",
+            [SMEM] + [ANY] * 2 + [VMEM] * 2 + [ANY] * len(unread),
+            [(16, 128)] + send_shapes,
+            [both, left_tokens, rows, pltpu.SemaphoreType.DMA((2,))],
+            flops,
+            2 * (2 * cot.size + 2 * tokens * cols + width * cols),
+        )(idx, cot, cot_s, mixed_o, mixed_s, *unread)
+        out_passed = swap(out_sends[3], 1) if line4 else token
+        left, w_full = call(
+            functools.partial(d_value_kernel, n_slots),
+            "d_value",
+            [SMEM] + [ANY] * (5 + n_slots),
+            [(cols, 2 * tokens), (width, cols)],
+            [halves, mix_scratch, pltpu.SemaphoreType.DMA((4,)), *slots_scratch],
+            flops,
+            2 * (2 * cot.size + mix.size + 2 * width * cols + 2 * tokens * cols),
+        )(idx, token, cot, cot_s, mix, mix_s, *out_slots)
+        w_full_s = sibling(w_full)
         if line4:
             out_onward = added(out_sends[2], out_passed)
             out_far = swap(out_onward, 2)
             out_near = swap(out_sends[1], 1)
         else:
-            out_onward = token
+            out_onward = left
         part = width // n_node
         half = tokens // 2
-        size = 2 * (2 * tokens * cols + 2 * width * cols + tokens * width)
-        if line4:
-            token, *terms = call(
-                terms_line_kernel,
-                "terms",
-                [SMEM] * 2 + [VMEM] * 6,
-                [(16, 128), (2, half, part), (2, half, part), (4, half, part)],
-                [],
-                flops,
-                size,
-            )(idx_node, idx, mixed_o, mixed_r, w_part, w_part_s, last_block, last_s)
-        else:
-            terms = call(
-                functools.partial(terms_kernel, n_node),
-                "terms",
-                [SMEM] + [VMEM] * 4,
-                [(tokens, part)] * n_node,
-                [],
-                flops,
-                size,
-            )(idx_node, mixed_o, mixed_r, w_full, w_full_s)
-
+        if n_node == 4:
+            term_shapes = [(2, half, part), (2, half, part), (4, half, part)]
+        else:
+            term_shapes = [(tokens, part)] * n_node
+        token, *terms = call(
+            functools.partial(terms_kernel, n_node),
+            "terms",
+            [SMEM] + [VMEM] * 4,
+            [(16, 128)] + term_shapes,
+            [],
+            flops,
+            2 * (2 * tokens * cols + 2 * width * cols + tokens * width),
+        )(idx_node, mixed_o, mixed_r, w_full, w_full_s)
         back_sends = call(
             gradient_kernel,
             "grad_value",
@@ -561,7 +468,7 @@
             grad_value = scatter_ring(back_sends, c)
             grad_out = scatter_ring(out_sends, c)
 
-        if line4:
+        if n_node == 4:
             along_x, along_y, kept = terms
             kept = kept.astype(F32)
             got_x = flip(along_x, 1).astype(F32)

time: 121 us -> 119 us (0.983)
  waiting for transfers between devices: 51.6 us -> 55.2 us
  local copies, waits for them, and re-layouts: 10.1 us -> 7.87 us
  Pallas kernels: 29.5 us -> 27.9 us
    ppermute x12, waiting for transfers between devices: 50.3 us -> 53.9 us  [move(): lax.ppermute(x, 'wide', [(2 * s + c, 2 * d + c) for s, d in pairs for c i...]
    unnamed x30 -> x24, local copies, waits for them, and re-layouts: 8.55 us -> 6.35 us
    pallas_call x4 -> x3, Pallas kernels: 16.3 us -> 14.8 us  [the longest x1 6.36 us: body(): call(functools.partial(d_value_kernel, n_slots), 'd_value', [SMEM] + [ANY...]
  transfers between devices with their start and end apart: 25 -> 24, of which waited for: 11 -> 11; matrix products, arithmetic and copies ran while one was open for 3% -> 3% of each run, Pallas kernels for 25% -> 18%
where the time goes in v15:
time: 119 us
  waiting for transfers between devices  55.2 us (46%)
  Pallas kernels  27.9 us (23%)
  starting transfers between devices  22.9 us (19%)
  local copies, waits for them, and re-layouts  7.87 us (7%)
  other arithmetic  3.98 us (3%)
    ppermute x12, waiting for transfers between devices, move(): lax.ppermute(x, 'wide', [(2 * s + c, 2 * d + c) for s, d in pairs for c i...  53.9 us
    ppermute x12, starting transfers between devices, move(): lax.ppermute(x, 'wide', [(2 * s + c, 2 * d + c) for s, d in pairs for c i...  16 us
    pallas_call x1, Pallas kernels, body(): call(functools.partial(d_value_kernel, n_slots), 'd_value', [SMEM] + [ANY...  6.36 us
    unnamed x24, local copies, waits for them, and re-layouts  6.35 us
    pallas_call x1, Pallas kernels, body(): call(functools.partial(grad_out_kernel, len(unread)), 'grad_out', [SMEM]...  5.29 us
    ppermute x4, starting transfers between devices, flip(): return lax.ppermute(x, 'node', [(i, i ^ j) for i in range(n_node)])  5.23 us
    pallas_call x1, Pallas kernels, body(): call(functools.partial(part_kernel, n_slots - 1), 'value_ahead', [SMEM] +...  4.9 us
    pallas_call x1, Pallas kernels, body(): call(gradient_kernel, 'grad_value', [SMEM] + [ANY] * 4 + [VMEM], send_sha...  4.63 us
  transfers between devices with their start and end apart: 24, of which 11 were waited for; matrix products, arithmetic and copies ran while one was open for 3% of the time, Pallas kernels for 18%

profile of v15, /device:TPU:0, one launch (start us, length us, event | category | flops | bytes accessed | tf_op | source)
XLA Modules:
  0.0 118.9 jit_solution(14750537763586436363)
XLA Ops:
  0.7 1.3 %slice_bitcast_fusion.5 = (bf16[1,320,256]{2,1,0:T(8,128)(2,1)S(1)}, bf16[1,320,256]{2,1,0:T(8,128)(2,1)S(1)}, bf16[1,320,256]{2,1,0:T(8,128)(2,1)S(1)}, bf16[1,320,256]{2,1,0:T(8,128)(2,1)S(1)}) fusion(bf16[320,512]{1,0:T(8,128)(2,1)} %param.8, bf16[320,512]{1,0:T(8,128)(2,1)} %param.9), kind=kLoop, calls=%fused_computation.34 | loop fusion | bytes 1310720 | tf_op jit(solution)/shard_map/stack | solution.py:291
  2.0 0.1 broadcast_select_fusion
  2.1 0.5 collective-permute-start
  2.6 1.3 %collective-permute-done = bf16[2,320,256]{2,1,0:T(8,128)(2,1)S(1)} collective-permute-done((bf16[2,320,256]{2,1,0:T(8,128)(2,1)S(1)}, bf16[2,320,256]{2,1,0:T(8,128)(2,1)S(1)}, u32[]{:S(2)}, u32[]{:S(2)}) %collective-permute-start) | collective-permute-done | bytes 327712 | tf_op jit(solution)/shard_map/ppermute | solution.py:283
  3.8 0.4 collective-permute-start.1
  4.2 0.1 collective-permute-start.7
  4.4 0.4 collective-permute-start.2
  4.8 2.8 %collective-permute-start.3 = (bf16[2,320,256]{2,1,0:T(8,128)(2,1)S(1)}, bf16[2,320,256]{2,1,0:T(8,128)(2,1)S(1)}, u32[]{:S(2)}, u32[]{:S(2)}) collective-permute-start(bf16[2,320,256]{2,1,0:T(8,128)(2,1)S(1)} %pad_maximum_fusion.5.rest_0_), channel_id=1, source_target_pairs={{0,8},{4,12},{8,0},{12,4},{16,24},{20,28},{24,16},{28,20},{1,9},{5... | collective-permute-start | bytes 983048 | tf_op jit(solution)/shard_map/ppermute | solution.py:275
  7.6 2.6 %collective-permute-start.4 = (bf16[2,320,256]{2,1,0:T(8,128)(2,1)S(1)}, bf16[2,320,256]{2,1,0:T(8,128)(2,1)S(1)}, u32[]{:S(2)}, u32[]{:S(2)}) collective-permute-start(bf16[2,320,256]{2,1,0:T(8,128)(2,1)S(1)} %pad_maximum_fusion.5.rest_0_), channel_id=1, source_target_pairs={{0,16},{4,20},{8,24},{12,28},{16,0},{20,4},{24,8},{28,12},{1,17},{... | collective-permute-start | bytes 983048 | tf_op jit(solution)/shard_map/ppermute | solution.py:275
  10.2 12.5 %collective-permute-done.3.unread.rest_1_ = bf16[2,320,256]{2,1,0:T(8,128)(2,1)S(1)} collective-permute-done((bf16[2,320,256]{2,1,0:T(8,128)(2,1)S(1)}, bf16[2,320,256]{2,1,0:T(8,128)(2,1)S(1)}, u32[]{:S(2)}, u32[]{:S(2)}) %collective-permute-start.3) | collective-permute-done | bytes 327712 | tf_op jit(solution)/shard_map/ppermute | solution.py:275
  22.8 2.5 %collective-permute-done.4.first = bf16[2,320,256]{2,1,0:T(8,128)(2,1)S(1)} collective-permute-done((bf16[2,320,256]{2,1,0:T(8,128)(2,1)S(1)}, bf16[2,320,256]{2,1,0:T(8,128)(2,1)S(1)}, u32[]{:S(2)}, u32[]{:S(2)}) %collective-permute-start.4) | collective-permute-done | bytes 327712 | tf_op jit(solution)/shard_map/ppermute | solution.py:275
  25.3 0.9 relay.1
  26.2 0.4 collective-permute-start.5
  26.6 2.6 %collective-permute-start.9 = (bf16[2,320,256]{2,1,0:T(8,128)(2,1)}, bf16[2,320,256]{2,1,0:T(8,128)(2,1)}, u32[]{:S(2)}, u32[]{:S(2)}) collective-permute-start(bf16[2,320,256]{2,1,0:T(8,128)(2,1)} %get-tuple-element.42.rest_0_), channel_id=1, source_target_pairs={{0,16},{4,20},{8,24},{12,28},{16,0},{20,4},{24,8},{28,12},{1,17},{... | collective-permute-start | bytes 983048 | tf_op jit(solution)/shard_map/ppermute | solution.py:275
  29.2 0.1 stack.67.idx
  29.3 0.0 collective-permute-start.8
  29.3 1.7 %copy-done.1 = bf16[2,2,128,2560]{3,2,1,0:T(8,128)(2,1)S(1)} copy-done((bf16[2,2,128,2560]{3,2,1,0:T(8,128)(2,1)S(1)}, bf16[2,2,128,2560]{3,2,1,0:T(8,128)(2,1)}, u32[]{:S(2)}) %copy-start.1) | copy-done | bytes 2621464
  31.1 1.2 %copy-done.3 = bf16[2,2,8,128,128]{4,3,2,1,0:T(8,128)(2,1)S(1)} copy-done((bf16[2,2,8,128,128]{4,3,2,1,0:T(8,128)(2,1)S(1)}, bf16[2,2,8,128,128]{4,3,2,1,0:T(8,128)(2,1)}, u32[]{:S(2)}) %copy-start.3) | copy-done | bytes 1048600
  32.3 4.9 %value_ahead.1 = (f32[2,512,256]{2,1,0:T(8,128)S(1)}, bf16[2,512,640]{2,1,0:T(8,128)(2,1)S(1)}, bf16[2,4,4,128,128]{4,3,2,1,0:T(8,128)(2,1)S(1)}) custom-call(s32[5]{0:T(128)S(1)} %stack.67.idx, bf16[512,2560]{1,0:T(8,128)(2,1)S(1)} %bitcast.54, bf16[512,2560]{1,0:T(8,128)(2,1)} %collective-permute-done.1.x_s.right_s, bf16[4,8,128,128]{3,2,1,0:T(8,128)(2,1)S(1)} %bitcast.57, ...), custom_call_target="tpu_custom_call" | custom-call | flops 1342177280 | bytes 11272192 | tf_op jit(solution)/shard_map/value_ahead/pallas_call | solution.py:374
  37.2 6.7 %collective-permute-done.5.slot = bf16[2,320,256]{2,1,0:T(8,128)(2,1)} collective-permute-done((bf16[2,320,256]{2,1,0:T(8,128)(2,1)}, bf16[2,320,256]{2,1,0:T(8,128)(2,1)}, u32[]{:S(2)}, u32[]{:S(2)}) %collective-permute-start.5) | collective-permute-done | bytes 327712 | tf_op jit(solution)/shard_map/ppermute | solution.py:275
  43.8 2.5 %mixed.1 = (bf16[512,256]{1,0:T(8,128)(2,1)S(1)}, bf16[512,256]{1,0:T(8,128)(2,1)S(1)}) custom-call(s32[5]{0:T(128)S(1)} %stack.67.idx, f32[2,512,256]{2,1,0:T(8,128)S(1)} %get-tuple-element.36.part, bf16[2,512,640]{2,1,0:T(8,128)(2,1)S(1)} %get-tuple-element.37.last, bf16[2,4,4,128,128]{4,3,2,1,0:T(8,128)(2,1)S(1)} %get-tuple-element.38.weights, ...), custom_call_target="tpu_custom_call" | custom-call | flops 335544320 | bytes 3932160 | tf_op jit(solution)/shard_map/mixed/pallas_call | solution.py:387
  46.4 0.1 collective-permute-start.6
  46.5 0.1 collective-permute-start.10
  46.5 1.7 %collective-permute-done.8.rest_1_ = bf16[2,320,256]{2,1,0:T(8,128)(2,1)S(1)} collective-permute-done((bf16[2,320,256]{2,1,0:T(8,128)(2,1)}, bf16[2,320,256]{2,1,0:T(8,128)(2,1)S(1)}, u32[]{:S(2)}, u32[]{:S(2)}) %collective-permute-start.8) | collective-permute-done | bytes 327712 | tf_op jit(solution)/shard_map/ppermute | solution.py:275
  48.3 5.3 %grad_out.1 = (bf16[16,128]{1,0:T(8,128)(2,1)S(1)}, bf16[2,320,256]{2,1,0:T(8,128)(2,1)S(1)}, bf16[2,320,256]{2,1,0:T(8,128)(2,1)S(1)}, bf16[2,320,256]{2,1,0:T(8,128)(2,1)S(1)}, bf16[2,320,256]{2,1,0:T(8,128)(2,1)}) custom-call(s32[5]{0:T(128)S(1)} %stack.67.idx, bf16[512,2560]{1,0:T(8,128)(2,1)S(1)} %bitcast.51, ...), custom_call_target="tpu_custom_call" | custom-call | flops 1342177280 | bytes 7077888 | tf_op jit(solution)/shard_map/grad_out/pallas_call | solution.py:409
  53.6 0.0 copy-start.5
  53.6 0.7 copy-done.5
  54.3 0.7 copy-done.11
  55.0 1.7 %collective-permute-done.10.rest_3_ = bf16[2,320,256]{2,1,0:T(8,128)(2,1)S(1)} collective-permute-done((bf16[2,320,256]{2,1,0:T(8,128)(2,1)}, bf16[2,320,256]{2,1,0:T(8,128)(2,1)S(1)}, u32[]{:S(2)}, u32[]{:S(2)}) %collective-permute-start.10) | collective-permute-done | bytes 327712 | tf_op jit(solution)/shard_map/ppermute | solution.py:275
  56.8 6.4 %d_value.1 = (bf16[256,1024]{1,0:T(8,128)(2,1)S(1)}, bf16[2560,256]{1,0:T(8,128)(2,1)}) custom-call(s32[5]{0:T(128)S(1)} %stack.67.idx, bf16[16,128]{1,0:T(8,128)(2,1)S(1)} %get-tuple-element.43.token, bf16[512,2560]{1,0:T(8,128)(2,1)S(1)} %bitcast.52, bf16[512,2560]{1,0:T(8,128)(2,1)} %collective-permute-done.7.cot_s, ...), custom_call_target="tpu_custom_call" | custom-call | flops 1342177280 | bytes 9437184 | tf_op jit(solution)/shard_map/d_value/pallas_call | solution.py:419
  63.2 0.1 collective-permute-start.11
  63.2 0.3 collective-permute-start.16
  63.6 0.1 pad_add_fusion.idx
  63.6 1.8 %collective-permute-start.18 = (bf16[2,320,256]{2,1,0:T(8,128)(2,1)}, bf16[2,320,256]{2,1,0:T(8,128)(2,1)S(1)}, u32[]{:S(2)}, u32[]{:S(2)}) collective-permute-start(bf16[2,320,256]{2,1,0:T(8,128)(2,1)} %copy-done.11), channel_id=1, source_target_pairs={{0,8},{4,12},{8,0},{12,4},{16,24},{20,28},{24,16},{28,20},{1,9},{5... | collective-permute-start | bytes 983048 | tf_op jit(solution)/shard_map/ppermute | solution.py:275
  65.4 8.6 %collective-permute-done.16 = bf16[2,320,256]{2,1,0:T(8,128)(2,1)S(1)} collective-permute-done((bf16[2,320,256]{2,1,0:T(8,128)(2,1)}, bf16[2,320,256]{2,1,0:T(8,128)(2,1)S(1)}, u32[]{:S(2)}, u32[]{:S(2)}) %collective-permute-start.16) | collective-permute-done | bytes 327712 | tf_op jit(solution)/shard_map/ppermute | solution.py:275
  74.0 0.1 add_convert_fusion.unread
  74.1 0.9 collective-permute-start.19
  75.0 0.9 copy-done.8
  76.0 0.9 copy-done.10
  76.9 3.2 %terms.1 = (bf16[16,128]{1,0:T(8,128)(2,1)S(1)}, bf16[2,256,640]{2,1,0:T(8,128)(2,1)S(1)}, bf16[2,256,640]{2,1,0:T(8,128)(2,1)S(1)}, bf16[4,256,640]{2,1,0:T(8,128)(2,1)S(1)}) custom-call(s32[4]{0:T(128)S(1)} %pad_add_fusion.idx, bf16[512,256]{1,0:T(8,128)(2,1)S(1)} %copy-done.8, bf16[512,256]{1,0:T(8,128)(2,1)S(1)} %copy-done.10, ...), custom_call_target="tpu_custom_call" | custom-call | flops 1342177280 | bytes 5767168 | tf_op jit(solution)/shard_map/terms/pallas_call | solution.py:441
  80.1 1.6 %collective-permute-start.12 = (bf16[2,256,640]{2,1,0:T(8,128)(2,1)S(1)}, bf16[2,256,640]{2,1,0:T(8,128)(2,1)S(1)}, u32[]{:S(2)}, u32[]{:S(2)}) collective-permute-start(bf16[2,256,640]{2,1,0:T(8,128)(2,1)S(1)} %get-tuple-element.46), channel_id=1, source_target_pairs={{0,1},{1,0},{2,3},{3,2},{4,5},{5,4},{6,7},{7,6},{8,9},{9,8},{10,11... | collective-permute-start | bytes 1966088 | tf_op jit(solution)/shard_map/ppermute | solution.py:286
  81.7 1.5 %collective-permute-start.14 = (bf16[2,256,640]{2,1,0:T(8,128)(2,1)S(1)}, bf16[2,256,640]{2,1,0:T(8,128)(2,1)S(1)}, u32[]{:S(2)}, u32[]{:S(2)}) collective-permute-start(bf16[2,256,640]{2,1,0:T(8,128)(2,1)S(1)} %get-tuple-element.47), channel_id=1, source_target_pairs={{0,2},{1,3},{2,0},{3,1},{4,6},{5,7},{6,4},{7,5},{8,10},{9,11},{10,... | collective-permute-start | bytes 1966088 | tf_op jit(solution)/shard_map/ppermute | solution.py:286
  83.2 4.6 %grad_value.1 = (bf16[2,320,256]{2,1,0:T(8,128)(2,1)S(1)}, bf16[2,320,256]{2,1,0:T(8,128)(2,1)S(1)}, bf16[2,320,256]{2,1,0:T(8,128)(2,1)S(1)}, bf16[2,320,256]{2,1,0:T(8,128)(2,1)S(1)}) custom-call(s32[5]{0:T(128)S(1)} %stack.67.idx, bf16[16,128]{1,0:T(8,128)(2,1)S(1)} %get-tuple-element.48.token, bf16[2,320,256]{2,1,0:T(8,128)(2,1)S(1)} %add_convert_fusion.unread, ...), custom_call_target="tpu_custom_call" | custom-call | flops 1342177280 | bytes 7077888 | tf_op jit(solution)/shard_map/grad_value/pallas_call | solution.py:450
  87.8 1.8 %collective-permute-start.17 = (bf16[2,320,256]{2,1,0:T(8,128)(2,1)S(1)}, bf16[2,320,256]{2,1,0:T(8,128)(2,1)S(1)}, u32[]{:S(2)}, u32[]{:S(2)}) collective-permute-start(bf16[2,320,256]{2,1,0:T(8,128)(2,1)S(1)} %get-tuple-element.54), channel_id=1, source_target_pairs={{0,8},{4,12},{8,0},{12,4},{16,24},{20,28},{24,16},{28,20},{1,9},{5... | collective-permute-start | bytes 983048 | tf_op jit(solution)/shard_map/ppermute | solution.py:275
  89.7 0.2 convert_element_type.50
  89.8 1.2 %collective-permute-done.19.far = bf16[2,320,256]{2,1,0:T(8,128)(2,1)S(1)} collective-permute-done((bf16[2,320,256]{2,1,0:T(8,128)(2,1)S(1)}, bf16[2,320,256]{2,1,0:T(8,128)(2,1)S(1)}, u32[]{:S(2)}, u32[]{:S(2)}) %collective-permute-start.19) | collective-permute-done | bytes 327712 | tf_op jit(solution)/shard_map/ppermute | solution.py:275
  91.1 6.9 %collective-permute-done.17.got = bf16[2,320,256]{2,1,0:T(8,128)(2,1)S(1)} collective-permute-done((bf16[2,320,256]{2,1,0:T(8,128)(2,1)S(1)}, bf16[2,320,256]{2,1,0:T(8,128)(2,1)S(1)}, u32[]{:S(2)}, u32[]{:S(2)}) %collective-permute-start.17) | collective-permute-done | bytes 327712 | tf_op jit(solution)/shard_map/ppermute | solution.py:275
  98.0 0.2 sum.1
  98.2 0.1 collective-permute-start.20
  98.3 2.6 %collective-permute-start.21 = (bf16[2,320,256]{2,1,0:T(8,128)(2,1)S(1)}, bf16[2,320,256]{2,1,0:T(8,128)(2,1)S(1)}, u32[]{:S(2)}, u32[]{:S(2)}) collective-permute-start(bf16[2,320,256]{2,1,0:T(8,128)(2,1)S(1)} %get-tuple-element.59), channel_id=1, source_target_pairs={{0,16},{4,20},{8,24},{12,28},{16,0},{20,4},{24,8},{28,12},{1,17},{... | collective-permute-start | bytes 983048 | tf_op jit(solution)/shard_map/ppermute | solution.py:275
  100.9 0.1 collective-permute-start.23
  101.0 0.1 convert_element_type.51
  101.1 0.1 convert_element_type.55
  101.2 0.1 fusion.8
  101.4 1.6 %collective-permute-start.13 = (bf16[256,640]{1,0:T(8,128)(2,1)S(1)}, bf16[256,640]{1,0:T(8,128)(2,1)S(1)}, u32[]{:S(2)}, u32[]{:S(2)}) collective-permute-start(bf16[256,640]{1,0:T(8,128)(2,1)S(1)} %get-tuple-element.63), channel_id=1, source_target_pairs={{0,2},{1,3},{2,0},{3,1},{4,6},{5,7},{6,4},{7,5},{8,10},{9,11},{10,... | collective-permute-start | bytes 983048 | tf_op jit(solution)/shard_map/ppermute | solution.py:286
  102.9 0.6 collective-permute-start.15
  103.5 10.6 %collective-permute-done.20 = bf16[2,320,256]{2,1,0:T(8,128)(2,1)S(1)} collective-permute-done((bf16[2,320,256]{2,1,0:T(8,128)(2,1)S(1)}, bf16[2,320,256]{2,1,0:T(8,128)(2,1)S(1)}, u32[]{:S(2)}, u32[]{:S(2)}) %collective-permute-start.20) | collective-permute-done | bytes 327712 | tf_op jit(solution)/shard_map/ppermute | solution.py:275
  114.1 1.4 %collective-permute-done.21 = bf16[2,320,256]{2,1,0:T(8,128)(2,1)S(1)} collective-permute-done((bf16[2,320,256]{2,1,0:T(8,128)(2,1)S(1)}, bf16[2,320,256]{2,1,0:T(8,128)(2,1)S(1)}, u32[]{:S(2)}, u32[]{:S(2)}) %collective-permute-start.21) | collective-permute-done | bytes 327712 | tf_op jit(solution)/shard_map/ppermute | solution.py:275
  115.5 0.1 convert_add_fusion
  115.7 0.1 collective-permute-start.22
  115.8 0.9 pad_maximum_fusion.2
  116.7 0.2 fusion.7
  117.0 0.9 pad_maximum_fusion
  117.9 0.9 pad_maximum_fusion.1
  (38 shorter events, 0.3 us)
Async XLA Ops:
  0.6 3.6 %copy-start = (bf16[2,2,128,2560]{3,2,1,0:T(8,128)(2,1)S(1)}, bf16[2,2,128,2560]{3,2,1,0:T(8,128)(2,1)}, u32[]{:S(2)}) copy-start(bf16[2,2,128,2560]{3,2,1,0:T(8,128)(2,1)} %param.7) | copy-start | bytes 7864324
  2.1 1.8 %collective-permute-start = (bf16[2,320,256]{2,1,0:T(8,128)(2,1)S(1)}, bf16[2,320,256]{2,1,0:T(8,128)(2,1)S(1)}, u32[]{:S(2)}, u32[]{:S(2)}) collective-permute-start(bf16[2,320,256]{2,1,0:T(8,128)(2,1)S(1)} %get-tuple-element.70), channel_id=1, source_target_pairs={{0,4},{4,0},{8,12},{12,8},{16,20},{20,16},{24,28},{28,24},{1,5},{5... | collective-permute-start | bytes 983048 | tf_op jit(solution)/shard_map/ppermute | solution.py:283
  3.8 25.5 %collective-permute-start.1 = (bf16[512,2560]{1,0:T(8,128)(2,1)}, bf16[512,2560]{1,0:T(8,128)(2,1)}, u32[]{:S(2)}, u32[]{:S(2)}) collective-permute-start(bf16[512,2560]{1,0:T(8,128)(2,1)} %bitcast.53), channel_id=1, source_target_pairs={{0,4},{4,0},{8,12},{12,8},{16,20},{20,16},{24,28},{28,24},{1,5},{5... | collective-permute-start | bytes 7864328 | tf_op jit(solution)/shard_map/ppermute | solution.py:283
  4.2 44.0 %collective-permute-start.7 = (bf16[512,2560]{1,0:T(8,128)(2,1)S(1)}, bf16[512,2560]{1,0:T(8,128)(2,1)}, u32[]{:S(2)}, u32[]{:S(2)}) collective-permute-start(bf16[512,2560]{1,0:T(8,128)(2,1)S(1)} %bitcast.50), channel_id=1, source_target_pairs={{0,4},{4,0},{8,12},{12,8},{16,20},{20,16},{24,28},{28,24},{1,5},{5... | collective-permute-start | bytes 7864328 | tf_op jit(solution)/shard_map/ppermute | solution.py:283
  4.4 24.9 %collective-permute-start.2 = (bf16[4,8,128,128]{3,2,1,0:T(8,128)(2,1)}, bf16[4,8,128,128]{3,2,1,0:T(8,128)(2,1)}, u32[]{:S(2)}, u32[]{:S(2)}) collective-permute-start(bf16[4,8,128,128]{3,2,1,0:T(8,128)(2,1)} %bitcast.56), channel_id=1, source_target_pairs={{0,4},{4,0},{8,12},{12,8},{16,20},{20,16},{24,28},{28,24},{1,5},{5... | collective-permute-start | bytes 3145736 | tf_op jit(solution)/shard_map/ppermute | solution.py:283
  4.8 17.9 %collective-permute-start.3 = (bf16[2,320,256]{2,1,0:T(8,128)(2,1)S(1)}, bf16[2,320,256]{2,1,0:T(8,128)(2,1)S(1)}, u32[]{:S(2)}, u32[]{:S(2)}) collective-permute-start(bf16[2,320,256]{2,1,0:T(8,128)(2,1)S(1)} %pad_maximum_fusion.5.rest_0_), channel_id=1, source_target_pairs={{0,8},{4,12},{8,0},{12,4},{16,24},{20,28},{24,16},{28,20},{1,9},{5... | collective-permute-start | bytes 983048 | tf_op jit(solution)/shard_map/ppermute | solution.py:275
  7.6 17.7 %collective-permute-start.4 = (bf16[2,320,256]{2,1,0:T(8,128)(2,1)S(1)}, bf16[2,320,256]{2,1,0:T(8,128)(2,1)S(1)}, u32[]{:S(2)}, u32[]{:S(2)}) collective-permute-start(bf16[2,320,256]{2,1,0:T(8,128)(2,1)S(1)} %pad_maximum_fusion.5.rest_0_), channel_id=1, source_target_pairs={{0,16},{4,20},{8,24},{12,28},{16,0},{20,4},{24,8},{28,12},{1,17},{... | collective-permute-start | bytes 983048 | tf_op jit(solution)/shard_map/ppermute | solution.py:275
  26.2 17.7 %collective-permute-start.5 = (bf16[2,320,256]{2,1,0:T(8,128)(2,1)}, bf16[2,320,256]{2,1,0:T(8,128)(2,1)}, u32[]{:S(2)}, u32[]{:S(2)}) collective-permute-start(bf16[2,320,256]{2,1,0:T(8,128)(2,1)} %get-tuple-element.35.rest_2_), channel_id=1, source_target_pairs={{0,8},{4,12},{8,0},{12,4},{16,24},{20,28},{24,16},{28,20},{1,9},{5... | collective-permute-start | bytes 983048 | tf_op jit(solution)/shard_map/ppermute | solution.py:275
  26.6 19.8 %collective-permute-start.9 = (bf16[2,320,256]{2,1,0:T(8,128)(2,1)}, bf16[2,320,256]{2,1,0:T(8,128)(2,1)}, u32[]{:S(2)}, u32[]{:S(2)}) collective-permute-start(bf16[2,320,256]{2,1,0:T(8,128)(2,1)} %get-tuple-element.42.rest_0_), channel_id=1, source_target_pairs={{0,16},{4,20},{8,24},{12,28},{16,0},{20,4},{24,8},{28,12},{1,17},{... | collective-permute-start | bytes 983048 | tf_op jit(solution)/shard_map/ppermute | solution.py:275
  29.3 19.0 %collective-permute-start.8 = (bf16[2,320,256]{2,1,0:T(8,128)(2,1)}, bf16[2,320,256]{2,1,0:T(8,128)(2,1)S(1)}, u32[]{:S(2)}, u32[]{:S(2)}) collective-permute-start(bf16[2,320,256]{2,1,0:T(8,128)(2,1)} %get-tuple-element.42.rest_0_), channel_id=1, source_target_pairs={{0,8},{4,12},{8,0},{12,4},{16,24},{20,28},{24,16},{28,20},{1,9},{5... | collective-permute-start | bytes 983048 | tf_op jit(solution)/shard_map/ppermute | solution.py:275
  29.3 1.7 %copy-start.1 = (bf16[2,2,128,2560]{3,2,1,0:T(8,128)(2,1)S(1)}, bf16[2,2,128,2560]{3,2,1,0:T(8,128)(2,1)}, u32[]{:S(2)}) copy-start(bf16[2,2,128,2560]{3,2,1,0:T(8,128)(2,1)} %param.5) | copy-start | bytes 7864324
  31.1 1.2 %copy-start.3 = (bf16[2,2,8,128,128]{4,3,2,1,0:T(8,128)(2,1)S(1)}, bf16[2,2,8,128,128]{4,3,2,1,0:T(8,128)(2,1)}, u32[]{:S(2)}) copy-start(bf16[2,2,8,128,128]{4,3,2,1,0:T(8,128)(2,1)} %param.6) | copy-start | bytes 3145732
  46.4 7.2 %copy-start.7 = (bf16[512,256]{1,0:T(8,128)(2,1)}, bf16[512,256]{1,0:T(8,128)(2,1)S(1)}, u32[]{:S(2)}) copy-start(bf16[512,256]{1,0:T(8,128)(2,1)S(1)} %get-tuple-element.39.mixed_o) | copy-start | bytes 786436
  46.4 1.9 %collective-permute-start.6 = (bf16[512,256]{1,0:T(8,128)(2,1)S(1)}, bf16[512,256]{1,0:T(8,128)(2,1)S(1)}, u32[]{:S(2)}, u32[]{:S(2)}) collective-permute-start(bf16[512,256]{1,0:T(8,128)(2,1)S(1)} %get-tuple-element.40.mixed_s), channel_id=1, source_target_pairs={{0,4},{4,0},{8,12},{12,8},{16,20},{20,16},{24,28},{28,24},{1,5},{5... | collective-permute-start | bytes 786440 | tf_op jit(solution)/shard_map/ppermute | solution.py:283
  46.5 10.3 %collective-permute-start.10 = (bf16[2,320,256]{2,1,0:T(8,128)(2,1)}, bf16[2,320,256]{2,1,0:T(8,128)(2,1)S(1)}, u32[]{:S(2)}, u32[]{:S(2)}) collective-permute-start(bf16[2,320,256]{2,1,0:T(8,128)(2,1)} %collective-permute-done.9.rest_2_), channel_id=1, source_target_pairs={{0,8},{4,12},{8,0},{12,4},{16,24},{20,28},{24,16},{28,20},{1,9},{5... | collective-permute-start | bytes 983048 | tf_op jit(solution)/shard_map/ppermute | solution.py:275
  48.2 5.3 %copy-start.9 = (bf16[512,256]{1,0:T(8,128)(2,1)}, bf16[512,256]{1,0:T(8,128)(2,1)S(1)}, u32[]{:S(2)}) copy-start(bf16[512,256]{1,0:T(8,128)(2,1)S(1)} %collective-permute-done.6.rest_0_.mixed_r) | copy-start | bytes 786436
  48.2 8.5 %copy-start.4 = (bf16[2,2,8,128,128]{4,3,2,1,0:T(8,128)(2,1)S(1)}, bf16[2,2,8,128,128]{4,3,2,1,0:T(8,128)(2,1)}, u32[]{:S(2)}) copy-start(bf16[2,2,8,128,128]{4,3,2,1,0:T(8,128)(2,1)} %param.6) | copy-start | bytes 3145732
  53.6 0.7 copy-start.5
  54.3 0.7 copy-start.11
  63.2 11.9 %collective-permute-start.11 = (bf16[2560,256]{1,0:T(8,128)(2,1)}, bf16[2560,256]{1,0:T(8,128)(2,1)S(1)}, u32[]{:S(2)}, u32[]{:S(2)}) collective-permute-start(bf16[2560,256]{1,0:T(8,128)(2,1)} %get-tuple-element.44.w_o), channel_id=1, source_target_pairs={{0,4},{4,0},{8,12},{12,8},{16,20},{20,16},{24,28},{28,24},{1,5},{5... | collective-permute-start | bytes 3932168 | tf_op jit(solution)/shard_map/ppermute | solution.py:283
  63.2 10.8 %collective-permute-start.16 = (bf16[2,320,256]{2,1,0:T(8,128)(2,1)}, bf16[2,320,256]{2,1,0:T(8,128)(2,1)S(1)}, u32[]{:S(2)}, u32[]{:S(2)}) collective-permute-start(bf16[2,320,256]{2,1,0:T(8,128)(2,1)} %get-tuple-element.50), channel_id=1, source_target_pairs={{0,8},{4,12},{8,0},{12,4},{16,24},{20,28},{24,16},{28,20},{1,9},{5... | collective-permute-start | bytes 983048 | tf_op jit(solution)/shard_map/ppermute | solution.py:275
  63.6 26.2 %collective-permute-start.18 = (bf16[2,320,256]{2,1,0:T(8,128)(2,1)}, bf16[2,320,256]{2,1,0:T(8,128)(2,1)S(1)}, u32[]{:S(2)}, u32[]{:S(2)}) collective-permute-start(bf16[2,320,256]{2,1,0:T(8,128)(2,1)} %copy-done.11), channel_id=1, source_target_pairs={{0,8},{4,12},{8,0},{12,4},{16,24},{20,28},{24,16},{28,20},{1,9},{5... | collective-permute-start | bytes 983048 | tf_op jit(solution)/shard_map/ppermute | solution.py:275
  74.1 9.1 %copy-start.2 = (bf16[2,2,128,2560]{3,2,1,0:T(8,128)(2,1)S(1)}, bf16[2,2,128,2560]{3,2,1,0:T(8,128)(2,1)}, u32[]{:S(2)}) copy-start(bf16[2,2,128,2560]{3,2,1,0:T(8,128)(2,1)} %param.5) | copy-start | bytes 7864324
  74.1 17.0 %collective-permute-start.19 = (bf16[2,320,256]{2,1,0:T(8,128)(2,1)S(1)}, bf16[2,320,256]{2,1,0:T(8,128)(2,1)S(1)}, u32[]{:S(2)}, u32[]{:S(2)}) collective-permute-start(bf16[2,320,256]{2,1,0:T(8,128)(2,1)S(1)} %add_convert_fusion.unread), channel_id=1, source_target_pairs={{0,16},{4,20},{8,24},{12,28},{16,0},{20,4},{24,8},{28,12},{1,17},{... | collective-permute-start | bytes 983048 | tf_op jit(solution)/shard_map/ppermute | solution.py:275
  75.0 1.0 copy-start.8
  76.0 0.9 copy-start.10
  80.1 20.9 %collective-permute-start.12 = (bf16[2,256,640]{2,1,0:T(8,128)(2,1)S(1)}, bf16[2,256,640]{2,1,0:T(8,128)(2,1)S(1)}, u32[]{:S(2)}, u32[]{:S(2)}) collective-permute-start(bf16[2,256,640]{2,1,0:T(8,128)(2,1)S(1)} %get-tuple-element.46), channel_id=1, source_target_pairs={{0,1},{1,0},{2,3},{3,2},{4,5},{5,4},{6,7},{7,6},{8,9},{9,8},{10,11... | collective-permute-start | bytes 1966088 | tf_op jit(solution)/shard_map/ppermute | solution.py:286
  81.7 19.4 %collective-permute-start.14 = (bf16[2,256,640]{2,1,0:T(8,128)(2,1)S(1)}, bf16[2,256,640]{2,1,0:T(8,128)(2,1)S(1)}, u32[]{:S(2)}, u32[]{:S(2)}) collective-permute-start(bf16[2,256,640]{2,1,0:T(8,128)(2,1)S(1)} %get-tuple-element.47), channel_id=1, source_target_pairs={{0,2},{1,3},{2,0},{3,1},{4,6},{5,7},{6,4},{7,5},{8,10},{9,11},{10,... | collective-permute-start | bytes 1966088 | tf_op jit(solution)/shard_map/ppermute | solution.py:286
  87.8 10.2 %collective-permute-start.17 = (bf16[2,320,256]{2,1,0:T(8,128)(2,1)S(1)}, bf16[2,320,256]{2,1,0:T(8,128)(2,1)S(1)}, u32[]{:S(2)}, u32[]{:S(2)}) collective-permute-start(bf16[2,320,256]{2,1,0:T(8,128)(2,1)S(1)} %get-tuple-element.54), channel_id=1, source_target_pairs={{0,8},{4,12},{8,0},{12,4},{16,24},{20,28},{24,16},{28,20},{1,9},{5... | collective-permute-start | bytes 983048 | tf_op jit(solution)/shard_map/ppermute | solution.py:275
  89.7 8.4 %copy-start.6 = (bf16[2,320,256]{2,1,0:T(8,128)(2,1)S(1)}, bf16[2,320,256]{2,1,0:T(8,128)(2,1)}, u32[]{:S(2)}) copy-start(bf16[2,320,256]{2,1,0:T(8,128)(2,1)} %copy-done.5) | copy-start | bytes 983044
  98.2 15.9 %collective-permute-start.20 = (bf16[2,320,256]{2,1,0:T(8,128)(2,1)S(1)}, bf16[2,320,256]{2,1,0:T(8,128)(2,1)S(1)}, u32[]{:S(2)}, u32[]{:S(2)}) collective-permute-start(bf16[2,320,256]{2,1,0:T(8,128)(2,1)S(1)} %get-tuple-element.58), channel_id=1, source_target_pairs={{0,8},{4,12},{8,0},{12,4},{16,24},{20,28},{24,16},{28,20},{1,9},{5... | collective-permute-start | bytes 983048 | tf_op jit(solution)/shard_map/ppermute | solution.py:275
  98.3 17.2 %collective-permute-start.21 = (bf16[2,320,256]{2,1,0:T(8,128)(2,1)S(1)}, bf16[2,320,256]{2,1,0:T(8,128)(2,1)S(1)}, u32[]{:S(2)}, u32[]{:S(2)}) collective-permute-start(bf16[2,320,256]{2,1,0:T(8,128)(2,1)S(1)} %get-tuple-element.59), channel_id=1, source_target_pairs={{0,16},{4,20},{8,24},{12,28},{16,0},{20,4},{24,8},{28,12},{1,17},{... | collective-permute-start | bytes 983048 | tf_op jit(solution)/shard_map/ppermute | solution.py:275
  100.9 14.8 %collective-permute-start.23 = (f32[320,256]{1,0:T(8,128)S(1)}, f32[320,256]{1,0:T(8,128)S(1)}, u32[]{:S(2)}, u32[]{:S(2)}) collective-permute-start(f32[320,256]{1,0:T(8,128)S(1)} %slice_bitcast_fusion.2), channel_id=1, source_target_pairs={{0,4},{4,0},{8,12},{12,8},{16,20},{20,16},{24,28},{28,24},{1,5},{5... | collective-permute-start | bytes 983048 | tf_op jit(solution)/shard_map/ppermute | solution.py:283
  101.4 15.4 %collective-permute-start.13 = (bf16[256,640]{1,0:T(8,128)(2,1)S(1)}, bf16[256,640]{1,0:T(8,128)(2,1)S(1)}, u32[]{:S(2)}, u32[]{:S(2)}) collective-permute-start(bf16[256,640]{1,0:T(8,128)(2,1)S(1)} %get-tuple-element.63), channel_id=1, source_target_pairs={{0,2},{1,3},{2,0},{3,1},{4,6},{5,7},{6,4},{7,5},{8,10},{9,11},{10,... | collective-permute-start | bytes 983048 | tf_op jit(solution)/shard_map/ppermute | solution.py:286
  102.9 13.8 %collective-permute-start.15 = (bf16[256,640]{1,0:T(8,128)(2,1)S(1)}, bf16[256,640]{1,0:T(8,128)(2,1)S(1)}, u32[]{:S(2)}, u32[]{:S(2)}) collective-permute-start(bf16[256,640]{1,0:T(8,128)(2,1)S(1)} %get-tuple-element.64), channel_id=1, source_target_pairs={{0,1},{1,0},{2,3},{3,2},{4,5},{5,4},{6,7},{7,6},{8,9},{9,8},{10,11... | collective-permute-start | bytes 983048 | tf_op jit(solution)/shard_map/ppermute | solution.py:286
  115.7 2.2 %collective-permute-start.22 = (f32[320,256]{1,0:T(8,128)S(1)}, f32[320,256]{1,0:T(8,128)S(1)}, u32[]{:S(2)}, u32[]{:S(2)}) collective-permute-start(f32[320,256]{1,0:T(8,128)S(1)} %slice_bitcast_fusion), channel_id=1, source_target_pairs={{0,4},{4,0},{8,12},{12,8},{16,20},{20,16},{24,28},{28,24},{1,5},{5... | collective-permute-start | bytes 983048 | tf_op jit(solution)/shard_map/ppermute | solution.py:283

commit v16 on v15

--- a/solution.py
+++ b/solution.py
@@ -138,6 +138,14 @@
     for half, out in enumerate((mixed_o, mixed_s)):
         value = (part[half] + dot(last[half], w_last)).astype(BF16)
         mix_values(value, weights.at[half], out)
+
+
+def assemble_kernel(n_slots, idx, unread, unread_too, *rest):
+    del unread, unread_too
+    slots, (w_out, slots_v, sems) = rest[:n_slots], rest[n_slots:]
+    for copy in begin_slots(slots, slots_v, sems):
+        copy.wait()
+    place(idx, idx[0], slots_v, w_out)
 
 
 def d_value_kernel(n_slots, idx, token, cot_o, cot_s, mix_o, mix_s, *rest):
@@ -416,22 +424,31 @@
             2 * (2 * cot.size + 2 * tokens * cols + width * cols),
         )(idx, cot, cot_s, mixed_o, mixed_s, *unread)
         out_passed = swap(out_sends[3], 1) if line4 else token
-        left, w_full = call(
+        left = call(
             functools.partial(d_value_kernel, n_slots),
             "d_value",
             [SMEM] + [ANY] * (5 + n_slots),
-            [(cols, 2 * tokens), (width, cols)],
-            [halves, mix_scratch, pltpu.SemaphoreType.DMA((4,)), *slots_scratch],
+            [(cols, 2 * tokens)],
+            [rows, halves, mix_scratch, pltpu.SemaphoreType.DMA((4,)), *slots_scratch],
             flops,
-            2 * (2 * cot.size + mix.size + 2 * width * cols + 2 * tokens * cols),
-        )(idx, token, cot, cot_s, mix, mix_s, *out_slots)
-        w_full_s = sibling(w_full)
+            2 * (2 * cot.size + mix.size + width * cols + 2 * tokens * cols),
+        )(idx, token, cot, cot_s, mix, mix_s, *out_slots)[0]
         if line4:
             out_onward = added(out_sends[2], out_passed)
             out_far = swap(out_onward, 2)
             out_near = swap(out_sends[1], 1)
         else:
             out_onward = left
+        w_full = call(
+            functools.partial(assemble_kernel, n_slots),
+            "assemble",
+            [SMEM] + [ANY] * (2 + n_slots),
+            [(width, cols)],
+            slots_scratch,
+            0,
+            4 * width * cols,
+        )(idx, out_onward, left, *out_slots)[0]
+        w_full_s = sibling(w_full)
         part = width // n_node
         half = tokens // 2
         if n_node == 4:

time: 119 us -> 116 us (0.975)
  waiting for transfers between devices: 55.2 us -> 48.3 us
  starting transfers between devices: 22.9 us -> 24.4 us
    ppermute x12, waiting for transfers between devices: 53.9 us -> 46.4 us  [move(): lax.ppermute(x, 'wide', [(2 * s + c, 2 * d + c) for s, d in pairs for c i...]
    pallas_call x0 -> x1, Pallas kernels: none -> 2.15 us  [body(): call(functools.partial(assemble_kernel, n_slots), 'assemble', [SMEM] + [A...]
    ppermute x12, starting transfers between devices: 16 us -> 17.9 us  [move(): lax.ppermute(x, 'wide', [(2 * s + c, 2 * d + c) for s, d in pairs for c i...]
    unnamed x24 -> x30, local copies, waits for them, and re-layouts: 6.35 us -> 7.26 us
  transfers between devices with their start and end apart: 24 -> 24, of which waited for: 11 -> 12; matrix products, arithmetic and copies ran while one was open for 3% -> 3% of each run, Pallas kernels for 18% -> 23%
where the time goes in v16:
time: 116 us; the launch traced here: 115 us
  waiting for transfers between devices  48.3 us (42%)
  Pallas kernels  28.7 us (25%)
  starting transfers between devices  24.4 us (21%)
  local copies, waits for them, and re-layouts  8.78 us (8%)
  other arithmetic  3.96 us (3%)
    ppermute x12, waiting for transfers between devices, move(): lax.ppermute(x, 'wide', [(2 * s + c, 2 * d + c) for s, d in pairs for c i...  46.4 us
    ppermute x12, starting transfers between devices, move(): lax.ppermute(x, 'wide', [(2 * s + c, 2 * d + c) for s, d in pairs for c i...  17.9 us
    unnamed x30, local copies, waits for them, and re-layouts  7.26 us
    pallas_call x1, Pallas kernels, body(): call(functools.partial(d_value_kernel, n_slots), 'd_value', [SMEM] + [ANY...  5.24 us
    pallas_call x1, Pallas kernels, body(): call(functools.partial(part_kernel, n_slots - 1), 'value_ahead', [SMEM] +...  4.9 us
    ppermute x4, starting transfers between devices, flip(): return lax.ppermute(x, 'node', [(i, i ^ j) for i in range(n_node)])  4.8 us
    pallas_call x1, Pallas kernels, body(): call(gradient_kernel, 'grad_value', [SMEM] + [ANY] * 4 + [VMEM], send_sha...  4.63 us
    pallas_call x1, Pallas kernels, body(): call(functools.partial(grad_out_kernel, len(unread)), 'grad_out', [SMEM]...  4.57 us
  transfers between devices with their start and end apart: 24, of which 12 were waited for; matrix products, arithmetic and copies ran while one was open for 3% of the time, Pallas kernels for 23%

profile of v16, /device:TPU:0, one launch (start us, length us, event | category | flops | bytes accessed | tf_op | source)
XLA Modules:
  0.0 115.1 jit_solution(8834323238635670835)
XLA Ops:
  0.7 1.3 %slice_bitcast_fusion.5 = (bf16[1,320,256]{2,1,0:T(8,128)(2,1)S(1)}, bf16[1,320,256]{2,1,0:T(8,128)(2,1)S(1)}, bf16[1,320,256]{2,1,0:T(8,128)(2,1)S(1)}, bf16[1,320,256]{2,1,0:T(8,128)(2,1)S(1)}) fusion(bf16[320,512]{1,0:T(8,128)(2,1)} %param.8, bf16[320,512]{1,0:T(8,128)(2,1)} %param.9), kind=kLoop, calls=%fused_computation.34 | loop fusion | bytes 1310720 | tf_op jit(solution)/shard_map/stack | solution.py:299
  2.1 0.5 collective-permute-start
  2.6 1.3 %collective-permute-done = bf16[2,320,256]{2,1,0:T(8,128)(2,1)S(1)} collective-permute-done((bf16[2,320,256]{2,1,0:T(8,128)(2,1)S(1)}, bf16[2,320,256]{2,1,0:T(8,128)(2,1)S(1)}, u32[]{:S(2)}, u32[]{:S(2)}) %collective-permute-start) | collective-permute-done | bytes 327712 | tf_op jit(solution)/shard_map/ppermute | solution.py:291
  3.8 0.4 collective-permute-start.1
  4.2 0.1 collective-permute-start.7
  4.4 0.4 collective-permute-start.2
  4.8 2.8 %collective-permute-start.3 = (bf16[2,320,256]{2,1,0:T(8,128)(2,1)S(1)}, bf16[2,320,256]{2,1,0:T(8,128)(2,1)S(1)}, u32[]{:S(2)}, u32[]{:S(2)}) collective-permute-start(bf16[2,320,256]{2,1,0:T(8,128)(2,1)S(1)} %pad_maximum_fusion.5.rest_0_), channel_id=1, source_target_pairs={{0,8},{4,12},{8,0},{12,4},{16,24},{20,28},{24,16},{28,20},{1,9},{5... | collective-permute-start | bytes 983048 | tf_op jit(solution)/shard_map/ppermute | solution.py:283
  7.6 2.6 %collective-permute-start.4 = (bf16[2,320,256]{2,1,0:T(8,128)(2,1)S(1)}, bf16[2,320,256]{2,1,0:T(8,128)(2,1)S(1)}, u32[]{:S(2)}, u32[]{:S(2)}) collective-permute-start(bf16[2,320,256]{2,1,0:T(8,128)(2,1)S(1)} %pad_maximum_fusion.5.rest_0_), channel_id=1, source_target_pairs={{0,16},{4,20},{8,24},{12,28},{16,0},{20,4},{24,8},{28,12},{1,17},{... | collective-permute-start | bytes 983048 | tf_op jit(solution)/shard_map/ppermute | solution.py:283
  10.2 12.5 %collective-permute-done.3.unread.rest_1_ = bf16[2,320,256]{2,1,0:T(8,128)(2,1)S(1)} collective-permute-done((bf16[2,320,256]{2,1,0:T(8,128)(2,1)S(1)}, bf16[2,320,256]{2,1,0:T(8,128)(2,1)S(1)}, u32[]{:S(2)}, u32[]{:S(2)}) %collective-permute-start.3) | collective-permute-done | bytes 327712 | tf_op jit(solution)/shard_map/ppermute | solution.py:283
  22.8 2.5 %collective-permute-done.4.first = bf16[2,320,256]{2,1,0:T(8,128)(2,1)S(1)} collective-permute-done((bf16[2,320,256]{2,1,0:T(8,128)(2,1)S(1)}, bf16[2,320,256]{2,1,0:T(8,128)(2,1)S(1)}, u32[]{:S(2)}, u32[]{:S(2)}) %collective-permute-start.4) | collective-permute-done | bytes 327712 | tf_op jit(solution)/shard_map/ppermute | solution.py:283
  25.3 0.8 relay.1
  26.1 0.7 copy-done.6
  26.8 0.4 collective-permute-start.5
  27.2 0.1 stack.67.idx
  27.3 1.6 %collective-permute-start.8 = (bf16[2,320,256]{2,1,0:T(8,128)(2,1)S(1)}, bf16[2,320,256]{2,1,0:T(8,128)(2,1)S(1)}, u32[]{:S(2)}, u32[]{:S(2)}) collective-permute-start(bf16[2,320,256]{2,1,0:T(8,128)(2,1)S(1)} %get-tuple-element.40.rest_0_), channel_id=1, source_target_pairs={{0,8},{4,12},{8,0},{12,4},{16,24},{20,28},{24,16},{28,20},{1,9},{5... | collective-permute-start | bytes 983048 | tf_op jit(solution)/shard_map/ppermute | solution.py:283
  28.9 1.1 collective-permute-start.9
  30.0 1.2 %copy-done.2 = bf16[2,2,8,128,128]{4,3,2,1,0:T(8,128)(2,1)S(1)} copy-done((bf16[2,2,8,128,128]{4,3,2,1,0:T(8,128)(2,1)S(1)}, bf16[2,2,8,128,128]{4,3,2,1,0:T(8,128)(2,1)}, u32[]{:S(2)}) %copy-start.2) | copy-done | bytes 1048600
  31.2 1.0 copy-done.7
  32.2 4.9 %value_ahead.1 = (f32[2,512,256]{2,1,0:T(8,128)S(1)}, bf16[2,512,640]{2,1,0:T(8,128)(2,1)S(1)}, bf16[2,4,4,128,128]{4,3,2,1,0:T(8,128)(2,1)S(1)}) custom-call(s32[5]{0:T(128)S(1)} %stack.67.idx, bf16[512,2560]{1,0:T(8,128)(2,1)S(1)} %bitcast.51, bf16[512,2560]{1,0:T(8,128)(2,1)} %collective-permute-done.1.x_s.right_s, bf16[4,8,128,128]{3,2,1,0:T(8,128)(2,1)S(1)} %bitcast.57, ...), custom_call_target="tpu_custom_call" | custom-call | flops 1342177280 | bytes 11272192 | tf_op jit(solution)/shard_map/value_ahead/pallas_call | solution.py:382
  37.1 7.3 %collective-permute-done.5.slot = bf16[2,320,256]{2,1,0:T(8,128)(2,1)} collective-permute-done((bf16[2,320,256]{2,1,0:T(8,128)(2,1)}, bf16[2,320,256]{2,1,0:T(8,128)(2,1)}, u32[]{:S(2)}, u32[]{:S(2)}) %collective-permute-start.5) | collective-permute-done | bytes 327712 | tf_op jit(solution)/shard_map/ppermute | solution.py:283
  44.4 2.7 %mixed.1 = (bf16[512,256]{1,0:T(8,128)(2,1)S(1)}, bf16[512,256]{1,0:T(8,128)(2,1)S(1)}) custom-call(s32[5]{0:T(128)S(1)} %stack.67.idx, f32[2,512,256]{2,1,0:T(8,128)S(1)} %get-tuple-element.34.part, bf16[2,512,640]{2,1,0:T(8,128)(2,1)S(1)} %get-tuple-element.35.last, bf16[2,4,4,128,128]{4,3,2,1,0:T(8,128)(2,1)S(1)} %get-tuple-element.36.weights, ...), custom_call_target="tpu_custom_call" | custom-call | flops 335544320 | bytes 3932160 | tf_op jit(solution)/shard_map/mixed/pallas_call | solution.py:395
  47.1 0.1 collective-permute-start.6
  47.2 0.9 collective-permute-done.9.rest_2_
  48.1 3.1 %collective-permute-start.11 = (bf16[2,320,256]{2,1,0:T(8,128)(2,1)S(1)}, bf16[2,320,256]{2,1,0:T(8,128)(2,1)S(1)}, u32[]{:S(2)}, u32[]{:S(2)}) collective-permute-start(bf16[2,320,256]{2,1,0:T(8,128)(2,1)S(1)} %collective-permute-done.9.rest_2_), channel_id=1, source_target_pairs={{0,8},{4,12},{8,0},{12,4},{16,24},{20,28},{24,16},{28,20},{1,9},{5... | collective-permute-start | bytes 983048 | tf_op jit(solution)/shard_map/ppermute | solution.py:283
  51.2 4.6 %grad_out.1 = (bf16[16,128]{1,0:T(8,128)(2,1)S(1)}, bf16[2,320,256]{2,1,0:T(8,128)(2,1)S(1)}, bf16[2,320,256]{2,1,0:T(8,128)(2,1)S(1)}, bf16[2,320,256]{2,1,0:T(8,128)(2,1)S(1)}, bf16[2,320,256]{2,1,0:T(8,128)(2,1)S(1)}) custom-call(s32[5]{0:T(128)S(1)} %stack.67.idx, bf16[512,2560]{1,0:T(8,128)(2,1)S(1)} %bitcast.54, ...), custom_call_target="tpu_custom_call" | custom-call | flops 1342177280 | bytes 7077888 | tf_op jit(solution)/shard_map/grad_out/pallas_call | solution.py:417
  55.8 0.7 copy-done.8
  56.5 0.7 copy-done.14
  57.3 0.5 collective-permute-done.11.rest_3_
  57.8 5.2 %d_value.1.unread_too.left_ref = bf16[256,1024]{1,0:T(8,128)(2,1)S(1)} custom-call(s32[5]{0:T(128)S(1)} %stack.67.idx, bf16[16,128]{1,0:T(8,128)(2,1)S(1)} %get-tuple-element.43.token, bf16[512,2560]{1,0:T(8,128)(2,1)S(1)} %bitcast.55, bf16[512,2560]{1,0:T(8,128)(2,1)} %collective-permute-done.7.cot_s, bf16[4,8,128,128]{3,2,1,0:T(8,128)(2,1)S(1)} %bitcast.58, ...), custom_call_target="tpu_custom_call" | custom-call | flops 1342177280 | bytes 8126464 | tf_op jit(solution)/shard_map/d_value/pallas_call | solution.py:427
  63.0 2.2 %collective-permute-done.10 = bf16[2,320,256]{2,1,0:T(8,128)(2,1)S(1)} collective-permute-done((bf16[2,320,256]{2,1,0:T(8,128)(2,1)S(1)}, bf16[2,320,256]{2,1,0:T(8,128)(2,1)S(1)}, u32[]{:S(2)}, u32[]{:S(2)}) %collective-permute-start.10) | collective-permute-done | bytes 327712 | tf_op jit(solution)/shard_map/ppermute | solution.py:283
  65.2 0.1 add_convert_fusion.unread
  65.3 1.0 copy-done.5
  66.3 2.1 %assemble.1.w_o = bf16[2560,256]{1,0:T(8,128)(2,1)} custom-call(s32[5]{0:T(128)S(1)} %stack.67.idx, bf16[2,320,256]{2,1,0:T(8,128)(2,1)S(1)} %add_convert_fusion.unread, bf16[256,1024]{1,0:T(8,128)(2,1)S(1)} %d_value.1.unread_too.left_ref, bf16[2,320,256]{2,1,0:T(8,128)(2,1)S(1)} %copy-done.5, bf16[2,320,256]{2,1,0:T(8,128)(2,1)S(1)} %collective-permute-done.8.rest_1_, ...), custom_call_target="tpu_custom_call" | custom-call | bytes 2621440 | tf_op jit(solution)/shard_map/assemble/pallas_call | solution.py:442
  68.4 0.1 collective-permute-start.12
  68.5 0.1 pad_add_fusion.idx
  68.6 1.2 %collective-permute-start.18 = (bf16[2,320,256]{2,1,0:T(8,128)(2,1)}, bf16[2,320,256]{2,1,0:T(8,128)(2,1)S(1)}, u32[]{:S(2)}, u32[]{:S(2)}) collective-permute-start(bf16[2,320,256]{2,1,0:T(8,128)(2,1)} %copy-done.14), channel_id=1, source_target_pairs={{0,8},{4,12},{8,0},{12,4},{16,24},{20,28},{24,16},{28,20},{1,9},{5... | collective-permute-start | bytes 983048 | tf_op jit(solution)/shard_map/ppermute | solution.py:283
  69.8 1.5 %collective-permute-start.19 = (bf16[2,320,256]{2,1,0:T(8,128)(2,1)S(1)}, bf16[2,320,256]{2,1,0:T(8,128)(2,1)S(1)}, u32[]{:S(2)}, u32[]{:S(2)}) collective-permute-start(bf16[2,320,256]{2,1,0:T(8,128)(2,1)S(1)} %add_convert_fusion.unread), channel_id=1, source_target_pairs={{0,16},{4,20},{8,24},{12,28},{16,0},{20,4},{24,8},{28,12},{1,17},{... | collective-permute-start | bytes 983048 | tf_op jit(solution)/shard_map/ppermute | solution.py:283
  71.3 0.6 collective-permute-done.12.w_r
  71.9 0.9 copy-done.11
  72.8 0.9 copy-done.13
  73.8 3.6 %terms.1 = (bf16[16,128]{1,0:T(8,128)(2,1)S(1)}, bf16[2,256,640]{2,1,0:T(8,128)(2,1)S(1)}, bf16[2,256,640]{2,1,0:T(8,128)(2,1)S(1)}, bf16[4,256,640]{2,1,0:T(8,128)(2,1)S(1)}) custom-call(s32[4]{0:T(128)S(1)} %pad_add_fusion.idx, bf16[512,256]{1,0:T(8,128)(2,1)S(1)} %copy-done.11, bf16[512,256]{1,0:T(8,128)(2,1)S(1)} %copy-done.13, ...), custom_call_target="tpu_custom_call" | custom-call | flops 1342177280 | bytes 5767168 | tf_op jit(solution)/shard_map/terms/pallas_call | solution.py:458
  77.3 1.6 %collective-permute-start.13 = (bf16[2,256,640]{2,1,0:T(8,128)(2,1)S(1)}, bf16[2,256,640]{2,1,0:T(8,128)(2,1)S(1)}, u32[]{:S(2)}, u32[]{:S(2)}) collective-permute-start(bf16[2,256,640]{2,1,0:T(8,128)(2,1)S(1)} %get-tuple-element.45), channel_id=1, source_target_pairs={{0,1},{1,0},{2,3},{3,2},{4,5},{5,4},{6,7},{7,6},{8,9},{9,8},{10,11... | collective-permute-start | bytes 1966088 | tf_op jit(solution)/shard_map/ppermute | solution.py:294
  78.9 1.5 %collective-permute-start.15 = (bf16[2,256,640]{2,1,0:T(8,128)(2,1)S(1)}, bf16[2,256,640]{2,1,0:T(8,128)(2,1)S(1)}, u32[]{:S(2)}, u32[]{:S(2)}) collective-permute-start(bf16[2,256,640]{2,1,0:T(8,128)(2,1)S(1)} %get-tuple-element.46), channel_id=1, source_target_pairs={{0,2},{1,3},{2,0},{3,1},{4,6},{5,7},{6,4},{7,5},{8,10},{9,11},{10,... | collective-permute-start | bytes 1966088 | tf_op jit(solution)/shard_map/ppermute | solution.py:294
  80.4 4.6 %grad_value.1 = (bf16[2,320,256]{2,1,0:T(8,128)(2,1)S(1)}, bf16[2,320,256]{2,1,0:T(8,128)(2,1)S(1)}, bf16[2,320,256]{2,1,0:T(8,128)(2,1)S(1)}, bf16[2,320,256]{2,1,0:T(8,128)(2,1)S(1)}) custom-call(s32[5]{0:T(128)S(1)} %stack.67.idx, bf16[16,128]{1,0:T(8,128)(2,1)S(1)} %get-tuple-element.47.token, bf16[2,320,256]{2,1,0:T(8,128)(2,1)S(1)} %add_convert_fusion.unread, ...), custom_call_target="tpu_custom_call" | custom-call | flops 1342177280 | bytes 7077888 | tf_op jit(solution)/shard_map/grad_value/pallas_call | solution.py:467
  85.0 1.3 %collective-permute-start.17 = (bf16[2,320,256]{2,1,0:T(8,128)(2,1)S(1)}, bf16[2,320,256]{2,1,0:T(8,128)(2,1)S(1)}, u32[]{:S(2)}, u32[]{:S(2)}) collective-permute-start(bf16[2,320,256]{2,1,0:T(8,128)(2,1)S(1)} %get-tuple-element.50), channel_id=1, source_target_pairs={{0,8},{4,12},{8,0},{12,4},{16,24},{20,28},{24,16},{28,20},{1,9},{5... | collective-permute-start | bytes 983048 | tf_op jit(solution)/shard_map/ppermute | solution.py:283
  86.3 0.2 convert_element_type.53
  86.5 1.1 collective-permute-done.19.far
  87.6 7.0 %collective-permute-done.17.got = bf16[2,320,256]{2,1,0:T(8,128)(2,1)S(1)} collective-permute-done((bf16[2,320,256]{2,1,0:T(8,128)(2,1)S(1)}, bf16[2,320,256]{2,1,0:T(8,128)(2,1)S(1)}, u32[]{:S(2)}, u32[]{:S(2)}) %collective-permute-start.17) | collective-permute-done | bytes 327712 | tf_op jit(solution)/shard_map/ppermute | solution.py:283
  94.6 0.2 sum.1
  94.8 1.0 collective-permute-start.20
  95.8 1.5 %collective-permute-start.21 = (bf16[2,320,256]{2,1,0:T(8,128)(2,1)S(1)}, bf16[2,320,256]{2,1,0:T(8,128)(2,1)S(1)}, u32[]{:S(2)}, u32[]{:S(2)}) collective-permute-start(bf16[2,320,256]{2,1,0:T(8,128)(2,1)S(1)} %get-tuple-element.55), channel_id=1, source_target_pairs={{0,16},{4,20},{8,24},{12,28},{16,0},{20,4},{24,8},{28,12},{1,17},{... | collective-permute-start | bytes 983048 | tf_op jit(solution)/shard_map/ppermute | solution.py:283
  97.3 0.1 convert_element_type.54
  97.5 0.1 convert_element_type.58
  97.6 0.1 fusion.8
  97.7 0.9 collective-permute-start.14
  98.6 0.8 collective-permute-start.16
  99.4 10.2 %collective-permute-done.20 = bf16[2,320,256]{2,1,0:T(8,128)(2,1)S(1)} collective-permute-done((bf16[2,320,256]{2,1,0:T(8,128)(2,1)S(1)}, bf16[2,320,256]{2,1,0:T(8,128)(2,1)S(1)}, u32[]{:S(2)}, u32[]{:S(2)}) %collective-permute-start.20) | collective-permute-done | bytes 327712 | tf_op jit(solution)/shard_map/ppermute | solution.py:283
  109.6 2.1 %collective-permute-done.21 = bf16[2,320,256]{2,1,0:T(8,128)(2,1)S(1)} collective-permute-done((bf16[2,320,256]{2,1,0:T(8,128)(2,1)S(1)}, bf16[2,320,256]{2,1,0:T(8,128)(2,1)S(1)}, u32[]{:S(2)}, u32[]{:S(2)}) %collective-permute-start.21) | collective-permute-done | bytes 327712 | tf_op jit(solution)/shard_map/ppermute | solution.py:283
  111.7 0.1 convert_add_fusion
  111.9 0.1 collective-permute-start.22
  112.0 0.9 pad_maximum_fusion.2
  113.0 0.2 fusion.7
  113.2 0.9 pad_maximum_fusion
  114.2 0.9 pad_maximum_fusion.1
  (45 shorter events, 0.5 us)
Async XLA Ops:
  0.6 3.2 %copy-start = (bf16[2,2,128,2560]{3,2,1,0:T(8,128)(2,1)S(1)}, bf16[2,2,128,2560]{3,2,1,0:T(8,128)(2,1)}, u32[]{:S(2)}) copy-start(bf16[2,2,128,2560]{3,2,1,0:T(8,128)(2,1)} %param.5) | copy-start | bytes 7864324
  2.1 1.8 %collective-permute-start = (bf16[2,320,256]{2,1,0:T(8,128)(2,1)S(1)}, bf16[2,320,256]{2,1,0:T(8,128)(2,1)S(1)}, u32[]{:S(2)}, u32[]{:S(2)}) collective-permute-start(bf16[2,320,256]{2,1,0:T(8,128)(2,1)S(1)} %get-tuple-element.66), channel_id=1, source_target_pairs={{0,4},{4,0},{8,12},{12,8},{16,20},{20,16},{24,28},{28,24},{1,5},{5... | collective-permute-start | bytes 983048 | tf_op jit(solution)/shard_map/ppermute | solution.py:291
  3.8 26.1 %collective-permute-start.1 = (bf16[512,2560]{1,0:T(8,128)(2,1)S(1)}, bf16[512,2560]{1,0:T(8,128)(2,1)}, u32[]{:S(2)}, u32[]{:S(2)}) collective-permute-start(bf16[512,2560]{1,0:T(8,128)(2,1)S(1)} %bitcast.50), channel_id=1, source_target_pairs={{0,4},{4,0},{8,12},{12,8},{16,20},{20,16},{24,28},{28,24},{1,5},{5... | collective-permute-start | bytes 7864328 | tf_op jit(solution)/shard_map/ppermute | solution.py:291
  4.2 47.0 %collective-permute-start.7 = (bf16[512,2560]{1,0:T(8,128)(2,1)}, bf16[512,2560]{1,0:T(8,128)(2,1)}, u32[]{:S(2)}, u32[]{:S(2)}) collective-permute-start(bf16[512,2560]{1,0:T(8,128)(2,1)} %bitcast.53), channel_id=1, source_target_pairs={{0,4},{4,0},{8,12},{12,8},{16,20},{20,16},{24,28},{28,24},{1,5},{5... | collective-permute-start | bytes 7864328 | tf_op jit(solution)/shard_map/ppermute | solution.py:291
  4.4 24.5 %collective-permute-start.2 = (bf16[4,8,128,128]{3,2,1,0:T(8,128)(2,1)}, bf16[4,8,128,128]{3,2,1,0:T(8,128)(2,1)}, u32[]{:S(2)}, u32[]{:S(2)}) collective-permute-start(bf16[4,8,128,128]{3,2,1,0:T(8,128)(2,1)} %bitcast.56), channel_id=1, source_target_pairs={{0,4},{4,0},{8,12},{12,8},{16,20},{20,16},{24,28},{28,24},{1,5},{5... | collective-permute-start | bytes 3145736 | tf_op jit(solution)/shard_map/ppermute | solution.py:291
  4.8 17.9 %collective-permute-start.3 = (bf16[2,320,256]{2,1,0:T(8,128)(2,1)S(1)}, bf16[2,320,256]{2,1,0:T(8,128)(2,1)S(1)}, u32[]{:S(2)}, u32[]{:S(2)}) collective-permute-start(bf16[2,320,256]{2,1,0:T(8,128)(2,1)S(1)} %pad_maximum_fusion.5.rest_0_), channel_id=1, source_target_pairs={{0,8},{4,12},{8,0},{12,4},{16,24},{20,28},{24,16},{28,20},{1,9},{5... | collective-permute-start | bytes 983048 | tf_op jit(solution)/shard_map/ppermute | solution.py:283
  7.6 17.7 %collective-permute-start.4 = (bf16[2,320,256]{2,1,0:T(8,128)(2,1)S(1)}, bf16[2,320,256]{2,1,0:T(8,128)(2,1)S(1)}, u32[]{:S(2)}, u32[]{:S(2)}) collective-permute-start(bf16[2,320,256]{2,1,0:T(8,128)(2,1)S(1)} %pad_maximum_fusion.5.rest_0_), channel_id=1, source_target_pairs={{0,16},{4,20},{8,24},{12,28},{16,0},{20,4},{24,8},{28,12},{1,17},{... | collective-permute-start | bytes 983048 | tf_op jit(solution)/shard_map/ppermute | solution.py:283
  26.1 0.7 copy-start.6
  26.8 31.0 %copy-start.4 = (bf16[2,320,256]{2,1,0:T(8,128)(2,1)}, bf16[2,320,256]{2,1,0:T(8,128)(2,1)S(1)}, u32[]{:S(2)}) copy-start(bf16[2,320,256]{2,1,0:T(8,128)(2,1)S(1)} %get-tuple-element.40.rest_0_) | copy-start | bytes 983044
  26.8 17.6 %collective-permute-start.5 = (bf16[2,320,256]{2,1,0:T(8,128)(2,1)}, bf16[2,320,256]{2,1,0:T(8,128)(2,1)}, u32[]{:S(2)}, u32[]{:S(2)}) collective-permute-start(bf16[2,320,256]{2,1,0:T(8,128)(2,1)} %get-tuple-element.33.rest_2_), channel_id=1, source_target_pairs={{0,8},{4,12},{8,0},{12,4},{16,24},{20,28},{24,16},{28,20},{1,9},{5... | collective-permute-start | bytes 983048 | tf_op jit(solution)/shard_map/ppermute | solution.py:283
  27.3 23.9 %collective-permute-start.8 = (bf16[2,320,256]{2,1,0:T(8,128)(2,1)S(1)}, bf16[2,320,256]{2,1,0:T(8,128)(2,1)S(1)}, u32[]{:S(2)}, u32[]{:S(2)}) collective-permute-start(bf16[2,320,256]{2,1,0:T(8,128)(2,1)S(1)} %get-tuple-element.40.rest_0_), channel_id=1, source_target_pairs={{0,8},{4,12},{8,0},{12,4},{16,24},{20,28},{24,16},{28,20},{1,9},{5... | collective-permute-start | bytes 983048 | tf_op jit(solution)/shard_map/ppermute | solution.py:283
  28.9 19.2 %collective-permute-start.9 = (bf16[2,320,256]{2,1,0:T(8,128)(2,1)S(1)}, bf16[2,320,256]{2,1,0:T(8,128)(2,1)S(1)}, u32[]{:S(2)}, u32[]{:S(2)}) collective-permute-start(bf16[2,320,256]{2,1,0:T(8,128)(2,1)S(1)} %get-tuple-element.40.rest_0_), channel_id=1, source_target_pairs={{0,16},{4,20},{8,24},{12,28},{16,0},{20,4},{24,8},{28,12},{1,17},{... | collective-permute-start | bytes 983048 | tf_op jit(solution)/shard_map/ppermute | solution.py:283
  30.0 1.2 %copy-start.2 = (bf16[2,2,8,128,128]{4,3,2,1,0:T(8,128)(2,1)S(1)}, bf16[2,2,8,128,128]{4,3,2,1,0:T(8,128)(2,1)}, u32[]{:S(2)}) copy-start(bf16[2,2,8,128,128]{4,3,2,1,0:T(8,128)(2,1)} %param.6) | copy-start | bytes 3145732
  31.2 1.0 copy-start.7
  44.4 6.8 %copy-start.1 = (bf16[2,2,128,2560]{3,2,1,0:T(8,128)(2,1)S(1)}, bf16[2,2,128,2560]{3,2,1,0:T(8,128)(2,1)}, u32[]{:S(2)}) copy-start(bf16[2,2,128,2560]{3,2,1,0:T(8,128)(2,1)} %param.7) | copy-start | bytes 7864324
  47.1 8.7 %copy-start.10 = (bf16[512,256]{1,0:T(8,128)(2,1)}, bf16[512,256]{1,0:T(8,128)(2,1)S(1)}, u32[]{:S(2)}) copy-start(bf16[512,256]{1,0:T(8,128)(2,1)S(1)} %get-tuple-element.37.mixed_o) | copy-start | bytes 786436
  47.1 4.1 %collective-permute-start.6 = (bf16[512,256]{1,0:T(8,128)(2,1)S(1)}, bf16[512,256]{1,0:T(8,128)(2,1)S(1)}, u32[]{:S(2)}, u32[]{:S(2)}) collective-permute-start(bf16[512,256]{1,0:T(8,128)(2,1)S(1)} %get-tuple-element.38.mixed_s), channel_id=1, source_target_pairs={{0,4},{4,0},{8,12},{12,8},{16,20},{20,16},{24,28},{28,24},{1,5},{5... | collective-permute-start | bytes 786440 | tf_op jit(solution)/shard_map/ppermute | solution.py:291
  48.1 9.6 %collective-permute-start.11 = (bf16[2,320,256]{2,1,0:T(8,128)(2,1)S(1)}, bf16[2,320,256]{2,1,0:T(8,128)(2,1)S(1)}, u32[]{:S(2)}, u32[]{:S(2)}) collective-permute-start(bf16[2,320,256]{2,1,0:T(8,128)(2,1)S(1)} %collective-permute-done.9.rest_2_), channel_id=1, source_target_pairs={{0,8},{4,12},{8,0},{12,4},{16,24},{20,28},{24,16},{28,20},{1,9},{5... | collective-permute-start | bytes 983048 | tf_op jit(solution)/shard_map/ppermute | solution.py:283
  51.2 4.6 %copy-start.12 = (bf16[512,256]{1,0:T(8,128)(2,1)}, bf16[512,256]{1,0:T(8,128)(2,1)S(1)}, u32[]{:S(2)}) copy-start(bf16[512,256]{1,0:T(8,128)(2,1)S(1)} %collective-permute-done.6.rest_0_.mixed_r) | copy-start | bytes 786436
  51.2 6.6 %copy-start.3 = (bf16[2,2,8,128,128]{4,3,2,1,0:T(8,128)(2,1)S(1)}, bf16[2,2,8,128,128]{4,3,2,1,0:T(8,128)(2,1)}, u32[]{:S(2)}) copy-start(bf16[2,2,8,128,128]{4,3,2,1,0:T(8,128)(2,1)} %param.6) | copy-start | bytes 3145732
  55.8 0.7 copy-start.8
  56.5 0.7 copy-start.14
  57.3 7.9 %collective-permute-start.10 = (bf16[2,320,256]{2,1,0:T(8,128)(2,1)S(1)}, bf16[2,320,256]{2,1,0:T(8,128)(2,1)S(1)}, u32[]{:S(2)}, u32[]{:S(2)}) collective-permute-start(bf16[2,320,256]{2,1,0:T(8,128)(2,1)S(1)} %get-tuple-element.42), channel_id=1, source_target_pairs={{0,8},{4,12},{8,0},{12,4},{16,24},{20,28},{24,16},{28,20},{1,9},{5... | collective-permute-start | bytes 983048 | tf_op jit(solution)/shard_map/ppermute | solution.py:283
  65.3 1.0 copy-start.5
  68.4 3.4 %collective-permute-start.12 = (bf16[2560,256]{1,0:T(8,128)(2,1)}, bf16[2560,256]{1,0:T(8,128)(2,1)}, u32[]{:S(2)}, u32[]{:S(2)}) collective-permute-start(bf16[2560,256]{1,0:T(8,128)(2,1)} %assemble.1.w_o), channel_id=1, source_target_pairs={{0,4},{4,0},{8,12},{12,8},{16,20},{20,16},{24,28},{28,24},{1,5},{5... | collective-permute-start | bytes 3932168 | tf_op jit(solution)/shard_map/ppermute | solution.py:291
  68.6 17.9 %collective-permute-start.18 = (bf16[2,320,256]{2,1,0:T(8,128)(2,1)}, bf16[2,320,256]{2,1,0:T(8,128)(2,1)S(1)}, u32[]{:S(2)}, u32[]{:S(2)}) collective-permute-start(bf16[2,320,256]{2,1,0:T(8,128)(2,1)} %copy-done.14), channel_id=1, source_target_pairs={{0,8},{4,12},{8,0},{12,4},{16,24},{20,28},{24,16},{28,20},{1,9},{5... | collective-permute-start | bytes 983048 | tf_op jit(solution)/shard_map/ppermute | solution.py:283
  69.8 17.8 %collective-permute-start.19 = (bf16[2,320,256]{2,1,0:T(8,128)(2,1)S(1)}, bf16[2,320,256]{2,1,0:T(8,128)(2,1)S(1)}, u32[]{:S(2)}, u32[]{:S(2)}) collective-permute-start(bf16[2,320,256]{2,1,0:T(8,128)(2,1)S(1)} %add_convert_fusion.unread), channel_id=1, source_target_pairs={{0,16},{4,20},{8,24},{12,28},{16,0},{20,4},{24,8},{28,12},{1,17},{... | collective-permute-start | bytes 983048 | tf_op jit(solution)/shard_map/ppermute | solution.py:283
  71.9 1.0 copy-start.11
  72.8 0.9 copy-start.13
  77.3 20.0 %collective-permute-start.13 = (bf16[2,256,640]{2,1,0:T(8,128)(2,1)S(1)}, bf16[2,256,640]{2,1,0:T(8,128)(2,1)S(1)}, u32[]{:S(2)}, u32[]{:S(2)}) collective-permute-start(bf16[2,256,640]{2,1,0:T(8,128)(2,1)S(1)} %get-tuple-element.45), channel_id=1, source_target_pairs={{0,1},{1,0},{2,3},{3,2},{4,5},{5,4},{6,7},{7,6},{8,9},{9,8},{10,11... | collective-permute-start | bytes 1966088 | tf_op jit(solution)/shard_map/ppermute | solution.py:294
  78.9 18.6 %collective-permute-start.15 = (bf16[2,256,640]{2,1,0:T(8,128)(2,1)S(1)}, bf16[2,256,640]{2,1,0:T(8,128)(2,1)S(1)}, u32[]{:S(2)}, u32[]{:S(2)}) collective-permute-start(bf16[2,256,640]{2,1,0:T(8,128)(2,1)S(1)} %get-tuple-element.46), channel_id=1, source_target_pairs={{0,2},{1,3},{2,0},{3,1},{4,6},{5,7},{6,4},{7,5},{8,10},{9,11},{10,... | collective-permute-start | bytes 1966088 | tf_op jit(solution)/shard_map/ppermute | solution.py:294
  85.0 9.6 %collective-permute-start.17 = (bf16[2,320,256]{2,1,0:T(8,128)(2,1)S(1)}, bf16[2,320,256]{2,1,0:T(8,128)(2,1)S(1)}, u32[]{:S(2)}, u32[]{:S(2)}) collective-permute-start(bf16[2,320,256]{2,1,0:T(8,128)(2,1)S(1)} %get-tuple-element.50), channel_id=1, source_target_pairs={{0,8},{4,12},{8,0},{12,4},{16,24},{20,28},{24,16},{28,20},{1,9},{5... | collective-permute-start | bytes 983048 | tf_op jit(solution)/shard_map/ppermute | solution.py:283
  86.3 8.3 %copy-start.9 = (bf16[2,320,256]{2,1,0:T(8,128)(2,1)S(1)}, bf16[2,320,256]{2,1,0:T(8,128)(2,1)}, u32[]{:S(2)}) copy-start(bf16[2,320,256]{2,1,0:T(8,128)(2,1)} %copy-done.8) | copy-start | bytes 983044
  94.8 14.8 %collective-permute-start.20 = (bf16[2,320,256]{2,1,0:T(8,128)(2,1)S(1)}, bf16[2,320,256]{2,1,0:T(8,128)(2,1)S(1)}, u32[]{:S(2)}, u32[]{:S(2)}) collective-permute-start(bf16[2,320,256]{2,1,0:T(8,128)(2,1)S(1)} %get-tuple-element.54), channel_id=1, source_target_pairs={{0,8},{4,12},{8,0},{12,4},{16,24},{20,28},{24,16},{28,20},{1,9},{5... | collective-permute-start | bytes 983048 | tf_op jit(solution)/shard_map/ppermute | solution.py:283
  95.8 16.0 %collective-permute-start.21 = (bf16[2,320,256]{2,1,0:T(8,128)(2,1)S(1)}, bf16[2,320,256]{2,1,0:T(8,128)(2,1)S(1)}, u32[]{:S(2)}, u32[]{:S(2)}) collective-permute-start(bf16[2,320,256]{2,1,0:T(8,128)(2,1)S(1)} %get-tuple-element.55), channel_id=1, source_target_pairs={{0,16},{4,20},{8,24},{12,28},{16,0},{20,4},{24,8},{28,12},{1,17},{... | collective-permute-start | bytes 983048 | tf_op jit(solution)/shard_map/ppermute | solution.py:283
  97.3 14.7 %collective-permute-start.23 = (f32[320,256]{1,0:T(8,128)S(1)}, f32[320,256]{1,0:T(8,128)S(1)}, u32[]{:S(2)}, u32[]{:S(2)}) collective-permute-start(f32[320,256]{1,0:T(8,128)S(1)} %slice_bitcast_fusion.2), channel_id=1, source_target_pairs={{0,4},{4,0},{8,12},{12,8},{16,20},{20,16},{24,28},{28,24},{1,5},{5... | collective-permute-start | bytes 983048 | tf_op jit(solution)/shard_map/ppermute | solution.py:291
  97.7 15.3 %collective-permute-start.14 = (bf16[256,640]{1,0:T(8,128)(2,1)S(1)}, bf16[256,640]{1,0:T(8,128)(2,1)S(1)}, u32[]{:S(2)}, u32[]{:S(2)}) collective-permute-start(bf16[256,640]{1,0:T(8,128)(2,1)S(1)} %get-tuple-element.59), channel_id=1, source_target_pairs={{0,2},{1,3},{2,0},{3,1},{4,6},{5,7},{6,4},{7,5},{8,10},{9,11},{10,... | collective-permute-start | bytes 983048 | tf_op jit(solution)/shard_map/ppermute | solution.py:294
  98.6 14.4 %collective-permute-start.16 = (bf16[256,640]{1,0:T(8,128)(2,1)S(1)}, bf16[256,640]{1,0:T(8,128)(2,1)S(1)}, u32[]{:S(2)}, u32[]{:S(2)}) collective-permute-start(bf16[256,640]{1,0:T(8,128)(2,1)S(1)} %get-tuple-element.60), channel_id=1, source_target_pairs={{0,1},{1,0},{2,3},{3,2},{4,5},{5,4},{6,7},{7,6},{8,9},{9,8},{10,11... | collective-permute-start | bytes 983048 | tf_op jit(solution)/shard_map/ppermute | solution.py:294
  111.9 2.2 %collective-permute-start.22 = (f32[320,256]{1,0:T(8,128)S(1)}, f32[320,256]{1,0:T(8,128)S(1)}, u32[]{:S(2)}, u32[]{:S(2)}) collective-permute-start(f32[320,256]{1,0:T(8,128)S(1)} %slice_bitcast_fusion), channel_id=1, source_target_pairs={{0,4},{4,0},{8,12},{12,8},{16,20},{20,16},{24,28},{28,24},{1,5},{5... | collective-permute-start | bytes 983048 | tf_op jit(solution)/shard_map/ppermute | solution.py:291

commit v17 on v16

--- a/solution.py
+++ b/solution.py
@@ -170,8 +170,8 @@
         mix_back(d_mixed, mix_v.at[half], left_v, half * tokens)
 
 
-def gradient_kernel(idx, token, unread, right_o, right_s, left_ref, *rest):
-    del token, unread
+def gradient_kernel(idx, unread, right_o, right_s, left_ref, *rest):
+    del unread
     outs, (right_v, grad_v, sems) = rest[:-3], rest[-3:]
     tokens, _ = right_o.shape
     copies = begin(
@@ -226,7 +226,8 @@
     second_out[...] = second[...]
 
 
-def sum_kernel(block, got, beside, own, near, far, onward, beside_out, total):
+def sum_kernel(token, block, got, beside, own, near, far, onward, beside_out, total):
+    del token
     onward[...] = (block[...].astype(F32) + got[...].astype(F32)).astype(BF16)
     beside_out[...] = beside[...]
     total[...] = own[...].astype(F32) + near[...].astype(F32) + far[...].astype(F32)
@@ -467,17 +468,17 @@
         back_sends = call(
             gradient_kernel,
             "grad_value",
-            [SMEM] + [ANY] * 4 + [VMEM],
+            [SMEM] + [ANY] * 3 + [VMEM],
             send_shapes,
             [both, rows, pltpu.SemaphoreType.DMA((2,))],
             flops,
             2 * (2 * act.size + 2 * tokens * cols + width * cols),
-        )(idx, token, out_onward, act, act_s, left)
+        )(idx, out_onward, act, act_s, left)
         if line4:
             back_passed = swap(back_sends[3], 1)
             onward, beside, out_total = call(
-                sum_kernel, "sum", [VMEM] * 6, [block] * 3, [], 0, kinds=[BF16, BF16, F32], vmem=8
-            )(back_sends[2], back_passed, back_sends[1], out_sends[0], out_near, out_far)
+                sum_kernel, "sum", [ANY] + [VMEM] * 6, [block] * 3, [], 0, kinds=[BF16, BF16, F32], vmem=8
+            )(token, back_sends[2], back_passed, back_sends[1], out_sends[0], out_near, out_far)
             back_far, back_near = swap(onward, 2), swap(beside, 1)
             grad_out = join(out_total[0], sibling(out_total[1]), c)
             grad_value = scatter_end(back_sends[0], (back_near, back_far), c)

time: 116 us -> 129 us (1.11)
  waiting for transfers between devices: 48.3 us -> 54.8 us
  starting transfers between devices: 24.4 us -> 29.9 us
  Pallas kernels: 28.7 us -> 31.1 us
    ppermute x4, waiting for transfers between devices: 0.01 us -> 10.1 us  [flip(): return lax.ppermute(x, 'node', [(i, i ^ j) for i in range(n_node)])]
    ppermute x12, starting transfers between devices: 17.9 us -> 23 us  [move(): lax.ppermute(x, 'wide', [(2 * s + c, 2 * d + c) for s, d in pairs for c i...]
    ppermute x12, waiting for transfers between devices: 46.4 us -> 43.4 us  [move(): lax.ppermute(x, 'wide', [(2 * s + c, 2 * d + c) for s, d in pairs for c i...]
    pallas_call x2, Pallas kernels: 4.82 us -> 6.51 us  [the longest x1 5.34 us: body(): call(gradient_kernel, 'grad_value', [SMEM] + [ANY] * 3 + [VMEM], send_sha...]
    unnamed x30 -> x28, local copies, waits for them, and re-layouts: 7.26 us -> 6.15 us
  transfers between devices with their start and end apart: 24 -> 24, of which waited for: 12 -> 13; matrix products, arithmetic and copies ran while one was open for 3% -> 2% of each run, Pallas kernels for 23% -> 22%
where the time goes in v17:
time: 129 us; the launch traced here: 128 us
  waiting for transfers between devices  54.8 us (42%)
  Pallas kernels  31.1 us (24%)
  starting transfers between devices  29.9 us (23%)
  local copies, waits for them, and re-layouts  7.68 us (6%)
  other arithmetic  3.93 us (3%)
    ppermute x12, waiting for transfers between devices, move(): lax.ppermute(x, 'wide', [(2 * s + c, 2 * d + c) for s, d in pairs for c i...  43.4 us
    ppermute x12, starting transfers between devices, move(): lax.ppermute(x, 'wide', [(2 * s + c, 2 * d + c) for s, d in pairs for c i...  23 us
    ppermute x4, waiting for transfers between devices, flip(): return lax.ppermute(x, 'node', [(i, i ^ j) for i in range(n_node)])  10.1 us
    unnamed x28, local copies, waits for them, and re-layouts  6.15 us
    pallas_call x1, Pallas kernels, body(): call(gradient_kernel, 'grad_value', [SMEM] + [ANY] * 3 + [VMEM], send_sha...  5.34 us
    pallas_call x1, Pallas kernels, body(): call(functools.partial(grad_out_kernel, len(unread)), 'grad_out', [SMEM]...  5.29 us
    pallas_call x1, Pallas kernels, body(): call(functools.partial(d_value_kernel, n_slots), 'd_value', [SMEM] + [ANY...  5.24 us
    ppermute x4, starting transfers between devices, flip(): return lax.ppermute(x, 'node', [(i, i ^ j) for i in range(n_node)])  5.19 us
  transfers between devices with their start and end apart: 24, of which 13 were waited for; matrix products, arithmetic and copies ran while one was open for 2% of the time, Pallas kernels for 22%

profile of v17, /device:TPU:0, one launch (start us, length us, event | category | flops | bytes accessed | tf_op | source)
XLA Modules:
  0.0 128.3 jit_solution(8495926737795132783)
XLA Ops:
  0.7 1.3 %slice_bitcast_fusion.5 = (bf16[1,320,256]{2,1,0:T(8,128)(2,1)S(1)}, bf16[1,320,256]{2,1,0:T(8,128)(2,1)S(1)}, bf16[1,320,256]{2,1,0:T(8,128)(2,1)S(1)}, bf16[1,320,256]{2,1,0:T(8,128)(2,1)S(1)}) fusion(bf16[320,512]{1,0:T(8,128)(2,1)} %param.8, bf16[320,512]{1,0:T(8,128)(2,1)} %param.9), kind=kLoop, calls=%fused_computation.34 | loop fusion | bytes 1310720 | tf_op jit(solution)/shard_map/stack | solution.py:300
  2.1 0.5 collective-permute-start
  2.6 1.3 collective-permute-done
  3.8 0.4 collective-permute-start.1
  4.2 0.1 collective-permute-start.7
  4.4 0.4 collective-permute-start.2
  4.8 3.8 %collective-permute-start.4 = (bf16[2,320,256]{2,1,0:T(8,128)(2,1)S(1)}, bf16[2,320,256]{2,1,0:T(8,128)(2,1)S(1)}, u32[]{:S(2)}, u32[]{:S(2)}) collective-permute-start(bf16[2,320,256]{2,1,0:T(8,128)(2,1)S(1)} %pad_maximum_fusion.5.rest_0_), channel_id=1, source_target_pairs={{0,16},{4,20},{8,24},{12,28},{16,0},{20,4},{24,8},{28,12},{1,17},{... | collective-permute-start | bytes 983048 | tf_op jit(solution)/shard_map/ppermute | solution.py:284
  8.6 1.6 %collective-permute-start.3 = (bf16[2,320,256]{2,1,0:T(8,128)(2,1)S(1)}, bf16[2,320,256]{2,1,0:T(8,128)(2,1)S(1)}, u32[]{:S(2)}, u32[]{:S(2)}) collective-permute-start(bf16[2,320,256]{2,1,0:T(8,128)(2,1)S(1)} %pad_maximum_fusion.5.rest_0_), channel_id=1, source_target_pairs={{0,8},{4,12},{8,0},{12,4},{16,24},{20,28},{24,16},{28,20},{1,9},{5... | collective-permute-start | bytes 983048 | tf_op jit(solution)/shard_map/ppermute | solution.py:284
  10.2 13.8 %collective-permute-done.4.first = bf16[2,320,256]{2,1,0:T(8,128)(2,1)S(1)} collective-permute-done((bf16[2,320,256]{2,1,0:T(8,128)(2,1)S(1)}, bf16[2,320,256]{2,1,0:T(8,128)(2,1)S(1)}, u32[]{:S(2)}, u32[]{:S(2)}) %collective-permute-start.4) | collective-permute-done | bytes 327712 | tf_op jit(solution)/shard_map/ppermute | solution.py:284
  24.0 0.2 collective-permute-done.3.unread.rest_1_
  24.2 0.8 relay.1
  25.0 0.7 copy-done.4
  25.7 1.5 %collective-permute-start.5 = (bf16[2,320,256]{2,1,0:T(8,128)(2,1)}, bf16[2,320,256]{2,1,0:T(8,128)(2,1)}, u32[]{:S(2)}, u32[]{:S(2)}) collective-permute-start(bf16[2,320,256]{2,1,0:T(8,128)(2,1)} %get-tuple-element.33.rest_2_), channel_id=1, source_target_pairs={{0,8},{4,12},{8,0},{12,4},{16,24},{20,28},{24,16},{28,20},{1,9},{5... | collective-permute-start | bytes 983048 | tf_op jit(solution)/shard_map/ppermute | solution.py:284
  27.2 0.1 stack.67.idx
  27.2 2.3 %collective-permute-start.9 = (bf16[2,320,256]{2,1,0:T(8,128)(2,1)S(1)}, bf16[2,320,256]{2,1,0:T(8,128)(2,1)S(1)}, u32[]{:S(2)}, u32[]{:S(2)}) collective-permute-start(bf16[2,320,256]{2,1,0:T(8,128)(2,1)S(1)} %get-tuple-element.40.rest_0_), channel_id=1, source_target_pairs={{0,16},{4,20},{8,24},{12,28},{16,0},{20,4},{24,8},{28,12},{1,17},{... | collective-permute-start | bytes 983048 | tf_op jit(solution)/shard_map/ppermute | solution.py:284
  29.6 1.2 copy-done.2
  30.8 1.0 copy-done.5
  31.8 4.9 %value_ahead.1 = (f32[2,512,256]{2,1,0:T(8,128)S(1)}, bf16[2,512,640]{2,1,0:T(8,128)(2,1)S(1)}, bf16[2,4,4,128,128]{4,3,2,1,0:T(8,128)(2,1)S(1)}) custom-call(s32[5]{0:T(128)S(1)} %stack.67.idx, bf16[512,2560]{1,0:T(8,128)(2,1)S(1)} %bitcast.51, bf16[512,2560]{1,0:T(8,128)(2,1)} %collective-permute-done.1.x_s.right_s, bf16[4,8,128,128]{3,2,1,0:T(8,128)(2,1)S(1)} %bitcast.57, ...), custom_call_target="tpu_custom_call" | custom-call | flops 1342177280 | bytes 11272192 | tf_op jit(solution)/shard_map/value_ahead/pallas_call | solution.py:383
  36.7 6.9 %collective-permute-done.5.slot = bf16[2,320,256]{2,1,0:T(8,128)(2,1)} collective-permute-done((bf16[2,320,256]{2,1,0:T(8,128)(2,1)}, bf16[2,320,256]{2,1,0:T(8,128)(2,1)}, u32[]{:S(2)}, u32[]{:S(2)}) %collective-permute-start.5) | collective-permute-done | bytes 327712 | tf_op jit(solution)/shard_map/ppermute | solution.py:284
  43.6 2.7 %mixed.1 = (bf16[512,256]{1,0:T(8,128)(2,1)S(1)}, bf16[512,256]{1,0:T(8,128)(2,1)S(1)}) custom-call(s32[5]{0:T(128)S(1)} %stack.67.idx, f32[2,512,256]{2,1,0:T(8,128)S(1)} %get-tuple-element.34.part, bf16[2,512,640]{2,1,0:T(8,128)(2,1)S(1)} %get-tuple-element.35.last, bf16[2,4,4,128,128]{4,3,2,1,0:T(8,128)(2,1)S(1)} %get-tuple-element.36.weights, ...), custom_call_target="tpu_custom_call" | custom-call | flops 335544320 | bytes 3932160 | tf_op jit(solution)/shard_map/mixed/pallas_call | solution.py:396
  46.2 0.1 collective-permute-start.6
  46.3 0.1 collective-permute-start.11
  46.4 2.7 %collective-permute-done.8.rest_1_ = bf16[2,320,256]{2,1,0:T(8,128)(2,1)S(1)} collective-permute-done((bf16[2,320,256]{2,1,0:T(8,128)(2,1)S(1)}, bf16[2,320,256]{2,1,0:T(8,128)(2,1)S(1)}, u32[]{:S(2)}, u32[]{:S(2)}) %collective-permute-start.8) | collective-permute-done | bytes 327712 | tf_op jit(solution)/shard_map/ppermute | solution.py:284
  49.1 5.3 %grad_out.1 = (bf16[16,128]{1,0:T(8,128)(2,1)S(1)}, bf16[2,320,256]{2,1,0:T(8,128)(2,1)S(1)}, bf16[2,320,256]{2,1,0:T(8,128)(2,1)}, bf16[2,320,256]{2,1,0:T(8,128)(2,1)S(1)}, bf16[2,320,256]{2,1,0:T(8,128)(2,1)S(1)}) custom-call(s32[5]{0:T(128)S(1)} %stack.67.idx, bf16[512,2560]{1,0:T(8,128)(2,1)S(1)} %bitcast.54, ...), custom_call_target="tpu_custom_call" | custom-call | flops 1342177280 | bytes 7077888 | tf_op jit(solution)/shard_map/grad_out/pallas_call | solution.py:418
  54.4 0.7 copy-done.6
  55.2 2.4 %collective-permute-start.10 = (bf16[2,320,256]{2,1,0:T(8,128)(2,1)S(1)}, bf16[2,320,256]{2,1,0:T(8,128)(2,1)S(1)}, u32[]{:S(2)}, u32[]{:S(2)}) collective-permute-start(bf16[2,320,256]{2,1,0:T(8,128)(2,1)S(1)} %get-tuple-element.42), channel_id=1, source_target_pairs={{0,8},{4,12},{8,0},{12,4},{16,24},{20,28},{24,16},{28,20},{1,9},{5... | collective-permute-start | bytes 983048 | tf_op jit(solution)/shard_map/ppermute | solution.py:284
  57.6 5.2 %d_value.1.unread_too.left_ref = bf16[256,1024]{1,0:T(8,128)(2,1)S(1)} custom-call(s32[5]{0:T(128)S(1)} %stack.67.idx, bf16[16,128]{1,0:T(8,128)(2,1)S(1)} %get-tuple-element.43.token, bf16[512,2560]{1,0:T(8,128)(2,1)S(1)} %bitcast.55, bf16[512,2560]{1,0:T(8,128)(2,1)} %collective-permute-done.7.cot_s, bf16[4,8,128,128]{3,2,1,0:T(8,128)(2,1)S(1)} %bitcast.58, ...), custom_call_target="tpu_custom_call" | custom-call | flops 1342177280 | bytes 8126464 | tf_op jit(solution)/shard_map/d_value/pallas_call | solution.py:428
  62.9 0.8 collective-permute-done.10
  63.6 0.1 add_convert_fusion.unread
  63.7 2.1 %assemble.1.w_o = bf16[2560,256]{1,0:T(8,128)(2,1)} custom-call(s32[5]{0:T(128)S(1)} %stack.67.idx, bf16[2,320,256]{2,1,0:T(8,128)(2,1)S(1)} %add_convert_fusion.unread, bf16[256,1024]{1,0:T(8,128)(2,1)S(1)} %d_value.1.unread_too.left_ref, bf16[2,320,256]{2,1,0:T(8,128)(2,1)S(1)} %get-tuple-element.40.rest_0_, ...), custom_call_target="tpu_custom_call" | custom-call | bytes 2621440 | tf_op jit(solution)/shard_map/assemble/pallas_call | solution.py:443
  65.9 0.1 collective-permute-start.12
  66.0 1.4 %collective-permute-start.18 = (bf16[2,320,256]{2,1,0:T(8,128)(2,1)}, bf16[2,320,256]{2,1,0:T(8,128)(2,1)}, u32[]{:S(2)}, u32[]{:S(2)}) collective-permute-start(bf16[2,320,256]{2,1,0:T(8,128)(2,1)} %get-tuple-element.53), channel_id=1, source_target_pairs={{0,8},{4,12},{8,0},{12,4},{16,24},{20,28},{24,16},{28,20},{1,9},{5... | collective-permute-start | bytes 983048 | tf_op jit(solution)/shard_map/ppermute | solution.py:284
  67.4 5.3 %grad_value.1 = (bf16[2,320,256]{2,1,0:T(8,128)(2,1)S(1)}, bf16[2,320,256]{2,1,0:T(8,128)(2,1)S(1)}, bf16[2,320,256]{2,1,0:T(8,128)(2,1)S(1)}, bf16[2,320,256]{2,1,0:T(8,128)(2,1)}) custom-call(s32[5]{0:T(128)S(1)} %stack.67.idx, bf16[2,320,256]{2,1,0:T(8,128)(2,1)S(1)} %add_convert_fusion.unread, bf16[512,2560]{1,0:T(8,128)(2,1)S(1)} %bitcast.52, ...), custom_call_target="tpu_custom_call" | custom-call | flops 1342177280 | bytes 7077888 | tf_op jit(solution)/shard_map/grad_value/pallas_call | solution.py:468
  72.7 0.7 copy-done.8
  73.5 0.7 copy-done.10
  74.2 0.7 collective-permute-start.17
  74.9 3.3 %collective-permute-start.19 = (bf16[2,320,256]{2,1,0:T(8,128)(2,1)S(1)}, bf16[2,320,256]{2,1,0:T(8,128)(2,1)S(1)}, u32[]{:S(2)}, u32[]{:S(2)}) collective-permute-start(bf16[2,320,256]{2,1,0:T(8,128)(2,1)S(1)} %add_convert_fusion.unread), channel_id=1, source_target_pairs={{0,16},{4,20},{8,24},{12,28},{16,0},{20,4},{24,8},{28,12},{1,17},{... | collective-permute-start | bytes 983048 | tf_op jit(solution)/shard_map/ppermute | solution.py:284
  78.2 0.1 pad_add_fusion.idx
  78.3 1.0 copy-done.13
  79.3 3.6 %terms.1 = (bf16[16,128]{1,0:T(8,128)(2,1)S(1)}, bf16[2,256,640]{2,1,0:T(8,128)(2,1)S(1)}, bf16[2,256,640]{2,1,0:T(8,128)(2,1)S(1)}, bf16[4,256,640]{2,1,0:T(8,128)(2,1)S(1)}) custom-call(s32[4]{0:T(128)S(1)} %pad_add_fusion.idx, bf16[512,256]{1,0:T(8,128)(2,1)S(1)} %get-tuple-element.37.mixed_o, bf16[512,256]{1,0:T(8,128)(2,1)S(1)} %copy-done.13, ...), custom_call_target="tpu_custom_call" | custom-call | flops 1342177280 | bytes 5767168 | tf_op jit(solution)/shard_map/terms/pallas_call | solution.py:459
  82.9 8.3 %collective-permute-done.17.got = bf16[2,320,256]{2,1,0:T(8,128)(2,1)S(1)} collective-permute-done((bf16[2,320,256]{2,1,0:T(8,128)(2,1)}, bf16[2,320,256]{2,1,0:T(8,128)(2,1)S(1)}, u32[]{:S(2)}, u32[]{:S(2)}) %collective-permute-start.17) | collective-permute-done | bytes 327712 | tf_op jit(solution)/shard_map/ppermute | solution.py:284
  91.2 1.2 sum.1
  92.4 3.4 %collective-permute-start.20 = (bf16[2,320,256]{2,1,0:T(8,128)(2,1)S(1)}, bf16[2,320,256]{2,1,0:T(8,128)(2,1)S(1)}, u32[]{:S(2)}, u32[]{:S(2)}) collective-permute-start(bf16[2,320,256]{2,1,0:T(8,128)(2,1)S(1)} %get-tuple-element.54), channel_id=1, source_target_pairs={{0,8},{4,12},{8,0},{12,4},{16,24},{20,28},{24,16},{28,20},{1,9},{5... | collective-permute-start | bytes 983048 | tf_op jit(solution)/shard_map/ppermute | solution.py:284
  95.8 2.5 %collective-permute-start.21 = (bf16[2,320,256]{2,1,0:T(8,128)(2,1)S(1)}, bf16[2,320,256]{2,1,0:T(8,128)(2,1)S(1)}, u32[]{:S(2)}, u32[]{:S(2)}) collective-permute-start(bf16[2,320,256]{2,1,0:T(8,128)(2,1)S(1)} %get-tuple-element.55), channel_id=1, source_target_pairs={{0,16},{4,20},{8,24},{12,28},{16,0},{20,4},{24,8},{28,12},{1,17},{... | collective-permute-start | bytes 983048 | tf_op jit(solution)/shard_map/ppermute | solution.py:284
  98.3 0.1 collective-permute-start.23
  98.4 1.6 %collective-permute-start.13 = (bf16[2,256,640]{2,1,0:T(8,128)(2,1)S(1)}, bf16[2,256,640]{2,1,0:T(8,128)(2,1)S(1)}, u32[]{:S(2)}, u32[]{:S(2)}) collective-permute-start(bf16[2,256,640]{2,1,0:T(8,128)(2,1)S(1)} %get-tuple-element.45), channel_id=1, source_target_pairs={{0,1},{1,0},{2,3},{3,2},{4,5},{5,4},{6,7},{7,6},{8,9},{9,8},{10,11... | collective-permute-start | bytes 1966088 | tf_op jit(solution)/shard_map/ppermute | solution.py:295
  100.0 1.5 %collective-permute-start.15 = (bf16[2,256,640]{2,1,0:T(8,128)(2,1)S(1)}, bf16[2,256,640]{2,1,0:T(8,128)(2,1)S(1)}, u32[]{:S(2)}, u32[]{:S(2)}) collective-permute-start(bf16[2,256,640]{2,1,0:T(8,128)(2,1)S(1)} %get-tuple-element.46), channel_id=1, source_target_pairs={{0,2},{1,3},{2,0},{3,1},{4,6},{5,7},{6,4},{7,5},{8,10},{9,11},{10,... | collective-permute-start | bytes 1966088 | tf_op jit(solution)/shard_map/ppermute | solution.py:295
  101.5 0.2 convert_element_type.53
  101.7 7.7 %collective-permute-done.20 = bf16[2,320,256]{2,1,0:T(8,128)(2,1)S(1)} collective-permute-done((bf16[2,320,256]{2,1,0:T(8,128)(2,1)S(1)}, bf16[2,320,256]{2,1,0:T(8,128)(2,1)S(1)}, u32[]{:S(2)}, u32[]{:S(2)}) %collective-permute-start.20) | collective-permute-done | bytes 327712 | tf_op jit(solution)/shard_map/ppermute | solution.py:284
  109.4 3.1 %collective-permute-done.21 = bf16[2,320,256]{2,1,0:T(8,128)(2,1)S(1)} collective-permute-done((bf16[2,320,256]{2,1,0:T(8,128)(2,1)S(1)}, bf16[2,320,256]{2,1,0:T(8,128)(2,1)S(1)}, u32[]{:S(2)}, u32[]{:S(2)}) %collective-permute-start.21) | collective-permute-done | bytes 327712 | tf_op jit(solution)/shard_map/ppermute | solution.py:284
  112.5 0.1 convert_add_fusion
  112.8 0.9 pad_maximum_fusion.2
  113.7 1.9 %collective-permute-done.13 = bf16[2,256,640]{2,1,0:T(8,128)(2,1)S(1)} collective-permute-done((bf16[2,256,640]{2,1,0:T(8,128)(2,1)S(1)}, bf16[2,256,640]{2,1,0:T(8,128)(2,1)S(1)}, u32[]{:S(2)}, u32[]{:S(2)}) %collective-permute-start.13) | collective-permute-done | bytes 655392 | tf_op jit(solution)/shard_map/ppermute | solution.py:295
  115.6 0.1 convert_element_type.54
  115.7 1.1 collective-permute-done.15
  116.8 0.1 convert_element_type.58
  116.9 0.1 fusion.8
  117.0 1.6 %collective-permute-start.14 = (bf16[256,640]{1,0:T(8,128)(2,1)S(1)}, bf16[256,640]{1,0:T(8,128)(2,1)S(1)}, u32[]{:S(2)}, u32[]{:S(2)}) collective-permute-start(bf16[256,640]{1,0:T(8,128)(2,1)S(1)} %get-tuple-element.59), channel_id=1, source_target_pairs={{0,2},{1,3},{2,0},{3,1},{4,6},{5,7},{6,4},{7,5},{8,10},{9,11},{10,... | collective-permute-start | bytes 983048 | tf_op jit(solution)/shard_map/ppermute | solution.py:295
  118.6 0.5 collective-permute-start.16
  119.2 0.9 pad_maximum_fusion.1
  120.1 5.9 %collective-permute-done.14 = bf16[256,640]{1,0:T(8,128)(2,1)S(1)} collective-permute-done((bf16[256,640]{1,0:T(8,128)(2,1)S(1)}, bf16[256,640]{1,0:T(8,128)(2,1)S(1)}, u32[]{:S(2)}, u32[]{:S(2)}) %collective-permute-start.14) | collective-permute-done | bytes 327712 | tf_op jit(solution)/shard_map/ppermute | solution.py:295
  126.0 1.2 collective-permute-done.16
  127.3 0.2 fusion.7
  127.5 0.9 pad_maximum_fusion
  (43 shorter events, 0.5 us)
Async XLA Ops:
  0.6 3.2 %copy-start = (bf16[2,2,128,2560]{3,2,1,0:T(8,128)(2,1)S(1)}, bf16[2,2,128,2560]{3,2,1,0:T(8,128)(2,1)}, u32[]{:S(2)}) copy-start(bf16[2,2,128,2560]{3,2,1,0:T(8,128)(2,1)} %param.5) | copy-start | bytes 7864324
  2.1 1.8 %collective-permute-start = (bf16[2,320,256]{2,1,0:T(8,128)(2,1)S(1)}, bf16[2,320,256]{2,1,0:T(8,128)(2,1)S(1)}, u32[]{:S(2)}, u32[]{:S(2)}) collective-permute-start(bf16[2,320,256]{2,1,0:T(8,128)(2,1)S(1)} %get-tuple-element.66), channel_id=1, source_target_pairs={{0,4},{4,0},{8,12},{12,8},{16,20},{20,16},{24,28},{28,24},{1,5},{5... | collective-permute-start | bytes 983048 | tf_op jit(solution)/shard_map/ppermute | solution.py:292
  3.8 25.7 %collective-permute-start.1 = (bf16[512,2560]{1,0:T(8,128)(2,1)S(1)}, bf16[512,2560]{1,0:T(8,128)(2,1)}, u32[]{:S(2)}, u32[]{:S(2)}) collective-permute-start(bf16[512,2560]{1,0:T(8,128)(2,1)S(1)} %bitcast.50), channel_id=1, source_target_pairs={{0,4},{4,0},{8,12},{12,8},{16,20},{20,16},{24,28},{28,24},{1,5},{5... | collective-permute-start | bytes 7864328 | tf_op jit(solution)/shard_map/ppermute | solution.py:292
  4.2 44.9 %collective-permute-start.7 = (bf16[512,2560]{1,0:T(8,128)(2,1)}, bf16[512,2560]{1,0:T(8,128)(2,1)}, u32[]{:S(2)}, u32[]{:S(2)}) collective-permute-start(bf16[512,2560]{1,0:T(8,128)(2,1)} %bitcast.53), channel_id=1, source_target_pairs={{0,4},{4,0},{8,12},{12,8},{16,20},{20,16},{24,28},{28,24},{1,5},{5... | collective-permute-start | bytes 7864328 | tf_op jit(solution)/shard_map/ppermute | solution.py:292
  4.4 25.2 %collective-permute-start.2 = (bf16[4,8,128,128]{3,2,1,0:T(8,128)(2,1)}, bf16[4,8,128,128]{3,2,1,0:T(8,128)(2,1)}, u32[]{:S(2)}, u32[]{:S(2)}) collective-permute-start(bf16[4,8,128,128]{3,2,1,0:T(8,128)(2,1)} %bitcast.56), channel_id=1, source_target_pairs={{0,4},{4,0},{8,12},{12,8},{16,20},{20,16},{24,28},{28,24},{1,5},{5... | collective-permute-start | bytes 3145736 | tf_op jit(solution)/shard_map/ppermute | solution.py:292
  4.8 19.2 %collective-permute-start.4 = (bf16[2,320,256]{2,1,0:T(8,128)(2,1)S(1)}, bf16[2,320,256]{2,1,0:T(8,128)(2,1)S(1)}, u32[]{:S(2)}, u32[]{:S(2)}) collective-permute-start(bf16[2,320,256]{2,1,0:T(8,128)(2,1)S(1)} %pad_maximum_fusion.5.rest_0_), channel_id=1, source_target_pairs={{0,16},{4,20},{8,24},{12,28},{16,0},{20,4},{24,8},{28,12},{1,17},{... | collective-permute-start | bytes 983048 | tf_op jit(solution)/shard_map/ppermute | solution.py:284
  8.6 15.6 %collective-permute-start.3 = (bf16[2,320,256]{2,1,0:T(8,128)(2,1)S(1)}, bf16[2,320,256]{2,1,0:T(8,128)(2,1)S(1)}, u32[]{:S(2)}, u32[]{:S(2)}) collective-permute-start(bf16[2,320,256]{2,1,0:T(8,128)(2,1)S(1)} %pad_maximum_fusion.5.rest_0_), channel_id=1, source_target_pairs={{0,8},{4,12},{8,0},{12,4},{16,24},{20,28},{24,16},{28,20},{1,9},{5... | collective-permute-start | bytes 983048 | tf_op jit(solution)/shard_map/ppermute | solution.py:284
  25.0 0.7 copy-start.4
  25.7 17.9 %collective-permute-start.5 = (bf16[2,320,256]{2,1,0:T(8,128)(2,1)}, bf16[2,320,256]{2,1,0:T(8,128)(2,1)}, u32[]{:S(2)}, u32[]{:S(2)}) collective-permute-start(bf16[2,320,256]{2,1,0:T(8,128)(2,1)} %get-tuple-element.33.rest_2_), channel_id=1, source_target_pairs={{0,8},{4,12},{8,0},{12,4},{16,24},{20,28},{24,16},{28,20},{1,9},{5... | collective-permute-start | bytes 983048 | tf_op jit(solution)/shard_map/ppermute | solution.py:284
  27.2 19.1 %collective-permute-start.9 = (bf16[2,320,256]{2,1,0:T(8,128)(2,1)S(1)}, bf16[2,320,256]{2,1,0:T(8,128)(2,1)S(1)}, u32[]{:S(2)}, u32[]{:S(2)}) collective-permute-start(bf16[2,320,256]{2,1,0:T(8,128)(2,1)S(1)} %get-tuple-element.40.rest_0_), channel_id=1, source_target_pairs={{0,16},{4,20},{8,24},{12,28},{16,0},{20,4},{24,8},{28,12},{1,17},{... | collective-permute-start | bytes 983048 | tf_op jit(solution)/shard_map/ppermute | solution.py:284
  29.6 19.5 %collective-permute-start.8 = (bf16[2,320,256]{2,1,0:T(8,128)(2,1)S(1)}, bf16[2,320,256]{2,1,0:T(8,128)(2,1)S(1)}, u32[]{:S(2)}, u32[]{:S(2)}) collective-permute-start(bf16[2,320,256]{2,1,0:T(8,128)(2,1)S(1)} %get-tuple-element.40.rest_0_), channel_id=1, source_target_pairs={{0,8},{4,12},{8,0},{12,4},{16,24},{20,28},{24,16},{28,20},{1,9},{5... | collective-permute-start | bytes 983048 | tf_op jit(solution)/shard_map/ppermute | solution.py:284
  29.6 1.2 copy-start.2
  30.8 1.0 copy-start.5
  43.6 5.6 %copy-start.1 = (bf16[2,2,128,2560]{3,2,1,0:T(8,128)(2,1)S(1)}, bf16[2,2,128,2560]{3,2,1,0:T(8,128)(2,1)}, u32[]{:S(2)}) copy-start(bf16[2,2,128,2560]{3,2,1,0:T(8,128)(2,1)} %param.7) | copy-start | bytes 7864324
  46.2 2.9 %collective-permute-start.6 = (bf16[512,256]{1,0:T(8,128)(2,1)S(1)}, bf16[512,256]{1,0:T(8,128)(2,1)S(1)}, u32[]{:S(2)}, u32[]{:S(2)}) collective-permute-start(bf16[512,256]{1,0:T(8,128)(2,1)S(1)} %get-tuple-element.38.mixed_s), channel_id=1, source_target_pairs={{0,4},{4,0},{8,12},{12,8},{16,20},{20,16},{24,28},{28,24},{1,5},{5... | collective-permute-start | bytes 786440 | tf_op jit(solution)/shard_map/ppermute | solution.py:292
  46.3 11.3 %collective-permute-start.11 = (bf16[2,320,256]{2,1,0:T(8,128)(2,1)S(1)}, bf16[2,320,256]{2,1,0:T(8,128)(2,1)S(1)}, u32[]{:S(2)}, u32[]{:S(2)}) collective-permute-start(bf16[2,320,256]{2,1,0:T(8,128)(2,1)S(1)} %collective-permute-done.9.rest_2_), channel_id=1, source_target_pairs={{0,8},{4,12},{8,0},{12,4},{16,24},{20,28},{24,16},{28,20},{1,9},{5... | collective-permute-start | bytes 983048 | tf_op jit(solution)/shard_map/ppermute | solution.py:284
  49.1 5.3 %copy-start.12 = (bf16[512,256]{1,0:T(8,128)(2,1)}, bf16[512,256]{1,0:T(8,128)(2,1)S(1)}, u32[]{:S(2)}) copy-start(bf16[512,256]{1,0:T(8,128)(2,1)S(1)} %collective-permute-done.6.rest_0_.mixed_r) | copy-start | bytes 786436
  49.1 8.5 %copy-start.3 = (bf16[2,2,8,128,128]{4,3,2,1,0:T(8,128)(2,1)S(1)}, bf16[2,2,8,128,128]{4,3,2,1,0:T(8,128)(2,1)}, u32[]{:S(2)}) copy-start(bf16[2,2,8,128,128]{4,3,2,1,0:T(8,128)(2,1)} %param.6) | copy-start | bytes 3145732
  54.4 0.7 copy-start.6
  55.2 8.5 %collective-permute-start.10 = (bf16[2,320,256]{2,1,0:T(8,128)(2,1)S(1)}, bf16[2,320,256]{2,1,0:T(8,128)(2,1)S(1)}, u32[]{:S(2)}, u32[]{:S(2)}) collective-permute-start(bf16[2,320,256]{2,1,0:T(8,128)(2,1)S(1)} %get-tuple-element.42), channel_id=1, source_target_pairs={{0,8},{4,12},{8,0},{12,4},{16,24},{20,28},{24,16},{28,20},{1,9},{5... | collective-permute-start | bytes 983048 | tf_op jit(solution)/shard_map/ppermute | solution.py:284
  65.9 12.4 %collective-permute-start.12 = (bf16[2560,256]{1,0:T(8,128)(2,1)}, bf16[2560,256]{1,0:T(8,128)(2,1)}, u32[]{:S(2)}, u32[]{:S(2)}) collective-permute-start(bf16[2560,256]{1,0:T(8,128)(2,1)} %assemble.1.w_o), channel_id=1, source_target_pairs={{0,4},{4,0},{8,12},{12,8},{16,20},{20,16},{24,28},{28,24},{1,5},{5... | collective-permute-start | bytes 3932168 | tf_op jit(solution)/shard_map/ppermute | solution.py:292
  66.0 16.9 %collective-permute-start.18 = (bf16[2,320,256]{2,1,0:T(8,128)(2,1)}, bf16[2,320,256]{2,1,0:T(8,128)(2,1)}, u32[]{:S(2)}, u32[]{:S(2)}) collective-permute-start(bf16[2,320,256]{2,1,0:T(8,128)(2,1)} %get-tuple-element.53), channel_id=1, source_target_pairs={{0,8},{4,12},{8,0},{12,4},{16,24},{20,28},{24,16},{28,20},{1,9},{5... | collective-permute-start | bytes 983048 | tf_op jit(solution)/shard_map/ppermute | solution.py:284
  72.7 0.7 copy-start.8
  73.5 0.7 copy-start.10
  74.2 17.0 %collective-permute-start.17 = (bf16[2,320,256]{2,1,0:T(8,128)(2,1)}, bf16[2,320,256]{2,1,0:T(8,128)(2,1)S(1)}, u32[]{:S(2)}, u32[]{:S(2)}) collective-permute-start(bf16[2,320,256]{2,1,0:T(8,128)(2,1)} %get-tuple-element.50), channel_id=1, source_target_pairs={{0,8},{4,12},{8,0},{12,4},{16,24},{20,28},{24,16},{28,20},{1,9},{5... | collective-permute-start | bytes 983048 | tf_op jit(solution)/shard_map/ppermute | solution.py:284
  74.9 16.3 %collective-permute-start.19 = (bf16[2,320,256]{2,1,0:T(8,128)(2,1)S(1)}, bf16[2,320,256]{2,1,0:T(8,128)(2,1)S(1)}, u32[]{:S(2)}, u32[]{:S(2)}) collective-permute-start(bf16[2,320,256]{2,1,0:T(8,128)(2,1)S(1)} %add_convert_fusion.unread), channel_id=1, source_target_pairs={{0,16},{4,20},{8,24},{12,28},{16,0},{20,4},{24,8},{28,12},{1,17},{... | collective-permute-start | bytes 983048 | tf_op jit(solution)/shard_map/ppermute | solution.py:284
  78.3 12.9 %copy-start.7 = (bf16[2,320,256]{2,1,0:T(8,128)(2,1)S(1)}, bf16[2,320,256]{2,1,0:T(8,128)(2,1)}, u32[]{:S(2)}) copy-start(bf16[2,320,256]{2,1,0:T(8,128)(2,1)} %copy-done.6) | copy-start | bytes 983044
  78.3 12.9 %copy-start.9 = (bf16[2,320,256]{2,1,0:T(8,128)(2,1)S(1)}, bf16[2,320,256]{2,1,0:T(8,128)(2,1)}, u32[]{:S(2)}) copy-start(bf16[2,320,256]{2,1,0:T(8,128)(2,1)} %copy-done.8) | copy-start | bytes 983044
  78.3 13.0 %copy-start.11 = (bf16[2,320,256]{2,1,0:T(8,128)(2,1)S(1)}, bf16[2,320,256]{2,1,0:T(8,128)(2,1)}, u32[]{:S(2)}) copy-start(bf16[2,320,256]{2,1,0:T(8,128)(2,1)} %copy-done.10) | copy-start | bytes 983044
  78.3 1.0 copy-start.13
  92.4 17.0 %collective-permute-start.20 = (bf16[2,320,256]{2,1,0:T(8,128)(2,1)S(1)}, bf16[2,320,256]{2,1,0:T(8,128)(2,1)S(1)}, u32[]{:S(2)}, u32[]{:S(2)}) collective-permute-start(bf16[2,320,256]{2,1,0:T(8,128)(2,1)S(1)} %get-tuple-element.54), channel_id=1, source_target_pairs={{0,8},{4,12},{8,0},{12,4},{16,24},{20,28},{24,16},{28,20},{1,9},{5... | collective-permute-start | bytes 983048 | tf_op jit(solution)/shard_map/ppermute | solution.py:284
  95.8 16.6 %collective-permute-start.21 = (bf16[2,320,256]{2,1,0:T(8,128)(2,1)S(1)}, bf16[2,320,256]{2,1,0:T(8,128)(2,1)S(1)}, u32[]{:S(2)}, u32[]{:S(2)}) collective-permute-start(bf16[2,320,256]{2,1,0:T(8,128)(2,1)S(1)} %get-tuple-element.55), channel_id=1, source_target_pairs={{0,16},{4,20},{8,24},{12,28},{16,0},{20,4},{24,8},{28,12},{1,17},{... | collective-permute-start | bytes 983048 | tf_op jit(solution)/shard_map/ppermute | solution.py:284
  98.3 14.4 %collective-permute-start.23 = (f32[320,256]{1,0:T(8,128)S(1)}, f32[320,256]{1,0:T(8,128)S(1)}, u32[]{:S(2)}, u32[]{:S(2)}) collective-permute-start(f32[320,256]{1,0:T(8,128)S(1)} %slice_bitcast_fusion.2), channel_id=1, source_target_pairs={{0,4},{4,0},{8,12},{12,8},{16,20},{20,16},{24,28},{28,24},{1,5},{5... | collective-permute-start | bytes 983048 | tf_op jit(solution)/shard_map/ppermute | solution.py:292
  98.4 17.1 %collective-permute-start.13 = (bf16[2,256,640]{2,1,0:T(8,128)(2,1)S(1)}, bf16[2,256,640]{2,1,0:T(8,128)(2,1)S(1)}, u32[]{:S(2)}, u32[]{:S(2)}) collective-permute-start(bf16[2,256,640]{2,1,0:T(8,128)(2,1)S(1)} %get-tuple-element.45), channel_id=1, source_target_pairs={{0,1},{1,0},{2,3},{3,2},{4,5},{5,4},{6,7},{7,6},{8,9},{9,8},{10,11... | collective-permute-start | bytes 1966088 | tf_op jit(solution)/shard_map/ppermute | solution.py:295
  100.0 16.8 %collective-permute-start.15 = (bf16[2,256,640]{2,1,0:T(8,128)(2,1)S(1)}, bf16[2,256,640]{2,1,0:T(8,128)(2,1)S(1)}, u32[]{:S(2)}, u32[]{:S(2)}) collective-permute-start(bf16[2,256,640]{2,1,0:T(8,128)(2,1)S(1)} %get-tuple-element.46), channel_id=1, source_target_pairs={{0,2},{1,3},{2,0},{3,1},{4,6},{5,7},{6,4},{7,5},{8,10},{9,11},{10,... | collective-permute-start | bytes 1966088 | tf_op jit(solution)/shard_map/ppermute | solution.py:295
  112.6 6.5 %collective-permute-start.22 = (f32[320,256]{1,0:T(8,128)S(1)}, f32[320,256]{1,0:T(8,128)S(1)}, u32[]{:S(2)}, u32[]{:S(2)}) collective-permute-start(f32[320,256]{1,0:T(8,128)S(1)} %slice_bitcast_fusion), channel_id=1, source_target_pairs={{0,4},{4,0},{8,12},{12,8},{16,20},{20,16},{24,28},{28,24},{1,5},{5... | collective-permute-start | bytes 983048 | tf_op jit(solution)/shard_map/ppermute | solution.py:292
  117.0 9.0 %collective-permute-start.14 = (bf16[256,640]{1,0:T(8,128)(2,1)S(1)}, bf16[256,640]{1,0:T(8,128)(2,1)S(1)}, u32[]{:S(2)}, u32[]{:S(2)}) collective-permute-start(bf16[256,640]{1,0:T(8,128)(2,1)S(1)} %get-tuple-element.59), channel_id=1, source_target_pairs={{0,2},{1,3},{2,0},{3,1},{4,6},{5,7},{6,4},{7,5},{8,10},{9,11},{10,... | collective-permute-start | bytes 983048 | tf_op jit(solution)/shard_map/ppermute | solution.py:295
  118.6 8.7 %collective-permute-start.16 = (bf16[256,640]{1,0:T(8,128)(2,1)S(1)}, bf16[256,640]{1,0:T(8,128)(2,1)S(1)}, u32[]{:S(2)}, u32[]{:S(2)}) collective-permute-start(bf16[256,640]{1,0:T(8,128)(2,1)S(1)} %get-tuple-element.60), channel_id=1, source_target_pairs={{0,1},{1,0},{2,3},{3,2},{4,5},{5,4},{6,7},{7,6},{8,9},{9,8},{10,11... | collective-permute-start | bytes 983048 | tf_op jit(solution)/shard_map/ppermute | solution.py:295

commit v18 on v16

--- a/solution.py
+++ b/solution.py
@@ -47,11 +47,27 @@
         out[1] = jnp.where(core == 0, high, low)
 
 
-def gradient_rows(left, right_ref, rows_ref, step):
-    width = right_ref.shape[1]
-    for start in range(0, width, step):
-        part = dot(left, right_ref[:, start : start + step])
-        rows_ref[start : start + step, :] = part.T.astype(BF16)
+def chunk_copies(own, other, right_ref, sems):
+    tokens, width = own.shape
+    step = width // sems.shape[0]
+    copies = []
+    for j in range(sems.shape[0]):
+        columns = pl.ds(j * step, step)
+        pairs = [
+            (own.at[:, columns], right_ref.at[pl.ds(0, tokens), columns]),
+            (other.at[:, columns], right_ref.at[pl.ds(tokens, tokens), columns]),
+        ]
+        copies.append(begin(pairs, sems.at[j]))
+    return copies
+
+
+def gradient_rows(left, right_ref, copies, rows_ref):
+    step = right_ref.shape[1] // len(copies)
+    for j, chunk in enumerate(copies):
+        for copy in chunk:
+            copy.wait()
+        part = dot(left, right_ref[:, j * step : (j + 1) * step])
+        rows_ref[j * step : (j + 1) * step, :] = part.T.astype(BF16)
 
 
 def head_pairs(heads):
@@ -173,14 +189,8 @@
 def gradient_kernel(idx, token, unread, right_o, right_s, left_ref, *rest):
     del token, unread
     outs, (right_v, grad_v, sems) = rest[:-3], rest[-3:]
-    tokens, _ = right_o.shape
-    copies = begin(
-        [(right_o, right_v.at[pl.ds(0, tokens)]), (right_s, right_v.at[pl.ds(tokens, tokens)])],
-        sems,
-    )
-    copies[0].wait()
-    copies[1].wait()
-    gradient_rows(left_ref[...], right_v, grad_v, 640)
+    copies = chunk_copies(right_o, right_s, right_v, sems)
+    gradient_rows(left_ref[...], right_v, copies, grad_v)
     hand_out(idx, 1, grad_v, outs)
 
 
@@ -209,14 +219,10 @@
     token, *outs, cot_v, left_v, grad_v, sems = rest[n_unread:]
     token[...] = jnp.zeros_like(token)
     tokens, _ = cot_o.shape
-    copies = begin(
-        [(cot_o, cot_v.at[pl.ds(0, tokens)]), (cot_s, cot_v.at[pl.ds(tokens, tokens)])], sems
-    )
+    copies = chunk_copies(cot_o, cot_s, cot_v, sems)
     left_v[:, :tokens] = mixed_o[...].astype(F32).T.astype(BF16)
     left_v[:, tokens:] = mixed_s[...].astype(F32).T.astype(BF16)
-    copies[0].wait()
-    copies[1].wait()
-    gradient_rows(left_v[...], cot_v, grad_v, 640)
+    gradient_rows(left_v[...], cot_v, copies, grad_v)
     hand_out(idx, 1, grad_v, outs)
 
 
@@ -419,7 +425,7 @@
             "grad_out",
             [SMEM] + [ANY] * 2 + [VMEM] * 2 + [ANY] * len(unread),
             [(16, 128)] + send_shapes,
-            [both, left_tokens, rows, pltpu.SemaphoreType.DMA((2,))],
+            [both, left_tokens, rows, pltpu.SemaphoreType.DMA((4, 2))],
             flops,
             2 * (2 * cot.size + 2 * tokens * cols + width * cols),
         )(idx, cot, cot_s, mixed_o, mixed_s, *unread)
@@ -469,7 +475,7 @@
             "grad_value",
             [SMEM] + [ANY] * 4 + [VMEM],
             send_shapes,
-            [both, rows, pltpu.SemaphoreType.DMA((2,))],
+            [both, rows, pltpu.SemaphoreType.DMA((4, 2))],
             flops,
             2 * (2 * act.size + 2 * tokens * cols + width * cols),
         )(idx, token, out_onward, act, act_s, left)

time: 116 us -> 116 us (level)
  no operation moved by 1% of the time
where the time goes in v18:
time: 116 us; the launch traced here: 115 us
  waiting for transfers between devices  48.6 us (42%)
  Pallas kernels  28.4 us (24%)
  starting transfers between devices  24.4 us (21%)
  local copies, waits for them, and re-layouts  8.78 us (8%)
  other arithmetic  3.96 us (3%)
    ppermute x12, waiting for transfers between devices, move(): lax.ppermute(x, 'wide', [(2 * s + c, 2 * d + c) for s, d in pairs for c i...  46.8 us
    ppermute x12, starting transfers between devices, move(): lax.ppermute(x, 'wide', [(2 * s + c, 2 * d + c) for s, d in pairs for c i...  18 us
    unnamed x30, local copies, waits for them, and re-layouts  7.26 us
    pallas_call x1, Pallas kernels, body(): call(functools.partial(d_value_kernel, n_slots), 'd_value', [SMEM] + [ANY...  5.24 us
    pallas_call x1, Pallas kernels, body(): call(functools.partial(part_kernel, n_slots - 1), 'value_ahead', [SMEM] +...  4.9 us
    ppermute x4, starting transfers between devices, flip(): return lax.ppermute(x, 'node', [(i, i ^ j) for i in range(n_node)])  4.71 us
    pallas_call x1, Pallas kernels, body(): call(functools.partial(grad_out_kernel, len(unread)), 'grad_out', [SMEM]...  4.47 us
    pallas_call x1, Pallas kernels, body(): call(gradient_kernel, 'grad_value', [SMEM] + [ANY] * 4 + [VMEM], send_sha...  4.45 us
  transfers between devices with their start and end apart: 24, of which 12 were waited for; matrix products, arithmetic and copies ran while one was open for 3% of the time, Pallas kernels for 23%

profile of v18, /device:TPU:0, one launch (start us, length us, event | category | flops | bytes accessed | tf_op | source)
XLA Modules:
  0.0 115.1 jit_solution(8900853383761633316)
XLA Ops:
  0.7 1.3 %slice_bitcast_fusion.5 = (bf16[1,320,256]{2,1,0:T(8,128)(2,1)S(1)}, bf16[1,320,256]{2,1,0:T(8,128)(2,1)S(1)}, bf16[1,320,256]{2,1,0:T(8,128)(2,1)S(1)}, bf16[1,320,256]{2,1,0:T(8,128)(2,1)S(1)}) fusion(bf16[320,512]{1,0:T(8,128)(2,1)} %param.8, bf16[320,512]{1,0:T(8,128)(2,1)} %param.9), kind=kLoop, calls=%fused_computation.34 | loop fusion | bytes 1310720 | tf_op jit(solution)/shard_map/stack | solution.py:305
  2.1 0.5 collective-permute-start
  2.6 1.3 %collective-permute-done = bf16[2,320,256]{2,1,0:T(8,128)(2,1)S(1)} collective-permute-done((bf16[2,320,256]{2,1,0:T(8,128)(2,1)S(1)}, bf16[2,320,256]{2,1,0:T(8,128)(2,1)S(1)}, u32[]{:S(2)}, u32[]{:S(2)}) %collective-permute-start) | collective-permute-done | bytes 327712 | tf_op jit(solution)/shard_map/ppermute | solution.py:297
  3.8 0.4 collective-permute-start.1
  4.2 0.1 collective-permute-start.7
  4.4 0.4 collective-permute-start.2
  4.8 2.8 %collective-permute-start.3 = (bf16[2,320,256]{2,1,0:T(8,128)(2,1)S(1)}, bf16[2,320,256]{2,1,0:T(8,128)(2,1)S(1)}, u32[]{:S(2)}, u32[]{:S(2)}) collective-permute-start(bf16[2,320,256]{2,1,0:T(8,128)(2,1)S(1)} %pad_maximum_fusion.5.rest_0_), channel_id=1, source_target_pairs={{0,8},{4,12},{8,0},{12,4},{16,24},{20,28},{24,16},{28,20},{1,9},{5... | collective-permute-start | bytes 983048 | tf_op jit(solution)/shard_map/ppermute | solution.py:289
  7.6 2.6 %collective-permute-start.4 = (bf16[2,320,256]{2,1,0:T(8,128)(2,1)S(1)}, bf16[2,320,256]{2,1,0:T(8,128)(2,1)S(1)}, u32[]{:S(2)}, u32[]{:S(2)}) collective-permute-start(bf16[2,320,256]{2,1,0:T(8,128)(2,1)S(1)} %pad_maximum_fusion.5.rest_0_), channel_id=1, source_target_pairs={{0,16},{4,20},{8,24},{12,28},{16,0},{20,4},{24,8},{28,12},{1,17},{... | collective-permute-start | bytes 983048 | tf_op jit(solution)/shard_map/ppermute | solution.py:289
  10.2 12.5 %collective-permute-done.3.unread.rest_1_ = bf16[2,320,256]{2,1,0:T(8,128)(2,1)S(1)} collective-permute-done((bf16[2,320,256]{2,1,0:T(8,128)(2,1)S(1)}, bf16[2,320,256]{2,1,0:T(8,128)(2,1)S(1)}, u32[]{:S(2)}, u32[]{:S(2)}) %collective-permute-start.3) | collective-permute-done | bytes 327712 | tf_op jit(solution)/shard_map/ppermute | solution.py:289
  22.8 2.5 %collective-permute-done.4.first = bf16[2,320,256]{2,1,0:T(8,128)(2,1)S(1)} collective-permute-done((bf16[2,320,256]{2,1,0:T(8,128)(2,1)S(1)}, bf16[2,320,256]{2,1,0:T(8,128)(2,1)S(1)}, u32[]{:S(2)}, u32[]{:S(2)}) %collective-permute-start.4) | collective-permute-done | bytes 327712 | tf_op jit(solution)/shard_map/ppermute | solution.py:289
  25.3 0.8 relay.1
  26.1 0.7 copy-done.6
  26.8 0.4 collective-permute-start.5
  27.2 0.1 stack.67.idx
  27.3 1.6 %collective-permute-start.8 = (bf16[2,320,256]{2,1,0:T(8,128)(2,1)S(1)}, bf16[2,320,256]{2,1,0:T(8,128)(2,1)S(1)}, u32[]{:S(2)}, u32[]{:S(2)}) collective-permute-start(bf16[2,320,256]{2,1,0:T(8,128)(2,1)S(1)} %get-tuple-element.40.rest_0_), channel_id=1, source_target_pairs={{0,8},{4,12},{8,0},{12,4},{16,24},{20,28},{24,16},{28,20},{1,9},{5... | collective-permute-start | bytes 983048 | tf_op jit(solution)/shard_map/ppermute | solution.py:289
  28.9 1.1 collective-permute-start.9
  30.0 1.2 %copy-done.2 = bf16[2,2,8,128,128]{4,3,2,1,0:T(8,128)(2,1)S(1)} copy-done((bf16[2,2,8,128,128]{4,3,2,1,0:T(8,128)(2,1)S(1)}, bf16[2,2,8,128,128]{4,3,2,1,0:T(8,128)(2,1)}, u32[]{:S(2)}) %copy-start.2) | copy-done | bytes 1048600
  31.2 1.0 copy-done.7
  32.2 4.9 %value_ahead.1 = (f32[2,512,256]{2,1,0:T(8,128)S(1)}, bf16[2,512,640]{2,1,0:T(8,128)(2,1)S(1)}, bf16[2,4,4,128,128]{4,3,2,1,0:T(8,128)(2,1)S(1)}) custom-call(s32[5]{0:T(128)S(1)} %stack.67.idx, bf16[512,2560]{1,0:T(8,128)(2,1)S(1)} %bitcast.51, bf16[512,2560]{1,0:T(8,128)(2,1)} %collective-permute-done.1.x_s.right_s, bf16[4,8,128,128]{3,2,1,0:T(8,128)(2,1)S(1)} %bitcast.57, ...), custom_call_target="tpu_custom_call" | custom-call | flops 1342177280 | bytes 11272192 | tf_op jit(solution)/shard_map/value_ahead/pallas_call | solution.py:388
  37.1 7.3 %collective-permute-done.5.slot = bf16[2,320,256]{2,1,0:T(8,128)(2,1)} collective-permute-done((bf16[2,320,256]{2,1,0:T(8,128)(2,1)}, bf16[2,320,256]{2,1,0:T(8,128)(2,1)}, u32[]{:S(2)}, u32[]{:S(2)}) %collective-permute-start.5) | collective-permute-done | bytes 327712 | tf_op jit(solution)/shard_map/ppermute | solution.py:289
  44.4 2.7 %mixed.1 = (bf16[512,256]{1,0:T(8,128)(2,1)S(1)}, bf16[512,256]{1,0:T(8,128)(2,1)S(1)}) custom-call(s32[5]{0:T(128)S(1)} %stack.67.idx, f32[2,512,256]{2,1,0:T(8,128)S(1)} %get-tuple-element.34.part, bf16[2,512,640]{2,1,0:T(8,128)(2,1)S(1)} %get-tuple-element.35.last, bf16[2,4,4,128,128]{4,3,2,1,0:T(8,128)(2,1)S(1)} %get-tuple-element.36.weights, ...), custom_call_target="tpu_custom_call" | custom-call | flops 335544320 | bytes 3932160 | tf_op jit(solution)/shard_map/mixed/pallas_call | solution.py:401
  47.1 0.1 collective-permute-start.6
  47.2 0.9 collective-permute-done.9.rest_2_
  48.1 3.1 %collective-permute-start.11 = (bf16[2,320,256]{2,1,0:T(8,128)(2,1)S(1)}, bf16[2,320,256]{2,1,0:T(8,128)(2,1)S(1)}, u32[]{:S(2)}, u32[]{:S(2)}) collective-permute-start(bf16[2,320,256]{2,1,0:T(8,128)(2,1)S(1)} %collective-permute-done.9.rest_2_), channel_id=1, source_target_pairs={{0,8},{4,12},{8,0},{12,4},{16,24},{20,28},{24,16},{28,20},{1,9},{5... | collective-permute-start | bytes 983048 | tf_op jit(solution)/shard_map/ppermute | solution.py:289
  51.2 4.5 %grad_out.1 = (bf16[16,128]{1,0:T(8,128)(2,1)S(1)}, bf16[2,320,256]{2,1,0:T(8,128)(2,1)S(1)}, bf16[2,320,256]{2,1,0:T(8,128)(2,1)S(1)}, bf16[2,320,256]{2,1,0:T(8,128)(2,1)S(1)}, bf16[2,320,256]{2,1,0:T(8,128)(2,1)S(1)}) custom-call(s32[5]{0:T(128)S(1)} %stack.67.idx, bf16[512,2560]{1,0:T(8,128)(2,1)S(1)} %bitcast.54, ...), custom_call_target="tpu_custom_call" | custom-call | flops 1342177280 | bytes 7077888 | tf_op jit(solution)/shard_map/grad_out/pallas_call | solution.py:423
  55.7 0.7 copy-done.8
  56.4 0.7 copy-done.14
  57.2 0.7 collective-permute-done.11.rest_3_
  57.9 5.2 %d_value.1.unread_too.left_ref = bf16[256,1024]{1,0:T(8,128)(2,1)S(1)} custom-call(s32[5]{0:T(128)S(1)} %stack.67.idx, bf16[16,128]{1,0:T(8,128)(2,1)S(1)} %get-tuple-element.43.token, bf16[512,2560]{1,0:T(8,128)(2,1)S(1)} %bitcast.55, bf16[512,2560]{1,0:T(8,128)(2,1)} %collective-permute-done.7.cot_s, bf16[4,8,128,128]{3,2,1,0:T(8,128)(2,1)S(1)} %bitcast.58, ...), custom_call_target="tpu_custom_call" | custom-call | flops 1342177280 | bytes 8126464 | tf_op jit(solution)/shard_map/d_value/pallas_call | solution.py:433
  63.1 2.0 %collective-permute-done.10 = bf16[2,320,256]{2,1,0:T(8,128)(2,1)S(1)} collective-permute-done((bf16[2,320,256]{2,1,0:T(8,128)(2,1)S(1)}, bf16[2,320,256]{2,1,0:T(8,128)(2,1)S(1)}, u32[]{:S(2)}, u32[]{:S(2)}) %collective-permute-start.10) | collective-permute-done | bytes 327712 | tf_op jit(solution)/shard_map/ppermute | solution.py:289
  65.1 0.1 add_convert_fusion.unread
  65.2 1.0 copy-done.5
  66.2 2.1 %assemble.1.w_o = bf16[2560,256]{1,0:T(8,128)(2,1)} custom-call(s32[5]{0:T(128)S(1)} %stack.67.idx, bf16[2,320,256]{2,1,0:T(8,128)(2,1)S(1)} %add_convert_fusion.unread, bf16[256,1024]{1,0:T(8,128)(2,1)S(1)} %d_value.1.unread_too.left_ref, bf16[2,320,256]{2,1,0:T(8,128)(2,1)S(1)} %copy-done.5, bf16[2,320,256]{2,1,0:T(8,128)(2,1)S(1)} %collective-permute-done.8.rest_1_, ...), custom_call_target="tpu_custom_call" | custom-call | bytes 2621440 | tf_op jit(solution)/shard_map/assemble/pallas_call | solution.py:448
  68.3 0.1 collective-permute-start.12
  68.4 0.1 pad_add_fusion.idx
  68.5 1.3 %collective-permute-start.18 = (bf16[2,320,256]{2,1,0:T(8,128)(2,1)}, bf16[2,320,256]{2,1,0:T(8,128)(2,1)S(1)}, u32[]{:S(2)}, u32[]{:S(2)}) collective-permute-start(bf16[2,320,256]{2,1,0:T(8,128)(2,1)} %copy-done.14), channel_id=1, source_target_pairs={{0,8},{4,12},{8,0},{12,4},{16,24},{20,28},{24,16},{28,20},{1,9},{5... | collective-permute-start | bytes 983048 | tf_op jit(solution)/shard_map/ppermute | solution.py:289
  69.8 1.4 %collective-permute-start.19 = (bf16[2,320,256]{2,1,0:T(8,128)(2,1)S(1)}, bf16[2,320,256]{2,1,0:T(8,128)(2,1)S(1)}, u32[]{:S(2)}, u32[]{:S(2)}) collective-permute-start(bf16[2,320,256]{2,1,0:T(8,128)(2,1)S(1)} %add_convert_fusion.unread), channel_id=1, source_target_pairs={{0,16},{4,20},{8,24},{12,28},{16,0},{20,4},{24,8},{28,12},{1,17},{... | collective-permute-start | bytes 983048 | tf_op jit(solution)/shard_map/ppermute | solution.py:289
  71.2 0.6 collective-permute-done.12.w_r
  71.8 0.9 copy-done.11
  72.7 0.9 copy-done.13
  73.7 3.6 %terms.1 = (bf16[16,128]{1,0:T(8,128)(2,1)S(1)}, bf16[2,256,640]{2,1,0:T(8,128)(2,1)S(1)}, bf16[2,256,640]{2,1,0:T(8,128)(2,1)S(1)}, bf16[4,256,640]{2,1,0:T(8,128)(2,1)S(1)}) custom-call(s32[4]{0:T(128)S(1)} %pad_add_fusion.idx, bf16[512,256]{1,0:T(8,128)(2,1)S(1)} %copy-done.11, bf16[512,256]{1,0:T(8,128)(2,1)S(1)} %copy-done.13, ...), custom_call_target="tpu_custom_call" | custom-call | flops 1342177280 | bytes 5767168 | tf_op jit(solution)/shard_map/terms/pallas_call | solution.py:464
  77.2 1.6 %collective-permute-start.13 = (bf16[2,256,640]{2,1,0:T(8,128)(2,1)S(1)}, bf16[2,256,640]{2,1,0:T(8,128)(2,1)S(1)}, u32[]{:S(2)}, u32[]{:S(2)}) collective-permute-start(bf16[2,256,640]{2,1,0:T(8,128)(2,1)S(1)} %get-tuple-element.45), channel_id=1, source_target_pairs={{0,1},{1,0},{2,3},{3,2},{4,5},{5,4},{6,7},{7,6},{8,9},{9,8},{10,11... | collective-permute-start | bytes 1966088 | tf_op jit(solution)/shard_map/ppermute | solution.py:300
  78.8 1.5 %collective-permute-start.15 = (bf16[2,256,640]{2,1,0:T(8,128)(2,1)S(1)}, bf16[2,256,640]{2,1,0:T(8,128)(2,1)S(1)}, u32[]{:S(2)}, u32[]{:S(2)}) collective-permute-start(bf16[2,256,640]{2,1,0:T(8,128)(2,1)S(1)} %get-tuple-element.46), channel_id=1, source_target_pairs={{0,2},{1,3},{2,0},{3,1},{4,6},{5,7},{6,4},{7,5},{8,10},{9,11},{10,... | collective-permute-start | bytes 1966088 | tf_op jit(solution)/shard_map/ppermute | solution.py:300
  80.3 4.5 %grad_value.1 = (bf16[2,320,256]{2,1,0:T(8,128)(2,1)S(1)}, bf16[2,320,256]{2,1,0:T(8,128)(2,1)S(1)}, bf16[2,320,256]{2,1,0:T(8,128)(2,1)S(1)}, bf16[2,320,256]{2,1,0:T(8,128)(2,1)S(1)}) custom-call(s32[5]{0:T(128)S(1)} %stack.67.idx, bf16[16,128]{1,0:T(8,128)(2,1)S(1)} %get-tuple-element.47.token, bf16[2,320,256]{2,1,0:T(8,128)(2,1)S(1)} %add_convert_fusion.unread, ...), custom_call_target="tpu_custom_call" | custom-call | flops 1342177280 | bytes 7077888 | tf_op jit(solution)/shard_map/grad_value/pallas_call | solution.py:473
  84.8 1.4 %collective-permute-start.17 = (bf16[2,320,256]{2,1,0:T(8,128)(2,1)S(1)}, bf16[2,320,256]{2,1,0:T(8,128)(2,1)S(1)}, u32[]{:S(2)}, u32[]{:S(2)}) collective-permute-start(bf16[2,320,256]{2,1,0:T(8,128)(2,1)S(1)} %get-tuple-element.50), channel_id=1, source_target_pairs={{0,8},{4,12},{8,0},{12,4},{16,24},{20,28},{24,16},{28,20},{1,9},{5... | collective-permute-start | bytes 983048 | tf_op jit(solution)/shard_map/ppermute | solution.py:289
  86.1 0.2 convert_element_type.53
  86.3 1.3 %collective-permute-done.19.far = bf16[2,320,256]{2,1,0:T(8,128)(2,1)S(1)} collective-permute-done((bf16[2,320,256]{2,1,0:T(8,128)(2,1)S(1)}, bf16[2,320,256]{2,1,0:T(8,128)(2,1)S(1)}, u32[]{:S(2)}, u32[]{:S(2)}) %collective-permute-start.19) | collective-permute-done | bytes 327712 | tf_op jit(solution)/shard_map/ppermute | solution.py:289
  87.6 7.0 %collective-permute-done.17.got = bf16[2,320,256]{2,1,0:T(8,128)(2,1)S(1)} collective-permute-done((bf16[2,320,256]{2,1,0:T(8,128)(2,1)S(1)}, bf16[2,320,256]{2,1,0:T(8,128)(2,1)S(1)}, u32[]{:S(2)}, u32[]{:S(2)}) %collective-permute-start.17) | collective-permute-done | bytes 327712 | tf_op jit(solution)/shard_map/ppermute | solution.py:289
  94.6 0.2 sum.1
  94.8 0.8 collective-permute-start.20
  95.6 1.6 %collective-permute-start.21 = (bf16[2,320,256]{2,1,0:T(8,128)(2,1)S(1)}, bf16[2,320,256]{2,1,0:T(8,128)(2,1)S(1)}, u32[]{:S(2)}, u32[]{:S(2)}) collective-permute-start(bf16[2,320,256]{2,1,0:T(8,128)(2,1)S(1)} %get-tuple-element.55), channel_id=1, source_target_pairs={{0,16},{4,20},{8,24},{12,28},{16,0},{20,4},{24,8},{28,12},{1,17},{... | collective-permute-start | bytes 983048 | tf_op jit(solution)/shard_map/ppermute | solution.py:289
  97.2 0.1 collective-permute-start.23
  97.3 0.1 convert_element_type.54
  97.4 0.1 convert_element_type.58
  97.5 0.1 fusion.8
  97.7 0.6 collective-permute-start.14
  98.3 1.0 collective-permute-start.16
  99.3 10.4 %collective-permute-done.20 = bf16[2,320,256]{2,1,0:T(8,128)(2,1)S(1)} collective-permute-done((bf16[2,320,256]{2,1,0:T(8,128)(2,1)S(1)}, bf16[2,320,256]{2,1,0:T(8,128)(2,1)S(1)}, u32[]{:S(2)}, u32[]{:S(2)}) %collective-permute-start.20) | collective-permute-done | bytes 327712 | tf_op jit(solution)/shard_map/ppermute | solution.py:289
  109.7 2.1 %collective-permute-done.21 = bf16[2,320,256]{2,1,0:T(8,128)(2,1)S(1)} collective-permute-done((bf16[2,320,256]{2,1,0:T(8,128)(2,1)S(1)}, bf16[2,320,256]{2,1,0:T(8,128)(2,1)S(1)}, u32[]{:S(2)}, u32[]{:S(2)}) %collective-permute-start.21) | collective-permute-done | bytes 327712 | tf_op jit(solution)/shard_map/ppermute | solution.py:289
  111.8 0.1 convert_add_fusion
  112.1 0.9 pad_maximum_fusion.2
  113.0 0.2 fusion.7
  113.3 0.9 pad_maximum_fusion
  114.2 0.9 pad_maximum_fusion.1
  (45 shorter events, 0.5 us)
Async XLA Ops:
  0.6 3.2 %copy-start = (bf16[2,2,128,2560]{3,2,1,0:T(8,128)(2,1)S(1)}, bf16[2,2,128,2560]{3,2,1,0:T(8,128)(2,1)}, u32[]{:S(2)}) copy-start(bf16[2,2,128,2560]{3,2,1,0:T(8,128)(2,1)} %param.5) | copy-start | bytes 7864324
  2.1 1.8 %collective-permute-start = (bf16[2,320,256]{2,1,0:T(8,128)(2,1)S(1)}, bf16[2,320,256]{2,1,0:T(8,128)(2,1)S(1)}, u32[]{:S(2)}, u32[]{:S(2)}) collective-permute-start(bf16[2,320,256]{2,1,0:T(8,128)(2,1)S(1)} %get-tuple-element.66), channel_id=1, source_target_pairs={{0,4},{4,0},{8,12},{12,8},{16,20},{20,16},{24,28},{28,24},{1,5},{5... | collective-permute-start | bytes 983048 | tf_op jit(solution)/shard_map/ppermute | solution.py:297
  3.8 26.1 %collective-permute-start.1 = (bf16[512,2560]{1,0:T(8,128)(2,1)S(1)}, bf16[512,2560]{1,0:T(8,128)(2,1)}, u32[]{:S(2)}, u32[]{:S(2)}) collective-permute-start(bf16[512,2560]{1,0:T(8,128)(2,1)S(1)} %bitcast.50), channel_id=1, source_target_pairs={{0,4},{4,0},{8,12},{12,8},{16,20},{20,16},{24,28},{28,24},{1,5},{5... | collective-permute-start | bytes 7864328 | tf_op jit(solution)/shard_map/ppermute | solution.py:297
  4.2 47.0 %collective-permute-start.7 = (bf16[512,2560]{1,0:T(8,128)(2,1)}, bf16[512,2560]{1,0:T(8,128)(2,1)}, u32[]{:S(2)}, u32[]{:S(2)}) collective-permute-start(bf16[512,2560]{1,0:T(8,128)(2,1)} %bitcast.53), channel_id=1, source_target_pairs={{0,4},{4,0},{8,12},{12,8},{16,20},{20,16},{24,28},{28,24},{1,5},{5... | collective-permute-start | bytes 7864328 | tf_op jit(solution)/shard_map/ppermute | solution.py:297
  4.4 24.5 %collective-permute-start.2 = (bf16[4,8,128,128]{3,2,1,0:T(8,128)(2,1)}, bf16[4,8,128,128]{3,2,1,0:T(8,128)(2,1)}, u32[]{:S(2)}, u32[]{:S(2)}) collective-permute-start(bf16[4,8,128,128]{3,2,1,0:T(8,128)(2,1)} %bitcast.56), channel_id=1, source_target_pairs={{0,4},{4,0},{8,12},{12,8},{16,20},{20,16},{24,28},{28,24},{1,5},{5... | collective-permute-start | bytes 3145736 | tf_op jit(solution)/shard_map/ppermute | solution.py:297
  4.8 17.9 %collective-permute-start.3 = (bf16[2,320,256]{2,1,0:T(8,128)(2,1)S(1)}, bf16[2,320,256]{2,1,0:T(8,128)(2,1)S(1)}, u32[]{:S(2)}, u32[]{:S(2)}) collective-permute-start(bf16[2,320,256]{2,1,0:T(8,128)(2,1)S(1)} %pad_maximum_fusion.5.rest_0_), channel_id=1, source_target_pairs={{0,8},{4,12},{8,0},{12,4},{16,24},{20,28},{24,16},{28,20},{1,9},{5... | collective-permute-start | bytes 983048 | tf_op jit(solution)/shard_map/ppermute | solution.py:289
  7.6 17.7 %collective-permute-start.4 = (bf16[2,320,256]{2,1,0:T(8,128)(2,1)S(1)}, bf16[2,320,256]{2,1,0:T(8,128)(2,1)S(1)}, u32[]{:S(2)}, u32[]{:S(2)}) collective-permute-start(bf16[2,320,256]{2,1,0:T(8,128)(2,1)S(1)} %pad_maximum_fusion.5.rest_0_), channel_id=1, source_target_pairs={{0,16},{4,20},{8,24},{12,28},{16,0},{20,4},{24,8},{28,12},{1,17},{... | collective-permute-start | bytes 983048 | tf_op jit(solution)/shard_map/ppermute | solution.py:289
  26.1 0.7 copy-start.6
  26.8 31.1 %copy-start.4 = (bf16[2,320,256]{2,1,0:T(8,128)(2,1)}, bf16[2,320,256]{2,1,0:T(8,128)(2,1)S(1)}, u32[]{:S(2)}) copy-start(bf16[2,320,256]{2,1,0:T(8,128)(2,1)S(1)} %get-tuple-element.40.rest_0_) | copy-start | bytes 983044
  26.8 17.6 %collective-permute-start.5 = (bf16[2,320,256]{2,1,0:T(8,128)(2,1)}, bf16[2,320,256]{2,1,0:T(8,128)(2,1)}, u32[]{:S(2)}, u32[]{:S(2)}) collective-permute-start(bf16[2,320,256]{2,1,0:T(8,128)(2,1)} %get-tuple-element.33.rest_2_), channel_id=1, source_target_pairs={{0,8},{4,12},{8,0},{12,4},{16,24},{20,28},{24,16},{28,20},{1,9},{5... | collective-permute-start | bytes 983048 | tf_op jit(solution)/shard_map/ppermute | solution.py:289
  27.3 23.9 %collective-permute-start.8 = (bf16[2,320,256]{2,1,0:T(8,128)(2,1)S(1)}, bf16[2,320,256]{2,1,0:T(8,128)(2,1)S(1)}, u32[]{:S(2)}, u32[]{:S(2)}) collective-permute-start(bf16[2,320,256]{2,1,0:T(8,128)(2,1)S(1)} %get-tuple-element.40.rest_0_), channel_id=1, source_target_pairs={{0,8},{4,12},{8,0},{12,4},{16,24},{20,28},{24,16},{28,20},{1,9},{5... | collective-permute-start | bytes 983048 | tf_op jit(solution)/shard_map/ppermute | solution.py:289
  28.9 19.2 %collective-permute-start.9 = (bf16[2,320,256]{2,1,0:T(8,128)(2,1)S(1)}, bf16[2,320,256]{2,1,0:T(8,128)(2,1)S(1)}, u32[]{:S(2)}, u32[]{:S(2)}) collective-permute-start(bf16[2,320,256]{2,1,0:T(8,128)(2,1)S(1)} %get-tuple-element.40.rest_0_), channel_id=1, source_target_pairs={{0,16},{4,20},{8,24},{12,28},{16,0},{20,4},{24,8},{28,12},{1,17},{... | collective-permute-start | bytes 983048 | tf_op jit(solution)/shard_map/ppermute | solution.py:289
  30.0 1.2 %copy-start.2 = (bf16[2,2,8,128,128]{4,3,2,1,0:T(8,128)(2,1)S(1)}, bf16[2,2,8,128,128]{4,3,2,1,0:T(8,128)(2,1)}, u32[]{:S(2)}) copy-start(bf16[2,2,8,128,128]{4,3,2,1,0:T(8,128)(2,1)} %param.6) | copy-start | bytes 3145732
  31.2 1.0 copy-start.7
  44.4 6.8 %copy-start.1 = (bf16[2,2,128,2560]{3,2,1,0:T(8,128)(2,1)S(1)}, bf16[2,2,128,2560]{3,2,1,0:T(8,128)(2,1)}, u32[]{:S(2)}) copy-start(bf16[2,2,128,2560]{3,2,1,0:T(8,128)(2,1)} %param.7) | copy-start | bytes 7864324
  47.1 8.6 %copy-start.10 = (bf16[512,256]{1,0:T(8,128)(2,1)}, bf16[512,256]{1,0:T(8,128)(2,1)S(1)}, u32[]{:S(2)}) copy-start(bf16[512,256]{1,0:T(8,128)(2,1)S(1)} %get-tuple-element.37.mixed_o) | copy-start | bytes 786436
  47.1 4.1 %collective-permute-start.6 = (bf16[512,256]{1,0:T(8,128)(2,1)S(1)}, bf16[512,256]{1,0:T(8,128)(2,1)S(1)}, u32[]{:S(2)}, u32[]{:S(2)}) collective-permute-start(bf16[512,256]{1,0:T(8,128)(2,1)S(1)} %get-tuple-element.38.mixed_s), channel_id=1, source_target_pairs={{0,4},{4,0},{8,12},{12,8},{16,20},{20,16},{24,28},{28,24},{1,5},{5... | collective-permute-start | bytes 786440 | tf_op jit(solution)/shard_map/ppermute | solution.py:297
  48.1 9.8 %collective-permute-start.11 = (bf16[2,320,256]{2,1,0:T(8,128)(2,1)S(1)}, bf16[2,320,256]{2,1,0:T(8,128)(2,1)S(1)}, u32[]{:S(2)}, u32[]{:S(2)}) collective-permute-start(bf16[2,320,256]{2,1,0:T(8,128)(2,1)S(1)} %collective-permute-done.9.rest_2_), channel_id=1, source_target_pairs={{0,8},{4,12},{8,0},{12,4},{16,24},{20,28},{24,16},{28,20},{1,9},{5... | collective-permute-start | bytes 983048 | tf_op jit(solution)/shard_map/ppermute | solution.py:289
  51.2 4.5 %copy-start.12 = (bf16[512,256]{1,0:T(8,128)(2,1)}, bf16[512,256]{1,0:T(8,128)(2,1)S(1)}, u32[]{:S(2)}) copy-start(bf16[512,256]{1,0:T(8,128)(2,1)S(1)} %collective-permute-done.6.rest_0_.mixed_r) | copy-start | bytes 786436
  51.2 6.7 %copy-start.3 = (bf16[2,2,8,128,128]{4,3,2,1,0:T(8,128)(2,1)S(1)}, bf16[2,2,8,128,128]{4,3,2,1,0:T(8,128)(2,1)}, u32[]{:S(2)}) copy-start(bf16[2,2,8,128,128]{4,3,2,1,0:T(8,128)(2,1)} %param.6) | copy-start | bytes 3145732
  55.7 0.7 copy-start.8
  56.4 0.7 copy-start.14
  57.2 7.9 %collective-permute-start.10 = (bf16[2,320,256]{2,1,0:T(8,128)(2,1)S(1)}, bf16[2,320,256]{2,1,0:T(8,128)(2,1)S(1)}, u32[]{:S(2)}, u32[]{:S(2)}) collective-permute-start(bf16[2,320,256]{2,1,0:T(8,128)(2,1)S(1)} %get-tuple-element.42), channel_id=1, source_target_pairs={{0,8},{4,12},{8,0},{12,4},{16,24},{20,28},{24,16},{28,20},{1,9},{5... | collective-permute-start | bytes 983048 | tf_op jit(solution)/shard_map/ppermute | solution.py:289
  65.2 1.0 copy-start.5
  68.3 3.4 %collective-permute-start.12 = (bf16[2560,256]{1,0:T(8,128)(2,1)}, bf16[2560,256]{1,0:T(8,128)(2,1)}, u32[]{:S(2)}, u32[]{:S(2)}) collective-permute-start(bf16[2560,256]{1,0:T(8,128)(2,1)} %assemble.1.w_o), channel_id=1, source_target_pairs={{0,4},{4,0},{8,12},{12,8},{16,20},{20,16},{24,28},{28,24},{1,5},{5... | collective-permute-start | bytes 3932168 | tf_op jit(solution)/shard_map/ppermute | solution.py:297
  68.5 17.8 %collective-permute-start.18 = (bf16[2,320,256]{2,1,0:T(8,128)(2,1)}, bf16[2,320,256]{2,1,0:T(8,128)(2,1)S(1)}, u32[]{:S(2)}, u32[]{:S(2)}) collective-permute-start(bf16[2,320,256]{2,1,0:T(8,128)(2,1)} %copy-done.14), channel_id=1, source_target_pairs={{0,8},{4,12},{8,0},{12,4},{16,24},{20,28},{24,16},{28,20},{1,9},{5... | collective-permute-start | bytes 983048 | tf_op jit(solution)/shard_map/ppermute | solution.py:289
  69.8 17.8 %collective-permute-start.19 = (bf16[2,320,256]{2,1,0:T(8,128)(2,1)S(1)}, bf16[2,320,256]{2,1,0:T(8,128)(2,1)S(1)}, u32[]{:S(2)}, u32[]{:S(2)}) collective-permute-start(bf16[2,320,256]{2,1,0:T(8,128)(2,1)S(1)} %add_convert_fusion.unread), channel_id=1, source_target_pairs={{0,16},{4,20},{8,24},{12,28},{16,0},{20,4},{24,8},{28,12},{1,17},{... | collective-permute-start | bytes 983048 | tf_op jit(solution)/shard_map/ppermute | solution.py:289
  71.8 1.0 copy-start.11
  72.7 0.9 copy-start.13
  77.2 20.1 %collective-permute-start.13 = (bf16[2,256,640]{2,1,0:T(8,128)(2,1)S(1)}, bf16[2,256,640]{2,1,0:T(8,128)(2,1)S(1)}, u32[]{:S(2)}, u32[]{:S(2)}) collective-permute-start(bf16[2,256,640]{2,1,0:T(8,128)(2,1)S(1)} %get-tuple-element.45), channel_id=1, source_target_pairs={{0,1},{1,0},{2,3},{3,2},{4,5},{5,4},{6,7},{7,6},{8,9},{9,8},{10,11... | collective-permute-start | bytes 1966088 | tf_op jit(solution)/shard_map/ppermute | solution.py:300
  78.8 18.6 %collective-permute-start.15 = (bf16[2,256,640]{2,1,0:T(8,128)(2,1)S(1)}, bf16[2,256,640]{2,1,0:T(8,128)(2,1)S(1)}, u32[]{:S(2)}, u32[]{:S(2)}) collective-permute-start(bf16[2,256,640]{2,1,0:T(8,128)(2,1)S(1)} %get-tuple-element.46), channel_id=1, source_target_pairs={{0,2},{1,3},{2,0},{3,1},{4,6},{5,7},{6,4},{7,5},{8,10},{9,11},{10,... | collective-permute-start | bytes 1966088 | tf_op jit(solution)/shard_map/ppermute | solution.py:300
  84.8 9.9 %collective-permute-start.17 = (bf16[2,320,256]{2,1,0:T(8,128)(2,1)S(1)}, bf16[2,320,256]{2,1,0:T(8,128)(2,1)S(1)}, u32[]{:S(2)}, u32[]{:S(2)}) collective-permute-start(bf16[2,320,256]{2,1,0:T(8,128)(2,1)S(1)} %get-tuple-element.50), channel_id=1, source_target_pairs={{0,8},{4,12},{8,0},{12,4},{16,24},{20,28},{24,16},{28,20},{1,9},{5... | collective-permute-start | bytes 983048 | tf_op jit(solution)/shard_map/ppermute | solution.py:289
  86.1 8.5 %copy-start.9 = (bf16[2,320,256]{2,1,0:T(8,128)(2,1)S(1)}, bf16[2,320,256]{2,1,0:T(8,128)(2,1)}, u32[]{:S(2)}) copy-start(bf16[2,320,256]{2,1,0:T(8,128)(2,1)} %copy-done.8) | copy-start | bytes 983044
  94.8 14.9 %collective-permute-start.20 = (bf16[2,320,256]{2,1,0:T(8,128)(2,1)S(1)}, bf16[2,320,256]{2,1,0:T(8,128)(2,1)S(1)}, u32[]{:S(2)}, u32[]{:S(2)}) collective-permute-start(bf16[2,320,256]{2,1,0:T(8,128)(2,1)S(1)} %get-tuple-element.54), channel_id=1, source_target_pairs={{0,8},{4,12},{8,0},{12,4},{16,24},{20,28},{24,16},{28,20},{1,9},{5... | collective-permute-start | bytes 983048 | tf_op jit(solution)/shard_map/ppermute | solution.py:289
  95.6 16.2 %collective-permute-start.21 = (bf16[2,320,256]{2,1,0:T(8,128)(2,1)S(1)}, bf16[2,320,256]{2,1,0:T(8,128)(2,1)S(1)}, u32[]{:S(2)}, u32[]{:S(2)}) collective-permute-start(bf16[2,320,256]{2,1,0:T(8,128)(2,1)S(1)} %get-tuple-element.55), channel_id=1, source_target_pairs={{0,16},{4,20},{8,24},{12,28},{16,0},{20,4},{24,8},{28,12},{1,17},{... | collective-permute-start | bytes 983048 | tf_op jit(solution)/shard_map/ppermute | solution.py:289
  97.2 14.8 %collective-permute-start.23 = (f32[320,256]{1,0:T(8,128)S(1)}, f32[320,256]{1,0:T(8,128)S(1)}, u32[]{:S(2)}, u32[]{:S(2)}) collective-permute-start(f32[320,256]{1,0:T(8,128)S(1)} %slice_bitcast_fusion.2), channel_id=1, source_target_pairs={{0,4},{4,0},{8,12},{12,8},{16,20},{20,16},{24,28},{28,24},{1,5},{5... | collective-permute-start | bytes 983048 | tf_op jit(solution)/shard_map/ppermute | solution.py:297
  97.7 15.4 %collective-permute-start.14 = (bf16[256,640]{1,0:T(8,128)(2,1)S(1)}, bf16[256,640]{1,0:T(8,128)(2,1)S(1)}, u32[]{:S(2)}, u32[]{:S(2)}) collective-permute-start(bf16[256,640]{1,0:T(8,128)(2,1)S(1)} %get-tuple-element.59), channel_id=1, source_target_pairs={{0,2},{1,3},{2,0},{3,1},{4,6},{5,7},{6,4},{7,5},{8,10},{9,11},{10,... | collective-permute-start | bytes 983048 | tf_op jit(solution)/shard_map/ppermute | solution.py:300
  98.3 14.7 %collective-permute-start.16 = (bf16[256,640]{1,0:T(8,128)(2,1)S(1)}, bf16[256,640]{1,0:T(8,128)(2,1)S(1)}, u32[]{:S(2)}, u32[]{:S(2)}) collective-permute-start(bf16[256,640]{1,0:T(8,128)(2,1)S(1)} %get-tuple-element.60), channel_id=1, source_target_pairs={{0,1},{1,0},{2,3},{3,2},{4,5},{5,4},{6,7},{7,6},{8,9},{9,8},{10,11... | collective-permute-start | bytes 983048 | tf_op jit(solution)/shard_map/ppermute | solution.py:300
  111.9 2.2 %collective-permute-start.22 = (f32[320,256]{1,0:T(8,128)S(1)}, f32[320,256]{1,0:T(8,128)S(1)}, u32[]{:S(2)}, u32[]{:S(2)}) collective-permute-start(f32[320,256]{1,0:T(8,128)S(1)} %slice_bitcast_fusion), channel_id=1, source_target_pairs={{0,4},{4,0},{8,12},{12,8},{16,20},{20,16},{24,28},{28,24},{1,5},{5... | collective-permute-start | bytes 983048 | tf_op jit(solution)/shard_map/ppermute | solution.py:297

commit v19 on v18

--- a/solution.py
+++ b/solution.py
@@ -67,7 +67,7 @@
         for copy in chunk:
             copy.wait()
         part = dot(left, right_ref[:, j * step : (j + 1) * step])
-        rows_ref[j * step : (j + 1) * step, :] = part.T.astype(BF16)
+        rows_ref[j * step : (j + 1) * step, :] = part.astype(BF16).T
 
 
 def head_pairs(heads):
@@ -131,7 +131,7 @@
 def mix_back(d_mixed, weights, left_v, start):
     groups, heads, seq, _ = weights.shape
     for g in range(groups):
-        turned = d_mixed[g * seq : (g + 1) * seq, :].T.astype(BF16)
+        turned = d_mixed[g * seq : (g + 1) * seq, :].astype(BF16).T
         at = start + g * seq
         for h, n in head_pairs(heads):
             part = turned[h * HEAD_DIM : (h + n) * HEAD_DIM, :]
@@ -156,18 +156,10 @@
         mix_values(value, weights.at[half], out)
 
 
-def assemble_kernel(n_slots, idx, unread, unread_too, *rest):
-    del unread, unread_too
-    slots, (w_out, slots_v, sems) = rest[:n_slots], rest[n_slots:]
-    for copy in begin_slots(slots, slots_v, sems):
-        copy.wait()
-    place(idx, idx[0], slots_v, w_out)
-
-
 def d_value_kernel(n_slots, idx, token, cot_o, cot_s, mix_o, mix_s, *rest):
     del token
     slots, rest = rest[:n_slots], rest[n_slots:]
-    left_v, w_out, cot_v, mix_v, sems, slots_v, slot_sems = rest
+    left_v, w_out, w_v, cot_v, mix_v, sems, slots_v, slot_sems, out_sems = rest
     tokens, heads = cot_o.shape[0], mix_v.shape[2]
     here = pl.ds(idx[0] * heads, heads)
     slot_copies = begin_slots(slots, slots_v, slot_sems)
@@ -178,12 +170,14 @@
     )
     for copy in slot_copies:
         copy.wait()
-    place(idx, idx[0], slots_v, w_out)
+    place(idx, idx[0], slots_v, w_v)
+    handed = begin([(w_v, w_out)], out_sems)
     for half in range(2):
         copies[2 * half].wait()
-        d_mixed = dot(cot_v[half], w_out[...])
+        d_mixed = dot(cot_v[half], w_v[...])
         copies[2 * half + 1].wait()
         mix_back(d_mixed, mix_v.at[half], left_v, half * tokens)
+    handed[0].wait()
 
 
 def gradient_kernel(idx, token, unread, right_o, right_s, left_ref, *rest):
@@ -220,8 +214,8 @@
     token[...] = jnp.zeros_like(token)
     tokens, _ = cot_o.shape
     copies = chunk_copies(cot_o, cot_s, cot_v, sems)
-    left_v[:, :tokens] = mixed_o[...].astype(F32).T.astype(BF16)
-    left_v[:, tokens:] = mixed_s[...].astype(F32).T.astype(BF16)
+    left_v[:, :tokens] = mixed_o[...].T
+    left_v[:, tokens:] = mixed_s[...].T
     gradient_rows(left_v[...], cot_v, copies, grad_v)
     hand_out(idx, 1, grad_v, outs)
 
@@ -266,12 +260,12 @@
 VMEM = pl.BlockSpec(memory_space=pltpu.VMEM)
 
 
-def call(kernel, name, in_specs, out_shapes, scratch, flops, size=1 << 20, kinds=None, vmem=24):
+def call(kernel, name, in_specs, out_shapes, scratch, flops, size=1 << 20, kinds=None, vmem=24, out_specs=None):
     return pl.pallas_call(
         kernel,
         name=name,
         in_specs=in_specs,
-        out_specs=[VMEM] * len(out_shapes),
+        out_specs=out_specs or [VMEM] * len(out_shapes),
         out_shape=[
             jax.ShapeDtypeStruct(s, k) for s, k in zip(out_shapes, kinds or [BF16] * len(out_shapes))
         ],
@@ -279,6 +273,20 @@
         compiler_params=pltpu.CompilerParams(vmem_limit_bytes=vmem << 20),
         cost_estimate=pl.CostEstimate(flops=flops, bytes_accessed=size, transcendentals=0),
     )
+
+
+def in_order(x, earlier):
+    def kernel(*refs):
+        del refs
+
+    return pl.pallas_call(
+        kernel,
+        name="in_order",
+        in_specs=[ANY, ANY],
+        out_specs=ANY,
+        out_shape=jax.ShapeDtypeStruct(x.shape, x.dtype),
+        input_output_aliases={0: 0},
+    )(x, earlier)
 
 
 def make_body(n_wide, n_node):
@@ -430,30 +438,24 @@
             2 * (2 * cot.size + 2 * tokens * cols + width * cols),
         )(idx, cot, cot_s, mixed_o, mixed_s, *unread)
         out_passed = swap(out_sends[3], 1) if line4 else token
-        left = call(
+        left, w_full = call(
             functools.partial(d_value_kernel, n_slots),
             "d_value",
             [SMEM] + [ANY] * (5 + n_slots),
-            [(cols, 2 * tokens)],
-            [rows, halves, mix_scratch, pltpu.SemaphoreType.DMA((4,)), *slots_scratch],
+            [(cols, 2 * tokens), (width, cols)],
+            [rows, halves, mix_scratch, pltpu.SemaphoreType.DMA((4,)), *slots_scratch]
+            + [pltpu.SemaphoreType.DMA((1,))],
             flops,
-            2 * (2 * cot.size + mix.size + width * cols + 2 * tokens * cols),
-        )(idx, token, cot, cot_s, mix, mix_s, *out_slots)[0]
+            2 * (2 * cot.size + mix.size + 2 * width * cols + 2 * tokens * cols),
+            out_specs=[VMEM, ANY],
+        )(idx, token, cot, cot_s, mix, mix_s, *out_slots)
         if line4:
             out_onward = added(out_sends[2], out_passed)
             out_far = swap(out_onward, 2)
             out_near = swap(out_sends[1], 1)
         else:
             out_onward = left
-        w_full = call(
-            functools.partial(assemble_kernel, n_slots),
-            "assemble",
-            [SMEM] + [ANY] * (2 + n_slots),
-            [(width, cols)],
-            slots_scratch,
-            0,
-            4 * width * cols,
-        )(idx, out_onward, left, *out_slots)[0]
+        w_full = in_order(w_full, out_onward)
         w_full_s = sibling(w_full)
         part = width // n_node
         half = tokens // 2

time: 116 us -> 115 us (level)
  Pallas kernels: 28.4 us -> 25.6 us
  local copies, waits for them, and re-layouts: 8.78 us -> 11 us
    unnamed x30 -> x32, local copies, waits for them, and re-layouts: 7.26 us -> 9.48 us
    pallas_call x1, Pallas kernels: 2.15 us -> 0.01 us  [in_order(): pl.pallas_call(kernel, name='in_order', in_specs=[ANY, ANY], out_specs=AN...]
    pallas_call x1, Pallas kernels: 3.56 us -> 2.37 us  [body(): call(functools.partial(terms_kernel, n_node), 'terms', [SMEM] + [VMEM] *...]
  transfers between devices with their start and end apart: 24 -> 24, of which waited for: 12 -> 9; matrix products, arithmetic and copies ran while one was open for 3% -> 3% of each run, Pallas kernels for 23% -> 22%
where the time goes in v19:
time: 115 us
  waiting for transfers between devices  47.9 us (42%)
  Pallas kernels  25.6 us (22%)
  starting transfers between devices  24.8 us (22%)
  local copies, waits for them, and re-layouts  11 us (10%)
  other arithmetic  4.64 us (4%)
    ppermute x12, waiting for transfers between devices, move(): lax.ppermute(x, 'wide', [(2 * s + c, 2 * d + c) for s, d in pairs for c i...  46.6 us
    ppermute x12, starting transfers between devices, move(): lax.ppermute(x, 'wide', [(2 * s + c, 2 * d + c) for s, d in pairs for c i...  19 us
    unnamed x32, local copies, waits for them, and re-layouts  9.48 us
    pallas_call x1, Pallas kernels, body(): call(functools.partial(d_value_kernel, n_slots), 'd_value', [SMEM] + [ANY...  5.32 us
    pallas_call x1, Pallas kernels, body(): call(functools.partial(grad_out_kernel, len(unread)), 'grad_out', [SMEM]...  5.11 us
    pallas_call x1, Pallas kernels, body(): call(functools.partial(part_kernel, n_slots - 1), 'value_ahead', [SMEM] +...  4.9 us
    pallas_call x1, Pallas kernels, body(): call(gradient_kernel, 'grad_value', [SMEM] + [ANY] * 4 + [VMEM], send_sha...  4.39 us
    ppermute x4, starting transfers between devices, flip(): return lax.ppermute(x, 'node', [(i, i ^ j) for i in range(n_node)])  4.18 us
  transfers between devices with their start and end apart: 24, of which 9 were waited for; matrix products, arithmetic and copies ran while one was open for 3% of the time, Pallas kernels for 22%

profile of v19, /device:TPU:0, one launch (start us, length us, event | category | flops | bytes accessed | tf_op | source)
XLA Modules:
  0.0 114.9 jit_solution(9165728968612646284)
XLA Ops:
  0.7 1.3 %slice_bitcast_fusion.5 = (bf16[1,320,256]{2,1,0:T(8,128)(2,1)S(1)}, bf16[1,320,256]{2,1,0:T(8,128)(2,1)S(1)}, bf16[1,320,256]{2,1,0:T(8,128)(2,1)S(1)}, bf16[1,320,256]{2,1,0:T(8,128)(2,1)S(1)}) fusion(bf16[320,512]{1,0:T(8,128)(2,1)} %param.8, bf16[320,512]{1,0:T(8,128)(2,1)} %param.9), kind=kLoop, calls=%fused_computation.34 | loop fusion | bytes 1310720 | tf_op jit(solution)/shard_map/stack | solution.py:313
  2.0 0.1 broadcast_select_fusion
  2.1 0.5 collective-permute-start
  2.6 1.3 %collective-permute-done = bf16[2,320,256]{2,1,0:T(8,128)(2,1)S(1)} collective-permute-done((bf16[2,320,256]{2,1,0:T(8,128)(2,1)S(1)}, bf16[2,320,256]{2,1,0:T(8,128)(2,1)S(1)}, u32[]{:S(2)}, u32[]{:S(2)}) %collective-permute-start) | collective-permute-done | bytes 327712 | tf_op jit(solution)/shard_map/ppermute | solution.py:305
  3.8 0.4 collective-permute-start.1
  4.2 0.1 collective-permute-start.7
  4.4 0.4 collective-permute-start.2
  4.8 2.8 %collective-permute-start.3 = (bf16[2,320,256]{2,1,0:T(8,128)(2,1)S(1)}, bf16[2,320,256]{2,1,0:T(8,128)(2,1)S(1)}, u32[]{:S(2)}, u32[]{:S(2)}) collective-permute-start(bf16[2,320,256]{2,1,0:T(8,128)(2,1)S(1)} %pad_maximum_fusion.5.rest_0_), channel_id=1, source_target_pairs={{0,8},{4,12},{8,0},{12,4},{16,24},{20,28},{24,16},{28,20},{1,9},{5... | collective-permute-start | bytes 983048 | tf_op jit(solution)/shard_map/ppermute | solution.py:297
  7.6 2.6 %collective-permute-start.4 = (bf16[2,320,256]{2,1,0:T(8,128)(2,1)S(1)}, bf16[2,320,256]{2,1,0:T(8,128)(2,1)S(1)}, u32[]{:S(2)}, u32[]{:S(2)}) collective-permute-start(bf16[2,320,256]{2,1,0:T(8,128)(2,1)S(1)} %pad_maximum_fusion.5.rest_0_), channel_id=1, source_target_pairs={{0,16},{4,20},{8,24},{12,28},{16,0},{20,4},{24,8},{28,12},{1,17},{... | collective-permute-start | bytes 983048 | tf_op jit(solution)/shard_map/ppermute | solution.py:297
  10.2 12.5 %collective-permute-done.3.unread.rest_1_ = bf16[2,320,256]{2,1,0:T(8,128)(2,1)S(1)} collective-permute-done((bf16[2,320,256]{2,1,0:T(8,128)(2,1)S(1)}, bf16[2,320,256]{2,1,0:T(8,128)(2,1)S(1)}, u32[]{:S(2)}, u32[]{:S(2)}) %collective-permute-start.3) | collective-permute-done | bytes 327712 | tf_op jit(solution)/shard_map/ppermute | solution.py:297
  22.8 2.5 %collective-permute-done.4.first = bf16[2,320,256]{2,1,0:T(8,128)(2,1)S(1)} collective-permute-done((bf16[2,320,256]{2,1,0:T(8,128)(2,1)S(1)}, bf16[2,320,256]{2,1,0:T(8,128)(2,1)S(1)}, u32[]{:S(2)}, u32[]{:S(2)}) %collective-permute-start.4) | collective-permute-done | bytes 327712 | tf_op jit(solution)/shard_map/ppermute | solution.py:297
  25.3 0.8 relay.1
  26.1 0.7 copy-done.8
  26.8 0.4 collective-permute-start.5
  27.2 0.1 stack.67.idx
  27.3 1.6 %collective-permute-start.8 = (bf16[2,320,256]{2,1,0:T(8,128)(2,1)}, bf16[2,320,256]{2,1,0:T(8,128)(2,1)S(1)}, u32[]{:S(2)}, u32[]{:S(2)}) collective-permute-start(bf16[2,320,256]{2,1,0:T(8,128)(2,1)} %copy-done.8), channel_id=1, source_target_pairs={{0,8},{4,12},{8,0},{12,4},{16,24},{20,28},{24,16},{28,20},{1,9},{5... | collective-permute-start | bytes 983048 | tf_op jit(solution)/shard_map/ppermute | solution.py:297
  28.9 1.1 collective-permute-start.9
  30.0 1.7 %copy-done.1 = bf16[2,2,128,2560]{3,2,1,0:T(8,128)(2,1)S(1)} copy-done((bf16[2,2,128,2560]{3,2,1,0:T(8,128)(2,1)S(1)}, bf16[2,2,128,2560]{3,2,1,0:T(8,128)(2,1)}, u32[]{:S(2)}) %copy-start.1) | copy-done | bytes 2621464
  31.7 1.2 %copy-done.3 = bf16[2,2,8,128,128]{4,3,2,1,0:T(8,128)(2,1)S(1)} copy-done((bf16[2,2,8,128,128]{4,3,2,1,0:T(8,128)(2,1)S(1)}, bf16[2,2,8,128,128]{4,3,2,1,0:T(8,128)(2,1)}, u32[]{:S(2)}) %copy-start.3) | copy-done | bytes 1048600
  32.9 4.9 %value_ahead.1 = (f32[2,512,256]{2,1,0:T(8,128)S(1)}, bf16[2,512,640]{2,1,0:T(8,128)(2,1)S(1)}, bf16[2,4,4,128,128]{4,3,2,1,0:T(8,128)(2,1)S(1)}) custom-call(s32[5]{0:T(128)S(1)} %stack.67.idx, bf16[512,2560]{1,0:T(8,128)(2,1)S(1)} %bitcast.54, bf16[512,2560]{1,0:T(8,128)(2,1)} %collective-permute-done.1.x_s.right_s, bf16[4,8,128,128]{3,2,1,0:T(8,128)(2,1)S(1)} %bitcast.57, ...), custom_call_target="tpu_custom_call" | custom-call | flops 1342177280 | bytes 11272192 | tf_op jit(solution)/shard_map/value_ahead/pallas_call | solution.py:396
  37.9 6.8 %collective-permute-done.5.slot = bf16[2,320,256]{2,1,0:T(8,128)(2,1)} collective-permute-done((bf16[2,320,256]{2,1,0:T(8,128)(2,1)}, bf16[2,320,256]{2,1,0:T(8,128)(2,1)}, u32[]{:S(2)}, u32[]{:S(2)}) %collective-permute-start.5) | collective-permute-done | bytes 327712 | tf_op jit(solution)/shard_map/ppermute | solution.py:297
  44.6 2.5 %mixed.1 = (bf16[512,256]{1,0:T(8,128)(2,1)S(1)}, bf16[512,256]{1,0:T(8,128)(2,1)S(1)}) custom-call(s32[5]{0:T(128)S(1)} %stack.67.idx, f32[2,512,256]{2,1,0:T(8,128)S(1)} %get-tuple-element.36.part, bf16[2,512,640]{2,1,0:T(8,128)(2,1)S(1)} %get-tuple-element.37.last, bf16[2,4,4,128,128]{4,3,2,1,0:T(8,128)(2,1)S(1)} %get-tuple-element.38.weights, ...), custom_call_target="tpu_custom_call" | custom-call | flops 335544320 | bytes 3932160 | tf_op jit(solution)/shard_map/mixed/pallas_call | solution.py:409
  47.2 0.1 collective-permute-start.6
  47.2 1.0 collective-permute-done.9.rest_2_
  48.2 3.0 %collective-permute-start.10 = (bf16[2,320,256]{2,1,0:T(8,128)(2,1)S(1)}, bf16[2,320,256]{2,1,0:T(8,128)(2,1)S(1)}, u32[]{:S(2)}, u32[]{:S(2)}) collective-permute-start(bf16[2,320,256]{2,1,0:T(8,128)(2,1)S(1)} %collective-permute-done.9.rest_2_), channel_id=1, source_target_pairs={{0,8},{4,12},{8,0},{12,4},{16,24},{20,28},{24,16},{28,20},{1,9},{5... | collective-permute-start | bytes 983048 | tf_op jit(solution)/shard_map/ppermute | solution.py:297
  51.2 0.0 copy-start.4
  51.2 5.1 %grad_out.1 = (bf16[16,128]{1,0:T(8,128)(2,1)S(1)}, bf16[2,320,256]{2,1,0:T(8,128)(2,1)S(1)}, bf16[2,320,256]{2,1,0:T(8,128)(2,1)}, bf16[2,320,256]{2,1,0:T(8,128)(2,1)S(1)}, bf16[2,320,256]{2,1,0:T(8,128)(2,1)S(1)}) custom-call(s32[5]{0:T(128)S(1)} %stack.67.idx, bf16[512,2560]{1,0:T(8,128)(2,1)S(1)} %bitcast.51, ...), custom_call_target="tpu_custom_call" | custom-call | flops 1342177280 | bytes 7077888 | tf_op jit(solution)/shard_map/grad_out/pallas_call | solution.py:431
  56.4 0.1 collective-permute-start.11
  56.4 2.2 %collective-permute-done.10.rest_3_ = bf16[2,320,256]{2,1,0:T(8,128)(2,1)S(1)} collective-permute-done((bf16[2,320,256]{2,1,0:T(8,128)(2,1)S(1)}, bf16[2,320,256]{2,1,0:T(8,128)(2,1)S(1)}, u32[]{:S(2)}, u32[]{:S(2)}) %collective-permute-start.10) | collective-permute-done | bytes 327712 | tf_op jit(solution)/shard_map/ppermute | solution.py:297
  58.6 5.3 %d_value.1 = (bf16[256,1024]{1,0:T(8,128)(2,1)S(1)}, bf16[2560,256]{1,0:T(8,128)(2,1)S(1)}) custom-call(s32[5]{0:T(128)S(1)} %stack.67.idx, bf16[16,128]{1,0:T(8,128)(2,1)S(1)} %get-tuple-element.43.token, bf16[512,2560]{1,0:T(8,128)(2,1)S(1)} %bitcast.52, bf16[512,2560]{1,0:T(8,128)(2,1)} %collective-permute-done.7.cot_s, ...), custom_call_target="tpu_custom_call" | custom-call | flops 1342177280 | bytes 9437184 | tf_op jit(solution)/shard_map/d_value/pallas_call | solution.py:441
  63.9 1.1 copy-done.6
  65.0 0.8 add_convert_fusion.refs_1_.unread
  65.9 0.1 pad_add_fusion.idx
  66.0 2.5 %collective-permute-start.18 = (bf16[2,320,256]{2,1,0:T(8,128)(2,1)}, bf16[2,320,256]{2,1,0:T(8,128)(2,1)S(1)}, u32[]{:S(2)}, u32[]{:S(2)}) collective-permute-start(bf16[2,320,256]{2,1,0:T(8,128)(2,1)} %get-tuple-element.57), channel_id=1, source_target_pairs={{0,8},{4,12},{8,0},{12,4},{16,24},{20,28},{24,16},{28,20},{1,9},{5... | collective-permute-start | bytes 983048 | tf_op jit(solution)/shard_map/ppermute | solution.py:297
  68.5 0.6 collective-permute-start.19
  69.1 0.0 collective-permute-done.12.w_r
  69.1 1.1 copy-done.14
  70.2 1.3 %copy-done.7 = bf16[2560,256]{1,0:T(8,128)(2,1)S(1)} copy-done((bf16[2560,256]{1,0:T(8,128)(2,1)S(1)}, bf16[2560,256]{1,0:T(8,128)(2,1)}, u32[]{:S(2)}) %copy-start.7) | copy-done | bytes 1310744
  71.5 0.9 copy-done.13
  72.5 1.3 %copy-done.15 = bf16[2560,256]{1,0:T(8,128)(2,1)S(1)} copy-done((bf16[2560,256]{1,0:T(8,128)(2,1)S(1)}, bf16[2560,256]{1,0:T(8,128)(2,1)}, u32[]{:S(2)}) %copy-start.15) | copy-done | bytes 1310744
  73.8 2.4 %terms.1 = (bf16[16,128]{1,0:T(8,128)(2,1)S(1)}, bf16[2,256,640]{2,1,0:T(8,128)(2,1)S(1)}, bf16[2,256,640]{2,1,0:T(8,128)(2,1)S(1)}, bf16[4,256,640]{2,1,0:T(8,128)(2,1)S(1)}) custom-call(s32[4]{0:T(128)S(1)} %pad_add_fusion.idx, bf16[512,256]{1,0:T(8,128)(2,1)S(1)} %copy-done.11, bf16[512,256]{1,0:T(8,128)(2,1)S(1)} %copy-done.13, ...), custom_call_target="tpu_custom_call" | custom-call | flops 1342177280 | bytes 5767168 | tf_op jit(solution)/shard_map/terms/pallas_call | solution.py:466
  76.2 1.6 %collective-permute-start.13 = (bf16[2,256,640]{2,1,0:T(8,128)(2,1)S(1)}, bf16[2,256,640]{2,1,0:T(8,128)(2,1)S(1)}, u32[]{:S(2)}, u32[]{:S(2)}) collective-permute-start(bf16[2,256,640]{2,1,0:T(8,128)(2,1)S(1)} %get-tuple-element.48), channel_id=1, source_target_pairs={{0,1},{1,0},{2,3},{3,2},{4,5},{5,4},{6,7},{7,6},{8,9},{9,8},{10,11... | collective-permute-start | bytes 1966088 | tf_op jit(solution)/shard_map/ppermute | solution.py:308
  77.7 1.5 %collective-permute-start.15 = (bf16[2,256,640]{2,1,0:T(8,128)(2,1)S(1)}, bf16[2,256,640]{2,1,0:T(8,128)(2,1)S(1)}, u32[]{:S(2)}, u32[]{:S(2)}) collective-permute-start(bf16[2,256,640]{2,1,0:T(8,128)(2,1)S(1)} %get-tuple-element.49), channel_id=1, source_target_pairs={{0,2},{1,3},{2,0},{3,1},{4,6},{5,7},{6,4},{7,5},{8,10},{9,11},{10,... | collective-permute-start | bytes 1966088 | tf_op jit(solution)/shard_map/ppermute | solution.py:308
  79.2 4.4 %grad_value.1 = (bf16[2,320,256]{2,1,0:T(8,128)(2,1)S(1)}, bf16[2,320,256]{2,1,0:T(8,128)(2,1)S(1)}, bf16[2,320,256]{2,1,0:T(8,128)(2,1)S(1)}, bf16[2,320,256]{2,1,0:T(8,128)(2,1)S(1)}) custom-call(s32[5]{0:T(128)S(1)} %stack.67.idx, bf16[16,128]{1,0:T(8,128)(2,1)S(1)} %get-tuple-element.50.token, bf16[2,320,256]{2,1,0:T(8,128)(2,1)S(1)} %copy-done.5, ...), custom_call_target="tpu_custom_call" | custom-call | flops 1342177280 | bytes 7077888 | tf_op jit(solution)/shard_map/grad_value/pallas_call | solution.py:475
  83.6 2.5 %collective-permute-start.17 = (bf16[2,320,256]{2,1,0:T(8,128)(2,1)S(1)}, bf16[2,320,256]{2,1,0:T(8,128)(2,1)S(1)}, u32[]{:S(2)}, u32[]{:S(2)}) collective-permute-start(bf16[2,320,256]{2,1,0:T(8,128)(2,1)S(1)} %get-tuple-element.54), channel_id=1, source_target_pairs={{0,8},{4,12},{8,0},{12,4},{16,24},{20,28},{24,16},{28,20},{1,9},{5... | collective-permute-start | bytes 983048 | tf_op jit(solution)/shard_map/ppermute | solution.py:297
  86.2 0.2 convert_element_type.53
  86.4 7.3 %collective-permute-done.17.got = bf16[2,320,256]{2,1,0:T(8,128)(2,1)S(1)} collective-permute-done((bf16[2,320,256]{2,1,0:T(8,128)(2,1)S(1)}, bf16[2,320,256]{2,1,0:T(8,128)(2,1)S(1)}, u32[]{:S(2)}, u32[]{:S(2)}) %collective-permute-start.17) | collective-permute-done | bytes 327712 | tf_op jit(solution)/shard_map/ppermute | solution.py:297
  93.6 0.2 sum.1
  93.8 1.8 %collective-permute-start.20 = (bf16[2,320,256]{2,1,0:T(8,128)(2,1)S(1)}, bf16[2,320,256]{2,1,0:T(8,128)(2,1)S(1)}, u32[]{:S(2)}, u32[]{:S(2)}) collective-permute-start(bf16[2,320,256]{2,1,0:T(8,128)(2,1)S(1)} %get-tuple-element.58), channel_id=1, source_target_pairs={{0,8},{4,12},{8,0},{12,4},{16,24},{20,28},{24,16},{28,20},{1,9},{5... | collective-permute-start | bytes 983048 | tf_op jit(solution)/shard_map/ppermute | solution.py:297
  95.6 0.0 collective-permute-start.21
  95.7 0.1 collective-permute-start.23
  95.8 0.1 convert_element_type.54
  95.9 0.1 convert_element_type.58
  96.0 0.1 fusion.8
  96.1 0.6 collective-permute-start.14
  96.7 0.5 collective-permute-start.16
  97.2 10.9 %collective-permute-done.20 = bf16[2,320,256]{2,1,0:T(8,128)(2,1)S(1)} collective-permute-done((bf16[2,320,256]{2,1,0:T(8,128)(2,1)S(1)}, bf16[2,320,256]{2,1,0:T(8,128)(2,1)S(1)}, u32[]{:S(2)}, u32[]{:S(2)}) %collective-permute-start.20) | collective-permute-done | bytes 327712 | tf_op jit(solution)/shard_map/ppermute | solution.py:297
  108.1 3.5 %collective-permute-done.21 = bf16[2,320,256]{2,1,0:T(8,128)(2,1)S(1)} collective-permute-done((bf16[2,320,256]{2,1,0:T(8,128)(2,1)S(1)}, bf16[2,320,256]{2,1,0:T(8,128)(2,1)S(1)}, u32[]{:S(2)}, u32[]{:S(2)}) %collective-permute-start.21) | collective-permute-done | bytes 327712 | tf_op jit(solution)/shard_map/ppermute | solution.py:297
  111.6 0.1 convert_add_fusion
  111.8 0.1 collective-permute-start.22
  111.9 0.9 pad_maximum_fusion.2
  112.8 0.2 fusion.7
  113.0 0.9 pad_maximum_fusion
  114.0 0.9 pad_maximum_fusion.1
  (47 shorter events, 0.3 us)
Async XLA Ops:
  0.6 3.6 %copy-start = (bf16[2,2,128,2560]{3,2,1,0:T(8,128)(2,1)S(1)}, bf16[2,2,128,2560]{3,2,1,0:T(8,128)(2,1)}, u32[]{:S(2)}) copy-start(bf16[2,2,128,2560]{3,2,1,0:T(8,128)(2,1)} %param.7) | copy-start | bytes 7864324
  2.1 1.8 %collective-permute-start = (bf16[2,320,256]{2,1,0:T(8,128)(2,1)S(1)}, bf16[2,320,256]{2,1,0:T(8,128)(2,1)S(1)}, u32[]{:S(2)}, u32[]{:S(2)}) collective-permute-start(bf16[2,320,256]{2,1,0:T(8,128)(2,1)S(1)} %get-tuple-element.70), channel_id=1, source_target_pairs={{0,4},{4,0},{8,12},{12,8},{16,20},{20,16},{24,28},{28,24},{1,5},{5... | collective-permute-start | bytes 983048 | tf_op jit(solution)/shard_map/ppermute | solution.py:305
  3.8 26.1 %collective-permute-start.1 = (bf16[512,2560]{1,0:T(8,128)(2,1)}, bf16[512,2560]{1,0:T(8,128)(2,1)}, u32[]{:S(2)}, u32[]{:S(2)}) collective-permute-start(bf16[512,2560]{1,0:T(8,128)(2,1)} %bitcast.53), channel_id=1, source_target_pairs={{0,4},{4,0},{8,12},{12,8},{16,20},{20,16},{24,28},{28,24},{1,5},{5... | collective-permute-start | bytes 7864328 | tf_op jit(solution)/shard_map/ppermute | solution.py:305
  4.2 47.0 %collective-permute-start.7 = (bf16[512,2560]{1,0:T(8,128)(2,1)S(1)}, bf16[512,2560]{1,0:T(8,128)(2,1)}, u32[]{:S(2)}, u32[]{:S(2)}) collective-permute-start(bf16[512,2560]{1,0:T(8,128)(2,1)S(1)} %bitcast.50), channel_id=1, source_target_pairs={{0,4},{4,0},{8,12},{12,8},{16,20},{20,16},{24,28},{28,24},{1,5},{5... | collective-permute-start | bytes 7864328 | tf_op jit(solution)/shard_map/ppermute | solution.py:305
  4.4 24.5 %collective-permute-start.2 = (bf16[4,8,128,128]{3,2,1,0:T(8,128)(2,1)}, bf16[4,8,128,128]{3,2,1,0:T(8,128)(2,1)}, u32[]{:S(2)}, u32[]{:S(2)}) collective-permute-start(bf16[4,8,128,128]{3,2,1,0:T(8,128)(2,1)} %bitcast.56), channel_id=1, source_target_pairs={{0,4},{4,0},{8,12},{12,8},{16,20},{20,16},{24,28},{28,24},{1,5},{5... | collective-permute-start | bytes 3145736 | tf_op jit(solution)/shard_map/ppermute | solution.py:305
  4.8 17.9 %collective-permute-start.3 = (bf16[2,320,256]{2,1,0:T(8,128)(2,1)S(1)}, bf16[2,320,256]{2,1,0:T(8,128)(2,1)S(1)}, u32[]{:S(2)}, u32[]{:S(2)}) collective-permute-start(bf16[2,320,256]{2,1,0:T(8,128)(2,1)S(1)} %pad_maximum_fusion.5.rest_0_), channel_id=1, source_target_pairs={{0,8},{4,12},{8,0},{12,4},{16,24},{20,28},{24,16},{28,20},{1,9},{5... | collective-permute-start | bytes 983048 | tf_op jit(solution)/shard_map/ppermute | solution.py:297
  7.6 17.7 %collective-permute-start.4 = (bf16[2,320,256]{2,1,0:T(8,128)(2,1)S(1)}, bf16[2,320,256]{2,1,0:T(8,128)(2,1)S(1)}, u32[]{:S(2)}, u32[]{:S(2)}) collective-permute-start(bf16[2,320,256]{2,1,0:T(8,128)(2,1)S(1)} %pad_maximum_fusion.5.rest_0_), channel_id=1, source_target_pairs={{0,16},{4,20},{8,24},{12,28},{16,0},{20,4},{24,8},{28,12},{1,17},{... | collective-permute-start | bytes 983048 | tf_op jit(solution)/shard_map/ppermute | solution.py:297
  26.1 0.7 copy-start.8
  26.8 17.9 %collective-permute-start.5 = (bf16[2,320,256]{2,1,0:T(8,128)(2,1)}, bf16[2,320,256]{2,1,0:T(8,128)(2,1)}, u32[]{:S(2)}, u32[]{:S(2)}) collective-permute-start(bf16[2,320,256]{2,1,0:T(8,128)(2,1)} %get-tuple-element.35.rest_2_), channel_id=1, source_target_pairs={{0,8},{4,12},{8,0},{12,4},{16,24},{20,28},{24,16},{28,20},{1,9},{5... | collective-permute-start | bytes 983048 | tf_op jit(solution)/shard_map/ppermute | solution.py:297
  27.3 23.9 %collective-permute-start.8 = (bf16[2,320,256]{2,1,0:T(8,128)(2,1)}, bf16[2,320,256]{2,1,0:T(8,128)(2,1)S(1)}, u32[]{:S(2)}, u32[]{:S(2)}) collective-permute-start(bf16[2,320,256]{2,1,0:T(8,128)(2,1)} %copy-done.8), channel_id=1, source_target_pairs={{0,8},{4,12},{8,0},{12,4},{16,24},{20,28},{24,16},{28,20},{1,9},{5... | collective-permute-start | bytes 983048 | tf_op jit(solution)/shard_map/ppermute | solution.py:297
  28.9 19.3 %collective-permute-start.9 = (bf16[2,320,256]{2,1,0:T(8,128)(2,1)}, bf16[2,320,256]{2,1,0:T(8,128)(2,1)S(1)}, u32[]{:S(2)}, u32[]{:S(2)}) collective-permute-start(bf16[2,320,256]{2,1,0:T(8,128)(2,1)} %copy-done.8), channel_id=1, source_target_pairs={{0,16},{4,20},{8,24},{12,28},{16,0},{20,4},{24,8},{28,12},{1,17},{... | collective-permute-start | bytes 983048 | tf_op jit(solution)/shard_map/ppermute | solution.py:297
  30.0 1.7 %copy-start.1 = (bf16[2,2,128,2560]{3,2,1,0:T(8,128)(2,1)S(1)}, bf16[2,2,128,2560]{3,2,1,0:T(8,128)(2,1)}, u32[]{:S(2)}) copy-start(bf16[2,2,128,2560]{3,2,1,0:T(8,128)(2,1)} %param.5) | copy-start | bytes 7864324
  31.7 1.2 %copy-start.3 = (bf16[2,2,8,128,128]{4,3,2,1,0:T(8,128)(2,1)S(1)}, bf16[2,2,8,128,128]{4,3,2,1,0:T(8,128)(2,1)}, u32[]{:S(2)}) copy-start(bf16[2,2,8,128,128]{4,3,2,1,0:T(8,128)(2,1)} %param.6) | copy-start | bytes 3145732
  47.1 9.2 %copy-start.10 = (bf16[512,256]{1,0:T(8,128)(2,1)}, bf16[512,256]{1,0:T(8,128)(2,1)S(1)}, u32[]{:S(2)}) copy-start(bf16[512,256]{1,0:T(8,128)(2,1)S(1)} %get-tuple-element.39.mixed_o) | copy-start | bytes 786436
  47.2 4.0 %collective-permute-start.6 = (bf16[512,256]{1,0:T(8,128)(2,1)S(1)}, bf16[512,256]{1,0:T(8,128)(2,1)S(1)}, u32[]{:S(2)}, u32[]{:S(2)}) collective-permute-start(bf16[512,256]{1,0:T(8,128)(2,1)S(1)} %get-tuple-element.40.mixed_s), channel_id=1, source_target_pairs={{0,4},{4,0},{8,12},{12,8},{16,20},{20,16},{24,28},{28,24},{1,5},{5... | collective-permute-start | bytes 786440 | tf_op jit(solution)/shard_map/ppermute | solution.py:305
  48.2 10.4 %collective-permute-start.10 = (bf16[2,320,256]{2,1,0:T(8,128)(2,1)S(1)}, bf16[2,320,256]{2,1,0:T(8,128)(2,1)S(1)}, u32[]{:S(2)}, u32[]{:S(2)}) collective-permute-start(bf16[2,320,256]{2,1,0:T(8,128)(2,1)S(1)} %collective-permute-done.9.rest_2_), channel_id=1, source_target_pairs={{0,8},{4,12},{8,0},{12,4},{16,24},{20,28},{24,16},{28,20},{1,9},{5... | collective-permute-start | bytes 983048 | tf_op jit(solution)/shard_map/ppermute | solution.py:297
  51.2 5.2 %copy-start.12 = (bf16[512,256]{1,0:T(8,128)(2,1)}, bf16[512,256]{1,0:T(8,128)(2,1)S(1)}, u32[]{:S(2)}) copy-start(bf16[512,256]{1,0:T(8,128)(2,1)S(1)} %collective-permute-done.6.rest_0_.mixed_r) | copy-start | bytes 786436
  51.2 7.4 %copy-start.4 = (bf16[2,2,8,128,128]{4,3,2,1,0:T(8,128)(2,1)S(1)}, bf16[2,2,8,128,128]{4,3,2,1,0:T(8,128)(2,1)}, u32[]{:S(2)}) copy-start(bf16[2,2,8,128,128]{4,3,2,1,0:T(8,128)(2,1)} %param.6) | copy-start | bytes 3145732
  51.2 7.4 %copy-start.9 = (bf16[2,320,256]{2,1,0:T(8,128)(2,1)S(1)}, bf16[2,320,256]{2,1,0:T(8,128)(2,1)}, u32[]{:S(2)}) copy-start(bf16[2,320,256]{2,1,0:T(8,128)(2,1)} %copy-done.8) | copy-start | bytes 983044
  56.4 8.7 %collective-permute-start.11 = (bf16[2,320,256]{2,1,0:T(8,128)(2,1)S(1)}, bf16[2,320,256]{2,1,0:T(8,128)(2,1)S(1)}, u32[]{:S(2)}, u32[]{:S(2)}) collective-permute-start(bf16[2,320,256]{2,1,0:T(8,128)(2,1)S(1)} %get-tuple-element.46), channel_id=1, source_target_pairs={{0,8},{4,12},{8,0},{12,4},{16,24},{20,28},{24,16},{28,20},{1,9},{5... | collective-permute-start | bytes 983048 | tf_op jit(solution)/shard_map/ppermute | solution.py:297
  63.9 1.1 copy-start.6
  65.9 2.6 %copy-start.5 = (bf16[2,320,256]{2,1,0:T(8,128)(2,1)S(1)}, bf16[2,320,256]{2,1,0:T(8,128)(2,1)}, u32[]{:S(2)}) copy-start(bf16[2,320,256]{2,1,0:T(8,128)(2,1)} %add_convert_fusion.refs_1_.unread) | copy-start | bytes 983044
  65.9 4.3 %copy-start.11 = (bf16[512,256]{1,0:T(8,128)(2,1)S(1)}, bf16[512,256]{1,0:T(8,128)(2,1)}, u32[]{:S(2)}) copy-start(bf16[512,256]{1,0:T(8,128)(2,1)} %copy-done.10) | copy-start | bytes 786436
  65.9 3.2 %collective-permute-start.12 = (bf16[2560,256]{1,0:T(8,128)(2,1)}, bf16[2560,256]{1,0:T(8,128)(2,1)S(1)}, u32[]{:S(2)}, u32[]{:S(2)}) collective-permute-start(bf16[2560,256]{1,0:T(8,128)(2,1)} %in_order.1.w_o), channel_id=1, source_target_pairs={{0,4},{4,0},{8,12},{12,8},{16,20},{20,16},{24,28},{28,24},{1,5},{5... | collective-permute-start | bytes 3932168 | tf_op jit(solution)/shard_map/ppermute | solution.py:305
  66.0 13.3 %copy-start.2 = (bf16[2,2,128,2560]{3,2,1,0:T(8,128)(2,1)S(1)}, bf16[2,2,128,2560]{3,2,1,0:T(8,128)(2,1)}, u32[]{:S(2)}) copy-start(bf16[2,2,128,2560]{3,2,1,0:T(8,128)(2,1)} %param.5) | copy-start | bytes 7864324
  66.0 20.4 %collective-permute-start.18 = (bf16[2,320,256]{2,1,0:T(8,128)(2,1)}, bf16[2,320,256]{2,1,0:T(8,128)(2,1)S(1)}, u32[]{:S(2)}, u32[]{:S(2)}) collective-permute-start(bf16[2,320,256]{2,1,0:T(8,128)(2,1)} %get-tuple-element.57), channel_id=1, source_target_pairs={{0,8},{4,12},{8,0},{12,4},{16,24},{20,28},{24,16},{28,20},{1,9},{5... | collective-permute-start | bytes 983048 | tf_op jit(solution)/shard_map/ppermute | solution.py:297
  68.5 17.9 %collective-permute-start.19 = (bf16[2,320,256]{2,1,0:T(8,128)(2,1)S(1)}, bf16[2,320,256]{2,1,0:T(8,128)(2,1)S(1)}, u32[]{:S(2)}, u32[]{:S(2)}) collective-permute-start(bf16[2,320,256]{2,1,0:T(8,128)(2,1)S(1)} %copy-done.5), channel_id=1, source_target_pairs={{0,16},{4,20},{8,24},{12,28},{16,0},{20,4},{24,8},{28,12},{1,17},{... | collective-permute-start | bytes 983048 | tf_op jit(solution)/shard_map/ppermute | solution.py:297
  69.1 1.1 copy-start.14
  70.2 1.3 %copy-start.7 = (bf16[2560,256]{1,0:T(8,128)(2,1)S(1)}, bf16[2560,256]{1,0:T(8,128)(2,1)}, u32[]{:S(2)}) copy-start(bf16[2560,256]{1,0:T(8,128)(2,1)} %in_order.1.w_o) | copy-start | bytes 3932164
  71.5 0.9 copy-start.13
  72.5 1.3 %copy-start.15 = (bf16[2560,256]{1,0:T(8,128)(2,1)S(1)}, bf16[2560,256]{1,0:T(8,128)(2,1)}, u32[]{:S(2)}) copy-start(bf16[2560,256]{1,0:T(8,128)(2,1)} %copy-done.14) | copy-start | bytes 3932164
  76.2 19.6 %collective-permute-start.13 = (bf16[2,256,640]{2,1,0:T(8,128)(2,1)S(1)}, bf16[2,256,640]{2,1,0:T(8,128)(2,1)S(1)}, u32[]{:S(2)}, u32[]{:S(2)}) collective-permute-start(bf16[2,256,640]{2,1,0:T(8,128)(2,1)S(1)} %get-tuple-element.48), channel_id=1, source_target_pairs={{0,1},{1,0},{2,3},{3,2},{4,5},{5,4},{6,7},{7,6},{8,9},{9,8},{10,11... | collective-permute-start | bytes 1966088 | tf_op jit(solution)/shard_map/ppermute | solution.py:308
  77.7 18.2 %collective-permute-start.15 = (bf16[2,256,640]{2,1,0:T(8,128)(2,1)S(1)}, bf16[2,256,640]{2,1,0:T(8,128)(2,1)S(1)}, u32[]{:S(2)}, u32[]{:S(2)}) collective-permute-start(bf16[2,256,640]{2,1,0:T(8,128)(2,1)S(1)} %get-tuple-element.49), channel_id=1, source_target_pairs={{0,2},{1,3},{2,0},{3,1},{4,6},{5,7},{6,4},{7,5},{8,10},{9,11},{10,... | collective-permute-start | bytes 1966088 | tf_op jit(solution)/shard_map/ppermute | solution.py:308
  83.6 10.0 %collective-permute-start.17 = (bf16[2,320,256]{2,1,0:T(8,128)(2,1)S(1)}, bf16[2,320,256]{2,1,0:T(8,128)(2,1)S(1)}, u32[]{:S(2)}, u32[]{:S(2)}) collective-permute-start(bf16[2,320,256]{2,1,0:T(8,128)(2,1)S(1)} %get-tuple-element.54), channel_id=1, source_target_pairs={{0,8},{4,12},{8,0},{12,4},{16,24},{20,28},{24,16},{28,20},{1,9},{5... | collective-permute-start | bytes 983048 | tf_op jit(solution)/shard_map/ppermute | solution.py:297
  93.8 14.3 %collective-permute-start.20 = (bf16[2,320,256]{2,1,0:T(8,128)(2,1)S(1)}, bf16[2,320,256]{2,1,0:T(8,128)(2,1)S(1)}, u32[]{:S(2)}, u32[]{:S(2)}) collective-permute-start(bf16[2,320,256]{2,1,0:T(8,128)(2,1)S(1)} %get-tuple-element.58), channel_id=1, source_target_pairs={{0,8},{4,12},{8,0},{12,4},{16,24},{20,28},{24,16},{28,20},{1,9},{5... | collective-permute-start | bytes 983048 | tf_op jit(solution)/shard_map/ppermute | solution.py:297
  95.6 16.0 %collective-permute-start.21 = (bf16[2,320,256]{2,1,0:T(8,128)(2,1)S(1)}, bf16[2,320,256]{2,1,0:T(8,128)(2,1)S(1)}, u32[]{:S(2)}, u32[]{:S(2)}) collective-permute-start(bf16[2,320,256]{2,1,0:T(8,128)(2,1)S(1)} %get-tuple-element.59), channel_id=1, source_target_pairs={{0,16},{4,20},{8,24},{12,28},{16,0},{20,4},{24,8},{28,12},{1,17},{... | collective-permute-start | bytes 983048 | tf_op jit(solution)/shard_map/ppermute | solution.py:297
  95.7 16.1 %collective-permute-start.23 = (f32[320,256]{1,0:T(8,128)S(1)}, f32[320,256]{1,0:T(8,128)S(1)}, u32[]{:S(2)}, u32[]{:S(2)}) collective-permute-start(f32[320,256]{1,0:T(8,128)S(1)} %slice_bitcast_fusion.2), channel_id=1, source_target_pairs={{0,4},{4,0},{8,12},{12,8},{16,20},{20,16},{24,28},{28,24},{1,5},{5... | collective-permute-start | bytes 983048 | tf_op jit(solution)/shard_map/ppermute | solution.py:305
  96.1 16.7 %collective-permute-start.14 = (bf16[256,640]{1,0:T(8,128)(2,1)S(1)}, bf16[256,640]{1,0:T(8,128)(2,1)S(1)}, u32[]{:S(2)}, u32[]{:S(2)}) collective-permute-start(bf16[256,640]{1,0:T(8,128)(2,1)S(1)} %get-tuple-element.63), channel_id=1, source_target_pairs={{0,2},{1,3},{2,0},{3,1},{4,6},{5,7},{6,4},{7,5},{8,10},{9,11},{10,... | collective-permute-start | bytes 983048 | tf_op jit(solution)/shard_map/ppermute | solution.py:308
  96.7 16.1 %collective-permute-start.16 = (bf16[256,640]{1,0:T(8,128)(2,1)S(1)}, bf16[256,640]{1,0:T(8,128)(2,1)S(1)}, u32[]{:S(2)}, u32[]{:S(2)}) collective-permute-start(bf16[256,640]{1,0:T(8,128)(2,1)S(1)} %get-tuple-element.64), channel_id=1, source_target_pairs={{0,1},{1,0},{2,3},{3,2},{4,5},{5,4},{6,7},{7,6},{8,9},{9,8},{10,11... | collective-permute-start | bytes 983048 | tf_op jit(solution)/shard_map/ppermute | solution.py:308
  111.8 2.1 %collective-permute-start.22 = (f32[320,256]{1,0:T(8,128)S(1)}, f32[320,256]{1,0:T(8,128)S(1)}, u32[]{:S(2)}, u32[]{:S(2)}) collective-permute-start(f32[320,256]{1,0:T(8,128)S(1)} %slice_bitcast_fusion), channel_id=1, source_target_pairs={{0,4},{4,0},{8,12},{12,8},{16,20},{20,16},{24,28},{28,24},{1,5},{5... | collective-permute-start | bytes 983048 | tf_op jit(solution)/shard_map/ppermute | solution.py:305

commit v20 on v19

--- a/solution.py
+++ b/solution.py
@@ -232,13 +232,18 @@
     total[...] = own[...].astype(F32) + near[...].astype(F32) + far[...].astype(F32)
 
 
-def terms_kernel(n_node, idx, mixed_o, mixed_r, w_o, w_r, token, *outs):
+def terms_kernel(n_node, idx, mixed_o, mixed_r, w_o, w_r, token, *rest):
+    *outs, mixed_v, w_v, mixed_sems, sems = rest
+    copies = begin([(w_o, w_v.at[0]), (w_r, w_v.at[1])], sems)
+    copies += begin([(mixed_o, mixed_v.at[0]), (mixed_r, mixed_v.at[1])], mixed_sems)
     token[...] = jnp.zeros_like(token)
     depth = w_o.shape[0] // n_node
     half = mixed_o.shape[0] // 2
+    for copy in copies:
+        copy.wait()
     for j in range(n_node):
         rows = rows_at(idx[j], depth)
-        term = dot(mixed_o[...], w_o[rows, :], 1, 1) + dot(mixed_r[...], w_r[rows, :], 1, 1)
+        term = dot(mixed_v[0], w_v[0, rows, :], 1, 1) + dot(mixed_v[1], w_v[1, rows, :], 1, 1)
         term = term.astype(BF16)
         if n_node != 4:
             outs[j][...] = term
@@ -447,6 +452,7 @@
             + [pltpu.SemaphoreType.DMA((1,))],
             flops,
             2 * (2 * cot.size + mix.size + 2 * width * cols + 2 * tokens * cols),
+            vmem=60,
             out_specs=[VMEM, ANY],
         )(idx, token, cot, cot_s, mix, mix_s, *out_slots)
         if line4:
@@ -466,11 +472,13 @@
         token, *terms = call(
             functools.partial(terms_kernel, n_node),
             "terms",
-            [SMEM] + [VMEM] * 4,
+            [SMEM] + [ANY] * 4,
             [(16, 128)] + term_shapes,
-            [],
+            [pltpu.VMEM((2, tokens, cols), BF16), pltpu.VMEM((2, width, cols), BF16)]
+            + [pltpu.SemaphoreType.DMA((2,))] * 2,
             flops,
             2 * (2 * tokens * cols + 2 * width * cols + tokens * width),
+            vmem=60,
         )(idx_node, mixed_o, mixed_r, w_full, w_full_s)
         back_sends = call(
             gradient_kernel,

time: 115 us -> 118 us (1.026)
  Pallas kernels: 25.6 us -> 33.3 us
  local copies, waits for them, and re-layouts: 11 us -> 7.23 us
    unnamed x32 -> x36, local copies, waits for them, and re-layouts: 9.48 us -> 5.71 us
    pallas_call x1, Pallas kernels: 2.37 us -> 5.76 us  [body(): call(functools.partial(terms_kernel, n_node), 'terms', [SMEM] + [ANY] * 4...]
    pallas_call x1, Pallas kernels: 5.32 us -> 8.57 us  [body(): call(functools.partial(d_value_kernel, n_slots), 'd_value', [SMEM] + [ANY...]
  transfers between devices with their start and end apart: 24 -> 24, of which waited for: 9 -> 11; matrix products, arithmetic and copies ran while one was open for 3% -> 3% of each run, Pallas kernels for 22% -> 28%
where the time goes in v20:
time: 118 us
  waiting for transfers between devices  46.9 us (40%)
  Pallas kernels  33.3 us (28%)
  starting transfers between devices  24.2 us (21%)
  local copies, waits for them, and re-layouts  7.23 us (6%)
  other arithmetic  5.17 us (4%)
    ppermute x12, waiting for transfers between devices, move(): lax.ppermute(x, 'wide', [(2 * s + c, 2 * d + c) for s, d in pairs for c i...  45.5 us
    ppermute x12, starting transfers between devices, move(): lax.ppermute(x, 'wide', [(2 * s + c, 2 * d + c) for s, d in pairs for c i...  18.2 us
    pallas_call x1, Pallas kernels, body(): call(functools.partial(d_value_kernel, n_slots), 'd_value', [SMEM] + [ANY...  8.57 us
    pallas_call x1, Pallas kernels, body(): call(functools.partial(terms_kernel, n_node), 'terms', [SMEM] + [ANY] * 4...  5.76 us
    unnamed x36, local copies, waits for them, and re-layouts  5.71 us
    pallas_call x1, Pallas kernels, body(): call(functools.partial(grad_out_kernel, len(unread)), 'grad_out', [SMEM]...  5.11 us
    pallas_call x1, Pallas kernels, body(): call(functools.partial(part_kernel, n_slots - 1), 'value_ahead', [SMEM] +...  4.9 us
    ppermute x4, starting transfers between devices, flip(): return lax.ppermute(x, 'node', [(i, i ^ j) for i in range(n_node)])  4.4 us
  transfers between devices with their start and end apart: 24, of which 11 were waited for; matrix products, arithmetic and copies ran while one was open for 3% of the time, Pallas kernels for 28%

profile of v20, /device:TPU:0, one launch (start us, length us, event | category | flops | bytes accessed | tf_op | source)
XLA Modules:
  0.0 117.8 jit_solution(736684858157543274)
XLA Ops:
  0.6 0.0 copy-start
  0.7 1.3 %slice_bitcast_fusion.5 = (bf16[1,320,256]{2,1,0:T(8,128)(2,1)S(1)}, bf16[1,320,256]{2,1,0:T(8,128)(2,1)S(1)}, bf16[1,320,256]{2,1,0:T(8,128)(2,1)S(1)}, bf16[1,320,256]{2,1,0:T(8,128)(2,1)S(1)}) fusion(bf16[320,512]{1,0:T(8,128)(2,1)} %param.8, bf16[320,512]{1,0:T(8,128)(2,1)} %param.9), kind=kLoop, calls=%fused_computation.34 | loop fusion | bytes 1310720 | tf_op jit(solution)/shard_map/stack | solution.py:318
  2.0 0.1 broadcast_select_fusion
  2.1 0.5 collective-permute-start
  2.6 1.3 %collective-permute-done = bf16[2,320,256]{2,1,0:T(8,128)(2,1)S(1)} collective-permute-done((bf16[2,320,256]{2,1,0:T(8,128)(2,1)S(1)}, bf16[2,320,256]{2,1,0:T(8,128)(2,1)S(1)}, u32[]{:S(2)}, u32[]{:S(2)}) %collective-permute-start) | collective-permute-done | bytes 327712 | tf_op jit(solution)/shard_map/ppermute | solution.py:310
  3.8 0.4 collective-permute-start.1
  4.2 0.1 collective-permute-start.7
  4.4 0.4 collective-permute-start.2
  4.8 2.8 %collective-permute-start.3 = (bf16[2,320,256]{2,1,0:T(8,128)(2,1)S(1)}, bf16[2,320,256]{2,1,0:T(8,128)(2,1)S(1)}, u32[]{:S(2)}, u32[]{:S(2)}) collective-permute-start(bf16[2,320,256]{2,1,0:T(8,128)(2,1)S(1)} %pad_maximum_fusion.5.rest_0_), channel_id=1, source_target_pairs={{0,8},{4,12},{8,0},{12,4},{16,24},{20,28},{24,16},{28,20},{1,9},{5... | collective-permute-start | bytes 983048 | tf_op jit(solution)/shard_map/ppermute | solution.py:302
  7.6 2.6 %collective-permute-start.4 = (bf16[2,320,256]{2,1,0:T(8,128)(2,1)S(1)}, bf16[2,320,256]{2,1,0:T(8,128)(2,1)S(1)}, u32[]{:S(2)}, u32[]{:S(2)}) collective-permute-start(bf16[2,320,256]{2,1,0:T(8,128)(2,1)S(1)} %pad_maximum_fusion.5.rest_0_), channel_id=1, source_target_pairs={{0,16},{4,20},{8,24},{12,28},{16,0},{20,4},{24,8},{28,12},{1,17},{... | collective-permute-start | bytes 983048 | tf_op jit(solution)/shard_map/ppermute | solution.py:302
  10.2 12.5 %collective-permute-done.3.unread.rest_1_ = bf16[2,320,256]{2,1,0:T(8,128)(2,1)S(1)} collective-permute-done((bf16[2,320,256]{2,1,0:T(8,128)(2,1)S(1)}, bf16[2,320,256]{2,1,0:T(8,128)(2,1)S(1)}, u32[]{:S(2)}, u32[]{:S(2)}) %collective-permute-start.3) | collective-permute-done | bytes 327712 | tf_op jit(solution)/shard_map/ppermute | solution.py:302
  22.8 2.5 %collective-permute-done.4.first = bf16[2,320,256]{2,1,0:T(8,128)(2,1)S(1)} collective-permute-done((bf16[2,320,256]{2,1,0:T(8,128)(2,1)S(1)}, bf16[2,320,256]{2,1,0:T(8,128)(2,1)S(1)}, u32[]{:S(2)}, u32[]{:S(2)}) %collective-permute-start.4) | collective-permute-done | bytes 327712 | tf_op jit(solution)/shard_map/ppermute | solution.py:302
  25.3 0.8 relay.1
  26.1 0.7 copy-done.8
  26.8 0.4 collective-permute-start.5
  27.2 0.1 stack.67.idx
  27.3 1.6 %collective-permute-start.8 = (bf16[2,320,256]{2,1,0:T(8,128)(2,1)}, bf16[2,320,256]{2,1,0:T(8,128)(2,1)S(1)}, u32[]{:S(2)}, u32[]{:S(2)}) collective-permute-start(bf16[2,320,256]{2,1,0:T(8,128)(2,1)} %copy-done.8), channel_id=1, source_target_pairs={{0,8},{4,12},{8,0},{12,4},{16,24},{20,28},{24,16},{28,20},{1,9},{5... | collective-permute-start | bytes 983048 | tf_op jit(solution)/shard_map/ppermute | solution.py:302
  28.9 0.0 collective-permute-done.2.mix_s
  28.9 1.1 collective-permute-start.9
  30.0 1.7 %copy-done.1 = bf16[2,2,128,2560]{3,2,1,0:T(8,128)(2,1)S(1)} copy-done((bf16[2,2,128,2560]{3,2,1,0:T(8,128)(2,1)S(1)}, bf16[2,2,128,2560]{3,2,1,0:T(8,128)(2,1)}, u32[]{:S(2)}) %copy-start.1) | copy-done | bytes 2621464
  31.7 1.2 %copy-done.3 = bf16[2,2,8,128,128]{4,3,2,1,0:T(8,128)(2,1)S(1)} copy-done((bf16[2,2,8,128,128]{4,3,2,1,0:T(8,128)(2,1)S(1)}, bf16[2,2,8,128,128]{4,3,2,1,0:T(8,128)(2,1)}, u32[]{:S(2)}) %copy-start.3) | copy-done | bytes 1048600
  33.0 4.9 %value_ahead.1 = (f32[2,512,256]{2,1,0:T(8,128)S(1)}, bf16[2,512,640]{2,1,0:T(8,128)(2,1)S(1)}, bf16[2,4,4,128,128]{4,3,2,1,0:T(8,128)(2,1)S(1)}) custom-call(s32[5]{0:T(128)S(1)} %stack.67.idx, bf16[512,2560]{1,0:T(8,128)(2,1)S(1)} %bitcast.54, bf16[512,2560]{1,0:T(8,128)(2,1)} %collective-permute-done.1.x_s.right_s, bf16[4,8,128,128]{3,2,1,0:T(8,128)(2,1)S(1)} %bitcast.58, ...), custom_call_target="tpu_custom_call" | custom-call | flops 1342177280 | bytes 11272192 | tf_op jit(solution)/shard_map/value_ahead/pallas_call | solution.py:401
  37.9 6.8 %collective-permute-done.5.slot = bf16[2,320,256]{2,1,0:T(8,128)(2,1)} collective-permute-done((bf16[2,320,256]{2,1,0:T(8,128)(2,1)}, bf16[2,320,256]{2,1,0:T(8,128)(2,1)}, u32[]{:S(2)}, u32[]{:S(2)}) %collective-permute-start.5) | collective-permute-done | bytes 327712 | tf_op jit(solution)/shard_map/ppermute | solution.py:302
  44.6 2.5 %mixed.1 = (bf16[512,256]{1,0:T(8,128)(2,1)S(1)}, bf16[512,256]{1,0:T(8,128)(2,1)S(1)}) custom-call(s32[5]{0:T(128)S(1)} %stack.67.idx, f32[2,512,256]{2,1,0:T(8,128)S(1)} %get-tuple-element.36.part, bf16[2,512,640]{2,1,0:T(8,128)(2,1)S(1)} %get-tuple-element.37.last, bf16[2,4,4,128,128]{4,3,2,1,0:T(8,128)(2,1)S(1)} %get-tuple-element.38.weights, ...), custom_call_target="tpu_custom_call" | custom-call | flops 335544320 | bytes 3932160 | tf_op jit(solution)/shard_map/mixed/pallas_call | solution.py:414
  47.2 0.1 collective-permute-start.6
  47.2 1.0 collective-permute-done.9.rest_2_
  48.2 3.0 %collective-permute-start.10 = (bf16[2,320,256]{2,1,0:T(8,128)(2,1)S(1)}, bf16[2,320,256]{2,1,0:T(8,128)(2,1)S(1)}, u32[]{:S(2)}, u32[]{:S(2)}) collective-permute-start(bf16[2,320,256]{2,1,0:T(8,128)(2,1)S(1)} %collective-permute-done.9.rest_2_), channel_id=1, source_target_pairs={{0,8},{4,12},{8,0},{12,4},{16,24},{20,28},{24,16},{28,20},{1,9},{5... | collective-permute-start | bytes 983048 | tf_op jit(solution)/shard_map/ppermute | solution.py:302
  51.2 5.1 %grad_out.1 = (bf16[16,128]{1,0:T(8,128)(2,1)S(1)}, bf16[2,320,256]{2,1,0:T(8,128)(2,1)S(1)}, bf16[2,320,256]{2,1,0:T(8,128)(2,1)S(1)}, bf16[2,320,256]{2,1,0:T(8,128)(2,1)S(1)}, bf16[2,320,256]{2,1,0:T(8,128)(2,1)}) custom-call(s32[5]{0:T(128)S(1)} %stack.67.idx, bf16[512,2560]{1,0:T(8,128)(2,1)S(1)} %bitcast.52, ...), custom_call_target="tpu_custom_call" | custom-call | flops 1342177280 | bytes 7077888 | tf_op jit(solution)/shard_map/grad_out/pallas_call | solution.py:436
  56.4 0.6 copy-done.13
  57.0 0.0 collective-permute-start.11
  57.0 0.9 collective-permute-done.10.rest_3_
  57.9 0.7 copy-done.17
  58.6 8.6 %d_value.1 = (bf16[256,1024]{1,0:T(8,128)(2,1)}, bf16[2560,256]{1,0:T(8,128)(2,1)}) custom-call(s32[5]{0:T(128)} %copy-done.11, bf16[16,128]{1,0:T(8,128)(2,1)} %copy-done.13, bf16[512,2560]{1,0:T(8,128)(2,1)} %bitcast.50, bf16[512,2560]{1,0:T(8,128)(2,1)} %collective-permute-done.7.cot_s, bf16[4,8,128,128]{3,2,1,0:T(8,128)(2,1)} %bitcast.57, ...), custom_call_target="tpu_custom_call" | custom-call | flops 1342177280 | bytes 9437184 | tf_op jit(solution)/shard_map/d_value/pallas_call | solution.py:446
  67.2 0.8 add_convert_fusion.refs_1_.unread
  68.0 0.6 pad_add_fusion.idx
  68.6 2.5 %collective-permute-start.18 = (bf16[2,320,256]{2,1,0:T(8,128)(2,1)}, bf16[2,320,256]{2,1,0:T(8,128)(2,1)}, u32[]{:S(2)}, u32[]{:S(2)}) collective-permute-start(bf16[2,320,256]{2,1,0:T(8,128)(2,1)} %copy-done.15), channel_id=1, source_target_pairs={{0,8},{4,12},{8,0},{12,4},{16,24},{20,28},{24,16},{28,20},{1,9},{5... | collective-permute-start | bytes 983048 | tf_op jit(solution)/shard_map/ppermute | solution.py:302
  71.1 0.2 collective-permute-start.19
  71.3 0.1 collective-permute-done.12.w_r
  71.4 5.8 %terms.1 = (bf16[16,128]{1,0:T(8,128)(2,1)}, bf16[2,256,640]{2,1,0:T(8,128)(2,1)}, bf16[2,256,640]{2,1,0:T(8,128)(2,1)}, bf16[4,256,640]{2,1,0:T(8,128)(2,1)}) custom-call(s32[4]{0:T(128)} %pad_add_fusion.idx, bf16[512,256]{1,0:T(8,128)(2,1)} %copy-done.9, bf16[512,256]{1,0:T(8,128)(2,1)} %copy-done.10, bf16[2560,256]{1,0:T(8,128)(2,1)} %in_order.1.w_o, ...), custom_call_target="tpu_custom_call" | custom-call | flops 1342177280 | bytes 5767168 | tf_op jit(solution)/shard_map/terms/pallas_call | solution.py:472
  77.1 1.6 %collective-permute-start.13 = (bf16[2,256,640]{2,1,0:T(8,128)(2,1)}, bf16[2,256,640]{2,1,0:T(8,128)(2,1)S(1)}, u32[]{:S(2)}, u32[]{:S(2)}) collective-permute-start(bf16[2,256,640]{2,1,0:T(8,128)(2,1)} %get-tuple-element.48), channel_id=1, source_target_pairs={{0,1},{1,0},{2,3},{3,2},{4,5},{5,4},{6,7},{7,6},{8,9},{9,8},{10,11... | collective-permute-start | bytes 1966088 | tf_op jit(solution)/shard_map/ppermute | solution.py:313
  78.7 1.5 %collective-permute-start.15 = (bf16[2,256,640]{2,1,0:T(8,128)(2,1)}, bf16[2,256,640]{2,1,0:T(8,128)(2,1)S(1)}, u32[]{:S(2)}, u32[]{:S(2)}) collective-permute-start(bf16[2,256,640]{2,1,0:T(8,128)(2,1)} %get-tuple-element.49), channel_id=1, source_target_pairs={{0,2},{1,3},{2,0},{3,1},{4,6},{5,7},{6,4},{7,5},{8,10},{9,11},{10,... | collective-permute-start | bytes 1966088 | tf_op jit(solution)/shard_map/ppermute | solution.py:313
  80.2 0.7 copy-done.14
  80.9 4.4 %grad_value.1 = (bf16[2,320,256]{2,1,0:T(8,128)(2,1)S(1)}, bf16[2,320,256]{2,1,0:T(8,128)(2,1)S(1)}, bf16[2,320,256]{2,1,0:T(8,128)(2,1)S(1)}, bf16[2,320,256]{2,1,0:T(8,128)(2,1)S(1)}) custom-call(s32[5]{0:T(128)S(1)} %copy-done.12, bf16[16,128]{1,0:T(8,128)(2,1)S(1)} %copy-done.14, bf16[2,320,256]{2,1,0:T(8,128)(2,1)S(1)} %copy-done.4, ...), custom_call_target="tpu_custom_call" | custom-call | flops 1342177280 | bytes 7077888 | tf_op jit(solution)/shard_map/grad_value/pallas_call | solution.py:483
  85.3 2.5 %collective-permute-start.17 = (bf16[2,320,256]{2,1,0:T(8,128)(2,1)S(1)}, bf16[2,320,256]{2,1,0:T(8,128)(2,1)S(1)}, u32[]{:S(2)}, u32[]{:S(2)}) collective-permute-start(bf16[2,320,256]{2,1,0:T(8,128)(2,1)S(1)} %get-tuple-element.54), channel_id=1, source_target_pairs={{0,8},{4,12},{8,0},{12,4},{16,24},{20,28},{24,16},{28,20},{1,9},{5... | collective-permute-start | bytes 983048 | tf_op jit(solution)/shard_map/ppermute | solution.py:302
  87.8 0.2 convert_element_type.53
  88.0 1.0 collective-permute-done.19.far
  89.1 6.9 %collective-permute-done.17.got = bf16[2,320,256]{2,1,0:T(8,128)(2,1)S(1)} collective-permute-done((bf16[2,320,256]{2,1,0:T(8,128)(2,1)S(1)}, bf16[2,320,256]{2,1,0:T(8,128)(2,1)S(1)}, u32[]{:S(2)}, u32[]{:S(2)}) %collective-permute-start.17) | collective-permute-done | bytes 327712 | tf_op jit(solution)/shard_map/ppermute | solution.py:302
  95.9 1.3 %sum.1 = (bf16[2,320,256]{2,1,0:T(8,128)(2,1)S(1)}, bf16[2,320,256]{2,1,0:T(8,128)(2,1)S(1)}, f32[2,320,256]{2,1,0:T(8,128)S(1)}) custom-call(bf16[2,320,256]{2,1,0:T(8,128)(2,1)S(1)} %get-tuple-element.53.block, bf16[2,320,256]{2,1,0:T(8,128)(2,1)S(1)} %collective-permute-done.17.got, bf16[2,320,256]{2,1,0:T(8,128)(2,1)S(1)} %get-tuple-element.55.beside, ...), custom_call_target="tpu_custom_call" | custom-call | bytes 1048576 | tf_op jit(solution)/shard_map/sum/pallas_call | solution.py:494
  97.2 1.2 %collective-permute-start.20 = (bf16[2,320,256]{2,1,0:T(8,128)(2,1)S(1)}, bf16[2,320,256]{2,1,0:T(8,128)(2,1)S(1)}, u32[]{:S(2)}, u32[]{:S(2)}) collective-permute-start(bf16[2,320,256]{2,1,0:T(8,128)(2,1)S(1)} %get-tuple-element.58), channel_id=1, source_target_pairs={{0,8},{4,12},{8,0},{12,4},{16,24},{20,28},{24,16},{28,20},{1,9},{5... | collective-permute-start | bytes 983048 | tf_op jit(solution)/shard_map/ppermute | solution.py:302
  98.4 0.4 collective-permute-start.21
  98.7 0.1 collective-permute-start.23
  98.8 0.1 convert_element_type.54
  98.9 0.1 convert_element_type.58
  99.0 0.1 fusion.8
  99.2 0.6 collective-permute-start.14
  99.7 0.8 collective-permute-start.16
  100.5 11.5 %collective-permute-done.20 = bf16[2,320,256]{2,1,0:T(8,128)(2,1)S(1)} collective-permute-done((bf16[2,320,256]{2,1,0:T(8,128)(2,1)S(1)}, bf16[2,320,256]{2,1,0:T(8,128)(2,1)S(1)}, u32[]{:S(2)}, u32[]{:S(2)}) %collective-permute-start.20) | collective-permute-done | bytes 327712 | tf_op jit(solution)/shard_map/ppermute | solution.py:302
  112.0 2.5 %collective-permute-done.21 = bf16[2,320,256]{2,1,0:T(8,128)(2,1)S(1)} collective-permute-done((bf16[2,320,256]{2,1,0:T(8,128)(2,1)S(1)}, bf16[2,320,256]{2,1,0:T(8,128)(2,1)S(1)}, u32[]{:S(2)}, u32[]{:S(2)}) %collective-permute-start.21) | collective-permute-done | bytes 327712 | tf_op jit(solution)/shard_map/ppermute | solution.py:302
  114.5 0.1 convert_add_fusion
  114.7 0.1 collective-permute-start.22
  114.8 0.9 pad_maximum_fusion.2
  115.7 0.2 fusion.7
  115.9 0.9 pad_maximum_fusion
  116.9 0.9 pad_maximum_fusion.1
  (51 shorter events, 0.3 us)
Async XLA Ops:
  0.6 3.6 %copy-start = (bf16[2,2,128,2560]{3,2,1,0:T(8,128)(2,1)S(1)}, bf16[2,2,128,2560]{3,2,1,0:T(8,128)(2,1)}, u32[]{:S(2)}) copy-start(bf16[2,2,128,2560]{3,2,1,0:T(8,128)(2,1)} %param.7) | copy-start | bytes 7864324
  2.1 1.8 %collective-permute-start = (bf16[2,320,256]{2,1,0:T(8,128)(2,1)S(1)}, bf16[2,320,256]{2,1,0:T(8,128)(2,1)S(1)}, u32[]{:S(2)}, u32[]{:S(2)}) collective-permute-start(bf16[2,320,256]{2,1,0:T(8,128)(2,1)S(1)} %get-tuple-element.70), channel_id=1, source_target_pairs={{0,4},{4,0},{8,12},{12,8},{16,20},{20,16},{24,28},{28,24},{1,5},{5... | collective-permute-start | bytes 983048 | tf_op jit(solution)/shard_map/ppermute | solution.py:310
  3.8 26.1 %collective-permute-start.1 = (bf16[512,2560]{1,0:T(8,128)(2,1)}, bf16[512,2560]{1,0:T(8,128)(2,1)}, u32[]{:S(2)}, u32[]{:S(2)}) collective-permute-start(bf16[512,2560]{1,0:T(8,128)(2,1)} %bitcast.53), channel_id=1, source_target_pairs={{0,4},{4,0},{8,12},{12,8},{16,20},{20,16},{24,28},{28,24},{1,5},{5... | collective-permute-start | bytes 7864328 | tf_op jit(solution)/shard_map/ppermute | solution.py:310
  4.2 47.0 %collective-permute-start.7 = (bf16[512,2560]{1,0:T(8,128)(2,1)S(1)}, bf16[512,2560]{1,0:T(8,128)(2,1)}, u32[]{:S(2)}, u32[]{:S(2)}) collective-permute-start(bf16[512,2560]{1,0:T(8,128)(2,1)S(1)} %bitcast.51), channel_id=1, source_target_pairs={{0,4},{4,0},{8,12},{12,8},{16,20},{20,16},{24,28},{28,24},{1,5},{5... | collective-permute-start | bytes 7864328 | tf_op jit(solution)/shard_map/ppermute | solution.py:310
  4.4 24.5 %collective-permute-start.2 = (bf16[4,8,128,128]{3,2,1,0:T(8,128)(2,1)}, bf16[4,8,128,128]{3,2,1,0:T(8,128)(2,1)}, u32[]{:S(2)}, u32[]{:S(2)}) collective-permute-start(bf16[4,8,128,128]{3,2,1,0:T(8,128)(2,1)} %bitcast.56), channel_id=1, source_target_pairs={{0,4},{4,0},{8,12},{12,8},{16,20},{20,16},{24,28},{28,24},{1,5},{5... | collective-permute-start | bytes 3145736 | tf_op jit(solution)/shard_map/ppermute | solution.py:310
  4.8 17.9 %collective-permute-start.3 = (bf16[2,320,256]{2,1,0:T(8,128)(2,1)S(1)}, bf16[2,320,256]{2,1,0:T(8,128)(2,1)S(1)}, u32[]{:S(2)}, u32[]{:S(2)}) collective-permute-start(bf16[2,320,256]{2,1,0:T(8,128)(2,1)S(1)} %pad_maximum_fusion.5.rest_0_), channel_id=1, source_target_pairs={{0,8},{4,12},{8,0},{12,4},{16,24},{20,28},{24,16},{28,20},{1,9},{5... | collective-permute-start | bytes 983048 | tf_op jit(solution)/shard_map/ppermute | solution.py:302
  7.6 17.7 %collective-permute-start.4 = (bf16[2,320,256]{2,1,0:T(8,128)(2,1)S(1)}, bf16[2,320,256]{2,1,0:T(8,128)(2,1)S(1)}, u32[]{:S(2)}, u32[]{:S(2)}) collective-permute-start(bf16[2,320,256]{2,1,0:T(8,128)(2,1)S(1)} %pad_maximum_fusion.5.rest_0_), channel_id=1, source_target_pairs={{0,16},{4,20},{8,24},{12,28},{16,0},{20,4},{24,8},{28,12},{1,17},{... | collective-permute-start | bytes 983048 | tf_op jit(solution)/shard_map/ppermute | solution.py:302
  26.1 0.7 copy-start.8
  26.8 17.9 %collective-permute-start.5 = (bf16[2,320,256]{2,1,0:T(8,128)(2,1)}, bf16[2,320,256]{2,1,0:T(8,128)(2,1)}, u32[]{:S(2)}, u32[]{:S(2)}) collective-permute-start(bf16[2,320,256]{2,1,0:T(8,128)(2,1)} %get-tuple-element.35.rest_2_), channel_id=1, source_target_pairs={{0,8},{4,12},{8,0},{12,4},{16,24},{20,28},{24,16},{28,20},{1,9},{5... | collective-permute-start | bytes 983048 | tf_op jit(solution)/shard_map/ppermute | solution.py:302
  27.3 23.9 %copy-start.11 = (s32[5]{0:T(128)}, s32[5]{0:T(128)S(1)}, u32[]{:S(2)}) copy-start(s32[5]{0:T(128)S(1)} %stack.67.idx) | copy-start | bytes 64
  27.3 23.9 %collective-permute-start.8 = (bf16[2,320,256]{2,1,0:T(8,128)(2,1)}, bf16[2,320,256]{2,1,0:T(8,128)(2,1)S(1)}, u32[]{:S(2)}, u32[]{:S(2)}) collective-permute-start(bf16[2,320,256]{2,1,0:T(8,128)(2,1)} %copy-done.8), channel_id=1, source_target_pairs={{0,8},{4,12},{8,0},{12,4},{16,24},{20,28},{24,16},{28,20},{1,9},{5... | collective-permute-start | bytes 983048 | tf_op jit(solution)/shard_map/ppermute | solution.py:302
  28.9 19.3 %collective-permute-start.9 = (bf16[2,320,256]{2,1,0:T(8,128)(2,1)}, bf16[2,320,256]{2,1,0:T(8,128)(2,1)S(1)}, u32[]{:S(2)}, u32[]{:S(2)}) collective-permute-start(bf16[2,320,256]{2,1,0:T(8,128)(2,1)} %copy-done.8), channel_id=1, source_target_pairs={{0,16},{4,20},{8,24},{12,28},{16,0},{20,4},{24,8},{28,12},{1,17},{... | collective-permute-start | bytes 983048 | tf_op jit(solution)/shard_map/ppermute | solution.py:302
  30.0 1.7 %copy-start.1 = (bf16[2,2,128,2560]{3,2,1,0:T(8,128)(2,1)S(1)}, bf16[2,2,128,2560]{3,2,1,0:T(8,128)(2,1)}, u32[]{:S(2)}) copy-start(bf16[2,2,128,2560]{3,2,1,0:T(8,128)(2,1)} %param.5) | copy-start | bytes 7864324
  31.7 1.2 %copy-start.3 = (bf16[2,2,8,128,128]{4,3,2,1,0:T(8,128)(2,1)S(1)}, bf16[2,2,8,128,128]{4,3,2,1,0:T(8,128)(2,1)}, u32[]{:S(2)}) copy-start(bf16[2,2,8,128,128]{4,3,2,1,0:T(8,128)(2,1)} %param.6) | copy-start | bytes 3145732
  47.1 9.2 %copy-start.9 = (bf16[512,256]{1,0:T(8,128)(2,1)}, bf16[512,256]{1,0:T(8,128)(2,1)S(1)}, u32[]{:S(2)}) copy-start(bf16[512,256]{1,0:T(8,128)(2,1)S(1)} %get-tuple-element.39.mixed_o) | copy-start | bytes 786436
  47.2 4.0 %collective-permute-start.6 = (bf16[512,256]{1,0:T(8,128)(2,1)S(1)}, bf16[512,256]{1,0:T(8,128)(2,1)S(1)}, u32[]{:S(2)}, u32[]{:S(2)}) collective-permute-start(bf16[512,256]{1,0:T(8,128)(2,1)S(1)} %get-tuple-element.40.mixed_s), channel_id=1, source_target_pairs={{0,4},{4,0},{8,12},{12,8},{16,20},{20,16},{24,28},{28,24},{1,5},{5... | collective-permute-start | bytes 786440 | tf_op jit(solution)/shard_map/ppermute | solution.py:310
  48.2 8.1 %copy-start.6 = (bf16[2,320,256]{2,1,0:T(8,128)(2,1)}, bf16[2,320,256]{2,1,0:T(8,128)(2,1)S(1)}, u32[]{:S(2)}) copy-start(bf16[2,320,256]{2,1,0:T(8,128)(2,1)S(1)} %collective-permute-done.9.rest_2_) | copy-start | bytes 983044
  48.2 9.6 %collective-permute-start.10 = (bf16[2,320,256]{2,1,0:T(8,128)(2,1)S(1)}, bf16[2,320,256]{2,1,0:T(8,128)(2,1)S(1)}, u32[]{:S(2)}, u32[]{:S(2)}) collective-permute-start(bf16[2,320,256]{2,1,0:T(8,128)(2,1)S(1)} %collective-permute-done.9.rest_2_), channel_id=1, source_target_pairs={{0,8},{4,12},{8,0},{12,4},{16,24},{20,28},{24,16},{28,20},{1,9},{5... | collective-permute-start | bytes 983048 | tf_op jit(solution)/shard_map/ppermute | solution.py:302
  51.2 5.2 %copy-start.5 = (bf16[2,320,256]{2,1,0:T(8,128)(2,1)}, bf16[2,320,256]{2,1,0:T(8,128)(2,1)S(1)}, u32[]{:S(2)}) copy-start(bf16[2,320,256]{2,1,0:T(8,128)(2,1)S(1)} %collective-permute-done.8.rest_1_) | copy-start | bytes 983044
  51.2 5.2 %copy-start.10 = (bf16[512,256]{1,0:T(8,128)(2,1)}, bf16[512,256]{1,0:T(8,128)(2,1)S(1)}, u32[]{:S(2)}) copy-start(bf16[512,256]{1,0:T(8,128)(2,1)S(1)} %collective-permute-done.6.rest_0_.mixed_r) | copy-start | bytes 786436
  56.4 0.6 copy-start.13
  57.0 10.2 %copy-start.15 = (bf16[2,320,256]{2,1,0:T(8,128)(2,1)}, bf16[2,320,256]{2,1,0:T(8,128)(2,1)S(1)}, u32[]{:S(2)}) copy-start(bf16[2,320,256]{2,1,0:T(8,128)(2,1)S(1)} %get-tuple-element.57) | copy-start | bytes 983044
  57.0 10.2 %collective-permute-start.11 = (bf16[2,320,256]{2,1,0:T(8,128)(2,1)}, bf16[2,320,256]{2,1,0:T(8,128)(2,1)S(1)}, u32[]{:S(2)}, u32[]{:S(2)}) collective-permute-start(bf16[2,320,256]{2,1,0:T(8,128)(2,1)} %get-tuple-element.46), channel_id=1, source_target_pairs={{0,8},{4,12},{8,0},{12,4},{16,24},{20,28},{24,16},{28,20},{1,9},{5... | collective-permute-start | bytes 983048 | tf_op jit(solution)/shard_map/ppermute | solution.py:302
  57.9 0.7 copy-start.17
  68.0 3.1 %copy-start.4 = (bf16[2,320,256]{2,1,0:T(8,128)(2,1)S(1)}, bf16[2,320,256]{2,1,0:T(8,128)(2,1)}, u32[]{:S(2)}) copy-start(bf16[2,320,256]{2,1,0:T(8,128)(2,1)} %add_convert_fusion.refs_1_.unread) | copy-start | bytes 983044
  68.0 3.4 %collective-permute-start.12 = (bf16[2560,256]{1,0:T(8,128)(2,1)}, bf16[2560,256]{1,0:T(8,128)(2,1)}, u32[]{:S(2)}, u32[]{:S(2)}) collective-permute-start(bf16[2560,256]{1,0:T(8,128)(2,1)} %in_order.1.w_o), channel_id=1, source_target_pairs={{0,4},{4,0},{8,12},{12,8},{16,20},{20,16},{24,28},{28,24},{1,5},{5... | collective-permute-start | bytes 3932168 | tf_op jit(solution)/shard_map/ppermute | solution.py:310
  68.6 11.6 %copy-start.2 = (bf16[2,2,128,2560]{3,2,1,0:T(8,128)(2,1)S(1)}, bf16[2,2,128,2560]{3,2,1,0:T(8,128)(2,1)}, u32[]{:S(2)}) copy-start(bf16[2,2,128,2560]{3,2,1,0:T(8,128)(2,1)} %param.5) | copy-start | bytes 7864324
  68.6 11.6 %copy-start.7 = (bf16[256,1024]{1,0:T(8,128)(2,1)S(1)}, bf16[256,1024]{1,0:T(8,128)(2,1)}, u32[]{:S(2)}) copy-start(bf16[256,1024]{1,0:T(8,128)(2,1)} %get-tuple-element.51.left_ref) | copy-start | bytes 1572868
  68.6 11.6 %copy-start.12 = (s32[5]{0:T(128)S(1)}, s32[5]{0:T(128)}, u32[]{:S(2)}) copy-start(s32[5]{0:T(128)} %copy-done.11) | copy-start | bytes 64
  68.6 19.4 %collective-permute-start.18 = (bf16[2,320,256]{2,1,0:T(8,128)(2,1)}, bf16[2,320,256]{2,1,0:T(8,128)(2,1)}, u32[]{:S(2)}, u32[]{:S(2)}) collective-permute-start(bf16[2,320,256]{2,1,0:T(8,128)(2,1)} %copy-done.15), channel_id=1, source_target_pairs={{0,8},{4,12},{8,0},{12,4},{16,24},{20,28},{24,16},{28,20},{1,9},{5... | collective-permute-start | bytes 983048 | tf_op jit(solution)/shard_map/ppermute | solution.py:302
  71.1 18.0 %collective-permute-start.19 = (bf16[2,320,256]{2,1,0:T(8,128)(2,1)S(1)}, bf16[2,320,256]{2,1,0:T(8,128)(2,1)}, u32[]{:S(2)}, u32[]{:S(2)}) collective-permute-start(bf16[2,320,256]{2,1,0:T(8,128)(2,1)S(1)} %copy-done.4), channel_id=1, source_target_pairs={{0,16},{4,20},{8,24},{12,28},{16,0},{20,4},{24,8},{28,12},{1,17},{... | collective-permute-start | bytes 983048 | tf_op jit(solution)/shard_map/ppermute | solution.py:302
  77.1 21.7 %collective-permute-start.13 = (bf16[2,256,640]{2,1,0:T(8,128)(2,1)}, bf16[2,256,640]{2,1,0:T(8,128)(2,1)S(1)}, u32[]{:S(2)}, u32[]{:S(2)}) collective-permute-start(bf16[2,256,640]{2,1,0:T(8,128)(2,1)} %get-tuple-element.48), channel_id=1, source_target_pairs={{0,1},{1,0},{2,3},{3,2},{4,5},{5,4},{6,7},{7,6},{8,9},{9,8},{10,11... | collective-permute-start | bytes 1966088 | tf_op jit(solution)/shard_map/ppermute | solution.py:313
  78.7 20.2 %collective-permute-start.15 = (bf16[2,256,640]{2,1,0:T(8,128)(2,1)}, bf16[2,256,640]{2,1,0:T(8,128)(2,1)S(1)}, u32[]{:S(2)}, u32[]{:S(2)}) collective-permute-start(bf16[2,256,640]{2,1,0:T(8,128)(2,1)} %get-tuple-element.49), channel_id=1, source_target_pairs={{0,2},{1,3},{2,0},{3,1},{4,6},{5,7},{6,4},{7,5},{8,10},{9,11},{10,... | collective-permute-start | bytes 1966088 | tf_op jit(solution)/shard_map/ppermute | solution.py:313
  80.2 0.7 copy-start.14
  80.9 6.9 %copy-start.16 = (bf16[4,256,640]{2,1,0:T(8,128)(2,1)S(1)}, bf16[4,256,640]{2,1,0:T(8,128)(2,1)}, u32[]{:S(2)}) copy-start(bf16[4,256,640]{2,1,0:T(8,128)(2,1)} %get-tuple-element.47) | copy-start | bytes 3932164
  85.3 10.6 %collective-permute-start.17 = (bf16[2,320,256]{2,1,0:T(8,128)(2,1)S(1)}, bf16[2,320,256]{2,1,0:T(8,128)(2,1)S(1)}, u32[]{:S(2)}, u32[]{:S(2)}) collective-permute-start(bf16[2,320,256]{2,1,0:T(8,128)(2,1)S(1)} %get-tuple-element.54), channel_id=1, source_target_pairs={{0,8},{4,12},{8,0},{12,4},{16,24},{20,28},{24,16},{28,20},{1,9},{5... | collective-permute-start | bytes 983048 | tf_op jit(solution)/shard_map/ppermute | solution.py:302
  97.2 14.8 %collective-permute-start.20 = (bf16[2,320,256]{2,1,0:T(8,128)(2,1)S(1)}, bf16[2,320,256]{2,1,0:T(8,128)(2,1)S(1)}, u32[]{:S(2)}, u32[]{:S(2)}) collective-permute-start(bf16[2,320,256]{2,1,0:T(8,128)(2,1)S(1)} %get-tuple-element.58), channel_id=1, source_target_pairs={{0,8},{4,12},{8,0},{12,4},{16,24},{20,28},{24,16},{28,20},{1,9},{5... | collective-permute-start | bytes 983048 | tf_op jit(solution)/shard_map/ppermute | solution.py:302
  98.4 16.1 %collective-permute-start.21 = (bf16[2,320,256]{2,1,0:T(8,128)(2,1)S(1)}, bf16[2,320,256]{2,1,0:T(8,128)(2,1)S(1)}, u32[]{:S(2)}, u32[]{:S(2)}) collective-permute-start(bf16[2,320,256]{2,1,0:T(8,128)(2,1)S(1)} %get-tuple-element.59), channel_id=1, source_target_pairs={{0,16},{4,20},{8,24},{12,28},{16,0},{20,4},{24,8},{28,12},{1,17},{... | collective-permute-start | bytes 983048 | tf_op jit(solution)/shard_map/ppermute | solution.py:302
  98.7 16.0 %collective-permute-start.23 = (f32[320,256]{1,0:T(8,128)S(1)}, f32[320,256]{1,0:T(8,128)S(1)}, u32[]{:S(2)}, u32[]{:S(2)}) collective-permute-start(f32[320,256]{1,0:T(8,128)S(1)} %slice_bitcast_fusion.2), channel_id=1, source_target_pairs={{0,4},{4,0},{8,12},{12,8},{16,20},{20,16},{24,28},{28,24},{1,5},{5... | collective-permute-start | bytes 983048 | tf_op jit(solution)/shard_map/ppermute | solution.py:310
  99.2 16.5 %collective-permute-start.14 = (bf16[256,640]{1,0:T(8,128)(2,1)S(1)}, bf16[256,640]{1,0:T(8,128)(2,1)S(1)}, u32[]{:S(2)}, u32[]{:S(2)}) collective-permute-start(bf16[256,640]{1,0:T(8,128)(2,1)S(1)} %get-tuple-element.63), channel_id=1, source_target_pairs={{0,2},{1,3},{2,0},{3,1},{4,6},{5,7},{6,4},{7,5},{8,10},{9,11},{10,... | collective-permute-start | bytes 983048 | tf_op jit(solution)/shard_map/ppermute | solution.py:313
  99.7 16.0 %collective-permute-start.16 = (bf16[256,640]{1,0:T(8,128)(2,1)S(1)}, bf16[256,640]{1,0:T(8,128)(2,1)S(1)}, u32[]{:S(2)}, u32[]{:S(2)}) collective-permute-start(bf16[256,640]{1,0:T(8,128)(2,1)S(1)} %get-tuple-element.64), channel_id=1, source_target_pairs={{0,1},{1,0},{2,3},{3,2},{4,5},{5,4},{6,7},{7,6},{8,9},{9,8},{10,11... | collective-permute-start | bytes 983048 | tf_op jit(solution)/shard_map/ppermute | solution.py:313
  114.7 2.1 %collective-permute-start.22 = (f32[320,256]{1,0:T(8,128)S(1)}, f32[320,256]{1,0:T(8,128)S(1)}, u32[]{:S(2)}, u32[]{:S(2)}) collective-permute-start(f32[320,256]{1,0:T(8,128)S(1)} %slice_bitcast_fusion), channel_id=1, source_target_pairs={{0,4},{4,0},{8,12},{12,8},{16,20},{20,16},{24,28},{28,24},{1,5},{5... | collective-permute-start | bytes 983048 | tf_op jit(solution)/shard_map/ppermute | solution.py:310

commit v21 on v20

--- a/solution.py
+++ b/solution.py
@@ -214,8 +214,8 @@
     token[...] = jnp.zeros_like(token)
     tokens, _ = cot_o.shape
     copies = chunk_copies(cot_o, cot_s, cot_v, sems)
-    left_v[:, :tokens] = mixed_o[...].T
-    left_v[:, tokens:] = mixed_s[...].T
+    left_v[:, :tokens] = mixed_o[...].astype(F32).T.astype(BF16)
+    left_v[:, tokens:] = mixed_s[...].astype(F32).T.astype(BF16)
     gradient_rows(left_v[...], cot_v, copies, grad_v)
     hand_out(idx, 1, grad_v, outs)
 
@@ -452,7 +452,6 @@
             + [pltpu.SemaphoreType.DMA((1,))],
             flops,
             2 * (2 * cot.size + mix.size + 2 * width * cols + 2 * tokens * cols),
-            vmem=60,
             out_specs=[VMEM, ANY],
         )(idx, token, cot, cot_s, mix, mix_s, *out_slots)
         if line4:

time: 118 us -> 116 us (0.983)
  Pallas kernels: 33.3 us -> 29.2 us
  waiting for transfers between devices: 46.9 us -> 48.4 us
    pallas_call x1, Pallas kernels: 8.57 us -> 5.32 us  [body(): call(functools.partial(d_value_kernel, n_slots), 'd_value', [SMEM] + [ANY...]
    ppermute x12, waiting for transfers between devices: 45.5 us -> 47 us  [move(): lax.ppermute(x, 'wide', [(2 * s + c, 2 * d + c) for s, d in pairs for c i...]
    unnamed x36 -> x32, local copies, waits for them, and re-layouts: 5.71 us -> 6.2 us
  transfers between devices with their start and end apart: 24 -> 24, of which waited for: 11 -> 11; matrix products, arithmetic and copies ran while one was open for 3% -> 3% of each run, Pallas kernels for 28% -> 25%
where the time goes in v21:
time: 116 us
  waiting for transfers between devices  48.4 us (42%)
  Pallas kernels  29.2 us (25%)
  starting transfers between devices  24.1 us (21%)
  local copies, waits for them, and re-layouts  7.72 us (7%)
  other arithmetic  5.14 us (4%)
    ppermute x12, waiting for transfers between devices, move(): lax.ppermute(x, 'wide', [(2 * s + c, 2 * d + c) for s, d in pairs for c i...  47 us
    ppermute x12, starting transfers between devices, move(): lax.ppermute(x, 'wide', [(2 * s + c, 2 * d + c) for s, d in pairs for c i...  18.2 us
    unnamed x32, local copies, waits for them, and re-layouts  6.2 us
    pallas_call x1, Pallas kernels, body(): call(functools.partial(terms_kernel, n_node), 'terms', [SMEM] + [ANY] * 4...  5.76 us
    pallas_call x1, Pallas kernels, body(): call(functools.partial(d_value_kernel, n_slots), 'd_value', [SMEM] + [ANY...  5.32 us
    pallas_call x1, Pallas kernels, body(): call(functools.partial(part_kernel, n_slots - 1), 'value_ahead', [SMEM] +...  4.9 us
    pallas_call x1, Pallas kernels, body(): call(functools.partial(grad_out_kernel, len(unread)), 'grad_out', [SMEM]...  4.4 us
    pallas_call x1, Pallas kernels, body(): call(gradient_kernel, 'grad_value', [SMEM] + [ANY] * 4 + [VMEM], send_sha...  4.39 us
  transfers between devices with their start and end apart: 24, of which 11 were waited for; matrix products, arithmetic and copies ran while one was open for 3% of the time, Pallas kernels for 25%

profile of v21, /device:TPU:0, one launch (start us, length us, event | category | flops | bytes accessed | tf_op | source)
XLA Modules:
  0.0 115.6 jit_solution(12378196256882411256)
XLA Ops:
  0.7 1.3 %slice_bitcast_fusion.5 = (bf16[1,320,256]{2,1,0:T(8,128)(2,1)S(1)}, bf16[1,320,256]{2,1,0:T(8,128)(2,1)S(1)}, bf16[1,320,256]{2,1,0:T(8,128)(2,1)S(1)}, bf16[1,320,256]{2,1,0:T(8,128)(2,1)S(1)}) fusion(bf16[320,512]{1,0:T(8,128)(2,1)} %param.8, bf16[320,512]{1,0:T(8,128)(2,1)} %param.9), kind=kLoop, calls=%fused_computation.34 | loop fusion | bytes 1310720 | tf_op jit(solution)/shard_map/stack | solution.py:318
  2.0 0.1 broadcast_select_fusion
  2.1 0.5 collective-permute-start
  2.6 1.3 %collective-permute-done = bf16[2,320,256]{2,1,0:T(8,128)(2,1)S(1)} collective-permute-done((bf16[2,320,256]{2,1,0:T(8,128)(2,1)S(1)}, bf16[2,320,256]{2,1,0:T(8,128)(2,1)S(1)}, u32[]{:S(2)}, u32[]{:S(2)}) %collective-permute-start) | collective-permute-done | bytes 327712 | tf_op jit(solution)/shard_map/ppermute | solution.py:310
  3.8 0.4 collective-permute-start.1
  4.2 0.1 collective-permute-start.7
  4.4 0.4 collective-permute-start.2
  4.8 2.8 %collective-permute-start.3 = (bf16[2,320,256]{2,1,0:T(8,128)(2,1)S(1)}, bf16[2,320,256]{2,1,0:T(8,128)(2,1)S(1)}, u32[]{:S(2)}, u32[]{:S(2)}) collective-permute-start(bf16[2,320,256]{2,1,0:T(8,128)(2,1)S(1)} %pad_maximum_fusion.5.rest_0_), channel_id=1, source_target_pairs={{0,8},{4,12},{8,0},{12,4},{16,24},{20,28},{24,16},{28,20},{1,9},{5... | collective-permute-start | bytes 983048 | tf_op jit(solution)/shard_map/ppermute | solution.py:302
  7.6 2.6 %collective-permute-start.4 = (bf16[2,320,256]{2,1,0:T(8,128)(2,1)S(1)}, bf16[2,320,256]{2,1,0:T(8,128)(2,1)S(1)}, u32[]{:S(2)}, u32[]{:S(2)}) collective-permute-start(bf16[2,320,256]{2,1,0:T(8,128)(2,1)S(1)} %pad_maximum_fusion.5.rest_0_), channel_id=1, source_target_pairs={{0,16},{4,20},{8,24},{12,28},{16,0},{20,4},{24,8},{28,12},{1,17},{... | collective-permute-start | bytes 983048 | tf_op jit(solution)/shard_map/ppermute | solution.py:302
  10.2 12.5 %collective-permute-done.3.unread.rest_1_ = bf16[2,320,256]{2,1,0:T(8,128)(2,1)S(1)} collective-permute-done((bf16[2,320,256]{2,1,0:T(8,128)(2,1)S(1)}, bf16[2,320,256]{2,1,0:T(8,128)(2,1)S(1)}, u32[]{:S(2)}, u32[]{:S(2)}) %collective-permute-start.3) | collective-permute-done | bytes 327712 | tf_op jit(solution)/shard_map/ppermute | solution.py:302
  22.8 2.5 %collective-permute-done.4.first = bf16[2,320,256]{2,1,0:T(8,128)(2,1)S(1)} collective-permute-done((bf16[2,320,256]{2,1,0:T(8,128)(2,1)S(1)}, bf16[2,320,256]{2,1,0:T(8,128)(2,1)S(1)}, u32[]{:S(2)}, u32[]{:S(2)}) %collective-permute-start.4) | collective-permute-done | bytes 327712 | tf_op jit(solution)/shard_map/ppermute | solution.py:302
  25.3 0.8 relay.1
  26.1 0.7 copy-done.7
  26.8 0.4 collective-permute-start.5
  27.2 0.1 stack.67.idx
  27.3 1.6 %collective-permute-start.8 = (bf16[2,320,256]{2,1,0:T(8,128)(2,1)}, bf16[2,320,256]{2,1,0:T(8,128)(2,1)S(1)}, u32[]{:S(2)}, u32[]{:S(2)}) collective-permute-start(bf16[2,320,256]{2,1,0:T(8,128)(2,1)} %copy-done.7), channel_id=1, source_target_pairs={{0,8},{4,12},{8,0},{12,4},{16,24},{20,28},{24,16},{28,20},{1,9},{5... | collective-permute-start | bytes 983048 | tf_op jit(solution)/shard_map/ppermute | solution.py:302
  28.9 1.1 collective-permute-start.9
  30.0 1.7 %copy-done.1 = bf16[2,2,128,2560]{3,2,1,0:T(8,128)(2,1)S(1)} copy-done((bf16[2,2,128,2560]{3,2,1,0:T(8,128)(2,1)S(1)}, bf16[2,2,128,2560]{3,2,1,0:T(8,128)(2,1)}, u32[]{:S(2)}) %copy-start.1) | copy-done | bytes 2621464
  31.7 1.2 %copy-done.3 = bf16[2,2,8,128,128]{4,3,2,1,0:T(8,128)(2,1)S(1)} copy-done((bf16[2,2,8,128,128]{4,3,2,1,0:T(8,128)(2,1)S(1)}, bf16[2,2,8,128,128]{4,3,2,1,0:T(8,128)(2,1)}, u32[]{:S(2)}) %copy-start.3) | copy-done | bytes 1048600
  32.9 4.9 %value_ahead.1 = (f32[2,512,256]{2,1,0:T(8,128)S(1)}, bf16[2,512,640]{2,1,0:T(8,128)(2,1)S(1)}, bf16[2,4,4,128,128]{4,3,2,1,0:T(8,128)(2,1)S(1)}) custom-call(s32[5]{0:T(128)S(1)} %stack.67.idx, bf16[512,2560]{1,0:T(8,128)(2,1)S(1)} %bitcast.54, bf16[512,2560]{1,0:T(8,128)(2,1)} %collective-permute-done.1.x_s.right_s, bf16[4,8,128,128]{3,2,1,0:T(8,128)(2,1)S(1)} %bitcast.57, ...), custom_call_target="tpu_custom_call" | custom-call | flops 1342177280 | bytes 11272192 | tf_op jit(solution)/shard_map/value_ahead/pallas_call | solution.py:401
  37.9 6.8 %collective-permute-done.5.slot = bf16[2,320,256]{2,1,0:T(8,128)(2,1)} collective-permute-done((bf16[2,320,256]{2,1,0:T(8,128)(2,1)}, bf16[2,320,256]{2,1,0:T(8,128)(2,1)}, u32[]{:S(2)}, u32[]{:S(2)}) %collective-permute-start.5) | collective-permute-done | bytes 327712 | tf_op jit(solution)/shard_map/ppermute | solution.py:302
  44.6 2.5 %mixed.1 = (bf16[512,256]{1,0:T(8,128)(2,1)S(1)}, bf16[512,256]{1,0:T(8,128)(2,1)S(1)}) custom-call(s32[5]{0:T(128)S(1)} %stack.67.idx, f32[2,512,256]{2,1,0:T(8,128)S(1)} %get-tuple-element.36.part, bf16[2,512,640]{2,1,0:T(8,128)(2,1)S(1)} %get-tuple-element.37.last, bf16[2,4,4,128,128]{4,3,2,1,0:T(8,128)(2,1)S(1)} %get-tuple-element.38.weights, ...), custom_call_target="tpu_custom_call" | custom-call | flops 335544320 | bytes 3932160 | tf_op jit(solution)/shard_map/mixed/pallas_call | solution.py:414
  47.1 0.1 collective-permute-start.6
  47.2 1.0 collective-permute-done.9.rest_2_
  48.2 3.0 %collective-permute-start.10 = (bf16[2,320,256]{2,1,0:T(8,128)(2,1)S(1)}, bf16[2,320,256]{2,1,0:T(8,128)(2,1)S(1)}, u32[]{:S(2)}, u32[]{:S(2)}) collective-permute-start(bf16[2,320,256]{2,1,0:T(8,128)(2,1)S(1)} %collective-permute-done.9.rest_2_), channel_id=1, source_target_pairs={{0,8},{4,12},{8,0},{12,4},{16,24},{20,28},{24,16},{28,20},{1,9},{5... | collective-permute-start | bytes 983048 | tf_op jit(solution)/shard_map/ppermute | solution.py:302
  51.2 0.0 copy-start.4
  51.2 4.4 %grad_out.1 = (bf16[16,128]{1,0:T(8,128)(2,1)S(1)}, bf16[2,320,256]{2,1,0:T(8,128)(2,1)S(1)}, bf16[2,320,256]{2,1,0:T(8,128)(2,1)S(1)}, bf16[2,320,256]{2,1,0:T(8,128)(2,1)S(1)}, bf16[2,320,256]{2,1,0:T(8,128)(2,1)S(1)}) custom-call(s32[5]{0:T(128)S(1)} %stack.67.idx, bf16[512,2560]{1,0:T(8,128)(2,1)S(1)} %bitcast.51, ...), custom_call_target="tpu_custom_call" | custom-call | flops 1342177280 | bytes 7077888 | tf_op jit(solution)/shard_map/grad_out/pallas_call | solution.py:436
  55.7 0.0 copy-start.9
  55.7 0.7 copy-done.9
  56.4 0.0 collective-permute-start.11
  56.4 2.3 %collective-permute-done.10.rest_3_ = bf16[2,320,256]{2,1,0:T(8,128)(2,1)S(1)} collective-permute-done((bf16[2,320,256]{2,1,0:T(8,128)(2,1)S(1)}, bf16[2,320,256]{2,1,0:T(8,128)(2,1)S(1)}, u32[]{:S(2)}, u32[]{:S(2)}) %collective-permute-start.10) | collective-permute-done | bytes 327712 | tf_op jit(solution)/shard_map/ppermute | solution.py:302
  58.7 5.3 %d_value.1 = (bf16[256,1024]{1,0:T(8,128)(2,1)S(1)}, bf16[2560,256]{1,0:T(8,128)(2,1)S(1)}) custom-call(s32[5]{0:T(128)S(1)} %stack.67.idx, bf16[16,128]{1,0:T(8,128)(2,1)S(1)} %get-tuple-element.43.token, bf16[512,2560]{1,0:T(8,128)(2,1)S(1)} %bitcast.52, bf16[512,2560]{1,0:T(8,128)(2,1)} %collective-permute-done.7.cot_s, ...), custom_call_target="tpu_custom_call" | custom-call | flops 1342177280 | bytes 9437184 | tf_op jit(solution)/shard_map/d_value/pallas_call | solution.py:446
  64.0 1.1 copy-done.6
  65.1 0.8 add_convert_fusion.refs_1_.unread
  65.9 0.6 pad_add_fusion.idx
  66.5 2.5 %collective-permute-start.18 = (bf16[2,320,256]{2,1,0:T(8,128)(2,1)}, bf16[2,320,256]{2,1,0:T(8,128)(2,1)S(1)}, u32[]{:S(2)}, u32[]{:S(2)}) collective-permute-start(bf16[2,320,256]{2,1,0:T(8,128)(2,1)} %copy-done.14), channel_id=1, source_target_pairs={{0,8},{4,12},{8,0},{12,4},{16,24},{20,28},{24,16},{28,20},{1,9},{5... | collective-permute-start | bytes 983048 | tf_op jit(solution)/shard_map/ppermute | solution.py:302
  69.0 0.2 collective-permute-start.19
  69.1 0.1 collective-permute-done.12.w_r
  69.3 5.8 %terms.1 = (bf16[16,128]{1,0:T(8,128)(2,1)}, bf16[2,256,640]{2,1,0:T(8,128)(2,1)}, bf16[2,256,640]{2,1,0:T(8,128)(2,1)}, bf16[4,256,640]{2,1,0:T(8,128)(2,1)}) custom-call(s32[4]{0:T(128)} %pad_add_fusion.idx, bf16[512,256]{1,0:T(8,128)(2,1)} %copy-done.11, bf16[512,256]{1,0:T(8,128)(2,1)} %copy-done.12, bf16[2560,256]{1,0:T(8,128)(2,1)} %in_order.1.w_o, ...), custom_call_target="tpu_custom_call" | custom-call | flops 1342177280 | bytes 5767168 | tf_op jit(solution)/shard_map/terms/pallas_call | solution.py:471
  75.0 1.6 %collective-permute-start.13 = (bf16[2,256,640]{2,1,0:T(8,128)(2,1)}, bf16[2,256,640]{2,1,0:T(8,128)(2,1)S(1)}, u32[]{:S(2)}, u32[]{:S(2)}) collective-permute-start(bf16[2,256,640]{2,1,0:T(8,128)(2,1)} %get-tuple-element.48), channel_id=1, source_target_pairs={{0,1},{1,0},{2,3},{3,2},{4,5},{5,4},{6,7},{7,6},{8,9},{9,8},{10,11... | collective-permute-start | bytes 1966088 | tf_op jit(solution)/shard_map/ppermute | solution.py:313
  76.6 1.5 %collective-permute-start.15 = (bf16[2,256,640]{2,1,0:T(8,128)(2,1)}, bf16[2,256,640]{2,1,0:T(8,128)(2,1)S(1)}, u32[]{:S(2)}, u32[]{:S(2)}) collective-permute-start(bf16[2,256,640]{2,1,0:T(8,128)(2,1)} %get-tuple-element.49), channel_id=1, source_target_pairs={{0,2},{1,3},{2,0},{3,1},{4,6},{5,7},{6,4},{7,5},{8,10},{9,11},{10,... | collective-permute-start | bytes 1966088 | tf_op jit(solution)/shard_map/ppermute | solution.py:313
  78.1 0.7 copy-done.13
  78.8 4.4 %grad_value.1 = (bf16[2,320,256]{2,1,0:T(8,128)(2,1)S(1)}, bf16[2,320,256]{2,1,0:T(8,128)(2,1)S(1)}, bf16[2,320,256]{2,1,0:T(8,128)(2,1)S(1)}, bf16[2,320,256]{2,1,0:T(8,128)(2,1)S(1)}) custom-call(s32[5]{0:T(128)S(1)} %stack.67.idx, bf16[16,128]{1,0:T(8,128)(2,1)S(1)} %copy-done.13, bf16[2,320,256]{2,1,0:T(8,128)(2,1)S(1)} %copy-done.5, ...), custom_call_target="tpu_custom_call" | custom-call | flops 1342177280 | bytes 7077888 | tf_op jit(solution)/shard_map/grad_value/pallas_call | solution.py:482
  83.2 2.6 %collective-permute-start.17 = (bf16[2,320,256]{2,1,0:T(8,128)(2,1)S(1)}, bf16[2,320,256]{2,1,0:T(8,128)(2,1)S(1)}, u32[]{:S(2)}, u32[]{:S(2)}) collective-permute-start(bf16[2,320,256]{2,1,0:T(8,128)(2,1)S(1)} %get-tuple-element.54), channel_id=1, source_target_pairs={{0,8},{4,12},{8,0},{12,4},{16,24},{20,28},{24,16},{28,20},{1,9},{5... | collective-permute-start | bytes 983048 | tf_op jit(solution)/shard_map/ppermute | solution.py:302
  85.8 0.2 convert_element_type.53
  85.9 1.0 collective-permute-done.19.far
  86.9 6.9 %collective-permute-done.17.got = bf16[2,320,256]{2,1,0:T(8,128)(2,1)S(1)} collective-permute-done((bf16[2,320,256]{2,1,0:T(8,128)(2,1)S(1)}, bf16[2,320,256]{2,1,0:T(8,128)(2,1)S(1)}, u32[]{:S(2)}, u32[]{:S(2)}) %collective-permute-start.17) | collective-permute-done | bytes 327712 | tf_op jit(solution)/shard_map/ppermute | solution.py:302
  93.8 1.2 %sum.1 = (bf16[2,320,256]{2,1,0:T(8,128)(2,1)S(1)}, bf16[2,320,256]{2,1,0:T(8,128)(2,1)S(1)}, f32[2,320,256]{2,1,0:T(8,128)S(1)}) custom-call(bf16[2,320,256]{2,1,0:T(8,128)(2,1)S(1)} %get-tuple-element.53.block, bf16[2,320,256]{2,1,0:T(8,128)(2,1)S(1)} %collective-permute-done.17.got, bf16[2,320,256]{2,1,0:T(8,128)(2,1)S(1)} %get-tuple-element.55.beside, ...), custom_call_target="tpu_custom_call" | custom-call | bytes 1048576 | tf_op jit(solution)/shard_map/sum/pallas_call | solution.py:493
  95.0 1.2 %collective-permute-start.20 = (bf16[2,320,256]{2,1,0:T(8,128)(2,1)S(1)}, bf16[2,320,256]{2,1,0:T(8,128)(2,1)S(1)}, u32[]{:S(2)}, u32[]{:S(2)}) collective-permute-start(bf16[2,320,256]{2,1,0:T(8,128)(2,1)S(1)} %get-tuple-element.58), channel_id=1, source_target_pairs={{0,8},{4,12},{8,0},{12,4},{16,24},{20,28},{24,16},{28,20},{1,9},{5... | collective-permute-start | bytes 983048 | tf_op jit(solution)/shard_map/ppermute | solution.py:302
  96.2 0.3 collective-permute-start.21
  96.5 0.1 collective-permute-start.23
  96.6 0.1 convert_element_type.54
  96.7 0.1 convert_element_type.58
  96.8 0.1 fusion.8
  97.0 0.6 collective-permute-start.14
  97.5 0.6 collective-permute-start.16
  98.2 11.6 %collective-permute-done.20 = bf16[2,320,256]{2,1,0:T(8,128)(2,1)S(1)} collective-permute-done((bf16[2,320,256]{2,1,0:T(8,128)(2,1)S(1)}, bf16[2,320,256]{2,1,0:T(8,128)(2,1)S(1)}, u32[]{:S(2)}, u32[]{:S(2)}) %collective-permute-start.20) | collective-permute-done | bytes 327712 | tf_op jit(solution)/shard_map/ppermute | solution.py:302
  109.8 2.5 %collective-permute-done.21 = bf16[2,320,256]{2,1,0:T(8,128)(2,1)S(1)} collective-permute-done((bf16[2,320,256]{2,1,0:T(8,128)(2,1)S(1)}, bf16[2,320,256]{2,1,0:T(8,128)(2,1)S(1)}, u32[]{:S(2)}, u32[]{:S(2)}) %collective-permute-start.21) | collective-permute-done | bytes 327712 | tf_op jit(solution)/shard_map/ppermute | solution.py:302
  112.3 0.1 convert_add_fusion
  112.4 0.1 collective-permute-start.22
  112.6 0.9 pad_maximum_fusion.2
  113.5 0.2 fusion.7
  113.7 0.9 pad_maximum_fusion
  114.6 0.9 pad_maximum_fusion.1
  (47 shorter events, 0.3 us)
Async XLA Ops:
  0.6 3.6 %copy-start = (bf16[2,2,128,2560]{3,2,1,0:T(8,128)(2,1)S(1)}, bf16[2,2,128,2560]{3,2,1,0:T(8,128)(2,1)}, u32[]{:S(2)}) copy-start(bf16[2,2,128,2560]{3,2,1,0:T(8,128)(2,1)} %param.7) | copy-start | bytes 7864324
  2.1 1.8 %collective-permute-start = (bf16[2,320,256]{2,1,0:T(8,128)(2,1)S(1)}, bf16[2,320,256]{2,1,0:T(8,128)(2,1)S(1)}, u32[]{:S(2)}, u32[]{:S(2)}) collective-permute-start(bf16[2,320,256]{2,1,0:T(8,128)(2,1)S(1)} %get-tuple-element.70), channel_id=1, source_target_pairs={{0,4},{4,0},{8,12},{12,8},{16,20},{20,16},{24,28},{28,24},{1,5},{5... | collective-permute-start | bytes 983048 | tf_op jit(solution)/shard_map/ppermute | solution.py:310
  3.8 26.1 %collective-permute-start.1 = (bf16[512,2560]{1,0:T(8,128)(2,1)}, bf16[512,2560]{1,0:T(8,128)(2,1)}, u32[]{:S(2)}, u32[]{:S(2)}) collective-permute-start(bf16[512,2560]{1,0:T(8,128)(2,1)} %bitcast.53), channel_id=1, source_target_pairs={{0,4},{4,0},{8,12},{12,8},{16,20},{20,16},{24,28},{28,24},{1,5},{5... | collective-permute-start | bytes 7864328 | tf_op jit(solution)/shard_map/ppermute | solution.py:310
  4.2 47.0 %collective-permute-start.7 = (bf16[512,2560]{1,0:T(8,128)(2,1)S(1)}, bf16[512,2560]{1,0:T(8,128)(2,1)}, u32[]{:S(2)}, u32[]{:S(2)}) collective-permute-start(bf16[512,2560]{1,0:T(8,128)(2,1)S(1)} %bitcast.50), channel_id=1, source_target_pairs={{0,4},{4,0},{8,12},{12,8},{16,20},{20,16},{24,28},{28,24},{1,5},{5... | collective-permute-start | bytes 7864328 | tf_op jit(solution)/shard_map/ppermute | solution.py:310
  4.4 24.5 %collective-permute-start.2 = (bf16[4,8,128,128]{3,2,1,0:T(8,128)(2,1)}, bf16[4,8,128,128]{3,2,1,0:T(8,128)(2,1)}, u32[]{:S(2)}, u32[]{:S(2)}) collective-permute-start(bf16[4,8,128,128]{3,2,1,0:T(8,128)(2,1)} %bitcast.56), channel_id=1, source_target_pairs={{0,4},{4,0},{8,12},{12,8},{16,20},{20,16},{24,28},{28,24},{1,5},{5... | collective-permute-start | bytes 3145736 | tf_op jit(solution)/shard_map/ppermute | solution.py:310
  4.8 17.9 %collective-permute-start.3 = (bf16[2,320,256]{2,1,0:T(8,128)(2,1)S(1)}, bf16[2,320,256]{2,1,0:T(8,128)(2,1)S(1)}, u32[]{:S(2)}, u32[]{:S(2)}) collective-permute-start(bf16[2,320,256]{2,1,0:T(8,128)(2,1)S(1)} %pad_maximum_fusion.5.rest_0_), channel_id=1, source_target_pairs={{0,8},{4,12},{8,0},{12,4},{16,24},{20,28},{24,16},{28,20},{1,9},{5... | collective-permute-start | bytes 983048 | tf_op jit(solution)/shard_map/ppermute | solution.py:302
  7.6 17.7 %collective-permute-start.4 = (bf16[2,320,256]{2,1,0:T(8,128)(2,1)S(1)}, bf16[2,320,256]{2,1,0:T(8,128)(2,1)S(1)}, u32[]{:S(2)}, u32[]{:S(2)}) collective-permute-start(bf16[2,320,256]{2,1,0:T(8,128)(2,1)S(1)} %pad_maximum_fusion.5.rest_0_), channel_id=1, source_target_pairs={{0,16},{4,20},{8,24},{12,28},{16,0},{20,4},{24,8},{28,12},{1,17},{... | collective-permute-start | bytes 983048 | tf_op jit(solution)/shard_map/ppermute | solution.py:302
  26.1 0.7 copy-start.7
  26.8 17.9 %collective-permute-start.5 = (bf16[2,320,256]{2,1,0:T(8,128)(2,1)}, bf16[2,320,256]{2,1,0:T(8,128)(2,1)}, u32[]{:S(2)}, u32[]{:S(2)}) collective-permute-start(bf16[2,320,256]{2,1,0:T(8,128)(2,1)} %get-tuple-element.35.rest_2_), channel_id=1, source_target_pairs={{0,8},{4,12},{8,0},{12,4},{16,24},{20,28},{24,16},{28,20},{1,9},{5... | collective-permute-start | bytes 983048 | tf_op jit(solution)/shard_map/ppermute | solution.py:302
  27.3 23.9 %collective-permute-start.8 = (bf16[2,320,256]{2,1,0:T(8,128)(2,1)}, bf16[2,320,256]{2,1,0:T(8,128)(2,1)S(1)}, u32[]{:S(2)}, u32[]{:S(2)}) collective-permute-start(bf16[2,320,256]{2,1,0:T(8,128)(2,1)} %copy-done.7), channel_id=1, source_target_pairs={{0,8},{4,12},{8,0},{12,4},{16,24},{20,28},{24,16},{28,20},{1,9},{5... | collective-permute-start | bytes 983048 | tf_op jit(solution)/shard_map/ppermute | solution.py:302
  28.9 19.3 %collective-permute-start.9 = (bf16[2,320,256]{2,1,0:T(8,128)(2,1)}, bf16[2,320,256]{2,1,0:T(8,128)(2,1)S(1)}, u32[]{:S(2)}, u32[]{:S(2)}) collective-permute-start(bf16[2,320,256]{2,1,0:T(8,128)(2,1)} %copy-done.7), channel_id=1, source_target_pairs={{0,16},{4,20},{8,24},{12,28},{16,0},{20,4},{24,8},{28,12},{1,17},{... | collective-permute-start | bytes 983048 | tf_op jit(solution)/shard_map/ppermute | solution.py:302
  30.0 1.7 %copy-start.1 = (bf16[2,2,128,2560]{3,2,1,0:T(8,128)(2,1)S(1)}, bf16[2,2,128,2560]{3,2,1,0:T(8,128)(2,1)}, u32[]{:S(2)}) copy-start(bf16[2,2,128,2560]{3,2,1,0:T(8,128)(2,1)} %param.5) | copy-start | bytes 7864324
  31.7 1.2 %copy-start.3 = (bf16[2,2,8,128,128]{4,3,2,1,0:T(8,128)(2,1)S(1)}, bf16[2,2,8,128,128]{4,3,2,1,0:T(8,128)(2,1)}, u32[]{:S(2)}) copy-start(bf16[2,2,8,128,128]{4,3,2,1,0:T(8,128)(2,1)} %param.6) | copy-start | bytes 3145732
  47.1 8.5 %copy-start.11 = (bf16[512,256]{1,0:T(8,128)(2,1)}, bf16[512,256]{1,0:T(8,128)(2,1)S(1)}, u32[]{:S(2)}) copy-start(bf16[512,256]{1,0:T(8,128)(2,1)S(1)} %get-tuple-element.39.mixed_o) | copy-start | bytes 786436
  47.1 4.0 %collective-permute-start.6 = (bf16[512,256]{1,0:T(8,128)(2,1)S(1)}, bf16[512,256]{1,0:T(8,128)(2,1)S(1)}, u32[]{:S(2)}, u32[]{:S(2)}) collective-permute-start(bf16[512,256]{1,0:T(8,128)(2,1)S(1)} %get-tuple-element.40.mixed_s), channel_id=1, source_target_pairs={{0,4},{4,0},{8,12},{12,8},{16,20},{20,16},{24,28},{28,24},{1,5},{5... | collective-permute-start | bytes 786440 | tf_op jit(solution)/shard_map/ppermute | solution.py:310
  48.2 10.4 %collective-permute-start.10 = (bf16[2,320,256]{2,1,0:T(8,128)(2,1)S(1)}, bf16[2,320,256]{2,1,0:T(8,128)(2,1)S(1)}, u32[]{:S(2)}, u32[]{:S(2)}) collective-permute-start(bf16[2,320,256]{2,1,0:T(8,128)(2,1)S(1)} %collective-permute-done.9.rest_2_), channel_id=1, source_target_pairs={{0,8},{4,12},{8,0},{12,4},{16,24},{20,28},{24,16},{28,20},{1,9},{5... | collective-permute-start | bytes 983048 | tf_op jit(solution)/shard_map/ppermute | solution.py:302
  51.2 4.5 %copy-start.12 = (bf16[512,256]{1,0:T(8,128)(2,1)}, bf16[512,256]{1,0:T(8,128)(2,1)S(1)}, u32[]{:S(2)}) copy-start(bf16[512,256]{1,0:T(8,128)(2,1)S(1)} %collective-permute-done.6.rest_0_.mixed_r) | copy-start | bytes 786436
  51.2 7.5 %copy-start.4 = (bf16[2,2,8,128,128]{4,3,2,1,0:T(8,128)(2,1)S(1)}, bf16[2,2,8,128,128]{4,3,2,1,0:T(8,128)(2,1)}, u32[]{:S(2)}) copy-start(bf16[2,2,8,128,128]{4,3,2,1,0:T(8,128)(2,1)} %param.6) | copy-start | bytes 3145732
  51.2 7.4 %copy-start.8 = (bf16[2,320,256]{2,1,0:T(8,128)(2,1)S(1)}, bf16[2,320,256]{2,1,0:T(8,128)(2,1)}, u32[]{:S(2)}) copy-start(bf16[2,320,256]{2,1,0:T(8,128)(2,1)} %copy-done.7) | copy-start | bytes 983044
  55.7 0.7 copy-start.9
  56.4 2.3 %copy-start.14 = (bf16[2,320,256]{2,1,0:T(8,128)(2,1)}, bf16[2,320,256]{2,1,0:T(8,128)(2,1)S(1)}, u32[]{:S(2)}) copy-start(bf16[2,320,256]{2,1,0:T(8,128)(2,1)S(1)} %get-tuple-element.57) | copy-start | bytes 983044
  56.4 8.7 %collective-permute-start.11 = (bf16[2,320,256]{2,1,0:T(8,128)(2,1)S(1)}, bf16[2,320,256]{2,1,0:T(8,128)(2,1)S(1)}, u32[]{:S(2)}, u32[]{:S(2)}) collective-permute-start(bf16[2,320,256]{2,1,0:T(8,128)(2,1)S(1)} %get-tuple-element.46), channel_id=1, source_target_pairs={{0,8},{4,12},{8,0},{12,4},{16,24},{20,28},{24,16},{28,20},{1,9},{5... | collective-permute-start | bytes 983048 | tf_op jit(solution)/shard_map/ppermute | solution.py:302
  64.0 1.1 copy-start.6
  65.9 3.1 %copy-start.5 = (bf16[2,320,256]{2,1,0:T(8,128)(2,1)S(1)}, bf16[2,320,256]{2,1,0:T(8,128)(2,1)}, u32[]{:S(2)}) copy-start(bf16[2,320,256]{2,1,0:T(8,128)(2,1)} %add_convert_fusion.refs_1_.unread) | copy-start | bytes 983044
  65.9 3.4 %collective-permute-start.12 = (bf16[2560,256]{1,0:T(8,128)(2,1)}, bf16[2560,256]{1,0:T(8,128)(2,1)}, u32[]{:S(2)}, u32[]{:S(2)}) collective-permute-start(bf16[2560,256]{1,0:T(8,128)(2,1)} %in_order.1.w_o), channel_id=1, source_target_pairs={{0,4},{4,0},{8,12},{12,8},{16,20},{20,16},{24,28},{28,24},{1,5},{5... | collective-permute-start | bytes 3932168 | tf_op jit(solution)/shard_map/ppermute | solution.py:310
  66.5 11.7 %copy-start.2 = (bf16[2,2,128,2560]{3,2,1,0:T(8,128)(2,1)S(1)}, bf16[2,2,128,2560]{3,2,1,0:T(8,128)(2,1)}, u32[]{:S(2)}) copy-start(bf16[2,2,128,2560]{3,2,1,0:T(8,128)(2,1)} %param.5) | copy-start | bytes 7864324
  66.5 19.5 %collective-permute-start.18 = (bf16[2,320,256]{2,1,0:T(8,128)(2,1)}, bf16[2,320,256]{2,1,0:T(8,128)(2,1)S(1)}, u32[]{:S(2)}, u32[]{:S(2)}) collective-permute-start(bf16[2,320,256]{2,1,0:T(8,128)(2,1)} %copy-done.14), channel_id=1, source_target_pairs={{0,8},{4,12},{8,0},{12,4},{16,24},{20,28},{24,16},{28,20},{1,9},{5... | collective-permute-start | bytes 983048 | tf_op jit(solution)/shard_map/ppermute | solution.py:302
  69.0 18.0 %collective-permute-start.19 = (bf16[2,320,256]{2,1,0:T(8,128)(2,1)S(1)}, bf16[2,320,256]{2,1,0:T(8,128)(2,1)}, u32[]{:S(2)}, u32[]{:S(2)}) collective-permute-start(bf16[2,320,256]{2,1,0:T(8,128)(2,1)S(1)} %copy-done.5), channel_id=1, source_target_pairs={{0,16},{4,20},{8,24},{12,28},{16,0},{20,4},{24,8},{28,12},{1,17},{... | collective-permute-start | bytes 983048 | tf_op jit(solution)/shard_map/ppermute | solution.py:302
  75.0 21.6 %collective-permute-start.13 = (bf16[2,256,640]{2,1,0:T(8,128)(2,1)}, bf16[2,256,640]{2,1,0:T(8,128)(2,1)S(1)}, u32[]{:S(2)}, u32[]{:S(2)}) collective-permute-start(bf16[2,256,640]{2,1,0:T(8,128)(2,1)} %get-tuple-element.48), channel_id=1, source_target_pairs={{0,1},{1,0},{2,3},{3,2},{4,5},{5,4},{6,7},{7,6},{8,9},{9,8},{10,11... | collective-permute-start | bytes 1966088 | tf_op jit(solution)/shard_map/ppermute | solution.py:313
  76.6 20.1 %collective-permute-start.15 = (bf16[2,256,640]{2,1,0:T(8,128)(2,1)}, bf16[2,256,640]{2,1,0:T(8,128)(2,1)S(1)}, u32[]{:S(2)}, u32[]{:S(2)}) collective-permute-start(bf16[2,256,640]{2,1,0:T(8,128)(2,1)} %get-tuple-element.49), channel_id=1, source_target_pairs={{0,2},{1,3},{2,0},{3,1},{4,6},{5,7},{6,4},{7,5},{8,10},{9,11},{10,... | collective-permute-start | bytes 1966088 | tf_op jit(solution)/shard_map/ppermute | solution.py:313
  78.1 0.7 copy-start.13
  78.8 7.0 %copy-start.15 = (bf16[4,256,640]{2,1,0:T(8,128)(2,1)S(1)}, bf16[4,256,640]{2,1,0:T(8,128)(2,1)}, u32[]{:S(2)}) copy-start(bf16[4,256,640]{2,1,0:T(8,128)(2,1)} %get-tuple-element.47) | copy-start | bytes 3932164
  83.2 10.6 %collective-permute-start.17 = (bf16[2,320,256]{2,1,0:T(8,128)(2,1)S(1)}, bf16[2,320,256]{2,1,0:T(8,128)(2,1)S(1)}, u32[]{:S(2)}, u32[]{:S(2)}) collective-permute-start(bf16[2,320,256]{2,1,0:T(8,128)(2,1)S(1)} %get-tuple-element.54), channel_id=1, source_target_pairs={{0,8},{4,12},{8,0},{12,4},{16,24},{20,28},{24,16},{28,20},{1,9},{5... | collective-permute-start | bytes 983048 | tf_op jit(solution)/shard_map/ppermute | solution.py:302
  85.8 8.0 %copy-start.10 = (bf16[2,320,256]{2,1,0:T(8,128)(2,1)S(1)}, bf16[2,320,256]{2,1,0:T(8,128)(2,1)}, u32[]{:S(2)}) copy-start(bf16[2,320,256]{2,1,0:T(8,128)(2,1)} %copy-done.9) | copy-start | bytes 983044
  95.0 14.8 %collective-permute-start.20 = (bf16[2,320,256]{2,1,0:T(8,128)(2,1)S(1)}, bf16[2,320,256]{2,1,0:T(8,128)(2,1)S(1)}, u32[]{:S(2)}, u32[]{:S(2)}) collective-permute-start(bf16[2,320,256]{2,1,0:T(8,128)(2,1)S(1)} %get-tuple-element.58), channel_id=1, source_target_pairs={{0,8},{4,12},{8,0},{12,4},{16,24},{20,28},{24,16},{28,20},{1,9},{5... | collective-permute-start | bytes 983048 | tf_op jit(solution)/shard_map/ppermute | solution.py:302
  96.2 16.1 %collective-permute-start.21 = (bf16[2,320,256]{2,1,0:T(8,128)(2,1)S(1)}, bf16[2,320,256]{2,1,0:T(8,128)(2,1)S(1)}, u32[]{:S(2)}, u32[]{:S(2)}) collective-permute-start(bf16[2,320,256]{2,1,0:T(8,128)(2,1)S(1)} %get-tuple-element.59), channel_id=1, source_target_pairs={{0,16},{4,20},{8,24},{12,28},{16,0},{20,4},{24,8},{28,12},{1,17},{... | collective-permute-start | bytes 983048 | tf_op jit(solution)/shard_map/ppermute | solution.py:302
  96.5 16.0 %collective-permute-start.23 = (f32[320,256]{1,0:T(8,128)S(1)}, f32[320,256]{1,0:T(8,128)S(1)}, u32[]{:S(2)}, u32[]{:S(2)}) collective-permute-start(f32[320,256]{1,0:T(8,128)S(1)} %slice_bitcast_fusion.2), channel_id=1, source_target_pairs={{0,4},{4,0},{8,12},{12,8},{16,20},{20,16},{24,28},{28,24},{1,5},{5... | collective-permute-start | bytes 983048 | tf_op jit(solution)/shard_map/ppermute | solution.py:310
  97.0 16.5 %collective-permute-start.14 = (bf16[256,640]{1,0:T(8,128)(2,1)S(1)}, bf16[256,640]{1,0:T(8,128)(2,1)S(1)}, u32[]{:S(2)}, u32[]{:S(2)}) collective-permute-start(bf16[256,640]{1,0:T(8,128)(2,1)S(1)} %get-tuple-element.63), channel_id=1, source_target_pairs={{0,2},{1,3},{2,0},{3,1},{4,6},{5,7},{6,4},{7,5},{8,10},{9,11},{10,... | collective-permute-start | bytes 983048 | tf_op jit(solution)/shard_map/ppermute | solution.py:313
  97.5 16.0 %collective-permute-start.16 = (bf16[256,640]{1,0:T(8,128)(2,1)S(1)}, bf16[256,640]{1,0:T(8,128)(2,1)S(1)}, u32[]{:S(2)}, u32[]{:S(2)}) collective-permute-start(bf16[256,640]{1,0:T(8,128)(2,1)S(1)} %get-tuple-element.64), channel_id=1, source_target_pairs={{0,1},{1,0},{2,3},{3,2},{4,5},{5,4},{6,7},{7,6},{8,9},{9,8},{10,11... | collective-permute-start | bytes 983048 | tf_op jit(solution)/shard_map/ppermute | solution.py:313
  112.4 2.1 %collective-permute-start.22 = (f32[320,256]{1,0:T(8,128)S(1)}, f32[320,256]{1,0:T(8,128)S(1)}, u32[]{:S(2)}, u32[]{:S(2)}) collective-permute-start(f32[320,256]{1,0:T(8,128)S(1)} %slice_bitcast_fusion), channel_id=1, source_target_pairs={{0,4},{4,0},{8,12},{12,8},{16,20},{20,16},{24,28},{28,24},{1,5},{5... | collective-permute-start | bytes 983048 | tf_op jit(solution)/shard_map/ppermute | solution.py:310

commit v22 on v19

--- a/solution.py
+++ b/solution.py
@@ -214,16 +214,17 @@
     token[...] = jnp.zeros_like(token)
     tokens, _ = cot_o.shape
     copies = chunk_copies(cot_o, cot_s, cot_v, sems)
-    left_v[:, :tokens] = mixed_o[...].T
-    left_v[:, tokens:] = mixed_s[...].T
+    left_v[:, :tokens] = mixed_o[...].astype(F32).T.astype(BF16)
+    left_v[:, tokens:] = mixed_s[...].astype(F32).T.astype(BF16)
     gradient_rows(left_v[...], cot_v, copies, grad_v)
     hand_out(idx, 1, grad_v, outs)
 
 
-def relay_kernel(unread, first, second, first_out, second_out):
+def relay_kernel(unread, first, second, first_out, second_out, again_out):
     del unread
     first_out[...] = first[...]
     second_out[...] = second[...]
+    again_out[...] = second[...]
 
 
 def sum_kernel(block, got, beside, own, near, far, onward, beside_out, total):
@@ -367,12 +368,12 @@
         block = u_out.shape
         if line4:
             far, near = swap(u_value, 2), swap(u_value, 1)
-            far, u_out = call(relay_kernel, "relay", [ANY, VMEM, VMEM], [block] * 2, [], 0, vmem=8)(
+            far, u_out, again = call(relay_kernel, "relay", [ANY, VMEM, VMEM], [block] * 3, [], 0, vmem=8)(
                 near, far, u_out
             )
             value_slots = [u_value, near, far, swap(far, 1)]
             far = swap(u_out, 2)
-            out_slots = [u_out, swap(u_out, 1), far, swap(far, 1)]
+            out_slots = [u_out, swap(in_order(again, mix_s), 1), far, swap(far, 1)]
         else:
             value_slots, out_slots = gather_ring(u_value), gather_ring(u_out)
         n_slots = len(out_slots)

time: 115 us -> 114 us (level)
  starting transfers between devices: 24.8 us -> 20.8 us
  local copies, waits for them, and re-layouts: 11 us -> 12.5 us
    ppermute x12, starting transfers between devices: 19 us -> 14.7 us  [move(): lax.ppermute(x, 'wide', [(2 * s + c, 2 * d + c) for s, d in pairs for c i...]
    unnamed x32 -> x34, local copies, waits for them, and re-layouts: 9.48 us -> 11 us
  transfers between devices with their start and end apart: 24 -> 24, of which waited for: 9 -> 11; matrix products, arithmetic and copies ran while one was open for 3% -> 3% of each run, Pallas kernels for 22% -> 23%
where the time goes in v22:
time: 114 us
  waiting for transfers between devices  48.4 us (42%)
  Pallas kernels  26.1 us (23%)
  starting transfers between devices  20.8 us (18%)
  local copies, waits for them, and re-layouts  12.5 us (11%)
  other arithmetic  4.78 us (4%)
    ppermute x12, waiting for transfers between devices, move(): lax.ppermute(x, 'wide', [(2 * s + c, 2 * d + c) for s, d in pairs for c i...  46.4 us
    ppermute x12, starting transfers between devices, move(): lax.ppermute(x, 'wide', [(2 * s + c, 2 * d + c) for s, d in pairs for c i...  14.7 us
    unnamed x34, local copies, waits for them, and re-layouts  11 us
    pallas_call x1, Pallas kernels, body(): call(functools.partial(d_value_kernel, n_slots), 'd_value', [SMEM] + [ANY...  5.87 us
    pallas_call x1, Pallas kernels, body(): call(functools.partial(grad_out_kernel, len(unread)), 'grad_out', [SMEM]...  5.12 us
    pallas_call x1, Pallas kernels, body(): call(functools.partial(part_kernel, n_slots - 1), 'value_ahead', [SMEM] +...  4.9 us
    ppermute x4, starting transfers between devices, flip(): return lax.ppermute(x, 'node', [(i, i ^ j) for i in range(n_node)])  4.41 us
    pallas_call x1, Pallas kernels, body(): call(gradient_kernel, 'grad_value', [SMEM] + [ANY] * 4 + [VMEM], send_sha...  4.39 us
  transfers between devices with their start and end apart: 24, of which 11 were waited for; matrix products, arithmetic and copies ran while one was open for 3% of the time, Pallas kernels for 23%

profile of v22, /device:TPU:0, one launch (start us, length us, event | category | flops | bytes accessed | tf_op | source)
XLA Modules:
  0.0 113.6 jit_solution(810669688448823741)
XLA Ops:
  0.7 1.3 %slice_bitcast_fusion.5 = (bf16[1,320,256]{2,1,0:T(8,128)(2,1)S(1)}, bf16[1,320,256]{2,1,0:T(8,128)(2,1)S(1)}, bf16[1,320,256]{2,1,0:T(8,128)(2,1)S(1)}, bf16[1,320,256]{2,1,0:T(8,128)(2,1)S(1)}) fusion(bf16[320,512]{1,0:T(8,128)(2,1)} %param.8, bf16[320,512]{1,0:T(8,128)(2,1)} %param.9), kind=kLoop, calls=%fused_computation.34 | loop fusion | bytes 1310720 | tf_op jit(solution)/shard_map/stack | solution.py:314
  2.1 0.5 collective-permute-start
  2.6 1.3 %collective-permute-done = bf16[2,320,256]{2,1,0:T(8,128)(2,1)S(1)} collective-permute-done((bf16[2,320,256]{2,1,0:T(8,128)(2,1)S(1)}, bf16[2,320,256]{2,1,0:T(8,128)(2,1)S(1)}, u32[]{:S(2)}, u32[]{:S(2)}) %collective-permute-start) | collective-permute-done | bytes 327712 | tf_op jit(solution)/shard_map/ppermute | solution.py:306
  3.8 0.4 collective-permute-start.1
  4.2 0.1 collective-permute-start.7
  4.4 0.4 collective-permute-start.2
  4.8 2.8 %collective-permute-start.3 = (bf16[2,320,256]{2,1,0:T(8,128)(2,1)S(1)}, bf16[2,320,256]{2,1,0:T(8,128)(2,1)S(1)}, u32[]{:S(2)}, u32[]{:S(2)}) collective-permute-start(bf16[2,320,256]{2,1,0:T(8,128)(2,1)S(1)} %pad_maximum_fusion.5.rest_0_), channel_id=1, source_target_pairs={{0,8},{4,12},{8,0},{12,4},{16,24},{20,28},{24,16},{28,20},{1,9},{5... | collective-permute-start | bytes 983048 | tf_op jit(solution)/shard_map/ppermute | solution.py:298
  7.6 2.6 %collective-permute-start.4 = (bf16[2,320,256]{2,1,0:T(8,128)(2,1)S(1)}, bf16[2,320,256]{2,1,0:T(8,128)(2,1)S(1)}, u32[]{:S(2)}, u32[]{:S(2)}) collective-permute-start(bf16[2,320,256]{2,1,0:T(8,128)(2,1)S(1)} %pad_maximum_fusion.5.rest_0_), channel_id=1, source_target_pairs={{0,16},{4,20},{8,24},{12,28},{16,0},{20,4},{24,8},{28,12},{1,17},{... | collective-permute-start | bytes 983048 | tf_op jit(solution)/shard_map/ppermute | solution.py:298
  10.2 12.5 %collective-permute-done.3.unread.rest_1_ = bf16[2,320,256]{2,1,0:T(8,128)(2,1)S(1)} collective-permute-done((bf16[2,320,256]{2,1,0:T(8,128)(2,1)S(1)}, bf16[2,320,256]{2,1,0:T(8,128)(2,1)S(1)}, u32[]{:S(2)}, u32[]{:S(2)}) %collective-permute-start.3) | collective-permute-done | bytes 327712 | tf_op jit(solution)/shard_map/ppermute | solution.py:298
  22.8 2.5 %collective-permute-done.4.first = bf16[2,320,256]{2,1,0:T(8,128)(2,1)S(1)} collective-permute-done((bf16[2,320,256]{2,1,0:T(8,128)(2,1)S(1)}, bf16[2,320,256]{2,1,0:T(8,128)(2,1)S(1)}, u32[]{:S(2)}, u32[]{:S(2)}) %collective-permute-start.4) | collective-permute-done | bytes 327712 | tf_op jit(solution)/shard_map/ppermute | solution.py:298
  25.3 0.8 relay.1
  26.1 0.7 copy-done.8
  26.8 0.7 copy-done.10
  27.5 0.4 collective-permute-start.5
  28.0 0.1 stack.67.idx
  28.1 2.6 %collective-permute-start.9 = (bf16[2,320,256]{2,1,0:T(8,128)(2,1)}, bf16[2,320,256]{2,1,0:T(8,128)(2,1)}, u32[]{:S(2)}, u32[]{:S(2)}) collective-permute-start(bf16[2,320,256]{2,1,0:T(8,128)(2,1)} %copy-done.8), channel_id=1, source_target_pairs={{0,16},{4,20},{8,24},{12,28},{16,0},{20,4},{24,8},{28,12},{1,17},{... | collective-permute-start | bytes 983048 | tf_op jit(solution)/shard_map/ppermute | solution.py:298
  30.7 1.7 %copy-done.1 = bf16[2,2,128,2560]{3,2,1,0:T(8,128)(2,1)S(1)} copy-done((bf16[2,2,128,2560]{3,2,1,0:T(8,128)(2,1)S(1)}, bf16[2,2,128,2560]{3,2,1,0:T(8,128)(2,1)}, u32[]{:S(2)}) %copy-start.1) | copy-done | bytes 2621464
  32.4 1.2 %copy-done.3 = bf16[2,2,8,128,128]{4,3,2,1,0:T(8,128)(2,1)S(1)} copy-done((bf16[2,2,8,128,128]{4,3,2,1,0:T(8,128)(2,1)S(1)}, bf16[2,2,8,128,128]{4,3,2,1,0:T(8,128)(2,1)}, u32[]{:S(2)}) %copy-start.3) | copy-done | bytes 1048600
  33.6 4.9 %value_ahead.1 = (f32[2,512,256]{2,1,0:T(8,128)S(1)}, bf16[2,512,640]{2,1,0:T(8,128)(2,1)S(1)}, bf16[2,4,4,128,128]{4,3,2,1,0:T(8,128)(2,1)S(1)}) custom-call(s32[5]{0:T(128)S(1)} %stack.67.idx, bf16[512,2560]{1,0:T(8,128)(2,1)S(1)} %bitcast.54, bf16[512,2560]{1,0:T(8,128)(2,1)} %collective-permute-done.1.x_s.right_s, bf16[4,8,128,128]{3,2,1,0:T(8,128)(2,1)S(1)} %bitcast.57, ...), custom_call_target="tpu_custom_call" | custom-call | flops 1342177280 | bytes 11272192 | tf_op jit(solution)/shard_map/value_ahead/pallas_call | solution.py:397
  38.5 6.8 %collective-permute-done.5.slot = bf16[2,320,256]{2,1,0:T(8,128)(2,1)} collective-permute-done((bf16[2,320,256]{2,1,0:T(8,128)(2,1)}, bf16[2,320,256]{2,1,0:T(8,128)(2,1)}, u32[]{:S(2)}, u32[]{:S(2)}) %collective-permute-start.5) | collective-permute-done | bytes 327712 | tf_op jit(solution)/shard_map/ppermute | solution.py:298
  45.3 2.5 %mixed.1 = (bf16[512,256]{1,0:T(8,128)(2,1)S(1)}, bf16[512,256]{1,0:T(8,128)(2,1)S(1)}) custom-call(s32[5]{0:T(128)S(1)} %stack.67.idx, f32[2,512,256]{2,1,0:T(8,128)S(1)} %get-tuple-element.37.part, bf16[2,512,640]{2,1,0:T(8,128)(2,1)S(1)} %get-tuple-element.38.last, bf16[2,4,4,128,128]{4,3,2,1,0:T(8,128)(2,1)S(1)} %get-tuple-element.39.weights, ...), custom_call_target="tpu_custom_call" | custom-call | flops 335544320 | bytes 3932160 | tf_op jit(solution)/shard_map/mixed/pallas_call | solution.py:410
  47.8 0.1 collective-permute-start.6
  47.9 0.1 collective-permute-start.10
  48.0 1.6 %collective-permute-done.8.rest_1_ = bf16[2,320,256]{2,1,0:T(8,128)(2,1)S(1)} collective-permute-done((bf16[2,320,256]{2,1,0:T(8,128)(2,1)}, bf16[2,320,256]{2,1,0:T(8,128)(2,1)S(1)}, u32[]{:S(2)}, u32[]{:S(2)}) %collective-permute-start.8) | collective-permute-done | bytes 327712 | tf_op jit(solution)/shard_map/ppermute | solution.py:298
  49.6 5.1 %grad_out.1 = (bf16[16,128]{1,0:T(8,128)(2,1)S(1)}, bf16[2,320,256]{2,1,0:T(8,128)(2,1)S(1)}, bf16[2,320,256]{2,1,0:T(8,128)(2,1)}, bf16[2,320,256]{2,1,0:T(8,128)(2,1)S(1)}, bf16[2,320,256]{2,1,0:T(8,128)(2,1)S(1)}) custom-call(s32[5]{0:T(128)S(1)} %stack.67.idx, bf16[512,2560]{1,0:T(8,128)(2,1)S(1)} %bitcast.51, ...), custom_call_target="tpu_custom_call" | custom-call | flops 1342177280 | bytes 7077888 | tf_op jit(solution)/shard_map/grad_out/pallas_call | solution.py:432
  54.8 1.9 %collective-permute-start.11 = (bf16[2,320,256]{2,1,0:T(8,128)(2,1)S(1)}, bf16[2,320,256]{2,1,0:T(8,128)(2,1)S(1)}, u32[]{:S(2)}, u32[]{:S(2)}) collective-permute-start(bf16[2,320,256]{2,1,0:T(8,128)(2,1)S(1)} %get-tuple-element.48), channel_id=1, source_target_pairs={{0,8},{4,12},{8,0},{12,4},{16,24},{20,28},{24,16},{28,20},{1,9},{5... | collective-permute-start | bytes 983048 | tf_op jit(solution)/shard_map/ppermute | solution.py:298
  56.6 2.1 %collective-permute-done.10.rest_3_ = bf16[2,320,256]{2,1,0:T(8,128)(2,1)S(1)} collective-permute-done((bf16[2,320,256]{2,1,0:T(8,128)(2,1)}, bf16[2,320,256]{2,1,0:T(8,128)(2,1)S(1)}, u32[]{:S(2)}, u32[]{:S(2)}) %collective-permute-start.10) | collective-permute-done | bytes 327712 | tf_op jit(solution)/shard_map/ppermute | solution.py:298
  58.7 5.9 %d_value.1 = (bf16[256,1024]{1,0:T(8,128)(2,1)S(1)}, bf16[2560,256]{1,0:T(8,128)(2,1)S(1)}) custom-call(s32[5]{0:T(128)S(1)} %stack.67.idx, bf16[16,128]{1,0:T(8,128)(2,1)S(1)} %get-tuple-element.45.token, bf16[512,2560]{1,0:T(8,128)(2,1)S(1)} %bitcast.52, bf16[512,2560]{1,0:T(8,128)(2,1)} %collective-permute-done.7.cot_s, ...), custom_call_target="tpu_custom_call" | custom-call | flops 1342177280 | bytes 9437184 | tf_op jit(solution)/shard_map/d_value/pallas_call | solution.py:442
  64.6 1.1 copy-done.6
  65.7 0.8 add_convert_fusion.refs_1_.unread
  66.5 0.1 pad_add_fusion.idx
  66.6 0.1 collective-permute-start.18
  66.7 0.8 copy-done.5
  67.5 1.6 %collective-permute-start.19 = (bf16[2,320,256]{2,1,0:T(8,128)(2,1)S(1)}, bf16[2,320,256]{2,1,0:T(8,128)(2,1)S(1)}, u32[]{:S(2)}, u32[]{:S(2)}) collective-permute-start(bf16[2,320,256]{2,1,0:T(8,128)(2,1)S(1)} %copy-done.5), channel_id=1, source_target_pairs={{0,16},{4,20},{8,24},{12,28},{16,0},{20,4},{24,8},{28,12},{1,17},{... | collective-permute-start | bytes 983048 | tf_op jit(solution)/shard_map/ppermute | solution.py:298
  69.1 0.7 collective-permute-done.12.w_r
  69.8 1.1 copy-done.15
  70.8 1.3 %copy-done.7 = bf16[2560,256]{1,0:T(8,128)(2,1)S(1)} copy-done((bf16[2560,256]{1,0:T(8,128)(2,1)S(1)}, bf16[2560,256]{1,0:T(8,128)(2,1)}, u32[]{:S(2)}) %copy-start.7) | copy-done | bytes 1310744
  72.2 0.9 copy-done.12
  73.1 1.3 %copy-done.16 = bf16[2560,256]{1,0:T(8,128)(2,1)S(1)} copy-done((bf16[2560,256]{1,0:T(8,128)(2,1)S(1)}, bf16[2560,256]{1,0:T(8,128)(2,1)}, u32[]{:S(2)}) %copy-start.16) | copy-done | bytes 1310744
  74.4 2.4 %terms.1 = (bf16[16,128]{1,0:T(8,128)(2,1)S(1)}, bf16[2,256,640]{2,1,0:T(8,128)(2,1)S(1)}, bf16[2,256,640]{2,1,0:T(8,128)(2,1)S(1)}, bf16[4,256,640]{2,1,0:T(8,128)(2,1)S(1)}) custom-call(s32[4]{0:T(128)S(1)} %pad_add_fusion.idx, bf16[512,256]{1,0:T(8,128)(2,1)S(1)} %copy-done.12, bf16[512,256]{1,0:T(8,128)(2,1)S(1)} %copy-done.14, ...), custom_call_target="tpu_custom_call" | custom-call | flops 1342177280 | bytes 5767168 | tf_op jit(solution)/shard_map/terms/pallas_call | solution.py:467
  76.8 1.6 %collective-permute-start.13 = (bf16[2,256,640]{2,1,0:T(8,128)(2,1)S(1)}, bf16[2,256,640]{2,1,0:T(8,128)(2,1)S(1)}, u32[]{:S(2)}, u32[]{:S(2)}) collective-permute-start(bf16[2,256,640]{2,1,0:T(8,128)(2,1)S(1)} %get-tuple-element.50), channel_id=1, source_target_pairs={{0,1},{1,0},{2,3},{3,2},{4,5},{5,4},{6,7},{7,6},{8,9},{9,8},{10,11... | collective-permute-start | bytes 1966088 | tf_op jit(solution)/shard_map/ppermute | solution.py:309
  78.4 1.5 %collective-permute-start.15 = (bf16[2,256,640]{2,1,0:T(8,128)(2,1)S(1)}, bf16[2,256,640]{2,1,0:T(8,128)(2,1)S(1)}, u32[]{:S(2)}, u32[]{:S(2)}) collective-permute-start(bf16[2,256,640]{2,1,0:T(8,128)(2,1)S(1)} %get-tuple-element.51), channel_id=1, source_target_pairs={{0,2},{1,3},{2,0},{3,1},{4,6},{5,7},{6,4},{7,5},{8,10},{9,11},{10,... | collective-permute-start | bytes 1966088 | tf_op jit(solution)/shard_map/ppermute | solution.py:309
  79.9 4.4 %grad_value.1 = (bf16[2,320,256]{2,1,0:T(8,128)(2,1)S(1)}, bf16[2,320,256]{2,1,0:T(8,128)(2,1)S(1)}, bf16[2,320,256]{2,1,0:T(8,128)(2,1)S(1)}, bf16[2,320,256]{2,1,0:T(8,128)(2,1)S(1)}) custom-call(s32[5]{0:T(128)S(1)} %stack.67.idx, bf16[16,128]{1,0:T(8,128)(2,1)S(1)} %get-tuple-element.52.token, bf16[2,320,256]{2,1,0:T(8,128)(2,1)S(1)} %copy-done.5, ...), custom_call_target="tpu_custom_call" | custom-call | flops 1342177280 | bytes 7077888 | tf_op jit(solution)/shard_map/grad_value/pallas_call | solution.py:476
  84.3 0.2 collective-permute-start.17
  84.5 0.2 convert_element_type.53
  84.7 0.1 collective-permute-done.19.far
  84.8 8.8 %collective-permute-done.17.got = bf16[2,320,256]{2,1,0:T(8,128)(2,1)S(1)} collective-permute-done((bf16[2,320,256]{2,1,0:T(8,128)(2,1)S(1)}, bf16[2,320,256]{2,1,0:T(8,128)(2,1)S(1)}, u32[]{:S(2)}, u32[]{:S(2)}) %collective-permute-start.17) | collective-permute-done | bytes 327712 | tf_op jit(solution)/shard_map/ppermute | solution.py:298
  93.5 0.2 sum.1
  93.7 0.4 collective-permute-start.20
  94.1 2.2 %collective-permute-start.21 = (bf16[2,320,256]{2,1,0:T(8,128)(2,1)S(1)}, bf16[2,320,256]{2,1,0:T(8,128)(2,1)S(1)}, u32[]{:S(2)}, u32[]{:S(2)}) collective-permute-start(bf16[2,320,256]{2,1,0:T(8,128)(2,1)S(1)} %get-tuple-element.61), channel_id=1, source_target_pairs={{0,16},{4,20},{8,24},{12,28},{16,0},{20,4},{24,8},{28,12},{1,17},{... | collective-permute-start | bytes 983048 | tf_op jit(solution)/shard_map/ppermute | solution.py:298
  96.3 0.1 collective-permute-start.23
  96.4 0.1 convert_element_type.54
  96.5 0.1 convert_element_type.58
  96.6 0.2 fusion.8
  96.8 0.6 collective-permute-start.14
  97.3 0.8 collective-permute-start.16
  98.1 10.2 %collective-permute-done.20 = bf16[2,320,256]{2,1,0:T(8,128)(2,1)S(1)} collective-permute-done((bf16[2,320,256]{2,1,0:T(8,128)(2,1)S(1)}, bf16[2,320,256]{2,1,0:T(8,128)(2,1)S(1)}, u32[]{:S(2)}, u32[]{:S(2)}) %collective-permute-start.20) | collective-permute-done | bytes 327712 | tf_op jit(solution)/shard_map/ppermute | solution.py:298
  108.3 1.9 %collective-permute-done.21 = bf16[2,320,256]{2,1,0:T(8,128)(2,1)S(1)} collective-permute-done((bf16[2,320,256]{2,1,0:T(8,128)(2,1)S(1)}, bf16[2,320,256]{2,1,0:T(8,128)(2,1)S(1)}, u32[]{:S(2)}, u32[]{:S(2)}) %collective-permute-start.21) | collective-permute-done | bytes 327712 | tf_op jit(solution)/shard_map/ppermute | solution.py:298
  110.2 0.1 convert_add_fusion
  110.3 0.1 collective-permute-start.22
  110.5 0.9 pad_maximum_fusion.2
  111.4 0.3 fusion.7
  111.7 0.9 pad_maximum_fusion
  112.6 0.9 pad_maximum_fusion.1
  (50 shorter events, 0.4 us)
Async XLA Ops:
  0.6 3.6 %copy-start = (bf16[2,2,128,2560]{3,2,1,0:T(8,128)(2,1)S(1)}, bf16[2,2,128,2560]{3,2,1,0:T(8,128)(2,1)}, u32[]{:S(2)}) copy-start(bf16[2,2,128,2560]{3,2,1,0:T(8,128)(2,1)} %param.7) | copy-start | bytes 7864324
  2.1 1.8 %collective-permute-start = (bf16[2,320,256]{2,1,0:T(8,128)(2,1)S(1)}, bf16[2,320,256]{2,1,0:T(8,128)(2,1)S(1)}, u32[]{:S(2)}, u32[]{:S(2)}) collective-permute-start(bf16[2,320,256]{2,1,0:T(8,128)(2,1)S(1)} %get-tuple-element.72), channel_id=1, source_target_pairs={{0,4},{4,0},{8,12},{12,8},{16,20},{20,16},{24,28},{28,24},{1,5},{5... | collective-permute-start | bytes 983048 | tf_op jit(solution)/shard_map/ppermute | solution.py:306
  3.8 26.8 %collective-permute-start.1 = (bf16[512,2560]{1,0:T(8,128)(2,1)}, bf16[512,2560]{1,0:T(8,128)(2,1)}, u32[]{:S(2)}, u32[]{:S(2)}) collective-permute-start(bf16[512,2560]{1,0:T(8,128)(2,1)} %bitcast.53), channel_id=1, source_target_pairs={{0,4},{4,0},{8,12},{12,8},{16,20},{20,16},{24,28},{28,24},{1,5},{5... | collective-permute-start | bytes 7864328 | tf_op jit(solution)/shard_map/ppermute | solution.py:306
  4.2 45.4 %collective-permute-start.7 = (bf16[512,2560]{1,0:T(8,128)(2,1)S(1)}, bf16[512,2560]{1,0:T(8,128)(2,1)}, u32[]{:S(2)}, u32[]{:S(2)}) collective-permute-start(bf16[512,2560]{1,0:T(8,128)(2,1)S(1)} %bitcast.50), channel_id=1, source_target_pairs={{0,4},{4,0},{8,12},{12,8},{16,20},{20,16},{24,28},{28,24},{1,5},{5... | collective-permute-start | bytes 7864328 | tf_op jit(solution)/shard_map/ppermute | solution.py:306
  4.4 26.3 %collective-permute-start.2 = (bf16[4,8,128,128]{3,2,1,0:T(8,128)(2,1)}, bf16[4,8,128,128]{3,2,1,0:T(8,128)(2,1)}, u32[]{:S(2)}, u32[]{:S(2)}) collective-permute-start(bf16[4,8,128,128]{3,2,1,0:T(8,128)(2,1)} %bitcast.56), channel_id=1, source_target_pairs={{0,4},{4,0},{8,12},{12,8},{16,20},{20,16},{24,28},{28,24},{1,5},{5... | collective-permute-start | bytes 3145736 | tf_op jit(solution)/shard_map/ppermute | solution.py:306
  4.8 17.9 %collective-permute-start.3 = (bf16[2,320,256]{2,1,0:T(8,128)(2,1)S(1)}, bf16[2,320,256]{2,1,0:T(8,128)(2,1)S(1)}, u32[]{:S(2)}, u32[]{:S(2)}) collective-permute-start(bf16[2,320,256]{2,1,0:T(8,128)(2,1)S(1)} %pad_maximum_fusion.5.rest_0_), channel_id=1, source_target_pairs={{0,8},{4,12},{8,0},{12,4},{16,24},{20,28},{24,16},{28,20},{1,9},{5... | collective-permute-start | bytes 983048 | tf_op jit(solution)/shard_map/ppermute | solution.py:298
  7.6 17.7 %collective-permute-start.4 = (bf16[2,320,256]{2,1,0:T(8,128)(2,1)S(1)}, bf16[2,320,256]{2,1,0:T(8,128)(2,1)S(1)}, u32[]{:S(2)}, u32[]{:S(2)}) collective-permute-start(bf16[2,320,256]{2,1,0:T(8,128)(2,1)S(1)} %pad_maximum_fusion.5.rest_0_), channel_id=1, source_target_pairs={{0,16},{4,20},{8,24},{12,28},{16,0},{20,4},{24,8},{28,12},{1,17},{... | collective-permute-start | bytes 983048 | tf_op jit(solution)/shard_map/ppermute | solution.py:298
  26.1 0.7 copy-start.8
  26.8 0.7 copy-start.10
  27.5 17.8 %collective-permute-start.5 = (bf16[2,320,256]{2,1,0:T(8,128)(2,1)}, bf16[2,320,256]{2,1,0:T(8,128)(2,1)}, u32[]{:S(2)}, u32[]{:S(2)}) collective-permute-start(bf16[2,320,256]{2,1,0:T(8,128)(2,1)} %get-tuple-element.36.rest_2_), channel_id=1, source_target_pairs={{0,8},{4,12},{8,0},{12,4},{16,24},{20,28},{24,16},{28,20},{1,9},{5... | collective-permute-start | bytes 983048 | tf_op jit(solution)/shard_map/ppermute | solution.py:298
  28.1 19.8 %collective-permute-start.9 = (bf16[2,320,256]{2,1,0:T(8,128)(2,1)}, bf16[2,320,256]{2,1,0:T(8,128)(2,1)}, u32[]{:S(2)}, u32[]{:S(2)}) collective-permute-start(bf16[2,320,256]{2,1,0:T(8,128)(2,1)} %copy-done.8), channel_id=1, source_target_pairs={{0,16},{4,20},{8,24},{12,28},{16,0},{20,4},{24,8},{28,12},{1,17},{... | collective-permute-start | bytes 983048 | tf_op jit(solution)/shard_map/ppermute | solution.py:298
  30.6 19.0 %collective-permute-start.8 = (bf16[2,320,256]{2,1,0:T(8,128)(2,1)}, bf16[2,320,256]{2,1,0:T(8,128)(2,1)S(1)}, u32[]{:S(2)}, u32[]{:S(2)}) collective-permute-start(bf16[2,320,256]{2,1,0:T(8,128)(2,1)} %in_order.2), channel_id=1, source_target_pairs={{0,8},{4,12},{8,0},{12,4},{16,24},{20,28},{24,16},{28,20},{1,9},{5... | collective-permute-start | bytes 983048 | tf_op jit(solution)/shard_map/ppermute | solution.py:298
  30.7 1.7 %copy-start.1 = (bf16[2,2,128,2560]{3,2,1,0:T(8,128)(2,1)S(1)}, bf16[2,2,128,2560]{3,2,1,0:T(8,128)(2,1)}, u32[]{:S(2)}) copy-start(bf16[2,2,128,2560]{3,2,1,0:T(8,128)(2,1)} %param.5) | copy-start | bytes 7864324
  32.4 1.2 %copy-start.3 = (bf16[2,2,8,128,128]{4,3,2,1,0:T(8,128)(2,1)S(1)}, bf16[2,2,8,128,128]{4,3,2,1,0:T(8,128)(2,1)}, u32[]{:S(2)}) copy-start(bf16[2,2,8,128,128]{4,3,2,1,0:T(8,128)(2,1)} %param.6) | copy-start | bytes 3145732
  47.8 7.0 %copy-start.11 = (bf16[512,256]{1,0:T(8,128)(2,1)}, bf16[512,256]{1,0:T(8,128)(2,1)S(1)}, u32[]{:S(2)}) copy-start(bf16[512,256]{1,0:T(8,128)(2,1)S(1)} %get-tuple-element.40.mixed_o) | copy-start | bytes 786436
  47.8 1.8 %collective-permute-start.6 = (bf16[512,256]{1,0:T(8,128)(2,1)S(1)}, bf16[512,256]{1,0:T(8,128)(2,1)S(1)}, u32[]{:S(2)}, u32[]{:S(2)}) collective-permute-start(bf16[512,256]{1,0:T(8,128)(2,1)S(1)} %get-tuple-element.41.mixed_s), channel_id=1, source_target_pairs={{0,4},{4,0},{8,12},{12,8},{16,20},{20,16},{24,28},{28,24},{1,5},{5... | collective-permute-start | bytes 786440 | tf_op jit(solution)/shard_map/ppermute | solution.py:306
  47.9 10.8 %collective-permute-start.10 = (bf16[2,320,256]{2,1,0:T(8,128)(2,1)}, bf16[2,320,256]{2,1,0:T(8,128)(2,1)S(1)}, u32[]{:S(2)}, u32[]{:S(2)}) collective-permute-start(bf16[2,320,256]{2,1,0:T(8,128)(2,1)} %collective-permute-done.9.rest_2_), channel_id=1, source_target_pairs={{0,8},{4,12},{8,0},{12,4},{16,24},{20,28},{24,16},{28,20},{1,9},{5... | collective-permute-start | bytes 983048 | tf_op jit(solution)/shard_map/ppermute | solution.py:298
  49.6 5.2 %copy-start.13 = (bf16[512,256]{1,0:T(8,128)(2,1)}, bf16[512,256]{1,0:T(8,128)(2,1)S(1)}, u32[]{:S(2)}) copy-start(bf16[512,256]{1,0:T(8,128)(2,1)S(1)} %collective-permute-done.6.rest_0_.mixed_r) | copy-start | bytes 786436
  49.6 9.1 %copy-start.4 = (bf16[2,2,8,128,128]{4,3,2,1,0:T(8,128)(2,1)S(1)}, bf16[2,2,8,128,128]{4,3,2,1,0:T(8,128)(2,1)}, u32[]{:S(2)}) copy-start(bf16[2,2,8,128,128]{4,3,2,1,0:T(8,128)(2,1)} %param.6) | copy-start | bytes 3145732
  49.6 9.1 %copy-start.9 = (bf16[2,320,256]{2,1,0:T(8,128)(2,1)S(1)}, bf16[2,320,256]{2,1,0:T(8,128)(2,1)}, u32[]{:S(2)}) copy-start(bf16[2,320,256]{2,1,0:T(8,128)(2,1)} %copy-done.8) | copy-start | bytes 983044
  54.8 10.9 %collective-permute-start.11 = (bf16[2,320,256]{2,1,0:T(8,128)(2,1)S(1)}, bf16[2,320,256]{2,1,0:T(8,128)(2,1)S(1)}, u32[]{:S(2)}, u32[]{:S(2)}) collective-permute-start(bf16[2,320,256]{2,1,0:T(8,128)(2,1)S(1)} %get-tuple-element.48), channel_id=1, source_target_pairs={{0,8},{4,12},{8,0},{12,4},{16,24},{20,28},{24,16},{28,20},{1,9},{5... | collective-permute-start | bytes 983048 | tf_op jit(solution)/shard_map/ppermute | solution.py:298
  64.6 1.1 copy-start.6
  66.5 1.0 copy-start.5
  66.5 4.3 %copy-start.14 = (bf16[512,256]{1,0:T(8,128)(2,1)S(1)}, bf16[512,256]{1,0:T(8,128)(2,1)}, u32[]{:S(2)}) copy-start(bf16[512,256]{1,0:T(8,128)(2,1)} %copy-done.13) | copy-start | bytes 786436
  66.5 3.2 %collective-permute-start.12 = (bf16[2560,256]{1,0:T(8,128)(2,1)}, bf16[2560,256]{1,0:T(8,128)(2,1)S(1)}, u32[]{:S(2)}, u32[]{:S(2)}) collective-permute-start(bf16[2560,256]{1,0:T(8,128)(2,1)} %in_order.3.w_o), channel_id=1, source_target_pairs={{0,4},{4,0},{8,12},{12,8},{16,20},{20,16},{24,28},{28,24},{1,5},{5... | collective-permute-start | bytes 3932168 | tf_op jit(solution)/shard_map/ppermute | solution.py:306
  66.6 13.3 %copy-start.2 = (bf16[2,2,128,2560]{3,2,1,0:T(8,128)(2,1)S(1)}, bf16[2,2,128,2560]{3,2,1,0:T(8,128)(2,1)}, u32[]{:S(2)}) copy-start(bf16[2,2,128,2560]{3,2,1,0:T(8,128)(2,1)} %param.5) | copy-start | bytes 7864324
  66.6 18.1 %collective-permute-start.18 = (bf16[2,320,256]{2,1,0:T(8,128)(2,1)}, bf16[2,320,256]{2,1,0:T(8,128)(2,1)S(1)}, u32[]{:S(2)}, u32[]{:S(2)}) collective-permute-start(bf16[2,320,256]{2,1,0:T(8,128)(2,1)} %get-tuple-element.59), channel_id=1, source_target_pairs={{0,8},{4,12},{8,0},{12,4},{16,24},{20,28},{24,16},{28,20},{1,9},{5... | collective-permute-start | bytes 983048 | tf_op jit(solution)/shard_map/ppermute | solution.py:298
  67.5 17.3 %collective-permute-start.19 = (bf16[2,320,256]{2,1,0:T(8,128)(2,1)S(1)}, bf16[2,320,256]{2,1,0:T(8,128)(2,1)S(1)}, u32[]{:S(2)}, u32[]{:S(2)}) collective-permute-start(bf16[2,320,256]{2,1,0:T(8,128)(2,1)S(1)} %copy-done.5), channel_id=1, source_target_pairs={{0,16},{4,20},{8,24},{12,28},{16,0},{20,4},{24,8},{28,12},{1,17},{... | collective-permute-start | bytes 983048 | tf_op jit(solution)/shard_map/ppermute | solution.py:298
  69.8 1.1 copy-start.15
  70.8 1.3 %copy-start.7 = (bf16[2560,256]{1,0:T(8,128)(2,1)S(1)}, bf16[2560,256]{1,0:T(8,128)(2,1)}, u32[]{:S(2)}) copy-start(bf16[2560,256]{1,0:T(8,128)(2,1)} %in_order.3.w_o) | copy-start | bytes 3932164
  72.2 0.9 copy-start.12
  73.1 1.3 %copy-start.16 = (bf16[2560,256]{1,0:T(8,128)(2,1)S(1)}, bf16[2560,256]{1,0:T(8,128)(2,1)}, u32[]{:S(2)}) copy-start(bf16[2560,256]{1,0:T(8,128)(2,1)} %copy-done.15) | copy-start | bytes 3932164
  76.8 19.5 %collective-permute-start.13 = (bf16[2,256,640]{2,1,0:T(8,128)(2,1)S(1)}, bf16[2,256,640]{2,1,0:T(8,128)(2,1)S(1)}, u32[]{:S(2)}, u32[]{:S(2)}) collective-permute-start(bf16[2,256,640]{2,1,0:T(8,128)(2,1)S(1)} %get-tuple-element.50), channel_id=1, source_target_pairs={{0,1},{1,0},{2,3},{3,2},{4,5},{5,4},{6,7},{7,6},{8,9},{9,8},{10,11... | collective-permute-start | bytes 1966088 | tf_op jit(solution)/shard_map/ppermute | solution.py:309
  78.4 18.1 %collective-permute-start.15 = (bf16[2,256,640]{2,1,0:T(8,128)(2,1)S(1)}, bf16[2,256,640]{2,1,0:T(8,128)(2,1)S(1)}, u32[]{:S(2)}, u32[]{:S(2)}) collective-permute-start(bf16[2,256,640]{2,1,0:T(8,128)(2,1)S(1)} %get-tuple-element.51), channel_id=1, source_target_pairs={{0,2},{1,3},{2,0},{3,1},{4,6},{5,7},{6,4},{7,5},{8,10},{9,11},{10,... | collective-permute-start | bytes 1966088 | tf_op jit(solution)/shard_map/ppermute | solution.py:309
  84.3 9.3 %collective-permute-start.17 = (bf16[2,320,256]{2,1,0:T(8,128)(2,1)S(1)}, bf16[2,320,256]{2,1,0:T(8,128)(2,1)S(1)}, u32[]{:S(2)}, u32[]{:S(2)}) collective-permute-start(bf16[2,320,256]{2,1,0:T(8,128)(2,1)S(1)} %get-tuple-element.56), channel_id=1, source_target_pairs={{0,8},{4,12},{8,0},{12,4},{16,24},{20,28},{24,16},{28,20},{1,9},{5... | collective-permute-start | bytes 983048 | tf_op jit(solution)/shard_map/ppermute | solution.py:298
  93.7 14.6 %collective-permute-start.20 = (bf16[2,320,256]{2,1,0:T(8,128)(2,1)S(1)}, bf16[2,320,256]{2,1,0:T(8,128)(2,1)S(1)}, u32[]{:S(2)}, u32[]{:S(2)}) collective-permute-start(bf16[2,320,256]{2,1,0:T(8,128)(2,1)S(1)} %get-tuple-element.60), channel_id=1, source_target_pairs={{0,8},{4,12},{8,0},{12,4},{16,24},{20,28},{24,16},{28,20},{1,9},{5... | collective-permute-start | bytes 983048 | tf_op jit(solution)/shard_map/ppermute | solution.py:298
  94.1 16.1 %collective-permute-start.21 = (bf16[2,320,256]{2,1,0:T(8,128)(2,1)S(1)}, bf16[2,320,256]{2,1,0:T(8,128)(2,1)S(1)}, u32[]{:S(2)}, u32[]{:S(2)}) collective-permute-start(bf16[2,320,256]{2,1,0:T(8,128)(2,1)S(1)} %get-tuple-element.61), channel_id=1, source_target_pairs={{0,16},{4,20},{8,24},{12,28},{16,0},{20,4},{24,8},{28,12},{1,17},{... | collective-permute-start | bytes 983048 | tf_op jit(solution)/shard_map/ppermute | solution.py:298
  96.3 14.2 %collective-permute-start.23 = (f32[320,256]{1,0:T(8,128)S(1)}, f32[320,256]{1,0:T(8,128)S(1)}, u32[]{:S(2)}, u32[]{:S(2)}) collective-permute-start(f32[320,256]{1,0:T(8,128)S(1)} %slice_bitcast_fusion.2), channel_id=1, source_target_pairs={{0,4},{4,0},{8,12},{12,8},{16,20},{20,16},{24,28},{28,24},{1,5},{5... | collective-permute-start | bytes 983048 | tf_op jit(solution)/shard_map/ppermute | solution.py:306
  96.8 14.6 %collective-permute-start.14 = (bf16[256,640]{1,0:T(8,128)(2,1)S(1)}, bf16[256,640]{1,0:T(8,128)(2,1)S(1)}, u32[]{:S(2)}, u32[]{:S(2)}) collective-permute-start(bf16[256,640]{1,0:T(8,128)(2,1)S(1)} %get-tuple-element.65), channel_id=1, source_target_pairs={{0,2},{1,3},{2,0},{3,1},{4,6},{5,7},{6,4},{7,5},{8,10},{9,11},{10,... | collective-permute-start | bytes 983048 | tf_op jit(solution)/shard_map/ppermute | solution.py:309
  97.3 14.1 %collective-permute-start.16 = (bf16[256,640]{1,0:T(8,128)(2,1)S(1)}, bf16[256,640]{1,0:T(8,128)(2,1)S(1)}, u32[]{:S(2)}, u32[]{:S(2)}) collective-permute-start(bf16[256,640]{1,0:T(8,128)(2,1)S(1)} %get-tuple-element.66), channel_id=1, source_target_pairs={{0,1},{1,0},{2,3},{3,2},{4,5},{5,4},{6,7},{7,6},{8,9},{9,8},{10,11... | collective-permute-start | bytes 983048 | tf_op jit(solution)/shard_map/ppermute | solution.py:309
  110.3 2.2 %collective-permute-start.22 = (f32[320,256]{1,0:T(8,128)S(1)}, f32[320,256]{1,0:T(8,128)S(1)}, u32[]{:S(2)}, u32[]{:S(2)}) collective-permute-start(f32[320,256]{1,0:T(8,128)S(1)} %slice_bitcast_fusion), channel_id=1, source_target_pairs={{0,4},{4,0},{8,12},{12,8},{16,20},{20,16},{24,28},{28,24},{1,5},{5... | collective-permute-start | bytes 983048 | tf_op jit(solution)/shard_map/ppermute | solution.py:306

commit v23 on v22

--- a/solution.py
+++ b/solution.py
@@ -159,7 +159,7 @@
 def d_value_kernel(n_slots, idx, token, cot_o, cot_s, mix_o, mix_s, *rest):
     del token
     slots, rest = rest[:n_slots], rest[n_slots:]
-    left_v, w_out, w_v, cot_v, mix_v, sems, slots_v, slot_sems, out_sems = rest
+    left_v, w_out, cot_v, mix_v, sems, slots_v, slot_sems = rest
     tokens, heads = cot_o.shape[0], mix_v.shape[2]
     here = pl.ds(idx[0] * heads, heads)
     slot_copies = begin_slots(slots, slots_v, slot_sems)
@@ -170,14 +170,12 @@
     )
     for copy in slot_copies:
         copy.wait()
-    place(idx, idx[0], slots_v, w_v)
-    handed = begin([(w_v, w_out)], out_sems)
+    place(idx, idx[0], slots_v, w_out)
     for half in range(2):
         copies[2 * half].wait()
-        d_mixed = dot(cot_v[half], w_v[...])
+        d_mixed = dot(cot_v[half], w_out[...])
         copies[2 * half + 1].wait()
         mix_back(d_mixed, mix_v.at[half], left_v, half * tokens)
-    handed[0].wait()
 
 
 def gradient_kernel(idx, token, unread, right_o, right_s, left_ref, *rest):
@@ -220,11 +218,11 @@
     hand_out(idx, 1, grad_v, outs)
 
 
-def relay_kernel(unread, first, second, first_out, second_out, again_out):
+def relay_kernel(unread, *refs):
     del unread
-    first_out[...] = first[...]
-    second_out[...] = second[...]
-    again_out[...] = second[...]
+    blocks, outs = refs[: len(refs) // 2], refs[len(refs) // 2 :]
+    for block, out in zip(blocks, outs):
+        out[...] = block[...]
 
 
 def sum_kernel(block, got, beside, own, near, far, onward, beside_out, total):
@@ -261,12 +259,12 @@
 VMEM = pl.BlockSpec(memory_space=pltpu.VMEM)
 
 
-def call(kernel, name, in_specs, out_shapes, scratch, flops, size=1 << 20, kinds=None, vmem=24, out_specs=None):
+def call(kernel, name, in_specs, out_shapes, scratch, flops, size=1 << 20, kinds=None, vmem=24):
     return pl.pallas_call(
         kernel,
         name=name,
         in_specs=in_specs,
-        out_specs=out_specs or [VMEM] * len(out_shapes),
+        out_specs=[VMEM] * len(out_shapes),
         out_shape=[
             jax.ShapeDtypeStruct(s, k) for s, k in zip(out_shapes, kinds or [BF16] * len(out_shapes))
         ],
@@ -368,12 +366,13 @@
         block = u_out.shape
         if line4:
             far, near = swap(u_value, 2), swap(u_value, 1)
-            far, u_out, again = call(relay_kernel, "relay", [ANY, VMEM, VMEM], [block] * 3, [], 0, vmem=8)(
+            far, u_out = call(relay_kernel, "relay", [ANY, VMEM, VMEM], [block] * 2, [], 0, vmem=8)(
                 near, far, u_out
             )
             value_slots = [u_value, near, far, swap(far, 1)]
             far = swap(u_out, 2)
-            out_slots = [u_out, swap(in_order(again, mix_s), 1), far, swap(far, 1)]
+            again = call(relay_kernel, "again", [ANY, VMEM], [block], [], 0, vmem=8)(mix_s, u_out)[0]
+            out_slots = [u_out, swap(again, 1), far, swap(far, 1)]
         else:
             value_slots, out_slots = gather_ring(u_value), gather_ring(u_out)
         n_slots = len(out_slots)
@@ -444,11 +443,9 @@
             "d_value",
             [SMEM] + [ANY] * (5 + n_slots),
             [(cols, 2 * tokens), (width, cols)],
-            [rows, halves, mix_scratch, pltpu.SemaphoreType.DMA((4,)), *slots_scratch]
-            + [pltpu.SemaphoreType.DMA((1,))],
+            [halves, mix_scratch, pltpu.SemaphoreType.DMA((4,)), *slots_scratch],
             flops,
             2 * (2 * cot.size + mix.size + 2 * width * cols + 2 * tokens * cols),
-            out_specs=[VMEM, ANY],
         )(idx, token, cot, cot_s, mix, mix_s, *out_slots)
         if line4:
             out_onward = added(out_sends[2], out_passed)

time: 114 us -> 111 us (0.974)
  starting transfers between devices: 20.8 us -> 26 us
  local copies, waits for them, and re-layouts: 12.5 us -> 7.34 us
  waiting for transfers between devices: 48.4 us -> 46.5 us
    unnamed x34 -> x30, local copies, waits for them, and re-layouts: 11 us -> 5.82 us
    ppermute x12, starting transfers between devices: 14.7 us -> 18.6 us  [move(): lax.ppermute(x, 'wide', [(2 * s + c, 2 * d + c) for s, d in pairs for c i...]
    ppermute x4, starting transfers between devices: 4.41 us -> 5.76 us  [flip(): return lax.ppermute(x, 'node', [(i, i ^ j) for i in range(n_node)])]
    ppermute x12, waiting for transfers between devices: 46.4 us -> 45.2 us  [move(): lax.ppermute(x, 'wide', [(2 * s + c, 2 * d + c) for s, d in pairs for c i...]
  transfers between devices with their start and end apart: 24 -> 24, of which waited for: 11 -> 12; matrix products, arithmetic and copies ran while one was open for 3% -> 3% of each run, Pallas kernels for 23% -> 23%
where the time goes in v23:
time: 111 us
  waiting for transfers between devices  46.5 us (42%)
  starting transfers between devices  26 us (23%)
  Pallas kernels  25.5 us (23%)
  local copies, waits for them, and re-layouts  7.34 us (7%)
  other arithmetic  4.69 us (4%)
    ppermute x12, waiting for transfers between devices, move(): lax.ppermute(x, 'wide', [(2 * s + c, 2 * d + c) for s, d in pairs for c i...  45.2 us
    ppermute x12, starting transfers between devices, move(): lax.ppermute(x, 'wide', [(2 * s + c, 2 * d + c) for s, d in pairs for c i...  18.6 us
    unnamed x30, local copies, waits for them, and re-layouts  5.82 us
    ppermute x4, starting transfers between devices, flip(): return lax.ppermute(x, 'node', [(i, i ^ j) for i in range(n_node)])  5.76 us
    pallas_call x1, Pallas kernels, body(): call(functools.partial(d_value_kernel, n_slots), 'd_value', [SMEM] + [ANY...  5.21 us
    pallas_call x1, Pallas kernels, body(): call(functools.partial(grad_out_kernel, len(unread)), 'grad_out', [SMEM]...  5.12 us
    pallas_call x1, Pallas kernels, body(): call(functools.partial(part_kernel, n_slots - 1), 'value_ahead', [SMEM] +...  4.9 us
    pallas_call x1, Pallas kernels, body(): call(gradient_kernel, 'grad_value', [SMEM] + [ANY] * 4 + [VMEM], send_sha...  4.39 us
  transfers between devices with their start and end apart: 24, of which 12 were waited for; matrix products, arithmetic and copies ran while one was open for 3% of the time, Pallas kernels for 23%

profile of v23, /device:TPU:0, one launch (start us, length us, event | category | flops | bytes accessed | tf_op | source)
XLA Modules:
  0.0 111.0 jit_solution(12831251807116841312)
XLA Ops:
  0.7 1.3 %slice_bitcast_fusion.5 = (bf16[1,320,256]{2,1,0:T(8,128)(2,1)S(1)}, bf16[1,320,256]{2,1,0:T(8,128)(2,1)S(1)}, bf16[1,320,256]{2,1,0:T(8,128)(2,1)S(1)}, bf16[1,320,256]{2,1,0:T(8,128)(2,1)S(1)}) fusion(bf16[320,512]{1,0:T(8,128)(2,1)} %param.8, bf16[320,512]{1,0:T(8,128)(2,1)} %param.9), kind=kLoop, calls=%fused_computation.34 | loop fusion | bytes 1310720 | tf_op jit(solution)/shard_map/stack | solution.py:312
  2.0 0.1 broadcast_select_fusion
  2.1 0.5 collective-permute-start
  2.6 1.3 %collective-permute-done = bf16[2,320,256]{2,1,0:T(8,128)(2,1)S(1)} collective-permute-done((bf16[2,320,256]{2,1,0:T(8,128)(2,1)S(1)}, bf16[2,320,256]{2,1,0:T(8,128)(2,1)S(1)}, u32[]{:S(2)}, u32[]{:S(2)}) %collective-permute-start) | collective-permute-done | bytes 327712 | tf_op jit(solution)/shard_map/ppermute | solution.py:304
  3.8 0.4 collective-permute-start.1
  4.2 0.1 collective-permute-start.7
  4.4 0.4 collective-permute-start.2
  4.8 2.8 %collective-permute-start.3 = (bf16[2,320,256]{2,1,0:T(8,128)(2,1)S(1)}, bf16[2,320,256]{2,1,0:T(8,128)(2,1)S(1)}, u32[]{:S(2)}, u32[]{:S(2)}) collective-permute-start(bf16[2,320,256]{2,1,0:T(8,128)(2,1)S(1)} %pad_maximum_fusion.5.rest_0_), channel_id=1, source_target_pairs={{0,8},{4,12},{8,0},{12,4},{16,24},{20,28},{24,16},{28,20},{1,9},{5... | collective-permute-start | bytes 983048 | tf_op jit(solution)/shard_map/ppermute | solution.py:296
  7.6 2.6 %collective-permute-start.4 = (bf16[2,320,256]{2,1,0:T(8,128)(2,1)S(1)}, bf16[2,320,256]{2,1,0:T(8,128)(2,1)S(1)}, u32[]{:S(2)}, u32[]{:S(2)}) collective-permute-start(bf16[2,320,256]{2,1,0:T(8,128)(2,1)S(1)} %pad_maximum_fusion.5.rest_0_), channel_id=1, source_target_pairs={{0,16},{4,20},{8,24},{12,28},{16,0},{20,4},{24,8},{28,12},{1,17},{... | collective-permute-start | bytes 983048 | tf_op jit(solution)/shard_map/ppermute | solution.py:296
  10.2 12.5 %collective-permute-done.3.unread.rest_1_ = bf16[2,320,256]{2,1,0:T(8,128)(2,1)S(1)} collective-permute-done((bf16[2,320,256]{2,1,0:T(8,128)(2,1)S(1)}, bf16[2,320,256]{2,1,0:T(8,128)(2,1)S(1)}, u32[]{:S(2)}, u32[]{:S(2)}) %collective-permute-start.3) | collective-permute-done | bytes 327712 | tf_op jit(solution)/shard_map/ppermute | solution.py:296
  22.8 2.5 %collective-permute-done.4.refs_0_ = bf16[2,320,256]{2,1,0:T(8,128)(2,1)S(1)} collective-permute-done((bf16[2,320,256]{2,1,0:T(8,128)(2,1)S(1)}, bf16[2,320,256]{2,1,0:T(8,128)(2,1)S(1)}, u32[]{:S(2)}, u32[]{:S(2)}) %collective-permute-start.4) | collective-permute-done | bytes 327712 | tf_op jit(solution)/shard_map/ppermute | solution.py:296
  25.3 0.8 relay.1
  26.1 0.7 copy-done.5
  26.8 0.4 collective-permute-start.5
  27.2 0.1 stack.67.idx
  27.3 2.6 %collective-permute-start.9 = (bf16[2,320,256]{2,1,0:T(8,128)(2,1)S(1)}, bf16[2,320,256]{2,1,0:T(8,128)(2,1)S(1)}, u32[]{:S(2)}, u32[]{:S(2)}) collective-permute-start(bf16[2,320,256]{2,1,0:T(8,128)(2,1)S(1)} %get-tuple-element.42.refs_0_.rest_0_), channel_id=1, source_target_pairs={{0,16},{4,20},{8,24},{12,28},{16,0},{20,4},{24,8},{28,12},{1,17},{... | collective-permute-start | bytes 983048 | tf_op jit(solution)/shard_map/ppermute | solution.py:296
  30.0 0.1 collective-permute-start.8
  30.1 0.0 copy-start.1
  30.1 1.7 %copy-done.1 = bf16[2,2,128,2560]{3,2,1,0:T(8,128)(2,1)S(1)} copy-done((bf16[2,2,128,2560]{3,2,1,0:T(8,128)(2,1)S(1)}, bf16[2,2,128,2560]{3,2,1,0:T(8,128)(2,1)}, u32[]{:S(2)}) %copy-start.1) | copy-done | bytes 2621464
  31.8 4.9 %value_ahead.1 = (f32[2,512,256]{2,1,0:T(8,128)S(1)}, bf16[2,512,640]{2,1,0:T(8,128)(2,1)S(1)}, bf16[2,4,4,128,128]{4,3,2,1,0:T(8,128)(2,1)S(1)}) custom-call(s32[5]{0:T(128)S(1)} %stack.67.idx, bf16[512,2560]{1,0:T(8,128)(2,1)S(1)} %bitcast.54, bf16[512,2560]{1,0:T(8,128)(2,1)} %collective-permute-done.1.x_s.right_s, bf16[4,8,128,128]{3,2,1,0:T(8,128)(2,1)S(1)} %bitcast.57, ...), custom_call_target="tpu_custom_call" | custom-call | flops 1342177280 | bytes 11272192 | tf_op jit(solution)/shard_map/value_ahead/pallas_call | solution.py:396
  36.7 7.7 %collective-permute-done.5.slot = bf16[2,320,256]{2,1,0:T(8,128)(2,1)} collective-permute-done((bf16[2,320,256]{2,1,0:T(8,128)(2,1)}, bf16[2,320,256]{2,1,0:T(8,128)(2,1)}, u32[]{:S(2)}, u32[]{:S(2)}) %collective-permute-start.5) | collective-permute-done | bytes 327712 | tf_op jit(solution)/shard_map/ppermute | solution.py:296
  44.4 2.5 %mixed.1 = (bf16[512,256]{1,0:T(8,128)(2,1)S(1)}, bf16[512,256]{1,0:T(8,128)(2,1)S(1)}) custom-call(s32[5]{0:T(128)S(1)} %stack.67.idx, f32[2,512,256]{2,1,0:T(8,128)S(1)} %get-tuple-element.36.part, bf16[2,512,640]{2,1,0:T(8,128)(2,1)S(1)} %get-tuple-element.37.last, bf16[2,4,4,128,128]{4,3,2,1,0:T(8,128)(2,1)S(1)} %get-tuple-element.38.weights, ...), custom_call_target="tpu_custom_call" | custom-call | flops 335544320 | bytes 3932160 | tf_op jit(solution)/shard_map/mixed/pallas_call | solution.py:409
  46.9 0.1 collective-permute-start.6
  47.0 0.1 collective-permute-start.10
  47.1 1.8 %collective-permute-done.8.rest_1_ = bf16[2,320,256]{2,1,0:T(8,128)(2,1)S(1)} collective-permute-done((bf16[2,320,256]{2,1,0:T(8,128)(2,1)S(1)}, bf16[2,320,256]{2,1,0:T(8,128)(2,1)S(1)}, u32[]{:S(2)}, u32[]{:S(2)}) %collective-permute-start.8) | collective-permute-done | bytes 327712 | tf_op jit(solution)/shard_map/ppermute | solution.py:296
  48.9 5.1 %grad_out.1 = (bf16[16,128]{1,0:T(8,128)(2,1)S(1)}, bf16[2,320,256]{2,1,0:T(8,128)(2,1)S(1)}, bf16[2,320,256]{2,1,0:T(8,128)(2,1)}, bf16[2,320,256]{2,1,0:T(8,128)(2,1)S(1)}, bf16[2,320,256]{2,1,0:T(8,128)(2,1)S(1)}) custom-call(s32[5]{0:T(128)S(1)} %stack.67.idx, bf16[512,2560]{1,0:T(8,128)(2,1)S(1)} %bitcast.51, ...), custom_call_target="tpu_custom_call" | custom-call | flops 1342177280 | bytes 7077888 | tf_op jit(solution)/shard_map/grad_out/pallas_call | solution.py:431
  54.0 0.7 copy-done.9
  54.7 2.0 %collective-permute-start.11 = (bf16[2,320,256]{2,1,0:T(8,128)(2,1)S(1)}, bf16[2,320,256]{2,1,0:T(8,128)(2,1)S(1)}, u32[]{:S(2)}, u32[]{:S(2)}) collective-permute-start(bf16[2,320,256]{2,1,0:T(8,128)(2,1)S(1)} %get-tuple-element.46), channel_id=1, source_target_pairs={{0,8},{4,12},{8,0},{12,4},{16,24},{20,28},{24,16},{28,20},{1,9},{5... | collective-permute-start | bytes 983048 | tf_op jit(solution)/shard_map/ppermute | solution.py:296
  56.8 0.3 collective-permute-done.10.rest_3_
  57.1 5.2 %d_value.1 = (bf16[256,1024]{1,0:T(8,128)(2,1)S(1)}, bf16[2560,256]{1,0:T(8,128)(2,1)S(1)}) custom-call(s32[5]{0:T(128)S(1)} %stack.67.idx, bf16[16,128]{1,0:T(8,128)(2,1)S(1)} %get-tuple-element.43.token, bf16[512,2560]{1,0:T(8,128)(2,1)S(1)} %bitcast.52, bf16[512,2560]{1,0:T(8,128)(2,1)} %collective-permute-done.7.cot_s, ...), custom_call_target="tpu_custom_call" | custom-call | flops 1342177280 | bytes 9437184 | tf_op jit(solution)/shard_map/d_value/pallas_call | solution.py:441
  62.3 1.1 copy-done.7
  63.4 0.7 collective-permute-done.11
  64.1 0.8 add_convert_fusion.refs_1_.unread
  65.0 0.1 pad_add_fusion.idx
  65.0 0.6 collective-permute-start.18
  65.7 0.2 copy-done.4
  65.9 2.6 %collective-permute-start.19 = (bf16[2,320,256]{2,1,0:T(8,128)(2,1)S(1)}, bf16[2,320,256]{2,1,0:T(8,128)(2,1)S(1)}, u32[]{:S(2)}, u32[]{:S(2)}) collective-permute-start(bf16[2,320,256]{2,1,0:T(8,128)(2,1)S(1)} %copy-done.4), channel_id=1, source_target_pairs={{0,16},{4,20},{8,24},{12,28},{16,0},{20,4},{24,8},{28,12},{1,17},{... | collective-permute-start | bytes 983048 | tf_op jit(solution)/shard_map/ppermute | solution.py:296
  68.5 1.3 %copy-done.8 = bf16[2560,256]{1,0:T(8,128)(2,1)S(1)} copy-done((bf16[2560,256]{1,0:T(8,128)(2,1)S(1)}, bf16[2560,256]{1,0:T(8,128)(2,1)}, u32[]{:S(2)}) %copy-start.8) | copy-done | bytes 1310744
  69.8 2.4 %terms.1 = (bf16[16,128]{1,0:T(8,128)(2,1)S(1)}, bf16[2,256,640]{2,1,0:T(8,128)(2,1)S(1)}, bf16[2,256,640]{2,1,0:T(8,128)(2,1)S(1)}, bf16[4,256,640]{2,1,0:T(8,128)(2,1)S(1)}) custom-call(s32[4]{0:T(128)S(1)} %pad_add_fusion.idx, bf16[512,256]{1,0:T(8,128)(2,1)S(1)} %copy-done.12, bf16[512,256]{1,0:T(8,128)(2,1)S(1)} %copy-done.14, ...), custom_call_target="tpu_custom_call" | custom-call | flops 1342177280 | bytes 5767168 | tf_op jit(solution)/shard_map/terms/pallas_call | solution.py:464
  72.2 1.5 %collective-permute-start.13 = (bf16[2,256,640]{2,1,0:T(8,128)(2,1)S(1)}, bf16[2,256,640]{2,1,0:T(8,128)(2,1)S(1)}, u32[]{:S(2)}, u32[]{:S(2)}) collective-permute-start(bf16[2,256,640]{2,1,0:T(8,128)(2,1)S(1)} %get-tuple-element.48), channel_id=1, source_target_pairs={{0,1},{1,0},{2,3},{3,2},{4,5},{5,4},{6,7},{7,6},{8,9},{9,8},{10,11... | collective-permute-start | bytes 1966088 | tf_op jit(solution)/shard_map/ppermute | solution.py:307
  73.7 1.5 %collective-permute-start.15 = (bf16[2,256,640]{2,1,0:T(8,128)(2,1)S(1)}, bf16[2,256,640]{2,1,0:T(8,128)(2,1)S(1)}, u32[]{:S(2)}, u32[]{:S(2)}) collective-permute-start(bf16[2,256,640]{2,1,0:T(8,128)(2,1)S(1)} %get-tuple-element.49), channel_id=1, source_target_pairs={{0,2},{1,3},{2,0},{3,1},{4,6},{5,7},{6,4},{7,5},{8,10},{9,11},{10,... | collective-permute-start | bytes 1966088 | tf_op jit(solution)/shard_map/ppermute | solution.py:307
  75.3 4.4 %grad_value.1 = (bf16[2,320,256]{2,1,0:T(8,128)(2,1)S(1)}, bf16[2,320,256]{2,1,0:T(8,128)(2,1)S(1)}, bf16[2,320,256]{2,1,0:T(8,128)(2,1)S(1)}, bf16[2,320,256]{2,1,0:T(8,128)(2,1)S(1)}) custom-call(s32[5]{0:T(128)S(1)} %stack.67.idx, bf16[16,128]{1,0:T(8,128)(2,1)S(1)} %get-tuple-element.50.token, bf16[2,320,256]{2,1,0:T(8,128)(2,1)S(1)} %copy-done.4, ...), custom_call_target="tpu_custom_call" | custom-call | flops 1342177280 | bytes 7077888 | tf_op jit(solution)/shard_map/grad_value/pallas_call | solution.py:473
  79.7 0.9 collective-permute-start.17
  80.6 0.2 convert_element_type.53
  80.8 2.0 %collective-permute-done.18.near = bf16[2,320,256]{2,1,0:T(8,128)(2,1)S(1)} collective-permute-done((bf16[2,320,256]{2,1,0:T(8,128)(2,1)}, bf16[2,320,256]{2,1,0:T(8,128)(2,1)S(1)}, u32[]{:S(2)}, u32[]{:S(2)}) %collective-permute-start.18) | collective-permute-done | bytes 327712 | tf_op jit(solution)/shard_map/ppermute | solution.py:296
  82.8 0.5 collective-permute-done.19.far
  83.3 6.1 %collective-permute-done.17.got = bf16[2,320,256]{2,1,0:T(8,128)(2,1)S(1)} collective-permute-done((bf16[2,320,256]{2,1,0:T(8,128)(2,1)S(1)}, bf16[2,320,256]{2,1,0:T(8,128)(2,1)S(1)}, u32[]{:S(2)}, u32[]{:S(2)}) %collective-permute-start.17) | collective-permute-done | bytes 327712 | tf_op jit(solution)/shard_map/ppermute | solution.py:296
  89.4 0.2 sum.1
  89.6 0.7 collective-permute-start.20
  90.3 3.2 %collective-permute-start.21 = (bf16[2,320,256]{2,1,0:T(8,128)(2,1)S(1)}, bf16[2,320,256]{2,1,0:T(8,128)(2,1)S(1)}, u32[]{:S(2)}, u32[]{:S(2)}) collective-permute-start(bf16[2,320,256]{2,1,0:T(8,128)(2,1)S(1)} %get-tuple-element.59), channel_id=1, source_target_pairs={{0,16},{4,20},{8,24},{12,28},{16,0},{20,4},{24,8},{28,12},{1,17},{... | collective-permute-start | bytes 983048 | tf_op jit(solution)/shard_map/ppermute | solution.py:296
  93.5 0.1 collective-permute-start.23
  93.6 0.1 convert_element_type.54
  93.7 0.1 convert_element_type.58
  93.8 0.2 fusion.8
  94.0 1.2 %collective-permute-start.14 = (bf16[256,640]{1,0:T(8,128)(2,1)S(1)}, bf16[256,640]{1,0:T(8,128)(2,1)S(1)}, u32[]{:S(2)}, u32[]{:S(2)}) collective-permute-start(bf16[256,640]{1,0:T(8,128)(2,1)S(1)} %get-tuple-element.63), channel_id=1, source_target_pairs={{0,2},{1,3},{2,0},{3,1},{4,6},{5,7},{6,4},{7,5},{8,10},{9,11},{10,... | collective-permute-start | bytes 983048 | tf_op jit(solution)/shard_map/ppermute | solution.py:307
  95.2 1.5 %collective-permute-start.16 = (bf16[256,640]{1,0:T(8,128)(2,1)S(1)}, bf16[256,640]{1,0:T(8,128)(2,1)S(1)}, u32[]{:S(2)}, u32[]{:S(2)}) collective-permute-start(bf16[256,640]{1,0:T(8,128)(2,1)S(1)} %get-tuple-element.64), channel_id=1, source_target_pairs={{0,1},{1,0},{2,3},{3,2},{4,5},{5,4},{6,7},{7,6},{8,9},{9,8},{10,11... | collective-permute-start | bytes 983048 | tf_op jit(solution)/shard_map/ppermute | solution.py:307
  96.7 8.6 %collective-permute-done.20 = bf16[2,320,256]{2,1,0:T(8,128)(2,1)S(1)} collective-permute-done((bf16[2,320,256]{2,1,0:T(8,128)(2,1)S(1)}, bf16[2,320,256]{2,1,0:T(8,128)(2,1)S(1)}, u32[]{:S(2)}, u32[]{:S(2)}) %collective-permute-start.20) | collective-permute-done | bytes 327712 | tf_op jit(solution)/shard_map/ppermute | solution.py:296
  105.2 2.4 %collective-permute-done.21 = bf16[2,320,256]{2,1,0:T(8,128)(2,1)S(1)} collective-permute-done((bf16[2,320,256]{2,1,0:T(8,128)(2,1)S(1)}, bf16[2,320,256]{2,1,0:T(8,128)(2,1)S(1)}, u32[]{:S(2)}, u32[]{:S(2)}) %collective-permute-start.21) | collective-permute-done | bytes 327712 | tf_op jit(solution)/shard_map/ppermute | solution.py:296
  107.7 0.1 convert_add_fusion
  107.8 0.1 collective-permute-start.22
  108.0 0.9 pad_maximum_fusion.2
  108.9 0.2 fusion.7
  109.1 0.9 pad_maximum_fusion
  110.1 0.9 pad_maximum_fusion.1
  (46 shorter events, 0.4 us)
Async XLA Ops:
  0.6 3.6 %copy-start = (bf16[2,2,128,2560]{3,2,1,0:T(8,128)(2,1)S(1)}, bf16[2,2,128,2560]{3,2,1,0:T(8,128)(2,1)}, u32[]{:S(2)}) copy-start(bf16[2,2,128,2560]{3,2,1,0:T(8,128)(2,1)} %param.7) | copy-start | bytes 7864324
  2.1 1.8 %collective-permute-start = (bf16[2,320,256]{2,1,0:T(8,128)(2,1)S(1)}, bf16[2,320,256]{2,1,0:T(8,128)(2,1)S(1)}, u32[]{:S(2)}, u32[]{:S(2)}) collective-permute-start(bf16[2,320,256]{2,1,0:T(8,128)(2,1)S(1)} %get-tuple-element.70), channel_id=1, source_target_pairs={{0,4},{4,0},{8,12},{12,8},{16,20},{20,16},{24,28},{28,24},{1,5},{5... | collective-permute-start | bytes 983048 | tf_op jit(solution)/shard_map/ppermute | solution.py:304
  3.8 26.2 %collective-permute-start.1 = (bf16[512,2560]{1,0:T(8,128)(2,1)}, bf16[512,2560]{1,0:T(8,128)(2,1)}, u32[]{:S(2)}, u32[]{:S(2)}) collective-permute-start(bf16[512,2560]{1,0:T(8,128)(2,1)} %bitcast.53), channel_id=1, source_target_pairs={{0,4},{4,0},{8,12},{12,8},{16,20},{20,16},{24,28},{28,24},{1,5},{5... | collective-permute-start | bytes 7864328 | tf_op jit(solution)/shard_map/ppermute | solution.py:304
  4.2 44.6 %collective-permute-start.7 = (bf16[512,2560]{1,0:T(8,128)(2,1)S(1)}, bf16[512,2560]{1,0:T(8,128)(2,1)}, u32[]{:S(2)}, u32[]{:S(2)}) collective-permute-start(bf16[512,2560]{1,0:T(8,128)(2,1)S(1)} %bitcast.50), channel_id=1, source_target_pairs={{0,4},{4,0},{8,12},{12,8},{16,20},{20,16},{24,28},{28,24},{1,5},{5... | collective-permute-start | bytes 7864328 | tf_op jit(solution)/shard_map/ppermute | solution.py:304
  4.4 25.6 %collective-permute-start.2 = (bf16[4,8,128,128]{3,2,1,0:T(8,128)(2,1)}, bf16[4,8,128,128]{3,2,1,0:T(8,128)(2,1)}, u32[]{:S(2)}, u32[]{:S(2)}) collective-permute-start(bf16[4,8,128,128]{3,2,1,0:T(8,128)(2,1)} %bitcast.56), channel_id=1, source_target_pairs={{0,4},{4,0},{8,12},{12,8},{16,20},{20,16},{24,28},{28,24},{1,5},{5... | collective-permute-start | bytes 3145736 | tf_op jit(solution)/shard_map/ppermute | solution.py:304
  4.8 17.9 %collective-permute-start.3 = (bf16[2,320,256]{2,1,0:T(8,128)(2,1)S(1)}, bf16[2,320,256]{2,1,0:T(8,128)(2,1)S(1)}, u32[]{:S(2)}, u32[]{:S(2)}) collective-permute-start(bf16[2,320,256]{2,1,0:T(8,128)(2,1)S(1)} %pad_maximum_fusion.5.rest_0_), channel_id=1, source_target_pairs={{0,8},{4,12},{8,0},{12,4},{16,24},{20,28},{24,16},{28,20},{1,9},{5... | collective-permute-start | bytes 983048 | tf_op jit(solution)/shard_map/ppermute | solution.py:296
  7.6 17.7 %collective-permute-start.4 = (bf16[2,320,256]{2,1,0:T(8,128)(2,1)S(1)}, bf16[2,320,256]{2,1,0:T(8,128)(2,1)S(1)}, u32[]{:S(2)}, u32[]{:S(2)}) collective-permute-start(bf16[2,320,256]{2,1,0:T(8,128)(2,1)S(1)} %pad_maximum_fusion.5.rest_0_), channel_id=1, source_target_pairs={{0,16},{4,20},{8,24},{12,28},{16,0},{20,4},{24,8},{28,12},{1,17},{... | collective-permute-start | bytes 983048 | tf_op jit(solution)/shard_map/ppermute | solution.py:296
  26.1 0.7 copy-start.5
  26.8 17.6 %collective-permute-start.5 = (bf16[2,320,256]{2,1,0:T(8,128)(2,1)}, bf16[2,320,256]{2,1,0:T(8,128)(2,1)}, u32[]{:S(2)}, u32[]{:S(2)}) collective-permute-start(bf16[2,320,256]{2,1,0:T(8,128)(2,1)} %get-tuple-element.35.rest_2_), channel_id=1, source_target_pairs={{0,8},{4,12},{8,0},{12,4},{16,24},{20,28},{24,16},{28,20},{1,9},{5... | collective-permute-start | bytes 983048 | tf_op jit(solution)/shard_map/ppermute | solution.py:296
  27.3 2.7 %copy-start.3 = (bf16[2,2,8,128,128]{4,3,2,1,0:T(8,128)(2,1)S(1)}, bf16[2,2,8,128,128]{4,3,2,1,0:T(8,128)(2,1)}, u32[]{:S(2)}) copy-start(bf16[2,2,8,128,128]{4,3,2,1,0:T(8,128)(2,1)} %param.6) | copy-start | bytes 3145732
  27.3 2.8 %copy-start.6 = (bf16[2,320,256]{2,1,0:T(8,128)(2,1)S(1)}, bf16[2,320,256]{2,1,0:T(8,128)(2,1)}, u32[]{:S(2)}) copy-start(bf16[2,320,256]{2,1,0:T(8,128)(2,1)} %copy-done.5) | copy-start | bytes 983044
  27.3 19.7 %collective-permute-start.9 = (bf16[2,320,256]{2,1,0:T(8,128)(2,1)S(1)}, bf16[2,320,256]{2,1,0:T(8,128)(2,1)S(1)}, u32[]{:S(2)}, u32[]{:S(2)}) collective-permute-start(bf16[2,320,256]{2,1,0:T(8,128)(2,1)S(1)} %get-tuple-element.42.refs_0_.rest_0_), channel_id=1, source_target_pairs={{0,16},{4,20},{8,24},{12,28},{16,0},{20,4},{24,8},{28,12},{1,17},{... | collective-permute-start | bytes 983048 | tf_op jit(solution)/shard_map/ppermute | solution.py:296
  30.0 18.9 %collective-permute-start.8 = (bf16[2,320,256]{2,1,0:T(8,128)(2,1)S(1)}, bf16[2,320,256]{2,1,0:T(8,128)(2,1)S(1)}, u32[]{:S(2)}, u32[]{:S(2)}) collective-permute-start(bf16[2,320,256]{2,1,0:T(8,128)(2,1)S(1)} %again.1), channel_id=1, source_target_pairs={{0,8},{4,12},{8,0},{12,4},{16,24},{20,28},{24,16},{28,20},{1,9},{5... | collective-permute-start | bytes 983048 | tf_op jit(solution)/shard_map/ppermute | solution.py:296
  30.1 1.7 %copy-start.1 = (bf16[2,2,128,2560]{3,2,1,0:T(8,128)(2,1)S(1)}, bf16[2,2,128,2560]{3,2,1,0:T(8,128)(2,1)}, u32[]{:S(2)}) copy-start(bf16[2,2,128,2560]{3,2,1,0:T(8,128)(2,1)} %param.5) | copy-start | bytes 7864324
  46.9 7.1 %copy-start.11 = (bf16[512,256]{1,0:T(8,128)(2,1)}, bf16[512,256]{1,0:T(8,128)(2,1)S(1)}, u32[]{:S(2)}) copy-start(bf16[512,256]{1,0:T(8,128)(2,1)S(1)} %get-tuple-element.39.mixed_o) | copy-start | bytes 786436
  46.9 2.0 %collective-permute-start.6 = (bf16[512,256]{1,0:T(8,128)(2,1)S(1)}, bf16[512,256]{1,0:T(8,128)(2,1)S(1)}, u32[]{:S(2)}, u32[]{:S(2)}) collective-permute-start(bf16[512,256]{1,0:T(8,128)(2,1)S(1)} %get-tuple-element.40.mixed_s), channel_id=1, source_target_pairs={{0,4},{4,0},{8,12},{12,8},{16,20},{20,16},{24,28},{28,24},{1,5},{5... | collective-permute-start | bytes 786440 | tf_op jit(solution)/shard_map/ppermute | solution.py:304
  47.0 10.1 %collective-permute-start.10 = (bf16[2,320,256]{2,1,0:T(8,128)(2,1)S(1)}, bf16[2,320,256]{2,1,0:T(8,128)(2,1)S(1)}, u32[]{:S(2)}, u32[]{:S(2)}) collective-permute-start(bf16[2,320,256]{2,1,0:T(8,128)(2,1)S(1)} %collective-permute-done.9.rest_2_), channel_id=1, source_target_pairs={{0,8},{4,12},{8,0},{12,4},{16,24},{20,28},{24,16},{28,20},{1,9},{5... | collective-permute-start | bytes 983048 | tf_op jit(solution)/shard_map/ppermute | solution.py:296
  48.9 5.1 %copy-start.13 = (bf16[512,256]{1,0:T(8,128)(2,1)}, bf16[512,256]{1,0:T(8,128)(2,1)S(1)}, u32[]{:S(2)}) copy-start(bf16[512,256]{1,0:T(8,128)(2,1)S(1)} %collective-permute-done.6.rest_0_.mixed_r) | copy-start | bytes 786436
  54.0 0.7 copy-start.9
  54.7 9.4 %collective-permute-start.11 = (bf16[2,320,256]{2,1,0:T(8,128)(2,1)S(1)}, bf16[2,320,256]{2,1,0:T(8,128)(2,1)S(1)}, u32[]{:S(2)}, u32[]{:S(2)}) collective-permute-start(bf16[2,320,256]{2,1,0:T(8,128)(2,1)S(1)} %get-tuple-element.46), channel_id=1, source_target_pairs={{0,8},{4,12},{8,0},{12,4},{16,24},{20,28},{24,16},{28,20},{1,9},{5... | collective-permute-start | bytes 983048 | tf_op jit(solution)/shard_map/ppermute | solution.py:296
  62.3 1.1 copy-start.7
  64.9 1.0 copy-start.4
  64.9 3.6 %copy-start.12 = (bf16[512,256]{1,0:T(8,128)(2,1)S(1)}, bf16[512,256]{1,0:T(8,128)(2,1)}, u32[]{:S(2)}) copy-start(bf16[512,256]{1,0:T(8,128)(2,1)} %copy-done.11) | copy-start | bytes 786436
  64.9 3.6 %copy-start.14 = (bf16[512,256]{1,0:T(8,128)(2,1)S(1)}, bf16[512,256]{1,0:T(8,128)(2,1)}, u32[]{:S(2)}) copy-start(bf16[512,256]{1,0:T(8,128)(2,1)} %copy-done.13) | copy-start | bytes 786436
  64.9 3.5 %collective-permute-start.12 = (bf16[2560,256]{1,0:T(8,128)(2,1)}, bf16[2560,256]{1,0:T(8,128)(2,1)S(1)}, u32[]{:S(2)}, u32[]{:S(2)}) collective-permute-start(bf16[2560,256]{1,0:T(8,128)(2,1)} %in_order.1.w_o), channel_id=1, source_target_pairs={{0,4},{4,0},{8,12},{12,8},{16,20},{20,16},{24,28},{28,24},{1,5},{5... | collective-permute-start | bytes 3932168 | tf_op jit(solution)/shard_map/ppermute | solution.py:304
  65.0 10.2 %copy-start.2 = (bf16[2,2,128,2560]{3,2,1,0:T(8,128)(2,1)S(1)}, bf16[2,2,128,2560]{3,2,1,0:T(8,128)(2,1)}, u32[]{:S(2)}) copy-start(bf16[2,2,128,2560]{3,2,1,0:T(8,128)(2,1)} %param.5) | copy-start | bytes 7864324
  65.0 17.7 %collective-permute-start.18 = (bf16[2,320,256]{2,1,0:T(8,128)(2,1)}, bf16[2,320,256]{2,1,0:T(8,128)(2,1)S(1)}, u32[]{:S(2)}, u32[]{:S(2)}) collective-permute-start(bf16[2,320,256]{2,1,0:T(8,128)(2,1)} %get-tuple-element.57), channel_id=1, source_target_pairs={{0,8},{4,12},{8,0},{12,4},{16,24},{20,28},{24,16},{28,20},{1,9},{5... | collective-permute-start | bytes 983048 | tf_op jit(solution)/shard_map/ppermute | solution.py:296
  65.9 17.4 %collective-permute-start.19 = (bf16[2,320,256]{2,1,0:T(8,128)(2,1)S(1)}, bf16[2,320,256]{2,1,0:T(8,128)(2,1)S(1)}, u32[]{:S(2)}, u32[]{:S(2)}) collective-permute-start(bf16[2,320,256]{2,1,0:T(8,128)(2,1)S(1)} %copy-done.4), channel_id=1, source_target_pairs={{0,16},{4,20},{8,24},{12,28},{16,0},{20,4},{24,8},{28,12},{1,17},{... | collective-permute-start | bytes 983048 | tf_op jit(solution)/shard_map/ppermute | solution.py:296
  68.5 1.3 %copy-start.8 = (bf16[2560,256]{1,0:T(8,128)(2,1)S(1)}, bf16[2560,256]{1,0:T(8,128)(2,1)}, u32[]{:S(2)}) copy-start(bf16[2560,256]{1,0:T(8,128)(2,1)} %in_order.1.w_o) | copy-start | bytes 3932164
  72.2 21.4 %collective-permute-start.13 = (bf16[2,256,640]{2,1,0:T(8,128)(2,1)S(1)}, bf16[2,256,640]{2,1,0:T(8,128)(2,1)S(1)}, u32[]{:S(2)}, u32[]{:S(2)}) collective-permute-start(bf16[2,256,640]{2,1,0:T(8,128)(2,1)S(1)} %get-tuple-element.48), channel_id=1, source_target_pairs={{0,1},{1,0},{2,3},{3,2},{4,5},{5,4},{6,7},{7,6},{8,9},{9,8},{10,11... | collective-permute-start | bytes 1966088 | tf_op jit(solution)/shard_map/ppermute | solution.py:307
  73.7 20.0 %collective-permute-start.15 = (bf16[2,256,640]{2,1,0:T(8,128)(2,1)S(1)}, bf16[2,256,640]{2,1,0:T(8,128)(2,1)S(1)}, u32[]{:S(2)}, u32[]{:S(2)}) collective-permute-start(bf16[2,256,640]{2,1,0:T(8,128)(2,1)S(1)} %get-tuple-element.49), channel_id=1, source_target_pairs={{0,2},{1,3},{2,0},{3,1},{4,6},{5,7},{6,4},{7,5},{8,10},{9,11},{10,... | collective-permute-start | bytes 1966088 | tf_op jit(solution)/shard_map/ppermute | solution.py:307
  79.7 9.7 %collective-permute-start.17 = (bf16[2,320,256]{2,1,0:T(8,128)(2,1)S(1)}, bf16[2,320,256]{2,1,0:T(8,128)(2,1)S(1)}, u32[]{:S(2)}, u32[]{:S(2)}) collective-permute-start(bf16[2,320,256]{2,1,0:T(8,128)(2,1)S(1)} %get-tuple-element.54), channel_id=1, source_target_pairs={{0,8},{4,12},{8,0},{12,4},{16,24},{20,28},{24,16},{28,20},{1,9},{5... | collective-permute-start | bytes 983048 | tf_op jit(solution)/shard_map/ppermute | solution.py:296
  80.6 8.8 %copy-start.10 = (bf16[2,320,256]{2,1,0:T(8,128)(2,1)S(1)}, bf16[2,320,256]{2,1,0:T(8,128)(2,1)}, u32[]{:S(2)}) copy-start(bf16[2,320,256]{2,1,0:T(8,128)(2,1)} %copy-done.9) | copy-start | bytes 983044
  89.6 15.6 %collective-permute-start.20 = (bf16[2,320,256]{2,1,0:T(8,128)(2,1)S(1)}, bf16[2,320,256]{2,1,0:T(8,128)(2,1)S(1)}, u32[]{:S(2)}, u32[]{:S(2)}) collective-permute-start(bf16[2,320,256]{2,1,0:T(8,128)(2,1)S(1)} %get-tuple-element.58), channel_id=1, source_target_pairs={{0,8},{4,12},{8,0},{12,4},{16,24},{20,28},{24,16},{28,20},{1,9},{5... | collective-permute-start | bytes 983048 | tf_op jit(solution)/shard_map/ppermute | solution.py:296
  90.3 17.3 %collective-permute-start.21 = (bf16[2,320,256]{2,1,0:T(8,128)(2,1)S(1)}, bf16[2,320,256]{2,1,0:T(8,128)(2,1)S(1)}, u32[]{:S(2)}, u32[]{:S(2)}) collective-permute-start(bf16[2,320,256]{2,1,0:T(8,128)(2,1)S(1)} %get-tuple-element.59), channel_id=1, source_target_pairs={{0,16},{4,20},{8,24},{12,28},{16,0},{20,4},{24,8},{28,12},{1,17},{... | collective-permute-start | bytes 983048 | tf_op jit(solution)/shard_map/ppermute | solution.py:296
  93.5 14.4 %collective-permute-start.23 = (f32[320,256]{1,0:T(8,128)S(1)}, f32[320,256]{1,0:T(8,128)S(1)}, u32[]{:S(2)}, u32[]{:S(2)}) collective-permute-start(f32[320,256]{1,0:T(8,128)S(1)} %slice_bitcast_fusion.2), channel_id=1, source_target_pairs={{0,4},{4,0},{8,12},{12,8},{16,20},{20,16},{24,28},{28,24},{1,5},{5... | collective-permute-start | bytes 983048 | tf_op jit(solution)/shard_map/ppermute | solution.py:304
  94.0 14.9 %collective-permute-start.14 = (bf16[256,640]{1,0:T(8,128)(2,1)S(1)}, bf16[256,640]{1,0:T(8,128)(2,1)S(1)}, u32[]{:S(2)}, u32[]{:S(2)}) collective-permute-start(bf16[256,640]{1,0:T(8,128)(2,1)S(1)} %get-tuple-element.63), channel_id=1, source_target_pairs={{0,2},{1,3},{2,0},{3,1},{4,6},{5,7},{6,4},{7,5},{8,10},{9,11},{10,... | collective-permute-start | bytes 983048 | tf_op jit(solution)/shard_map/ppermute | solution.py:307
  95.2 13.7 %collective-permute-start.16 = (bf16[256,640]{1,0:T(8,128)(2,1)S(1)}, bf16[256,640]{1,0:T(8,128)(2,1)S(1)}, u32[]{:S(2)}, u32[]{:S(2)}) collective-permute-start(bf16[256,640]{1,0:T(8,128)(2,1)S(1)} %get-tuple-element.64), channel_id=1, source_target_pairs={{0,1},{1,0},{2,3},{3,2},{4,5},{5,4},{6,7},{7,6},{8,9},{9,8},{10,11... | collective-permute-start | bytes 983048 | tf_op jit(solution)/shard_map/ppermute | solution.py:307
  107.8 2.2 %collective-permute-start.22 = (f32[320,256]{1,0:T(8,128)S(1)}, f32[320,256]{1,0:T(8,128)S(1)}, u32[]{:S(2)}, u32[]{:S(2)}) collective-permute-start(f32[320,256]{1,0:T(8,128)S(1)} %slice_bitcast_fusion), channel_id=1, source_target_pairs={{0,4},{4,0},{8,12},{12,8},{16,20},{20,16},{24,28},{28,24},{1,5},{5... | collective-permute-start | bytes 983048 | tf_op jit(solution)/shard_map/ppermute | solution.py:304

commit v24 on v23

--- a/solution.py
+++ b/solution.py
@@ -272,20 +272,6 @@
         compiler_params=pltpu.CompilerParams(vmem_limit_bytes=vmem << 20),
         cost_estimate=pl.CostEstimate(flops=flops, bytes_accessed=size, transcendentals=0),
     )
-
-
-def in_order(x, earlier):
-    def kernel(*refs):
-        del refs
-
-    return pl.pallas_call(
-        kernel,
-        name="in_order",
-        in_specs=[ANY, ANY],
-        out_specs=ANY,
-        out_shape=jax.ShapeDtypeStruct(x.shape, x.dtype),
-        input_output_aliases={0: 0},
-    )(x, earlier)
 
 
 def make_body(n_wide, n_node):
@@ -453,7 +439,9 @@
             out_near = swap(out_sends[1], 1)
         else:
             out_onward = left
-        w_full = in_order(w_full, out_onward)
+        w_full = call(relay_kernel, "order", [ANY, VMEM], [(width, cols)], [], 0, vmem=8)(
+            out_onward, w_full
+        )[0]
         w_full_s = sibling(w_full)
         part = width // n_node
         half = tokens // 2

time: 111 us -> 110 us (level)
  waiting for transfers between devices: 46.5 us -> 50.3 us
  local copies, waits for them, and re-layouts: 7.34 us -> 4.74 us
  starting transfers between devices: 26 us -> 24.8 us
    ppermute x12, waiting for transfers between devices: 45.2 us -> 48.9 us  [move(): lax.ppermute(x, 'wide', [(2 * s + c, 2 * d + c) for s, d in pairs for c i...]
    unnamed x30 -> x26, local copies, waits for them, and re-layouts: 5.82 us -> 3.22 us
    ppermute x12, starting transfers between devices: 18.6 us -> 17 us  [move(): lax.ppermute(x, 'wide', [(2 * s + c, 2 * d + c) for s, d in pairs for c i...]
where the time goes in v24:
time: 110 us
  waiting for transfers between devices  50.3 us (46%)
  Pallas kernels  24.9 us (23%)
  starting transfers between devices  24.8 us (23%)
  local copies, waits for them, and re-layouts  4.74 us (4%)
  other arithmetic  4.06 us (4%)
    ppermute x12, waiting for transfers between devices, move(): lax.ppermute(x, 'wide', [(2 * s + c, 2 * d + c) for s, d in pairs for c i...  48.9 us
    ppermute x12, starting transfers between devices, move(): lax.ppermute(x, 'wide', [(2 * s + c, 2 * d + c) for s, d in pairs for c i...  17 us
    ppermute x4, starting transfers between devices, flip(): return lax.ppermute(x, 'node', [(i, i ^ j) for i in range(n_node)])  6.15 us
    pallas_call x1, Pallas kernels, body(): call(functools.partial(d_value_kernel, n_slots), 'd_value', [SMEM] + [ANY...  5.21 us
    pallas_call x1, Pallas kernels, body(): call(functools.partial(part_kernel, n_slots - 1), 'value_ahead', [SMEM] +...  4.9 us
    pallas_call x1, Pallas kernels, body(): call(functools.partial(grad_out_kernel, len(unread)), 'grad_out', [SMEM]...  4.4 us
    pallas_call x1, Pallas kernels, body(): call(gradient_kernel, 'grad_value', [SMEM] + [ANY] * 4 + [VMEM], send_sha...  4.39 us
    unnamed x26, local copies, waits for them, and re-layouts  3.22 us
  transfers between devices with their start and end apart: 24, of which 12 were waited for; matrix products, arithmetic and copies ran while one was open for 3% of the time, Pallas kernels for 23%

profile of v24, /device:TPU:0, one launch (start us, length us, event | category | flops | bytes accessed | tf_op | source)
XLA Modules:
  0.0 109.8 jit_solution(4458031374658030848)
XLA Ops:
  0.7 1.3 %slice_bitcast_fusion.5 = (bf16[1,320,256]{2,1,0:T(8,128)(2,1)S(1)}, bf16[1,320,256]{2,1,0:T(8,128)(2,1)S(1)}, bf16[1,320,256]{2,1,0:T(8,128)(2,1)S(1)}, bf16[1,320,256]{2,1,0:T(8,128)(2,1)S(1)}) fusion(bf16[320,512]{1,0:T(8,128)(2,1)} %param.8, bf16[320,512]{1,0:T(8,128)(2,1)} %param.9), kind=kLoop, calls=%fused_computation.34 | loop fusion | bytes 1310720 | tf_op jit(solution)/shard_map/stack | solution.py:298
  2.0 0.1 broadcast_select_fusion
  2.1 0.5 collective-permute-start
  2.6 1.3 %collective-permute-done = bf16[2,320,256]{2,1,0:T(8,128)(2,1)S(1)} collective-permute-done((bf16[2,320,256]{2,1,0:T(8,128)(2,1)S(1)}, bf16[2,320,256]{2,1,0:T(8,128)(2,1)S(1)}, u32[]{:S(2)}, u32[]{:S(2)}) %collective-permute-start) | collective-permute-done | bytes 327712 | tf_op jit(solution)/shard_map/ppermute | solution.py:290
  3.8 0.4 collective-permute-start.1
  4.2 0.1 collective-permute-start.7
  4.4 0.4 collective-permute-start.2
  4.8 2.8 %collective-permute-start.3 = (bf16[2,320,256]{2,1,0:T(8,128)(2,1)S(1)}, bf16[2,320,256]{2,1,0:T(8,128)(2,1)S(1)}, u32[]{:S(2)}, u32[]{:S(2)}) collective-permute-start(bf16[2,320,256]{2,1,0:T(8,128)(2,1)S(1)} %pad_maximum_fusion.5.rest_0_), channel_id=1, source_target_pairs={{0,8},{4,12},{8,0},{12,4},{16,24},{20,28},{24,16},{28,20},{1,9},{5... | collective-permute-start | bytes 983048 | tf_op jit(solution)/shard_map/ppermute | solution.py:282
  7.6 2.6 %collective-permute-start.4 = (bf16[2,320,256]{2,1,0:T(8,128)(2,1)S(1)}, bf16[2,320,256]{2,1,0:T(8,128)(2,1)S(1)}, u32[]{:S(2)}, u32[]{:S(2)}) collective-permute-start(bf16[2,320,256]{2,1,0:T(8,128)(2,1)S(1)} %pad_maximum_fusion.5.rest_0_), channel_id=1, source_target_pairs={{0,16},{4,20},{8,24},{12,28},{16,0},{20,4},{24,8},{28,12},{1,17},{... | collective-permute-start | bytes 983048 | tf_op jit(solution)/shard_map/ppermute | solution.py:282
  10.2 12.5 %collective-permute-done.3.unread.rest_1_ = bf16[2,320,256]{2,1,0:T(8,128)(2,1)S(1)} collective-permute-done((bf16[2,320,256]{2,1,0:T(8,128)(2,1)S(1)}, bf16[2,320,256]{2,1,0:T(8,128)(2,1)S(1)}, u32[]{:S(2)}, u32[]{:S(2)}) %collective-permute-start.3) | collective-permute-done | bytes 327712 | tf_op jit(solution)/shard_map/ppermute | solution.py:282
  22.8 2.5 %collective-permute-done.4.refs_0_ = bf16[2,320,256]{2,1,0:T(8,128)(2,1)S(1)} collective-permute-done((bf16[2,320,256]{2,1,0:T(8,128)(2,1)S(1)}, bf16[2,320,256]{2,1,0:T(8,128)(2,1)S(1)}, u32[]{:S(2)}, u32[]{:S(2)}) %collective-permute-start.4) | collective-permute-done | bytes 327712 | tf_op jit(solution)/shard_map/ppermute | solution.py:282
  25.3 0.8 relay.1
  26.1 0.7 copy-done.4
  26.8 0.4 collective-permute-start.5
  27.2 0.1 stack.67.idx
  27.3 2.6 %collective-permute-start.9 = (bf16[2,320,256]{2,1,0:T(8,128)(2,1)S(1)}, bf16[2,320,256]{2,1,0:T(8,128)(2,1)S(1)}, u32[]{:S(2)}, u32[]{:S(2)}) collective-permute-start(bf16[2,320,256]{2,1,0:T(8,128)(2,1)S(1)} %get-tuple-element.42.refs_0_.rest_0_), channel_id=1, source_target_pairs={{0,16},{4,20},{8,24},{12,28},{16,0},{20,4},{24,8},{28,12},{1,17},{... | collective-permute-start | bytes 983048 | tf_op jit(solution)/shard_map/ppermute | solution.py:282
  30.0 0.1 collective-permute-start.8
  30.1 0.0 copy-start.1
  30.1 1.7 %copy-done.1 = bf16[2,2,128,2560]{3,2,1,0:T(8,128)(2,1)S(1)} copy-done((bf16[2,2,128,2560]{3,2,1,0:T(8,128)(2,1)S(1)}, bf16[2,2,128,2560]{3,2,1,0:T(8,128)(2,1)}, u32[]{:S(2)}) %copy-start.1) | copy-done | bytes 2621464
  31.8 4.9 %value_ahead.1 = (f32[2,512,256]{2,1,0:T(8,128)S(1)}, bf16[2,512,640]{2,1,0:T(8,128)(2,1)S(1)}, bf16[2,4,4,128,128]{4,3,2,1,0:T(8,128)(2,1)S(1)}) custom-call(s32[5]{0:T(128)S(1)} %stack.67.idx, bf16[512,2560]{1,0:T(8,128)(2,1)S(1)} %bitcast.54, bf16[512,2560]{1,0:T(8,128)(2,1)} %collective-permute-done.1.x_s.right_s, bf16[4,8,128,128]{3,2,1,0:T(8,128)(2,1)S(1)} %bitcast.57, ...), custom_call_target="tpu_custom_call" | custom-call | flops 1342177280 | bytes 11272192 | tf_op jit(solution)/shard_map/value_ahead/pallas_call | solution.py:382
  36.7 7.7 %collective-permute-done.5.slot = bf16[2,320,256]{2,1,0:T(8,128)(2,1)} collective-permute-done((bf16[2,320,256]{2,1,0:T(8,128)(2,1)}, bf16[2,320,256]{2,1,0:T(8,128)(2,1)}, u32[]{:S(2)}, u32[]{:S(2)}) %collective-permute-start.5) | collective-permute-done | bytes 327712 | tf_op jit(solution)/shard_map/ppermute | solution.py:282
  44.4 2.5 %mixed.1 = (bf16[512,256]{1,0:T(8,128)(2,1)S(1)}, bf16[512,256]{1,0:T(8,128)(2,1)S(1)}) custom-call(s32[5]{0:T(128)S(1)} %stack.67.idx, f32[2,512,256]{2,1,0:T(8,128)S(1)} %get-tuple-element.36.part, bf16[2,512,640]{2,1,0:T(8,128)(2,1)S(1)} %get-tuple-element.37.last, bf16[2,4,4,128,128]{4,3,2,1,0:T(8,128)(2,1)S(1)} %get-tuple-element.38.weights, ...), custom_call_target="tpu_custom_call" | custom-call | flops 335544320 | bytes 3932160 | tf_op jit(solution)/shard_map/mixed/pallas_call | solution.py:395
  46.9 0.1 collective-permute-start.6
  47.0 0.1 collective-permute-start.11
  47.1 1.8 %collective-permute-done.8.rest_1_ = bf16[2,320,256]{2,1,0:T(8,128)(2,1)S(1)} collective-permute-done((bf16[2,320,256]{2,1,0:T(8,128)(2,1)S(1)}, bf16[2,320,256]{2,1,0:T(8,128)(2,1)S(1)}, u32[]{:S(2)}, u32[]{:S(2)}) %collective-permute-start.8) | collective-permute-done | bytes 327712 | tf_op jit(solution)/shard_map/ppermute | solution.py:282
  48.9 4.4 %grad_out.1 = (bf16[16,128]{1,0:T(8,128)(2,1)S(1)}, bf16[2,320,256]{2,1,0:T(8,128)(2,1)S(1)}, bf16[2,320,256]{2,1,0:T(8,128)(2,1)S(1)}, bf16[2,320,256]{2,1,0:T(8,128)(2,1)S(1)}, bf16[2,320,256]{2,1,0:T(8,128)(2,1)S(1)}) custom-call(s32[5]{0:T(128)S(1)} %stack.67.idx, bf16[512,2560]{1,0:T(8,128)(2,1)S(1)} %bitcast.51, ...), custom_call_target="tpu_custom_call" | custom-call | flops 1342177280 | bytes 7077888 | tf_op jit(solution)/shard_map/grad_out/pallas_call | solution.py:417
  53.3 0.7 copy-done.8
  54.0 2.0 %collective-permute-start.10 = (bf16[2,320,256]{2,1,0:T(8,128)(2,1)S(1)}, bf16[2,320,256]{2,1,0:T(8,128)(2,1)S(1)}, u32[]{:S(2)}, u32[]{:S(2)}) collective-permute-start(bf16[2,320,256]{2,1,0:T(8,128)(2,1)S(1)} %get-tuple-element.44), channel_id=1, source_target_pairs={{0,8},{4,12},{8,0},{12,4},{16,24},{20,28},{24,16},{28,20},{1,9},{5... | collective-permute-start | bytes 983048 | tf_op jit(solution)/shard_map/ppermute | solution.py:282
  56.0 1.5 %collective-permute-done.11.rest_3_ = bf16[2,320,256]{2,1,0:T(8,128)(2,1)S(1)} collective-permute-done((bf16[2,320,256]{2,1,0:T(8,128)(2,1)S(1)}, bf16[2,320,256]{2,1,0:T(8,128)(2,1)S(1)}, u32[]{:S(2)}, u32[]{:S(2)}) %collective-permute-start.11) | collective-permute-done | bytes 327712 | tf_op jit(solution)/shard_map/ppermute | solution.py:282
  57.6 5.2 %d_value.1 = (bf16[256,1024]{1,0:T(8,128)(2,1)S(1)}, bf16[2560,256]{1,0:T(8,128)(2,1)S(1)}) custom-call(s32[5]{0:T(128)S(1)} %stack.67.idx, bf16[16,128]{1,0:T(8,128)(2,1)S(1)} %get-tuple-element.45.token, bf16[512,2560]{1,0:T(8,128)(2,1)S(1)} %bitcast.52, bf16[512,2560]{1,0:T(8,128)(2,1)} %collective-permute-done.7.cot_s, ...), custom_call_target="tpu_custom_call" | custom-call | flops 1342177280 | bytes 9437184 | tf_op jit(solution)/shard_map/d_value/pallas_call | solution.py:427
  62.8 0.0 copy-start.6
  62.8 1.3 %collective-permute-done.10 = bf16[2,320,256]{2,1,0:T(8,128)(2,1)S(1)} collective-permute-done((bf16[2,320,256]{2,1,0:T(8,128)(2,1)S(1)}, bf16[2,320,256]{2,1,0:T(8,128)(2,1)S(1)}, u32[]{:S(2)}, u32[]{:S(2)}) %collective-permute-start.10) | collective-permute-done | bytes 327712 | tf_op jit(solution)/shard_map/ppermute | solution.py:282
  64.1 0.1 add_convert_fusion.unread
  64.2 0.1 order.1.w_o
  64.3 0.1 collective-permute-start.12
  64.4 0.1 pad_add_fusion.idx
  64.5 0.6 collective-permute-start.18
  65.1 2.3 %collective-permute-start.19 = (bf16[2,320,256]{2,1,0:T(8,128)(2,1)S(1)}, bf16[2,320,256]{2,1,0:T(8,128)(2,1)S(1)}, u32[]{:S(2)}, u32[]{:S(2)}) collective-permute-start(bf16[2,320,256]{2,1,0:T(8,128)(2,1)S(1)} %add_convert_fusion.unread), channel_id=1, source_target_pairs={{0,16},{4,20},{8,24},{12,28},{16,0},{20,4},{24,8},{28,12},{1,17},{... | collective-permute-start | bytes 983048 | tf_op jit(solution)/shard_map/ppermute | solution.py:282
  67.4 0.1 collective-permute-done.12.w_r
  67.4 2.4 %terms.1 = (bf16[16,128]{1,0:T(8,128)(2,1)S(1)}, bf16[2,256,640]{2,1,0:T(8,128)(2,1)S(1)}, bf16[2,256,640]{2,1,0:T(8,128)(2,1)S(1)}, bf16[4,256,640]{2,1,0:T(8,128)(2,1)S(1)}) custom-call(s32[4]{0:T(128)S(1)} %pad_add_fusion.idx, bf16[512,256]{1,0:T(8,128)(2,1)S(1)} %get-tuple-element.39.mixed_o, bf16[512,256]{1,0:T(8,128)(2,1)S(1)} %copy-done.11, ...), custom_call_target="tpu_custom_call" | custom-call | flops 1342177280 | bytes 5767168 | tf_op jit(solution)/shard_map/terms/pallas_call | solution.py:452
  69.8 1.6 %collective-permute-start.13 = (bf16[2,256,640]{2,1,0:T(8,128)(2,1)S(1)}, bf16[2,256,640]{2,1,0:T(8,128)(2,1)S(1)}, u32[]{:S(2)}, u32[]{:S(2)}) collective-permute-start(bf16[2,256,640]{2,1,0:T(8,128)(2,1)S(1)} %get-tuple-element.48), channel_id=1, source_target_pairs={{0,1},{1,0},{2,3},{3,2},{4,5},{5,4},{6,7},{7,6},{8,9},{9,8},{10,11... | collective-permute-start | bytes 1966088 | tf_op jit(solution)/shard_map/ppermute | solution.py:293
  71.4 1.5 %collective-permute-start.15 = (bf16[2,256,640]{2,1,0:T(8,128)(2,1)S(1)}, bf16[2,256,640]{2,1,0:T(8,128)(2,1)S(1)}, u32[]{:S(2)}, u32[]{:S(2)}) collective-permute-start(bf16[2,256,640]{2,1,0:T(8,128)(2,1)S(1)} %get-tuple-element.49), channel_id=1, source_target_pairs={{0,2},{1,3},{2,0},{3,1},{4,6},{5,7},{6,4},{7,5},{8,10},{9,11},{10,... | collective-permute-start | bytes 1966088 | tf_op jit(solution)/shard_map/ppermute | solution.py:293
  72.9 4.4 %grad_value.1 = (bf16[2,320,256]{2,1,0:T(8,128)(2,1)S(1)}, bf16[2,320,256]{2,1,0:T(8,128)(2,1)S(1)}, bf16[2,320,256]{2,1,0:T(8,128)(2,1)S(1)}, bf16[2,320,256]{2,1,0:T(8,128)(2,1)S(1)}) custom-call(s32[5]{0:T(128)S(1)} %stack.67.idx, bf16[16,128]{1,0:T(8,128)(2,1)S(1)} %get-tuple-element.50.token, bf16[2,320,256]{2,1,0:T(8,128)(2,1)S(1)} %add_convert_fusion.unread, ...), custom_call_target="tpu_custom_call" | custom-call | flops 1342177280 | bytes 7077888 | tf_op jit(solution)/shard_map/grad_value/pallas_call | solution.py:461
  77.3 0.6 collective-permute-start.17
  77.9 0.2 convert_element_type.53
  78.1 3.8 %collective-permute-done.18.near = bf16[2,320,256]{2,1,0:T(8,128)(2,1)S(1)} collective-permute-done((bf16[2,320,256]{2,1,0:T(8,128)(2,1)}, bf16[2,320,256]{2,1,0:T(8,128)(2,1)S(1)}, u32[]{:S(2)}, u32[]{:S(2)}) %collective-permute-start.18) | collective-permute-done | bytes 327712 | tf_op jit(solution)/shard_map/ppermute | solution.py:282
  81.9 0.9 collective-permute-done.19.far
  82.9 6.0 %collective-permute-done.17.got = bf16[2,320,256]{2,1,0:T(8,128)(2,1)S(1)} collective-permute-done((bf16[2,320,256]{2,1,0:T(8,128)(2,1)S(1)}, bf16[2,320,256]{2,1,0:T(8,128)(2,1)S(1)}, u32[]{:S(2)}, u32[]{:S(2)}) %collective-permute-start.17) | collective-permute-done | bytes 327712 | tf_op jit(solution)/shard_map/ppermute | solution.py:282
  88.9 0.2 sum.1
  89.1 1.3 %collective-permute-start.21 = (bf16[2,320,256]{2,1,0:T(8,128)(2,1)S(1)}, bf16[2,320,256]{2,1,0:T(8,128)(2,1)S(1)}, u32[]{:S(2)}, u32[]{:S(2)}) collective-permute-start(bf16[2,320,256]{2,1,0:T(8,128)(2,1)S(1)} %get-tuple-element.59), channel_id=1, source_target_pairs={{0,16},{4,20},{8,24},{12,28},{16,0},{20,4},{24,8},{28,12},{1,17},{... | collective-permute-start | bytes 983048 | tf_op jit(solution)/shard_map/ppermute | solution.py:282
  90.3 1.7 %collective-permute-start.20 = (bf16[2,320,256]{2,1,0:T(8,128)(2,1)S(1)}, bf16[2,320,256]{2,1,0:T(8,128)(2,1)S(1)}, u32[]{:S(2)}, u32[]{:S(2)}) collective-permute-start(bf16[2,320,256]{2,1,0:T(8,128)(2,1)S(1)} %get-tuple-element.58), channel_id=1, source_target_pairs={{0,8},{4,12},{8,0},{12,4},{16,24},{20,28},{24,16},{28,20},{1,9},{5... | collective-permute-start | bytes 983048 | tf_op jit(solution)/shard_map/ppermute | solution.py:282
  92.0 0.1 collective-permute-start.23
  92.1 0.1 convert_element_type.54
  92.2 0.1 convert_element_type.58
  92.3 0.2 fusion.8
  92.5 1.6 %collective-permute-start.14 = (bf16[256,640]{1,0:T(8,128)(2,1)S(1)}, bf16[256,640]{1,0:T(8,128)(2,1)S(1)}, u32[]{:S(2)}, u32[]{:S(2)}) collective-permute-start(bf16[256,640]{1,0:T(8,128)(2,1)S(1)} %get-tuple-element.63), channel_id=1, source_target_pairs={{0,2},{1,3},{2,0},{3,1},{4,6},{5,7},{6,4},{7,5},{8,10},{9,11},{10,... | collective-permute-start | bytes 983048 | tf_op jit(solution)/shard_map/ppermute | solution.py:293
  94.1 1.5 %collective-permute-start.16 = (bf16[256,640]{1,0:T(8,128)(2,1)S(1)}, bf16[256,640]{1,0:T(8,128)(2,1)S(1)}, u32[]{:S(2)}, u32[]{:S(2)}) collective-permute-start(bf16[256,640]{1,0:T(8,128)(2,1)S(1)} %get-tuple-element.64), channel_id=1, source_target_pairs={{0,1},{1,0},{2,3},{3,2},{4,5},{5,4},{6,7},{7,6},{8,9},{9,8},{10,11... | collective-permute-start | bytes 983048 | tf_op jit(solution)/shard_map/ppermute | solution.py:293
  95.6 10.8 %collective-permute-done.21 = bf16[2,320,256]{2,1,0:T(8,128)(2,1)S(1)} collective-permute-done((bf16[2,320,256]{2,1,0:T(8,128)(2,1)S(1)}, bf16[2,320,256]{2,1,0:T(8,128)(2,1)S(1)}, u32[]{:S(2)}, u32[]{:S(2)}) %collective-permute-start.21) | collective-permute-done | bytes 327712 | tf_op jit(solution)/shard_map/ppermute | solution.py:282
  106.4 0.1 convert_add_fusion
  106.5 0.1 collective-permute-start.22
  106.7 0.9 pad_maximum_fusion.2
  107.6 0.3 fusion.7
  107.9 0.9 pad_maximum_fusion
  108.8 0.9 pad_maximum_fusion.1
  (42 shorter events, 0.3 us)
Async XLA Ops:
  0.6 3.6 %copy-start = (bf16[2,2,128,2560]{3,2,1,0:T(8,128)(2,1)S(1)}, bf16[2,2,128,2560]{3,2,1,0:T(8,128)(2,1)}, u32[]{:S(2)}) copy-start(bf16[2,2,128,2560]{3,2,1,0:T(8,128)(2,1)} %param.7) | copy-start | bytes 7864324
  2.1 1.8 %collective-permute-start = (bf16[2,320,256]{2,1,0:T(8,128)(2,1)S(1)}, bf16[2,320,256]{2,1,0:T(8,128)(2,1)S(1)}, u32[]{:S(2)}, u32[]{:S(2)}) collective-permute-start(bf16[2,320,256]{2,1,0:T(8,128)(2,1)S(1)} %get-tuple-element.70), channel_id=1, source_target_pairs={{0,4},{4,0},{8,12},{12,8},{16,20},{20,16},{24,28},{28,24},{1,5},{5... | collective-permute-start | bytes 983048 | tf_op jit(solution)/shard_map/ppermute | solution.py:290
  3.8 26.2 %collective-permute-start.1 = (bf16[512,2560]{1,0:T(8,128)(2,1)}, bf16[512,2560]{1,0:T(8,128)(2,1)}, u32[]{:S(2)}, u32[]{:S(2)}) collective-permute-start(bf16[512,2560]{1,0:T(8,128)(2,1)} %bitcast.53), channel_id=1, source_target_pairs={{0,4},{4,0},{8,12},{12,8},{16,20},{20,16},{24,28},{28,24},{1,5},{5... | collective-permute-start | bytes 7864328 | tf_op jit(solution)/shard_map/ppermute | solution.py:290
  4.2 44.6 %collective-permute-start.7 = (bf16[512,2560]{1,0:T(8,128)(2,1)S(1)}, bf16[512,2560]{1,0:T(8,128)(2,1)}, u32[]{:S(2)}, u32[]{:S(2)}) collective-permute-start(bf16[512,2560]{1,0:T(8,128)(2,1)S(1)} %bitcast.50), channel_id=1, source_target_pairs={{0,4},{4,0},{8,12},{12,8},{16,20},{20,16},{24,28},{28,24},{1,5},{5... | collective-permute-start | bytes 7864328 | tf_op jit(solution)/shard_map/ppermute | solution.py:290
  4.4 25.6 %collective-permute-start.2 = (bf16[4,8,128,128]{3,2,1,0:T(8,128)(2,1)}, bf16[4,8,128,128]{3,2,1,0:T(8,128)(2,1)}, u32[]{:S(2)}, u32[]{:S(2)}) collective-permute-start(bf16[4,8,128,128]{3,2,1,0:T(8,128)(2,1)} %bitcast.56), channel_id=1, source_target_pairs={{0,4},{4,0},{8,12},{12,8},{16,20},{20,16},{24,28},{28,24},{1,5},{5... | collective-permute-start | bytes 3145736 | tf_op jit(solution)/shard_map/ppermute | solution.py:290
  4.8 17.9 %collective-permute-start.3 = (bf16[2,320,256]{2,1,0:T(8,128)(2,1)S(1)}, bf16[2,320,256]{2,1,0:T(8,128)(2,1)S(1)}, u32[]{:S(2)}, u32[]{:S(2)}) collective-permute-start(bf16[2,320,256]{2,1,0:T(8,128)(2,1)S(1)} %pad_maximum_fusion.5.rest_0_), channel_id=1, source_target_pairs={{0,8},{4,12},{8,0},{12,4},{16,24},{20,28},{24,16},{28,20},{1,9},{5... | collective-permute-start | bytes 983048 | tf_op jit(solution)/shard_map/ppermute | solution.py:282
  7.6 17.7 %collective-permute-start.4 = (bf16[2,320,256]{2,1,0:T(8,128)(2,1)S(1)}, bf16[2,320,256]{2,1,0:T(8,128)(2,1)S(1)}, u32[]{:S(2)}, u32[]{:S(2)}) collective-permute-start(bf16[2,320,256]{2,1,0:T(8,128)(2,1)S(1)} %pad_maximum_fusion.5.rest_0_), channel_id=1, source_target_pairs={{0,16},{4,20},{8,24},{12,28},{16,0},{20,4},{24,8},{28,12},{1,17},{... | collective-permute-start | bytes 983048 | tf_op jit(solution)/shard_map/ppermute | solution.py:282
  26.1 0.7 copy-start.4
  26.8 17.6 %collective-permute-start.5 = (bf16[2,320,256]{2,1,0:T(8,128)(2,1)}, bf16[2,320,256]{2,1,0:T(8,128)(2,1)}, u32[]{:S(2)}, u32[]{:S(2)}) collective-permute-start(bf16[2,320,256]{2,1,0:T(8,128)(2,1)} %get-tuple-element.35.rest_2_), channel_id=1, source_target_pairs={{0,8},{4,12},{8,0},{12,4},{16,24},{20,28},{24,16},{28,20},{1,9},{5... | collective-permute-start | bytes 983048 | tf_op jit(solution)/shard_map/ppermute | solution.py:282
  27.3 2.7 %copy-start.3 = (bf16[2,2,8,128,128]{4,3,2,1,0:T(8,128)(2,1)S(1)}, bf16[2,2,8,128,128]{4,3,2,1,0:T(8,128)(2,1)}, u32[]{:S(2)}) copy-start(bf16[2,2,8,128,128]{4,3,2,1,0:T(8,128)(2,1)} %param.6) | copy-start | bytes 3145732
  27.3 2.8 %copy-start.5 = (bf16[2,320,256]{2,1,0:T(8,128)(2,1)S(1)}, bf16[2,320,256]{2,1,0:T(8,128)(2,1)}, u32[]{:S(2)}) copy-start(bf16[2,320,256]{2,1,0:T(8,128)(2,1)} %copy-done.4) | copy-start | bytes 983044
  27.3 19.7 %collective-permute-start.9 = (bf16[2,320,256]{2,1,0:T(8,128)(2,1)S(1)}, bf16[2,320,256]{2,1,0:T(8,128)(2,1)S(1)}, u32[]{:S(2)}, u32[]{:S(2)}) collective-permute-start(bf16[2,320,256]{2,1,0:T(8,128)(2,1)S(1)} %get-tuple-element.42.refs_0_.rest_0_), channel_id=1, source_target_pairs={{0,16},{4,20},{8,24},{12,28},{16,0},{20,4},{24,8},{28,12},{1,17},{... | collective-permute-start | bytes 983048 | tf_op jit(solution)/shard_map/ppermute | solution.py:282
  30.0 18.9 %collective-permute-start.8 = (bf16[2,320,256]{2,1,0:T(8,128)(2,1)S(1)}, bf16[2,320,256]{2,1,0:T(8,128)(2,1)S(1)}, u32[]{:S(2)}, u32[]{:S(2)}) collective-permute-start(bf16[2,320,256]{2,1,0:T(8,128)(2,1)S(1)} %again.1), channel_id=1, source_target_pairs={{0,8},{4,12},{8,0},{12,4},{16,24},{20,28},{24,16},{28,20},{1,9},{5... | collective-permute-start | bytes 983048 | tf_op jit(solution)/shard_map/ppermute | solution.py:282
  30.1 1.7 %copy-start.1 = (bf16[2,2,128,2560]{3,2,1,0:T(8,128)(2,1)S(1)}, bf16[2,2,128,2560]{3,2,1,0:T(8,128)(2,1)}, u32[]{:S(2)}) copy-start(bf16[2,2,128,2560]{3,2,1,0:T(8,128)(2,1)} %param.5) | copy-start | bytes 7864324
  46.9 2.0 %collective-permute-start.6 = (bf16[512,256]{1,0:T(8,128)(2,1)S(1)}, bf16[512,256]{1,0:T(8,128)(2,1)S(1)}, u32[]{:S(2)}, u32[]{:S(2)}) collective-permute-start(bf16[512,256]{1,0:T(8,128)(2,1)S(1)} %get-tuple-element.40.mixed_s), channel_id=1, source_target_pairs={{0,4},{4,0},{8,12},{12,8},{16,20},{20,16},{24,28},{28,24},{1,5},{5... | collective-permute-start | bytes 786440 | tf_op jit(solution)/shard_map/ppermute | solution.py:290
  47.0 10.6 %collective-permute-start.11 = (bf16[2,320,256]{2,1,0:T(8,128)(2,1)S(1)}, bf16[2,320,256]{2,1,0:T(8,128)(2,1)S(1)}, u32[]{:S(2)}, u32[]{:S(2)}) collective-permute-start(bf16[2,320,256]{2,1,0:T(8,128)(2,1)S(1)} %collective-permute-done.9.rest_2_), channel_id=1, source_target_pairs={{0,8},{4,12},{8,0},{12,4},{16,24},{20,28},{24,16},{28,20},{1,9},{5... | collective-permute-start | bytes 983048 | tf_op jit(solution)/shard_map/ppermute | solution.py:282
  48.9 4.4 %copy-start.10 = (bf16[512,256]{1,0:T(8,128)(2,1)}, bf16[512,256]{1,0:T(8,128)(2,1)S(1)}, u32[]{:S(2)}) copy-start(bf16[512,256]{1,0:T(8,128)(2,1)S(1)} %collective-permute-done.6.rest_0_.mixed_r) | copy-start | bytes 786436
  53.3 0.7 copy-start.8
  54.0 3.6 %copy-start.12 = (bf16[2,320,256]{2,1,0:T(8,128)(2,1)}, bf16[2,320,256]{2,1,0:T(8,128)(2,1)S(1)}, u32[]{:S(2)}) copy-start(bf16[2,320,256]{2,1,0:T(8,128)(2,1)S(1)} %get-tuple-element.57) | copy-start | bytes 983044
  54.0 10.1 %collective-permute-start.10 = (bf16[2,320,256]{2,1,0:T(8,128)(2,1)S(1)}, bf16[2,320,256]{2,1,0:T(8,128)(2,1)S(1)}, u32[]{:S(2)}, u32[]{:S(2)}) collective-permute-start(bf16[2,320,256]{2,1,0:T(8,128)(2,1)S(1)} %get-tuple-element.44), channel_id=1, source_target_pairs={{0,8},{4,12},{8,0},{12,4},{16,24},{20,28},{24,16},{28,20},{1,9},{5... | collective-permute-start | bytes 983048 | tf_op jit(solution)/shard_map/ppermute | solution.py:282
  62.8 1.5 %copy-start.6 = (bf16[256,1024]{1,0:T(8,128)(2,1)}, bf16[256,1024]{1,0:T(8,128)(2,1)S(1)}, u32[]{:S(2)}) copy-start(bf16[256,1024]{1,0:T(8,128)(2,1)S(1)} %get-tuple-element.51.left_ref) | copy-start | bytes 1572868
  64.2 3.2 %copy-start.11 = (bf16[512,256]{1,0:T(8,128)(2,1)S(1)}, bf16[512,256]{1,0:T(8,128)(2,1)}, u32[]{:S(2)}) copy-start(bf16[512,256]{1,0:T(8,128)(2,1)} %copy-done.10) | copy-start | bytes 786436
  64.3 3.1 %collective-permute-start.12 = (bf16[2560,256]{1,0:T(8,128)(2,1)S(1)}, bf16[2560,256]{1,0:T(8,128)(2,1)S(1)}, u32[]{:S(2)}, u32[]{:S(2)}) collective-permute-start(bf16[2560,256]{1,0:T(8,128)(2,1)S(1)} %order.1.w_o), channel_id=1, source_target_pairs={{0,4},{4,0},{8,12},{12,8},{16,20},{20,16},{24,28},{28,24},{1,5},{5... | collective-permute-start | bytes 3932168 | tf_op jit(solution)/shard_map/ppermute | solution.py:290
  64.5 8.4 %copy-start.2 = (bf16[2,2,128,2560]{3,2,1,0:T(8,128)(2,1)S(1)}, bf16[2,2,128,2560]{3,2,1,0:T(8,128)(2,1)}, u32[]{:S(2)}) copy-start(bf16[2,2,128,2560]{3,2,1,0:T(8,128)(2,1)} %param.5) | copy-start | bytes 7864324
  64.5 8.4 %copy-start.7 = (bf16[256,1024]{1,0:T(8,128)(2,1)S(1)}, bf16[256,1024]{1,0:T(8,128)(2,1)}, u32[]{:S(2)}) copy-start(bf16[256,1024]{1,0:T(8,128)(2,1)} %copy-done.6) | copy-start | bytes 1572868
  64.5 17.4 %collective-permute-start.18 = (bf16[2,320,256]{2,1,0:T(8,128)(2,1)}, bf16[2,320,256]{2,1,0:T(8,128)(2,1)S(1)}, u32[]{:S(2)}, u32[]{:S(2)}) collective-permute-start(bf16[2,320,256]{2,1,0:T(8,128)(2,1)} %copy-done.12), channel_id=1, source_target_pairs={{0,8},{4,12},{8,0},{12,4},{16,24},{20,28},{24,16},{28,20},{1,9},{5... | collective-permute-start | bytes 983048 | tf_op jit(solution)/shard_map/ppermute | solution.py:282
  65.1 17.8 %collective-permute-start.19 = (bf16[2,320,256]{2,1,0:T(8,128)(2,1)S(1)}, bf16[2,320,256]{2,1,0:T(8,128)(2,1)S(1)}, u32[]{:S(2)}, u32[]{:S(2)}) collective-permute-start(bf16[2,320,256]{2,1,0:T(8,128)(2,1)S(1)} %add_convert_fusion.unread), channel_id=1, source_target_pairs={{0,16},{4,20},{8,24},{12,28},{16,0},{20,4},{24,8},{28,12},{1,17},{... | collective-permute-start | bytes 983048 | tf_op jit(solution)/shard_map/ppermute | solution.py:282
  69.8 22.3 %collective-permute-start.13 = (bf16[2,256,640]{2,1,0:T(8,128)(2,1)S(1)}, bf16[2,256,640]{2,1,0:T(8,128)(2,1)S(1)}, u32[]{:S(2)}, u32[]{:S(2)}) collective-permute-start(bf16[2,256,640]{2,1,0:T(8,128)(2,1)S(1)} %get-tuple-element.48), channel_id=1, source_target_pairs={{0,1},{1,0},{2,3},{3,2},{4,5},{5,4},{6,7},{7,6},{8,9},{9,8},{10,11... | collective-permute-start | bytes 1966088 | tf_op jit(solution)/shard_map/ppermute | solution.py:293
  71.4 20.8 %collective-permute-start.15 = (bf16[2,256,640]{2,1,0:T(8,128)(2,1)S(1)}, bf16[2,256,640]{2,1,0:T(8,128)(2,1)S(1)}, u32[]{:S(2)}, u32[]{:S(2)}) collective-permute-start(bf16[2,256,640]{2,1,0:T(8,128)(2,1)S(1)} %get-tuple-element.49), channel_id=1, source_target_pairs={{0,2},{1,3},{2,0},{3,1},{4,6},{5,7},{6,4},{7,5},{8,10},{9,11},{10,... | collective-permute-start | bytes 1966088 | tf_op jit(solution)/shard_map/ppermute | solution.py:293
  77.3 11.6 %collective-permute-start.17 = (bf16[2,320,256]{2,1,0:T(8,128)(2,1)S(1)}, bf16[2,320,256]{2,1,0:T(8,128)(2,1)S(1)}, u32[]{:S(2)}, u32[]{:S(2)}) collective-permute-start(bf16[2,320,256]{2,1,0:T(8,128)(2,1)S(1)} %get-tuple-element.54), channel_id=1, source_target_pairs={{0,8},{4,12},{8,0},{12,4},{16,24},{20,28},{24,16},{28,20},{1,9},{5... | collective-permute-start | bytes 983048 | tf_op jit(solution)/shard_map/ppermute | solution.py:282
  77.9 11.0 %copy-start.9 = (bf16[2,320,256]{2,1,0:T(8,128)(2,1)S(1)}, bf16[2,320,256]{2,1,0:T(8,128)(2,1)}, u32[]{:S(2)}) copy-start(bf16[2,320,256]{2,1,0:T(8,128)(2,1)} %copy-done.8) | copy-start | bytes 983044
  89.1 17.3 %collective-permute-start.21 = (bf16[2,320,256]{2,1,0:T(8,128)(2,1)S(1)}, bf16[2,320,256]{2,1,0:T(8,128)(2,1)S(1)}, u32[]{:S(2)}, u32[]{:S(2)}) collective-permute-start(bf16[2,320,256]{2,1,0:T(8,128)(2,1)S(1)} %get-tuple-element.59), channel_id=1, source_target_pairs={{0,16},{4,20},{8,24},{12,28},{16,0},{20,4},{24,8},{28,12},{1,17},{... | collective-permute-start | bytes 983048 | tf_op jit(solution)/shard_map/ppermute | solution.py:282
  90.3 16.1 %collective-permute-start.20 = (bf16[2,320,256]{2,1,0:T(8,128)(2,1)S(1)}, bf16[2,320,256]{2,1,0:T(8,128)(2,1)S(1)}, u32[]{:S(2)}, u32[]{:S(2)}) collective-permute-start(bf16[2,320,256]{2,1,0:T(8,128)(2,1)S(1)} %get-tuple-element.58), channel_id=1, source_target_pairs={{0,8},{4,12},{8,0},{12,4},{16,24},{20,28},{24,16},{28,20},{1,9},{5... | collective-permute-start | bytes 983048 | tf_op jit(solution)/shard_map/ppermute | solution.py:282
  92.0 14.6 %collective-permute-start.23 = (f32[320,256]{1,0:T(8,128)S(1)}, f32[320,256]{1,0:T(8,128)S(1)}, u32[]{:S(2)}, u32[]{:S(2)}) collective-permute-start(f32[320,256]{1,0:T(8,128)S(1)} %slice_bitcast_fusion.2), channel_id=1, source_target_pairs={{0,4},{4,0},{8,12},{12,8},{16,20},{20,16},{24,28},{28,24},{1,5},{5... | collective-permute-start | bytes 983048 | tf_op jit(solution)/shard_map/ppermute | solution.py:290
  92.5 15.1 %collective-permute-start.14 = (bf16[256,640]{1,0:T(8,128)(2,1)S(1)}, bf16[256,640]{1,0:T(8,128)(2,1)S(1)}, u32[]{:S(2)}, u32[]{:S(2)}) collective-permute-start(bf16[256,640]{1,0:T(8,128)(2,1)S(1)} %get-tuple-element.63), channel_id=1, source_target_pairs={{0,2},{1,3},{2,0},{3,1},{4,6},{5,7},{6,4},{7,5},{8,10},{9,11},{10,... | collective-permute-start | bytes 983048 | tf_op jit(solution)/shard_map/ppermute | solution.py:293
  94.1 13.5 %collective-permute-start.16 = (bf16[256,640]{1,0:T(8,128)(2,1)S(1)}, bf16[256,640]{1,0:T(8,128)(2,1)S(1)}, u32[]{:S(2)}, u32[]{:S(2)}) collective-permute-start(bf16[256,640]{1,0:T(8,128)(2,1)S(1)} %get-tuple-element.64), channel_id=1, source_target_pairs={{0,1},{1,0},{2,3},{3,2},{4,5},{5,4},{6,7},{7,6},{8,9},{9,8},{10,11... | collective-permute-start | bytes 983048 | tf_op jit(solution)/shard_map/ppermute | solution.py:293
  106.5 2.2 %collective-permute-start.22 = (f32[320,256]{1,0:T(8,128)S(1)}, f32[320,256]{1,0:T(8,128)S(1)}, u32[]{:S(2)}, u32[]{:S(2)}) collective-permute-start(f32[320,256]{1,0:T(8,128)S(1)} %slice_bitcast_fusion), channel_id=1, source_target_pairs={{0,4},{4,0},{8,12},{12,8},{16,20},{20,16},{24,28},{28,24},{1,5},{5... | collective-permute-start | bytes 983048 | tf_op jit(solution)/shard_map/ppermute | solution.py:290

commit v25 on v24

--- a/solution.py
+++ b/solution.py
@@ -229,6 +229,13 @@
     onward[...] = (block[...].astype(F32) + got[...].astype(F32)).astype(BF16)
     beside_out[...] = beside[...]
     total[...] = own[...].astype(F32) + near[...].astype(F32) + far[...].astype(F32)
+
+
+def last_sum_kernel(unread, unread_too, own, near, far, mine, other):
+    del unread, unread_too
+    total = own[...].astype(F32) + near[...].astype(F32) + far[...].astype(F32)
+    mine[...] = total[0]
+    other[...] = total[1]
 
 
 def terms_kernel(n_node, idx, mixed_o, mixed_r, w_o, w_r, token, *outs):
@@ -474,7 +481,6 @@
             )(back_sends[2], back_passed, back_sends[1], out_sends[0], out_near, out_far)
             back_far, back_near = swap(onward, 2), swap(beside, 1)
             grad_out = join(out_total[0], sibling(out_total[1]), c)
-            grad_value = scatter_end(back_sends[0], (back_near, back_far), c)
         else:
             grad_value = scatter_ring(back_sends, c)
             grad_out = scatter_ring(out_sends, c)
@@ -498,6 +504,18 @@
             for j in range(1, n_node):
                 layer_out = layer_out + flip(terms[j], j).astype(F32)
         layer_out = layer_out.astype(BF16).reshape(micro, images, seq, part)
+        if line4:
+            mine, other = call(
+                last_sum_kernel,
+                "last_sum",
+                [ANY] * 2 + [VMEM] * 3,
+                [block[1:]] * 2,
+                [],
+                0,
+                kinds=[F32] * 2,
+                vmem=8,
+            )(layer_out, grad_out, back_sends[0], back_near, back_far)
+            grad_value = join(mine, sibling(other), c)
         return layer_out, grad_value, grad_out
 
     return body

time: 110 us -> 111 us (level)
  waiting for transfers between devices: 50.3 us -> 52.9 us
  other arithmetic: 4.06 us -> 2.2 us
    ppermute x4, waiting for transfers between devices: 0.01 us -> 7.63 us  [flip(): return lax.ppermute(x, 'node', [(i, i ^ j) for i in range(n_node)])]
    ppermute x12, waiting for transfers between devices: 48.9 us -> 42.3 us  [move(): lax.ppermute(x, 'wide', [(2 * s + c, 2 * d + c) for s, d in pairs for c i...]
    ppermute x8, waiting for transfers between devices: 1.34 us -> 2.95 us  [sibling(): return lax.ppermute(x, 'wide', [(i, i ^ 1) for i in range(n_wide)])]
    unnamed x26 -> x30, local copies, waits for them, and re-layouts: 3.22 us -> 3.23 us
  transfers between devices with their start and end apart: 24 -> 24, of which waited for: 12 -> 16; matrix products, arithmetic and copies ran while one was open for 3% -> 1% of each run, Pallas kernels for 23% -> 22%
where the time goes in v25:
time: 111 us
  waiting for transfers between devices  52.9 us (48%)
  Pallas kernels  25 us (23%)
  starting transfers between devices  24.8 us (22%)
  local copies, waits for them, and re-layouts  4.73 us (4%)
  other arithmetic  2.2 us (2%)
    ppermute x12, waiting for transfers between devices, move(): lax.ppermute(x, 'wide', [(2 * s + c, 2 * d + c) for s, d in pairs for c i...  42.3 us
    ppermute x12, starting transfers between devices, move(): lax.ppermute(x, 'wide', [(2 * s + c, 2 * d + c) for s, d in pairs for c i...  17 us
    ppermute x4, waiting for transfers between devices, flip(): return lax.ppermute(x, 'node', [(i, i ^ j) for i in range(n_node)])  7.63 us
    ppermute x4, starting transfers between devices, flip(): return lax.ppermute(x, 'node', [(i, i ^ j) for i in range(n_node)])  6.15 us
    pallas_call x1, Pallas kernels, body(): call(functools.partial(d_value_kernel, n_slots), 'd_value', [SMEM] + [ANY...  5.21 us
    pallas_call x1, Pallas kernels, body(): call(functools.partial(part_kernel, n_slots - 1), 'value_ahead', [SMEM] +...  4.9 us
    pallas_call x1, Pallas kernels, body(): call(functools.partial(grad_out_kernel, len(unread)), 'grad_out', [SMEM]...  4.4 us
    pallas_call x1, Pallas kernels, body(): call(gradient_kernel, 'grad_value', [SMEM] + [ANY] * 4 + [VMEM], send_sha...  4.39 us
  transfers between devices with their start and end apart: 24, of which 16 were waited for; matrix products, arithmetic and copies ran while one was open for 1% of the time, Pallas kernels for 22%

profile of v25, /device:TPU:0, one launch (start us, length us, event | category | flops | bytes accessed | tf_op | source)
XLA Modules:
  0.0 110.6 jit_solution(7918239093131947581)
XLA Ops:
  0.7 1.3 %slice_bitcast_fusion.3 = (bf16[1,320,256]{2,1,0:T(8,128)(2,1)S(1)}, bf16[1,320,256]{2,1,0:T(8,128)(2,1)S(1)}, bf16[1,320,256]{2,1,0:T(8,128)(2,1)S(1)}, bf16[1,320,256]{2,1,0:T(8,128)(2,1)S(1)}) fusion(bf16[320,512]{1,0:T(8,128)(2,1)} %param.8, bf16[320,512]{1,0:T(8,128)(2,1)} %param.9), kind=kLoop, calls=%fused_computation.29 | loop fusion | bytes 1310720 | tf_op jit(solution)/shard_map/stack | solution.py:305
  2.1 0.5 collective-permute-start
  2.6 1.3 %collective-permute-done = bf16[2,320,256]{2,1,0:T(8,128)(2,1)S(1)} collective-permute-done((bf16[2,320,256]{2,1,0:T(8,128)(2,1)S(1)}, bf16[2,320,256]{2,1,0:T(8,128)(2,1)S(1)}, u32[]{:S(2)}, u32[]{:S(2)}) %collective-permute-start) | collective-permute-done | bytes 327712 | tf_op jit(solution)/shard_map/ppermute | solution.py:297
  3.8 0.4 collective-permute-start.1
  4.2 0.1 collective-permute-start.7
  4.4 0.4 collective-permute-start.2
  4.8 2.8 %collective-permute-start.3 = (bf16[2,320,256]{2,1,0:T(8,128)(2,1)S(1)}, bf16[2,320,256]{2,1,0:T(8,128)(2,1)S(1)}, u32[]{:S(2)}, u32[]{:S(2)}) collective-permute-start(bf16[2,320,256]{2,1,0:T(8,128)(2,1)S(1)} %pad_maximum_fusion.5.rest_0_), channel_id=1, source_target_pairs={{0,8},{4,12},{8,0},{12,4},{16,24},{20,28},{24,16},{28,20},{1,9},{5... | collective-permute-start | bytes 983048 | tf_op jit(solution)/shard_map/ppermute | solution.py:289
  7.6 2.6 %collective-permute-start.4 = (bf16[2,320,256]{2,1,0:T(8,128)(2,1)S(1)}, bf16[2,320,256]{2,1,0:T(8,128)(2,1)S(1)}, u32[]{:S(2)}, u32[]{:S(2)}) collective-permute-start(bf16[2,320,256]{2,1,0:T(8,128)(2,1)S(1)} %pad_maximum_fusion.5.rest_0_), channel_id=1, source_target_pairs={{0,16},{4,20},{8,24},{12,28},{16,0},{20,4},{24,8},{28,12},{1,17},{... | collective-permute-start | bytes 983048 | tf_op jit(solution)/shard_map/ppermute | solution.py:289
  10.2 12.5 %collective-permute-done.3.unread.rest_1_ = bf16[2,320,256]{2,1,0:T(8,128)(2,1)S(1)} collective-permute-done((bf16[2,320,256]{2,1,0:T(8,128)(2,1)S(1)}, bf16[2,320,256]{2,1,0:T(8,128)(2,1)S(1)}, u32[]{:S(2)}, u32[]{:S(2)}) %collective-permute-start.3) | collective-permute-done | bytes 327712 | tf_op jit(solution)/shard_map/ppermute | solution.py:289
  22.8 2.5 %collective-permute-done.4.refs_0_ = bf16[2,320,256]{2,1,0:T(8,128)(2,1)S(1)} collective-permute-done((bf16[2,320,256]{2,1,0:T(8,128)(2,1)S(1)}, bf16[2,320,256]{2,1,0:T(8,128)(2,1)S(1)}, u32[]{:S(2)}, u32[]{:S(2)}) %collective-permute-start.4) | collective-permute-done | bytes 327712 | tf_op jit(solution)/shard_map/ppermute | solution.py:289
  25.3 0.8 relay.1
  26.1 0.7 copy-done.6
  26.8 0.4 collective-permute-start.5
  27.2 0.1 stack.67.idx
  27.3 2.6 %collective-permute-start.9 = (bf16[2,320,256]{2,1,0:T(8,128)(2,1)S(1)}, bf16[2,320,256]{2,1,0:T(8,128)(2,1)S(1)}, u32[]{:S(2)}, u32[]{:S(2)}) collective-permute-start(bf16[2,320,256]{2,1,0:T(8,128)(2,1)S(1)} %get-tuple-element.44.refs_0_.rest_0_), channel_id=1, source_target_pairs={{0,16},{4,20},{8,24},{12,28},{16,0},{20,4},{24,8},{28,12},{1,17},{... | collective-permute-start | bytes 983048 | tf_op jit(solution)/shard_map/ppermute | solution.py:289
  30.0 0.1 collective-permute-start.8
  30.1 1.7 %copy-done.1 = bf16[2,2,128,2560]{3,2,1,0:T(8,128)(2,1)S(1)} copy-done((bf16[2,2,128,2560]{3,2,1,0:T(8,128)(2,1)S(1)}, bf16[2,2,128,2560]{3,2,1,0:T(8,128)(2,1)}, u32[]{:S(2)}) %copy-start.1) | copy-done | bytes 2621464
  31.8 4.9 %value_ahead.1 = (f32[2,512,256]{2,1,0:T(8,128)S(1)}, bf16[2,512,640]{2,1,0:T(8,128)(2,1)S(1)}, bf16[2,4,4,128,128]{4,3,2,1,0:T(8,128)(2,1)S(1)}) custom-call(s32[5]{0:T(128)S(1)} %stack.67.idx, bf16[512,2560]{1,0:T(8,128)(2,1)S(1)} %bitcast.46, bf16[512,2560]{1,0:T(8,128)(2,1)} %collective-permute-done.1.x_s.right_s, bf16[4,8,128,128]{3,2,1,0:T(8,128)(2,1)S(1)} %bitcast.49, ...), custom_call_target="tpu_custom_call" | custom-call | flops 1342177280 | bytes 11272192 | tf_op jit(solution)/shard_map/value_ahead/pallas_call | solution.py:389
  36.7 7.7 %collective-permute-done.5.slot = bf16[2,320,256]{2,1,0:T(8,128)(2,1)} collective-permute-done((bf16[2,320,256]{2,1,0:T(8,128)(2,1)}, bf16[2,320,256]{2,1,0:T(8,128)(2,1)}, u32[]{:S(2)}, u32[]{:S(2)}) %collective-permute-start.5) | collective-permute-done | bytes 327712 | tf_op jit(solution)/shard_map/ppermute | solution.py:289
  44.4 2.5 %mixed.1 = (bf16[512,256]{1,0:T(8,128)(2,1)S(1)}, bf16[512,256]{1,0:T(8,128)(2,1)S(1)}) custom-call(s32[5]{0:T(128)S(1)} %stack.67.idx, f32[2,512,256]{2,1,0:T(8,128)S(1)} %get-tuple-element.38.part, bf16[2,512,640]{2,1,0:T(8,128)(2,1)S(1)} %get-tuple-element.39.last, bf16[2,4,4,128,128]{4,3,2,1,0:T(8,128)(2,1)S(1)} %get-tuple-element.40.weights, ...), custom_call_target="tpu_custom_call" | custom-call | flops 335544320 | bytes 3932160 | tf_op jit(solution)/shard_map/mixed/pallas_call | solution.py:402
  46.9 0.1 collective-permute-start.6
  47.0 0.1 collective-permute-start.11
  47.1 1.8 %collective-permute-done.8.rest_1_ = bf16[2,320,256]{2,1,0:T(8,128)(2,1)S(1)} collective-permute-done((bf16[2,320,256]{2,1,0:T(8,128)(2,1)S(1)}, bf16[2,320,256]{2,1,0:T(8,128)(2,1)S(1)}, u32[]{:S(2)}, u32[]{:S(2)}) %collective-permute-start.8) | collective-permute-done | bytes 327712 | tf_op jit(solution)/shard_map/ppermute | solution.py:289
  48.9 4.4 %grad_out.1 = (bf16[16,128]{1,0:T(8,128)(2,1)S(1)}, bf16[2,320,256]{2,1,0:T(8,128)(2,1)S(1)}, bf16[2,320,256]{2,1,0:T(8,128)(2,1)S(1)}, bf16[2,320,256]{2,1,0:T(8,128)(2,1)S(1)}, bf16[2,320,256]{2,1,0:T(8,128)(2,1)S(1)}) custom-call(s32[5]{0:T(128)S(1)} %stack.67.idx, bf16[512,2560]{1,0:T(8,128)(2,1)S(1)} %bitcast.43, ...), custom_call_target="tpu_custom_call" | custom-call | flops 1342177280 | bytes 7077888 | tf_op jit(solution)/shard_map/grad_out/pallas_call | solution.py:424
  53.3 0.7 copy-done.10
  54.0 2.0 %collective-permute-start.10 = (bf16[2,320,256]{2,1,0:T(8,128)(2,1)S(1)}, bf16[2,320,256]{2,1,0:T(8,128)(2,1)S(1)}, u32[]{:S(2)}, u32[]{:S(2)}) collective-permute-start(bf16[2,320,256]{2,1,0:T(8,128)(2,1)S(1)} %get-tuple-element.46), channel_id=1, source_target_pairs={{0,8},{4,12},{8,0},{12,4},{16,24},{20,28},{24,16},{28,20},{1,9},{5... | collective-permute-start | bytes 983048 | tf_op jit(solution)/shard_map/ppermute | solution.py:289
  56.0 1.5 %collective-permute-done.11.rest_3_ = bf16[2,320,256]{2,1,0:T(8,128)(2,1)S(1)} collective-permute-done((bf16[2,320,256]{2,1,0:T(8,128)(2,1)S(1)}, bf16[2,320,256]{2,1,0:T(8,128)(2,1)S(1)}, u32[]{:S(2)}, u32[]{:S(2)}) %collective-permute-start.11) | collective-permute-done | bytes 327712 | tf_op jit(solution)/shard_map/ppermute | solution.py:289
  57.6 5.2 %d_value.1 = (bf16[256,1024]{1,0:T(8,128)(2,1)S(1)}, bf16[2560,256]{1,0:T(8,128)(2,1)S(1)}) custom-call(s32[5]{0:T(128)S(1)} %stack.67.idx, bf16[16,128]{1,0:T(8,128)(2,1)S(1)} %get-tuple-element.47.token, bf16[512,2560]{1,0:T(8,128)(2,1)S(1)} %bitcast.44, bf16[512,2560]{1,0:T(8,128)(2,1)} %collective-permute-done.7.cot_s, ...), custom_call_target="tpu_custom_call" | custom-call | flops 1342177280 | bytes 9437184 | tf_op jit(solution)/shard_map/d_value/pallas_call | solution.py:434
  62.8 1.3 %collective-permute-done.10 = bf16[2,320,256]{2,1,0:T(8,128)(2,1)S(1)} collective-permute-done((bf16[2,320,256]{2,1,0:T(8,128)(2,1)S(1)}, bf16[2,320,256]{2,1,0:T(8,128)(2,1)S(1)}, u32[]{:S(2)}, u32[]{:S(2)}) %collective-permute-start.10) | collective-permute-done | bytes 327712 | tf_op jit(solution)/shard_map/ppermute | solution.py:289
  64.1 0.1 add_convert_fusion.unread
  64.2 0.1 order.1.w_o
  64.3 0.1 collective-permute-start.12
  64.4 0.1 pad_add_fusion.idx
  64.5 0.6 collective-permute-start.18
  65.1 2.3 %collective-permute-start.19 = (bf16[2,320,256]{2,1,0:T(8,128)(2,1)S(1)}, bf16[2,320,256]{2,1,0:T(8,128)(2,1)S(1)}, u32[]{:S(2)}, u32[]{:S(2)}) collective-permute-start(bf16[2,320,256]{2,1,0:T(8,128)(2,1)S(1)} %add_convert_fusion.unread), channel_id=1, source_target_pairs={{0,16},{4,20},{8,24},{12,28},{16,0},{20,4},{24,8},{28,12},{1,17},{... | collective-permute-start | bytes 983048 | tf_op jit(solution)/shard_map/ppermute | solution.py:289
  67.4 0.1 collective-permute-done.12.w_r
  67.4 2.4 %terms.1 = (bf16[16,128]{1,0:T(8,128)(2,1)S(1)}, bf16[2,256,640]{2,1,0:T(8,128)(2,1)S(1)}, bf16[2,256,640]{2,1,0:T(8,128)(2,1)S(1)}, bf16[4,256,640]{2,1,0:T(8,128)(2,1)S(1)}) custom-call(s32[4]{0:T(128)S(1)} %pad_add_fusion.idx, bf16[512,256]{1,0:T(8,128)(2,1)S(1)} %get-tuple-element.41.mixed_o, bf16[512,256]{1,0:T(8,128)(2,1)S(1)} %copy-done.13, ...), custom_call_target="tpu_custom_call" | custom-call | flops 1342177280 | bytes 5767168 | tf_op jit(solution)/shard_map/terms/pallas_call | solution.py:459
  69.8 1.6 %collective-permute-start.13 = (bf16[2,256,640]{2,1,0:T(8,128)(2,1)S(1)}, bf16[2,256,640]{2,1,0:T(8,128)(2,1)S(1)}, u32[]{:S(2)}, u32[]{:S(2)}) collective-permute-start(bf16[2,256,640]{2,1,0:T(8,128)(2,1)S(1)} %get-tuple-element.50), channel_id=1, source_target_pairs={{0,1},{1,0},{2,3},{3,2},{4,5},{5,4},{6,7},{7,6},{8,9},{9,8},{10,11... | collective-permute-start | bytes 1966088 | tf_op jit(solution)/shard_map/ppermute | solution.py:300
  71.4 1.5 %collective-permute-start.15 = (bf16[2,256,640]{2,1,0:T(8,128)(2,1)S(1)}, bf16[2,256,640]{2,1,0:T(8,128)(2,1)S(1)}, u32[]{:S(2)}, u32[]{:S(2)}) collective-permute-start(bf16[2,256,640]{2,1,0:T(8,128)(2,1)S(1)} %get-tuple-element.51), channel_id=1, source_target_pairs={{0,2},{1,3},{2,0},{3,1},{4,6},{5,7},{6,4},{7,5},{8,10},{9,11},{10,... | collective-permute-start | bytes 1966088 | tf_op jit(solution)/shard_map/ppermute | solution.py:300
  72.9 4.4 %grad_value.1 = (bf16[2,320,256]{2,1,0:T(8,128)(2,1)S(1)}, bf16[2,320,256]{2,1,0:T(8,128)(2,1)S(1)}, bf16[2,320,256]{2,1,0:T(8,128)(2,1)S(1)}, bf16[2,320,256]{2,1,0:T(8,128)(2,1)S(1)}) custom-call(s32[5]{0:T(128)S(1)} %stack.67.idx, bf16[16,128]{1,0:T(8,128)(2,1)S(1)} %get-tuple-element.52.token, bf16[2,320,256]{2,1,0:T(8,128)(2,1)S(1)} %add_convert_fusion.unread, ...), custom_call_target="tpu_custom_call" | custom-call | flops 1342177280 | bytes 7077888 | tf_op jit(solution)/shard_map/grad_value/pallas_call | solution.py:468
  77.3 0.6 collective-permute-start.17
  77.9 4.0 %collective-permute-done.18.near = bf16[2,320,256]{2,1,0:T(8,128)(2,1)S(1)} collective-permute-done((bf16[2,320,256]{2,1,0:T(8,128)(2,1)}, bf16[2,320,256]{2,1,0:T(8,128)(2,1)S(1)}, u32[]{:S(2)}, u32[]{:S(2)}) %collective-permute-start.18) | collective-permute-done | bytes 327712 | tf_op jit(solution)/shard_map/ppermute | solution.py:289
  81.9 0.9 collective-permute-done.19.far
  82.9 6.0 %collective-permute-done.17.got = bf16[2,320,256]{2,1,0:T(8,128)(2,1)S(1)} collective-permute-done((bf16[2,320,256]{2,1,0:T(8,128)(2,1)S(1)}, bf16[2,320,256]{2,1,0:T(8,128)(2,1)S(1)}, u32[]{:S(2)}, u32[]{:S(2)}) %collective-permute-start.17) | collective-permute-done | bytes 327712 | tf_op jit(solution)/shard_map/ppermute | solution.py:289
  88.9 0.2 sum.1
  89.1 0.1 collective-permute-start.20
  89.2 0.2 convert_element_type.44
  89.4 0.7 collective-permute-start.21
  90.0 2.2 %collective-permute-start.22 = (bf16[2,320,256]{2,1,0:T(8,128)(2,1)S(1)}, bf16[2,320,256]{2,1,0:T(8,128)(2,1)S(1)}, u32[]{:S(2)}, u32[]{:S(2)}) collective-permute-start(bf16[2,320,256]{2,1,0:T(8,128)(2,1)S(1)} %get-tuple-element.62), channel_id=1, source_target_pairs={{0,16},{4,20},{8,24},{12,28},{16,0},{20,4},{24,8},{28,12},{1,17},{... | collective-permute-start | bytes 983048 | tf_op jit(solution)/shard_map/ppermute | solution.py:289
  92.3 0.1 convert_element_type.45
  92.4 0.1 convert_element_type.49
  92.5 0.2 fusion.8
  92.6 1.6 %collective-permute-start.14 = (bf16[256,640]{1,0:T(8,128)(2,1)S(1)}, bf16[256,640]{1,0:T(8,128)(2,1)S(1)}, u32[]{:S(2)}, u32[]{:S(2)}) collective-permute-start(bf16[256,640]{1,0:T(8,128)(2,1)S(1)} %get-tuple-element.67), channel_id=1, source_target_pairs={{0,2},{1,3},{2,0},{3,1},{4,6},{5,7},{6,4},{7,5},{8,10},{9,11},{10,... | collective-permute-start | bytes 983048 | tf_op jit(solution)/shard_map/ppermute | solution.py:300
  94.2 1.5 %collective-permute-start.16 = (bf16[256,640]{1,0:T(8,128)(2,1)S(1)}, bf16[256,640]{1,0:T(8,128)(2,1)S(1)}, u32[]{:S(2)}, u32[]{:S(2)}) collective-permute-start(bf16[256,640]{1,0:T(8,128)(2,1)S(1)} %get-tuple-element.68), channel_id=1, source_target_pairs={{0,1},{1,0},{2,3},{3,2},{4,5},{5,4},{6,7},{7,6},{8,9},{9,8},{10,11... | collective-permute-start | bytes 983048 | tf_op jit(solution)/shard_map/ppermute | solution.py:300
  95.8 0.1 pad_maximum_fusion.1.unread_too
  95.9 6.4 %collective-permute-done.14 = bf16[256,640]{1,0:T(8,128)(2,1)S(1)} collective-permute-done((bf16[256,640]{1,0:T(8,128)(2,1)S(1)}, bf16[256,640]{1,0:T(8,128)(2,1)S(1)}, u32[]{:S(2)}, u32[]{:S(2)}) %collective-permute-start.14) | collective-permute-done | bytes 327712 | tf_op jit(solution)/shard_map/ppermute | solution.py:300
  102.3 1.2 %collective-permute-done.16 = bf16[256,640]{1,0:T(8,128)(2,1)S(1)} collective-permute-done((bf16[256,640]{1,0:T(8,128)(2,1)S(1)}, bf16[256,640]{1,0:T(8,128)(2,1)S(1)}, u32[]{:S(2)}, u32[]{:S(2)}) %collective-permute-start.16) | collective-permute-done | bytes 327712 | tf_op jit(solution)/shard_map/ppermute | solution.py:300
  103.5 0.2 fusion.7
  103.8 2.2 %collective-permute-done.21.near = bf16[2,320,256]{2,1,0:T(8,128)(2,1)S(1)} collective-permute-done((bf16[2,320,256]{2,1,0:T(8,128)(2,1)S(1)}, bf16[2,320,256]{2,1,0:T(8,128)(2,1)S(1)}, u32[]{:S(2)}, u32[]{:S(2)}) %collective-permute-start.21) | collective-permute-done | bytes 327712 | tf_op jit(solution)/shard_map/ppermute | solution.py:289
  106.0 1.8 %collective-permute-done.22.far = bf16[2,320,256]{2,1,0:T(8,128)(2,1)S(1)} collective-permute-done((bf16[2,320,256]{2,1,0:T(8,128)(2,1)S(1)}, bf16[2,320,256]{2,1,0:T(8,128)(2,1)S(1)}, u32[]{:S(2)}, u32[]{:S(2)}) %collective-permute-start.22) | collective-permute-done | bytes 327712 | tf_op jit(solution)/shard_map/ppermute | solution.py:289
  107.8 0.1 last_sum.1
  108.0 0.1 collective-permute-start.23
  108.0 1.6 %collective-permute-done.23 = f32[320,256]{1,0:T(8,128)S(1)} collective-permute-done((f32[320,256]{1,0:T(8,128)S(1)}, f32[320,256]{1,0:T(8,128)S(1)}, u32[]{:S(2)}, u32[]{:S(2)}) %collective-permute-start.23) | collective-permute-done | bytes 327712 | tf_op jit(solution)/shard_map/ppermute | solution.py:297
  109.7 0.9 pad_maximum_fusion.2
  (45 shorter events, 0.5 us)
Async XLA Ops:
  0.6 3.6 %copy-start = (bf16[2,2,128,2560]{3,2,1,0:T(8,128)(2,1)S(1)}, bf16[2,2,128,2560]{3,2,1,0:T(8,128)(2,1)}, u32[]{:S(2)}) copy-start(bf16[2,2,128,2560]{3,2,1,0:T(8,128)(2,1)} %param.7) | copy-start | bytes 7864324
  2.1 1.8 %collective-permute-start = (bf16[2,320,256]{2,1,0:T(8,128)(2,1)S(1)}, bf16[2,320,256]{2,1,0:T(8,128)(2,1)S(1)}, u32[]{:S(2)}, u32[]{:S(2)}) collective-permute-start(bf16[2,320,256]{2,1,0:T(8,128)(2,1)S(1)} %get-tuple-element.74), channel_id=1, source_target_pairs={{0,4},{4,0},{8,12},{12,8},{16,20},{20,16},{24,28},{28,24},{1,5},{5... | collective-permute-start | bytes 983048 | tf_op jit(solution)/shard_map/ppermute | solution.py:297
  3.8 26.2 %collective-permute-start.1 = (bf16[512,2560]{1,0:T(8,128)(2,1)}, bf16[512,2560]{1,0:T(8,128)(2,1)}, u32[]{:S(2)}, u32[]{:S(2)}) collective-permute-start(bf16[512,2560]{1,0:T(8,128)(2,1)} %bitcast.45), channel_id=1, source_target_pairs={{0,4},{4,0},{8,12},{12,8},{16,20},{20,16},{24,28},{28,24},{1,5},{5... | collective-permute-start | bytes 7864328 | tf_op jit(solution)/shard_map/ppermute | solution.py:297
  4.2 44.6 %collective-permute-start.7 = (bf16[512,2560]{1,0:T(8,128)(2,1)S(1)}, bf16[512,2560]{1,0:T(8,128)(2,1)}, u32[]{:S(2)}, u32[]{:S(2)}) collective-permute-start(bf16[512,2560]{1,0:T(8,128)(2,1)S(1)} %bitcast.42), channel_id=1, source_target_pairs={{0,4},{4,0},{8,12},{12,8},{16,20},{20,16},{24,28},{28,24},{1,5},{5... | collective-permute-start | bytes 7864328 | tf_op jit(solution)/shard_map/ppermute | solution.py:297
  4.4 25.6 %collective-permute-start.2 = (bf16[4,8,128,128]{3,2,1,0:T(8,128)(2,1)}, bf16[4,8,128,128]{3,2,1,0:T(8,128)(2,1)}, u32[]{:S(2)}, u32[]{:S(2)}) collective-permute-start(bf16[4,8,128,128]{3,2,1,0:T(8,128)(2,1)} %bitcast.48), channel_id=1, source_target_pairs={{0,4},{4,0},{8,12},{12,8},{16,20},{20,16},{24,28},{28,24},{1,5},{5... | collective-permute-start | bytes 3145736 | tf_op jit(solution)/shard_map/ppermute | solution.py:297
  4.8 17.9 %collective-permute-start.3 = (bf16[2,320,256]{2,1,0:T(8,128)(2,1)S(1)}, bf16[2,320,256]{2,1,0:T(8,128)(2,1)S(1)}, u32[]{:S(2)}, u32[]{:S(2)}) collective-permute-start(bf16[2,320,256]{2,1,0:T(8,128)(2,1)S(1)} %pad_maximum_fusion.5.rest_0_), channel_id=1, source_target_pairs={{0,8},{4,12},{8,0},{12,4},{16,24},{20,28},{24,16},{28,20},{1,9},{5... | collective-permute-start | bytes 983048 | tf_op jit(solution)/shard_map/ppermute | solution.py:289
  7.6 17.7 %collective-permute-start.4 = (bf16[2,320,256]{2,1,0:T(8,128)(2,1)S(1)}, bf16[2,320,256]{2,1,0:T(8,128)(2,1)S(1)}, u32[]{:S(2)}, u32[]{:S(2)}) collective-permute-start(bf16[2,320,256]{2,1,0:T(8,128)(2,1)S(1)} %pad_maximum_fusion.5.rest_0_), channel_id=1, source_target_pairs={{0,16},{4,20},{8,24},{12,28},{16,0},{20,4},{24,8},{28,12},{1,17},{... | collective-permute-start | bytes 983048 | tf_op jit(solution)/shard_map/ppermute | solution.py:289
  26.1 0.7 copy-start.6
  26.8 17.6 %collective-permute-start.5 = (bf16[2,320,256]{2,1,0:T(8,128)(2,1)}, bf16[2,320,256]{2,1,0:T(8,128)(2,1)}, u32[]{:S(2)}, u32[]{:S(2)}) collective-permute-start(bf16[2,320,256]{2,1,0:T(8,128)(2,1)} %get-tuple-element.37.rest_2_), channel_id=1, source_target_pairs={{0,8},{4,12},{8,0},{12,4},{16,24},{20,28},{24,16},{28,20},{1,9},{5... | collective-permute-start | bytes 983048 | tf_op jit(solution)/shard_map/ppermute | solution.py:289
  27.3 2.7 %copy-start.3 = (bf16[2,2,8,128,128]{4,3,2,1,0:T(8,128)(2,1)S(1)}, bf16[2,2,8,128,128]{4,3,2,1,0:T(8,128)(2,1)}, u32[]{:S(2)}) copy-start(bf16[2,2,8,128,128]{4,3,2,1,0:T(8,128)(2,1)} %param.6) | copy-start | bytes 3145732
  27.3 2.8 %copy-start.7 = (bf16[2,320,256]{2,1,0:T(8,128)(2,1)S(1)}, bf16[2,320,256]{2,1,0:T(8,128)(2,1)}, u32[]{:S(2)}) copy-start(bf16[2,320,256]{2,1,0:T(8,128)(2,1)} %copy-done.6) | copy-start | bytes 983044
  27.3 19.7 %collective-permute-start.9 = (bf16[2,320,256]{2,1,0:T(8,128)(2,1)S(1)}, bf16[2,320,256]{2,1,0:T(8,128)(2,1)S(1)}, u32[]{:S(2)}, u32[]{:S(2)}) collective-permute-start(bf16[2,320,256]{2,1,0:T(8,128)(2,1)S(1)} %get-tuple-element.44.refs_0_.rest_0_), channel_id=1, source_target_pairs={{0,16},{4,20},{8,24},{12,28},{16,0},{20,4},{24,8},{28,12},{1,17},{... | collective-permute-start | bytes 983048 | tf_op jit(solution)/shard_map/ppermute | solution.py:289
  30.0 18.9 %collective-permute-start.8 = (bf16[2,320,256]{2,1,0:T(8,128)(2,1)S(1)}, bf16[2,320,256]{2,1,0:T(8,128)(2,1)S(1)}, u32[]{:S(2)}, u32[]{:S(2)}) collective-permute-start(bf16[2,320,256]{2,1,0:T(8,128)(2,1)S(1)} %again.1), channel_id=1, source_target_pairs={{0,8},{4,12},{8,0},{12,4},{16,24},{20,28},{24,16},{28,20},{1,9},{5... | collective-permute-start | bytes 983048 | tf_op jit(solution)/shard_map/ppermute | solution.py:289
  30.1 1.7 %copy-start.1 = (bf16[2,2,128,2560]{3,2,1,0:T(8,128)(2,1)S(1)}, bf16[2,2,128,2560]{3,2,1,0:T(8,128)(2,1)}, u32[]{:S(2)}) copy-start(bf16[2,2,128,2560]{3,2,1,0:T(8,128)(2,1)} %param.5) | copy-start | bytes 7864324
  46.9 2.0 %collective-permute-start.6 = (bf16[512,256]{1,0:T(8,128)(2,1)S(1)}, bf16[512,256]{1,0:T(8,128)(2,1)S(1)}, u32[]{:S(2)}, u32[]{:S(2)}) collective-permute-start(bf16[512,256]{1,0:T(8,128)(2,1)S(1)} %get-tuple-element.42.mixed_s), channel_id=1, source_target_pairs={{0,4},{4,0},{8,12},{12,8},{16,20},{20,16},{24,28},{28,24},{1,5},{5... | collective-permute-start | bytes 786440 | tf_op jit(solution)/shard_map/ppermute | solution.py:297
  47.0 10.6 %collective-permute-start.11 = (bf16[2,320,256]{2,1,0:T(8,128)(2,1)S(1)}, bf16[2,320,256]{2,1,0:T(8,128)(2,1)S(1)}, u32[]{:S(2)}, u32[]{:S(2)}) collective-permute-start(bf16[2,320,256]{2,1,0:T(8,128)(2,1)S(1)} %collective-permute-done.9.rest_2_), channel_id=1, source_target_pairs={{0,8},{4,12},{8,0},{12,4},{16,24},{20,28},{24,16},{28,20},{1,9},{5... | collective-permute-start | bytes 983048 | tf_op jit(solution)/shard_map/ppermute | solution.py:289
  48.9 4.4 %copy-start.12 = (bf16[512,256]{1,0:T(8,128)(2,1)}, bf16[512,256]{1,0:T(8,128)(2,1)S(1)}, u32[]{:S(2)}) copy-start(bf16[512,256]{1,0:T(8,128)(2,1)S(1)} %collective-permute-done.6.rest_0_.mixed_r) | copy-start | bytes 786436
  53.3 0.7 copy-start.10
  54.0 3.6 %copy-start.14 = (bf16[2,320,256]{2,1,0:T(8,128)(2,1)}, bf16[2,320,256]{2,1,0:T(8,128)(2,1)S(1)}, u32[]{:S(2)}) copy-start(bf16[2,320,256]{2,1,0:T(8,128)(2,1)S(1)} %get-tuple-element.58) | copy-start | bytes 983044
  54.0 10.1 %collective-permute-start.10 = (bf16[2,320,256]{2,1,0:T(8,128)(2,1)S(1)}, bf16[2,320,256]{2,1,0:T(8,128)(2,1)S(1)}, u32[]{:S(2)}, u32[]{:S(2)}) collective-permute-start(bf16[2,320,256]{2,1,0:T(8,128)(2,1)S(1)} %get-tuple-element.46), channel_id=1, source_target_pairs={{0,8},{4,12},{8,0},{12,4},{16,24},{20,28},{24,16},{28,20},{1,9},{5... | collective-permute-start | bytes 983048 | tf_op jit(solution)/shard_map/ppermute | solution.py:289
  62.8 1.5 %copy-start.8 = (bf16[256,1024]{1,0:T(8,128)(2,1)}, bf16[256,1024]{1,0:T(8,128)(2,1)S(1)}, u32[]{:S(2)}) copy-start(bf16[256,1024]{1,0:T(8,128)(2,1)S(1)} %get-tuple-element.53.left_ref) | copy-start | bytes 1572868
  64.2 3.2 %copy-start.13 = (bf16[512,256]{1,0:T(8,128)(2,1)S(1)}, bf16[512,256]{1,0:T(8,128)(2,1)}, u32[]{:S(2)}) copy-start(bf16[512,256]{1,0:T(8,128)(2,1)} %copy-done.12) | copy-start | bytes 786436
  64.3 3.1 %collective-permute-start.12 = (bf16[2560,256]{1,0:T(8,128)(2,1)S(1)}, bf16[2560,256]{1,0:T(8,128)(2,1)S(1)}, u32[]{:S(2)}, u32[]{:S(2)}) collective-permute-start(bf16[2560,256]{1,0:T(8,128)(2,1)S(1)} %order.1.w_o), channel_id=1, source_target_pairs={{0,4},{4,0},{8,12},{12,8},{16,20},{20,16},{24,28},{28,24},{1,5},{5... | collective-permute-start | bytes 3932168 | tf_op jit(solution)/shard_map/ppermute | solution.py:297
  64.5 8.4 %copy-start.2 = (bf16[2,2,128,2560]{3,2,1,0:T(8,128)(2,1)S(1)}, bf16[2,2,128,2560]{3,2,1,0:T(8,128)(2,1)}, u32[]{:S(2)}) copy-start(bf16[2,2,128,2560]{3,2,1,0:T(8,128)(2,1)} %param.5) | copy-start | bytes 7864324
  64.5 8.4 %copy-start.9 = (bf16[256,1024]{1,0:T(8,128)(2,1)S(1)}, bf16[256,1024]{1,0:T(8,128)(2,1)}, u32[]{:S(2)}) copy-start(bf16[256,1024]{1,0:T(8,128)(2,1)} %copy-done.8) | copy-start | bytes 1572868
  64.5 17.4 %collective-permute-start.18 = (bf16[2,320,256]{2,1,0:T(8,128)(2,1)}, bf16[2,320,256]{2,1,0:T(8,128)(2,1)S(1)}, u32[]{:S(2)}, u32[]{:S(2)}) collective-permute-start(bf16[2,320,256]{2,1,0:T(8,128)(2,1)} %copy-done.14), channel_id=1, source_target_pairs={{0,8},{4,12},{8,0},{12,4},{16,24},{20,28},{24,16},{28,20},{1,9},{5... | collective-permute-start | bytes 983048 | tf_op jit(solution)/shard_map/ppermute | solution.py:289
  65.1 17.8 %collective-permute-start.19 = (bf16[2,320,256]{2,1,0:T(8,128)(2,1)S(1)}, bf16[2,320,256]{2,1,0:T(8,128)(2,1)S(1)}, u32[]{:S(2)}, u32[]{:S(2)}) collective-permute-start(bf16[2,320,256]{2,1,0:T(8,128)(2,1)S(1)} %add_convert_fusion.unread), channel_id=1, source_target_pairs={{0,16},{4,20},{8,24},{12,28},{16,0},{20,4},{24,8},{28,12},{1,17},{... | collective-permute-start | bytes 983048 | tf_op jit(solution)/shard_map/ppermute | solution.py:289
  69.8 22.5 %collective-permute-start.13 = (bf16[2,256,640]{2,1,0:T(8,128)(2,1)S(1)}, bf16[2,256,640]{2,1,0:T(8,128)(2,1)S(1)}, u32[]{:S(2)}, u32[]{:S(2)}) collective-permute-start(bf16[2,256,640]{2,1,0:T(8,128)(2,1)S(1)} %get-tuple-element.50), channel_id=1, source_target_pairs={{0,1},{1,0},{2,3},{3,2},{4,5},{5,4},{6,7},{7,6},{8,9},{9,8},{10,11... | collective-permute-start | bytes 1966088 | tf_op jit(solution)/shard_map/ppermute | solution.py:300
  71.4 21.0 %collective-permute-start.15 = (bf16[2,256,640]{2,1,0:T(8,128)(2,1)S(1)}, bf16[2,256,640]{2,1,0:T(8,128)(2,1)S(1)}, u32[]{:S(2)}, u32[]{:S(2)}) collective-permute-start(bf16[2,256,640]{2,1,0:T(8,128)(2,1)S(1)} %get-tuple-element.51), channel_id=1, source_target_pairs={{0,2},{1,3},{2,0},{3,1},{4,6},{5,7},{6,4},{7,5},{8,10},{9,11},{10,... | collective-permute-start | bytes 1966088 | tf_op jit(solution)/shard_map/ppermute | solution.py:300
  72.9 16.0 %copy-start.11 = (bf16[2,320,256]{2,1,0:T(8,128)(2,1)S(1)}, bf16[2,320,256]{2,1,0:T(8,128)(2,1)}, u32[]{:S(2)}) copy-start(bf16[2,320,256]{2,1,0:T(8,128)(2,1)} %copy-done.10) | copy-start | bytes 983044
  77.3 11.6 %collective-permute-start.17 = (bf16[2,320,256]{2,1,0:T(8,128)(2,1)S(1)}, bf16[2,320,256]{2,1,0:T(8,128)(2,1)S(1)}, u32[]{:S(2)}, u32[]{:S(2)}) collective-permute-start(bf16[2,320,256]{2,1,0:T(8,128)(2,1)S(1)} %get-tuple-element.55), channel_id=1, source_target_pairs={{0,8},{4,12},{8,0},{12,4},{16,24},{20,28},{24,16},{28,20},{1,9},{5... | collective-permute-start | bytes 983048 | tf_op jit(solution)/shard_map/ppermute | solution.py:289
  89.1 6.6 %collective-permute-start.20 = (f32[320,256]{1,0:T(8,128)S(1)}, f32[320,256]{1,0:T(8,128)S(1)}, u32[]{:S(2)}, u32[]{:S(2)}) collective-permute-start(f32[320,256]{1,0:T(8,128)S(1)} %slice_bitcast_fusion), channel_id=1, source_target_pairs={{0,4},{4,0},{8,12},{12,8},{16,20},{20,16},{24,28},{28,24},{1,5},{5... | collective-permute-start | bytes 983048 | tf_op jit(solution)/shard_map/ppermute | solution.py:297
  89.4 16.6 %collective-permute-start.21 = (bf16[2,320,256]{2,1,0:T(8,128)(2,1)S(1)}, bf16[2,320,256]{2,1,0:T(8,128)(2,1)S(1)}, u32[]{:S(2)}, u32[]{:S(2)}) collective-permute-start(bf16[2,320,256]{2,1,0:T(8,128)(2,1)S(1)} %get-tuple-element.61), channel_id=1, source_target_pairs={{0,8},{4,12},{8,0},{12,4},{16,24},{20,28},{24,16},{28,20},{1,9},{5... | collective-permute-start | bytes 983048 | tf_op jit(solution)/shard_map/ppermute | solution.py:289
  90.0 17.8 %collective-permute-start.22 = (bf16[2,320,256]{2,1,0:T(8,128)(2,1)S(1)}, bf16[2,320,256]{2,1,0:T(8,128)(2,1)S(1)}, u32[]{:S(2)}, u32[]{:S(2)}) collective-permute-start(bf16[2,320,256]{2,1,0:T(8,128)(2,1)S(1)} %get-tuple-element.62), channel_id=1, source_target_pairs={{0,16},{4,20},{8,24},{12,28},{16,0},{20,4},{24,8},{28,12},{1,17},{... | collective-permute-start | bytes 983048 | tf_op jit(solution)/shard_map/ppermute | solution.py:289
  92.6 9.6 %collective-permute-start.14 = (bf16[256,640]{1,0:T(8,128)(2,1)S(1)}, bf16[256,640]{1,0:T(8,128)(2,1)S(1)}, u32[]{:S(2)}, u32[]{:S(2)}) collective-permute-start(bf16[256,640]{1,0:T(8,128)(2,1)S(1)} %get-tuple-element.67), channel_id=1, source_target_pairs={{0,2},{1,3},{2,0},{3,1},{4,6},{5,7},{6,4},{7,5},{8,10},{9,11},{10,... | collective-permute-start | bytes 983048 | tf_op jit(solution)/shard_map/ppermute | solution.py:300
  94.2 9.3 %collective-permute-start.16 = (bf16[256,640]{1,0:T(8,128)(2,1)S(1)}, bf16[256,640]{1,0:T(8,128)(2,1)S(1)}, u32[]{:S(2)}, u32[]{:S(2)}) collective-permute-start(bf16[256,640]{1,0:T(8,128)(2,1)S(1)} %get-tuple-element.68), channel_id=1, source_target_pairs={{0,1},{1,0},{2,3},{3,2},{4,5},{5,4},{6,7},{7,6},{8,9},{9,8},{10,11... | collective-permute-start | bytes 983048 | tf_op jit(solution)/shard_map/ppermute | solution.py:300
  95.9 12.0 %copy-start.4 = (f32[320,512]{1,0:T(8,128)}, f32[320,512]{1,0:T(8,128)S(1)}, u32[]{:S(2)}) copy-start(f32[320,512]{1,0:T(8,128)S(1)} %pad_maximum_fusion.1.unread_too) | copy-start | bytes 1966084
  103.8 5.9 %copy-start.5 = (bf16[512,640]{1,0:T(8,128)(2,1)}, bf16[512,640]{1,0:T(8,128)(2,1)S(1)}, u32[]{:S(2)}) copy-start(bf16[512,640]{1,0:T(8,128)(2,1)S(1)} %pad_maximum_fusion) | copy-start | bytes 1966084
  108.0 1.7 %collective-permute-start.23 = (f32[320,256]{1,0:T(8,128)S(1)}, f32[320,256]{1,0:T(8,128)S(1)}, u32[]{:S(2)}, u32[]{:S(2)}) collective-permute-start(f32[320,256]{1,0:T(8,128)S(1)} %get-tuple-element.64), channel_id=1, source_target_pairs={{0,4},{4,0},{8,12},{12,8},{16,20},{20,16},{24,28},{28,24},{1,5},{5... | collective-permute-start | bytes 983048 | tf_op jit(solution)/shard_map/ppermute | solution.py:297
